TPU v7x, 32 devices: a whole 2x2x4 slice. The times are simulated.
32 devices in a mesh: seq: 4 (over y, x), dp: 8 (over z, core).
Axes of the slice: x: 2, y: 2, z: 4, core: 2. Of those that a mesh axis runs over, the one named last changes fastest.
Arguments:
- tokens: bfloat16 [8, 1536, 2048], P('dp', 'seq'), may hold values from -6 to 6
- seq_lengths: int32 [8, 4], P('dp'), may hold values from 1 to 768, 1536 in all within a row
- out_grad: bfloat16 [8, 1536, 2048], P('dp', 'seq'), may hold values from -6 to 6
- w_receptance: bfloat16 [2048, 2048], P(('seq', 'dp')), may hold values from -0.125 to 0.125
- w_key: bfloat16 [2048, 2048], P(('seq', 'dp')), may hold values from -0.125 to 0.125
- w_value: bfloat16 [2048, 2048], P(('seq', 'dp')), may hold values from -0.125 to 0.125
- w_gate: bfloat16 [2048, 2048], P(('seq', 'dp')), may hold values from -0.125 to 0.125
- w_output: bfloat16 [2048, 2048], P(('seq', 'dp')), may hold values from -0.25 to 0.25
- ffn_key: bfloat16 [2048, 7168], P(('seq', 'dp')), may hold values from -0.125 to 0.125
- ffn_receptance: bfloat16 [2048, 2048], P(('seq', 'dp')), may hold values from -0.125 to 0.125
- ffn_value: bfloat16 [7168, 2048], P(('seq', 'dp')), may hold values from -0.0625 to 0.0625
- vectors: bfloat16 [14, 2048], P(None, ('seq', 'dp')), as said below
Outputs:
- out: bfloat16 [8, 1536, 2048], P('dp', 'seq')
- tokens_grad: float32 [8, 1536, 2048], P('dp', 'seq')
- w_receptance_grad: float32 [2048, 2048], P(('seq', 'dp'))
- w_key_grad: float32 [2048, 2048], P(('seq', 'dp'))
- w_value_grad: float32 [2048, 2048], P(('seq', 'dp'))
- w_gate_grad: float32 [2048, 2048], P(('seq', 'dp'))
- w_output_grad: float32 [2048, 2048], P(('seq', 'dp'))
- ffn_key_grad: float32 [2048, 7168], P(('seq', 'dp'))
- ffn_receptance_grad: float32 [2048, 2048], P(('seq', 'dp'))
- ffn_value_grad: float32 [7168, 2048], P(('seq', 'dp'))
- vectors_grad: float32 [14, 2048], P(None, ('seq', 'dp'))
Inputs may be any that keep to these rules, and one draw needn't show every extreme that they name: `seq_lengths`: row g lists in order the lengths of the 4 sequences that fill group g's 1536 tokens; they sum to 1536 and the longest of each row has exactly 768 tokens. `vectors`: rows 0, 8, 10 lie in 0.5 to 1.5, rows 1, 9, 11 in -0.5 to 0.5, mixes in 0 to 1, decay parameters in -9.3 to -2.9, bonus in -1 to 1.
All inputs are finite; a program needn't handle non-finite values.
Results may differ from a plain program's by a relative error of at most 0.019.
Values may be sent and summed in bfloat16 or wider, within the bound.
No kernel may reach another device: no remote copies, remote signals or barrier semaphores. Data moves between devices by JAX's collectives and lax.ppermute only.
A program may use at most 448 MiB of HBM per device.

v0:
```python
from functools import partial

import jax
import jax.numpy as jnp
from jax import lax
from jax.sharding import PartitionSpec as P

ATTENDER_WIDTH = 64
SPAN = 64


EPSILON = 1e-05
GROUP_EPSILON = 1.0
HIGH = lax.Precision.HIGHEST


def passed_along(value, axis, by):
    devices = lax.axis_size(axis)
    pairs = [(i, i + by) for i in range(devices) if 0 <= i + by < devices]
    return lax.ppermute(value, axis, pairs)


def entering(value, axis, combine, identity):
    devices, place = (lax.axis_size(axis), lax.axis_index(axis))
    everything = jax.tree.map(
        lambda part, kind: lax.all_gather(part.astype(kind), axis),
        value,
        (jnp.bfloat16, jnp.bfloat16),
    )
    start = jax.tree.map(
        lambda part, zero: jnp.broadcast_to(jnp.asarray(zero, part.dtype), part.shape),
        value,
        identity,
    )

    def step(k, before):
        reached = k < place
        new = combine(
            before, jax.tree.map(lambda part, own: part[k].astype(own.dtype), everything, value)
        )
        return jax.tree.map(lambda a, b: jnp.where(reached, a, b), new, before)

    return lax.fori_loop(0, devices, step, start)


def carried_in(value, axis, join, neutral):
    count = lax.axis_size(axis)
    place = lax.axis_index(axis)
    ahead = count - 1 - place
    gathered = jax.tree.map(
        lambda a, kind: lax.all_gather(a.astype(kind), axis),
        value,
        jax.tree.map(lambda a: jnp.bfloat16 if a.dtype == jnp.float32 else a.dtype, value),
    )
    state = jax.tree.map(lambda a, e: jnp.zeros_like(a) + jnp.asarray(e, a.dtype), value, neutral)

    def one(step, state):
        source = count - 1 - step
        return join(
            state,
            jax.tree.map(
                lambda a, own: lax.dynamic_index_in_dim(a, source, 0, False).astype(own.dtype),
                gathered,
                value,
            ),
        )

    return lax.fori_loop(0, ahead, one, state)


def layer_norm(values, norm_gain, norm_bias):
    mean_value = jnp.mean(values, axis=-1, keepdims=True)
    centred = values - mean_value
    spread = jnp.mean(centred * centred, axis=-1, keepdims=True)
    return centred * lax.rsqrt(spread + EPSILON) * norm_gain + norm_bias


def segment_of(lengths, positions):
    starts = jnp.cumsum(lengths) - lengths
    later_flags = (positions[:, None] >= starts[None, 1:]).astype(jnp.int32)
    first_flags = jnp.any(positions[:, None] == starts[None, :], axis=1)
    return (jnp.sum(later_flags, axis=1), first_flags)


def mix_inputs(normed, received, mixes, keep_rows=None):
    previous = jnp.concatenate([received, normed[:-1]], axis=0) * keep_rows[:, None]
    return tuple((normed * factor + previous * (1.0 - factor) for factor in mixes))


def stretch_carry(
    logged_fading, starting_reward, attention_recurrence_memory, stretch_source_entries
):
    acceptor_entries, lookup_entries, payload_entries, piece_number, seg_before = (
        stretch_source_entries
    )
    span_len = acceptor_entries.shape[0]
    offsets = jnp.arange(span_len).astype(jnp.float32)
    growth = jnp.exp(offsets[:, None, None] * logged_fading)
    shrink = jnp.exp(-(offsets[:, None, None] + 1.0) * logged_fading)
    recept_grown = acceptor_entries * growth
    scores = jnp.einsum("thi,shi->hts", recept_grown, lookup_entries * shrink, precision=HIGH)
    allowed = (piece_number[:, None] == piece_number[None, :]) & (
        offsets[:, None] > offsets[None, :]
    )
    scores = jnp.where(allowed[None], scores, 0.0)
    diagonal_share = jnp.sum(acceptor_entries * starting_reward * lookup_entries, axis=-1)
    reaches = (piece_number == seg_before).astype(jnp.float32)
    result_entries = (
        jnp.einsum("hts,shj->thj", scores, payload_entries, precision=HIGH)
        + diagonal_share[:, :, None] * payload_entries
    )
    result_entries = result_entries + reaches[:, None, None] * jnp.einsum(
        "thi,hij->thj", recept_grown, attention_recurrence_memory, precision=HIGH
    )
    tail_decay = jnp.exp((span_len - 1.0 - offsets)[:, None, None] * logged_fading)
    last_same = (piece_number == piece_number[span_len - 1]).astype(jnp.float32)
    fresh_part = jnp.einsum(
        "shi,shj->hij",
        lookup_entries * tail_decay * last_same[:, None, None],
        payload_entries,
        precision=HIGH,
    )
    attention_recurrence_memory = (
        reaches[span_len - 1]
        * jnp.exp(span_len * logged_fading)[:, :, None]
        * attention_recurrence_memory
        + fresh_part
    )
    return (attention_recurrence_memory, result_entries)


def attention_recurrence_results(
    acceptor_entries,
    lookup_entries,
    payload_entries,
    fading_coefficient,
    starting_reward,
    arriving_memory,
    piece_number=None,
    prior_stretch=None,
):
    resident_entries, head_count, head_size = acceptor_entries.shape
    blocks = resident_entries // SPAN
    logged_fading = -jnp.exp(fading_coefficient)
    stretch_source_entries = (
        acceptor_entries.reshape(blocks, SPAN, head_count, head_size),
        lookup_entries.reshape(blocks, SPAN, head_count, head_size),
        payload_entries.reshape(blocks, SPAN, head_count, head_size),
        piece_number.reshape(blocks, SPAN),
        prior_stretch,
    )
    closing_memory, result_entries = lax.scan(
        partial(stretch_carry, logged_fading, starting_reward),
        arriving_memory,
        stretch_source_entries,
    )
    return result_entries.reshape(resident_entries, head_count * head_size)


def wkv_summary(
    lookup_entries, payload_entries, fading_coefficient, piece_number=None, seg_lead=None
):
    resident_entries = lookup_entries.shape[0]
    logged_fading = -jnp.exp(fading_coefficient)
    offsets = jnp.arange(resident_entries).astype(jnp.float32)
    tail_decay = jnp.exp((resident_entries - 1.0 - offsets)[:, None, None] * logged_fading)
    last_same = (piece_number == piece_number[resident_entries - 1]).astype(jnp.float32)
    total_map = jnp.einsum(
        "shi,shj->hij",
        lookup_entries * tail_decay * last_same[:, None, None],
        payload_entries,
        precision=HIGH,
    )
    carried = (piece_number[resident_entries - 1] == seg_lead).astype(jnp.float32)
    return (total_map, carried * jnp.exp(resident_entries * logged_fading))


def compose(earlier, later):
    return (later[0] * earlier[0], later[0][:, :, None] * earlier[1] + later[1])


def norm_gate(attention_recurrence_entries, gate_pre, norm_gain, norm_bias):
    resident_entries = attention_recurrence_entries.shape[0]
    grouped = attention_recurrence_entries.reshape(resident_entries, -1, ATTENDER_WIDTH)
    mean_value = jnp.mean(grouped, axis=-1, keepdims=True)
    centred = grouped - mean_value
    spread = jnp.mean(centred * centred, axis=-1, keepdims=True)
    normed = (centred * lax.rsqrt(spread + GROUP_EPSILON)).reshape(resident_entries, -1)
    return (normed * norm_gain + norm_bias) * jax.nn.silu(gate_pre)


def project(rows_b, weight):
    return jnp.dot(rows_b, weight, preferred_element_type=jnp.float32)


def weight_grad(left_rows, right_rows):
    return lax.dot_general(
        left_rows, right_rows, (((0,), (0,)), ((), ())), preferred_element_type=jnp.float32
    )


def input_grad(grad_rows, weight):
    return lax.dot_general(
        grad_rows, weight, (((1,), (1,)), ((), ())), preferred_element_type=jnp.float32
    )


def shards(
    tokens,
    seq_lengths,
    out_grad,
    w_receptance,
    w_key,
    w_value,
    w_gate,
    w_output,
    ffn_key,
    ffn_receptance,
    ffn_value,
    vectors,
):
    inputs_f = tokens[0].astype(jnp.float32)
    resident_entries = inputs_f.shape[0]
    width = inputs_f.shape[1]
    lengths = seq_lengths[0]
    start_pos = lax.axis_index("seq") * resident_entries
    positions = start_pos + jnp.arange(resident_entries, dtype=jnp.int32)
    piece_number, first_flags = segment_of(lengths, positions)
    keep_rows = 1.0 - first_flags.astype(jnp.float32)
    span_starts = start_pos + jnp.arange(resident_entries // SPAN, dtype=jnp.int32) * SPAN - 1
    prior_stretch = segment_of(lengths, span_starts)[0]
    seg_lead = segment_of(lengths, jnp.reshape(start_pos - 1, (1,)))[0][0]
    gathered = (
        lax.all_gather(w_receptance, ("seq", "dp"), axis=0, tiled=True),
        lax.all_gather(w_key, ("seq", "dp"), axis=0, tiled=True),
        lax.all_gather(w_value, ("seq", "dp"), axis=0, tiled=True),
        lax.all_gather(w_gate, ("seq", "dp"), axis=0, tiled=True),
        lax.all_gather(w_output, ("seq", "dp"), axis=0, tiled=True),
        lax.all_gather(vectors, ("seq", "dp"), axis=1, tiled=True),
    )
    full_r, full_k, full_v, full_g, full_o, full_vec = gathered
    single_real_array = full_vec.astype(jnp.float32)
    normed, ln_one_pull = jax.vjp(layer_norm, inputs_f, single_real_array[0], single_real_array[1])
    received = passed_along(normed[resident_entries - 1 :], "seq", 1)
    mixes_one = (
        single_real_array[2],
        single_real_array[3],
        single_real_array[4],
        single_real_array[5],
    )
    (mix_r, mix_k, mix_v, mix_g), mix_one_pull = jax.vjp(
        partial(mix_inputs, keep_rows=keep_rows), normed, received, mixes_one
    )
    mix_r_b = mix_r.astype(jnp.bfloat16)
    mix_k_b = mix_k.astype(jnp.bfloat16)
    mix_v_b = mix_v.astype(jnp.bfloat16)
    mix_g_b = mix_g.astype(jnp.bfloat16)
    acceptor_mapping = (
        project(mix_r_b, full_r)
        .astype(jnp.bfloat16)
        .astype(jnp.float32)
        .reshape(resident_entries, -1, ATTENDER_WIDTH)
    )
    lookup_mapping = (
        project(mix_k_b, full_k)
        .astype(jnp.bfloat16)
        .astype(jnp.float32)
        .reshape(resident_entries, -1, ATTENDER_WIDTH)
    )
    payload_mapping = (
        project(mix_v_b, full_v)
        .astype(jnp.bfloat16)
        .astype(jnp.float32)
        .reshape(resident_entries, -1, ATTENDER_WIDTH)
    )
    gate_pre = project(mix_g_b, full_g)
    fading_coefficient = single_real_array[6].reshape(-1, ATTENDER_WIDTH)
    starting_reward = single_real_array[7].reshape(-1, ATTENDER_WIDTH)
    (total_map, carry_decay), summary_pull = jax.vjp(
        partial(wkv_summary, piece_number=piece_number, seg_lead=seg_lead),
        lookup_mapping,
        payload_mapping,
        fading_coefficient,
    )
    head_count = fading_coefficient.shape[0]
    identity = (
        jnp.ones((head_count, ATTENDER_WIDTH), jnp.float32),
        jnp.zeros((head_count, ATTENDER_WIDTH, ATTENDER_WIDTH), jnp.float32),
    )
    arriving_memory = entering((carry_decay, total_map), "seq", compose, identity)[1]
    attention_recurrence_entries, weighted_key_value_pullback = jax.vjp(
        partial(
            attention_recurrence_results, piece_number=piece_number, prior_stretch=prior_stretch
        ),
        acceptor_mapping,
        lookup_mapping,
        payload_mapping,
        fading_coefficient,
        starting_reward,
        arriving_memory,
    )
    gated, gate_pull = jax.vjp(
        norm_gate,
        attention_recurrence_entries,
        gate_pre,
        single_real_array[8],
        single_real_array[9],
    )
    mixed_b = gated.astype(jnp.bfloat16)
    after = inputs_f + project(mixed_b, full_o)
    full_ck, full_cr, full_cv = (
        lax.all_gather(ffn_key, ("seq", "dp"), axis=0, tiled=True),
        lax.all_gather(ffn_receptance, ("seq", "dp"), axis=0, tiled=True),
        lax.all_gather(ffn_value, ("seq", "dp"), axis=0, tiled=True),
    )
    normed_two, ln_two_pull = jax.vjp(
        layer_norm, after, single_real_array[10], single_real_array[11]
    )
    received_two = passed_along(normed_two[resident_entries - 1 :], "seq", 1)
    (mix_k2, mix_r2), mix_two_pull = jax.vjp(
        partial(mix_inputs, keep_rows=keep_rows),
        normed_two,
        received_two,
        (single_real_array[12], single_real_array[13]),
    )
    mix_k2_b = mix_k2.astype(jnp.bfloat16)
    mix_r2_b = mix_r2.astype(jnp.bfloat16)
    key_pre = project(mix_k2_b, full_ck)
    smooth_part = jax.nn.softplus(key_pre)
    hidden_b = (smooth_part * smooth_part).astype(jnp.bfloat16)
    recept_pre = project(mix_r2_b, full_cr)
    value_pre = project(hidden_b, full_cv)
    sigmoid_part = jax.nn.sigmoid(recept_pre)
    out_rows = (after + sigmoid_part * value_pre).astype(jnp.bfloat16)
    full_ck, full_cr, full_cv = (
        lax.all_gather(ffn_key, ("seq", "dp"), axis=0, tiled=True),
        lax.all_gather(ffn_receptance, ("seq", "dp"), axis=0, tiled=True),
        lax.all_gather(ffn_value, ("seq", "dp"), axis=0, tiled=True),
    )
    cotangent = out_grad[0].astype(jnp.float32)
    d_value_b = (cotangent * sigmoid_part).astype(jnp.bfloat16)
    d_recept_two_b = (cotangent * value_pre * sigmoid_part * (1.0 - sigmoid_part)).astype(
        jnp.bfloat16
    )
    d_hidden = input_grad(d_value_b, full_cv)
    d_key_two_b = (d_hidden * 2.0 * smooth_part * jax.nn.sigmoid(key_pre)).astype(jnp.bfloat16)
    grad_cv = weight_grad(hidden_b, d_value_b)
    grad_ck = weight_grad(mix_k2_b, d_key_two_b)
    grad_cr = weight_grad(mix_r2_b, d_recept_two_b)
    d_mix_k2 = input_grad(d_key_two_b, full_ck)
    d_mix_r2 = input_grad(d_recept_two_b, full_cr)
    d_normed_two, d_received_two, d_mixes_two = mix_two_pull((d_mix_k2, d_mix_r2))
    d_last_two = passed_along(d_received_two, "seq", -1)
    d_normed_two = d_normed_two.at[resident_entries - 1].add(d_last_two[0])
    d_after_ln, d_gain_two, d_bias_two = ln_two_pull(d_normed_two)
    d_after = cotangent + d_after_ln
    full_r, full_k, full_v, full_g, full_o = (
        lax.all_gather(w_receptance, ("seq", "dp"), axis=0, tiled=True),
        lax.all_gather(w_key, ("seq", "dp"), axis=0, tiled=True),
        lax.all_gather(w_value, ("seq", "dp"), axis=0, tiled=True),
        lax.all_gather(w_gate, ("seq", "dp"), axis=0, tiled=True),
        lax.all_gather(w_output, ("seq", "dp"), axis=0, tiled=True),
    )
    d_attn_b = d_after.astype(jnp.bfloat16)
    grad_wo = weight_grad(mixed_b, d_attn_b)
    d_mixed = input_grad(d_attn_b, full_o)
    weighted_key_value_gradient, d_gate_pre, d_gn_gain, d_gn_bias = gate_pull(d_mixed)
    d_gate_b = d_gate_pre.astype(jnp.bfloat16)
    (
        receptance_gradient,
        first_keyed_gradient,
        first_valued_gradient,
        first_decay_gradient,
        reward_derivative,
        local_state_gradient,
    ) = weighted_key_value_pullback(weighted_key_value_gradient)
    grads_out = carried_in((carry_decay, local_state_gradient), "seq", compose, identity)[1]
    d_carry = jnp.sum(grads_out * arriving_memory, axis=-1)
    d_keyed_two, d_valued_two, d_decay_two = summary_pull((grads_out, d_carry))
    d_recept_b = receptance_gradient.reshape(resident_entries, width).astype(jnp.bfloat16)
    d_keyed_b = (
        (first_keyed_gradient + d_keyed_two).reshape(resident_entries, width).astype(jnp.bfloat16)
    )
    d_valued_b = (
        (first_valued_gradient + d_valued_two).reshape(resident_entries, width).astype(jnp.bfloat16)
    )
    grad_wr = weight_grad(mix_r_b, d_recept_b)
    grad_wk = weight_grad(mix_k_b, d_keyed_b)
    grad_wv = weight_grad(mix_v_b, d_valued_b)
    grad_wg = weight_grad(mix_g_b, d_gate_b)
    d_mix_r = input_grad(d_recept_b, full_r)
    d_mix_k = input_grad(d_keyed_b, full_k)
    d_mix_v = input_grad(d_valued_b, full_v)
    d_mix_g = input_grad(d_gate_b, full_g)
    d_normed, d_received, d_mixes_one = mix_one_pull((d_mix_r, d_mix_k, d_mix_v, d_mix_g))
    d_last = passed_along(d_received, "seq", -1)
    d_normed = d_normed.at[resident_entries - 1].add(d_last[0])
    d_inputs_ln, d_gain_one, d_bias_one = ln_one_pull(d_normed)
    tokens_grad = d_after + d_inputs_ln
    vector_rows = jnp.stack(
        [
            d_gain_one,
            d_bias_one,
            d_mixes_one[0],
            d_mixes_one[1],
            d_mixes_one[2],
            d_mixes_one[3],
            (first_decay_gradient + d_decay_two).reshape(-1),
            reward_derivative.reshape(-1),
            d_gn_gain,
            d_gn_bias,
            d_gain_two,
            d_bias_two,
            d_mixes_two[0],
            d_mixes_two[1],
        ],
        axis=0,
    )
    all_sums = (
        lax.psum_scatter(grad_wr, ("seq", "dp"), scatter_dimension=0, tiled=True),
        lax.psum_scatter(grad_wk, ("seq", "dp"), scatter_dimension=0, tiled=True),
        lax.psum_scatter(grad_wv, ("seq", "dp"), scatter_dimension=0, tiled=True),
        lax.psum_scatter(grad_wg, ("seq", "dp"), scatter_dimension=0, tiled=True),
        lax.psum_scatter(grad_wo, ("seq", "dp"), scatter_dimension=0, tiled=True),
        lax.psum_scatter(grad_ck, ("seq", "dp"), scatter_dimension=0, tiled=True),
        lax.psum_scatter(grad_cr, ("seq", "dp"), scatter_dimension=0, tiled=True),
        lax.psum_scatter(grad_cv, ("seq", "dp"), scatter_dimension=0, tiled=True),
        lax.psum_scatter(vector_rows, ("seq", "dp"), scatter_dimension=1, tiled=True),
    )
    sum_r, sum_k, sum_v, sum_g, sum_o, sum_ck, sum_cr, sum_cv, sum_vec = all_sums
    return (
        out_rows[None],
        tokens_grad[None],
        sum_r,
        sum_k,
        sum_v,
        sum_g,
        sum_o,
        sum_ck,
        sum_cr,
        sum_cv,
        sum_vec,
    )


def solution(mesh):
    return jax.shard_map(
        shards,
        mesh=mesh,
        in_specs=(
            P("dp", "seq", None),
            P("dp", None),
            P("dp", "seq", None),
            P(("seq", "dp"), None),
            P(("seq", "dp"), None),
            P(("seq", "dp"), None),
            P(("seq", "dp"), None),
            P(("seq", "dp"), None),
            P(("seq", "dp"), None),
            P(("seq", "dp"), None),
            P(("seq", "dp"), None),
            P(None, ("seq", "dp")),
        ),
        out_specs=(
            P("dp", "seq", None),
            P("dp", "seq", None),
            P(("seq", "dp"), None),
            P(("seq", "dp"), None),
            P(("seq", "dp"), None),
            P(("seq", "dp"), None),
            P(("seq", "dp"), None),
            P(("seq", "dp"), None),
            P(("seq", "dp"), None),
            P(("seq", "dp"), None),
            P(None, ("seq", "dp")),
        ),
        check_vma=False,
    )
```

profile of v0, /device:TPU:0, one launch (start us, length us, event | category | flops | bytes accessed | tf_op | source)
XLA Modules:
  0.0 4193.0 jit_solution(3775484090753938448)
XLA Ops:
  9.5 44.5 %all-gather.2 = bf16[32,64,14]{1,2,0:T(8,128)(2,1)S(1)} all-gather(bf16[1,64,14]{1,2,0:T(8,128)(2,1)} %bitcast.764), channel_id=1, replica_groups=mesh['seq'=4,'dp'=8] {'seq','dp'}, dimensions={0}, use_global_device_ids=true | all-gather | bytes 59136 | tf_op jit(solution)/shard_map/all_gather | solution.py:239
  69.9 21.5 all-gather.14.cloned.1.call-done
  91.4 9.9 fusion.168
  104.9 65.5 %all-gather.16.cloned.1.call-done = bf16[2048,2048]{1,0:T(8,128)(2,1)} async-done(((bf16[64,2048]{1,0:T(8,128)(2,1)}), bf16[2048,2048]{1,0:T(8,128)(2,1)}) %all-gather.16.cloned.1.call-update) | async-done | bytes 8388624 | tf_op jit(solution)/shard_map/all_gather | solution.py:236
  170.4 9.4 convolution_convert_fusion.1
  193.1 8.1 all_gather.54
  213.4 9.1 copy.150
  228.7 20.8 all-gather.18.cloned.1.call-done
  249.4 9.9 fusion.169
  259.4 6.5 reshape.973
  265.9 9.0 copy.152
  274.9 10.8 all-gather.30.cloned.1.call-done
  285.6 6.8 while.101
  308.4 168.1 %while.102 = (s32[]{:T(128)}, f32[32,64,64]{2,1,0:T(8,128)S(1)}, f32[6,64,32,64]{3,1,2,0:T(8,128)}, f32[6,64,32,64]{3,1,2,0:T(8,128)}, f32[6,64,32,64]{3,1,2,0:T...) while((s32[]{:T(128)}, f32[32,64,64]{2,1,0:T(8,128)S(1)}, ...), condition=%wide.region_11.12_spmd.clone.clone.clone, body=%wide.region_9.11_spmd.clone.clone.sunk.clone | while | flops 406206976 | bytes 48718688 | solution.py:152
  476.6 9.1 copy.153
  515.6 15.3 multiply_convert_fusion.2
  530.9 6.8 fusion.241
  544.7 8.9 copy.159
  553.6 7.3 reshape.954
  565.9 9.1 add_divide_fusion
  575.0 124.8 %all-gather.26.cloned.1.call-done = bf16[2048,7168]{1,0:T(8,128)(2,1)} async-done(((bf16[64,7168]{1,0:T(8,128)(2,1)}), bf16[2048,7168]{1,0:T(8,128)(2,1)}) %all-gather.26.cloned.1.call-update) | async-done | bytes 29360144 | tf_op jit(solution)/shard_map/all_gather | solution.py:312
  699.8 19.8 fusion.244
  719.6 156.1 %all-gather.28.cloned.1.call-done = bf16[7168,2048]{1,0:T(8,128)(2,1)} async-done(((bf16[224,2048]{1,0:T(8,128)(2,1)}), bf16[7168,2048]{1,0:T(8,128)(2,1)}) %all-gather.28.cloned.1.call-update) | async-done | bytes 29360144 | tf_op jit(solution)/shard_map/all_gather | solution.py:314
  875.7 26.5 multiply_convert_fusion
  902.2 30.4 fusion.159
  932.6 17.5 fusion.245
  950.2 10.2 multiply_reduce_fusion.2
  1000.0 10.8 fusion.128
  1019.4 564.7 %while.103 = (s32[]{:T(128)}, f32[32,64]{1,0:T(8,128)S(1)}, f32[32,64]{1,0:T(8,128)S(1)}, f32[32,64,64]{2,1,0:T(8,128)S(1)}, bf16[6,64,32,64]{3,1,2,0:T(8,128)(2...) while((s32[]{:T(128)}, f32[32,64]{1,0:T(8,128)S(1)}, ...), condition=%wide.region_27.28_spmd.clone.clone.clone.clone, body=%wide.region_20.27_spmd.clone.clone.clone.sunk.clone | while | flops 811344256 | bytes 37196900 | solution.py:152
  1042.8 27.9 dynamic_update_slice.185
  1078.3 27.8 dynamic_update_slice.186
  1136.8 27.9 dynamic_update_slice.185
  1172.2 27.8 dynamic_update_slice.186
  1230.8 27.9 dynamic_update_slice.185
  1266.3 27.8 dynamic_update_slice.186
  1324.8 27.9 dynamic_update_slice.185
  1360.3 27.8 dynamic_update_slice.186
  1418.8 27.9 dynamic_update_slice.185
  1454.2 27.8 dynamic_update_slice.186
  1512.8 27.9 dynamic_update_slice.185
  1548.3 27.8 dynamic_update_slice.186
  1585.0 7.2 reshape.957
  1592.2 7.3 reshape.956
  1608.1 9.0 fusion.249
  1619.4 6.9 while.100
  1636.3 9.1 fusion.247
  1645.5 8.6 fusion.248
  1654.2 11.5 multiply_reduce_fusion.8
  1682.6 9.6 fusion.252
  1693.5 9.9 fusion.250
  1704.8 11.2 fusion.178
  1717.5 11.3 fusion.233
  1730.2 10.9 fusion.174
  1742.4 11.1 fusion.176
  1754.9 25.4 fusion.251
  1781.7 31.2 fusion.225
  1820.5 184.0 %reduce-scatter.24.cloned.1.call-done = f32[64,2048]{1,0:T(8,128)} async-done(((f32[2048,2048]{1,0:T(8,128)}), f32[64,2048]{1,0:T(8,128)}) %reduce-scatter.24.cloned.1.call-update) | async-done | bytes 524304 | tf_op jit(solution)/shard_map/reduce_scatter | solution.py:426
  2004.5 187.3 %reduce-scatter.20.cloned.1.call-done = f32[64,2048]{1,0:T(8,128)} async-done(((f32[2048,2048]{1,0:T(8,128)}), f32[64,2048]{1,0:T(8,128)}) %reduce-scatter.20.cloned.1.call-update) | async-done | bytes 524304 | tf_op jit(solution)/shard_map/reduce_scatter | solution.py:424
  2191.9 187.2 %reduce-scatter.12.cloned.1.call-done = f32[64,2048]{1,0:T(8,128)} async-done(((f32[2048,2048]{1,0:T(8,128)}), f32[64,2048]{1,0:T(8,128)}) %reduce-scatter.12.cloned.1.call-update) | async-done | bytes 524304 | tf_op jit(solution)/shard_map/reduce_scatter | solution.py:420
  2379.1 187.2 %reduce-scatter.18.cloned.1.call-done = f32[64,2048]{1,0:T(8,128)} async-done(((f32[2048,2048]{1,0:T(8,128)}), f32[64,2048]{1,0:T(8,128)}) %reduce-scatter.18.cloned.1.call-update) | async-done | bytes 524304 | tf_op jit(solution)/shard_map/reduce_scatter | solution.py:423
  2566.3 187.2 %reduce-scatter.16.cloned.1.call-done = f32[64,2048]{1,0:T(8,128)} async-done(((f32[2048,2048]{1,0:T(8,128)}), f32[64,2048]{1,0:T(8,128)}) %reduce-scatter.16.cloned.1.call-update) | async-done | bytes 524304 | tf_op jit(solution)/shard_map/reduce_scatter | solution.py:422
  2753.5 187.2 %reduce-scatter.14.cloned.1.call-done = f32[64,2048]{1,0:T(8,128)} async-done(((f32[2048,2048]{1,0:T(8,128)}), f32[64,2048]{1,0:T(8,128)}) %reduce-scatter.14.cloned.1.call-update) | async-done | bytes 524304 | tf_op jit(solution)/shard_map/reduce_scatter | solution.py:421
  2940.7 623.3 %reduce-scatter.22.cloned.1.call-done = f32[64,7168]{1,0:T(8,128)} async-done(((f32[2048,7168]{1,0:T(8,128)}), f32[64,7168]{1,0:T(8,128)}) %reduce-scatter.22.cloned.1.call-update) | async-done | bytes 1835024 | tf_op jit(solution)/shard_map/reduce_scatter | solution.py:425
  3564.0 622.3 %reduce-scatter.26.cloned.1.call-done = f32[224,2048]{1,0:T(8,128)} async-done(((f32[7168,2048]{1,0:T(8,128)}), f32[224,2048]{1,0:T(8,128)}) %reduce-scatter.26.cloned.1.call-update) | async-done | bytes 1835024 | tf_op jit(solution)/shard_map/reduce_scatter | solution.py:427
  (714 shorter events, 623.0 us)
Async XLA Ops:
  7.2 48.7 %copy-start.3 = (bf16[1,384,2048]{2,1,0:T(8,128)(2,1)S(1)}, bf16[1,384,2048]{2,1,0:T(8,128)(2,1)}, u32[]{:S(2)}) copy-start(bf16[1,384,2048]{2,1,0:T(8,128)(2,1)} %param.24) | copy-start | bytes 4718596
  7.2 84.2 %all-gather.14.cloned.1.call-start = ((), (), s32[]{:S(2)}) async-start(), calls=%async_computation.9 | async-start | bytes 8650752 | tf_op jit(solution)/shard_map/all_gather | solution.py:235
  7.9 162.5 %all-gather.16.cloned.1.call-start = ((), (), s32[]{:S(2)}) async-start(), calls=%async_computation.10 | async-start | bytes 8650752 | tf_op jit(solution)/shard_map/all_gather | solution.py:236
  8.7 240.8 %all-gather.18.cloned.1.call-start = ((), (), s32[]{:S(2)}) async-start(), calls=%async_computation.11 | async-start | bytes 8650752 | tf_op jit(solution)/shard_map/all_gather | solution.py:234
  9.4 276.2 %all-gather.30.cloned.1.call-start = ((), (), s32[]{:S(2)}) async-start(), calls=%async_computation.25 | async-start | bytes 2621440 | tf_op jit(solution)/shard_map/all_gather | solution.py:26
  55.8 459.7 %copy-start.66 = (f32[384]{0:T(512)}, f32[384]{0:T(512)S(1)}, u32[]{:S(2)}) copy-start(f32[384]{0:T(512)S(1)} %broadcast_multiply_fusion.3) | copy-start | bytes 4612
  56.4 459.1 %copy-start.69 = (f32[384]{0:T(512)}, f32[384]{0:T(512)S(1)}, u32[]{:S(2)}) copy-start(f32[384]{0:T(512)S(1)} %fusion.216) | copy-start | bytes 4612
  56.5 459.1 %copy-start.48 = (f32[1,2048]{1,0:T(1,128)}, f32[1,2048]{1,0:T(1,128)S(1)}, u32[]{:S(2)}) copy-start(f32[1,2048]{1,0:T(1,128)S(1)} %get-tuple-element.1942) | copy-start | bytes 24580
  56.5 459.1 %copy-start.59 = (f32[1,2048]{1,0:T(1,128)}, f32[1,2048]{1,0:T(1,128)S(1)}, u32[]{:S(2)}) copy-start(f32[1,2048]{1,0:T(1,128)S(1)} %get-tuple-element.1943) | copy-start | bytes 24580
  58.8 11.1 collective-permute-start
  62.6 28.7 copy-start.78
  62.6 28.7 copy-start.88
  62.6 107.7 %copy-start.80 = (f32[1,2048]{1,0:T(1,128)}, f32[1,2048]{1,0:T(1,128)S(1)}, u32[]{:S(2)}) copy-start(f32[1,2048]{1,0:T(1,128)S(1)} %get-tuple-element.1940) | copy-start | bytes 24580
  62.7 107.7 %copy-start.90 = (f32[1,2048]{1,0:T(1,128)}, f32[1,2048]{1,0:T(1,128)S(1)}, u32[]{:S(2)}) copy-start(f32[1,2048]{1,0:T(1,128)S(1)} %get-tuple-element.1925) | copy-start | bytes 24580
  62.7 186.8 %copy-start.94 = (f32[1,2048]{1,0:T(1,128)}, f32[1,2048]{1,0:T(1,128)S(1)}, u32[]{:S(2)}) copy-start(f32[1,2048]{1,0:T(1,128)S(1)} %get-tuple-element.1939) | copy-start | bytes 24580
  62.7 186.8 %copy-start.105 = (f32[1,2048]{1,0:T(1,128)}, f32[1,2048]{1,0:T(1,128)S(1)}, u32[]{:S(2)}) copy-start(f32[1,2048]{1,0:T(1,128)S(1)} %get-tuple-element.1926) | copy-start | bytes 24580
  62.7 452.9 %copy-start.86 = (f32[1,2048]{1,0:T(1,128)}, f32[1,2048]{1,0:T(1,128)S(1)}, u32[]{:S(2)}) copy-start(f32[1,2048]{1,0:T(1,128)S(1)} %get-tuple-element.1935) | copy-start | bytes 24580
  62.7 452.9 %copy-start.92 = (f32[1,2048]{1,0:T(1,128)}, f32[1,2048]{1,0:T(1,128)S(1)}, u32[]{:S(2)}) copy-start(f32[1,2048]{1,0:T(1,128)S(1)} %get-tuple-element.1933) | copy-start | bytes 24580
  62.7 452.9 %copy-start.99 = (f32[1,2048]{1,0:T(1,128)}, f32[1,2048]{1,0:T(1,128)S(1)}, u32[]{:S(2)}) copy-start(f32[1,2048]{1,0:T(1,128)S(1)} %get-tuple-element.1934) | copy-start | bytes 24580
  62.7 452.9 %copy-start.103 = (f32[1,2048]{1,0:T(1,128)}, f32[1,2048]{1,0:T(1,128)S(1)}, u32[]{:S(2)}) copy-start(f32[1,2048]{1,0:T(1,128)S(1)} %get-tuple-element.1927) | copy-start | bytes 24580
  62.9 887.3 %copy-start.72 = (f32[384]{0:T(512)}, f32[384]{0:T(512)S(1)}, u32[]{:S(2)}) copy-start(f32[384]{0:T(512)S(1)} %convert_subtract_fusion.2) | copy-start | bytes 4612
  63.6 118.8 %copy-start.111 = (f32[384]{0:T(512)}, f32[384]{0:T(512)S(1)}, u32[]{:S(2)}) copy-start(f32[384]{0:T(512)S(1)} %compare_convert_fusion.4) | copy-start | bytes 4612
  69.9 112.6 %copy-start.113 = (f32[384]{0:T(512)}, f32[384]{0:T(512)S(1)}, u32[]{:S(2)}) copy-start(f32[384]{0:T(512)S(1)} %convert_subtract_fusion.1) | copy-start | bytes 4612
  69.9 445.7 %copy-start.76 = (f32[1,2048]{1,0:T(1,128)}, f32[1,2048]{1,0:T(1,128)S(1)}, u32[]{:S(2)}) copy-start(f32[1,2048]{1,0:T(1,128)S(1)} %collective-permute-done) | copy-start | bytes 24580
  188.0 327.6 %all-gather.20.cloned.1.call-start = ((), (), s32[]{:S(2)}) async-start(), calls=%async_computation.12 | async-start | bytes 8650752 | tf_op jit(solution)/shard_map/all_gather | solution.py:237
  188.5 342.4 %all-gather.22.cloned.1.call-start = ((), (), s32[]{:S(2)}) async-start(), calls=%async_computation.13 | async-start | bytes 8650752 | tf_op jit(solution)/shard_map/all_gather | solution.py:238
  189.1 376.8 %all-gather.24.cloned.1.call-start = ((), (), s32[]{:S(2)}) async-start(), calls=%async_computation.14 | async-start | bytes 8650752 | tf_op jit(solution)/shard_map/all_gather | solution.py:313
  189.9 510.0 %all-gather.26.cloned.1.call-start = ((), (), s32[]{:S(2)}) async-start(), calls=%async_computation.15 | async-start | bytes 30277632 | tf_op jit(solution)/shard_map/all_gather | solution.py:312
  190.6 685.1 %all-gather.28.cloned.1.call-start = ((), (), s32[]{:S(2)}) async-start(), calls=%async_computation.16 | async-start | bytes 30277632 | tf_op jit(solution)/shard_map/all_gather | solution.py:314
  191.4 1427.9 %all-gather.32.cloned.1.call-start = ((), (), s32[]{:S(2)}) async-start(), calls=%async_computation.26 | async-start | bytes 2621440 | tf_op jit(solution)/shard_map/all_gather | solution.py:51
  213.4 9.1 copy-start.15
  476.6 9.1 copy-start.16
  476.6 9.1 copy-start.39
  476.6 9.1 copy-start.54
  476.6 9.1 copy-start.82
  476.6 9.1 copy-start.84
  476.6 9.1 copy-start.122
  541.0 19.9 collective-permute-start.1
  932.6 17.5 copy-start.23
  960.7 5.7 collective-permute-start.2
  1584.9 234.2 %reduce-scatter.28.cloned.1.call-start = ((), (), s32[]{:S(2)}) async-start(), calls=%async_computation.27 | async-start | bytes 1081344
  1608.0 9.1 copy-start.36
  1632.5 12.9 copy-start.28
  1636.3 9.1 copy-start.32
  1645.3 8.7 copy-start.4
  1645.3 8.7 copy-start.26
  1645.3 8.7 copy-start.34
  1645.4 8.7 copy-start.43
  1645.4 8.7 copy-start.49
  1645.4 8.7 copy-start.60
  1645.4 8.7 copy-start.67
  1645.4 8.7 copy-start.70
  1645.4 8.7 copy-start.73
  1645.4 8.7 copy-start.77
  1645.4 8.7 copy-start.89
  1666.3 8.1 collective-permute-start.3
  1682.5 322.0 %reduce-scatter.24.cloned.1.call-start = ((), (), s32[]{:S(2)}) async-start(), calls=%async_computation.23 | async-start | bytes 17301504 | tf_op jit(solution)/shard_map/reduce_scatter | solution.py:426
  1692.2 499.7 %reduce-scatter.20.cloned.1.call-start = ((), (), s32[]{:S(2)}) async-start(), calls=%async_computation.21 | async-start | bytes 17301504 | tf_op jit(solution)/shard_map/reduce_scatter | solution.py:424
  1703.5 675.6 %reduce-scatter.12.cloned.1.call-start = ((), (), s32[]{:S(2)}) async-start(), calls=%async_computation.17 | async-start | bytes 17301504 | tf_op jit(solution)/shard_map/reduce_scatter | solution.py:420
  1716.1 850.2 %reduce-scatter.18.cloned.1.call-start = ((), (), s32[]{:S(2)}) async-start(), calls=%async_computation.20 | async-start | bytes 17301504 | tf_op jit(solution)/shard_map/reduce_scatter | solution.py:423
  1728.8 1024.7 %reduce-scatter.16.cloned.1.call-start = ((), (), s32[]{:S(2)}) async-start(), calls=%async_computation.19 | async-start | bytes 17301504 | tf_op jit(solution)/shard_map/reduce_scatter | solution.py:422
  1741.1 1199.6 %reduce-scatter.14.cloned.1.call-start = ((), (), s32[]{:S(2)}) async-start(), calls=%async_computation.18 | async-start | bytes 17301504 | tf_op jit(solution)/shard_map/reduce_scatter | solution.py:421
  1753.5 1810.4 %reduce-scatter.22.cloned.1.call-start = ((), (), s32[]{:S(2)}) async-start(), calls=%async_computation.22 | async-start | bytes 60555264 | tf_op jit(solution)/shard_map/reduce_scatter | solution.py:425
  1780.3 2405.9 %reduce-scatter.26.cloned.1.call-start = ((), (), s32[]{:S(2)}) async-start(), calls=%async_computation.24 | async-start | bytes 60555264 | tf_op jit(solution)/shard_map/reduce_scatter | solution.py:427
  (100 other events, 393.4 us)
Sparse Core Ops, SparseCore 0:
  11.0 80.2 all-gather.13
  94.3 76.0 all-gather.15
  173.4 75.9 all-gather.17
  251.7 33.8 all-gather.29
  288.5 77.3 all-gather.19
  368.7 75.9 all-gather.21
  447.7 75.8 all-gather.23
  526.4 173.3 all-gather.25
  702.7 172.9 all-gather.27
  1585.1 34.1 all-gather.31
  1682.6 136.4 reduce-scatter.27
  1821.9 182.5 reduce-scatter.23
  2007.5 184.3 reduce-scatter.19
  2194.7 184.3 reduce-scatter.11
  2381.9 184.3 reduce-scatter.17
  2569.1 184.3 reduce-scatter.15
  2756.3 184.3 reduce-scatter.13
  2943.5 620.4 reduce-scatter.21
  3566.9 619.2 reduce-scatter.25
where the time goes:
time: 4210 us; the launch traced here: 4190 us
  waiting for transfers between devices  2780 us (66%)
  matrix products  589 us (14%)
  local copies, waits for them, and re-layouts  570 us (14%)
  other arithmetic  179 us (4%)
  blocking collectives  52.6 us (1%)
    reduce_scatter x1, waiting for transfers between devices, shards(): lax.psum_scatter(grad_ck, ('seq', 'dp'), scatter_dimension=0, tiled=True)  623 us
    reduce_scatter x1, waiting for transfers between devices, shards(): lax.psum_scatter(grad_cv, ('seq', 'dp'), scatter_dimension=0, tiled=True)  622 us
    dynamic_update_slice x48, local copies, waits for them, and re-layouts, attention_recurrence_results(): lax.scan(partial(stretch_carry, logged_fading, starting_reward), arriving...  360 us
    reduce_scatter x1, waiting for transfers between devices, shards(): lax.psum_scatter(grad_wo, ('seq', 'dp'), scatter_dimension=0, tiled=True)  187 us
    reduce_scatter x1, waiting for transfers between devices, shards(): lax.psum_scatter(grad_wv, ('seq', 'dp'), scatter_dimension=0, tiled=True)  187 us
    reduce_scatter x1, waiting for transfers between devices, shards(): lax.psum_scatter(grad_wr, ('seq', 'dp'), scatter_dimension=0, tiled=True)  187 us
    reduce_scatter x1, waiting for transfers between devices, shards(): lax.psum_scatter(grad_wg, ('seq', 'dp'), scatter_dimension=0, tiled=True)  187 us
    reduce_scatter x1, waiting for transfers between devices, shards(): lax.psum_scatter(grad_wk, ('seq', 'dp'), scatter_dimension=0, tiled=True)  187 us
  transfers between devices with their start and end apart: 23, of which 17 were waited for; matrix products, arithmetic and copies ran while one was open for 13% of the time, Pallas kernels for 0%

commit v1 on v0

--- a/solution.py
+++ b/solution.py
@@ -76,7 +76,8 @@
 
 
 def segment_of(lengths, positions):
-    starts = jnp.cumsum(lengths) - lengths
+    rank = jnp.arange(lengths.shape[0])
+    starts = jnp.sum(jnp.where(rank[:, None] > rank[None, :], lengths[None, :], 0), axis=1)
     later_flags = (positions[:, None] >= starts[None, 1:]).astype(jnp.int32)
     first_flags = jnp.any(positions[:, None] == starts[None, :], axis=1)
     return (jnp.sum(later_flags, axis=1), first_flags)

time: 4210 us -> 4210 us (level)
  no operation moved by 1% of the time
where the time goes in v1:
time: 4210 us; the launch traced here: 4190 us
  waiting for transfers between devices  2780 us (66%)
  matrix products  589 us (14%)
  local copies, waits for them, and re-layouts  570 us (14%)
  other arithmetic  179 us (4%)
  blocking collectives  52.6 us (1%)
    reduce_scatter x1, waiting for transfers between devices, shards(): lax.psum_scatter(grad_ck, ('seq', 'dp'), scatter_dimension=0, tiled=True)  623 us
    reduce_scatter x1, waiting for transfers between devices, shards(): lax.psum_scatter(grad_cv, ('seq', 'dp'), scatter_dimension=0, tiled=True)  622 us
    dynamic_update_slice x48, local copies, waits for them, and re-layouts, attention_recurrence_results(): lax.scan(partial(stretch_carry, logged_fading, starting_reward), arriving...  360 us
    reduce_scatter x1, waiting for transfers between devices, shards(): lax.psum_scatter(grad_wo, ('seq', 'dp'), scatter_dimension=0, tiled=True)  187 us
    reduce_scatter x1, waiting for transfers between devices, shards(): lax.psum_scatter(grad_wv, ('seq', 'dp'), scatter_dimension=0, tiled=True)  187 us
    reduce_scatter x1, waiting for transfers between devices, shards(): lax.psum_scatter(grad_wr, ('seq', 'dp'), scatter_dimension=0, tiled=True)  187 us
    reduce_scatter x1, waiting for transfers between devices, shards(): lax.psum_scatter(grad_wg, ('seq', 'dp'), scatter_dimension=0, tiled=True)  187 us
    reduce_scatter x1, waiting for transfers between devices, shards(): lax.psum_scatter(grad_wk, ('seq', 'dp'), scatter_dimension=0, tiled=True)  187 us
  transfers between devices with their start and end apart: 23, of which 17 were waited for; matrix products, arithmetic and copies ran while one was open for 13% of the time, Pallas kernels for 0%

profile of v1, /device:TPU:0, one launch (start us, length us, event | category | flops | bytes accessed | tf_op | source)
XLA Modules:
  0.0 4193.6 jit_solution(5746866823743667113)
XLA Ops:
  9.5 44.5 %all-gather.2 = bf16[32,64,14]{1,2,0:T(8,128)(2,1)S(1)} all-gather(bf16[1,64,14]{1,2,0:T(8,128)(2,1)} %bitcast.754), channel_id=1, replica_groups=mesh['seq'=4,'dp'=8] {'seq','dp'}, dimensions={0}, use_global_device_ids=true | all-gather | bytes 59136 | tf_op jit(solution)/shard_map/all_gather | solution.py:240
  69.8 21.7 all-gather.14.cloned.1.call-done
  91.5 9.9 fusion.168
  105.0 65.5 %all-gather.16.cloned.1.call-done = bf16[2048,2048]{1,0:T(8,128)(2,1)} async-done(((bf16[64,2048]{1,0:T(8,128)(2,1)}), bf16[2048,2048]{1,0:T(8,128)(2,1)}) %all-gather.16.cloned.1.call-update) | async-done | bytes 8388624 | tf_op jit(solution)/shard_map/all_gather | solution.py:237
  170.5 9.4 convolution_convert_fusion.1
  193.2 8.1 all_gather.54
  213.5 9.1 copy.150
  228.8 20.8 all-gather.18.cloned.1.call-done
  249.5 9.9 fusion.169
  259.5 6.5 reshape.961
  266.0 9.0 copy.152
  275.0 10.8 all-gather.30.cloned.1.call-done
  285.7 6.8 while.101
  308.5 168.1 %while.102 = (s32[]{:T(128)}, f32[32,64,64]{2,1,0:T(8,128)S(1)}, f32[6,64,32,64]{3,1,2,0:T(8,128)}, f32[6,64,32,64]{3,1,2,0:T(8,128)}, f32[6,64,32,64]{3,1,2,0:T...) while((s32[]{:T(128)}, f32[32,64,64]{2,1,0:T(8,128)S(1)}, ...), condition=%wide.region_11.12_spmd.clone.clone.clone, body=%wide.region_9.11_spmd.clone.clone.sunk.clone | while | flops 406206976 | bytes 48718688 | solution.py:153
  476.7 9.1 copy.153
  515.7 15.2 multiply_convert_fusion.2
  530.9 6.7 fusion.240
  544.6 8.9 copy.159
  553.5 7.3 reshape.942
  565.8 9.1 add_divide_fusion
  574.9 125.2 %all-gather.26.cloned.1.call-done = bf16[2048,7168]{1,0:T(8,128)(2,1)} async-done(((bf16[64,7168]{1,0:T(8,128)(2,1)}), bf16[2048,7168]{1,0:T(8,128)(2,1)}) %all-gather.26.cloned.1.call-update) | async-done | bytes 29360144 | tf_op jit(solution)/shard_map/all_gather | solution.py:313
  700.1 19.8 fusion.243
  719.9 156.1 %all-gather.28.cloned.1.call-done = bf16[7168,2048]{1,0:T(8,128)(2,1)} async-done(((bf16[224,2048]{1,0:T(8,128)(2,1)}), bf16[7168,2048]{1,0:T(8,128)(2,1)}) %all-gather.28.cloned.1.call-update) | async-done | bytes 29360144 | tf_op jit(solution)/shard_map/all_gather | solution.py:315
  875.9 26.5 multiply_convert_fusion
  902.5 30.4 fusion.159
  932.9 17.5 fusion.244
  950.4 10.2 multiply_reduce_fusion.2
  1000.2 10.8 fusion.128
  1019.6 564.7 %while.103 = (s32[]{:T(128)}, f32[32,64]{1,0:T(8,128)S(1)}, f32[32,64]{1,0:T(8,128)S(1)}, f32[32,64,64]{2,1,0:T(8,128)S(1)}, bf16[6,64,32,64]{3,1,2,0:T(8,128)(2...) while((s32[]{:T(128)}, f32[32,64]{1,0:T(8,128)S(1)}, ...), condition=%wide.region_27.28_spmd.clone.clone.clone.clone, body=%wide.region_20.27_spmd.clone.clone.clone.sunk.clone | while | flops 811344256 | bytes 37196900 | solution.py:153
  1043.1 27.9 dynamic_update_slice.185
  1078.5 27.8 dynamic_update_slice.186
  1137.0 27.9 dynamic_update_slice.185
  1172.5 27.8 dynamic_update_slice.186
  1231.0 27.9 dynamic_update_slice.185
  1266.5 27.8 dynamic_update_slice.186
  1325.1 27.9 dynamic_update_slice.185
  1360.5 27.8 dynamic_update_slice.186
  1419.0 27.9 dynamic_update_slice.185
  1454.5 27.8 dynamic_update_slice.186
  1513.1 27.9 dynamic_update_slice.185
  1548.5 27.8 dynamic_update_slice.186
  1585.2 7.2 reshape.945
  1592.5 7.3 reshape.944
  1608.4 9.0 fusion.248
  1619.6 6.9 while.100
  1636.5 9.1 fusion.246
  1645.7 8.6 fusion.247
  1654.4 11.5 multiply_reduce_fusion.8
  1682.8 9.6 fusion.251
  1693.8 9.9 fusion.249
  1705.1 11.2 fusion.178
  1717.7 11.3 fusion.232
  1730.4 10.9 fusion.174
  1742.7 11.1 fusion.176
  1755.2 25.4 fusion.250
  1782.0 31.2 fusion.224
  1820.8 184.3 %reduce-scatter.24.cloned.1.call-done = f32[64,2048]{1,0:T(8,128)} async-done(((f32[2048,2048]{1,0:T(8,128)}), f32[64,2048]{1,0:T(8,128)}) %reduce-scatter.24.cloned.1.call-update) | async-done | bytes 524304 | tf_op jit(solution)/shard_map/reduce_scatter | solution.py:427
  2005.1 187.3 %reduce-scatter.20.cloned.1.call-done = f32[64,2048]{1,0:T(8,128)} async-done(((f32[2048,2048]{1,0:T(8,128)}), f32[64,2048]{1,0:T(8,128)}) %reduce-scatter.20.cloned.1.call-update) | async-done | bytes 524304 | tf_op jit(solution)/shard_map/reduce_scatter | solution.py:425
  2192.4 187.2 %reduce-scatter.12.cloned.1.call-done = f32[64,2048]{1,0:T(8,128)} async-done(((f32[2048,2048]{1,0:T(8,128)}), f32[64,2048]{1,0:T(8,128)}) %reduce-scatter.12.cloned.1.call-update) | async-done | bytes 524304 | tf_op jit(solution)/shard_map/reduce_scatter | solution.py:421
  2379.7 187.2 %reduce-scatter.18.cloned.1.call-done = f32[64,2048]{1,0:T(8,128)} async-done(((f32[2048,2048]{1,0:T(8,128)}), f32[64,2048]{1,0:T(8,128)}) %reduce-scatter.18.cloned.1.call-update) | async-done | bytes 524304 | tf_op jit(solution)/shard_map/reduce_scatter | solution.py:424
  2566.8 187.2 %reduce-scatter.16.cloned.1.call-done = f32[64,2048]{1,0:T(8,128)} async-done(((f32[2048,2048]{1,0:T(8,128)}), f32[64,2048]{1,0:T(8,128)}) %reduce-scatter.16.cloned.1.call-update) | async-done | bytes 524304 | tf_op jit(solution)/shard_map/reduce_scatter | solution.py:423
  2754.0 187.2 %reduce-scatter.14.cloned.1.call-done = f32[64,2048]{1,0:T(8,128)} async-done(((f32[2048,2048]{1,0:T(8,128)}), f32[64,2048]{1,0:T(8,128)}) %reduce-scatter.14.cloned.1.call-update) | async-done | bytes 524304 | tf_op jit(solution)/shard_map/reduce_scatter | solution.py:422
  2941.2 623.3 %reduce-scatter.22.cloned.1.call-done = f32[64,7168]{1,0:T(8,128)} async-done(((f32[2048,7168]{1,0:T(8,128)}), f32[64,7168]{1,0:T(8,128)}) %reduce-scatter.22.cloned.1.call-update) | async-done | bytes 1835024 | tf_op jit(solution)/shard_map/reduce_scatter | solution.py:426
  3564.5 622.3 %reduce-scatter.26.cloned.1.call-done = f32[224,2048]{1,0:T(8,128)} async-done(((f32[7168,2048]{1,0:T(8,128)}), f32[224,2048]{1,0:T(8,128)}) %reduce-scatter.26.cloned.1.call-update) | async-done | bytes 1835024 | tf_op jit(solution)/shard_map/reduce_scatter | solution.py:428
  (712 shorter events, 622.9 us)
Async XLA Ops:
  7.2 48.7 %copy-start.3 = (bf16[1,384,2048]{2,1,0:T(8,128)(2,1)S(1)}, bf16[1,384,2048]{2,1,0:T(8,128)(2,1)}, u32[]{:S(2)}) copy-start(bf16[1,384,2048]{2,1,0:T(8,128)(2,1)} %param.24) | copy-start | bytes 4718596
  7.2 84.3 %all-gather.14.cloned.1.call-start = ((), (), s32[]{:S(2)}) async-start(), calls=%async_computation.9 | async-start | bytes 8650752 | tf_op jit(solution)/shard_map/all_gather | solution.py:236
  7.9 162.6 %all-gather.16.cloned.1.call-start = ((), (), s32[]{:S(2)}) async-start(), calls=%async_computation.10 | async-start | bytes 8650752 | tf_op jit(solution)/shard_map/all_gather | solution.py:237
  8.7 240.9 %all-gather.18.cloned.1.call-start = ((), (), s32[]{:S(2)}) async-start(), calls=%async_computation.11 | async-start | bytes 8650752 | tf_op jit(solution)/shard_map/all_gather | solution.py:235
  9.4 276.3 %all-gather.30.cloned.1.call-start = ((), (), s32[]{:S(2)}) async-start(), calls=%async_computation.25 | async-start | bytes 2621440 | tf_op jit(solution)/shard_map/all_gather | solution.py:26
  55.8 459.7 %copy-start.66 = (f32[384]{0:T(512)}, f32[384]{0:T(512)S(1)}, u32[]{:S(2)}) copy-start(f32[384]{0:T(512)S(1)} %broadcast_multiply_fusion.3) | copy-start | bytes 4612
  56.4 459.2 %copy-start.69 = (f32[384]{0:T(512)}, f32[384]{0:T(512)S(1)}, u32[]{:S(2)}) copy-start(f32[384]{0:T(512)S(1)} %fusion.216) | copy-start | bytes 4612
  56.5 459.1 %copy-start.48 = (f32[1,2048]{1,0:T(1,128)}, f32[1,2048]{1,0:T(1,128)S(1)}, u32[]{:S(2)}) copy-start(f32[1,2048]{1,0:T(1,128)S(1)} %get-tuple-element.1942) | copy-start | bytes 24580
  56.5 459.1 %copy-start.59 = (f32[1,2048]{1,0:T(1,128)}, f32[1,2048]{1,0:T(1,128)S(1)}, u32[]{:S(2)}) copy-start(f32[1,2048]{1,0:T(1,128)S(1)} %get-tuple-element.1943) | copy-start | bytes 24580
  58.8 11.0 collective-permute-start
  62.6 28.9 copy-start.78
  62.6 28.9 copy-start.88
  62.6 107.9 %copy-start.80 = (f32[1,2048]{1,0:T(1,128)}, f32[1,2048]{1,0:T(1,128)S(1)}, u32[]{:S(2)}) copy-start(f32[1,2048]{1,0:T(1,128)S(1)} %get-tuple-element.1940) | copy-start | bytes 24580
  62.6 107.9 %copy-start.90 = (f32[1,2048]{1,0:T(1,128)}, f32[1,2048]{1,0:T(1,128)S(1)}, u32[]{:S(2)}) copy-start(f32[1,2048]{1,0:T(1,128)S(1)} %get-tuple-element.1925) | copy-start | bytes 24580
  62.6 186.9 %copy-start.94 = (f32[1,2048]{1,0:T(1,128)}, f32[1,2048]{1,0:T(1,128)S(1)}, u32[]{:S(2)}) copy-start(f32[1,2048]{1,0:T(1,128)S(1)} %get-tuple-element.1939) | copy-start | bytes 24580
  62.6 186.9 %copy-start.105 = (f32[1,2048]{1,0:T(1,128)}, f32[1,2048]{1,0:T(1,128)S(1)}, u32[]{:S(2)}) copy-start(f32[1,2048]{1,0:T(1,128)S(1)} %get-tuple-element.1926) | copy-start | bytes 24580
  62.6 453.0 %copy-start.86 = (f32[1,2048]{1,0:T(1,128)}, f32[1,2048]{1,0:T(1,128)S(1)}, u32[]{:S(2)}) copy-start(f32[1,2048]{1,0:T(1,128)S(1)} %get-tuple-element.1935) | copy-start | bytes 24580
  62.6 453.0 %copy-start.92 = (f32[1,2048]{1,0:T(1,128)}, f32[1,2048]{1,0:T(1,128)S(1)}, u32[]{:S(2)}) copy-start(f32[1,2048]{1,0:T(1,128)S(1)} %get-tuple-element.1933) | copy-start | bytes 24580
  62.6 453.0 %copy-start.99 = (f32[1,2048]{1,0:T(1,128)}, f32[1,2048]{1,0:T(1,128)S(1)}, u32[]{:S(2)}) copy-start(f32[1,2048]{1,0:T(1,128)S(1)} %get-tuple-element.1934) | copy-start | bytes 24580
  62.7 453.0 %copy-start.103 = (f32[1,2048]{1,0:T(1,128)}, f32[1,2048]{1,0:T(1,128)S(1)}, u32[]{:S(2)}) copy-start(f32[1,2048]{1,0:T(1,128)S(1)} %get-tuple-element.1927) | copy-start | bytes 24580
  62.8 887.6 %copy-start.72 = (f32[384]{0:T(512)}, f32[384]{0:T(512)S(1)}, u32[]{:S(2)}) copy-start(f32[384]{0:T(512)S(1)} %convert_subtract_fusion.2) | copy-start | bytes 4612
  63.5 119.0 %copy-start.111 = (f32[384]{0:T(512)}, f32[384]{0:T(512)S(1)}, u32[]{:S(2)}) copy-start(f32[384]{0:T(512)S(1)} %compare_convert_fusion.4) | copy-start | bytes 4612
  69.8 112.7 %copy-start.113 = (f32[384]{0:T(512)}, f32[384]{0:T(512)S(1)}, u32[]{:S(2)}) copy-start(f32[384]{0:T(512)S(1)} %convert_subtract_fusion.1) | copy-start | bytes 4612
  69.8 445.9 %copy-start.76 = (f32[1,2048]{1,0:T(1,128)}, f32[1,2048]{1,0:T(1,128)S(1)}, u32[]{:S(2)}) copy-start(f32[1,2048]{1,0:T(1,128)S(1)} %collective-permute-done) | copy-start | bytes 24580
  188.1 327.5 %all-gather.20.cloned.1.call-start = ((), (), s32[]{:S(2)}) async-start(), calls=%async_computation.12 | async-start | bytes 8650752 | tf_op jit(solution)/shard_map/all_gather | solution.py:238
  188.7 342.2 %all-gather.22.cloned.1.call-start = ((), (), s32[]{:S(2)}) async-start(), calls=%async_computation.13 | async-start | bytes 8650752 | tf_op jit(solution)/shard_map/all_gather | solution.py:239
  189.2 376.5 %all-gather.24.cloned.1.call-start = ((), (), s32[]{:S(2)}) async-start(), calls=%async_computation.14 | async-start | bytes 8650752 | tf_op jit(solution)/shard_map/all_gather | solution.py:314
  190.0 510.1 %all-gather.26.cloned.1.call-start = ((), (), s32[]{:S(2)}) async-start(), calls=%async_computation.15 | async-start | bytes 30277632 | tf_op jit(solution)/shard_map/all_gather | solution.py:313
  190.7 685.2 %all-gather.28.cloned.1.call-start = ((), (), s32[]{:S(2)}) async-start(), calls=%async_computation.16 | async-start | bytes 30277632 | tf_op jit(solution)/shard_map/all_gather | solution.py:315
  191.5 1428.0 %all-gather.32.cloned.1.call-start = ((), (), s32[]{:S(2)}) async-start(), calls=%async_computation.26 | async-start | bytes 2621440 | tf_op jit(solution)/shard_map/all_gather | solution.py:51
  213.5 9.1 copy-start.15
  476.7 9.1 copy-start.16
  476.7 9.1 copy-start.39
  476.7 9.1 copy-start.54
  476.7 9.1 copy-start.82
  476.7 9.1 copy-start.84
  476.7 9.1 copy-start.122
  540.9 19.9 collective-permute-start.1
  932.9 17.5 copy-start.23
  961.0 5.7 collective-permute-start.2
  1585.2 234.2 %reduce-scatter.28.cloned.1.call-start = ((), (), s32[]{:S(2)}) async-start(), calls=%async_computation.27 | async-start | bytes 1081344
  1608.3 9.1 copy-start.36
  1632.7 12.9 copy-start.28
  1636.5 9.1 copy-start.32
  1645.6 8.7 copy-start.4
  1645.6 8.7 copy-start.26
  1645.6 8.7 copy-start.34
  1645.6 8.7 copy-start.43
  1645.6 8.7 copy-start.49
  1645.6 8.7 copy-start.60
  1645.6 8.7 copy-start.67
  1645.6 8.7 copy-start.70
  1645.6 8.7 copy-start.73
  1645.7 8.7 copy-start.77
  1645.7 8.7 copy-start.89
  1666.5 8.1 collective-permute-start.3
  1682.7 322.4 %reduce-scatter.24.cloned.1.call-start = ((), (), s32[]{:S(2)}) async-start(), calls=%async_computation.23 | async-start | bytes 17301504 | tf_op jit(solution)/shard_map/reduce_scatter | solution.py:427
  1692.4 500.0 %reduce-scatter.20.cloned.1.call-start = ((), (), s32[]{:S(2)}) async-start(), calls=%async_computation.21 | async-start | bytes 17301504 | tf_op jit(solution)/shard_map/reduce_scatter | solution.py:425
  1703.7 676.0 %reduce-scatter.12.cloned.1.call-start = ((), (), s32[]{:S(2)}) async-start(), calls=%async_computation.17 | async-start | bytes 17301504 | tf_op jit(solution)/shard_map/reduce_scatter | solution.py:421
  1716.3 850.5 %reduce-scatter.18.cloned.1.call-start = ((), (), s32[]{:S(2)}) async-start(), calls=%async_computation.20 | async-start | bytes 17301504 | tf_op jit(solution)/shard_map/reduce_scatter | solution.py:424
  1729.0 1025.0 %reduce-scatter.16.cloned.1.call-start = ((), (), s32[]{:S(2)}) async-start(), calls=%async_computation.19 | async-start | bytes 17301504 | tf_op jit(solution)/shard_map/reduce_scatter | solution.py:423
  1741.3 1199.9 %reduce-scatter.14.cloned.1.call-start = ((), (), s32[]{:S(2)}) async-start(), calls=%async_computation.18 | async-start | bytes 17301504 | tf_op jit(solution)/shard_map/reduce_scatter | solution.py:422
  1753.8 1810.8 %reduce-scatter.22.cloned.1.call-start = ((), (), s32[]{:S(2)}) async-start(), calls=%async_computation.22 | async-start | bytes 60555264 | tf_op jit(solution)/shard_map/reduce_scatter | solution.py:426
  1780.6 2406.2 %reduce-scatter.26.cloned.1.call-start = ((), (), s32[]{:S(2)}) async-start(), calls=%async_computation.24 | async-start | bytes 60555264 | tf_op jit(solution)/shard_map/reduce_scatter | solution.py:428
  (100 other events, 393.4 us)
Sparse Core Ops, SparseCore 0:
  11.0 80.4 all-gather.13
  94.5 75.9 all-gather.15
  173.5 75.9 all-gather.17
  251.8 33.8 all-gather.29
  288.6 77.3 all-gather.19
  368.8 75.9 all-gather.21
  447.8 75.9 all-gather.23
  526.7 173.3 all-gather.25
  702.9 172.9 all-gather.27
  1585.3 34.1 all-gather.31
  1682.9 136.4 reduce-scatter.27
  1822.2 182.9 reduce-scatter.23
  2008.1 184.3 reduce-scatter.19
  2195.3 184.3 reduce-scatter.11
  2382.5 184.3 reduce-scatter.17
  2569.7 184.3 reduce-scatter.15
  2756.9 184.3 reduce-scatter.13
  2944.1 620.4 reduce-scatter.21
  3567.5 619.2 reduce-scatter.25

commit v2 on v1

v2 whole, which is shorter than its diff:
```python
from functools import partial

import jax
import jax.numpy as jnp
from jax import lax
from jax.experimental import pallas as pl
from jax.experimental.pallas import tpu as pltpu
from jax.sharding import PartitionSpec as P

HEAD = 64
PAIR = 128
CHUNK = 128
EPSILON = 1e-05
GROUP_EPSILON = 1.0
BF = jnp.bfloat16
F32 = jnp.float32
NT = (((1,), (1,)), ((), ()))
TN = (((0,), (0,)), ((), ()))
NN = (((1,), (0,)), ((), ()))


def swap(value, axis, distance):
    size = lax.axis_size(axis)
    return lax.ppermute(value, axis, [(i, i ^ distance) for i in range(size)])


def gather_seq(part):
    size, here = lax.axis_size("seq"), lax.axis_index("seq")
    whole = jnp.zeros((size,) + part.shape, part.dtype)

    def put(whole, piece, distance, start=0):
        at = (here ^ distance, start) + (0,) * (part.ndim - 1)
        return lax.dynamic_update_slice(whole, piece[None], at)

    whole = put(whole, part, 0)
    if size == 4:
        half = part.shape[0] // 2
        one, two = swap(part, "seq", 1), swap(part, "seq", 2)
        low, high = swap(one[:half], "seq", 2), swap(two[half:], "seq", 1)
        whole = put(put(whole, one, 1), two, 2)
        return put(put(whole, low, 3), high, 3, half)
    for distance in range(1, size):
        whole = put(whole, swap(part, "seq", distance), distance)
    return whole


def scatter_seq(parts):
    size, here = lax.axis_size("seq"), lax.axis_index("seq")

    def take(distance):
        return lax.dynamic_index_in_dim(parts, here ^ distance, 0, False)

    own = take(0).astype(F32)
    if size == 4:
        far = take(3)
        half = far.shape[0] // 2
        low, high = swap(far[:half], "seq", 1), swap(far[half:], "seq", 2)
        one, two = take(1), take(2)
        two = jnp.concatenate([(two[:half].astype(F32) + low.astype(F32)).astype(BF), two[half:]], axis=0)
        one = jnp.concatenate([one[:half], (one[half:].astype(F32) + high.astype(F32)).astype(BF)], axis=0)
        return own + swap(one, "seq", 1).astype(F32) + swap(two, "seq", 2).astype(F32)
    for distance in range(1, size):
        own = own + swap(take(distance), "seq", distance).astype(F32)
    return own


def trade_seq(parts):
    size, here = lax.axis_size("seq"), lax.axis_index("seq")
    result = jnp.zeros_like(parts)
    for distance in range(size):
        piece = lax.dynamic_index_in_dim(parts, here ^ distance, 0, True)
        if distance:
            piece = swap(piece, "seq", distance)
        result = lax.dynamic_update_slice_in_dim(result, piece, here ^ distance, 0)
    return result


def bits_of(size):
    return [1 << b for b in range(size.bit_length() - 1)]


def gather_small(part):
    for axis in ("dp", "seq"):
        for bit in bits_of(lax.axis_size(axis)):
            other = swap(part, axis, bit)
            second = (lax.axis_index(axis) & bit) != 0
            part = jnp.concatenate(
                [jnp.where(second, other, part), jnp.where(second, part, other)], axis=0
            )
    return part


def scatter_small(parts):
    for axis in ("seq", "dp"):
        for bit in reversed(bits_of(lax.axis_size(axis))):
            half = parts.shape[0] // 2
            second = (lax.axis_index(axis) & bit) != 0
            low, high = parts[:half], parts[half:]
            parts = jnp.where(second, high, low) + swap(jnp.where(second, low, high), axis, bit)
    return parts[0]


def by_columns(weight):
    rows, columns = weight.shape
    size = lax.axis_size("seq")
    return trade_seq(weight.reshape(rows, size, columns // size).transpose(1, 0, 2))


def all_rows(parts):
    gathered = lax.all_gather(parts, "dp", axis=0)
    return gathered.transpose(1, 0, 2, 3).reshape(-1, parts.shape[-1])


def owners_rows(grad):
    seq, dp = lax.axis_size("seq"), lax.axis_size("dp")
    rows, columns = grad.shape[0] // (seq * dp), grad.shape[1]
    parts = grad.astype(BF).reshape(seq, dp, rows, columns).transpose(1, 0, 2, 3).reshape(-1, columns)
    summed = lax.psum_scatter(parts, "dp", scatter_dimension=0, tiled=True).reshape(seq, rows, columns)
    return trade_seq(summed).transpose(1, 0, 2).reshape(rows, seq * columns).astype(F32)


def head_masks():
    lane = lax.broadcasted_iota(jnp.int32, (1, PAIR), 1)
    first = (lane < HEAD).astype(F32)
    return first, 1.0 - first


def same_head():
    row = lax.broadcasted_iota(jnp.int32, (PAIR, PAIR), 0) < HEAD
    column = lax.broadcasted_iota(jnp.int32, (PAIR, PAIR), 1) < HEAD
    return row == column


def dot(left, right, dims):
    return lax.dot_general(left, right, dims, preferred_element_type=F32)


def head_sum(values, ones):
    return dot(values.astype(BF), ones, NN)


def head_sum_fine(values, ones):
    coarse = values.astype(BF)
    rest = (values - coarse.astype(F32)).astype(BF)
    return dot(coarse, ones, NN) + dot(rest, ones, NN)


def stacked(values, first, second):
    return jnp.concatenate([(values * first).astype(BF), (values * second).astype(BF)], axis=0)


def masks_of(rows_ref, columns_ref):
    segment = rows_ref[:, 0:1]
    reaches = rows_ref[:, 1:2]
    last_same = rows_ref[:, 2:3]
    reach_last = rows_ref[CHUNK - 1 : CHUNK, 1:2]
    before = lax.broadcasted_iota(jnp.int32, (CHUNK, CHUNK), 1) < lax.broadcasted_iota(
        jnp.int32, (CHUNK, CHUNK), 0
    )
    allowed = jnp.where((segment == columns_ref[0:1, :]) & before, 1.0, 0.0)
    return reaches, last_same, reach_last, jnp.concatenate([allowed, allowed], axis=0)


def wkv_forward_body(
    r_ref, k_ref, v_ref, g_ref, rows_ref, columns_ref, grow_ref, shrink_ref, tail_ref, par_ref,
    mixed_ref, wkv_ref, states_ref, state,
):
    @pl.when(pl.program_id(0) == 0)
    def _():
        state[...] = jnp.zeros_like(state)

    first, second = head_masks()
    block = same_head()
    ones = jnp.where(block, 1.0, 0.0).astype(BF)
    reaches, last_same, reach_last, allowed = masks_of(rows_ref, columns_ref)
    for pair in range(r_ref.shape[1] // PAIR):
        at = slice(pair * PAIR, (pair + 1) * PAIR)
        r, k, v = r_ref[:, at].astype(F32), k_ref[:, at].astype(F32), v_ref[:, at].astype(F32)
        bonus, gain, bias, decay = (par_ref[i : i + 1, at] for i in range(4))
        held = state[at, :]
        held_b = held.astype(BF)
        states_ref[0, at, :] = held_b
        grown = r * grow_ref[:, at]
        shrunk = (k * shrink_ref[:, at]).astype(BF)
        scores = (dot(stacked(grown, first, second), shrunk, NT) * allowed).astype(BF)
        both = jnp.concatenate([scores[:CHUNK], scores[CHUNK:]], axis=1)
        wkv = dot(both, stacked(v, first, second), NN)
        wkv = wkv + dot((grown * reaches).astype(BF), held_b, NT)
        wkv = wkv + head_sum(r * bonus * k, ones) * v
        fresh = dot(v_ref[:, at], (k * tail_ref[:, at] * last_same).astype(BF), TN)
        state[at, :] = held * (decay * reach_last) + jnp.where(block, fresh, 0.0)
        wkv_ref[:, at] = wkv
        centred = wkv - head_sum_fine(wkv, ones) * (1.0 / HEAD)
        spread = head_sum(centred * centred, ones) * (1.0 / HEAD)
        normed = centred * lax.rsqrt(spread + GROUP_EPSILON) * gain + bias
        gate = g_ref[:, at]
        mixed_ref[:, at] = (normed * (gate / (1.0 + jnp.exp(-gate)))).astype(BF)


def wkv_backward_body(
    r_ref, k_ref, v_ref, g_ref, wkv_ref, d_mixed_ref, states_ref,
    rows_ref, columns_ref, grow_ref, shrink_ref, tail_ref, par_ref,
    d_r_ref, d_k_ref, d_v_ref, d_g_ref, sums_ref, d_state,
):
    @pl.when(pl.program_id(0) == 0)
    def _():
        d_state[...] = jnp.zeros_like(d_state)
        sums_ref[...] = jnp.zeros_like(sums_ref)

    first, second = head_masks()
    block = same_head()
    ones = jnp.where(block, 1.0, 0.0).astype(BF)
    reaches, last_same, reach_last, allowed = masks_of(rows_ref, columns_ref)
    offset = lax.broadcasted_iota(jnp.int32, (CHUNK, PAIR), 0).astype(F32)
    for pair in range(r_ref.shape[1] // PAIR):
        at = slice(pair * PAIR, (pair + 1) * PAIR)
        bonus, gain, bias, decay = (par_ref[i : i + 1, at] for i in range(4))
        wkv, gate, d_mixed = wkv_ref[:, at], g_ref[:, at], d_mixed_ref[:, at]
        centred = wkv - head_sum_fine(wkv, ones) * (1.0 / HEAD)
        spread = head_sum(centred * centred, ones) * (1.0 / HEAD)
        inverse = lax.rsqrt(spread + GROUP_EPSILON)
        normed = centred * inverse
        opened = 1.0 / (1.0 + jnp.exp(-gate))
        d_scaled = d_mixed * gate * opened
        d_g = d_mixed * (normed * gain + bias) * opened * (1.0 + gate * (1.0 - opened))
        d_g_ref[:, at] = d_g.astype(BF)
        d_normed = d_scaled * gain
        mean_one = head_sum(d_normed, ones) * (1.0 / HEAD)
        mean_two = head_sum(d_normed * normed, ones) * (1.0 / HEAD)
        d_wkv = inverse * (d_normed - mean_one - normed * mean_two)
        r, k, v = r_ref[:, at].astype(F32), k_ref[:, at].astype(F32), v_ref[:, at].astype(F32)
        v_b, d_wkv_b = v_ref[:, at], d_wkv.astype(BF)
        grow, shrink, tail = grow_ref[:, at], shrink_ref[:, at], tail_ref[:, at] * last_same
        held = states_ref[0, at, :]
        later = d_state[at, :]
        later_b = later.astype(BF)
        grown = r * grow
        shrunk = k * shrink
        shrunk_b = shrunk.astype(BF)
        tailed_b = (k * tail).astype(BF)
        grown_two = stacked(grown, first, second)
        d_wkv_two = stacked(d_wkv, first, second)
        scores = (dot(grown_two, shrunk_b, NT) * allowed).astype(BF)
        d_scores = (dot(d_wkv_two, v_b, NT) * allowed).astype(BF)
        d_both = jnp.concatenate([d_scores[:CHUNK], d_scores[CHUNK:]], axis=1)
        d_grown = dot(d_both, stacked(shrunk, first, second), NN)
        d_grown = d_grown + dot((d_wkv * reaches).astype(BF), held, NN)
        d_shrunk = dot(d_scores, grown_two, TN)
        d_tailed = dot(v_b, later_b, NN)
        share = head_sum(r * bonus * k, ones)
        d_share = head_sum(d_wkv * v, ones)
        d_v = dot(scores, d_wkv_two, TN) + dot(tailed_b, later_b, NT) + share * d_wkv
        d_r_ref[:, at] = (d_grown * grow + d_share * bonus * k).astype(BF)
        d_k_ref[:, at] = (d_shrunk * shrink + d_tailed * tail + d_share * bonus * r).astype(BF)
        d_v_ref[:, at] = d_v.astype(BF)
        carried = decay * reach_last
        d_fresh = dot(d_wkv_b, (grown * reaches).astype(BF), TN)
        d_state[at, :] = later * carried + jnp.where(block, d_fresh, 0.0)
        grown_b = grown.astype(BF).astype(F32)
        d_log = (
            offset * grown_b * d_grown
            - (offset + 1.0) * shrunk_b.astype(F32) * d_shrunk
            + (CHUNK - 1.0 - offset) * tailed_b.astype(F32) * d_tailed
        )
        kept = CHUNK * carried * jnp.sum(held.astype(F32) * later, axis=0, keepdims=True)
        sums_ref[0:1, at] += jnp.sum(d_log, axis=0, keepdims=True) + kept
        sums_ref[1:2, at] += jnp.sum(d_share * r * k, axis=0, keepdims=True)
        sums_ref[2:3, at] += jnp.sum(d_scaled * normed, axis=0, keepdims=True)
        sums_ref[3:4, at] += jnp.sum(d_scaled, axis=0, keepdims=True)


def wkv_specs(width, chunks, backward):
    def chunk(i):
        return chunks - 1 - i if backward else i

    tokens = pl.BlockSpec((CHUNK, width), lambda i: (chunk(i), 0))
    states = pl.BlockSpec((1, width, PAIR), lambda i: (chunk(i), 0, 0))
    rows = pl.BlockSpec((CHUNK, PAIR), lambda i: (chunk(i), 0))
    columns = pl.BlockSpec((8, CHUNK), lambda i: (0, chunk(i)))
    table = pl.BlockSpec((CHUNK, width), lambda i: (0, 0))
    params = pl.BlockSpec((8, width), lambda i: (0, 0))
    return tokens, states, [rows, columns, table, table, table, params], params


def wkv_forward(r, k, v, gate, tables):
    length, width = r.shape
    chunks = length // CHUNK
    tokens, states, fixed, _ = wkv_specs(width, chunks, False)
    return pl.pallas_call(
        wkv_forward_body,
        grid=(chunks,),
        in_specs=[tokens] * 4 + fixed,
        out_specs=[tokens, tokens, states],
        out_shape=[
            jax.ShapeDtypeStruct((length, width), BF),
            jax.ShapeDtypeStruct((length, width), F32),
            jax.ShapeDtypeStruct((chunks, width, PAIR), BF),
        ],
        scratch_shapes=[pltpu.VMEM((width, PAIR), F32)],
        compiler_params=pltpu.CompilerParams(vmem_limit_bytes=40 * 2**20),
        name="wkv_forward",
    )(r, k, v, gate, *tables)


def wkv_backward(r, k, v, gate, wkv, d_mixed, states_kept, tables):
    length, width = r.shape
    chunks = length // CHUNK
    tokens, states, fixed, params = wkv_specs(width, chunks, True)
    return pl.pallas_call(
        wkv_backward_body,
        grid=(chunks,),
        in_specs=[tokens] * 6 + [states] + fixed,
        out_specs=[tokens] * 4 + [params],
        out_shape=[jax.ShapeDtypeStruct((length, width), BF)] * 4
        + [jax.ShapeDtypeStruct((8, width), F32)],
        scratch_shapes=[pltpu.VMEM((width, PAIR), F32)],
        compiler_params=pltpu.CompilerParams(vmem_limit_bytes=40 * 2**20),
        name="wkv_backward",
    )(r, k, v, gate, wkv, d_mixed, states_kept, *tables)


def wkv_tables(piece, log_decay, bonus, gain, bias):
    length, width = piece.shape[0], log_decay.shape[0]
    chunks = length // CHUNK
    by_chunk = piece.reshape(chunks, CHUNK)
    before = jnp.concatenate([jnp.full((1,), -1, piece.dtype), by_chunk[:-1, -1]])
    reaches = (by_chunk == before[:, None]).reshape(-1)
    last_same = (by_chunk == by_chunk[:, -1:]).reshape(-1)
    marks = jnp.stack([piece.astype(F32), reaches.astype(F32), last_same.astype(F32)], axis=1)
    rows = jnp.pad(marks, ((0, 0), (0, PAIR - 3)))
    columns = jnp.broadcast_to(piece.astype(F32)[None], (8, length))
    offset = jnp.arange(CHUNK).astype(F32)[:, None]
    grow = jnp.exp(offset * log_decay)
    shrink = jnp.exp(-(offset + 1.0) * log_decay)
    tail = jnp.exp((CHUNK - 1.0 - offset) * log_decay)
    zero = jnp.zeros_like(bonus)
    params = jnp.stack([bonus, gain, bias, jnp.exp(CHUNK * log_decay)] + [zero] * 4)
    return rows, columns, grow, shrink, tail, params


def layer_norm(values, norm_gain, norm_bias):
    mean_value = jnp.mean(values, axis=-1, keepdims=True)
    centred = values - mean_value
    spread = jnp.mean(centred * centred, axis=-1, keepdims=True)
    return centred * lax.rsqrt(spread + EPSILON) * norm_gain + norm_bias


def segment_of(lengths, positions):
    rank = jnp.arange(lengths.shape[0])
    starts = jnp.sum(jnp.where(rank[:, None] > rank[None, :], lengths[None, :], 0), axis=1)
    later_flags = (positions[:, None] >= starts[None, 1:]).astype(jnp.int32)
    first_flags = jnp.any(positions[:, None] == starts[None, :], axis=1)
    return (jnp.sum(later_flags, axis=1), first_flags)


def before(values, keep):
    return jnp.concatenate([jnp.zeros_like(values[:1]), values[:-1]], axis=0) * keep


def to_before(values, keep):
    kept = values * keep
    return jnp.concatenate([kept[1:], jnp.zeros_like(kept[:1])], axis=0)


def mix(values, previous, factor):
    return (values * factor + previous * (1.0 - factor)).astype(BF)


def project(rows_b, weight):
    return dot(rows_b, weight, NN)


def weight_grad(left_rows, right_rows):
    return dot(left_rows, right_rows, TN)


def input_grad(grad_rows, weight):
    return dot(grad_rows, weight, NT)


def shards(
    tokens, seq_lengths, out_grad, w_receptance, w_key, w_value, w_gate, w_output,
    ffn_key, ffn_receptance, ffn_value, vectors,
):
    seq = lax.axis_size("seq")
    here = lax.axis_index("seq")
    inputs_b, grad_b = tokens[0], out_grad[0]
    own_rows, width = inputs_b.shape
    length = own_rows * seq
    part = width // seq

    def own_columns(values):
        return lax.dynamic_slice_in_dim(values, here * part, part, 1)

    def whole(values):
        return gather_seq(values).reshape(length, width)

    positions = jnp.arange(length, dtype=jnp.int32)
    piece, first_flags = segment_of(seq_lengths[0], positions)
    keep = 1.0 - first_flags.astype(F32)[:, None]

    vec = gather_small(vectors[None]).transpose(1, 0, 2).reshape(vectors.shape[0], width).astype(F32)
    vec_own = own_columns(vec)
    tokens_all = whole(inputs_b)
    projections = jnp.stack([by_columns(w) for w in (w_receptance, w_key, w_value, w_gate)], axis=1)
    gathered = lax.all_gather(projections, "dp", axis=0)
    full_r, full_k, full_v, full_g = (
        gathered[:, :, i].transpose(1, 0, 2, 3).reshape(width, part) for i in range(4)
    )
    full_o = lax.all_gather(w_output, "dp", axis=0, tiled=True)
    grad_all = whole(grad_b)
    ffn_columns = jnp.concatenate([by_columns(ffn_key), by_columns(ffn_receptance)], axis=2)
    full_c = all_rows(ffn_columns)
    hidden_width = ffn_key.shape[1] // seq
    full_ck, full_cr = full_c[:, :hidden_width], full_c[:, hidden_width:]
    full_cv = lax.all_gather(ffn_value, "dp", axis=0, tiled=True)

    normed = layer_norm(tokens_all.astype(F32), vec[0], vec[1])
    previous = before(normed, keep)
    mix_r, mix_k, mix_v, mix_g = (mix(normed, previous, vec[i]) for i in (2, 3, 4, 5))
    recept = project(mix_r, full_r).astype(BF)
    keyed = project(mix_k, full_k).astype(BF)
    valued = project(mix_v, full_v).astype(BF)
    gate_pre = project(mix_g, full_g)
    log_decay = -jnp.exp(vec_own[6])
    tables = wkv_tables(piece, log_decay, vec_own[7], vec_own[8], vec_own[9])
    mixed, wkv, states = wkv_forward(recept, keyed, valued, gate_pre, tables)
    attn = project(mixed, full_o).astype(BF).reshape(seq, own_rows, width)
    inputs_f = inputs_b.astype(F32)
    after = inputs_f + scatter_seq(attn)

    normed_two, norm_two_pull = jax.vjp(layer_norm, after, vec[10], vec[11])
    normed_two = whole(normed_two.astype(BF)).astype(F32)
    previous_two = before(normed_two, keep)
    mix_k2, mix_r2 = mix(normed_two, previous_two, vec[12]), mix(normed_two, previous_two, vec[13])
    opened = jax.nn.sigmoid(project(mix_r2, full_cr))
    opened_all = gather_seq(opened.astype(BF))
    key_pre = project(mix_k2, full_ck)
    smooth = jax.nn.softplus(key_pre)
    hidden = (smooth * smooth).astype(BF)
    value_parts = project(hidden, full_cv).astype(BF).reshape(length, seq, part).transpose(1, 0, 2)
    value_pre = scatter_seq(value_parts)
    channel = trade_seq((opened * value_pre).astype(BF).reshape(seq, own_rows, part))
    out_rows = (after + channel.transpose(1, 0, 2).reshape(own_rows, width).astype(F32)).astype(BF)

    d_value = (
        (grad_all.reshape(length, seq, part).astype(F32) * opened_all.transpose(1, 0, 2).astype(F32))
        .astype(BF)
        .reshape(length, width)
    )
    d_recept_two = (
        own_columns(grad_all).astype(F32) * value_pre * opened * (1.0 - opened)
    ).astype(BF)
    d_hidden = input_grad(d_value, full_cv)
    d_key_two = (d_hidden * 2.0 * smooth * jax.nn.sigmoid(key_pre)).astype(BF)
    d_mix_k2 = input_grad(d_key_two, full_ck)
    d_mix_r2 = input_grad(d_recept_two, full_cr)
    step_two = normed_two - previous_two
    d_normed_two = (
        d_mix_k2 * vec[12]
        + d_mix_r2 * vec[13]
        + to_before(d_mix_k2 * (1.0 - vec[12]) + d_mix_r2 * (1.0 - vec[13]), keep)
    )
    d_mixes_two = [jnp.sum(d * step_two, axis=0) for d in (d_mix_k2, d_mix_r2)]
    d_normed_two = scatter_seq(d_normed_two.astype(BF).reshape(seq, own_rows, width))
    grad_cv = weight_grad(hidden, d_value)
    grad_ck = weight_grad(mix_k2, d_key_two)
    grad_cr = weight_grad(mix_r2, d_recept_two)
    d_after_norm, d_gain_two, d_bias_two = norm_two_pull(d_normed_two)
    d_after = grad_b.astype(F32) + d_after_norm

    d_attn = whole(d_after.astype(BF))
    d_mixed = input_grad(d_attn, full_o)
    grad_wo = weight_grad(mixed, d_attn)
    d_recept, d_keyed, d_valued, d_gate, sums = wkv_backward(
        recept, keyed, valued, gate_pre, wkv, d_mixed, states, tables
    )
    d_mix = [
        input_grad(d, w)
        for d, w in ((d_recept, full_r), (d_keyed, full_k), (d_valued, full_v), (d_gate, full_g))
    ]
    step = normed - previous
    d_normed = sum(d * vec[2 + i] for i, d in enumerate(d_mix)) + to_before(
        sum(d * (1.0 - vec[2 + i]) for i, d in enumerate(d_mix)), keep
    )
    d_mixes = [jnp.sum(d * step, axis=0) for d in d_mix]
    d_normed = scatter_seq(d_normed.astype(BF).reshape(seq, own_rows, width))
    grads_in = (
        weight_grad(mix_r, d_recept),
        weight_grad(mix_k, d_keyed),
        weight_grad(mix_v, d_valued),
        weight_grad(mix_g, d_gate),
    )
    _, norm_pull = jax.vjp(layer_norm, inputs_f, vec[0], vec[1])
    d_inputs, d_gain_one, d_bias_one = norm_pull(d_normed)
    tokens_grad = d_after + d_inputs

    own_sums = jnp.stack([sums[0] * log_decay, sums[1], sums[2], sums[3]])
    placed = lax.dynamic_update_slice(jnp.zeros((4, width), F32), own_sums, (0, here * part))
    vector_rows = jnp.concatenate(
        [
            jnp.stack([d_gain_one, d_bias_one] + d_mixes),
            placed,
            jnp.stack([d_gain_two, d_bias_two] + d_mixes_two),
        ]
    )
    rows = vector_rows.shape[0]
    sum_vec = scatter_small(vector_rows.reshape(rows, -1, vectors.shape[1]).transpose(1, 0, 2))

    def natural(grad):
        return lax.psum_scatter(grad.astype(BF), "dp", scatter_dimension=0, tiled=True).astype(F32)

    sum_cv = natural(grad_cv)
    sum_c = owners_rows(jnp.concatenate([grad_ck, grad_cr], axis=1))
    own = sum_c.reshape(sum_c.shape[0], seq, hidden_width + part)
    sum_ck = own[:, :, :hidden_width].reshape(ffn_key.shape)
    sum_cr = own[:, :, hidden_width:].reshape(ffn_receptance.shape)
    sum_o = natural(grad_wo)
    sum_in = owners_rows(jnp.concatenate(grads_in, axis=1)).reshape(-1, seq, 4, part)
    sum_r, sum_k, sum_v, sum_g = (sum_in[:, :, i].reshape(w_key.shape) for i in range(4))
    return (
        out_rows[None], tokens_grad[None], sum_r, sum_k, sum_v, sum_g, sum_o,
        sum_ck, sum_cr, sum_cv, sum_vec,
    )


def solution(mesh):
    tokens = P("dp", "seq", None)
    rows = P(("seq", "dp"), None)
    columns = P(None, ("seq", "dp"))
    return jax.shard_map(
        shards,
        mesh=mesh,
        in_specs=(tokens, P("dp", None), tokens) + (rows,) * 8 + (columns,),
        out_specs=(tokens, tokens) + (rows,) * 8 + (columns,),
        check_vma=False,
    )
```

time: 4210 us -> 1190 us (0.28)
  waiting for transfers between devices: 2780 us -> 298 us
  matrix products: 589 us -> 240 us
  local copies, waits for them, and re-layouts: 570 us -> 260 us
  starting transfers between devices: 6.35 us -> 93.5 us
  Pallas kernels: 0 us -> 60.2 us
  blocking collectives: 52.6 us -> 0 us
    reduce_scatter x8 -> x4, waiting for transfers between devices: 2370 us -> 0.05 us  [the longest x2 0.04 us: owners_rows(): lax.psum_scatter(parts, 'dp', scatter_dimension=0, tiled=True)]
    all_gather x10 -> x4, waiting for transfers between devices: 402 us -> 0.01 us  [the longest x1 0.01 us: shards(): gathered = lax.all_gather(projections, 'dp', axis=0)]
    dot_general x99 -> x24, matrix products: 589 us -> 240 us  [dot(): return lax.dot_general(left, right, dims, preferred_element_type=F32)]
    ppermute x4 -> x73, waiting for transfers between devices: 3.04 us -> 298 us  [swap(): return lax.ppermute(value, axis, [(i, i ^ distance) for i in range(size)])]
    dynamic_update_slice x48 -> x58, local copies, waits for them, and re-layouts: 360 us -> 71.1 us  [the longest x35 38.6 us: trade_seq(): result = lax.dynamic_update_slice_in_dim(result, piece, here ^ distance, 0)]
    ppermute x4 -> x73, starting transfers between devices: 5.59 us -> 92.9 us  [swap(): return lax.ppermute(value, axis, [(i, i ^ distance) for i in range(size)])]
    pallas_call x0 -> x2, Pallas kernels: none -> 60.2 us  [the longest x1 35.4 us: wkv_backward(): pl.pallas_call(wkv_backward_body, grid=(chunks,), in_specs=[tokens] * 6 +...]
    all_gather x2 -> x0, blocking collectives: 52.6 us -> none  [the longest x1 44.5 us: shards(): lax.all_gather(vectors, ('seq', 'dp'), axis=1, tiled=True)]
  transfers between devices with their start and end apart: 23 -> 81, of which waited for: 17 -> 37; matrix products, arithmetic and copies ran while one was open for 13% -> 50% of each run, Pallas kernels for 0% -> 5%
where the time goes in v2:
time: 1190 us; the launch traced here: 1180 us
  waiting for transfers between devices  298 us (25%)
  local copies, waits for them, and re-layouts  260 us (22%)
  matrix products  240 us (20%)
  other arithmetic  211 us (18%)
  starting transfers between devices  93.5 us (8%)
  Pallas kernels  60.2 us (5%)
  between operations  17.2 us (1%)
    ppermute x73, waiting for transfers between devices, swap(): return lax.ppermute(value, axis, [(i, i ^ distance) for i in range(size)])  298 us
    dot_general x24, matrix products, dot(): return lax.dot_general(left, right, dims, preferred_element_type=F32)  240 us
    ppermute x73, starting transfers between devices, swap(): return lax.ppermute(value, axis, [(i, i ^ distance) for i in range(size)])  92.9 us
    dynamic_update_slice x35, local copies, waits for them, and re-layouts, trade_seq(): result = lax.dynamic_update_slice_in_dim(result, piece, here ^ distance, 0)  38.6 us
    mul x2, other arithmetic, to_before(): kept = values * keep  36.3 us
    pallas_call x1, Pallas kernels, wkv_backward(): pl.pallas_call(wkv_backward_body, grid=(chunks,), in_specs=[tokens] * 6 +...  35.4 us
    unnamed x275, local copies, waits for them, and re-layouts  34 us
    dynamic_update_slice x23, local copies, waits for them, and re-layouts, put(): return lax.dynamic_update_slice(whole, piece[None], at)  32.5 us
  transfers between devices with their start and end apart: 81, of which 37 were waited for; matrix products, arithmetic and copies ran while one was open for 50% of the time, Pallas kernels for 5%

profile of v2, /device:TPU:0, one launch (start us, length us, event | category | flops | bytes accessed | tf_op | source)
XLA Modules:
  0.0 1180.0 jit_solution(6458802240745301856)
XLA Ops:
  55.0 23.2 %collective-permute-done.32 = bf16[1,64,512]{2,1,0:T(8,128)(2,1)S(1)} collective-permute-done((bf16[1,64,512]{2,1,0:T(8,128)(2,1)S(1)}, bf16[1,64,512]{2,1,0:T(8,128)(2,1)S(1)}, u32[]{:S(2)}, u32[]{:S(2)}) %collective-permute-start.32) | collective-permute-done | bytes 65568 | tf_op jit(solution)/shard_map/ppermute | solution.py:24
  83.1 5.3 collective-permute-done.34
  90.2 6.7 collective-permute-done.30
  141.2 4.6 multiply_reduce_fusion.6
  145.8 5.1 fusion.9
  150.9 18.3 %fusion.11 = (f32[1536,2048]{1,0:T(8,128)}, bf16[1536,2048]{1,0:T(8,128)(2,1)}, bf16[1536,2048]{1,0:T(8,128)(2,1)}, bf16[1536,2048]{1,0:T(8,128)(2,1)}, bf16[1536,2048]{1,0:T(8,128)(2,1)}) fusion(f32[1535,2048]{1,0:T(8,128)S(1)} %bitcast.429, f32[1536]{0:T(1024)S(1)} %convert_subtract_fusion.1, f32[2048]{0:T(1024)S(1)} %add.353, f32[2048]{0:T(1024)S(1)} %mul.446, ...), kind=kLoop, calls=%fused_computation.45 | loop fusion | flops 72351744 | bytes 56715264 | tf_op jit(solution)/shard_map/sub | solution.py:482
  169.2 4.4 slice_bitcast_fusion
  179.5 5.1 fusion.58.g_ref
  195.2 24.8 %wkv_forward.1 = (bf16[1536,512]{1,0:T(8,128)(2,1)S(1)}, f32[1536,512]{1,0:T(8,128)S(1)}, bf16[12,512,128]{2,1,0:T(8,128)(2,1)S(1)}) custom-call(bf16[1536,512]{1,0:T(8,128)(2,1)S(1)} %convolution_convert_fusion.12.r_ref, bf16[1536,512]{1,0:T(8,128)(2,1)S(1)} %convolution_convert_fusion.11.k_ref, bf16[1536,512]{1,0:T(8,128)(2,1)S(1)} %convolution_convert_fusion.10.v_ref, ...), custom_call_target="tpu_custom_call" | custom-call | tf_op jit(solution)/shard_map/wkv_forward/pallas_call | solution.py:289
  224.6 5.8 convolution_convert_fusion.3
  235.8 12.8 %collective-permute-done.21 = bf16[192,2048]{1,0:T(8,128)(2,1)S(1)} collective-permute-done((bf16[192,2048]{1,0:T(8,128)(2,1)}, bf16[192,2048]{1,0:T(8,128)(2,1)S(1)}, u32[]{:S(2)}, u32[]{:S(2)}) %collective-permute-start.21) | collective-permute-done | bytes 786464 | tf_op jit(solution)/shard_map/ppermute | solution.py:24
  260.4 19.8 %collective-permute-done.22 = bf16[384,2048]{1,0:T(8,128)(2,1)} collective-permute-done((bf16[384,2048]{1,0:T(8,128)(2,1)}, bf16[384,2048]{1,0:T(8,128)(2,1)}, u32[]{:S(2)}, u32[]{:S(2)}) %collective-permute-start.22) | collective-permute-done | bytes 1572896 | tf_op jit(solution)/shard_map/ppermute | solution.py:24
  280.1 4.5 fusion.53
  295.3 8.3 copy.137
  303.6 25.0 %collective-permute-done.25 = bf16[384,2048]{1,0:T(8,128)(2,1)} collective-permute-done((bf16[384,2048]{1,0:T(8,128)(2,1)}, bf16[384,2048]{1,0:T(8,128)(2,1)}, u32[]{:S(2)}, u32[]{:S(2)}) %collective-permute-start.25) | collective-permute-done | bytes 1572896 | tf_op jit(solution)/shard_map/ppermute | solution.py:24
  339.5 26.5 %collective-permute-done.27 = bf16[192,2048]{1,0:T(8,128)(2,1)S(1)} collective-permute-done((bf16[192,2048]{1,0:T(8,128)(2,1)S(1)}, bf16[192,2048]{1,0:T(8,128)(2,1)S(1)}, u32[]{:S(2)}, u32[]{:S(2)}) %collective-permute-start.27) | collective-permute-done | bytes 786464 | tf_op jit(solution)/shard_map/ppermute | solution.py:24
  372.1 11.9 %add_convert_fusion.2 = (bf16[1536,2048]{1,0:T(8,128)(2,1)S(1)}, bf16[1536,2048]{1,0:T(8,128)(2,1)}) fusion(f32[1535,2048]{1,0:T(8,128)S(1)} %bitcast.427, bf16[4,384,2048]{2,1,0:T(8,128)(2,1)} %bitcast_dynamic-update-slice_fusion.14, f32[2048]{0:T(1024)S(1)} %mul.502, f32[2048]{0:T(1024)S(1)} %mul.499, f32[1536]{0:T(1024)S(1)} %convert_subtract_fusion.1, ...), kind=kLoop, calls=%fused_computation.27 | loop fusion | flops 31457280 | bytes 31488000 | tf_op jit(solution)/shard_map/convert_element_type | solution.py:366
  386.8 17.2 %fusion.14 = f32[1536,1792]{1,0:T(8,128)} fusion(bf16[1536,2048]{1,0:T(8,128)(2,1)S(1)} %get-tuple-element.74, bf16[2048,2304]{1,0:T(8,128)(2,1)} %bitcast.448), kind=kOutput, calls=%fused_computation.48 | convolution fusion | flops 11274289152 | bytes 24641536 | tf_op jit(solution)/shard_map/dot_general | solution.py:135
  404.0 22.0 %convolution_convert_fusion.2 = bf16[1536,2048]{1,0:T(8,128)(2,1)} fusion(bf16[1792,2048]{1,0:T(8,128)(2,1)} %all-gather.9.cloned.1.call-done, f32[1536,1792]{1,0:T(8,128)} %fusion.14), kind=kOutput, calls=%fused_computation.43 | convolution fusion | flops 11299454976 | bytes 24641536 | tf_op jit(solution)/shard_map/dot_general | solution.py:135
  426.0 8.7 copy.138
  434.6 5.6 constant_dynamic-slice_fusion.13
  468.2 25.8 %collective-permute-done.37 = bf16[768,512]{1,0:T(8,128)(2,1)} collective-permute-done((bf16[768,512]{1,0:T(8,128)(2,1)}, bf16[768,512]{1,0:T(8,128)(2,1)}, u32[]{:S(2)}, u32[]{:S(2)}) %collective-permute-start.37) | collective-permute-done | bytes 786464 | tf_op jit(solution)/shard_map/ppermute | solution.py:24
  512.0 9.2 collective-permute-done.38
  521.2 12.4 %multiply_convert_fusion.2 = (bf16[1536,512]{1,0:T(8,128)(2,1)}, bf16[1536,512]{1,0:T(8,128)(2,1)}, bf16[1536,512]{1,0:T(8,128)(2,1)}) fusion(bf16[1536,512]{1,0:T(8,128)(2,1)} %collective-permute-done.38, bf16[1536,512]{1,0:T(8,128)(2,1)} %collective-permute-done.36, bf16[1536,1,512]{2,0,1:T(8,128)(2,1)} %copy.193, bf16[1536,2048]{1,0:T(8,128)(2,1)} %bitcast.80, ...), kind=kOutput, calls=%fused_computation.81 | convolution fusion | flops 3234594816 | bytes 19398660 | tf_op jit(solution)/shard_map/dot_general | solution.py:135
  537.2 15.2 %reshape.514 = f32[1536,4,512]{2,1,0:T(4,128)} reshape(bf16[4,384,2048]{2,1,0:T(8,128)(2,1)} %bitcast_dynamic-update-slice_fusion.12) | data formatting | bytes 18874368 | tf_op jit(solution)/shard_map/convert_element_type | solution.py:447
  552.4 14.6 %copy.166 = f32[1536,4,512]{0,2,1:T(8,128)} copy(f32[1536,4,512]{2,1,0:T(4,128)} %reshape.514) | data formatting | bytes 25165824 | tf_op jit(solution)/shard_map/convert_element_type | solution.py:447
  568.8 8.1 convolution_convert_fusion.4
  597.3 11.2 fusion.6
  608.5 25.8 %multiply_convert_fusion = bf16[1536,1792]{1,0:T(8,128)(2,1)} fusion(f32[1536,1792]{1,0:T(8,128)} %fusion.14, bf16[1536,2048]{0,1:T(8,128)(2,1)} %bitcast.465, bf16[1792,2048]{1,0:T(8,128)(2,1)} %all-gather.9.cloned.1.call-done), kind=kOutput, calls=%fused_computation.36 | convolution fusion | flops 11310071808 | bytes 30146560 | tf_op jit(solution)/shard_map/dot_general | solution.py:135
  634.3 16.1 %convolution_convert_fusion.1 = bf16[2048,1792]{1,0:T(8,128)(2,1)S(1)} fusion(bf16[1536,2048]{1,0:T(8,128)(2,1)} %copy-done.38, bf16[1536,1792]{1,0:T(8,128)(2,1)} %multiply_convert_fusion), kind=kOutput, calls=%fused_computation.42 | convolution fusion | flops 11277959168 | bytes 19136512 | tf_op jit(solution)/shard_map/dot_general | solution.py:135
  654.3 8.3 copy.168
  664.0 5.2 fusion.32
  669.2 22.2 %fusion.12 = f32[1536,2048]{1,0:T(8,128)} fusion(bf16[1536,1792]{1,0:T(8,128)(2,1)} %multiply_convert_fusion, bf16[2048,2304]{1,0:T(8,128)(2,1)} %bitcast.451), kind=kOutput, calls=%fused_computation.46 | convolution fusion | flops 11274289152 | bytes 25427968 | tf_op jit(solution)/shard_map/dot_general | solution.py:135
  691.5 12.2 %fusion.5 = f32[1535,2048]{1,0:T(8,128)} fusion(f32[1536,2048]{1,0:T(8,128)S(1)} %fusion.32, f32[1536,2048]{1,0:T(8,128)} %fusion.12, f32[1535]{0:T(1024)S(1)} %slice.445, f32[2048]{0:T(1024)S(1)} %copy-done.76, f32[2048]{0:T(1024)S(1)} %copy-done.78), kind=kLoop, calls=%fused_computation.11 | loop fusion | flops 12574720 | bytes 37746684 | tf_op jit(solution)/shard_map/mul | solution.py:361
  703.6 21.7 %multiply_reduce_fusion = (f32[2048]{0:T(1024)}, f32[2048]{0:T(1024)}, bf16[1536,2048]{1,0:T(8,128)(2,1)S(1)}) fusion(f32[1536,2048]{1,0:T(8,128)} %copy-done.28, f32[1535,2048]{1,0:T(8,128)} %bitcast.428, bf16[4,384,2048]{2,1,0:T(8,128)(2,1)} %bitcast_dynamic-update-slice_fusion.14, f32[1536]{0:T(1024)S(1)} %copy-done.64, f32[1536,2048]{1,0:T(8,128)} %fusion.12, ...), kind=kLoop, calls=%fused_computation.19 | loop fusion | flops 37744640 | bytes 62937088 | tf_op jit(solution)/shard_map/reduce_sum | solution.py:464
  729.1 17.9 %collective-permute-done.50 = bf16[192,2048]{1,0:T(8,128)(2,1)S(1)} collective-permute-done((bf16[192,2048]{1,0:T(8,128)(2,1)S(1)}, bf16[192,2048]{1,0:T(8,128)(2,1)S(1)}, u32[]{:S(2)}, u32[]{:S(2)}) %collective-permute-start.50) | collective-permute-done | bytes 786464 | tf_op jit(solution)/shard_map/ppermute | solution.py:24
  759.3 6.6 dynamic_update_slice.236
  765.9 8.5 collective-permute-done.39
  776.0 6.6 dynamic_update_slice.237
  784.2 6.8 dynamic_update_slice.238
  791.7 6.6 dynamic_update_slice.239
  800.6 4.6 multiply_reduce_fusion.7
  805.2 5.0 fusion.52
  816.4 17.3 %collective-permute-done.54 = bf16[384,2048]{1,0:T(8,128)(2,1)S(1)} collective-permute-done((bf16[384,2048]{1,0:T(8,128)(2,1)S(1)}, bf16[384,2048]{1,0:T(8,128)(2,1)S(1)}, u32[]{:S(2)}, u32[]{:S(2)}) %collective-permute-start.54) | collective-permute-done | bytes 1572896 | tf_op jit(solution)/shard_map/ppermute | solution.py:24
  837.5 8.4 collective-permute-done.56
  850.5 4.6 convolution_convert_fusion.5
  855.2 29.4 %convolution_convert_fusion = bf16[1792,2048]{1,0:T(8,128)(2,1)} fusion(bf16[1536,2048]{0,1:T(8,128)(2,1)} %bitcast.466, f32[1536,1792]{1,0:T(8,128)} %fusion.14), kind=kOutput, calls=%fused_computation.41 | convolution fusion | flops 11299979264 | bytes 24641536 | tf_op jit(solution)/shard_map/dot_general | solution.py:135
  884.8 8.7 fusion.59.d_mixed_ref
  893.6 35.4 %wkv_backward.1 = (bf16[1536,512]{1,0:T(8,128)(2,1)S(1)}, bf16[1536,512]{1,0:T(8,128)(2,1)S(1)}, bf16[1536,512]{1,0:T(8,128)(2,1)S(1)}, bf16[1536,512]{1,0:T(8,128)(2,1)S(1)}, f32[8,512]{1,0:T(8,128)S(1)}) custom-call(bf16[1536,512]{1,0:T(8,128)(2,1)S(1)} %copy-done.5, bf16[1536,512]{1,0:T(8,128)(2,1)S(1)} %copy-done.3, bf16[1536,512]{1,0:T(8,128)(2,1)S(1)} %copy-done.1, ...), custom_call_target="tpu_custom_call" | custom-call | tf_op jit(solution)/shard_map/wkv_backward/pallas_call | solution.py:309
  929.0 7.9 convolution_convert_fusion.9
  952.1 8.6 copy.167
  960.7 6.4 fusion.60
  967.1 6.9 fusion.61
  975.4 8.2 fusion.62
  983.7 6.5 fusion.63
  990.2 24.1 %fusion.1 = f32[1535,2048]{1,0:T(8,128)} fusion(f32[1536,2048]{1,0:T(8,128)} %fusion.63, f32[1536,2048]{1,0:T(8,128)} %fusion.62, f32[1536,2048]{1,0:T(8,128)} %fusion.61, f32[1536,2048]{1,0:T(8,128)} %fusion.60, f32[2048]{0:T(1024)S(1)} %copy-done.86, f32[2048]{0:T(1024)S(1)} %copy-done.84, f32[2048]{0:T(1024)S(1)} %copy-done.82, f32[2048]{0:T(1024)S(1)} %copy-done.80, ...), kind=kLoop, calls=%fused_computation.3 | loop fusion | flops 25149440 | bytes 62912508 | tf_op jit(solution)/shard_map/mul | solution.py:361
  1014.4 26.6 %multiply_reduce_fusion.2 = (f32[2048]{0:T(1024)S(1)}, f32[2048]{0:T(1024)S(1)}, f32[2048]{0:T(1024)S(1)}, f32[2048]{0:T(1024)S(1)}, bf16[1536,2048]{1,0:T(8,128)(2,1)S(1)}) fusion(f32[1536,2048]{1,0:T(8,128)} %fusion.63, f32[1536,2048]{1,0:T(8,128)} %get-tuple-element.69, f32[1536,2048]{1,0:T(8,128)} %fusion.62, f32[1536,2048]{1,0:T(8,128)} %fusion.61, ...), kind=kLoop, calls=%fused_computation.21 | loop fusion | flops 53469184 | bytes 81846272 | tf_op jit(solution)/shard_map/reduce_sum | solution.py:486
  1043.5 11.1 collective-permute-done.58
  1060.9 16.5 %collective-permute-done.59 = bf16[384,2048]{1,0:T(8,128)(2,1)} collective-permute-done((bf16[384,2048]{1,0:T(8,128)(2,1)}, bf16[384,2048]{1,0:T(8,128)(2,1)}, u32[]{:S(2)}, u32[]{:S(2)}) %collective-permute-start.59) | collective-permute-done | bytes 1572896 | tf_op jit(solution)/shard_map/ppermute | solution.py:24
  1097.4 5.4 fusion.50
  1102.8 4.4 collective-permute-start.71
  1113.5 4.6 add_bitcast_fusion
  1126.4 12.2 %collective-permute-done.66 = bf16[1,64,2304]{2,1,0:T(8,128)(2,1)S(1)} collective-permute-done((bf16[1,64,2304]{2,1,0:T(8,128)(2,1)S(1)}, bf16[1,64,2304]{2,1,0:T(8,128)(2,1)S(1)}, u32[]{:S(2)}, u32[]{:S(2)}) %collective-permute-start.66) | collective-permute-done | bytes 294944 | tf_op jit(solution)/shard_map/ppermute | solution.py:24
  1155.5 5.5 collective-permute-done.63
  (683 shorter events, 367.9 us)
Async XLA Ops:
  7.2 162.0 %all-gather.11.cloned.1.call-start = ((), (), s32[]{:S(2)}) async-start(), calls=%async_computation.10 | async-start | bytes 9437184 | tf_op jit(solution)/shard_map/all_gather | solution.py:406
  11.3 10.1 collective-permute-start.18
  15.9 9.4 collective-permute-start.20
  16.0 11.7 collective-permute-start.15
  18.0 10.7 collective-permute-start.16
  21.5 10.0 collective-permute-start.17
  22.5 10.5 collective-permute-start.12
  39.4 185.2 %all-gather.7.cloned.1.call-start = ((), (), s32[]{:S(2)}) async-start(), calls=%async_computation.4 | async-start | bytes 2359296 | tf_op jit(solution)/shard_map/all_gather | solution.py:410
  39.5 80.7 %collective-permute-start = (bf16[384,2048]{1,0:T(8,128)(2,1)S(1)}, bf16[384,2048]{1,0:T(8,128)(2,1)}, u32[]{:S(2)}, u32[]{:S(2)}) collective-permute-start(bf16[384,2048]{1,0:T(8,128)(2,1)S(1)} %bitcast.430), channel_id=1, source_target_pairs={{0,8},{8,0},{16,24},{24,16},{1,9},{9,1},{17,25},{25,17},{2,10},{10... | collective-permute-start | bytes 4718600 | tf_op jit(solution)/shard_map/ppermute | solution.py:24
  40.4 82.8 %collective-permute-start.1 = (bf16[384,2048]{1,0:T(8,128)(2,1)S(1)}, bf16[384,2048]{1,0:T(8,128)(2,1)}, u32[]{:S(2)}, u32[]{:S(2)}) collective-permute-start(bf16[384,2048]{1,0:T(8,128)(2,1)S(1)} %bitcast.431), channel_id=1, source_target_pairs={{0,16},{8,24},{16,0},{24,8},{1,17},{9,25},{17,1},{25,9},{2,18},{10... | collective-permute-start | bytes 4718600 | tf_op jit(solution)/shard_map/ppermute | solution.py:24
  40.4 58.1 %collective-permute-start.4 = (bf16[1,14,64]{2,1,0:T(8,128)(2,1)}, bf16[1,14,64]{2,1,0:T(8,128)(2,1)S(1)}, u32[]{:S(2)}, u32[]{:S(2)}) collective-permute-start(bf16[1,14,64]{2,1,0:T(8,128)(2,1)} %bitcast.6), channel_id=1, source_target_pairs={{0,1},{1,0},{2,3},{3,2},{4,5},{5,4},{6,7},{7,6},{8,9},{9,8},{10,11... | collective-permute-start | bytes 5384 | tf_op jit(solution)/shard_map/ppermute | solution.py:24
  46.1 43.1 %collective-permute-start.29 = (bf16[1,64,1792]{2,1,0:T(8,128)(2,1)}, bf16[1,64,1792]{2,1,0:T(8,128)(2,1)S(1)}, u32[]{:S(2)}, u32[]{:S(2)}) collective-permute-start(bf16[1,64,1792]{2,1,0:T(8,128)(2,1)} %bitcast.409), channel_id=1, source_target_pairs={{0,8},{8,0},{16,24},{24,16},{1,9},{9,1},{17,25},{25,17},{2,10},{10... | collective-permute-start | bytes 688136 | tf_op jit(solution)/shard_map/ppermute | solution.py:24
  48.6 29.7 %collective-permute-start.32 = (bf16[1,64,512]{2,1,0:T(8,128)(2,1)S(1)}, bf16[1,64,512]{2,1,0:T(8,128)(2,1)S(1)}, u32[]{:S(2)}, u32[]{:S(2)}) collective-permute-start(bf16[1,64,512]{2,1,0:T(8,128)(2,1)S(1)} %bitcast.526), channel_id=1, source_target_pairs={{0,8},{8,0},{16,24},{24,16},{1,9},{9,1},{17,25},{25,17},{2,10},{10... | collective-permute-start | bytes 196616 | tf_op jit(solution)/shard_map/ppermute | solution.py:24
  49.0 246.3 %all-gather.13.cloned.1.call-start = ((), (), s32[]{:S(2)}) async-start(), calls=%async_computation.11 | async-start | bytes 10616832 | tf_op jit(solution)/shard_map/all_gather | solution.py:110
  88.5 8.5 collective-permute-start.30
  98.1 305.8 %all-gather.9.cloned.1.call-start = ((), (), s32[]{:S(2)}) async-start(), calls=%async_computation.5 | async-start | bytes 8257536 | tf_op jit(solution)/shard_map/all_gather | solution.py:416
  121.7 12.1 %collective-permute-start.2 = (bf16[192,2048]{1,0:T(8,128)(2,1)S(1)}, bf16[192,2048]{1,0:T(8,128)(2,1)S(1)}, u32[]{:S(2)}, u32[]{:S(2)}) collective-permute-start(bf16[192,2048]{1,0:T(8,128)(2,1)S(1)} %slice.409), channel_id=1, source_target_pairs={{0,16},{8,24},{16,0},{24,8},{1,17},{9,25},{17,1},{25,9},{2,18},{10... | collective-permute-start | bytes 2359304 | tf_op jit(solution)/shard_map/ppermute | solution.py:24
  124.4 12.1 %collective-permute-start.3 = (bf16[192,2048]{1,0:T(8,128)(2,1)S(1)}, bf16[192,2048]{1,0:T(8,128)(2,1)S(1)}, u32[]{:S(2)}, u32[]{:S(2)}) collective-permute-start(bf16[192,2048]{1,0:T(8,128)(2,1)S(1)} %slice.410), channel_id=1, source_target_pairs={{0,8},{8,0},{16,24},{24,16},{1,9},{9,1},{17,25},{25,17},{2,10},{10... | collective-permute-start | bytes 2359304 | tf_op jit(solution)/shard_map/ppermute | solution.py:24
  233.7 14.9 %collective-permute-start.21 = (bf16[192,2048]{1,0:T(8,128)(2,1)}, bf16[192,2048]{1,0:T(8,128)(2,1)S(1)}, u32[]{:S(2)}, u32[]{:S(2)}) collective-permute-start(bf16[192,2048]{1,0:T(8,128)(2,1)} %get-tuple-element.99), channel_id=1, source_target_pairs={{0,16},{8,24},{16,0},{24,8},{1,17},{9,25},{17,1},{25,9},{2,18},{10... | collective-permute-start | bytes 2359304 | tf_op jit(solution)/shard_map/ppermute | solution.py:24
  234.3 16.6 %collective-permute-start.23 = (bf16[192,2048]{1,0:T(8,128)(2,1)S(1)}, bf16[192,2048]{1,0:T(8,128)(2,1)}, u32[]{:S(2)}, u32[]{:S(2)}) collective-permute-start(bf16[192,2048]{1,0:T(8,128)(2,1)S(1)} %get-tuple-element.101), channel_id=1, source_target_pairs={{0,8},{8,0},{16,24},{24,16},{1,9},{9,1},{17,25},{25,17},{2,10},{10... | collective-permute-start | bytes 2359304 | tf_op jit(solution)/shard_map/ppermute | solution.py:24
  235.8 873.3 %reduce-scatter.9.cloned.1.call-start = ((), (), s32[]{:S(2)}) async-start(), calls=%async_computation.8 | async-start | bytes 10616832 | tf_op jit(solution)/shard_map/reduce_scatter | solution.py:118
  254.6 25.5 %collective-permute-start.22 = (bf16[384,2048]{1,0:T(8,128)(2,1)}, bf16[384,2048]{1,0:T(8,128)(2,1)}, u32[]{:S(2)}, u32[]{:S(2)}) collective-permute-start(bf16[384,2048]{1,0:T(8,128)(2,1)} %pad_maximum_fusion.2), channel_id=1, source_target_pairs={{0,8},{8,0},{16,24},{24,16},{1,9},{9,1},{17,25},{25,17},{2,10},{10... | collective-permute-start | bytes 4718600 | tf_op jit(solution)/shard_map/ppermute | solution.py:24
  258.5 21.6 %collective-permute-start.24 = (bf16[384,2048]{1,0:T(8,128)(2,1)}, bf16[384,2048]{1,0:T(8,128)(2,1)}, u32[]{:S(2)}, u32[]{:S(2)}) collective-permute-start(bf16[384,2048]{1,0:T(8,128)(2,1)} %pad_maximum_fusion.3), channel_id=1, source_target_pairs={{0,16},{8,24},{16,0},{24,8},{1,17},{9,25},{17,1},{25,9},{2,18},{10... | collective-permute-start | bytes 4718600 | tf_op jit(solution)/shard_map/ppermute | solution.py:24
  290.9 37.6 %collective-permute-start.25 = (bf16[384,2048]{1,0:T(8,128)(2,1)}, bf16[384,2048]{1,0:T(8,128)(2,1)}, u32[]{:S(2)}, u32[]{:S(2)}) collective-permute-start(bf16[384,2048]{1,0:T(8,128)(2,1)} %get-tuple-element.62), channel_id=1, source_target_pairs={{0,8},{8,0},{16,24},{24,16},{1,9},{9,1},{17,25},{25,17},{2,10},{10... | collective-permute-start | bytes 4718600 | tf_op jit(solution)/shard_map/ppermute | solution.py:24
  292.3 38.8 %collective-permute-start.26 = (bf16[384,2048]{1,0:T(8,128)(2,1)}, bf16[384,2048]{1,0:T(8,128)(2,1)}, u32[]{:S(2)}, u32[]{:S(2)}) collective-permute-start(bf16[384,2048]{1,0:T(8,128)(2,1)} %get-tuple-element.62), channel_id=1, source_target_pairs={{0,16},{8,24},{16,0},{24,8},{1,17},{9,25},{17,1},{25,9},{2,18},{10... | collective-permute-start | bytes 4718600 | tf_op jit(solution)/shard_map/ppermute | solution.py:24
  293.8 157.9 %collective-permute-start.42 = (bf16[384,2048]{1,0:T(8,128)(2,1)S(1)}, bf16[384,2048]{1,0:T(8,128)(2,1)}, u32[]{:S(2)}, u32[]{:S(2)}) collective-permute-start(bf16[384,2048]{1,0:T(8,128)(2,1)S(1)} %bitcast.443), channel_id=1, source_target_pairs={{0,8},{8,0},{16,24},{24,16},{1,9},{9,1},{17,25},{25,17},{2,10},{10... | collective-permute-start | bytes 4718600 | tf_op jit(solution)/shard_map/ppermute | solution.py:24
  294.3 160.0 %collective-permute-start.43 = (bf16[384,2048]{1,0:T(8,128)(2,1)S(1)}, bf16[384,2048]{1,0:T(8,128)(2,1)}, u32[]{:S(2)}, u32[]{:S(2)}) collective-permute-start(bf16[384,2048]{1,0:T(8,128)(2,1)S(1)} %bitcast.444), channel_id=1, source_target_pairs={{0,16},{8,24},{16,0},{24,8},{1,17},{9,25},{17,1},{25,9},{2,18},{10... | collective-permute-start | bytes 4718600 | tf_op jit(solution)/shard_map/ppermute | solution.py:24
  329.8 36.2 %collective-permute-start.27 = (bf16[192,2048]{1,0:T(8,128)(2,1)S(1)}, bf16[192,2048]{1,0:T(8,128)(2,1)S(1)}, u32[]{:S(2)}, u32[]{:S(2)}) collective-permute-start(bf16[192,2048]{1,0:T(8,128)(2,1)S(1)} %slice.426), channel_id=1, source_target_pairs={{0,16},{8,24},{16,0},{24,8},{1,17},{9,25},{17,1},{25,9},{2,18},{10... | collective-permute-start | bytes 2359304 | tf_op jit(solution)/shard_map/ppermute | solution.py:24
  332.3 34.5 %collective-permute-start.28 = (bf16[192,2048]{1,0:T(8,128)(2,1)S(1)}, bf16[192,2048]{1,0:T(8,128)(2,1)S(1)}, u32[]{:S(2)}, u32[]{:S(2)}) collective-permute-start(bf16[192,2048]{1,0:T(8,128)(2,1)S(1)} %slice.427), channel_id=1, source_target_pairs={{0,8},{8,0},{16,24},{24,16},{1,9},{9,1},{17,25},{25,17},{2,10},{10... | collective-permute-start | bytes 2359304 | tf_op jit(solution)/shard_map/ppermute | solution.py:24
  445.5 18.6 %collective-permute-start.35 = (bf16[768,512]{1,0:T(8,128)(2,1)}, bf16[768,512]{1,0:T(8,128)(2,1)}, u32[]{:S(2)}, u32[]{:S(2)}) collective-permute-start(bf16[768,512]{1,0:T(8,128)(2,1)} %get-tuple-element.115), channel_id=1, source_target_pairs={{0,16},{8,24},{16,0},{24,8},{1,17},{9,25},{17,1},{25,9},{2,18},{10... | collective-permute-start | bytes 2359304 | tf_op jit(solution)/shard_map/ppermute | solution.py:24
  453.8 50.1 %collective-permute-start.44 = (bf16[192,2048]{1,0:T(8,128)(2,1)}, bf16[192,2048]{1,0:T(8,128)(2,1)S(1)}, u32[]{:S(2)}, u32[]{:S(2)}) collective-permute-start(bf16[192,2048]{1,0:T(8,128)(2,1)} %slice.439), channel_id=1, source_target_pairs={{0,16},{8,24},{16,0},{24,8},{1,17},{9,25},{17,1},{25,9},{2,18},{10... | collective-permute-start | bytes 2359304 | tf_op jit(solution)/shard_map/ppermute | solution.py:24
  456.4 48.4 %collective-permute-start.45 = (bf16[192,2048]{1,0:T(8,128)(2,1)}, bf16[192,2048]{1,0:T(8,128)(2,1)}, u32[]{:S(2)}, u32[]{:S(2)}) collective-permute-start(bf16[192,2048]{1,0:T(8,128)(2,1)} %slice.440), channel_id=1, source_target_pairs={{0,8},{8,0},{16,24},{24,16},{1,9},{9,1},{17,25},{25,17},{2,10},{10... | collective-permute-start | bytes 2359304 | tf_op jit(solution)/shard_map/ppermute | solution.py:24
  460.3 33.8 %collective-permute-start.37 = (bf16[768,512]{1,0:T(8,128)(2,1)}, bf16[768,512]{1,0:T(8,128)(2,1)}, u32[]{:S(2)}, u32[]{:S(2)}) collective-permute-start(bf16[768,512]{1,0:T(8,128)(2,1)} %get-tuple-element.116), channel_id=1, source_target_pairs={{0,8},{8,0},{16,24},{24,16},{1,9},{9,1},{17,25},{25,17},{2,10},{10... | collective-permute-start | bytes 2359304 | tf_op jit(solution)/shard_map/ppermute | solution.py:24
  467.0 45.0 %collective-permute-start.36 = (bf16[1536,512]{1,0:T(8,128)(2,1)}, bf16[1536,512]{1,0:T(8,128)(2,1)}, u32[]{:S(2)}, u32[]{:S(2)}) collective-permute-start(bf16[1536,512]{1,0:T(8,128)(2,1)} %pad_maximum_fusion.4), channel_id=1, source_target_pairs={{0,8},{8,0},{16,24},{24,16},{1,9},{9,1},{17,25},{25,17},{2,10},{10... | collective-permute-start | bytes 4718600 | tf_op jit(solution)/shard_map/ppermute | solution.py:24
  496.6 24.5 %collective-permute-start.38 = (bf16[1536,512]{1,0:T(8,128)(2,1)}, bf16[1536,512]{1,0:T(8,128)(2,1)}, u32[]{:S(2)}, u32[]{:S(2)}) collective-permute-start(bf16[1536,512]{1,0:T(8,128)(2,1)} %pad_maximum_fusion.5), channel_id=1, source_target_pairs={{0,16},{8,24},{16,0},{24,8},{1,17},{9,25},{17,1},{25,9},{2,18},{10... | collective-permute-start | bytes 4718600 | tf_op jit(solution)/shard_map/ppermute | solution.py:24
  533.6 43.3 %collective-permute-start.46 = (bf16[1536,512]{1,0:T(8,128)(2,1)}, bf16[1536,512]{1,0:T(8,128)(2,1)}, u32[]{:S(2)}, u32[]{:S(2)}) collective-permute-start(bf16[1536,512]{1,0:T(8,128)(2,1)} %get-tuple-element.105), channel_id=1, source_target_pairs={{0,8},{8,0},{16,24},{24,16},{1,9},{9,1},{17,25},{25,17},{2,10},{10... | collective-permute-start | bytes 4718600 | tf_op jit(solution)/shard_map/ppermute | solution.py:24
  535.7 43.8 %collective-permute-start.47 = (bf16[1536,512]{1,0:T(8,128)(2,1)}, bf16[1536,512]{1,0:T(8,128)(2,1)}, u32[]{:S(2)}, u32[]{:S(2)}) collective-permute-start(bf16[1536,512]{1,0:T(8,128)(2,1)} %get-tuple-element.105), channel_id=1, source_target_pairs={{0,16},{8,24},{16,0},{24,8},{1,17},{9,25},{17,1},{25,9},{2,18},{10... | collective-permute-start | bytes 4718600 | tf_op jit(solution)/shard_map/ppermute | solution.py:24
  579.0 14.7 %collective-permute-start.48 = (bf16[768,512]{1,0:T(8,128)(2,1)}, bf16[768,512]{1,0:T(8,128)(2,1)S(1)}, u32[]{:S(2)}, u32[]{:S(2)}) collective-permute-start(bf16[768,512]{1,0:T(8,128)(2,1)} %slice.441), channel_id=1, source_target_pairs={{0,16},{8,24},{16,0},{24,8},{1,17},{9,25},{17,1},{25,9},{2,18},{10... | collective-permute-start | bytes 2359304 | tf_op jit(solution)/shard_map/ppermute | solution.py:24
  581.6 12.3 %collective-permute-start.49 = (bf16[768,512]{1,0:T(8,128)(2,1)}, bf16[768,512]{1,0:T(8,128)(2,1)}, u32[]{:S(2)}, u32[]{:S(2)}) collective-permute-start(bf16[768,512]{1,0:T(8,128)(2,1)} %slice.442), channel_id=1, source_target_pairs={{0,8},{8,0},{16,24},{24,16},{1,9},{9,1},{17,25},{25,17},{2,10},{10... | collective-permute-start | bytes 2359304 | tf_op jit(solution)/shard_map/ppermute | solution.py:24
  662.6 456.1 %reduce-scatter.7.cloned.1.call-start = ((), (), s32[]{:S(2)}) async-start(), calls=%async_computation.7 | async-start | bytes 2359296 | tf_op jit(solution)/shard_map/reduce_scatter | solution.py:511
  725.6 21.4 %collective-permute-start.50 = (bf16[192,2048]{1,0:T(8,128)(2,1)S(1)}, bf16[192,2048]{1,0:T(8,128)(2,1)S(1)}, u32[]{:S(2)}, u32[]{:S(2)}) collective-permute-start(bf16[192,2048]{1,0:T(8,128)(2,1)S(1)} %get-tuple-element.89), channel_id=1, source_target_pairs={{0,16},{8,24},{16,0},{24,8},{1,17},{9,25},{17,1},{25,9},{2,18},{10... | collective-permute-start | bytes 2359304 | tf_op jit(solution)/shard_map/ppermute | solution.py:24
  727.1 20.5 %collective-permute-start.52 = (bf16[192,2048]{1,0:T(8,128)(2,1)S(1)}, bf16[192,2048]{1,0:T(8,128)(2,1)S(1)}, u32[]{:S(2)}, u32[]{:S(2)}) collective-permute-start(bf16[192,2048]{1,0:T(8,128)(2,1)S(1)} %get-tuple-element.91), channel_id=1, source_target_pairs={{0,8},{8,0},{16,24},{24,16},{1,9},{9,1},{17,25},{25,17},{2,10},{10... | collective-permute-start | bytes 2359304 | tf_op jit(solution)/shard_map/ppermute | solution.py:24
  749.4 50.8 %collective-permute-start.51 = (bf16[384,2048]{1,0:T(8,128)(2,1)}, bf16[384,2048]{1,0:T(8,128)(2,1)}, u32[]{:S(2)}, u32[]{:S(2)}) collective-permute-start(bf16[384,2048]{1,0:T(8,128)(2,1)} %pad_maximum_fusion.6), channel_id=1, source_target_pairs={{0,8},{8,0},{16,24},{24,16},{1,9},{9,1},{17,25},{25,17},{2,10},{10... | collective-permute-start | bytes 4718600 | tf_op jit(solution)/shard_map/ppermute | solution.py:24
  752.7 47.6 %collective-permute-start.53 = (bf16[384,2048]{1,0:T(8,128)(2,1)}, bf16[384,2048]{1,0:T(8,128)(2,1)}, u32[]{:S(2)}, u32[]{:S(2)}) collective-permute-start(bf16[384,2048]{1,0:T(8,128)(2,1)} %pad_maximum_fusion.7), channel_id=1, source_target_pairs={{0,16},{8,24},{16,0},{24,8},{1,17},{9,25},{17,1},{25,9},{2,18},{10... | collective-permute-start | bytes 4718600 | tf_op jit(solution)/shard_map/ppermute | solution.py:24
  754.8 19.6 %collective-permute-start.39 = (bf16[1,384,512]{2,1,0:T(8,128)(2,1)}, bf16[1,384,512]{2,1,0:T(8,128)(2,1)}, u32[]{:S(2)}, u32[]{:S(2)}) collective-permute-start(bf16[1,384,512]{2,1,0:T(8,128)(2,1)} %get-tuple-element.113), channel_id=1, source_target_pairs={{0,8},{8,0},{16,24},{24,16},{1,9},{9,1},{17,25},{25,17},{2,10},{10... | collective-permute-start | bytes 1179656 | tf_op jit(solution)/shard_map/ppermute | solution.py:24
  754.8 27.8 %collective-permute-start.40 = (bf16[1,384,512]{2,1,0:T(8,128)(2,1)}, bf16[1,384,512]{2,1,0:T(8,128)(2,1)}, u32[]{:S(2)}, u32[]{:S(2)}) collective-permute-start(bf16[1,384,512]{2,1,0:T(8,128)(2,1)} %get-tuple-element.112), channel_id=1, source_target_pairs={{0,16},{8,24},{16,0},{24,8},{1,17},{9,25},{17,1},{25,9},{2,18},{10... | collective-permute-start | bytes 1179656 | tf_op jit(solution)/shard_map/ppermute | solution.py:24
  755.8 35.3 %collective-permute-start.41 = (bf16[1,384,512]{2,1,0:T(8,128)(2,1)}, bf16[1,384,512]{2,1,0:T(8,128)(2,1)S(1)}, u32[]{:S(2)}, u32[]{:S(2)}) collective-permute-start(bf16[1,384,512]{2,1,0:T(8,128)(2,1)} %get-tuple-element.111), channel_id=1, source_target_pairs={{0,24},{8,16},{16,8},{24,0},{1,25},{9,17},{17,9},{25,1},{2,26},{10... | collective-permute-start | bytes 1179656 | tf_op jit(solution)/shard_map/ppermute | solution.py:24
  813.3 20.5 %collective-permute-start.54 = (bf16[384,2048]{1,0:T(8,128)(2,1)S(1)}, bf16[384,2048]{1,0:T(8,128)(2,1)S(1)}, u32[]{:S(2)}, u32[]{:S(2)}) collective-permute-start(bf16[384,2048]{1,0:T(8,128)(2,1)S(1)} %get-tuple-element.58), channel_id=1, source_target_pairs={{0,8},{8,0},{16,24},{24,16},{1,9},{9,1},{17,25},{25,17},{2,10},{10... | collective-permute-start | bytes 4718600 | tf_op jit(solution)/shard_map/ppermute | solution.py:24
  815.3 20.4 %collective-permute-start.55 = (bf16[384,2048]{1,0:T(8,128)(2,1)S(1)}, bf16[384,2048]{1,0:T(8,128)(2,1)S(1)}, u32[]{:S(2)}, u32[]{:S(2)}) collective-permute-start(bf16[384,2048]{1,0:T(8,128)(2,1)S(1)} %get-tuple-element.58), channel_id=1, source_target_pairs={{0,16},{8,24},{16,0},{24,8},{1,17},{9,25},{17,1},{25,9},{2,18},{10... | collective-permute-start | bytes 4718600 | tf_op jit(solution)/shard_map/ppermute | solution.py:24
  833.8 12.1 %collective-permute-start.56 = (bf16[192,2048]{1,0:T(8,128)(2,1)S(1)}, bf16[192,2048]{1,0:T(8,128)(2,1)S(1)}, u32[]{:S(2)}, u32[]{:S(2)}) collective-permute-start(bf16[192,2048]{1,0:T(8,128)(2,1)S(1)} %slice.446), channel_id=1, source_target_pairs={{0,16},{8,24},{16,0},{24,8},{1,17},{9,25},{17,1},{25,9},{2,18},{10... | collective-permute-start | bytes 2359304 | tf_op jit(solution)/shard_map/ppermute | solution.py:24
  835.8 12.1 %collective-permute-start.57 = (bf16[192,2048]{1,0:T(8,128)(2,1)S(1)}, bf16[192,2048]{1,0:T(8,128)(2,1)S(1)}, u32[]{:S(2)}, u32[]{:S(2)}) collective-permute-start(bf16[192,2048]{1,0:T(8,128)(2,1)S(1)} %slice.447), channel_id=1, source_target_pairs={{0,8},{8,0},{16,24},{24,16},{1,9},{9,1},{17,25},{25,17},{2,10},{10... | collective-permute-start | bytes 2359304 | tf_op jit(solution)/shard_map/ppermute | solution.py:24
  855.2 265.4 %reduce-scatter.11.cloned.1.call-start = ((), (), s32[]{:S(2)}) async-start(), calls=%async_computation.9 | async-start | bytes 8257536 | tf_op jit(solution)/shard_map/reduce_scatter | solution.py:511
  884.7 260.9 %reduce-scatter.5.cloned.1.call-start = ((), (), s32[]{:S(2)}) async-start(), calls=%async_computation.6 | async-start | bytes 9437184 | tf_op jit(solution)/shard_map/reduce_scatter | solution.py:118
  1041.4 13.2 %collective-permute-start.58 = (bf16[192,2048]{1,0:T(8,128)(2,1)S(1)}, bf16[192,2048]{1,0:T(8,128)(2,1)S(1)}, u32[]{:S(2)}, u32[]{:S(2)}) collective-permute-start(bf16[192,2048]{1,0:T(8,128)(2,1)S(1)} %get-tuple-element.83), channel_id=1, source_target_pairs={{0,16},{8,24},{16,0},{24,8},{1,17},{9,25},{17,1},{25,9},{2,18},{10... | collective-permute-start | bytes 2359304 | tf_op jit(solution)/shard_map/ppermute | solution.py:24
  1042.4 12.2 %collective-permute-start.60 = (bf16[192,2048]{1,0:T(8,128)(2,1)S(1)}, bf16[192,2048]{1,0:T(8,128)(2,1)S(1)}, u32[]{:S(2)}, u32[]{:S(2)}) collective-permute-start(bf16[192,2048]{1,0:T(8,128)(2,1)S(1)} %get-tuple-element.85), channel_id=1, source_target_pairs={{0,8},{8,0},{16,24},{24,16},{1,9},{9,1},{17,25},{25,17},{2,10},{10... | collective-permute-start | bytes 2359304 | tf_op jit(solution)/shard_map/ppermute | solution.py:24
  1056.7 20.7 %collective-permute-start.59 = (bf16[384,2048]{1,0:T(8,128)(2,1)}, bf16[384,2048]{1,0:T(8,128)(2,1)}, u32[]{:S(2)}, u32[]{:S(2)}) collective-permute-start(bf16[384,2048]{1,0:T(8,128)(2,1)} %pad_maximum_fusion.8), channel_id=1, source_target_pairs={{0,8},{8,0},{16,24},{24,16},{1,9},{9,1},{17,25},{25,17},{2,10},{10... | collective-permute-start | bytes 4718600 | tf_op jit(solution)/shard_map/ppermute | solution.py:24
  1058.8 20.7 %collective-permute-start.61 = (bf16[384,2048]{1,0:T(8,128)(2,1)}, bf16[384,2048]{1,0:T(8,128)(2,1)}, u32[]{:S(2)}, u32[]{:S(2)}) collective-permute-start(bf16[384,2048]{1,0:T(8,128)(2,1)} %pad_maximum_fusion.9), channel_id=1, source_target_pairs={{0,16},{8,24},{16,0},{24,8},{1,17},{9,25},{17,1},{25,9},{2,18},{10... | collective-permute-start | bytes 4718600 | tf_op jit(solution)/shard_map/ppermute | solution.py:24
  1093.7 9.1 collective-permute-start.70
  1109.0 9.1 collective-permute-start.72
  1112.5 13.2 %collective-permute-start.65 = (bf16[1,64,2304]{2,1,0:T(8,128)(2,1)}, bf16[1,64,2304]{2,1,0:T(8,128)(2,1)S(1)}, u32[]{:S(2)}, u32[]{:S(2)}) collective-permute-start(bf16[1,64,2304]{2,1,0:T(8,128)(2,1)} %get-tuple-element.119), channel_id=1, source_target_pairs={{0,8},{8,0},{16,24},{24,16},{1,9},{9,1},{17,25},{25,17},{2,10},{10... | collective-permute-start | bytes 884744 | tf_op jit(solution)/shard_map/ppermute | solution.py:24
  1123.2 15.4 %collective-permute-start.66 = (bf16[1,64,2304]{2,1,0:T(8,128)(2,1)S(1)}, bf16[1,64,2304]{2,1,0:T(8,128)(2,1)S(1)}, u32[]{:S(2)}, u32[]{:S(2)}) collective-permute-start(bf16[1,64,2304]{2,1,0:T(8,128)(2,1)S(1)} %copy-done.57), channel_id=1, source_target_pairs={{0,16},{8,24},{16,0},{24,8},{1,17},{9,25},{17,1},{25,9},{2,18},{10... | collective-permute-start | bytes 884744 | tf_op jit(solution)/shard_map/ppermute | solution.py:24
  1124.0 17.5 %collective-permute-start.67 = (bf16[1,64,2304]{2,1,0:T(8,128)(2,1)S(1)}, bf16[1,64,2304]{2,1,0:T(8,128)(2,1)S(1)}, u32[]{:S(2)}, u32[]{:S(2)}) collective-permute-start(bf16[1,64,2304]{2,1,0:T(8,128)(2,1)S(1)} %copy-done.56), channel_id=1, source_target_pairs={{0,24},{8,16},{16,8},{24,0},{1,25},{9,17},{17,9},{25,1},{2,26},{10... | collective-permute-start | bytes 884744 | tf_op jit(solution)/shard_map/ppermute | solution.py:24
  1148.1 12.9 %collective-permute-start.63 = (bf16[1,64,2048]{2,1,0:T(8,128)(2,1)S(1)}, bf16[1,64,2048]{2,1,0:T(8,128)(2,1)S(1)}, u32[]{:S(2)}, u32[]{:S(2)}) collective-permute-start(bf16[1,64,2048]{2,1,0:T(8,128)(2,1)S(1)} %get-tuple-element.122), channel_id=1, source_target_pairs={{0,16},{8,24},{16,0},{24,8},{1,17},{9,25},{17,1},{25,9},{2,18},{10... | collective-permute-start | bytes 786440 | tf_op jit(solution)/shard_map/ppermute | solution.py:24
  1152.0 9.1 collective-permute-start.64
  (141 other events, 2219.7 us)
Sparse Core Ops, SparseCore 0:
  39.6 82.4 all-gather.10
  123.6 27.4 all-gather.6
  153.4 90.2 all-gather.12
  245.2 71.8 all-gather.8
  662.7 104.6 reduce-scatter.8
  855.3 39.1 reduce-scatter.6
  896.8 78.4 reduce-scatter.10
  977.5 89.9 reduce-scatter.4

commit v3 on v2

v3 whole, which is shorter than its diff:
```python
from functools import partial

import jax
import jax.numpy as jnp
from jax import lax
from jax.experimental import pallas as pl
from jax.experimental.pallas import tpu as pltpu
from jax.sharding import PartitionSpec as P

HEAD = 64
PAIR = 128
CHUNK = 128
EPSILON = 1e-05
GROUP_EPSILON = 1.0
BF = jnp.bfloat16
F32 = jnp.float32
NT = (((1,), (1,)), ((), ()))
TN = (((0,), (0,)), ((), ()))
NN = (((1,), (0,)), ((), ()))


def swap(value, axis, distance):
    size = lax.axis_size(axis)
    return lax.ppermute(value, axis, [(i, i ^ distance) for i in range(size)])


def gather_seq(part):
    size = lax.axis_size("seq")
    if size == 4:
        half = part.shape[0] // 2
        one, two = swap(part, "seq", 1), swap(part, "seq", 2)
        low, high = swap(one[:half], "seq", 2), swap(two[half:], "seq", 1)
        return [part, one, two, jnp.concatenate([low, high], axis=0)]
    return [part] + [swap(part, "seq", distance) for distance in range(1, size)]


def scatter_seq(parts):
    size = lax.axis_size("seq")
    if size == 4:
        own, one, two, far = parts
        half = far.shape[0] // 2
        low, high = swap(far[:half], "seq", 1), swap(far[half:], "seq", 2)
        two = jnp.concatenate([(two[:half].astype(F32) + low.astype(F32)).astype(BF), two[half:]], axis=0)
        one = jnp.concatenate([one[:half], (one[half:].astype(F32) + high.astype(F32)).astype(BF)], axis=0)
        return [own, swap(one, "seq", 1), swap(two, "seq", 2)]
    return [parts[0]] + [swap(parts[distance], "seq", distance) for distance in range(1, size)]


def trade_seq(parts):
    return [parts[0]] + [swap(part, "seq", j + 1) for j, part in enumerate(parts[1:])]


def blocks_of(values, size):
    rows = values.shape[0] // size
    return [values[j * rows : (j + 1) * rows] for j in range(size)]


def bits_of(size):
    return [1 << b for b in range(size.bit_length() - 1)]


def gather_small(part, axis):
    for bit in bits_of(lax.axis_size(axis)):
        other = swap(part, axis, bit)
        second = (lax.axis_index(axis) & bit) != 0
        part = jnp.concatenate([jnp.where(second, other, part), jnp.where(second, part, other)], axis=0)
    return part


def scatter_small(parts):
    for axis in ("seq", "dp"):
        for bit in reversed(bits_of(lax.axis_size(axis))):
            half = parts.shape[0] // 2
            second = (lax.axis_index(axis) & bit) != 0
            low, high = parts[:half], parts[half:]
            parts = jnp.where(second, high, low) + swap(jnp.where(second, low, high), axis, bit)
    return parts[0]


def block(shape, index):
    return pl.BlockSpec(shape, lambda *i: index(*i[:-1], i[-1][0]))


def fixed(shape):
    return pl.BlockSpec(shape, lambda *i: (0,) * len(shape))


def relative(tile, per, here):
    return (lax.div(tile, per) ^ here) * per + lax.rem(tile, per)


def kernel(body, name, grid, here, ins, outs, scratch=(), vmem=48):
    return pl.pallas_call(
        body,
        out_shape=[jax.ShapeDtypeStruct(shape, kind) for shape, kind, _ in outs],
        grid_spec=pltpu.PrefetchScalarGridSpec(
            num_scalar_prefetch=1,
            grid=grid,
            in_specs=[spec for _, spec in ins],
            out_specs=[spec for _, _, spec in outs],
            scratch_shapes=list(scratch),
        ),
        compiler_params=pltpu.CompilerParams(vmem_limit_bytes=vmem * 2**20),
        name=name,
    )(here, *[array for array, _ in ins])


def row_index(rows):
    return lax.broadcasted_iota(jnp.int32, (rows, 1), 0)


def placed(place, width):
    return pl.ds(pl.multiple_of(place * width, width), width)


def cut_body(count, parts, here, *refs):
    ins, outs = refs[:count], refs[count:]
    at = 0
    for ref in ins:
        width = ref.shape[1] // parts
        for j in range(parts):
            outs[j][:, at : at + width] = ref[:, placed(here[0] ^ j, width)]
        at += width


def cut_columns(weights, here, parts):
    rows, width = weights[0].shape[0], sum(w.shape[1] for w in weights) // parts
    return kernel(
        partial(cut_body, len(weights), parts), "cut_columns", (1,), here,
        [(w, fixed(w.shape)) for w in weights],
        [((rows, width), BF, fixed((rows, width)))] * parts,
    )


def stack_body(parts, here, *refs):
    for j in range(parts):
        refs[-1][here[0] ^ j] = refs[j][...]


def stack_rows(pieces, here):
    parts, (rows, width) = len(pieces), pieces[0].shape
    (stacked,) = kernel(
        partial(stack_body, parts), "stack_rows", (1,), here,
        [(p, fixed(p.shape)) for p in pieces],
        [((parts, rows, width), BF, fixed((parts, rows, width)))],
    )
    return stacked


def join_body(parts, count, here, *refs):
    ins, outs = refs[:parts], refs[parts:]
    at = 0
    for ref in outs:
        width = ref.shape[1] // parts
        for j in range(parts):
            ref[:, placed(here[0] ^ j, width)] = ins[j][:, at : at + width].astype(F32)
        at += width


def join_columns(pieces, widths, here):
    parts, rows = len(pieces), pieces[0].shape[0]
    return kernel(
        partial(join_body, parts, len(widths)), "join_columns", (1,), here,
        [(p, fixed(p.shape)) for p in pieces],
        [((rows, width), F32, fixed((rows, width))) for width in widths],
    )


def spread_body(parts, product, here, base_ref, *refs):
    out = refs[-1]
    width = refs[0].shape[1]
    for j in range(parts):
        at = placed(here[0] ^ j, width)
        piece, base = refs[j][...].astype(F32), base_ref[:, at].astype(F32)
        out[:, at] = (base * piece if product else base + piece).astype(BF)


def spread_columns(base, pieces, here, product, turn, tile):
    rows, width = base.shape
    (result,) = kernel(
        partial(spread_body, len(pieces), product), "spread_columns", (rows // tile,), here,
        [(base, block((tile, width), lambda i, h: (i, 0)))]
        + [(p, block((tile, p.shape[1]), lambda i, h, j=j: (i ^ j if turn else i, 0))) for j, p in enumerate(pieces)],
        [((rows, width), BF, block((tile, width), lambda i, h: (i, 0)))],
    )
    return result


def shuffled(values, groups, back=False):
    seq, dp = groups
    if back:
        seq, dp = dp, seq
    lane = lax.broadcasted_iota(jnp.int32, (1, PAIR), 1) < HEAD
    source = [s * dp + d for d in range(dp) for s in range(seq)]
    columns = []
    for one, two in zip(source[::2], source[1::2]):
        low = values[:, one // 2 * PAIR : (one // 2 + 1) * PAIR]
        high = values[:, two // 2 * PAIR : (two // 2 + 1) * PAIR]
        low = pltpu.roll(low, HEAD, 1) if one % 2 else low
        high = high if two % 2 else pltpu.roll(high, HEAD, 1)
        columns.append(jnp.where(lane, low, high))
    return jnp.concatenate(columns, axis=1)


def outside(values, groups, channels, back=False):
    seq, dp = groups[::-1] if back else groups
    return values.reshape(-1, seq, dp, channels).swapaxes(1, 2).reshape(values.shape)


def centre(values):
    centred = values - jnp.mean(values, axis=-1, keepdims=True)
    spread = jnp.mean(centred * centred, axis=-1, keepdims=True)
    return centred, lax.rsqrt(spread + EPSILON)


def mix_body(count, norm, groups, here, x_ref, marks_ref, vec_ref, *refs):
    outs, last = refs[:-1], refs[-1]

    @pl.when(pl.program_id(0) == 0)
    def _():
        last[...] = jnp.zeros_like(last)

    values = x_ref[...].astype(F32)
    if norm:
        centred, inverse = centre(values)
        values = centred * inverse
    if groups:
        values = shuffled(values, groups)
    if norm:
        values = values * vec_ref[0:1, :] + vec_ref[1:2, :]
    rows = values.shape[0]
    previous = jnp.where(row_index(rows) == 0, last[0:1, :], pltpu.roll(values, 1, 0)) * marks_ref[:, 3:4]
    last[0:1, :] = values[rows - 1 :, :]
    step = values - previous
    outs[count][...] = step.astype(BF)
    for i in range(count):
        outs[i][...] = (previous + step * vec_ref[2 + i : 3 + i, :]).astype(BF)


def mixes(values, marks, vec, count, norm, groups, here, per):
    rows, width = values.shape
    tile = CHUNK
    own = block((tile, width), lambda i, h: (relative(i, per, h), 0))
    return kernel(
        partial(mix_body, count, norm, groups), "mixes", (rows // tile,), here,
        [
            (values, own),
            (marks, block((tile, PAIR), lambda i, h: (i, 0))),
            (vec, fixed(vec.shape)),
        ],
        [((rows, width), BF, own)] * (count + 1),
        [pltpu.VMEM((8, width), F32)],
    )


def mixes_back_body(count, here, *refs):
    grads, weights = refs[:count], refs[count : 2 * count]
    step_ref, marks_ref, vec_ref, out_ref, sums_ref, later = refs[2 * count :]

    @pl.when(pl.program_id(1) == 0)
    def _():
        later[...] = jnp.zeros_like(later)
        sums_ref[...] = jnp.zeros_like(sums_ref)

    step = step_ref[...].astype(F32)
    for i in range(count):
        grad = dot(grads[i][...], weights[i][...], NT)
        sums_ref[i : i + 1, :] += jnp.sum(grad * step, axis=0, keepdims=True)
        part = grad * vec_ref[i : i + 1, :]
        total, straight = (total + grad, straight + part) if i else (grad, part)
    kept = (total - straight) * marks_ref[:, 3:4]
    rows = kept.shape[0]
    up = jnp.where(row_index(rows) == rows - 1, later[0:1, :], pltpu.roll(kept, rows - 1, 0))
    later[0:1, :] = kept[0:1, :]
    out_ref[...] = (straight + up).astype(BF)


def mixes_back(grads, weights, step, marks, vec, here, seq):
    rows, width = step.shape
    tile, columns, count = rows // seq, min(512, width), len(grads)
    last = rows // tile - 1

    def natural(i):
        return last - i

    ins = [(g, block((tile, g.shape[1]), lambda c, i, h: (relative(natural(i), 1, h), 0))) for g in grads]
    for g, (w, at) in zip(grads, weights):
        ins.append((w, pl.BlockSpec((columns, g.shape[1]), lambda c, i, h, at=at: (c, at))))
    ins += [
        (step, block((tile, columns), lambda c, i, h: (relative(natural(i), 1, h), c))),
        (marks, block((tile, PAIR), lambda c, i, h: (natural(i), 0))),
        (vec, block((8, columns), lambda c, i, h: (0, c))),
    ]
    return kernel(
        partial(mixes_back_body, count), "mixes_back", (width // columns, last + 1), here, ins,
        [
            ((rows, width), BF, block((tile, columns), lambda c, i, h: (relative(natural(i), 1, h), c))),
            ((8, width), F32, block((8, columns), lambda c, i, h: (0, c))),
        ],
        [pltpu.VMEM((8, columns), F32)],
    )


def after_body(count, here, x_ref, vec_ref, *refs):
    after_ref, normed_ref = refs[count:]
    after = x_ref[...].astype(F32)
    for ref in refs[:count]:
        after = after + ref[...].astype(F32)
    after_ref[...] = after
    centred, inverse = centre(after)
    normed_ref[...] = (centred * inverse * vec_ref[0:1, :] + vec_ref[1:2, :]).astype(BF)


def after_norm(inputs, terms, vec, here):
    rows, width = inputs.shape
    own = block((CHUNK, width), lambda i, h: (i, 0))
    return kernel(
        partial(after_body, len(terms)), "after_norm", (rows // CHUNK,), here,
        [(inputs, own), (vec, fixed(vec.shape))] + [(t, own) for t in terms],
        [((rows, width), F32, own), ((rows, width), BF, own)],
    )


def norm_back_body(count, groups, here, x_ref, base_ref, vec_ref, *refs):
    wide_ref, narrow_ref, sums_ref = refs[count:]

    @pl.when(pl.program_id(0) == 0)
    def _():
        sums_ref[...] = jnp.zeros_like(sums_ref)

    grad = refs[0][...].astype(F32)
    for ref in refs[1:count]:
        grad = grad + ref[...].astype(F32)
    if groups:
        grad = shuffled(grad, groups, back=True)
    centred, inverse = centre(x_ref[...].astype(F32))
    normed = centred * inverse
    sums_ref[0:1, :] += jnp.sum(grad * normed, axis=0, keepdims=True)
    sums_ref[1:2, :] += jnp.sum(grad, axis=0, keepdims=True)
    grad = grad * vec_ref[0:1, :]
    grad = grad - jnp.mean(grad, axis=-1, keepdims=True) - normed * jnp.mean(grad * normed, axis=-1, keepdims=True)
    result = base_ref[...].astype(F32) + inverse * grad
    wide_ref[...] = result
    narrow_ref[...] = result.astype(BF)


def norm_back(terms, inputs, base, vec, groups, here):
    rows, width = inputs.shape
    own = block((CHUNK, width), lambda i, h: (i, 0))
    return kernel(
        partial(norm_back_body, len(terms), groups), "norm_back", (rows // CHUNK,), here,
        [(inputs, own), (base, own), (vec, fixed(vec.shape))] + [(t, own) for t in terms],
        [((rows, width), F32, own), ((rows, width), BF, own), ((8, width), F32, fixed((8, width)))],
    )


def gate_body(mix_ref, weight_ref, wkv_ref, par_ref, gate_ref, mixed_ref):
    gate = dot(mix_ref[...], weight_ref[...], NN)
    gate_ref[...] = gate
    ones = jnp.where(same_head(), 1.0, 0.0).astype(BF)
    for pair in range(gate.shape[1] // PAIR):
        at = slice(pair * PAIR, (pair + 1) * PAIR)
        wkv = wkv_ref[:, at]
        centred = wkv - head_sum_fine(wkv, ones) * (1.0 / HEAD)
        spread = head_sum(centred * centred, ones) * (1.0 / HEAD)
        normed = centred * lax.rsqrt(spread + GROUP_EPSILON) * par_ref[1:2, at] + par_ref[2:3, at]
        mixed_ref[:, at] = (normed * (gate[:, at] / (1.0 + jnp.exp(-gate[:, at])))).astype(BF)


def gated(mix_g, weights, wkv, params, here, seq):
    rows, width = mix_g.shape
    tile, part = rows // seq, wkv.shape[1]
    own = block((tile, part), lambda i, h: (i, 0))
    return kernel(
        lambda here, *refs: gate_body(*refs), "gate", (seq,), here,
        [
            (mix_g, block((tile, width), lambda i, h: (i, 0))),
            (weights, block((width, part), lambda i, h: (0, 0))),
            (wkv, own),
            (params, fixed(params.shape)),
        ],
        [((rows, part), F32, own), ((rows, part), BF, own)],
    )


def columns_body(here, left_ref, right_ref, out_ref):
    out_ref[...] = dot(left_ref[...], right_ref[...], NN).astype(BF)


def columns_product(left, right, part, relative_to, here, seq):
    rows, depth = left.shape
    tile = rows // seq
    (result,) = kernel(
        columns_body, "value_columns", (seq,), here,
        [
            (left, block((tile, depth), lambda i, h: (i, 0))),
            (right, block((depth, part), lambda i, h: (0, h ^ relative_to))),
        ],
        [((rows, part), BF, block((tile, part), lambda i, h: (i ^ relative_to, 0)))],
    )
    return result


def channel_body(count, here, pre_ref, grad_ref, *refs):
    channel_ref, d_recept_ref = refs[count:]
    value = refs[0][...].astype(F32)
    for ref in refs[1:count]:
        value = value + ref[...].astype(F32)
    opened = 1.0 / (1.0 + jnp.exp(-pre_ref[...]))
    channel = opened * value
    channel_ref[...] = channel.astype(BF)
    d_recept_ref[...] = (grad_ref[...].astype(F32) * channel * (1.0 - opened)).astype(BF)


def channel_out(terms, pre, grad_all, here, seq):
    rows, part = pre.shape
    tile = rows // seq
    own = block((tile, part), lambda i, h: (i, 0))
    return kernel(
        partial(channel_body, len(terms)), "channel", (seq,), here,
        [(pre, own), (grad_all, block((tile, part), lambda i, h: (i, h)))] + [(t, own) for t in terms],
        [((rows, part), BF, own)] * 2,
    )


def head_masks():
    lane = lax.broadcasted_iota(jnp.int32, (1, PAIR), 1)
    first = (lane < HEAD).astype(F32)
    return first, 1.0 - first


def same_head():
    row = lax.broadcasted_iota(jnp.int32, (PAIR, PAIR), 0) < HEAD
    column = lax.broadcasted_iota(jnp.int32, (PAIR, PAIR), 1) < HEAD
    return row == column


def dot(left, right, dims):
    return lax.dot_general(left, right, dims, preferred_element_type=F32)


def head_sum(values, ones):
    return dot(values.astype(BF), ones, NN)


def head_sum_fine(values, ones):
    coarse = values.astype(BF)
    rest = (values - coarse.astype(F32)).astype(BF)
    return dot(coarse, ones, NN) + dot(rest, ones, NN)


def stacked(values, first, second):
    return jnp.concatenate([(values * first).astype(BF), (values * second).astype(BF)], axis=0)


def masks_of(rows_ref, columns_ref):
    segment = rows_ref[:, 0:1]
    reaches = rows_ref[:, 1:2]
    last_same = rows_ref[:, 2:3]
    reach_last = rows_ref[CHUNK - 1 : CHUNK, 1:2]
    before = lax.broadcasted_iota(jnp.int32, (CHUNK, CHUNK), 1) < lax.broadcasted_iota(
        jnp.int32, (CHUNK, CHUNK), 0
    )
    allowed = jnp.where((segment == columns_ref[0:1, :]) & before, 1.0, 0.0)
    return reaches, last_same, reach_last, jnp.concatenate([allowed, allowed], axis=0)


def wkv_forward_body(
    here, r_ref, k_ref, v_ref, rows_ref, columns_ref, grow_ref, shrink_ref, tail_ref, par_ref,
    wkv_ref, states_ref, state,
):
    @pl.when(pl.program_id(0) == 0)
    def _():
        state[...] = jnp.zeros_like(state)

    first, second = head_masks()
    block = same_head()
    ones = jnp.where(block, 1.0, 0.0).astype(BF)
    reaches, last_same, reach_last, allowed = masks_of(rows_ref, columns_ref)
    for pair in range(r_ref.shape[1] // PAIR):
        at = slice(pair * PAIR, (pair + 1) * PAIR)
        r, k, v = r_ref[:, at].astype(F32), k_ref[:, at].astype(F32), v_ref[:, at].astype(F32)
        bonus, decay = par_ref[0:1, at], par_ref[3:4, at]
        held = state[at, :]
        held_b = held.astype(BF)
        states_ref[0, at, :] = held_b
        grown = r * grow_ref[:, at]
        shrunk = (k * shrink_ref[:, at]).astype(BF)
        scores = (dot(stacked(grown, first, second), shrunk, NT) * allowed).astype(BF)
        both = jnp.concatenate([scores[:CHUNK], scores[CHUNK:]], axis=1)
        wkv = dot(both, stacked(v, first, second), NN)
        wkv = wkv + dot((grown * reaches).astype(BF), held_b, NT)
        wkv = wkv + head_sum(r * bonus * k, ones) * v
        fresh = dot(v_ref[:, at], (k * tail_ref[:, at] * last_same).astype(BF), TN)
        state[at, :] = held * (decay * reach_last) + jnp.where(block, fresh, 0.0)
        wkv_ref[:, at] = wkv


def wkv_backward_body(
    here, r_ref, k_ref, v_ref, g_ref, wkv_ref, d_mixed_ref, states_ref,
    rows_ref, columns_ref, grow_ref, shrink_ref, tail_ref, par_ref,
    d_r_ref, d_k_ref, d_v_ref, d_g_ref, sums_ref, d_state,
):
    @pl.when(pl.program_id(0) == 0)
    def _():
        d_state[...] = jnp.zeros_like(d_state)
        sums_ref[...] = jnp.zeros_like(sums_ref)

    first, second = head_masks()
    block = same_head()
    ones = jnp.where(block, 1.0, 0.0).astype(BF)
    reaches, last_same, reach_last, allowed = masks_of(rows_ref, columns_ref)
    offset = lax.broadcasted_iota(jnp.int32, (CHUNK, PAIR), 0).astype(F32)
    for pair in range(r_ref.shape[1] // PAIR):
        at = slice(pair * PAIR, (pair + 1) * PAIR)
        bonus, gain, bias, decay = (par_ref[i : i + 1, at] for i in range(4))
        wkv, gate, d_mixed = wkv_ref[:, at], g_ref[:, at], d_mixed_ref[:, at]
        centred = wkv - head_sum_fine(wkv, ones) * (1.0 / HEAD)
        spread = head_sum(centred * centred, ones) * (1.0 / HEAD)
        inverse = lax.rsqrt(spread + GROUP_EPSILON)
        normed = centred * inverse
        opened = 1.0 / (1.0 + jnp.exp(-gate))
        d_scaled = d_mixed * gate * opened
        d_g = d_mixed * (normed * gain + bias) * opened * (1.0 + gate * (1.0 - opened))
        d_g_ref[:, at] = d_g.astype(BF)
        d_normed = d_scaled * gain
        mean_one = head_sum(d_normed, ones) * (1.0 / HEAD)
        mean_two = head_sum(d_normed * normed, ones) * (1.0 / HEAD)
        d_wkv = inverse * (d_normed - mean_one - normed * mean_two)
        r, k, v = r_ref[:, at].astype(F32), k_ref[:, at].astype(F32), v_ref[:, at].astype(F32)
        v_b, d_wkv_b = v_ref[:, at], d_wkv.astype(BF)
        grow, shrink, tail = grow_ref[:, at], shrink_ref[:, at], tail_ref[:, at] * last_same
        held = states_ref[0, at, :]
        later = d_state[at, :]
        later_b = later.astype(BF)
        grown = r * grow
        shrunk = k * shrink
        shrunk_b = shrunk.astype(BF)
        tailed_b = (k * tail).astype(BF)
        grown_two = stacked(grown, first, second)
        d_wkv_two = stacked(d_wkv, first, second)
        scores = (dot(grown_two, shrunk_b, NT) * allowed).astype(BF)
        d_scores = (dot(d_wkv_two, v_b, NT) * allowed).astype(BF)
        d_both = jnp.concatenate([d_scores[:CHUNK], d_scores[CHUNK:]], axis=1)
        d_grown = dot(d_both, stacked(shrunk, first, second), NN)
        d_grown = d_grown + dot((d_wkv * reaches).astype(BF), held, NN)
        d_shrunk = dot(d_scores, grown_two, TN)
        d_tailed = dot(v_b, later_b, NN)
        share = head_sum(r * bonus * k, ones)
        d_share = head_sum(d_wkv * v, ones)
        d_v = dot(scores, d_wkv_two, TN) + dot(tailed_b, later_b, NT) + share * d_wkv
        d_r_ref[:, at] = (d_grown * grow + d_share * bonus * k).astype(BF)
        d_k_ref[:, at] = (d_shrunk * shrink + d_tailed * tail + d_share * bonus * r).astype(BF)
        d_v_ref[:, at] = d_v.astype(BF)
        carried = decay * reach_last
        d_fresh = dot(d_wkv_b, (grown * reaches).astype(BF), TN)
        d_state[at, :] = later * carried + jnp.where(block, d_fresh, 0.0)
        grown_b = grown.astype(BF).astype(F32)
        d_log = (
            offset * grown_b * d_grown
            - (offset + 1.0) * shrunk_b.astype(F32) * d_shrunk
            + (CHUNK - 1.0 - offset) * tailed_b.astype(F32) * d_tailed
        )
        kept = CHUNK * carried * jnp.sum(held.astype(F32) * later, axis=0, keepdims=True)
        sums_ref[0:1, at] += jnp.sum(d_log, axis=0, keepdims=True) + kept
        sums_ref[1:2, at] += jnp.sum(d_share * r * k, axis=0, keepdims=True)
        sums_ref[2:3, at] += jnp.sum(d_scaled * normed, axis=0, keepdims=True)
        sums_ref[3:4, at] += jnp.sum(d_scaled, axis=0, keepdims=True)


def wkv_blocks(width, chunks, per, backward):
    def chunk(i):
        return chunks - 1 - i if backward else i

    tokens = block((CHUNK, width), lambda i, h: (relative(chunk(i), per, h), 0))
    states = block((1, width, PAIR), lambda i, h: (chunk(i), 0, 0))
    tables = [
        block((CHUNK, PAIR), lambda i, h: (chunk(i), 0)),
        block((8, CHUNK), lambda i, h: (0, chunk(i))),
    ]
    return tokens, states, tables + [fixed((CHUNK, width))] * 3 + [fixed((8, width))]


def wkv_forward(r, k, v, tables, here, per):
    length, width = r.shape
    chunks = length // CHUNK
    tokens, states, blocks = wkv_blocks(width, chunks, per, False)
    return kernel(
        wkv_forward_body, "wkv_forward", (chunks,), here,
        [(a, tokens) for a in (r, k, v)] + list(zip(tables, blocks)),
        [((length, width), F32, tokens), ((chunks, width, PAIR), BF, states)],
        [pltpu.VMEM((width, PAIR), F32)],
    )


def wkv_backward(r, k, v, gate, wkv, d_mixed, states_kept, tables, here, per):
    length, width = r.shape
    chunks = length // CHUNK
    tokens, states, blocks = wkv_blocks(width, chunks, per, True)
    return kernel(
        wkv_backward_body, "wkv_backward", (chunks,), here,
        [(a, tokens) for a in (r, k, v, gate, wkv, d_mixed)] + [(states_kept, states)] + list(zip(tables, blocks)),
        [((length, width), BF, tokens)] * 4 + [((8, width), F32, fixed((8, width)))],
        [pltpu.VMEM((width, PAIR), F32)],
    )


def wkv_tables(piece, keep, log_decay, bonus, gain, bias):
    length = piece.shape[0]
    by_chunk = piece.reshape(length // CHUNK, CHUNK)
    before = jnp.concatenate([jnp.full((1,), -1, piece.dtype), by_chunk[:-1, -1]])
    reaches = (by_chunk == before[:, None]).reshape(-1)
    last_same = (by_chunk == by_chunk[:, -1:]).reshape(-1)
    marks = jnp.stack([piece.astype(F32), reaches.astype(F32), last_same.astype(F32), keep], axis=1)
    rows = jnp.pad(marks, ((0, 0), (0, PAIR - 4)))
    columns = jnp.broadcast_to(piece.astype(F32)[None], (8, length))
    offset = jnp.arange(CHUNK).astype(F32)[:, None]
    grow = jnp.exp(offset * log_decay)
    shrink = jnp.exp(-(offset + 1.0) * log_decay)
    tail = jnp.exp((CHUNK - 1.0 - offset) * log_decay)
    zero = jnp.zeros_like(bonus)
    params = jnp.stack([bonus, gain, bias, jnp.exp(CHUNK * log_decay)] + [zero] * 4)
    return rows, columns, grow, shrink, tail, params


def segment_of(lengths, positions):
    rank = jnp.arange(lengths.shape[0])
    starts = jnp.sum(jnp.where(rank[:, None] > rank[None, :], lengths[None, :], 0), axis=1)
    later_flags = (positions[:, None] >= starts[None, 1:]).astype(jnp.int32)
    first_flags = jnp.any(positions[:, None] == starts[None, :], axis=1)
    return (jnp.sum(later_flags, axis=1), first_flags)


def rows_of(vec, *rows):
    return jnp.pad(jnp.stack([vec[i] for i in rows]), ((0, 8 - len(rows)), (0, 0)))


def shards(
    tokens, seq_lengths, out_grad, w_receptance, w_key, w_value, w_gate, w_output,
    ffn_key, ffn_receptance, ffn_value, vectors,
):
    seq, dp = lax.axis_size("seq"), lax.axis_size("dp")
    place = lax.axis_index("seq")
    here = jnp.reshape(place, (1,)).astype(jnp.int32)
    inputs_b, grad_b = tokens[0], out_grad[0]
    own_rows, width = inputs_b.shape
    length, part, unit = own_rows * seq, width // seq, vectors.shape[1]
    per = own_rows // CHUNK
    hidden_width = ffn_key.shape[1] // seq
    groups = (seq, dp)
    within = groups if unit == HEAD else None

    def whole(values):
        return jnp.concatenate(gather_seq(values), axis=0)

    def all_rows(weights):
        pieces = trade_seq(cut_columns(weights, here, seq))
        stacked = stack_rows(pieces, here)
        return lax.all_gather(stacked.reshape(-1, stacked.shape[-1]), "dp", axis=0, tiled=True)

    def owners_rows(grads, widths):
        grad = jnp.concatenate([g.astype(BF) for g in grads], axis=1)
        summed = lax.psum_scatter(grad, "dp", scatter_dimension=0, tiled=True)
        rows = summed.shape[0] // seq
        parts = [lax.dynamic_slice_in_dim(summed, (place ^ j) * rows, rows, 0) for j in range(seq)]
        return join_columns(trade_seq(parts), widths, here)

    def natural(grad):
        return lax.psum_scatter(grad.astype(BF), "dp", scatter_dimension=0, tiled=True).astype(F32)

    full_in = all_rows([w_receptance, w_key, w_value])
    vec_own = gather_small(vectors[None], "dp")
    vec_parts = gather_small(vec_own[None], "seq").astype(F32)
    vec_own = vec_own.transpose(1, 0, 2).reshape(-1, part).astype(F32)
    vec = vec_parts.transpose(2, 0, 1, 3).reshape(-1, width)
    turned = vec_parts.transpose(2, 1, 0, 3).reshape(-1, width)
    tokens_all = whole(inputs_b)
    full_gc = all_rows([w_gate, ffn_receptance])
    full_o = lax.all_gather(w_output, "dp", axis=0, tiled=True)
    grad_all = whole(grad_b)
    full_ck = all_rows([ffn_key])
    full_cv = lax.all_gather(ffn_value, "dp", axis=0, tiled=True)

    positions = jnp.arange(length, dtype=jnp.int32)
    piece, first_flags = segment_of(seq_lengths[0], positions)
    log_decay = -jnp.exp(vec_own[6])
    tables = wkv_tables(
        piece, 1.0 - first_flags.astype(F32), log_decay, vec_own[7], vec_own[8], vec_own[9]
    )
    marks = tables[0]

    if within is None:
        tokens_all = outside(tokens_all, groups, unit)
    mix_r, mix_k, mix_v, mix_g, step = mixes(
        tokens_all, marks, rows_of(turned, 0, 1, 2, 3, 4, 5), 4, True, within, here, per
    )
    recept, keyed, valued = (
        dot(m, full_in[:, i * part : (i + 1) * part], NN).astype(BF)
        for i, m in enumerate((mix_r, mix_k, mix_v))
    )
    wkv, states = wkv_forward(recept, keyed, valued, tables, here, per)
    gate_pre, mixed = gated(mix_g, full_gc, wkv, tables[5], here, seq)
    attn = [dot(rows, full_o, NN).astype(BF) for rows in blocks_of(mixed, seq)]
    after, normed_two = after_norm(inputs_b, scatter_seq(attn), rows_of(vec, 10, 11), here)

    normed_two = whole(normed_two)
    if within is None:
        normed_two = outside(normed_two, groups, unit)
    mix_k2, mix_r2, step_two = mixes(
        normed_two, marks, rows_of(turned, 10, 11, 12, 13), 2, False, within, here, per
    )
    recept_pre = dot(mix_r2, full_gc[:, part:], NN)
    opened = gather_seq(jax.nn.sigmoid(recept_pre).astype(BF))
    key_pre = dot(mix_k2, full_ck, NN)
    smooth = jax.nn.softplus(key_pre)
    hidden = (smooth * smooth).astype(BF)
    value_parts = [columns_product(hidden, full_cv, part, j, here, seq) for j in reversed(range(seq))]
    value_terms = scatter_seq(value_parts[::-1])
    d_value = spread_columns(grad_all, opened, here, True, True, own_rows)
    channel, d_recept_two = channel_out(value_terms, recept_pre, grad_all, here, seq)
    channel = trade_seq(blocks_of(channel, seq))
    out_rows = spread_columns(after, channel, here, False, False, CHUNK)

    d_hidden = dot(d_value, full_cv, NT)
    d_key_two = (d_hidden * 2.0 * smooth * jax.nn.sigmoid(key_pre)).astype(BF)
    d_normed_two, sums_two = mixes_back(
        [d_key_two, d_recept_two], [(full_ck, 0), (full_gc, 1)], step_two, marks,
        rows_of(turned, 12, 13), here, seq,
    )
    terms_two = scatter_seq(blocks_of(d_normed_two, seq))
    grad_cv = dot(hidden, d_value, TN)
    grad_ck = dot(mix_k2, d_key_two, TN)
    grad_cr = dot(mix_r2, d_recept_two, TN)
    if within is None:
        terms_two = [outside(t, groups, unit, back=True) for t in terms_two]
    d_after, d_attn, norm_sums_two = norm_back(terms_two, after, grad_b, rows_of(vec, 10), within, here)

    d_attn = whole(d_attn)
    d_mixed = dot(d_attn, full_o, NT)
    grad_wo = dot(mixed, d_attn, TN)
    d_recept, d_keyed, d_valued, d_gate, sums = wkv_backward(
        recept, keyed, valued, gate_pre, wkv, d_mixed, states, tables, here, per
    )
    d_normed, sums_one = mixes_back(
        [d_recept, d_keyed, d_valued, d_gate], [(full_in, 0), (full_in, 1), (full_in, 2), (full_gc, 0)],
        step, marks, rows_of(turned, 2, 3, 4, 5), here, seq,
    )
    terms = scatter_seq(blocks_of(d_normed, seq))
    grads_in = [
        dot(mix_r, d_recept, TN), dot(mix_k, d_keyed, TN), dot(mix_v, d_valued, TN), dot(mix_g, d_gate, TN)
    ]
    if within is None:
        terms = [outside(t, groups, unit, back=True) for t in terms]
    tokens_grad, _, norm_sums = norm_back(terms, inputs_b, d_after, rows_of(vec, 0), within, here)

    sum_cv = natural(grad_cv)
    sum_ck, sum_cr = owners_rows([grad_ck, grad_cr], [ffn_key.shape[1], width])
    sum_o = natural(grad_wo)
    sum_r, sum_k, sum_v, sum_g = owners_rows(grads_in, [width] * 4)

    def by_device(rows, turn):
        if turn:
            return rows.reshape(-1, dp, seq, unit).transpose(2, 1, 0, 3)
        return rows.reshape(-1, seq, dp, unit).transpose(1, 2, 0, 3)

    own_sums = jnp.stack([sums[0] * log_decay, sums[1], sums[2], sums[3]])
    own_sums = lax.dynamic_update_slice(jnp.zeros((4, width), F32), own_sums, (0, place * part))
    vector_rows = jnp.concatenate(
        [
            by_device(norm_sums[:2], False), by_device(sums_one[:4], True), by_device(own_sums, False),
            by_device(norm_sums_two[:2], False), by_device(sums_two[:2], True),
        ],
        axis=2,
    )
    sum_vec = scatter_small(vector_rows.reshape((-1,) + vector_rows.shape[2:]))
    return (
        out_rows[None], tokens_grad[None], sum_r, sum_k, sum_v, sum_g, sum_o,
        sum_ck, sum_cr, sum_cv, sum_vec,
    )


def solution(mesh):
    tokens = P("dp", "seq", None)
    rows = P(("seq", "dp"), None)
    columns = P(None, ("seq", "dp"))
    return jax.shard_map(
        shards,
        mesh=mesh,
        in_specs=(tokens, P("dp", None), tokens) + (rows,) * 8 + (columns,),
        out_specs=(tokens, tokens) + (rows,) * 8 + (columns,),
        check_vma=False,
    )
```

time: 1190 us -> 937 us (0.79)
  other arithmetic: 211 us -> 29.9 us
  local copies, waits for them, and re-layouts: 260 us -> 86.2 us
  Pallas kernels: 60.2 us -> 218 us
  matrix products: 240 us -> 156 us
  waiting for transfers between devices: 298 us -> 344 us
  starting transfers between devices: 93.5 us -> 80.7 us
    pallas_call x2 -> x25, Pallas kernels: 60.2 us -> 218 us  [kernel(): pl.pallas_call(body, out_shape=[jax.ShapeDtypeStruct(shape, kind) for sha...]
    dot_general x24 -> x19, matrix products: 240 us -> 156 us  [dot(): return lax.dot_general(left, right, dims, preferred_element_type=F32)]
    reduce_sum x11 -> x0, other arithmetic: 80.8 us -> none  [the longest x1 26.6 us: shards(): d_mixes = [jnp.sum(d * step, axis=0) for d in d_mix]]
    dynamic_update_slice x58 -> x0, local copies, waits for them, and re-layouts: 71.1 us -> none  [the longest x35 38.6 us: trade_seq(): result = lax.dynamic_update_slice_in_dim(result, piece, here ^ distance, 0)]
    convert_element_type x6 -> x0, local copies, waits for them, and re-layouts: 41.7 us -> none  [the longest x2 29.8 us: shards(): grad_all.reshape(length, seq, part).astype(F32)]
    mul x2 -> x0, other arithmetic: 36.3 us -> none  [to_before(): kept = values * keep]
    reduce_scatter x2, waiting for transfers between devices: 0.01 us -> 35.6 us  [natural(): lax.psum_scatter(grad.astype(BF), 'dp', scatter_dimension=0, tiled=True)]
    convert_element_type x7 -> x1, other arithmetic: 29.5 us -> 0.02 us  [shards(): vec_own = vec_own.transpose(1, 0, 2).reshape(-1, part).astype(F32)]
  transfers between devices with their start and end apart: 81 -> 73, of which waited for: 37 -> 39; matrix products, arithmetic and copies ran while one was open for 50% -> 26% of each run, Pallas kernels for 5% -> 23%
where the time goes in v3:
time: 937 us; the launch traced here: 930 us
  waiting for transfers between devices  344 us (37%)
  Pallas kernels  218 us (23%)
  matrix products  156 us (17%)
  local copies, waits for them, and re-layouts  86.2 us (9%)
  starting transfers between devices  80.7 us (9%)
  other arithmetic  29.9 us (3%)
  between operations  15.4 us (2%)
    ppermute x64, waiting for transfers between devices, swap(): return lax.ppermute(value, axis, [(i, i ^ distance) for i in range(size)])  307 us
    pallas_call x25, Pallas kernels, kernel(): pl.pallas_call(body, out_shape=[jax.ShapeDtypeStruct(shape, kind) for sha...  218 us
    dot_general x19, matrix products, dot(): return lax.dot_general(left, right, dims, preferred_element_type=F32)  156 us
    ppermute x64, starting transfers between devices, swap(): return lax.ppermute(value, axis, [(i, i ^ distance) for i in range(size)])  80.4 us
    unnamed x139, local copies, waits for them, and re-layouts  45.2 us
    reduce_scatter x2, waiting for transfers between devices, natural(): lax.psum_scatter(grad.astype(BF), 'dp', scatter_dimension=0, tiled=True)  35.6 us
  transfers between devices with their start and end apart: 73, of which 39 were waited for; matrix products, arithmetic and copies ran while one was open for 26% of the time, Pallas kernels for 23%

profile of v3, /device:TPU:0, one launch (start us, length us, event | category | flops | bytes accessed | tf_op | source)
XLA Modules:
  0.0 930.3 jit_solution(17230345772868818981)
XLA Ops:
  10.3 3.0 collective-permute-start.12
  14.8 4.2 collective-permute-done.12.refs_1_
  19.0 4.8 collective-permute-done.13.refs_2_
  38.4 4.1 collective-permute-done.27.refs_1_
  42.6 3.7 collective-permute-done.28.refs_2_
  59.3 3.1 collective-permute-done.2
  65.6 15.1 %collective-permute-done.3 = bf16[1,8,14,64]{3,2,1,0:T(8,128)(2,1)S(1)} collective-permute-done((bf16[1,8,14,64]{3,2,1,0:T(8,128)(2,1)S(1)}, bf16[1,8,14,64]{3,2,1,0:T(8,128)(2,1)S(1)}, u32[]{:S(2)}, u32[]{:S(2)}) %collective-permute-start.3) | collective-permute-done | bytes 14368 | tf_op jit(solution)/shard_map/ppermute | solution.py:24
  81.8 3.4 collective-permute-done.4
  99.2 3.0 constant_dynamic-update-slice_fusion.2
  107.7 18.9 %mixes.2 = (bf16[1536,2048]{1,0:T(8,128)(2,1)}, bf16[1536,2048]{1,0:T(8,128)(2,1)}, bf16[1536,2048]{1,0:T(8,128)(2,1)}, bf16[1536,2048]{1,0:T(8,128)(2,1)}, bf16[1536,2048]{1,0:T(8,128)(2,1)}) custom-call(s32[1]{0:T(128)} %bitcast.here, bf16[1536,2048]{1,0:T(8,128)(2,1)} %constant_dynamic-update-slice_fusion.x_ref, ...), custom_call_target="tpu_custom_call" | custom-call | tf_op jit(solution)/shard_map/mixes/pallas_call | solution.py:93
  126.7 8.2 convolution_convert_fusion.8.v_ref
  134.8 4.5 convolution_convert_fusion.9.k_ref
  139.4 3.5 convolution_convert_fusion.10.r_ref
  142.9 13.5 %wkv_forward.1 = (f32[1536,512]{1,0:T(8,128)}, bf16[12,512,128]{2,1,0:T(8,128)(2,1)S(1)}) custom-call(s32[1]{0:T(128)} %bitcast.here, bf16[1536,512]{1,0:T(8,128)(2,1)S(1)} %convolution_convert_fusion.10.r_ref, bf16[1536,512]{1,0:T(8,128)(2,1)} %convolution_convert_fusion.9.k_ref, bf16[1536,512]{1,0:T(8,128)(2,1)} %convolution_convert_fusion.8.v_ref, ...), custom_call_target="tpu_custom_call" | custom-call | tf_op jit(solution)/shard_map/wkv_forward/pallas_call | solution.py:93
  159.2 10.3 %gate.1 = (f32[1536,512]{1,0:T(8,128)S(1)}, bf16[1536,512]{1,0:T(8,128)(2,1)S(1)}) custom-call(s32[1]{0:T(128)} %bitcast.here, bf16[1536,2048]{1,0:T(8,128)(2,1)} %get-tuple-element.59.refs_0_, bf16[2048,1024]{1,0:T(8,128)(2,1)} %all-gather.6.cloned.1.call-done.refs_1_.refs_3_.refs_7_, f32[1536,512]{1,0:T(8,128)} %get-tuple-element.71.refs_2_.wkv_ref, ...), custom_call_target="tpu_custom_call" | custom-call | tf_op jit(solution)/shard_map/gate/pallas_call | solution.py:93
  179.7 11.1 %collective-permute-done.17 = bf16[192,2048]{1,0:T(8,128)(2,1)S(1)} collective-permute-done((bf16[192,2048]{1,0:T(8,128)(2,1)S(1)}, bf16[192,2048]{1,0:T(8,128)(2,1)S(1)}, u32[]{:S(2)}, u32[]{:S(2)}) %collective-permute-start.17) | collective-permute-done | bytes 786464 | tf_op jit(solution)/shard_map/ppermute | solution.py:24
  201.7 28.3 %collective-permute-done.18.refs_2_ = bf16[384,2048]{1,0:T(8,128)(2,1)} collective-permute-done((bf16[384,2048]{1,0:T(8,128)(2,1)}, bf16[384,2048]{1,0:T(8,128)(2,1)}, u32[]{:S(2)}, u32[]{:S(2)}) %collective-permute-start.18) | collective-permute-done | bytes 1572896 | tf_op jit(solution)/shard_map/ppermute | solution.py:24
  230.0 3.0 collective-permute-done.16.refs_1_
  233.0 5.5 after_norm.1
  243.8 22.9 %collective-permute-done.23 = bf16[384,2048]{1,0:T(8,128)(2,1)} collective-permute-done((bf16[384,2048]{1,0:T(8,128)(2,1)}, bf16[384,2048]{1,0:T(8,128)(2,1)}, u32[]{:S(2)}, u32[]{:S(2)}) %collective-permute-start.23) | collective-permute-done | bytes 1572896 | tf_op jit(solution)/shard_map/ppermute | solution.py:24
  273.0 27.4 %collective-permute-done.19 = bf16[384,2048]{1,0:T(8,128)(2,1)} collective-permute-done((bf16[384,2048]{1,0:T(8,128)(2,1)}, bf16[384,2048]{1,0:T(8,128)(2,1)}, u32[]{:S(2)}, u32[]{:S(2)}) %collective-permute-start.19) | collective-permute-done | bytes 1572896 | tf_op jit(solution)/shard_map/ppermute | solution.py:24
  309.8 17.0 %collective-permute-done.21 = bf16[192,2048]{1,0:T(8,128)(2,1)S(1)} collective-permute-done((bf16[192,2048]{1,0:T(8,128)(2,1)S(1)}, bf16[192,2048]{1,0:T(8,128)(2,1)S(1)}, u32[]{:S(2)}, u32[]{:S(2)}) %collective-permute-start.21) | collective-permute-done | bytes 786464 | tf_op jit(solution)/shard_map/ppermute | solution.py:24
  331.1 14.4 %mixes.3 = (bf16[1536,2048]{1,0:T(8,128)(2,1)}, bf16[1536,2048]{1,0:T(8,128)(2,1)}, bf16[1536,2048]{1,0:T(8,128)(2,1)}) custom-call(s32[1]{0:T(128)} %bitcast.here, bf16[1536,2048]{1,0:T(8,128)(2,1)} %copy-done.30, f32[1536,128]{1,0:T(8,128)S(1)} %pad.30.marks_ref.rows_ref.refs_5_.refs_9_, f32[8,2048]{1,0:T(8,128)S(1)} %get-tuple-element.163.vec_ref), custom_call_target="tpu_custom_call" | custom-call | tf_op jit(solution)/shard_map/mixes/pallas_call | solution.py:93
  345.5 8.0 divide_convert_fusion
  355.5 22.6 %multiply_convert_fusion.1 = (bf16[1536,1792]{1,0:T(8,128)(2,1)}, f32[1536,1792]{1,0:T(8,128)}) fusion(bf16[1536,2048]{1,0:T(8,128)(2,1)} %get-tuple-element.76, bf16[2048,1792]{1,0:T(8,128)(2,1)} %all-gather.12.cloned.1.call-done.refs_2_), kind=kOutput, calls=%fused_computation.2 | convolution fusion | flops 11296309248 | bytes 30146560 | tf_op jit(solution)/shard_map/dot_general | solution.py:439
  378.2 6.0 value_columns.6
  387.4 2.8 constant_dynamic-update-slice_fusion.12
  396.2 6.0 value_columns.7
  402.2 6.6 value_columns.5
  408.9 6.0 value_columns.4.refs_0_
  424.6 12.4 %collective-permute-done.39 = bf16[768,512]{1,0:T(8,128)(2,1)S(1)} collective-permute-done((bf16[768,512]{1,0:T(8,128)(2,1)S(1)}, bf16[768,512]{1,0:T(8,128)(2,1)S(1)}, u32[]{:S(2)}, u32[]{:S(2)}) %collective-permute-start.39) | collective-permute-done | bytes 786464 | tf_op jit(solution)/shard_map/ppermute | solution.py:24
  439.8 7.8 spread_columns.3
  447.6 25.3 %multiply_convert_fusion.refs_0_ = bf16[1536,1792]{1,0:T(8,128)(2,1)} fusion(f32[1536,1792]{1,0:T(8,128)} %get-tuple-element.176, bf16[1536,2048]{1,0:T(8,128)(2,1)} %spread_columns.3, bf16[1792,2048]{1,0:T(8,128)(2,1)} %all-gather.14.cloned.1.call-done.right_ref), kind=kOutput, calls=%fused_computation.1 | convolution fusion | flops 11310071808 | bytes 30146560 | tf_op jit(solution)/shard_map/dot_general | solution.py:439
  472.9 15.8 %convolution_convert_fusion.1 = bf16[2048,1792]{1,0:T(8,128)(2,1)S(1)} fusion(bf16[1536,2048]{1,0:T(8,128)(2,1)} %get-tuple-element.76, bf16[1536,1792]{1,0:T(8,128)(2,1)} %multiply_convert_fusion.refs_0_), kind=kOutput, calls=%fused_computation.6 | convolution fusion | flops 11277959168 | bytes 19136512 | tf_op jit(solution)/shard_map/dot_general | solution.py:439
  488.7 4.6 channel.1
  493.3 7.8 convolution_convert_fusion.2
  501.1 4.6 pad_maximum_fusion
  507.2 29.1 %mixes_back.2 = (bf16[1536,2048]{1,0:T(8,128)(2,1)}, f32[8,2048]{1,0:T(8,128)S(1)}) custom-call(s32[1]{0:T(128)} %bitcast.here, bf16[1536,1792]{1,0:T(8,128)(2,1)} %multiply_convert_fusion.refs_0_, bf16[1536,512]{1,0:T(8,128)(2,1)S(1)} %copy-done.14, bf16[2048,1792]{1,0:T(8,128)(2,1)} %all-gather.12.cloned.1.call-done.refs_2_, ...), custom_call_target="tpu_custom_call" | custom-call | tf_op jit(solution)/shard_map/mixes_back/pallas_call | solution.py:93
  542.6 16.7 %collective-permute-done.41 = bf16[192,2048]{1,0:T(8,128)(2,1)S(1)} collective-permute-done((bf16[192,2048]{1,0:T(8,128)(2,1)S(1)}, bf16[192,2048]{1,0:T(8,128)(2,1)S(1)}, u32[]{:S(2)}, u32[]{:S(2)}) %collective-permute-start.41) | collective-permute-done | bytes 786464 | tf_op jit(solution)/shard_map/ppermute | solution.py:24
  564.6 22.0 %collective-permute-done.44.refs_2_ = bf16[384,2048]{1,0:T(8,128)(2,1)S(1)} collective-permute-done((bf16[384,2048]{1,0:T(8,128)(2,1)S(1)}, bf16[384,2048]{1,0:T(8,128)(2,1)S(1)}, u32[]{:S(2)}, u32[]{:S(2)}) %collective-permute-start.44) | collective-permute-done | bytes 1572896 | tf_op jit(solution)/shard_map/ppermute | solution.py:24
  589.5 7.0 norm_back.2
  599.0 2.9 collective-permute-start.46
  601.9 23.9 %collective-permute-done.45 = bf16[384,2048]{1,0:T(8,128)(2,1)S(1)} collective-permute-done((bf16[384,2048]{1,0:T(8,128)(2,1)S(1)}, bf16[384,2048]{1,0:T(8,128)(2,1)S(1)}, u32[]{:S(2)}, u32[]{:S(2)}) %collective-permute-start.45) | collective-permute-done | bytes 1572896 | tf_op jit(solution)/shard_map/ppermute | solution.py:24
  625.8 3.0 collective-permute-start.47
  631.3 7.5 collective-permute-done.47
  641.0 5.2 fusion.21.d_mixed_ref
  646.2 37.1 %wkv_backward.1 = (bf16[1536,512]{1,0:T(8,128)(2,1)S(1)}, bf16[1536,512]{1,0:T(8,128)(2,1)S(1)}, bf16[1536,512]{1,0:T(8,128)(2,1)}, bf16[1536,512]{1,0:T(8,128)(2,1)}, f32[8,512]{1,0:T(8,128)S(1)}) custom-call(s32[1]{0:T(128)} %bitcast.here, bf16[1536,512]{1,0:T(8,128)(2,1)} %copy-done.2, bf16[1536,512]{1,0:T(8,128)(2,1)} %convolution_convert_fusion.9.k_ref, ...), custom_call_target="tpu_custom_call" | custom-call | tf_op jit(solution)/shard_map/wkv_backward/pallas_call | solution.py:93
  683.3 7.8 convolution_convert_fusion.7
  691.2 7.0 convolution_convert_fusion.6
  698.3 3.7 convolution_convert_fusion.5
  702.0 3.7 convolution_convert_fusion.4
  705.8 4.0 pad_maximum_fusion.1
  709.8 8.1 convolution_convert_fusion.3
  718.0 17.5 %convolution_convert_fusion = bf16[1792,2048]{1,0:T(8,128)(2,1)} fusion(bf16[1536,1792]{1,0:T(8,128)(2,1)} %get-tuple-element.175.left_ref, bf16[1536,2048]{1,0:T(8,128)(2,1)} %spread_columns.3), kind=kOutput, calls=%fused_computation.5 | convolution fusion | flops 11277959168 | bytes 19136512 | tf_op jit(solution)/shard_map/dot_general | solution.py:439
  740.5 26.4 %mixes_back.3 = (bf16[1536,2048]{1,0:T(8,128)(2,1)}, f32[8,2048]{1,0:T(8,128)S(1)}) custom-call(s32[1]{0:T(128)} %bitcast.here, bf16[1536,512]{1,0:T(8,128)(2,1)S(1)} %copy-done.7, bf16[1536,512]{1,0:T(8,128)(2,1)S(1)} %copy-done.9, bf16[1536,512]{1,0:T(8,128)(2,1)S(1)} %copy-done.11, bf16[1536,512]{1,0:T(8,128)(2,1)} %get-tuple-element.92.refs_3_, ...), custom_call_target="tpu_custom_call" | custom-call | tf_op jit(solution)/shard_map/mixes_back/pallas_call | solution.py:93
  771.3 18.3 %collective-permute-done.49 = bf16[192,2048]{1,0:T(8,128)(2,1)S(1)} collective-permute-done((bf16[192,2048]{1,0:T(8,128)(2,1)S(1)}, bf16[192,2048]{1,0:T(8,128)(2,1)S(1)}, u32[]{:S(2)}, u32[]{:S(2)}) %collective-permute-start.49) | collective-permute-done | bytes 786464 | tf_op jit(solution)/shard_map/ppermute | solution.py:24
  801.5 14.5 %collective-permute-done.52.refs_2_ = bf16[384,2048]{1,0:T(8,128)(2,1)} collective-permute-done((bf16[384,2048]{1,0:T(8,128)(2,1)}, bf16[384,2048]{1,0:T(8,128)(2,1)}, u32[]{:S(2)}, u32[]{:S(2)}) %collective-permute-start.52) | collective-permute-done | bytes 1572896 | tf_op jit(solution)/shard_map/ppermute | solution.py:24
  818.9 7.2 norm_back.3
  827.8 8.8 collective-permute-done.59
  837.2 3.8 collective-permute-done.60
  842.4 4.8 collective-permute-done.61
  859.3 5.7 collective-permute-done.35.refs_2_
  873.5 3.5 spread_columns.2
  880.1 35.6 %reduce-scatter.11.cloned.1.call-done = bf16[224,2048]{1,0:T(8,128)(2,1)} async-done(((bf16[1792,2048]{1,0:T(8,128)(2,1)}), bf16[224,2048]{1,0:T(8,128)(2,1)}) %reduce-scatter.11.cloned.1.call-update) | async-done | bytes 917520 | tf_op jit(solution)/shard_map/reduce_scatter | solution.py:669
  (424 shorter events, 210.9 us)
Async XLA Ops:
  7.2 119.4 %all-gather.8.cloned.1.call-start = ((), (), s32[]{:S(2)}) async-start(), calls=%async_computation.5 | async-start | bytes 7077888 | tf_op jit(solution)/shard_map/all_gather | solution.py:659
  10.3 8.7 collective-permute-start.12
  13.3 10.6 %collective-permute-start.13 = (bf16[64,1536]{1,0:T(8,128)(2,1)S(1)}, bf16[64,1536]{1,0:T(8,128)(2,1)S(1)}, u32[]{:S(2)}, u32[]{:S(2)}) collective-permute-start(bf16[64,1536]{1,0:T(8,128)(2,1)S(1)} %get-tuple-element.67), channel_id=1, source_target_pairs={{0,16},{8,24},{16,0},{24,8},{1,17},{9,25},{17,1},{25,9},{2,18},{10... | collective-permute-start | bytes 589832 | tf_op jit(solution)/shard_map/ppermute | solution.py:24
  14.8 9.1 collective-permute-start.14
  24.8 134.4 %all-gather.6.cloned.1.call-start = ((), (), s32[]{:S(2)}) async-start(), calls=%async_computation.4 | async-start | bytes 4718592 | tf_op jit(solution)/shard_map/all_gather | solution.py:659
  34.0 138.3 %all-gather.10.cloned.1.call-start = ((), (), s32[]{:S(2)}) async-start(), calls=%async_computation.6 | async-start | bytes 2359296 | tf_op jit(solution)/shard_map/all_gather | solution.py:679
  34.8 320.8 %all-gather.12.cloned.1.call-start = ((), (), s32[]{:S(2)}) async-start(), calls=%async_computation.7 | async-start | bytes 8257536 | tf_op jit(solution)/shard_map/all_gather | solution.py:659
  34.9 7.7 collective-permute-start.27
  36.4 9.9 %collective-permute-start.28 = (bf16[64,1792]{1,0:T(8,128)(2,1)S(1)}, bf16[64,1792]{1,0:T(8,128)(2,1)S(1)}, u32[]{:S(2)}, u32[]{:S(2)}) collective-permute-start(bf16[64,1792]{1,0:T(8,128)(2,1)S(1)} %get-tuple-element.79), channel_id=1, source_target_pairs={{0,16},{8,24},{16,0},{24,8},{1,17},{9,25},{17,1},{25,9},{2,18},{10... | collective-permute-start | bytes 688136 | tf_op jit(solution)/shard_map/ppermute | solution.py:24
  37.0 9.3 collective-permute-start.29
  47.3 330.8 %all-gather.14.cloned.1.call-start = ((), (), s32[]{:S(2)}) async-start(), calls=%async_computation.8 | async-start | bytes 8257536 | tf_op jit(solution)/shard_map/all_gather | solution.py:682
  47.4 37.8 %collective-permute-start.5 = (bf16[384,2048]{1,0:T(8,128)(2,1)S(1)}, bf16[384,2048]{1,0:T(8,128)(2,1)}, u32[]{:S(2)}, u32[]{:S(2)}) collective-permute-start(bf16[384,2048]{1,0:T(8,128)(2,1)S(1)} %bitcast.91), channel_id=1, source_target_pairs={{0,8},{8,0},{16,24},{24,16},{1,9},{9,1},{17,25},{25,17},{2,10},{10... | collective-permute-start | bytes 4718600 | tf_op jit(solution)/shard_map/ppermute | solution.py:24
  47.8 40.3 %collective-permute-start.6 = (bf16[384,2048]{1,0:T(8,128)(2,1)S(1)}, bf16[384,2048]{1,0:T(8,128)(2,1)}, u32[]{:S(2)}, u32[]{:S(2)}) collective-permute-start(bf16[384,2048]{1,0:T(8,128)(2,1)S(1)} %bitcast.92), channel_id=1, source_target_pairs={{0,16},{8,24},{16,0},{24,8},{1,17},{9,25},{17,1},{25,9},{2,18},{10... | collective-permute-start | bytes 4718600 | tf_op jit(solution)/shard_map/ppermute | solution.py:24
  49.4 804.5 %reduce-scatter.9.cloned.1.call-start = ((), (), s32[]{:S(2)}) async-start(), calls=%async_computation.11 | async-start | bytes 10616832 | tf_op jit(solution)/shard_map/reduce_scatter | solution.py:663
  55.6 6.9 collective-permute-start.2
  62.5 18.3 %collective-permute-start.3 = (bf16[1,8,14,64]{3,2,1,0:T(8,128)(2,1)S(1)}, bf16[1,8,14,64]{3,2,1,0:T(8,128)(2,1)S(1)}, u32[]{:S(2)}, u32[]{:S(2)}) collective-permute-start(bf16[1,8,14,64]{3,2,1,0:T(8,128)(2,1)S(1)} %get-tuple-element.159), channel_id=1, source_target_pairs={{0,8},{8,0},{16,24},{24,16},{1,9},{9,1},{17,25},{25,17},{2,10},{10... | collective-permute-start | bytes 43016 | tf_op jit(solution)/shard_map/ppermute | solution.py:24
  87.3 15.3 %collective-permute-start.7 = (bf16[192,2048]{1,0:T(8,128)(2,1)}, bf16[192,2048]{1,0:T(8,128)(2,1)}, u32[]{:S(2)}, u32[]{:S(2)}) collective-permute-start(bf16[192,2048]{1,0:T(8,128)(2,1)} %slice.420), channel_id=1, source_target_pairs={{0,16},{8,24},{16,0},{24,8},{1,17},{9,25},{17,1},{25,9},{2,18},{10... | collective-permute-start | bytes 2359304 | tf_op jit(solution)/shard_map/ppermute | solution.py:24
  90.2 15.4 %collective-permute-start.8 = (bf16[192,2048]{1,0:T(8,128)(2,1)}, bf16[192,2048]{1,0:T(8,128)(2,1)}, u32[]{:S(2)}, u32[]{:S(2)}) collective-permute-start(bf16[192,2048]{1,0:T(8,128)(2,1)} %slice.421), channel_id=1, source_target_pairs={{0,8},{8,0},{16,24},{24,16},{1,9},{9,1},{17,25},{25,17},{2,10},{10... | collective-permute-start | bytes 2359304 | tf_op jit(solution)/shard_map/ppermute | solution.py:24
  175.3 15.5 %collective-permute-start.17 = (bf16[192,2048]{1,0:T(8,128)(2,1)S(1)}, bf16[192,2048]{1,0:T(8,128)(2,1)S(1)}, u32[]{:S(2)}, u32[]{:S(2)}) collective-permute-start(bf16[192,2048]{1,0:T(8,128)(2,1)S(1)} %get-tuple-element.130), channel_id=1, source_target_pairs={{0,8},{8,0},{16,24},{24,16},{1,9},{9,1},{17,25},{25,17},{2,10},{10... | collective-permute-start | bytes 2359304 | tf_op jit(solution)/shard_map/ppermute | solution.py:24
  177.1 16.7 %collective-permute-start.15 = (bf16[192,2048]{1,0:T(8,128)(2,1)S(1)}, bf16[192,2048]{1,0:T(8,128)(2,1)S(1)}, u32[]{:S(2)}, u32[]{:S(2)}) collective-permute-start(bf16[192,2048]{1,0:T(8,128)(2,1)S(1)} %get-tuple-element.131), channel_id=1, source_target_pairs={{0,16},{8,24},{16,0},{24,8},{1,17},{9,25},{17,1},{25,9},{2,18},{10... | collective-permute-start | bytes 2359304 | tf_op jit(solution)/shard_map/ppermute | solution.py:24
  192.4 37.6 %collective-permute-start.18 = (bf16[384,2048]{1,0:T(8,128)(2,1)}, bf16[384,2048]{1,0:T(8,128)(2,1)}, u32[]{:S(2)}, u32[]{:S(2)}) collective-permute-start(bf16[384,2048]{1,0:T(8,128)(2,1)} %pad_maximum_fusion.3), channel_id=1, source_target_pairs={{0,16},{8,24},{16,0},{24,8},{1,17},{9,25},{17,1},{25,9},{2,18},{10... | collective-permute-start | bytes 4718600 | tf_op jit(solution)/shard_map/ppermute | solution.py:24
  195.3 37.7 %collective-permute-start.16 = (bf16[384,2048]{1,0:T(8,128)(2,1)}, bf16[384,2048]{1,0:T(8,128)(2,1)}, u32[]{:S(2)}, u32[]{:S(2)}) collective-permute-start(bf16[384,2048]{1,0:T(8,128)(2,1)} %pad_maximum_fusion.2), channel_id=1, source_target_pairs={{0,8},{8,0},{16,24},{24,16},{1,9},{9,1},{17,25},{25,17},{2,10},{10... | collective-permute-start | bytes 4718600 | tf_op jit(solution)/shard_map/ppermute | solution.py:24
  196.8 69.8 %collective-permute-start.23 = (bf16[384,2048]{1,0:T(8,128)(2,1)}, bf16[384,2048]{1,0:T(8,128)(2,1)}, u32[]{:S(2)}, u32[]{:S(2)}) collective-permute-start(bf16[384,2048]{1,0:T(8,128)(2,1)} %bitcast.11.base_ref), channel_id=1, source_target_pairs={{0,8},{8,0},{16,24},{24,16},{1,9},{9,1},{17,25},{25,17},{2,10},{10... | collective-permute-start | bytes 4718600 | tf_op jit(solution)/shard_map/ppermute | solution.py:24
  197.3 72.2 %collective-permute-start.24 = (bf16[384,2048]{1,0:T(8,128)(2,1)}, bf16[384,2048]{1,0:T(8,128)(2,1)}, u32[]{:S(2)}, u32[]{:S(2)}) collective-permute-start(bf16[384,2048]{1,0:T(8,128)(2,1)} %bitcast.11.base_ref), channel_id=1, source_target_pairs={{0,16},{8,24},{16,0},{24,8},{1,17},{9,25},{17,1},{25,9},{2,18},{10... | collective-permute-start | bytes 4718600 | tf_op jit(solution)/shard_map/ppermute | solution.py:24
  238.5 61.9 %collective-permute-start.19 = (bf16[384,2048]{1,0:T(8,128)(2,1)}, bf16[384,2048]{1,0:T(8,128)(2,1)}, u32[]{:S(2)}, u32[]{:S(2)}) collective-permute-start(bf16[384,2048]{1,0:T(8,128)(2,1)} %get-tuple-element.74), channel_id=1, source_target_pairs={{0,8},{8,0},{16,24},{24,16},{1,9},{9,1},{17,25},{25,17},{2,10},{10... | collective-permute-start | bytes 4718600 | tf_op jit(solution)/shard_map/ppermute | solution.py:24
  240.0 62.4 %collective-permute-start.20 = (bf16[384,2048]{1,0:T(8,128)(2,1)}, bf16[384,2048]{1,0:T(8,128)(2,1)}, u32[]{:S(2)}, u32[]{:S(2)}) collective-permute-start(bf16[384,2048]{1,0:T(8,128)(2,1)} %get-tuple-element.74), channel_id=1, source_target_pairs={{0,16},{8,24},{16,0},{24,8},{1,17},{9,25},{17,1},{25,9},{2,18},{10... | collective-permute-start | bytes 4718600 | tf_op jit(solution)/shard_map/ppermute | solution.py:24
  268.8 121.5 %collective-permute-start.25 = (bf16[192,2048]{1,0:T(8,128)(2,1)}, bf16[192,2048]{1,0:T(8,128)(2,1)}, u32[]{:S(2)}, u32[]{:S(2)}) collective-permute-start(bf16[192,2048]{1,0:T(8,128)(2,1)} %slice.448), channel_id=1, source_target_pairs={{0,16},{8,24},{16,0},{24,8},{1,17},{9,25},{17,1},{25,9},{2,18},{10... | collective-permute-start | bytes 2359304 | tf_op jit(solution)/shard_map/ppermute | solution.py:24
  271.7 122.4 %collective-permute-start.26 = (bf16[192,2048]{1,0:T(8,128)(2,1)}, bf16[192,2048]{1,0:T(8,128)(2,1)}, u32[]{:S(2)}, u32[]{:S(2)}) collective-permute-start(bf16[192,2048]{1,0:T(8,128)(2,1)} %slice.449), channel_id=1, source_target_pairs={{0,8},{8,0},{16,24},{24,16},{1,9},{9,1},{17,25},{25,17},{2,10},{10... | collective-permute-start | bytes 2359304 | tf_op jit(solution)/shard_map/ppermute | solution.py:24
  301.6 25.2 %collective-permute-start.21 = (bf16[192,2048]{1,0:T(8,128)(2,1)S(1)}, bf16[192,2048]{1,0:T(8,128)(2,1)S(1)}, u32[]{:S(2)}, u32[]{:S(2)}) collective-permute-start(bf16[192,2048]{1,0:T(8,128)(2,1)S(1)} %slice.441), channel_id=1, source_target_pairs={{0,16},{8,24},{16,0},{24,8},{1,17},{9,25},{17,1},{25,9},{2,18},{10... | collective-permute-start | bytes 2359304 | tf_op jit(solution)/shard_map/ppermute | solution.py:24
  303.7 24.8 %collective-permute-start.22 = (bf16[192,2048]{1,0:T(8,128)(2,1)S(1)}, bf16[192,2048]{1,0:T(8,128)(2,1)S(1)}, u32[]{:S(2)}, u32[]{:S(2)}) collective-permute-start(bf16[192,2048]{1,0:T(8,128)(2,1)S(1)} %slice.442), channel_id=1, source_target_pairs={{0,8},{8,0},{16,24},{24,16},{1,9},{9,1},{17,25},{25,17},{2,10},{10... | collective-permute-start | bytes 2359304 | tf_op jit(solution)/shard_map/ppermute | solution.py:24
  353.5 61.7 %collective-permute-start.37 = (bf16[1536,512]{1,0:T(8,128)(2,1)}, bf16[1536,512]{1,0:T(8,128)(2,1)}, u32[]{:S(2)}, u32[]{:S(2)}) collective-permute-start(bf16[1536,512]{1,0:T(8,128)(2,1)} %get-tuple-element.177.refs_0_), channel_id=1, source_target_pairs={{0,8},{8,0},{16,24},{24,16},{1,9},{9,1},{17,25},{25,17},{2,10},{10... | collective-permute-start | bytes 4718600 | tf_op jit(solution)/shard_map/ppermute | solution.py:24
  355.2 61.6 %collective-permute-start.38 = (bf16[1536,512]{1,0:T(8,128)(2,1)}, bf16[1536,512]{1,0:T(8,128)(2,1)}, u32[]{:S(2)}, u32[]{:S(2)}) collective-permute-start(bf16[1536,512]{1,0:T(8,128)(2,1)} %get-tuple-element.177.refs_0_), channel_id=1, source_target_pairs={{0,16},{8,24},{16,0},{24,8},{1,17},{9,25},{17,1},{25,9},{2,18},{10... | collective-permute-start | bytes 4718600 | tf_op jit(solution)/shard_map/ppermute | solution.py:24
  384.3 30.6 %collective-permute-start.32 = (bf16[768,512]{1,0:T(8,128)(2,1)S(1)}, bf16[768,512]{1,0:T(8,128)(2,1)S(1)}, u32[]{:S(2)}, u32[]{:S(2)}) collective-permute-start(bf16[768,512]{1,0:T(8,128)(2,1)S(1)} %get-tuple-element.128), channel_id=1, source_target_pairs={{0,8},{8,0},{16,24},{24,16},{1,9},{9,1},{17,25},{25,17},{2,10},{10... | collective-permute-start | bytes 2359304 | tf_op jit(solution)/shard_map/ppermute | solution.py:24
  392.4 30.5 %collective-permute-start.30 = (bf16[768,512]{1,0:T(8,128)(2,1)S(1)}, bf16[768,512]{1,0:T(8,128)(2,1)S(1)}, u32[]{:S(2)}, u32[]{:S(2)}) collective-permute-start(bf16[768,512]{1,0:T(8,128)(2,1)S(1)} %get-tuple-element.129), channel_id=1, source_target_pairs={{0,16},{8,24},{16,0},{24,8},{1,17},{9,25},{17,1},{25,9},{2,18},{10... | collective-permute-start | bytes 2359304 | tf_op jit(solution)/shard_map/ppermute | solution.py:24
  416.5 20.5 %collective-permute-start.39 = (bf16[768,512]{1,0:T(8,128)(2,1)S(1)}, bf16[768,512]{1,0:T(8,128)(2,1)S(1)}, u32[]{:S(2)}, u32[]{:S(2)}) collective-permute-start(bf16[768,512]{1,0:T(8,128)(2,1)S(1)} %slice.456), channel_id=1, source_target_pairs={{0,16},{8,24},{16,0},{24,8},{1,17},{9,25},{17,1},{25,9},{2,18},{10... | collective-permute-start | bytes 2359304 | tf_op jit(solution)/shard_map/ppermute | solution.py:24
  418.0 20.5 %collective-permute-start.40 = (bf16[768,512]{1,0:T(8,128)(2,1)S(1)}, bf16[768,512]{1,0:T(8,128)(2,1)S(1)}, u32[]{:S(2)}, u32[]{:S(2)}) collective-permute-start(bf16[768,512]{1,0:T(8,128)(2,1)S(1)} %slice.457), channel_id=1, source_target_pairs={{0,8},{8,0},{16,24},{24,16},{1,9},{9,1},{17,25},{25,17},{2,10},{10... | collective-permute-start | bytes 2359304 | tf_op jit(solution)/shard_map/ppermute | solution.py:24
  421.2 67.5 %collective-permute-start.33 = (bf16[1536,512]{1,0:T(8,128)(2,1)}, bf16[1536,512]{1,0:T(8,128)(2,1)}, u32[]{:S(2)}, u32[]{:S(2)}) collective-permute-start(bf16[1536,512]{1,0:T(8,128)(2,1)} %pad_maximum_fusion.5), channel_id=1, source_target_pairs={{0,16},{8,24},{16,0},{24,8},{1,17},{9,25},{17,1},{25,9},{2,18},{10... | collective-permute-start | bytes 4718600 | tf_op jit(solution)/shard_map/ppermute | solution.py:24
  424.4 64.3 %collective-permute-start.31 = (bf16[1536,512]{1,0:T(8,128)(2,1)}, bf16[1536,512]{1,0:T(8,128)(2,1)}, u32[]{:S(2)}, u32[]{:S(2)}) collective-permute-start(bf16[1536,512]{1,0:T(8,128)(2,1)} %pad_maximum_fusion.4), channel_id=1, source_target_pairs={{0,8},{8,0},{16,24},{24,16},{1,9},{9,1},{17,25},{25,17},{2,10},{10... | collective-permute-start | bytes 4718600 | tf_op jit(solution)/shard_map/ppermute | solution.py:24
  505.7 361.1 %reduce-scatter.5.cloned.1.call-start = ((), (), s32[]{:S(2)}) async-start(), calls=%async_computation.9 | async-start | bytes 9437184 | tf_op jit(solution)/shard_map/reduce_scatter | solution.py:663
  538.7 20.7 %collective-permute-start.41 = (bf16[192,2048]{1,0:T(8,128)(2,1)S(1)}, bf16[192,2048]{1,0:T(8,128)(2,1)S(1)}, u32[]{:S(2)}, u32[]{:S(2)}) collective-permute-start(bf16[192,2048]{1,0:T(8,128)(2,1)S(1)} %get-tuple-element.122), channel_id=1, source_target_pairs={{0,16},{8,24},{16,0},{24,8},{1,17},{9,25},{17,1},{25,9},{2,18},{10... | collective-permute-start | bytes 2359304 | tf_op jit(solution)/shard_map/ppermute | solution.py:24
  540.9 20.5 %collective-permute-start.43 = (bf16[192,2048]{1,0:T(8,128)(2,1)S(1)}, bf16[192,2048]{1,0:T(8,128)(2,1)S(1)}, u32[]{:S(2)}, u32[]{:S(2)}) collective-permute-start(bf16[192,2048]{1,0:T(8,128)(2,1)S(1)} %get-tuple-element.120), channel_id=1, source_target_pairs={{0,8},{8,0},{16,24},{24,16},{1,9},{9,1},{17,25},{25,17},{2,10},{10... | collective-permute-start | bytes 2359304 | tf_op jit(solution)/shard_map/ppermute | solution.py:24
  562.1 24.5 %collective-permute-start.44 = (bf16[384,2048]{1,0:T(8,128)(2,1)S(1)}, bf16[384,2048]{1,0:T(8,128)(2,1)S(1)}, u32[]{:S(2)}, u32[]{:S(2)}) collective-permute-start(bf16[384,2048]{1,0:T(8,128)(2,1)S(1)} %pad_maximum_fusion.8), channel_id=1, source_target_pairs={{0,16},{8,24},{16,0},{24,8},{1,17},{9,25},{17,1},{25,9},{2,18},{10... | collective-permute-start | bytes 4718600 | tf_op jit(solution)/shard_map/ppermute | solution.py:24
  562.3 26.0 %collective-permute-start.42 = (bf16[384,2048]{1,0:T(8,128)(2,1)S(1)}, bf16[384,2048]{1,0:T(8,128)(2,1)S(1)}, u32[]{:S(2)}, u32[]{:S(2)}) collective-permute-start(bf16[384,2048]{1,0:T(8,128)(2,1)S(1)} %pad_maximum_fusion.7), channel_id=1, source_target_pairs={{0,8},{8,0},{16,24},{24,16},{1,9},{9,1},{17,25},{25,17},{2,10},{10... | collective-permute-start | bytes 4718600 | tf_op jit(solution)/shard_map/ppermute | solution.py:24
  596.5 29.3 %collective-permute-start.45 = (bf16[384,2048]{1,0:T(8,128)(2,1)S(1)}, bf16[384,2048]{1,0:T(8,128)(2,1)S(1)}, u32[]{:S(2)}, u32[]{:S(2)}) collective-permute-start(bf16[384,2048]{1,0:T(8,128)(2,1)S(1)} %get-tuple-element.87), channel_id=1, source_target_pairs={{0,8},{8,0},{16,24},{24,16},{1,9},{9,1},{17,25},{25,17},{2,10},{10... | collective-permute-start | bytes 4718600 | tf_op jit(solution)/shard_map/ppermute | solution.py:24
  599.0 29.9 %collective-permute-start.46 = (bf16[384,2048]{1,0:T(8,128)(2,1)S(1)}, bf16[384,2048]{1,0:T(8,128)(2,1)S(1)}, u32[]{:S(2)}, u32[]{:S(2)}) collective-permute-start(bf16[384,2048]{1,0:T(8,128)(2,1)S(1)} %get-tuple-element.87), channel_id=1, source_target_pairs={{0,16},{8,24},{16,0},{24,8},{1,17},{9,25},{17,1},{25,9},{2,18},{10... | collective-permute-start | bytes 4718600 | tf_op jit(solution)/shard_map/ppermute | solution.py:24
  625.8 12.9 %collective-permute-start.47 = (bf16[192,2048]{1,0:T(8,128)(2,1)S(1)}, bf16[192,2048]{1,0:T(8,128)(2,1)S(1)}, u32[]{:S(2)}, u32[]{:S(2)}) collective-permute-start(bf16[192,2048]{1,0:T(8,128)(2,1)S(1)} %slice.459), channel_id=1, source_target_pairs={{0,16},{8,24},{16,0},{24,8},{1,17},{9,25},{17,1},{25,9},{2,18},{10... | collective-permute-start | bytes 2359304 | tf_op jit(solution)/shard_map/ppermute | solution.py:24
  628.9 12.1 %collective-permute-start.48 = (bf16[192,2048]{1,0:T(8,128)(2,1)S(1)}, bf16[192,2048]{1,0:T(8,128)(2,1)S(1)}, u32[]{:S(2)}, u32[]{:S(2)}) collective-permute-start(bf16[192,2048]{1,0:T(8,128)(2,1)S(1)} %slice.460), channel_id=1, source_target_pairs={{0,8},{8,0},{16,24},{24,16},{1,9},{9,1},{17,25},{25,17},{2,10},{10... | collective-permute-start | bytes 2359304 | tf_op jit(solution)/shard_map/ppermute | solution.py:24
  709.8 168.5 %reduce-scatter.7.cloned.1.call-start = ((), (), s32[]{:S(2)}) async-start(), calls=%async_computation.10 | async-start | bytes 2359296 | tf_op jit(solution)/shard_map/reduce_scatter | solution.py:669
  717.9 197.8 %reduce-scatter.11.cloned.1.call-start = ((), (), s32[]{:S(2)}) async-start(), calls=%async_computation.12 | async-start | bytes 8257536 | tf_op jit(solution)/shard_map/reduce_scatter | solution.py:669
  769.0 20.5 %collective-permute-start.49 = (bf16[192,2048]{1,0:T(8,128)(2,1)S(1)}, bf16[192,2048]{1,0:T(8,128)(2,1)S(1)}, u32[]{:S(2)}, u32[]{:S(2)}) collective-permute-start(bf16[192,2048]{1,0:T(8,128)(2,1)S(1)} %get-tuple-element.116), channel_id=1, source_target_pairs={{0,16},{8,24},{16,0},{24,8},{1,17},{9,25},{17,1},{25,9},{2,18},{10... | collective-permute-start | bytes 2359304 | tf_op jit(solution)/shard_map/ppermute | solution.py:24
  770.2 20.5 %collective-permute-start.51 = (bf16[192,2048]{1,0:T(8,128)(2,1)S(1)}, bf16[192,2048]{1,0:T(8,128)(2,1)S(1)}, u32[]{:S(2)}, u32[]{:S(2)}) collective-permute-start(bf16[192,2048]{1,0:T(8,128)(2,1)S(1)} %get-tuple-element.114), channel_id=1, source_target_pairs={{0,8},{8,0},{16,24},{24,16},{1,9},{9,1},{17,25},{25,17},{2,10},{10... | collective-permute-start | bytes 2359304 | tf_op jit(solution)/shard_map/ppermute | solution.py:24
  793.9 22.1 %collective-permute-start.52 = (bf16[384,2048]{1,0:T(8,128)(2,1)}, bf16[384,2048]{1,0:T(8,128)(2,1)}, u32[]{:S(2)}, u32[]{:S(2)}) collective-permute-start(bf16[384,2048]{1,0:T(8,128)(2,1)} %pad_maximum_fusion.10), channel_id=1, source_target_pairs={{0,16},{8,24},{16,0},{24,8},{1,17},{9,25},{17,1},{25,9},{2,18},{10... | collective-permute-start | bytes 4718600 | tf_op jit(solution)/shard_map/ppermute | solution.py:24
  796.0 21.4 %collective-permute-start.50 = (bf16[384,2048]{1,0:T(8,128)(2,1)}, bf16[384,2048]{1,0:T(8,128)(2,1)}, u32[]{:S(2)}, u32[]{:S(2)}) collective-permute-start(bf16[384,2048]{1,0:T(8,128)(2,1)} %pad_maximum_fusion.9), channel_id=1, source_target_pairs={{0,8},{8,0},{16,24},{24,16},{1,9},{9,1},{17,25},{25,17},{2,10},{10... | collective-permute-start | bytes 4718600 | tf_op jit(solution)/shard_map/ppermute | solution.py:24
  826.6 10.0 %collective-permute-start.59 = (f32[16,14,64]{2,1,0:T(8,128)S(1)}, f32[16,14,64]{2,1,0:T(8,128)S(1)}, u32[]{:S(2)}, u32[]{:S(2)}) collective-permute-start(f32[16,14,64]{2,1,0:T(8,128)S(1)} %bitcast.102), channel_id=1, source_target_pairs={{0,16},{8,24},{16,0},{24,8},{1,17},{9,25},{17,1},{25,9},{2,18},{10... | collective-permute-start | bytes 172040 | tf_op jit(solution)/shard_map/ppermute | solution.py:24
  850.3 8.1 collective-permute-start.34
  851.0 14.0 %collective-permute-start.35 = (bf16[384,512]{1,0:T(8,128)(2,1)}, bf16[384,512]{1,0:T(8,128)(2,1)}, u32[]{:S(2)}, u32[]{:S(2)}) collective-permute-start(bf16[384,512]{1,0:T(8,128)(2,1)} %get-tuple-element.125), channel_id=1, source_target_pairs={{0,16},{8,24},{16,0},{24,8},{1,17},{9,25},{17,1},{25,9},{2,18},{10... | collective-permute-start | bytes 1179656 | tf_op jit(solution)/shard_map/ppermute | solution.py:24
  851.4 17.7 %collective-permute-start.36 = (bf16[384,512]{1,0:T(8,128)(2,1)}, bf16[384,512]{1,0:T(8,128)(2,1)}, u32[]{:S(2)}, u32[]{:S(2)}) collective-permute-start(bf16[384,512]{1,0:T(8,128)(2,1)} %get-tuple-element.124), channel_id=1, source_target_pairs={{0,24},{8,16},{16,8},{24,0},{1,25},{9,17},{17,9},{25,1},{2,26},{10... | collective-permute-start | bytes 1179656 | tf_op jit(solution)/shard_map/ppermute | solution.py:24
  856.1 15.9 %collective-permute-start.56 = (bf16[64,2304]{1,0:T(8,128)(2,1)}, bf16[64,2304]{1,0:T(8,128)(2,1)}, u32[]{:S(2)}, u32[]{:S(2)}) collective-permute-start(bf16[64,2304]{1,0:T(8,128)(2,1)} %get-tuple-element.134), channel_id=1, source_target_pairs={{0,8},{8,0},{16,24},{24,16},{1,9},{9,1},{17,25},{25,17},{2,10},{10... | collective-permute-start | bytes 884744 | tf_op jit(solution)/shard_map/ppermute | solution.py:24
  857.4 13.1 %collective-permute-start.63 = (f32[1,14,64]{2,1,0:T(8,128)}, f32[1,14,64]{2,1,0:T(8,128)}, u32[]{:S(2)}, u32[]{:S(2)}) collective-permute-start(f32[1,14,64]{2,1,0:T(8,128)} %slice_select_fusion.5), channel_id=1, source_target_pairs={{0,1},{1,0},{2,3},{3,2},{4,5},{5,4},{6,7},{7,6},{8,9},{9,8},{10,11... | collective-permute-start | bytes 10760 | tf_op jit(solution)/shard_map/ppermute | solution.py:24
  858.4 59.9 %collective-permute-start.57 = (bf16[64,2304]{1,0:T(8,128)(2,1)}, bf16[64,2304]{1,0:T(8,128)(2,1)}, u32[]{:S(2)}, u32[]{:S(2)}) collective-permute-start(bf16[64,2304]{1,0:T(8,128)(2,1)} %get-tuple-element.133), channel_id=1, source_target_pairs={{0,16},{8,24},{16,0},{24,8},{1,17},{9,25},{17,1},{25,9},{2,18},{10... | collective-permute-start | bytes 884744 | tf_op jit(solution)/shard_map/ppermute | solution.py:24
  865.0 53.4 %collective-permute-start.58 = (bf16[64,2304]{1,0:T(8,128)(2,1)}, bf16[64,2304]{1,0:T(8,128)(2,1)}, u32[]{:S(2)}, u32[]{:S(2)}) collective-permute-start(bf16[64,2304]{1,0:T(8,128)(2,1)} %get-tuple-element.132), channel_id=1, source_target_pairs={{0,24},{8,16},{16,8},{24,0},{1,25},{9,17},{17,9},{25,1},{2,26},{10... | collective-permute-start | bytes 884744 | tf_op jit(solution)/shard_map/ppermute | solution.py:24
  869.1 52.0 %collective-permute-start.53 = (bf16[64,2048]{1,0:T(8,128)(2,1)}, bf16[64,2048]{1,0:T(8,128)(2,1)}, u32[]{:S(2)}, u32[]{:S(2)}) collective-permute-start(bf16[64,2048]{1,0:T(8,128)(2,1)} %get-tuple-element.138), channel_id=1, source_target_pairs={{0,8},{8,0},{16,24},{24,16},{1,9},{9,1},{17,25},{25,17},{2,10},{10... | collective-permute-start | bytes 786440 | tf_op jit(solution)/shard_map/ppermute | solution.py:24
  870.5 50.6 %collective-permute-start.54 = (bf16[64,2048]{1,0:T(8,128)(2,1)}, bf16[64,2048]{1,0:T(8,128)(2,1)}, u32[]{:S(2)}, u32[]{:S(2)}) collective-permute-start(bf16[64,2048]{1,0:T(8,128)(2,1)} %get-tuple-element.137), channel_id=1, source_target_pairs={{0,16},{8,24},{16,0},{24,8},{1,17},{9,25},{17,1},{25,9},{2,18},{10... | collective-permute-start | bytes 786440 | tf_op jit(solution)/shard_map/ppermute | solution.py:24
  872.0 49.0 %collective-permute-start.55 = (bf16[64,2048]{1,0:T(8,128)(2,1)}, bf16[64,2048]{1,0:T(8,128)(2,1)}, u32[]{:S(2)}, u32[]{:S(2)}) collective-permute-start(bf16[64,2048]{1,0:T(8,128)(2,1)} %get-tuple-element.136), channel_id=1, source_target_pairs={{0,24},{8,16},{16,8},{24,0},{1,25},{9,17},{17,9},{25,1},{2,26},{10... | collective-permute-start | bytes 786440 | tf_op jit(solution)/shard_map/ppermute | solution.py:24
  (71 other events, 580.8 us)
Sparse Core Ops, SparseCore 0:
  24.9 65.6 all-gather.7
  92.8 45.7 all-gather.5
  140.2 27.8 all-gather.9
  169.6 72.8 all-gather.11
  244.0 71.9 all-gather.13
  505.9 99.3 reduce-scatter.8
  709.9 87.8 reduce-scatter.4
  800.1 34.1 reduce-scatter.6
  836.6 79.0 reduce-scatter.10

commit v4 on v3

--- a/solution.py
+++ b/solution.py
@@ -1,3 +1,4 @@
+import math
 from functools import partial
 
 import jax
@@ -24,26 +25,45 @@
     return lax.ppermute(value, axis, [(i, i ^ distance) for i in range(size)])
 
 
-def gather_seq(part):
+def after(value, *others):
+    return lax.optimization_barrier((value, others))[0]
+
+
+def gather_seq(part, first=()):
     size = lax.axis_size("seq")
     if size == 4:
         half = part.shape[0] // 2
         one, two = swap(part, "seq", 1), swap(part, "seq", 2)
+        one, two = after((one, two), first)
         low, high = swap(one[:half], "seq", 2), swap(two[half:], "seq", 1)
-        return [part, one, two, jnp.concatenate([low, high], axis=0)]
+        return [part, one, two, low, high]
     return [part] + [swap(part, "seq", distance) for distance in range(1, size)]
 
 
-def scatter_seq(parts):
+def by_block(pieces):
+    if lax.axis_size("seq") == 4:
+        return pieces[:3] + [jnp.concatenate(pieces[3:], axis=0)]
+    return pieces
+
+
+def scatter_start(parts):
+    if lax.axis_size("seq") != 4:
+        return ()
+    half = parts[3].shape[0] // 2
+    return swap(parts[3][:half], "seq", 1), swap(parts[3][half:], "seq", 2)
+
+
+def scatter_seq(parts, first=(), second=(), started=None):
+    started = scatter_start(parts) if started is None else started
     size = lax.axis_size("seq")
     if size == 4:
         own, one, two, far = parts
         half = far.shape[0] // 2
-        low, high = swap(far[:half], "seq", 1), swap(far[half:], "seq", 2)
+        low, high = after(started, first)
         two = jnp.concatenate([(two[:half].astype(F32) + low.astype(F32)).astype(BF), two[half:]], axis=0)
         one = jnp.concatenate([one[:half], (one[half:].astype(F32) + high.astype(F32)).astype(BF)], axis=0)
-        return [own, swap(one, "seq", 1), swap(two, "seq", 2)]
-    return [parts[0]] + [swap(parts[distance], "seq", distance) for distance in range(1, size)]
+        return after([own, swap(one, "seq", 1), swap(two, "seq", 2)], second)
+    return after([parts[0]] + [swap(parts[distance], "seq", distance) for distance in range(1, size)], first, second)
 
 
 def trade_seq(parts):
@@ -89,7 +109,9 @@
     return (lax.div(tile, per) ^ here) * per + lax.rem(tile, per)
 
 
-def kernel(body, name, grid, here, ins, outs, scratch=(), vmem=48):
+def kernel(body, name, grid, here, ins, outs, scratch=(), vmem=48, flops=0):
+    moved = sum(a.size * a.dtype.itemsize for a, _ in ins)
+    moved += sum(math.prod(shape) * jnp.dtype(kind).itemsize for shape, kind, _ in outs)
     return pl.pallas_call(
         body,
         out_shape=[jax.ShapeDtypeStruct(shape, kind) for shape, kind, _ in outs],
@@ -100,9 +122,39 @@
             out_specs=[spec for _, _, spec in outs],
             scratch_shapes=list(scratch),
         ),
+        cost_estimate=pl.CostEstimate(flops=flops, bytes_accessed=moved, transcendentals=0),
         compiler_params=pltpu.CompilerParams(vmem_limit_bytes=vmem * 2**20),
         name=name,
     )(here, *[array for array, _ in ins])
+
+
+def pieced(pieces, tile, columns, column, place):
+    ins, start = [], 0
+    for piece in pieces:
+        count = piece.shape[0] // tile
+
+        def index(i, h, start=start, count=count):
+            return jnp.clip(place(i, h) - start, 0, count - 1), column(h)
+
+        ins.append((piece, block((tile, columns), index)))
+        start += count
+    return ins
+
+
+def picked(refs, counts, tile, held):
+    start = 0
+    for ref, count in zip(refs, counts):
+
+        @pl.when((tile >= start) & (tile < start + count))
+        def _(ref=ref):
+            held[...] = ref[...]
+
+        start += count
+    return held[...].astype(F32)
+
+
+def counts_of(pieces, tile):
+    return [piece.shape[0] // tile for piece in pieces]
 
 
 def row_index(rows):
@@ -166,22 +218,28 @@
     )
 
 
-def spread_body(parts, product, here, base_ref, *refs):
-    out = refs[-1]
-    width = refs[0].shape[1]
+def spread_body(counts, parts, product, here, *refs):
+    bases, pieces, out, held = refs[: len(counts)], refs[len(counts) : -2], refs[-2], refs[-1]
+    picked(bases, counts, pl.program_id(0), held)
+    width = pieces[0].shape[1]
     for j in range(parts):
         at = placed(here[0] ^ j, width)
-        piece, base = refs[j][...].astype(F32), base_ref[:, at].astype(F32)
+        piece, base = pieces[j][...].astype(F32), held[:, at].astype(F32)
         out[:, at] = (base * piece if product else base + piece).astype(BF)
 
 
-def spread_columns(base, pieces, here, product, turn, tile):
-    rows, width = base.shape
+def spread_columns(bases, columns, here, product, turn, tile, per):
+    rows, width = sum(base.shape[0] for base in bases), bases[0].shape[1]
+
+    def turned(i, j):
+        return (lax.div(i, per) ^ j) * per + lax.rem(i, per) if turn else i
+
     (result,) = kernel(
-        partial(spread_body, len(pieces), product), "spread_columns", (rows // tile,), here,
-        [(base, block((tile, width), lambda i, h: (i, 0)))]
-        + [(p, block((tile, p.shape[1]), lambda i, h, j=j: (i ^ j if turn else i, 0))) for j, p in enumerate(pieces)],
+        partial(spread_body, counts_of(bases, tile), len(columns), product), "spread_columns", (rows // tile,), here,
+        pieced(bases, tile, width, lambda h: 0, lambda i, h: i)
+        + [(c, block((tile, c.shape[1]), lambda i, h, j=j: (turned(i, j), 0))) for j, c in enumerate(columns)],
         [((rows, width), BF, block((tile, width), lambda i, h: (i, 0)))],
+        [pltpu.VMEM((tile, width), bases[0].dtype)],
     )
     return result
 
@@ -213,14 +271,15 @@
     return centred, lax.rsqrt(spread + EPSILON)
 
 
-def mix_body(count, norm, groups, here, x_ref, marks_ref, vec_ref, *refs):
-    outs, last = refs[:-1], refs[-1]
+def mix_body(count, norm, groups, counts, per, here, *refs):
+    pieces, (marks_ref, vec_ref) = refs[: len(counts)], refs[len(counts) : len(counts) + 2]
+    outs, last, held = refs[len(counts) + 2 : -2], refs[-2], refs[-1]
 
     @pl.when(pl.program_id(0) == 0)
     def _():
         last[...] = jnp.zeros_like(last)
 
-    values = x_ref[...].astype(F32)
+    values = picked(pieces, counts, relative(pl.program_id(0), per, here[0]), held)
     if norm:
         centred, inverse = centre(values)
         values = centred * inverse
@@ -237,23 +296,20 @@
         outs[i][...] = (previous + step * vec_ref[2 + i : 3 + i, :]).astype(BF)
 
 
-def mixes(values, marks, vec, count, norm, groups, here, per):
-    rows, width = values.shape
-    tile = CHUNK
+def mixes(pieces, marks, vec, count, norm, groups, here, tile, per):
+    rows, width = marks.shape[0], pieces[0].shape[1]
     own = block((tile, width), lambda i, h: (relative(i, per, h), 0))
     return kernel(
-        partial(mix_body, count, norm, groups), "mixes", (rows // tile,), here,
-        [
-            (values, own),
-            (marks, block((tile, PAIR), lambda i, h: (i, 0))),
-            (vec, fixed(vec.shape)),
-        ],
+        partial(mix_body, count, norm, groups, counts_of(pieces, tile), per), "mixes", (rows // tile,), here,
+        pieced(pieces, tile, width, lambda h: 0, lambda i, h: relative(i, per, h))
+        + [(marks, block((tile, PAIR), lambda i, h: (i, 0))), (vec, fixed(vec.shape))],
         [((rows, width), BF, own)] * (count + 1),
-        [pltpu.VMEM((8, width), F32)],
-    )
-
-
-def mixes_back_body(count, here, *refs):
+        [pltpu.VMEM((8, width), F32), pltpu.VMEM((tile, width), BF)],
+    )
+
+
+def mixes_back_body(which, here, *refs):
+    count = len(which)
     grads, weights = refs[:count], refs[count : 2 * count]
     step_ref, marks_ref, vec_ref, out_ref, sums_ref, later = refs[2 * count :]
 
@@ -263,8 +319,9 @@
         sums_ref[...] = jnp.zeros_like(sums_ref)
 
     step = step_ref[...].astype(F32)
-    for i in range(count):
-        grad = dot(grads[i][...], weights[i][...], NT)
+    total = straight = None
+    for i in range(which[-1] + 1):
+        grad = sum(dot(grads[k][...], weights[k][...], NT) for k in range(count) if which[k] == i)
         sums_ref[i : i + 1, :] += jnp.sum(grad * step, axis=0, keepdims=True)
         part = grad * vec_ref[i : i + 1, :]
         total, straight = (total + grad, straight + part) if i else (grad, part)
@@ -275,49 +332,56 @@
     out_ref[...] = (straight + up).astype(BF)
 
 
-def mixes_back(grads, weights, step, marks, vec, here, seq):
+def mixes_back(terms, step, marks, vec, here, seq):
     rows, width = step.shape
-    tile, columns, count = rows // seq, min(512, width), len(grads)
+    tile, columns = rows // seq, min(512, width)
     last = rows // tile - 1
 
-    def natural(i):
-        return last - i
-
-    ins = [(g, block((tile, g.shape[1]), lambda c, i, h: (relative(natural(i), 1, h), 0))) for g in grads]
-    for g, (w, at) in zip(grads, weights):
-        ins.append((w, pl.BlockSpec((columns, g.shape[1]), lambda c, i, h, at=at: (c, at))))
+    def own(i, h):
+        return relative(last - i, 1, h)
+
+    ins = [(g, block((tile, n), lambda c, i, h, at=at: (own(i, h), at))) for _, g, at, _, _, n in terms]
+    ins += [(w, block((columns, n), lambda c, i, h, at=at: (c, at))) for _, _, _, w, at, n in terms]
     ins += [
-        (step, block((tile, columns), lambda c, i, h: (relative(natural(i), 1, h), c))),
-        (marks, block((tile, PAIR), lambda c, i, h: (natural(i), 0))),
+        (step, block((tile, columns), lambda c, i, h: (own(i, h), c))),
+        (marks, block((tile, PAIR), lambda c, i, h: (last - i, 0))),
         (vec, block((8, columns), lambda c, i, h: (0, c))),
     ]
     return kernel(
-        partial(mixes_back_body, count), "mixes_back", (width // columns, last + 1), here, ins,
+        partial(mixes_back_body, [t[0] for t in terms]), "mixes_back", (width // columns, last + 1), here, ins,
         [
-            ((rows, width), BF, block((tile, columns), lambda c, i, h: (relative(natural(i), 1, h), c))),
+            ((rows, width), BF, block((tile, columns), lambda c, i, h: (own(i, h), c))),
             ((8, width), F32, block((8, columns), lambda c, i, h: (0, c))),
         ],
         [pltpu.VMEM((8, columns), F32)],
-    )
-
-
-def after_body(count, here, x_ref, vec_ref, *refs):
-    after_ref, normed_ref = refs[count:]
+        flops=2 * rows * width * sum(t[-1] for t in terms),
+    )
+
+
+def after_body(parts, count, here, x_ref, vec_ref, *refs):
+    mixed, weights, (after_ref, normed_ref) = refs[:parts], refs[parts : parts + count], refs[parts + count :]
     after = x_ref[...].astype(F32)
-    for ref in refs[:count]:
-        after = after + ref[...].astype(F32)
+    start, width = 0, mixed[0].shape[1]
+    for ref in weights:
+        stop = start + ref.shape[0]
+        left = mixed[start // width][:, start % width : (stop - 1) % width + 1]
+        after = after + dot(left, ref[...], NN)
+        start = stop
     after_ref[...] = after
     centred, inverse = centre(after)
     normed_ref[...] = (centred * inverse * vec_ref[0:1, :] + vec_ref[1:2, :]).astype(BF)
 
 
-def after_norm(inputs, terms, vec, here):
+def after_norm(inputs, mixed, weights, vec, here):
     rows, width = inputs.shape
     own = block((CHUNK, width), lambda i, h: (i, 0))
     return kernel(
-        partial(after_body, len(terms)), "after_norm", (rows // CHUNK,), here,
-        [(inputs, own), (vec, fixed(vec.shape))] + [(t, own) for t in terms],
+        partial(after_body, len(mixed), len(weights)), "after_norm", (rows // CHUNK,), here,
+        [(inputs, own), (vec, fixed(vec.shape))]
+        + [(m, block((CHUNK, m.shape[1]), lambda i, h: (i, 0))) for m in mixed]
+        + [(w, fixed(w.shape)) for w in weights],
         [((rows, width), F32, own), ((rows, width), BF, own)],
+        flops=2 * rows * width * width,
     )
 
 
@@ -380,6 +444,7 @@
             (params, fixed(params.shape)),
         ],
         [((rows, part), F32, own), ((rows, part), BF, own)],
+        flops=2 * rows * width * part,
     )
 
 
@@ -397,29 +462,29 @@
             (right, block((depth, part), lambda i, h: (0, h ^ relative_to))),
         ],
         [((rows, part), BF, block((tile, part), lambda i, h: (i ^ relative_to, 0)))],
+        flops=2 * rows * depth * part,
     )
     return result
 
 
-def channel_body(count, here, pre_ref, grad_ref, *refs):
-    channel_ref, d_recept_ref = refs[count:]
-    value = refs[0][...].astype(F32)
-    for ref in refs[1:count]:
-        value = value + ref[...].astype(F32)
+def channel_body(counts, here, pre_ref, *refs):
+    grads, terms, (channel_ref, d_recept_ref, held) = refs[: len(counts)], refs[len(counts) : -3], refs[-3:]
+    value = sum(ref[...].astype(F32) for ref in terms)
     opened = 1.0 / (1.0 + jnp.exp(-pre_ref[...]))
     channel = opened * value
     channel_ref[...] = channel.astype(BF)
-    d_recept_ref[...] = (grad_ref[...].astype(F32) * channel * (1.0 - opened)).astype(BF)
-
-
-def channel_out(terms, pre, grad_all, here, seq):
+    grad = picked(grads, counts, pl.program_id(0), held)
+    d_recept_ref[...] = (grad * channel * (1.0 - opened)).astype(BF)
+
+
+def channel_out(terms, pre, grads, here, tile):
     rows, part = pre.shape
-    tile = rows // seq
     own = block((tile, part), lambda i, h: (i, 0))
     return kernel(
-        partial(channel_body, len(terms)), "channel", (seq,), here,
-        [(pre, own), (grad_all, block((tile, part), lambda i, h: (i, h)))] + [(t, own) for t in terms],
+        partial(channel_body, counts_of(grads, tile)), "channel", (rows // tile,), here,
+        [(pre, own)] + pieced(grads, tile, part, lambda h: h, lambda i, h: i) + [(t, own) for t in terms],
         [((rows, part), BF, own)] * 2,
+        [pltpu.VMEM((tile, part), BF)],
     )
 
 
@@ -514,7 +579,7 @@
     for pair in range(r_ref.shape[1] // PAIR):
         at = slice(pair * PAIR, (pair + 1) * PAIR)
         bonus, gain, bias, decay = (par_ref[i : i + 1, at] for i in range(4))
-        wkv, gate, d_mixed = wkv_ref[:, at], g_ref[:, at], d_mixed_ref[:, at]
+        wkv, gate, d_mixed = wkv_ref[:, at], g_ref[:, at], d_mixed_ref[:, at].astype(F32)
         centred = wkv - head_sum_fine(wkv, ones) * (1.0 / HEAD)
         spread = head_sum(centred * centred, ones) * (1.0 / HEAD)
         inverse = lax.rsqrt(spread + GROUP_EPSILON)
@@ -590,6 +655,7 @@
         [(a, tokens) for a in (r, k, v)] + list(zip(tables, blocks)),
         [((length, width), F32, tokens), ((chunks, width, PAIR), BF, states)],
         [pltpu.VMEM((width, PAIR), F32)],
+        flops=length * width * 8000,
     )
 
 
@@ -602,6 +668,7 @@
         [(a, tokens) for a in (r, k, v, gate, wkv, d_mixed)] + [(states_kept, states)] + list(zip(tables, blocks)),
         [((length, width), BF, tokens)] * 4 + [((8, width), F32, fixed((8, width)))],
         [pltpu.VMEM((width, PAIR), F32)],
+        flops=length * width * 32000,
     )
 
 
@@ -645,41 +712,43 @@
     inputs_b, grad_b = tokens[0], out_grad[0]
     own_rows, width = inputs_b.shape
     length, part, unit = own_rows * seq, width // seq, vectors.shape[1]
-    per = own_rows // CHUNK
+    per, tile = own_rows // CHUNK, own_rows // 2
     hidden_width = ffn_key.shape[1] // seq
     groups = (seq, dp)
     within = groups if unit == HEAD else None
 
-    def whole(values):
-        return jnp.concatenate(gather_seq(values), axis=0)
-
-    def all_rows(weights):
-        pieces = trade_seq(cut_columns(weights, here, seq))
-        stacked = stack_rows(pieces, here)
-        return lax.all_gather(stacked.reshape(-1, stacked.shape[-1]), "dp", axis=0, tiled=True)
-
-    def owners_rows(grads, widths):
-        grad = jnp.concatenate([g.astype(BF) for g in grads], axis=1)
-        summed = lax.psum_scatter(grad, "dp", scatter_dimension=0, tiled=True)
+    def stacked_columns(weights, beside=()):
+        stacked = stack_rows(after(trade_seq(cut_columns(weights, here, seq)), beside), here)
+        return stacked.reshape(-1, stacked.shape[-1])
+
+    def gather_dp(rows):
+        return lax.all_gather(rows, "dp", axis=0, tiled=True)
+
+    def scatter_dp(grad):
+        return lax.psum_scatter(grad, "dp", scatter_dimension=0, tiled=True)
+
+    def owners_rows(summed, widths, beside=()):
         rows = summed.shape[0] // seq
         parts = [lax.dynamic_slice_in_dim(summed, (place ^ j) * rows, rows, 0) for j in range(seq)]
-        return join_columns(trade_seq(parts), widths, here)
-
-    def natural(grad):
-        return lax.psum_scatter(grad.astype(BF), "dp", scatter_dimension=0, tiled=True).astype(F32)
-
-    full_in = all_rows([w_receptance, w_key, w_value])
+        return join_columns(after(trade_seq(parts), beside), widths, here)
+
+    def turn_pieces(pieces):
+        if within is not None:
+            return pieces
+        return [outside(p, groups, unit) for p in pieces]
+
+    columns_in = stacked_columns([w_receptance, w_key, w_value])
+    full_in = gather_dp(columns_in)
     vec_own = gather_small(vectors[None], "dp")
-    vec_parts = gather_small(vec_own[None], "seq").astype(F32)
+    vec_parts = gather_small(vec_own[None], "seq")
+    tokens_all = gather_seq(after(inputs_b, columns_in), vec_parts)
+    vectors_there, vec_parts = vec_parts, vec_parts.astype(F32)
     vec_own = vec_own.transpose(1, 0, 2).reshape(-1, part).astype(F32)
     vec = vec_parts.transpose(2, 0, 1, 3).reshape(-1, width)
     turned = vec_parts.transpose(2, 1, 0, 3).reshape(-1, width)
-    tokens_all = whole(inputs_b)
-    full_gc = all_rows([w_gate, ffn_receptance])
-    full_o = lax.all_gather(w_output, "dp", axis=0, tiled=True)
-    grad_all = whole(grad_b)
-    full_ck = all_rows([ffn_key])
-    full_cv = lax.all_gather(ffn_value, "dp", axis=0, tiled=True)
+    arrived = tokens_all[1:3] + [vectors_there]
+    own_o = gather_dp(after(w_output, arrived))
+    full_g = gather_dp(stacked_columns([after(w_gate, arrived)]))
 
     positions = jnp.arange(length, dtype=jnp.int32)
     piece, first_flags = segment_of(seq_lengths[0], positions)
@@ -689,74 +758,97 @@
     )
     marks = tables[0]
 
-    if within is None:
-        tokens_all = outside(tokens_all, groups, unit)
     mix_r, mix_k, mix_v, mix_g, step = mixes(
-        tokens_all, marks, rows_of(turned, 0, 1, 2, 3, 4, 5), 4, True, within, here, per
-    )
+        turn_pieces(tokens_all), marks, rows_of(turned, 0, 1, 2, 3, 4, 5), 4, True, within, here, tile, own_rows // tile
+    )
+    full_c = gather_dp(stacked_columns(after([ffn_key, ffn_receptance], tokens_all), mix_r))
+    full_ck, full_cr = full_c[:, :hidden_width], full_c[:, hidden_width:]
+    full_cv = gather_dp(after(ffn_value, mix_r))
     recept, keyed, valued = (
         dot(m, full_in[:, i * part : (i + 1) * part], NN).astype(BF)
         for i, m in enumerate((mix_r, mix_k, mix_v))
     )
+    projected = (recept, keyed, valued)
+    grad_all = gather_seq(after(grad_b, arrived), projected)
+    recept = after(recept, grad_all[1:3], projected)
+    own_o = after(own_o, grad_all[1:3], projected)
     wkv, states = wkv_forward(recept, keyed, valued, tables, here, per)
-    gate_pre, mixed = gated(mix_g, full_gc, wkv, tables[5], here, seq)
-    attn = [dot(rows, full_o, NN).astype(BF) for rows in blocks_of(mixed, seq)]
-    after, normed_two = after_norm(inputs_b, scatter_seq(attn), rows_of(vec, 10, 11), here)
-
-    normed_two = whole(normed_two)
-    if within is None:
-        normed_two = outside(normed_two, groups, unit)
+    gate_pre, mixed = gated(mix_g, full_g, after(wkv, grad_all), tables[5], here, seq)
+    full_o = gather_seq(own_o, mixed)
+    mixed = trade_seq(blocks_of(mixed, seq))
+    after_mix, normed_two = after_norm(inputs_b, mixed, full_o, rows_of(vec, 10, 11), here)
+
     mix_k2, mix_r2, step_two = mixes(
-        normed_two, marks, rows_of(turned, 10, 11, 12, 13), 2, False, within, here, per
-    )
-    recept_pre = dot(mix_r2, full_gc[:, part:], NN)
+        turn_pieces(gather_seq(normed_two)), marks, rows_of(turned, 10, 11, 12, 13), 2, False, within, here, tile,
+        own_rows // tile,
+    )
+    recept_pre = dot(mix_r2, full_cr, NN)
     opened = gather_seq(jax.nn.sigmoid(recept_pre).astype(BF))
     key_pre = dot(mix_k2, full_ck, NN)
     smooth = jax.nn.softplus(key_pre)
     hidden = (smooth * smooth).astype(BF)
-    value_parts = [columns_product(hidden, full_cv, part, j, here, seq) for j in reversed(range(seq))]
-    value_terms = scatter_seq(value_parts[::-1])
-    d_value = spread_columns(grad_all, opened, here, True, True, own_rows)
-    channel, d_recept_two = channel_out(value_terms, recept_pre, grad_all, here, seq)
-    channel = trade_seq(blocks_of(channel, seq))
-    out_rows = spread_columns(after, channel, here, False, False, CHUNK)
-
-    d_hidden = dot(d_value, full_cv, NT)
-    d_key_two = (d_hidden * 2.0 * smooth * jax.nn.sigmoid(key_pre)).astype(BF)
+    slope = (2.0 * smooth * jax.nn.sigmoid(key_pre)).astype(BF)
+    hidden, slope = lax.optimization_barrier((hidden, slope))
+    later = after(hidden, opened[1:3])
+    value_parts = [columns_product(later if j < 2 else hidden, full_cv, part, j, here, seq) for j in reversed(range(seq))]
+    value_started = scatter_start(value_parts[::-1])
+    d_value = spread_columns(grad_all, by_block(after(opened, value_parts)), here, True, True, tile, own_rows // tile)
+
+    grad_cv = dot(hidden, after(d_value, value_started), TN).astype(BF)
+    summed_cv = scatter_dp(grad_cv)
+    d_hidden = dot(after(d_value, grad_cv), full_cv, NT)
+    d_key_two = (d_hidden * slope.astype(F32)).astype(BF)
+    value_terms = scatter_seq(value_parts[::-1], started=value_started)
+    channel, d_recept_two = channel_out(value_terms, recept_pre, grad_all, here, tile)
+    half, first = part // 2, hidden_width // (part // 2)
     d_normed_two, sums_two = mixes_back(
-        [d_key_two, d_recept_two], [(full_ck, 0), (full_gc, 1)], step_two, marks,
-        rows_of(turned, 12, 13), here, seq,
-    )
-    terms_two = scatter_seq(blocks_of(d_normed_two, seq))
-    grad_cv = dot(hidden, d_value, TN)
-    grad_ck = dot(mix_k2, d_key_two, TN)
-    grad_cr = dot(mix_r2, d_recept_two, TN)
+        [(0, d_key_two, 0, full_c, 0, hidden_width)]
+        + [(1, d_recept_two, i, full_c, first + i, half) for i in range(2)],
+        step_two, marks, rows_of(turned, 12, 13), here, seq,
+    )
+    grad_ck = dot(after(mix_k2, d_normed_two), d_key_two, TN).astype(BF)
+    d_normed_two = blocks_of(d_normed_two, seq)
+    started = scatter_start(d_normed_two)
+    grad_cr = dot(after(mix_r2, grad_ck, started), d_recept_two, TN).astype(BF)
+    terms_two = scatter_seq(d_normed_two, grad_ck, (grad_cr, summed_cv), started)
+    summed_ck = scatter_dp(grad_ck)
+    summed_cr = scatter_dp(grad_cr)
     if within is None:
         terms_two = [outside(t, groups, unit, back=True) for t in terms_two]
-    d_after, d_attn, norm_sums_two = norm_back(terms_two, after, grad_b, rows_of(vec, 10), within, here)
-
-    d_attn = whole(d_attn)
-    d_mixed = dot(d_attn, full_o, NT)
-    grad_wo = dot(mixed, d_attn, TN)
+    d_after, d_attn, norm_sums_two = norm_back(terms_two, after_mix, grad_b, rows_of(vec, 10), within, here)
+
+    o_parts = by_block(full_o)
+    d_mixed = trade_seq([dot(d_attn, w, NT).astype(BF) for w in o_parts])
+    grads_o = [dot(m, d_attn, TN).astype(BF) for m in mixed]
+    d_mixed = after(jnp.concatenate(d_mixed, axis=0), grads_o)
     d_recept, d_keyed, d_valued, d_gate, sums = wkv_backward(
         recept, keyed, valued, gate_pre, wkv, d_mixed, states, tables, here, per
     )
+    grad_wo = sum(t.astype(F32) for t in scatter_seq(grads_o)).astype(BF)
+    grads_in = [
+        dot(m, d, TN).astype(BF)
+        for m, d in ((mix_r, d_recept), (mix_k, d_keyed), (mix_v, d_valued), (mix_g, d_gate))
+    ]
+    summed_o = scatter_dp(grad_wo)
+    summed_in = scatter_dp(after(jnp.concatenate(grads_in, axis=1), grad_wo))
+    d_recept = after(d_recept, grads_in)
     d_normed, sums_one = mixes_back(
-        [d_recept, d_keyed, d_valued, d_gate], [(full_in, 0), (full_in, 1), (full_in, 2), (full_gc, 0)],
+        [(i, d, 0, full_in, i, part) for i, d in enumerate((d_recept, d_keyed, d_valued))]
+        + [(3, d_gate, 0, full_g, 0, part)],
         step, marks, rows_of(turned, 2, 3, 4, 5), here, seq,
     )
-    terms = scatter_seq(blocks_of(d_normed, seq))
-    grads_in = [
-        dot(mix_r, d_recept, TN), dot(mix_k, d_keyed, TN), dot(mix_v, d_valued, TN), dot(mix_g, d_gate, TN)
-    ]
+    channel = after(trade_seq(blocks_of(channel, seq)), d_normed)
+    out_rows = spread_columns([after_mix], channel, here, False, False, CHUNK, per)
+    (sum_ck,) = owners_rows(summed_ck, [ffn_key.shape[1]], d_normed)
+    (sum_cr,) = owners_rows(summed_cr, [width], d_normed)
+    sum_cv = after(summed_cv, d_normed).astype(F32)
+    terms = scatter_seq(blocks_of(d_normed, seq), (out_rows, sum_cv), (sum_ck, sum_cr))
     if within is None:
         terms = [outside(t, groups, unit, back=True) for t in terms]
     tokens_grad, _, norm_sums = norm_back(terms, inputs_b, d_after, rows_of(vec, 0), within, here)
 
-    sum_cv = natural(grad_cv)
-    sum_ck, sum_cr = owners_rows([grad_ck, grad_cr], [ffn_key.shape[1], width])
-    sum_o = natural(grad_wo)
-    sum_r, sum_k, sum_v, sum_g = owners_rows(grads_in, [width] * 4)
+    sum_o = summed_o.astype(F32)
+    sum_r, sum_k, sum_v, sum_g = owners_rows(summed_in, [width] * 4)
 
     def by_device(rows, turn):
         if turn:

time: 937 us -> 899 us (0.959)
  waiting for transfers between devices: 344 us -> 293 us
    reduce_scatter x4 -> x5, waiting for transfers between devices: 35.6 us -> 0.05 us  [scatter_dp(): return lax.psum_scatter(grad, 'dp', scatter_dimension=0, tiled=True)]
    ppermute x64 -> x73, waiting for transfers between devices: 307 us -> 292 us  [swap(): return lax.ppermute(value, axis, [(i, i ^ distance) for i in range(size)])]
    unnamed x139 -> x219, local copies, waits for them, and re-layouts: 45.2 us -> 34.7 us
    pallas_call x25 -> x26, Pallas kernels: 218 us -> 223 us  [kernel(): pl.pallas_call(body, out_shape=[jax.ShapeDtypeStruct(shape, kind) for sha...]
    dot_general x19 -> x21, matrix products: 156 us -> 151 us  [dot(): return lax.dot_general(left, right, dims, preferred_element_type=F32)]
    ppermute x64 -> x73, starting transfers between devices: 80.4 us -> 85.1 us  [swap(): return lax.ppermute(value, axis, [(i, i ^ distance) for i in range(size)])]
  transfers between devices with their start and end apart: 73 -> 83, of which waited for: 39 -> 39; matrix products, arithmetic and copies ran while one was open for 26% -> 25% of each run, Pallas kernels for 23% -> 25%
where the time goes in v4:
time: 899 us; the launch traced here: 890 us
  waiting for transfers between devices  293 us (33%)
  Pallas kernels  223 us (25%)
  matrix products  151 us (17%)
  starting transfers between devices  85.6 us (10%)
  local copies, waits for them, and re-layouts  84.4 us (9%)
  other arithmetic  36.5 us (4%)
  between operations  16.2 us (2%)
    ppermute x73, waiting for transfers between devices, swap(): return lax.ppermute(value, axis, [(i, i ^ distance) for i in range(size)])  292 us
    pallas_call x26, Pallas kernels, kernel(): pl.pallas_call(body, out_shape=[jax.ShapeDtypeStruct(shape, kind) for sha...  223 us
    dot_general x21, matrix products, dot(): return lax.dot_general(left, right, dims, preferred_element_type=F32)  151 us
    ppermute x73, starting transfers between devices, swap(): return lax.ppermute(value, axis, [(i, i ^ distance) for i in range(size)])  85.1 us
    unnamed x219, local copies, waits for them, and re-layouts  34.7 us
  transfers between devices with their start and end apart: 83, of which 39 were waited for; matrix products, arithmetic and copies ran while one was open for 25% of the time, Pallas kernels for 25%

profile of v4, /device:TPU:0, one launch (start us, length us, event | category | flops | bytes accessed | tf_op | source)
XLA Modules:
  0.0 890.2 jit_solution(17990591069327518410)
XLA Ops:
  10.3 3.0 collective-permute-start.5
  14.8 4.2 collective-permute-done.5.refs_1_
  19.0 4.8 collective-permute-done.6.refs_2_
  37.7 24.8 %collective-permute-done.3 = bf16[1,8,14,64]{3,2,1,0:T(8,128)(2,1)S(1)} collective-permute-done((bf16[1,8,14,64]{3,2,1,0:T(8,128)(2,1)S(1)}, bf16[1,8,14,64]{3,2,1,0:T(8,128)(2,1)S(1)}, u32[]{:S(2)}, u32[]{:S(2)}) %collective-permute-start.3) | collective-permute-done | bytes 14368 | tf_op jit(solution)/shard_map/ppermute | solution.py:25
  64.1 2.7 collective-permute-done.4
  81.4 15.0 %collective-permute-done.10.refs_3_ = bf16[192,2048]{1,0:T(8,128)(2,1)S(1)} collective-permute-done((bf16[192,2048]{1,0:T(8,128)(2,1)S(1)}, bf16[192,2048]{1,0:T(8,128)(2,1)S(1)}, u32[]{:S(2)}, u32[]{:S(2)}) %collective-permute-start.10) | collective-permute-done | bytes 786464 | tf_op jit(solution)/shard_map/ppermute | solution.py:25
  111.7 17.6 %mixes.2 = (bf16[1536,2048]{1,0:T(8,128)(2,1)}, bf16[1536,2048]{1,0:T(8,128)(2,1)}, bf16[1536,2048]{1,0:T(8,128)(2,1)}, bf16[1536,2048]{1,0:T(8,128)(2,1)}, bf16[1536,2048]{1,0:T(8,128)(2,1)}) custom-call(s32[1]{0:T(128)} %bitcast.here, bf16[384,2048]{1,0:T(8,128)(2,1)S(1)} %bitcast.102, bf16[384,2048]{1,0:T(8,128)(2,1)} %collective-permute-done.8.refs_1_, ...), custom_call_target="tpu_custom_call" | custom-call | bytes 38600704 | tf_op jit(solution)/shard_map/mixes/pallas_call | solution.py:115
  134.6 8.2 convolution_convert_fusion.13.r_ref
  142.8 8.0 convolution_convert_fusion.12.k_ref
  150.8 4.5 convolution_convert_fusion.11.v_ref
  155.3 10.0 %collective-permute-done.15.refs_1_ = bf16[384,2048]{1,0:T(8,128)(2,1)S(1)} collective-permute-done((bf16[384,2048]{1,0:T(8,128)(2,1)S(1)}, bf16[384,2048]{1,0:T(8,128)(2,1)S(1)}, u32[]{:S(2)}, u32[]{:S(2)}) %collective-permute-start.15) | collective-permute-done | bytes 1572896 | tf_op jit(solution)/shard_map/ppermute | solution.py:25
  176.8 13.5 %wkv_forward.1 = (f32[1536,512]{1,0:T(8,128)}, bf16[12,512,128]{2,1,0:T(8,128)(2,1)S(1)}) custom-call(s32[1]{0:T(128)} %bitcast.here, bf16[1536,512]{1,0:T(8,128)(2,1)S(1)} %copy-done.59, bf16[1536,512]{1,0:T(8,128)(2,1)} %convolution_convert_fusion.12.k_ref, bf16[1536,512]{1,0:T(8,128)(2,1)} %convolution_convert_fusion.11.v_ref, f32[1536,128]{1,0:T(8,128)S(1)} %copy-done.5, ...), custom_call_target="tpu_custom_call" | custom-call | flops 6291456000 | bytes 11075584 | tf_op jit(solution)/shard_map/wkv_forward/pallas_call | solution.py:115
  191.5 36.1 %collective-permute-done.17.refs_3_ = bf16[192,2048]{1,0:T(8,128)(2,1)S(1)} collective-permute-done((bf16[192,2048]{1,0:T(8,128)(2,1)S(1)}, bf16[192,2048]{1,0:T(8,128)(2,1)S(1)}, u32[]{:S(2)}, u32[]{:S(2)}) %collective-permute-start.17) | collective-permute-done | bytes 786464 | tf_op jit(solution)/shard_map/ppermute | solution.py:25
  231.0 10.1 %gate.1 = (f32[1536,512]{1,0:T(8,128)}, bf16[1536,512]{1,0:T(8,128)(2,1)S(1)}) custom-call(s32[1]{0:T(128)} %bitcast.here, bf16[1536,2048]{1,0:T(8,128)(2,1)} %get-tuple-element.152.refs_0_, bf16[2048,512]{1,0:T(8,128)(2,1)S(1)} %copy-done.58, f32[1536,512]{1,0:T(8,128)} %get-tuple-element.170.refs_2_.wkv_ref, f32[8,512]{1,0:T(8,128)S(1)} %maximum_maximum_fusion.par_ref.refs_3_), custom_call_target="tpu_custom_call" | custom-call | flops 3221225472 | bytes 16269312 | tf_op jit(solution)/shard_map/gate/pallas_call | solution.py:115
  241.1 2.9 slice.358
  258.4 20.8 %collective-permute-done.19.refs_1_ = bf16[384,512]{1,0:T(8,128)(2,1)} collective-permute-done((bf16[384,512]{1,0:T(8,128)(2,1)}, bf16[384,512]{1,0:T(8,128)(2,1)}, u32[]{:S(2)}, u32[]{:S(2)}) %collective-permute-start.19) | collective-permute-done | bytes 393248 | tf_op jit(solution)/shard_map/ppermute | solution.py:25
  279.2 4.9 collective-permute-done.21.refs_3_
  284.1 9.6 %after_norm.1 = (f32[384,2048]{1,0:T(8,128)}, bf16[384,2048]{1,0:T(8,128)(2,1)S(1)}) custom-call(s32[1]{0:T(128)} %bitcast.here, bf16[384,2048]{1,0:T(8,128)(2,1)} %bitcast.99, f32[8,2048]{1,0:T(8,128)S(1)} %get-tuple-element.342.vec_ref, bf16[384,512]{1,0:T(8,128)(2,1)S(1)} %get-tuple-element.301.refs_0_, bf16[384,512]{1,0:T(8,128)(2,1)} %collective-permute-done.19.refs_1_, ...), custom_call_target="tpu_custom_call" | custom-call | flops 3221225472 | bytes 16318464 | tf_op jit(solution)/shard_map/after_norm/pallas_call | solution.py:115
  296.3 26.9 %collective-permute-done.26.refs_1_ = bf16[384,2048]{1,0:T(8,128)(2,1)S(1)} collective-permute-done((bf16[384,2048]{1,0:T(8,128)(2,1)S(1)}, bf16[384,2048]{1,0:T(8,128)(2,1)S(1)}, u32[]{:S(2)}, u32[]{:S(2)}) %collective-permute-start.26) | collective-permute-done | bytes 1572896 | tf_op jit(solution)/shard_map/ppermute | solution.py:25
  323.2 3.4 collective-permute-done.27.refs_2_
  332.3 8.9 %collective-permute-done.28.refs_3_ = bf16[192,2048]{1,0:T(8,128)(2,1)} collective-permute-done((bf16[192,2048]{1,0:T(8,128)(2,1)}, bf16[192,2048]{1,0:T(8,128)(2,1)}, u32[]{:S(2)}, u32[]{:S(2)}) %collective-permute-start.28) | collective-permute-done | bytes 786464 | tf_op jit(solution)/shard_map/ppermute | solution.py:25
  341.2 2.8 collective-permute-done.29.refs_4_
  347.9 12.2 %mixes.3 = (bf16[1536,2048]{1,0:T(8,128)(2,1)}, bf16[1536,2048]{1,0:T(8,128)(2,1)}, bf16[1536,2048]{1,0:T(8,128)(2,1)}) custom-call(s32[1]{0:T(128)} %bitcast.here, bf16[384,2048]{1,0:T(8,128)(2,1)S(1)} %copy-done.25, bf16[384,2048]{1,0:T(8,128)(2,1)S(1)} %copy-done.17, bf16[384,2048]{1,0:T(8,128)(2,1)} %copy-done.67, ...), custom_call_target="tpu_custom_call" | custom-call | bytes 26017792 | tf_op jit(solution)/shard_map/mixes/pallas_call | solution.py:115
  360.2 9.6 %divide_convert_fusion = (bf16[1536,512]{1,0:T(8,128)(2,1)}, f32[1536,512]{1,0:T(8,128)}) fusion(bf16[1536,2048]{1,0:T(8,128)(2,1)} %get-tuple-element.218, bf16[2048,2304]{1,0:T(8,128)(2,1)} %all-gather.12.cloned.1.call-done.refs_3_.refs_4_.refs_5_), kind=kOutput, calls=%fused_computation.10 | convolution fusion | flops 3224371200 | bytes 13107200 | tf_op jit(solution)/shard_map/dot_general | solution.py:504
  371.6 22.7 %multiply_convert_fusion.1 = (bf16[1536,1792]{1,0:T(8,128)(2,1)}, bf16[1536,1792]{1,0:T(8,128)(2,1)}) fusion(bf16[1536,2048]{1,0:T(8,128)(2,1)} %get-tuple-element.215, bf16[2048,2304]{1,0:T(8,128)(2,1)S(1)} %copy-done.93), kind=kOutput, calls=%fused_computation.2 | convolution fusion | flops 11312824320 | bytes 24641536 | tf_op jit(solution)/shard_map/dot_general | solution.py:504
  394.3 6.0 value_columns.6
  407.0 6.2 value_columns.7
  414.4 6.0 value_columns.4.refs_5_
  421.6 6.0 value_columns.5
  430.9 9.5 %spread_columns.2 = bf16[1536,2048]{1,0:T(8,128)(2,1)} custom-call(s32[1]{0:T(128)} %bitcast.here, bf16[384,2048]{1,0:T(8,128)(2,1)S(1)} %bitcast.97, bf16[384,2048]{1,0:T(8,128)(2,1)S(1)} %collective-permute-done.15.refs_1_, bf16[384,2048]{1,0:T(8,128)(2,1)} %collective-permute-done.16.refs_2_, bf16[192,2048]{1,0:T(8,128)(2,1)S(1)} %copy-done.19, ...), custom_call_target="tpu_custom_call" | custom-call | bytes 18874368 | tf_op jit(solution)/shard_map/spread_columns/pallas_call | solution.py:115
  441.3 15.9 %convolution_convert_fusion.1 = bf16[1792,2048]{1,0:T(8,128)(2,1)} fusion(bf16[1536,1792]{1,0:T(8,128)(2,1)S(1)} %bitcast.105, bf16[1536,2048]{1,0:T(8,128)(2,1)} %spread_columns.2), kind=kOutput, calls=%fused_computation.6 | convolution fusion | flops 11277959168 | bytes 19136512 | tf_op jit(solution)/shard_map/dot_general | solution.py:504
  463.8 18.6 %multiply_convert_fusion.refs_0_ = bf16[1536,1792]{1,0:T(8,128)(2,1)} fusion(bf16[1536,1792]{1,0:T(8,128)(2,1)} %get-tuple-element.211, bf16[1536,2048]{1,0:T(8,128)(2,1)} %spread_columns.2, bf16[1792,2048]{1,0:T(8,128)(2,1)} %all-gather.14.cloned.1.call-done.right_ref), kind=kOutput, calls=%fused_computation.1 | convolution fusion | flops 11282546688 | bytes 24641536 | tf_op jit(solution)/shard_map/dot_general | solution.py:504
  482.4 5.8 collective-permute-done.38.refs_7_
  488.2 2.8 collective-permute-done.37.refs_6_
  492.1 7.1 channel.1
  500.4 28.7 %mixes_back.2 = (bf16[1536,2048]{1,0:T(8,128)(2,1)}, f32[8,2048]{1,0:T(8,128)S(1)}) custom-call(s32[1]{0:T(128)} %bitcast.here, bf16[1536,1792]{1,0:T(8,128)(2,1)} %multiply_convert_fusion.refs_0_, bf16[1536,512]{1,0:T(8,128)(2,1)S(1)} %get-tuple-element.212.refs_1_.refs_2_, bf16[1536,512]{1,0:T(8,128)(2,1)S(1)} %get-tuple-element.212.refs_1_.refs_2_, ...), custom_call_target="tpu_custom_call" | custom-call | flops 14495514624 | bytes 50462720 | tf_op jit(solution)/shard_map/mixes_back/pallas_call | solution.py:115
  529.1 3.6 fusion.22
  534.1 13.8 %convolution_convert_fusion = bf16[2048,1792]{1,0:T(8,128)(2,1)} fusion(bf16[1536,2048]{1,0:T(8,128)(2,1)S(1)} %bitcast.124, bf16[1536,1792]{1,0:T(8,128)(2,1)S(1)} %copy-done.97), kind=kOutput, calls=%fused_computation.5 | convolution fusion | flops 11277959168 | bytes 19136512 | tf_op jit(solution)/shard_map/dot_general | solution.py:504
  547.9 7.7 convolution_convert_fusion.10
  562.1 2.9 slice.384.refs_0_
  565.0 21.0 %collective-permute-done.46.refs_1_ = bf16[384,2048]{1,0:T(8,128)(2,1)} collective-permute-done((bf16[384,2048]{1,0:T(8,128)(2,1)S(1)}, bf16[384,2048]{1,0:T(8,128)(2,1)}, u32[]{:S(2)}, u32[]{:S(2)}) %collective-permute-start.46) | collective-permute-done | bytes 1572896 | tf_op jit(solution)/shard_map/ppermute | solution.py:25
  588.2 6.6 norm_back.2
  599.1 3.0 convolution_convert_fusion.14
  603.2 2.7 convolution_convert_fusion.15
  612.9 3.6 convolution_convert_fusion.9
  625.2 37.5 %wkv_backward.1 = (bf16[1536,512]{1,0:T(8,128)(2,1)S(1)}, bf16[1536,512]{1,0:T(8,128)(2,1)S(1)}, bf16[1536,512]{1,0:T(8,128)(2,1)}, bf16[1536,512]{1,0:T(8,128)(2,1)}, f32[8,512]{1,0:T(8,128)S(1)}) custom-call(s32[1]{0:T(128)} %bitcast.here, bf16[1536,512]{1,0:T(8,128)(2,1)} %convolution_convert_fusion.13.r_ref, ...), custom_call_target="tpu_custom_call" | custom-call | flops 25165824000 | bytes 22102016 | tf_op jit(solution)/shard_map/wkv_backward/pallas_call | solution.py:115
  662.7 8.2 convolution_convert_fusion.5
  670.9 6.9 convolution_convert_fusion.4
  685.3 3.7 convolution_convert_fusion.3
  689.0 3.7 convolution_convert_fusion.2
  692.7 4.0 pad_maximum_fusion
  696.6 19.8 %collective-permute-done.63 = bf16[512,2048]{1,0:T(8,128)(2,1)} collective-permute-done((bf16[512,2048]{1,0:T(8,128)(2,1)}, bf16[512,2048]{1,0:T(8,128)(2,1)}, u32[]{:S(2)}, u32[]{:S(2)}) %collective-permute-start.63) | collective-permute-done | bytes 2097184 | tf_op jit(solution)/shard_map/ppermute | solution.py:25
  716.5 3.4 collective-permute-done.64
  719.8 5.6 add_convert_fusion
  730.5 27.3 %mixes_back.3 = (bf16[1536,2048]{1,0:T(8,128)(2,1)}, f32[8,2048]{1,0:T(8,128)S(1)}) custom-call(s32[1]{0:T(128)} %bitcast.here, bf16[1536,512]{1,0:T(8,128)(2,1)S(1)} %copy-done.61, bf16[1536,512]{1,0:T(8,128)(2,1)S(1)} %copy-done.63, bf16[1536,512]{1,0:T(8,128)(2,1)S(1)} %copy-done.65, bf16[1536,512]{1,0:T(8,128)(2,1)} %get-tuple-element.228.refs_3_, ...), custom_call_target="tpu_custom_call" | custom-call | flops 12884901888 | bytes 40763392 | tf_op jit(solution)/shard_map/mixes_back/pallas_call | solution.py:115
  764.6 13.4 %collective-permute-done.39.refs_2_ = bf16[384,512]{1,0:T(8,128)(2,1)S(1)} collective-permute-done((bf16[384,512]{1,0:T(8,128)(2,1)S(1)}, bf16[384,512]{1,0:T(8,128)(2,1)S(1)}, u32[]{:S(2)}, u32[]{:S(2)}) %collective-permute-start.39) | collective-permute-done | bytes 393248 | tf_op jit(solution)/shard_map/ppermute | solution.py:25
  778.3 9.1 %collective-permute-done.41.refs_4_ = bf16[384,512]{1,0:T(8,128)(2,1)S(1)} collective-permute-done((bf16[384,512]{1,0:T(8,128)(2,1)S(1)}, bf16[384,512]{1,0:T(8,128)(2,1)S(1)}, u32[]{:S(2)}, u32[]{:S(2)}) %collective-permute-start.41) | collective-permute-done | bytes 393248 | tf_op jit(solution)/shard_map/ppermute | solution.py:25
  804.0 18.6 %collective-permute-done.58.refs_1_ = bf16[64,512]{1,0:T(8,128)(2,1)S(1)} collective-permute-done((bf16[64,512]{1,0:T(8,128)(2,1)S(1)}, bf16[64,512]{1,0:T(8,128)(2,1)S(1)}, u32[]{:S(2)}, u32[]{:S(2)}) %collective-permute-start.58) | collective-permute-done | bytes 65568 | tf_op jit(solution)/shard_map/ppermute | solution.py:25
  841.1 7.2 norm_back.3
  849.3 4.6 collective-permute-done.68
  855.3 3.8 collective-permute-done.69
  859.1 2.8 collective-permute-start.70
  864.0 5.1 collective-permute-start.71
  872.3 3.4 collective-permute-start.67
  (530 shorter events, 221.3 us)
Async XLA Ops:
  7.2 127.3 %all-gather.8.cloned.1.call-start = ((), (), s32[]{:S(2)}) async-start(), calls=%async_computation.6 | async-start | bytes 7077888 | tf_op jit(solution)/shard_map/all_gather | solution.py:725
  13.3 10.6 %collective-permute-start.6 = (bf16[64,1536]{1,0:T(8,128)(2,1)S(1)}, bf16[64,1536]{1,0:T(8,128)(2,1)S(1)}, u32[]{:S(2)}, u32[]{:S(2)}) collective-permute-start(bf16[64,1536]{1,0:T(8,128)(2,1)S(1)} %get-tuple-element.143), channel_id=1, source_target_pairs={{0,16},{8,24},{16,0},{24,8},{1,17},{9,25},{17,1},{25,9},{2,18},{10... | collective-permute-start | bytes 589832 | tf_op jit(solution)/shard_map/ppermute | solution.py:25
  24.8 142.6 %all-gather.10.cloned.1.call-start = ((), (), s32[]{:S(2)}) async-start(), calls=%async_computation.7 | async-start | bytes 2359296 | tf_op jit(solution)/shard_map/all_gather | solution.py:725
  25.0 42.7 %collective-permute-start.8 = (bf16[384,2048]{1,0:T(8,128)(2,1)S(1)}, bf16[384,2048]{1,0:T(8,128)(2,1)}, u32[]{:S(2)}, u32[]{:S(2)}) collective-permute-start(bf16[384,2048]{1,0:T(8,128)(2,1)S(1)} %bitcast.100), channel_id=1, source_target_pairs={{0,8},{8,0},{16,24},{24,16},{1,9},{9,1},{17,25},{25,17},{2,10},{10... | collective-permute-start | bytes 4718600 | tf_op jit(solution)/shard_map/ppermute | solution.py:25
  26.3 41.4 %collective-permute-start.9 = (bf16[384,2048]{1,0:T(8,128)(2,1)S(1)}, bf16[384,2048]{1,0:T(8,128)(2,1)}, u32[]{:S(2)}, u32[]{:S(2)}) collective-permute-start(bf16[384,2048]{1,0:T(8,128)(2,1)S(1)} %bitcast.101), channel_id=1, source_target_pairs={{0,16},{8,24},{16,0},{24,8},{1,17},{9,25},{17,1},{25,9},{2,18},{10... | collective-permute-start | bytes 4718600 | tf_op jit(solution)/shard_map/ppermute | solution.py:25
  36.2 26.2 %collective-permute-start.3 = (bf16[1,8,14,64]{3,2,1,0:T(8,128)(2,1)S(1)}, bf16[1,8,14,64]{3,2,1,0:T(8,128)(2,1)S(1)}, u32[]{:S(2)}, u32[]{:S(2)}) collective-permute-start(bf16[1,8,14,64]{3,2,1,0:T(8,128)(2,1)S(1)} %get-tuple-element.334), channel_id=1, source_target_pairs={{0,8},{8,0},{16,24},{24,16},{1,9},{9,1},{17,25},{25,17},{2,10},{10... | collective-permute-start | bytes 43016 | tf_op jit(solution)/shard_map/ppermute | solution.py:25
  67.7 161.7 %all-gather.6.cloned.1.call-start = ((), (), s32[]{:S(2)}) async-start(), calls=%async_computation.5 | async-start | bytes 2359296 | tf_op jit(solution)/shard_map/all_gather | solution.py:725
  75.9 284.3 %all-gather.12.cloned.1.call-start = ((), (), s32[]{:S(2)}) async-start(), calls=%async_computation.8 | async-start | bytes 10616832 | tf_op jit(solution)/shard_map/all_gather | solution.py:725
  79.0 17.4 %collective-permute-start.10 = (bf16[192,2048]{1,0:T(8,128)(2,1)S(1)}, bf16[192,2048]{1,0:T(8,128)(2,1)S(1)}, u32[]{:S(2)}, u32[]{:S(2)}) collective-permute-start(bf16[192,2048]{1,0:T(8,128)(2,1)S(1)} %slice.329), channel_id=1, source_target_pairs={{0,16},{8,24},{16,0},{24,8},{1,17},{9,25},{17,1},{25,9},{2,18},{10... | collective-permute-start | bytes 2359304 | tf_op jit(solution)/shard_map/ppermute | solution.py:25
  80.3 17.4 %collective-permute-start.11 = (bf16[192,2048]{1,0:T(8,128)(2,1)S(1)}, bf16[192,2048]{1,0:T(8,128)(2,1)S(1)}, u32[]{:S(2)}, u32[]{:S(2)}) collective-permute-start(bf16[192,2048]{1,0:T(8,128)(2,1)S(1)} %slice.330), channel_id=1, source_target_pairs={{0,8},{8,0},{16,24},{24,16},{1,9},{9,1},{17,25},{25,17},{2,10},{10... | collective-permute-start | bytes 2359304 | tf_op jit(solution)/shard_map/ppermute | solution.py:25
  100.2 29.1 %collective-permute-start.30 = (bf16[64,2304]{1,0:T(8,128)(2,1)}, bf16[64,2304]{1,0:T(8,128)(2,1)S(1)}, u32[]{:S(2)}, u32[]{:S(2)}) collective-permute-start(bf16[64,2304]{1,0:T(8,128)(2,1)} %get-tuple-element.184), channel_id=1, source_target_pairs={{0,8},{8,0},{16,24},{24,16},{1,9},{9,1},{17,25},{25,17},{2,10},{10... | collective-permute-start | bytes 884744 | tf_op jit(solution)/shard_map/ppermute | solution.py:25
  101.4 27.9 %collective-permute-start.31 = (bf16[64,2304]{1,0:T(8,128)(2,1)}, bf16[64,2304]{1,0:T(8,128)(2,1)}, u32[]{:S(2)}, u32[]{:S(2)}) collective-permute-start(bf16[64,2304]{1,0:T(8,128)(2,1)} %get-tuple-element.185), channel_id=1, source_target_pairs={{0,16},{8,24},{16,0},{24,8},{1,17},{9,25},{17,1},{25,9},{2,18},{10... | collective-permute-start | bytes 884744 | tf_op jit(solution)/shard_map/ppermute | solution.py:25
  102.3 27.1 %collective-permute-start.32 = (bf16[64,2304]{1,0:T(8,128)(2,1)}, bf16[64,2304]{1,0:T(8,128)(2,1)}, u32[]{:S(2)}, u32[]{:S(2)}) collective-permute-start(bf16[64,2304]{1,0:T(8,128)(2,1)} %get-tuple-element.186), channel_id=1, source_target_pairs={{0,24},{8,16},{16,8},{24,0},{1,25},{9,17},{17,9},{25,1},{2,26},{10... | collective-permute-start | bytes 884744 | tf_op jit(solution)/shard_map/ppermute | solution.py:25
  131.7 262.5 %all-gather.14.cloned.1.call-start = ((), (), s32[]{:S(2)}) async-start(), calls=%async_computation.9 | async-start | bytes 8257536 | tf_op jit(solution)/shard_map/all_gather | solution.py:725
  131.8 33.5 %collective-permute-start.15 = (bf16[384,2048]{1,0:T(8,128)(2,1)S(1)}, bf16[384,2048]{1,0:T(8,128)(2,1)S(1)}, u32[]{:S(2)}, u32[]{:S(2)}) collective-permute-start(bf16[384,2048]{1,0:T(8,128)(2,1)S(1)} %bitcast.95), channel_id=1, source_target_pairs={{0,8},{8,0},{16,24},{24,16},{1,9},{9,1},{17,25},{25,17},{2,10},{10... | collective-permute-start | bytes 4718600 | tf_op jit(solution)/shard_map/ppermute | solution.py:25
  133.6 33.9 %collective-permute-start.16 = (bf16[384,2048]{1,0:T(8,128)(2,1)S(1)}, bf16[384,2048]{1,0:T(8,128)(2,1)}, u32[]{:S(2)}, u32[]{:S(2)}) collective-permute-start(bf16[384,2048]{1,0:T(8,128)(2,1)S(1)} %bitcast.96), channel_id=1, source_target_pairs={{0,16},{8,24},{16,0},{24,8},{1,17},{9,25},{17,1},{25,9},{2,18},{10... | collective-permute-start | bytes 4718600 | tf_op jit(solution)/shard_map/ppermute | solution.py:25
  134.5 452.3 %reduce-scatter.6.cloned.1.call-start = ((), (), s32[]{:S(2)}) async-start(), calls=%async_computation.10 | async-start | bytes 8257536 | tf_op jit(solution)/shard_map/reduce_scatter | solution.py:728
  167.5 73.6 %collective-permute-start.22 = (bf16[512,2048]{1,0:T(8,128)(2,1)}, bf16[512,2048]{1,0:T(8,128)(2,1)}, u32[]{:S(2)}, u32[]{:S(2)}) collective-permute-start(bf16[512,2048]{1,0:T(8,128)(2,1)} %all-gather.10.cloned.1.call-done.refs_4_), channel_id=1, source_target_pairs={{0,8},{8,0},{16,24},{24,16},{1,9},{9,1},{17,25},{25,17},{2,10},{10... | collective-permute-start | bytes 6291464 | tf_op jit(solution)/shard_map/ppermute | solution.py:25
  167.8 73.3 %collective-permute-start.23 = (bf16[512,2048]{1,0:T(8,128)(2,1)}, bf16[512,2048]{1,0:T(8,128)(2,1)}, u32[]{:S(2)}, u32[]{:S(2)}) collective-permute-start(bf16[512,2048]{1,0:T(8,128)(2,1)} %all-gather.10.cloned.1.call-done.refs_4_), channel_id=1, source_target_pairs={{0,16},{8,24},{16,0},{24,8},{1,17},{9,25},{17,1},{25,9},{2,18},{10... | collective-permute-start | bytes 6291464 | tf_op jit(solution)/shard_map/ppermute | solution.py:25
  174.6 53.0 %collective-permute-start.17 = (bf16[192,2048]{1,0:T(8,128)(2,1)S(1)}, bf16[192,2048]{1,0:T(8,128)(2,1)S(1)}, u32[]{:S(2)}, u32[]{:S(2)}) collective-permute-start(bf16[192,2048]{1,0:T(8,128)(2,1)S(1)} %slice.352), channel_id=1, source_target_pairs={{0,16},{8,24},{16,0},{24,8},{1,17},{9,25},{17,1},{25,9},{2,18},{10... | collective-permute-start | bytes 2359304 | tf_op jit(solution)/shard_map/ppermute | solution.py:25
  175.0 53.5 %collective-permute-start.18 = (bf16[192,2048]{1,0:T(8,128)(2,1)S(1)}, bf16[192,2048]{1,0:T(8,128)(2,1)S(1)}, u32[]{:S(2)}, u32[]{:S(2)}) collective-permute-start(bf16[192,2048]{1,0:T(8,128)(2,1)S(1)} %slice.353), channel_id=1, source_target_pairs={{0,8},{8,0},{16,24},{24,16},{1,9},{9,1},{17,25},{25,17},{2,10},{10... | collective-permute-start | bytes 2359304 | tf_op jit(solution)/shard_map/ppermute | solution.py:25
  244.0 40.1 %collective-permute-start.24 = (bf16[256,2048]{1,0:T(8,128)(2,1)}, bf16[256,2048]{1,0:T(8,128)(2,1)}, u32[]{:S(2)}, u32[]{:S(2)}) collective-permute-start(bf16[256,2048]{1,0:T(8,128)(2,1)} %slice.358), channel_id=1, source_target_pairs={{0,16},{8,24},{16,0},{24,8},{1,17},{9,25},{17,1},{25,9},{2,18},{10... | collective-permute-start | bytes 3145736 | tf_op jit(solution)/shard_map/ppermute | solution.py:25
  247.2 36.9 %collective-permute-start.25 = (bf16[256,2048]{1,0:T(8,128)(2,1)}, bf16[256,2048]{1,0:T(8,128)(2,1)}, u32[]{:S(2)}, u32[]{:S(2)}) collective-permute-start(bf16[256,2048]{1,0:T(8,128)(2,1)} %slice.359), channel_id=1, source_target_pairs={{0,8},{8,0},{16,24},{24,16},{1,9},{9,1},{17,25},{25,17},{2,10},{10... | collective-permute-start | bytes 3145736 | tf_op jit(solution)/shard_map/ppermute | solution.py:25
  249.7 29.5 %collective-permute-start.19 = (bf16[384,512]{1,0:T(8,128)(2,1)}, bf16[384,512]{1,0:T(8,128)(2,1)}, u32[]{:S(2)}, u32[]{:S(2)}) collective-permute-start(bf16[384,512]{1,0:T(8,128)(2,1)} %get-tuple-element.300), channel_id=1, source_target_pairs={{0,8},{8,0},{16,24},{24,16},{1,9},{9,1},{17,25},{25,17},{2,10},{10... | collective-permute-start | bytes 1179656 | tf_op jit(solution)/shard_map/ppermute | solution.py:25
  250.3 28.9 %collective-permute-start.20 = (bf16[384,512]{1,0:T(8,128)(2,1)}, bf16[384,512]{1,0:T(8,128)(2,1)}, u32[]{:S(2)}, u32[]{:S(2)}) collective-permute-start(bf16[384,512]{1,0:T(8,128)(2,1)} %get-tuple-element.299), channel_id=1, source_target_pairs={{0,16},{8,24},{16,0},{24,8},{1,17},{9,25},{17,1},{25,9},{2,18},{10... | collective-permute-start | bytes 1179656 | tf_op jit(solution)/shard_map/ppermute | solution.py:25
  251.5 32.7 %collective-permute-start.21 = (bf16[384,512]{1,0:T(8,128)(2,1)}, bf16[384,512]{1,0:T(8,128)(2,1)}, u32[]{:S(2)}, u32[]{:S(2)}) collective-permute-start(bf16[384,512]{1,0:T(8,128)(2,1)} %get-tuple-element.298), channel_id=1, source_target_pairs={{0,24},{8,16},{16,8},{24,0},{1,25},{9,17},{17,9},{25,1},{2,26},{10... | collective-permute-start | bytes 1179656 | tf_op jit(solution)/shard_map/ppermute | solution.py:25
  293.7 29.5 %collective-permute-start.26 = (bf16[384,2048]{1,0:T(8,128)(2,1)S(1)}, bf16[384,2048]{1,0:T(8,128)(2,1)S(1)}, u32[]{:S(2)}, u32[]{:S(2)}) collective-permute-start(bf16[384,2048]{1,0:T(8,128)(2,1)S(1)} %get-tuple-element.177.refs_0_), channel_id=1, source_target_pairs={{0,8},{8,0},{16,24},{24,16},{1,9},{9,1},{17,25},{25,17},{2,10},{10... | collective-permute-start | bytes 4718600 | tf_op jit(solution)/shard_map/ppermute | solution.py:25
  294.5 32.1 %collective-permute-start.27 = (bf16[384,2048]{1,0:T(8,128)(2,1)S(1)}, bf16[384,2048]{1,0:T(8,128)(2,1)S(1)}, u32[]{:S(2)}, u32[]{:S(2)}) collective-permute-start(bf16[384,2048]{1,0:T(8,128)(2,1)S(1)} %get-tuple-element.177.refs_0_), channel_id=1, source_target_pairs={{0,16},{8,24},{16,0},{24,8},{1,17},{9,25},{17,1},{25,9},{2,18},{10... | collective-permute-start | bytes 4718600 | tf_op jit(solution)/shard_map/ppermute | solution.py:25
  328.9 12.3 %collective-permute-start.28 = (bf16[192,2048]{1,0:T(8,128)(2,1)}, bf16[192,2048]{1,0:T(8,128)(2,1)}, u32[]{:S(2)}, u32[]{:S(2)}) collective-permute-start(bf16[192,2048]{1,0:T(8,128)(2,1)} %slice.360), channel_id=1, source_target_pairs={{0,16},{8,24},{16,0},{24,8},{1,17},{9,25},{17,1},{25,9},{2,18},{10... | collective-permute-start | bytes 2359304 | tf_op jit(solution)/shard_map/ppermute | solution.py:25
  331.6 12.3 %collective-permute-start.29 = (bf16[192,2048]{1,0:T(8,128)(2,1)}, bf16[192,2048]{1,0:T(8,128)(2,1)}, u32[]{:S(2)}, u32[]{:S(2)}) collective-permute-start(bf16[192,2048]{1,0:T(8,128)(2,1)} %slice.361), channel_id=1, source_target_pairs={{0,8},{8,0},{16,24},{24,16},{1,9},{9,1},{17,25},{25,17},{2,10},{10... | collective-permute-start | bytes 2359304 | tf_op jit(solution)/shard_map/ppermute | solution.py:25
  369.8 33.0 %collective-permute-start.33 = (bf16[1536,512]{1,0:T(8,128)(2,1)}, bf16[1536,512]{1,0:T(8,128)(2,1)}, u32[]{:S(2)}, u32[]{:S(2)}) collective-permute-start(bf16[1536,512]{1,0:T(8,128)(2,1)} %get-tuple-element.204.refs_5_), channel_id=1, source_target_pairs={{0,8},{8,0},{16,24},{24,16},{1,9},{9,1},{17,25},{25,17},{2,10},{10... | collective-permute-start | bytes 4718600 | tf_op jit(solution)/shard_map/ppermute | solution.py:25
  370.5 32.2 %collective-permute-start.34 = (bf16[1536,512]{1,0:T(8,128)(2,1)}, bf16[1536,512]{1,0:T(8,128)(2,1)}, u32[]{:S(2)}, u32[]{:S(2)}) collective-permute-start(bf16[1536,512]{1,0:T(8,128)(2,1)} %get-tuple-element.204.refs_5_), channel_id=1, source_target_pairs={{0,16},{8,24},{16,0},{24,8},{1,17},{9,25},{17,1},{25,9},{2,18},{10... | collective-permute-start | bytes 4718600 | tf_op jit(solution)/shard_map/ppermute | solution.py:25
  400.4 40.0 %collective-permute-start.35 = (bf16[768,512]{1,0:T(8,128)(2,1)S(1)}, bf16[768,512]{1,0:T(8,128)(2,1)S(1)}, u32[]{:S(2)}, u32[]{:S(2)}) collective-permute-start(bf16[768,512]{1,0:T(8,128)(2,1)S(1)} %get-tuple-element.297), channel_id=1, source_target_pairs={{0,8},{8,0},{16,24},{24,16},{1,9},{9,1},{17,25},{25,17},{2,10},{10... | collective-permute-start | bytes 2359304 | tf_op jit(solution)/shard_map/ppermute | solution.py:25
  400.9 40.4 %collective-permute-start.36 = (bf16[768,512]{1,0:T(8,128)(2,1)S(1)}, bf16[768,512]{1,0:T(8,128)(2,1)}, u32[]{:S(2)}, u32[]{:S(2)}) collective-permute-start(bf16[768,512]{1,0:T(8,128)(2,1)S(1)} %get-tuple-element.296), channel_id=1, source_target_pairs={{0,16},{8,24},{16,0},{24,8},{1,17},{9,25},{17,1},{25,9},{2,18},{10... | collective-permute-start | bytes 2359304 | tf_op jit(solution)/shard_map/ppermute | solution.py:25
  403.9 25.8 %collective-permute-start.42 = (bf16[768,512]{1,0:T(8,128)(2,1)S(1)}, bf16[768,512]{1,0:T(8,128)(2,1)S(1)}, u32[]{:S(2)}, u32[]{:S(2)}) collective-permute-start(bf16[768,512]{1,0:T(8,128)(2,1)S(1)} %slice.382), channel_id=1, source_target_pairs={{0,16},{8,24},{16,0},{24,8},{1,17},{9,25},{17,1},{25,9},{2,18},{10... | collective-permute-start | bytes 2359304 | tf_op jit(solution)/shard_map/ppermute | solution.py:25
  405.4 24.3 %collective-permute-start.43 = (bf16[768,512]{1,0:T(8,128)(2,1)S(1)}, bf16[768,512]{1,0:T(8,128)(2,1)S(1)}, u32[]{:S(2)}, u32[]{:S(2)}) collective-permute-start(bf16[768,512]{1,0:T(8,128)(2,1)S(1)} %slice.383), channel_id=1, source_target_pairs={{0,8},{8,0},{16,24},{24,16},{1,9},{9,1},{17,25},{25,17},{2,10},{10... | collective-permute-start | bytes 2359304 | tf_op jit(solution)/shard_map/ppermute | solution.py:25
  457.3 339.0 %reduce-scatter.10.cloned.1.call-start = ((), (), s32[]{:S(2)}) async-start(), calls=%async_computation.12 | async-start | bytes 2359296 | tf_op jit(solution)/shard_map/reduce_scatter | solution.py:728
  460.2 28.0 %collective-permute-start.38 = (bf16[1536,512]{1,0:T(8,128)(2,1)S(1)}, bf16[1536,512]{1,0:T(8,128)(2,1)S(1)}, u32[]{:S(2)}, u32[]{:S(2)}) collective-permute-start(bf16[1536,512]{1,0:T(8,128)(2,1)S(1)} %pad_maximum_fusion.4), channel_id=1, source_target_pairs={{0,16},{8,24},{16,0},{24,8},{1,17},{9,25},{17,1},{25,9},{2,18},{10... | collective-permute-start | bytes 4718600 | tf_op jit(solution)/shard_map/ppermute | solution.py:25
  463.0 28.0 %collective-permute-start.37 = (bf16[1536,512]{1,0:T(8,128)(2,1)S(1)}, bf16[1536,512]{1,0:T(8,128)(2,1)S(1)}, u32[]{:S(2)}, u32[]{:S(2)}) collective-permute-start(bf16[1536,512]{1,0:T(8,128)(2,1)S(1)} %pad_maximum_fusion.3), channel_id=1, source_target_pairs={{0,8},{8,0},{16,24},{24,16},{1,9},{9,1},{17,25},{25,17},{2,10},{10... | collective-permute-start | bytes 4718600 | tf_op jit(solution)/shard_map/ppermute | solution.py:25
  532.7 15.2 %collective-permute-start.44 = (bf16[192,2048]{1,0:T(8,128)(2,1)}, bf16[192,2048]{1,0:T(8,128)(2,1)}, u32[]{:S(2)}, u32[]{:S(2)}) collective-permute-start(bf16[192,2048]{1,0:T(8,128)(2,1)} %get-tuple-element.288), channel_id=1, source_target_pairs={{0,8},{8,0},{16,24},{24,16},{1,9},{9,1},{17,25},{25,17},{2,10},{10... | collective-permute-start | bytes 2359304 | tf_op jit(solution)/shard_map/ppermute | solution.py:25
  533.2 14.7 %collective-permute-start.45 = (bf16[192,2048]{1,0:T(8,128)(2,1)}, bf16[192,2048]{1,0:T(8,128)(2,1)}, u32[]{:S(2)}, u32[]{:S(2)}) collective-permute-start(bf16[192,2048]{1,0:T(8,128)(2,1)} %get-tuple-element.287), channel_id=1, source_target_pairs={{0,16},{8,24},{16,0},{24,8},{1,17},{9,25},{17,1},{25,9},{2,18},{10... | collective-permute-start | bytes 2359304 | tf_op jit(solution)/shard_map/ppermute | solution.py:25
  555.6 269.9 %reduce-scatter.8.cloned.1.call-start = ((), (), s32[]{:S(2)}) async-start(), calls=%async_computation.11 | async-start | bytes 8257536 | tf_op jit(solution)/shard_map/reduce_scatter | solution.py:728
  556.4 314.5 %reduce-scatter.12.cloned.1.call-start = ((), (), s32[]{:S(2)}) async-start(), calls=%async_computation.13 | async-start | bytes 9437184 | tf_op jit(solution)/shard_map/reduce_scatter | solution.py:728
  559.2 26.8 %collective-permute-start.46 = (bf16[384,2048]{1,0:T(8,128)(2,1)S(1)}, bf16[384,2048]{1,0:T(8,128)(2,1)}, u32[]{:S(2)}, u32[]{:S(2)}) collective-permute-start(bf16[384,2048]{1,0:T(8,128)(2,1)S(1)} %pad_maximum_fusion.6), channel_id=1, source_target_pairs={{0,8},{8,0},{16,24},{24,16},{1,9},{9,1},{17,25},{25,17},{2,10},{10... | collective-permute-start | bytes 4718600 | tf_op jit(solution)/shard_map/ppermute | solution.py:25
  560.6 26.2 %collective-permute-start.47 = (bf16[384,2048]{1,0:T(8,128)(2,1)S(1)}, bf16[384,2048]{1,0:T(8,128)(2,1)}, u32[]{:S(2)}, u32[]{:S(2)}) collective-permute-start(bf16[384,2048]{1,0:T(8,128)(2,1)S(1)} %pad_maximum_fusion.7), channel_id=1, source_target_pairs={{0,16},{8,24},{16,0},{24,8},{1,17},{9,25},{17,1},{25,9},{2,18},{10... | collective-permute-start | bytes 4718600 | tf_op jit(solution)/shard_map/ppermute | solution.py:25
  597.5 26.3 %collective-permute-start.50 = (bf16[384,512]{1,0:T(8,128)(2,1)S(1)}, bf16[384,512]{1,0:T(8,128)(2,1)S(1)}, u32[]{:S(2)}, u32[]{:S(2)}) collective-permute-start(bf16[384,512]{1,0:T(8,128)(2,1)S(1)} %fusion.11), channel_id=1, source_target_pairs={{0,24},{8,16},{16,8},{24,0},{1,25},{9,17},{17,9},{25,1},{2,26},{10... | collective-permute-start | bytes 1179656 | tf_op jit(solution)/shard_map/ppermute | solution.py:25
  602.1 21.8 %collective-permute-start.49 = (bf16[384,512]{1,0:T(8,128)(2,1)S(1)}, bf16[384,512]{1,0:T(8,128)(2,1)S(1)}, u32[]{:S(2)}, u32[]{:S(2)}) collective-permute-start(bf16[384,512]{1,0:T(8,128)(2,1)S(1)} %convolution_convert_fusion.14), channel_id=1, source_target_pairs={{0,16},{8,24},{16,0},{24,8},{1,17},{9,25},{17,1},{25,9},{2,18},{10... | collective-permute-start | bytes 1179656 | tf_op jit(solution)/shard_map/ppermute | solution.py:25
  605.9 18.0 %collective-permute-start.48 = (bf16[384,512]{1,0:T(8,128)(2,1)S(1)}, bf16[384,512]{1,0:T(8,128)(2,1)S(1)}, u32[]{:S(2)}, u32[]{:S(2)}) collective-permute-start(bf16[384,512]{1,0:T(8,128)(2,1)S(1)} %convolution_convert_fusion.15), channel_id=1, source_target_pairs={{0,8},{8,0},{16,24},{24,16},{1,9},{9,1},{17,25},{25,17},{2,10},{10... | collective-permute-start | bytes 1179656 | tf_op jit(solution)/shard_map/ppermute | solution.py:25
  610.7 67.1 %collective-permute-start.61 = (bf16[256,2048]{1,0:T(8,128)(2,1)}, bf16[256,2048]{1,0:T(8,128)(2,1)S(1)}, u32[]{:S(2)}, u32[]{:S(2)}) collective-permute-start(bf16[256,2048]{1,0:T(8,128)(2,1)} %get-tuple-element.291), channel_id=1, source_target_pairs={{0,8},{8,0},{16,24},{24,16},{1,9},{9,1},{17,25},{25,17},{2,10},{10... | collective-permute-start | bytes 3145736 | tf_op jit(solution)/shard_map/ppermute | solution.py:25
  611.9 65.8 %collective-permute-start.62 = (bf16[256,2048]{1,0:T(8,128)(2,1)}, bf16[256,2048]{1,0:T(8,128)(2,1)}, u32[]{:S(2)}, u32[]{:S(2)}) collective-permute-start(bf16[256,2048]{1,0:T(8,128)(2,1)} %get-tuple-element.290), channel_id=1, source_target_pairs={{0,16},{8,24},{16,0},{24,8},{1,17},{9,25},{17,1},{25,9},{2,18},{10... | collective-permute-start | bytes 3145736 | tf_op jit(solution)/shard_map/ppermute | solution.py:25
  681.1 35.3 %collective-permute-start.63 = (bf16[512,2048]{1,0:T(8,128)(2,1)}, bf16[512,2048]{1,0:T(8,128)(2,1)}, u32[]{:S(2)}, u32[]{:S(2)}) collective-permute-start(bf16[512,2048]{1,0:T(8,128)(2,1)} %pad_maximum_fusion.1), channel_id=1, source_target_pairs={{0,8},{8,0},{16,24},{24,16},{1,9},{9,1},{17,25},{25,17},{2,10},{10... | collective-permute-start | bytes 6291464 | tf_op jit(solution)/shard_map/ppermute | solution.py:25
  685.0 34.9 %collective-permute-start.64 = (bf16[512,2048]{1,0:T(8,128)(2,1)}, bf16[512,2048]{1,0:T(8,128)(2,1)}, u32[]{:S(2)}, u32[]{:S(2)}) collective-permute-start(bf16[512,2048]{1,0:T(8,128)(2,1)} %pad_maximum_fusion.2), channel_id=1, source_target_pairs={{0,16},{8,24},{16,0},{24,8},{1,17},{9,25},{17,1},{25,9},{2,18},{10... | collective-permute-start | bytes 6291464 | tf_op jit(solution)/shard_map/ppermute | solution.py:25
  725.5 152.0 %reduce-scatter.14.cloned.1.call-start = ((), (), s32[]{:S(2)}) async-start(), calls=%async_computation.14 | async-start | bytes 2359296 | tf_op jit(solution)/shard_map/reduce_scatter | solution.py:728
  760.1 30.6 %collective-permute-start.51 = (bf16[192,2048]{1,0:T(8,128)(2,1)S(1)}, bf16[192,2048]{1,0:T(8,128)(2,1)S(1)}, u32[]{:S(2)}, u32[]{:S(2)}) collective-permute-start(bf16[192,2048]{1,0:T(8,128)(2,1)S(1)} %get-tuple-element.282), channel_id=1, source_target_pairs={{0,8},{8,0},{16,24},{24,16},{1,9},{9,1},{17,25},{25,17},{2,10},{10... | collective-permute-start | bytes 2359304 | tf_op jit(solution)/shard_map/ppermute | solution.py:25
  760.2 30.5 %collective-permute-start.52 = (bf16[192,2048]{1,0:T(8,128)(2,1)S(1)}, bf16[192,2048]{1,0:T(8,128)(2,1)S(1)}, u32[]{:S(2)}, u32[]{:S(2)}) collective-permute-start(bf16[192,2048]{1,0:T(8,128)(2,1)S(1)} %get-tuple-element.281), channel_id=1, source_target_pairs={{0,16},{8,24},{16,0},{24,8},{1,17},{9,25},{17,1},{25,9},{2,18},{10... | collective-permute-start | bytes 2359304 | tf_op jit(solution)/shard_map/ppermute | solution.py:25
  761.1 16.9 %collective-permute-start.39 = (bf16[384,512]{1,0:T(8,128)(2,1)S(1)}, bf16[384,512]{1,0:T(8,128)(2,1)S(1)}, u32[]{:S(2)}, u32[]{:S(2)}) collective-permute-start(bf16[384,512]{1,0:T(8,128)(2,1)S(1)} %get-tuple-element.294), channel_id=1, source_target_pairs={{0,8},{8,0},{16,24},{24,16},{1,9},{9,1},{17,25},{25,17},{2,10},{10... | collective-permute-start | bytes 1179656 | tf_op jit(solution)/shard_map/ppermute | solution.py:25
  762.4 15.9 %collective-permute-start.40 = (bf16[384,512]{1,0:T(8,128)(2,1)S(1)}, bf16[384,512]{1,0:T(8,128)(2,1)S(1)}, u32[]{:S(2)}, u32[]{:S(2)}) collective-permute-start(bf16[384,512]{1,0:T(8,128)(2,1)S(1)} %get-tuple-element.293), channel_id=1, source_target_pairs={{0,16},{8,24},{16,0},{24,8},{1,17},{9,25},{17,1},{25,9},{2,18},{10... | collective-permute-start | bytes 1179656 | tf_op jit(solution)/shard_map/ppermute | solution.py:25
  764.4 22.9 %collective-permute-start.41 = (bf16[384,512]{1,0:T(8,128)(2,1)S(1)}, bf16[384,512]{1,0:T(8,128)(2,1)S(1)}, u32[]{:S(2)}, u32[]{:S(2)}) collective-permute-start(bf16[384,512]{1,0:T(8,128)(2,1)S(1)} %get-tuple-element.292), channel_id=1, source_target_pairs={{0,24},{8,16},{16,8},{24,0},{1,25},{9,17},{17,9},{25,1},{2,26},{10... | collective-permute-start | bytes 1179656 | tf_op jit(solution)/shard_map/ppermute | solution.py:25
  794.0 47.1 %collective-permute-start.53 = (bf16[384,2048]{1,0:T(8,128)(2,1)}, bf16[384,2048]{1,0:T(8,128)(2,1)}, u32[]{:S(2)}, u32[]{:S(2)}) collective-permute-start(bf16[384,2048]{1,0:T(8,128)(2,1)} %pad_maximum_fusion.9), channel_id=1, source_target_pairs={{0,8},{8,0},{16,24},{24,16},{1,9},{9,1},{17,25},{25,17},{2,10},{10... | collective-permute-start | bytes 4718600 | tf_op jit(solution)/shard_map/ppermute | solution.py:25
  796.2 44.8 %collective-permute-start.54 = (bf16[384,2048]{1,0:T(8,128)(2,1)}, bf16[384,2048]{1,0:T(8,128)(2,1)}, u32[]{:S(2)}, u32[]{:S(2)}) collective-permute-start(bf16[384,2048]{1,0:T(8,128)(2,1)} %pad_maximum_fusion.10), channel_id=1, source_target_pairs={{0,16},{8,24},{16,0},{24,8},{1,17},{9,25},{17,1},{25,9},{2,18},{10... | collective-permute-start | bytes 4718600 | tf_op jit(solution)/shard_map/ppermute | solution.py:25
  797.3 25.2 %collective-permute-start.58 = (bf16[64,512]{1,0:T(8,128)(2,1)S(1)}, bf16[64,512]{1,0:T(8,128)(2,1)S(1)}, u32[]{:S(2)}, u32[]{:S(2)}) collective-permute-start(bf16[64,512]{1,0:T(8,128)(2,1)S(1)} %get-tuple-element.314), channel_id=1, source_target_pairs={{0,8},{8,0},{16,24},{24,16},{1,9},{9,1},{17,25},{25,17},{2,10},{10... | collective-permute-start | bytes 196616 | tf_op jit(solution)/shard_map/ppermute | solution.py:25
  798.9 25.7 %collective-permute-start.59 = (bf16[64,512]{1,0:T(8,128)(2,1)S(1)}, bf16[64,512]{1,0:T(8,128)(2,1)S(1)}, u32[]{:S(2)}, u32[]{:S(2)}) collective-permute-start(bf16[64,512]{1,0:T(8,128)(2,1)S(1)} %get-tuple-element.313), channel_id=1, source_target_pairs={{0,16},{8,24},{16,0},{24,8},{1,17},{9,25},{17,1},{25,9},{2,18},{10... | collective-permute-start | bytes 196616 | tf_op jit(solution)/shard_map/ppermute | solution.py:25
  800.4 24.2 %collective-permute-start.60 = (bf16[64,512]{1,0:T(8,128)(2,1)S(1)}, bf16[64,512]{1,0:T(8,128)(2,1)S(1)}, u32[]{:S(2)}, u32[]{:S(2)}) collective-permute-start(bf16[64,512]{1,0:T(8,128)(2,1)S(1)} %get-tuple-element.312), channel_id=1, source_target_pairs={{0,24},{8,16},{16,8},{24,0},{1,25},{9,17},{17,9},{25,1},{2,26},{10... | collective-permute-start | bytes 196616 | tf_op jit(solution)/shard_map/ppermute | solution.py:25
  828.7 9.9 %collective-permute-start.56 = (bf16[64,1792]{1,0:T(8,128)(2,1)}, bf16[64,1792]{1,0:T(8,128)(2,1)}, u32[]{:S(2)}, u32[]{:S(2)}) collective-permute-start(bf16[64,1792]{1,0:T(8,128)(2,1)} %get-tuple-element.307), channel_id=1, source_target_pairs={{0,16},{8,24},{16,0},{24,8},{1,17},{9,25},{17,1},{25,9},{2,18},{10... | collective-permute-start | bytes 688136 | tf_op jit(solution)/shard_map/ppermute | solution.py:25
  (130 other events, 1591.7 us)
Sparse Core Ops, SparseCore 0:
  24.9 65.0 all-gather.7
  91.6 27.7 all-gather.9
  121.0 28.5 all-gather.5
  151.2 90.2 all-gather.11
  242.9 71.8 all-gather.13
  457.4 80.1 reduce-scatter.5
  555.7 36.7 reduce-scatter.9
  594.8 78.5 reduce-scatter.7
  725.6 89.5 reduce-scatter.11
  817.3 34.7 reduce-scatter.13

commit v5 on v4

--- a/solution.py
+++ b/solution.py
@@ -358,30 +358,23 @@
     )
 
 
-def after_body(parts, count, here, x_ref, vec_ref, *refs):
-    mixed, weights, (after_ref, normed_ref) = refs[:parts], refs[parts : parts + count], refs[parts + count :]
+def after_body(count, here, x_ref, vec_ref, *refs):
+    after_ref, normed_ref = refs[count:]
     after = x_ref[...].astype(F32)
-    start, width = 0, mixed[0].shape[1]
-    for ref in weights:
-        stop = start + ref.shape[0]
-        left = mixed[start // width][:, start % width : (stop - 1) % width + 1]
-        after = after + dot(left, ref[...], NN)
-        start = stop
+    for ref in refs[:count]:
+        after = after + ref[...].astype(F32)
     after_ref[...] = after
     centred, inverse = centre(after)
     normed_ref[...] = (centred * inverse * vec_ref[0:1, :] + vec_ref[1:2, :]).astype(BF)
 
 
-def after_norm(inputs, mixed, weights, vec, here):
+def after_norm(inputs, terms, vec, here):
     rows, width = inputs.shape
     own = block((CHUNK, width), lambda i, h: (i, 0))
     return kernel(
-        partial(after_body, len(mixed), len(weights)), "after_norm", (rows // CHUNK,), here,
-        [(inputs, own), (vec, fixed(vec.shape))]
-        + [(m, block((CHUNK, m.shape[1]), lambda i, h: (i, 0))) for m in mixed]
-        + [(w, fixed(w.shape)) for w in weights],
+        partial(after_body, len(terms)), "after_norm", (rows // CHUNK,), here,
+        [(inputs, own), (vec, fixed(vec.shape))] + [(t, own) for t in terms],
         [((rows, width), F32, own), ((rows, width), BF, own)],
-        flops=2 * rows * width * width,
     )
 
 
@@ -737,18 +730,19 @@
             return pieces
         return [outside(p, groups, unit) for p in pieces]
 
+    vec_seq = gather_small(vectors[None], "seq")
     columns_in = stacked_columns([w_receptance, w_key, w_value])
     full_in = gather_dp(columns_in)
-    vec_own = gather_small(vectors[None], "dp")
-    vec_parts = gather_small(vec_own[None], "seq")
-    tokens_all = gather_seq(after(inputs_b, columns_in), vec_parts)
-    vectors_there, vec_parts = vec_parts, vec_parts.astype(F32)
-    vec_own = vec_own.transpose(1, 0, 2).reshape(-1, part).astype(F32)
-    vec = vec_parts.transpose(2, 0, 1, 3).reshape(-1, width)
-    turned = vec_parts.transpose(2, 1, 0, 3).reshape(-1, width)
-    arrived = tokens_all[1:3] + [vectors_there]
-    own_o = gather_dp(after(w_output, arrived))
-    full_g = gather_dp(stacked_columns([after(w_gate, arrived)]))
+    vec_parts = gather_small(vec_seq[None], "dp")
+    tokens_all = gather_seq(after(inputs_b, vec_seq), vec_parts)
+    arrived = tokens_all[1:3] + [vec_parts]
+    vec_parts = vec_parts.astype(F32)
+    vec = vec_parts.transpose(2, 1, 0, 3).reshape(-1, width)
+    turned = vec_parts.transpose(2, 0, 1, 3).reshape(-1, width)
+    vec_own = lax.dynamic_slice_in_dim(vec, place * part, part, 1)
+    full_g = gather_dp(stacked_columns([after(w_gate, arrived)], tokens_all))
+    own_o = gather_dp(after(w_output, tokens_all))
+    grad_b_later = after(grad_b, tokens_all)
 
     positions = jnp.arange(length, dtype=jnp.int32)
     piece, first_flags = segment_of(seq_lengths[0], positions)
@@ -761,7 +755,7 @@
     mix_r, mix_k, mix_v, mix_g, step = mixes(
         turn_pieces(tokens_all), marks, rows_of(turned, 0, 1, 2, 3, 4, 5), 4, True, within, here, tile, own_rows // tile
     )
-    full_c = gather_dp(stacked_columns(after([ffn_key, ffn_receptance], tokens_all), mix_r))
+    full_c = gather_dp(stacked_columns(after([ffn_key, ffn_receptance], arrived), mix_r))
     full_ck, full_cr = full_c[:, :hidden_width], full_c[:, hidden_width:]
     full_cv = gather_dp(after(ffn_value, mix_r))
     recept, keyed, valued = (
@@ -769,14 +763,11 @@
         for i, m in enumerate((mix_r, mix_k, mix_v))
     )
     projected = (recept, keyed, valued)
-    grad_all = gather_seq(after(grad_b, arrived), projected)
-    recept = after(recept, grad_all[1:3], projected)
-    own_o = after(own_o, grad_all[1:3], projected)
+    grad_all = gather_seq(grad_b_later, projected)
     wkv, states = wkv_forward(recept, keyed, valued, tables, here, per)
-    gate_pre, mixed = gated(mix_g, full_g, after(wkv, grad_all), tables[5], here, seq)
-    full_o = gather_seq(own_o, mixed)
-    mixed = trade_seq(blocks_of(mixed, seq))
-    after_mix, normed_two = after_norm(inputs_b, mixed, full_o, rows_of(vec, 10, 11), here)
+    gate_pre, mixed = gated(mix_g, full_g, wkv, tables[5], here, seq)
+    attn = [dot(rows, own_o, NN).astype(BF) for rows in blocks_of(after(mixed, grad_all[3:]), seq)]
+    after_mix, normed_two = after_norm(inputs_b, scatter_seq(attn), rows_of(vec, 10, 11), here)
 
     mix_k2, mix_r2, step_two = mixes(
         turn_pieces(gather_seq(normed_two)), marks, rows_of(turned, 10, 11, 12, 13), 2, False, within, here, tile,
@@ -817,36 +808,35 @@
         terms_two = [outside(t, groups, unit, back=True) for t in terms_two]
     d_after, d_attn, norm_sums_two = norm_back(terms_two, after_mix, grad_b, rows_of(vec, 10), within, here)
 
-    o_parts = by_block(full_o)
-    d_mixed = trade_seq([dot(d_attn, w, NT).astype(BF) for w in o_parts])
-    grads_o = [dot(m, d_attn, TN).astype(BF) for m in mixed]
-    d_mixed = after(jnp.concatenate(d_mixed, axis=0), grads_o)
+    d_attn = jnp.concatenate(gather_seq(d_attn), axis=0)
+    d_mixed = dot(d_attn, own_o, NT).astype(BF)
+    grad_wo = dot(mixed, d_attn, TN).astype(BF)
+    d_mixed = after(d_mixed, grad_wo)
+    summed_o = scatter_dp(grad_wo)
     d_recept, d_keyed, d_valued, d_gate, sums = wkv_backward(
         recept, keyed, valued, gate_pre, wkv, d_mixed, states, tables, here, per
     )
-    grad_wo = sum(t.astype(F32) for t in scatter_seq(grads_o)).astype(BF)
+    channel = after(trade_seq(blocks_of(after(channel, d_mixed), seq)), d_recept)
+    out_rows = spread_columns([after_mix], channel, here, False, False, CHUNK, per)
+    (sum_ck,) = owners_rows(after(summed_ck, d_mixed), [ffn_key.shape[1]], d_recept)
     grads_in = [
-        dot(m, d, TN).astype(BF)
+        dot(after(m, out_rows, sum_ck), d, TN).astype(BF)
         for m, d in ((mix_r, d_recept), (mix_k, d_keyed), (mix_v, d_valued), (mix_g, d_gate))
     ]
-    summed_o = scatter_dp(grad_wo)
-    summed_in = scatter_dp(after(jnp.concatenate(grads_in, axis=1), grad_wo))
-    d_recept = after(d_recept, grads_in)
+    summed_in = scatter_dp(jnp.concatenate(grads_in, axis=1))
+    d_recept = after(d_recept, grads_in, summed_o)
     d_normed, sums_one = mixes_back(
         [(i, d, 0, full_in, i, part) for i, d in enumerate((d_recept, d_keyed, d_valued))]
         + [(3, d_gate, 0, full_g, 0, part)],
         step, marks, rows_of(turned, 2, 3, 4, 5), here, seq,
     )
-    channel = after(trade_seq(blocks_of(channel, seq)), d_normed)
-    out_rows = spread_columns([after_mix], channel, here, False, False, CHUNK, per)
-    (sum_ck,) = owners_rows(summed_ck, [ffn_key.shape[1]], d_normed)
-    (sum_cr,) = owners_rows(summed_cr, [width], d_normed)
     sum_cv = after(summed_cv, d_normed).astype(F32)
-    terms = scatter_seq(blocks_of(d_normed, seq), (out_rows, sum_cv), (sum_ck, sum_cr))
+    terms = scatter_seq(blocks_of(d_normed, seq), sum_cv)
     if within is None:
         terms = [outside(t, groups, unit, back=True) for t in terms]
     tokens_grad, _, norm_sums = norm_back(terms, inputs_b, d_after, rows_of(vec, 0), within, here)
 
+    (sum_cr,) = owners_rows(summed_cr, [width])
     sum_o = summed_o.astype(F32)
     sum_r, sum_k, sum_v, sum_g = owners_rows(summed_in, [width] * 4)
 

time: 899 us -> 882 us (0.981)
  waiting for transfers between devices: 293 us -> 313 us
  starting transfers between devices: 85.6 us -> 74.6 us
  local copies, waits for them, and re-layouts: 84.4 us -> 73.8 us
    ppermute x73 -> x67, waiting for transfers between devices: 292 us -> 311 us  [swap(): return lax.ppermute(value, axis, [(i, i ^ distance) for i in range(size)])]
    ppermute x73 -> x67, starting transfers between devices: 85.1 us -> 74.2 us  [swap(): return lax.ppermute(value, axis, [(i, i ^ distance) for i in range(size)])]
    unnamed x219 -> x197, local copies, waits for them, and re-layouts: 34.7 us -> 40.1 us
    dot_general x21 -> x19, matrix products: 151 us -> 148 us  [dot(): return lax.dot_general(left, right, dims, preferred_element_type=F32)]
  transfers between devices with their start and end apart: 83 -> 77, of which waited for: 39 -> 38; matrix products, arithmetic and copies ran while one was open for 25% -> 23% of each run, Pallas kernels for 25% -> 25%
where the time goes in v5:
time: 882 us; the launch traced here: 872 us
  waiting for transfers between devices  313 us (35%)
  Pallas kernels  217 us (25%)
  matrix products  148 us (17%)
  starting transfers between devices  74.6 us (8%)
  local copies, waits for them, and re-layouts  73.8 us (8%)
  other arithmetic  30.5 us (3%)
  between operations  15.8 us (2%)
    ppermute x67, waiting for transfers between devices, swap(): return lax.ppermute(value, axis, [(i, i ^ distance) for i in range(size)])  311 us
    pallas_call x26, Pallas kernels, kernel(): pl.pallas_call(body, out_shape=[jax.ShapeDtypeStruct(shape, kind) for sha...  217 us
    dot_general x19, matrix products, dot(): return lax.dot_general(left, right, dims, preferred_element_type=F32)  148 us
    ppermute x67, starting transfers between devices, swap(): return lax.ppermute(value, axis, [(i, i ^ distance) for i in range(size)])  74.2 us
    unnamed x197, local copies, waits for them, and re-layouts  40.1 us
  transfers between devices with their start and end apart: 77, of which 38 were waited for; matrix products, arithmetic and copies ran while one was open for 23% of the time, Pallas kernels for 25%

profile of v5, /device:TPU:0, one launch (start us, length us, event | category | flops | bytes accessed | tf_op | source)
XLA Modules:
  0.0 872.3 jit_solution(3106315549639452864)
XLA Ops:
  10.3 3.0 collective-permute-start.12
  14.8 4.2 collective-permute-done.12.refs_1_
  19.0 4.8 collective-permute-done.13.refs_2_
  30.3 31.4 %collective-permute-done.1 = bf16[2,14,64]{2,1,0:T(8,128)(2,1)S(1)} collective-permute-done((bf16[2,14,64]{2,1,0:T(8,128)(2,1)S(1)}, bf16[2,14,64]{2,1,0:T(8,128)(2,1)S(1)}, u32[]{:S(2)}, u32[]{:S(2)}) %collective-permute-start.1) | collective-permute-done | bytes 3616 | tf_op jit(solution)/shard_map/ppermute | solution.py:25
  64.6 5.1 collective-permute-done.3
  72.1 9.1 %collective-permute-done.4 = bf16[4,4,14,64]{3,2,1,0:T(8,128)(2,1)} collective-permute-done((bf16[4,4,14,64]{3,2,1,0:T(8,128)(2,1)S(1)}, bf16[4,4,14,64]{3,2,1,0:T(8,128)(2,1)}, u32[]{:S(2)}, u32[]{:S(2)}) %collective-permute-start.4) | collective-permute-done | bytes 28704 | tf_op jit(solution)/shard_map/ppermute | solution.py:25
  90.7 15.9 %collective-permute-done.9.refs_1_ = bf16[64,512]{1,0:T(8,128)(2,1)S(1)} collective-permute-done((bf16[64,512]{1,0:T(8,128)(2,1)S(1)}, bf16[64,512]{1,0:T(8,128)(2,1)S(1)}, u32[]{:S(2)}, u32[]{:S(2)}) %collective-permute-start.9) | collective-permute-done | bytes 65568 | tf_op jit(solution)/shard_map/ppermute | solution.py:25
  121.1 2.8 slice_reduce_fusion.3
  129.2 17.1 %mixes.2 = (bf16[1536,2048]{1,0:T(8,128)(2,1)}, bf16[1536,2048]{1,0:T(8,128)(2,1)}, bf16[1536,2048]{1,0:T(8,128)(2,1)}, bf16[1536,2048]{1,0:T(8,128)(2,1)}, bf16[1536,2048]{1,0:T(8,128)(2,1)}) custom-call(s32[1]{0:T(128)} %bitcast.here, bf16[384,2048]{1,0:T(8,128)(2,1)S(1)} %bitcast.89, bf16[384,2048]{1,0:T(8,128)(2,1)S(1)} %copy-done.17, ...), custom_call_target="tpu_custom_call" | custom-call | bytes 38600704 | tf_op jit(solution)/shard_map/mixes/pallas_call | solution.py:115
  158.2 7.0 convolution_convert_fusion.11.r_ref
  165.3 8.3 convolution_convert_fusion.10.k_ref
  173.5 4.5 convolution_convert_fusion.9.v_ref
  178.1 11.9 %collective-permute-done.15.refs_1_ = bf16[384,2048]{1,0:T(8,128)(2,1)} collective-permute-done((bf16[384,2048]{1,0:T(8,128)(2,1)S(1)}, bf16[384,2048]{1,0:T(8,128)(2,1)}, u32[]{:S(2)}, u32[]{:S(2)}) %collective-permute-start.15) | collective-permute-done | bytes 1572896 | tf_op jit(solution)/shard_map/ppermute | solution.py:25
  196.4 13.5 %wkv_forward.1 = (f32[1536,512]{1,0:T(8,128)}, bf16[12,512,128]{2,1,0:T(8,128)(2,1)S(1)}) custom-call(s32[1]{0:T(128)} %bitcast.here, bf16[1536,512]{1,0:T(8,128)(2,1)S(1)} %convolution_convert_fusion.11.r_ref, bf16[1536,512]{1,0:T(8,128)(2,1)} %convolution_convert_fusion.10.k_ref, bf16[1536,512]{1,0:T(8,128)(2,1)} %convolution_convert_fusion.9.v_ref, ...), custom_call_target="tpu_custom_call" | custom-call | flops 6291456000 | bytes 11075584 | tf_op jit(solution)/shard_map/wkv_forward/pallas_call | solution.py:115
  213.3 10.1 %gate.1 = (f32[1536,512]{1,0:T(8,128)}, bf16[1536,512]{1,0:T(8,128)(2,1)S(1)}) custom-call(s32[1]{0:T(128)} %bitcast.here, bf16[1536,2048]{1,0:T(8,128)(2,1)} %get-tuple-element.248.refs_0_, bf16[2048,512]{1,0:T(8,128)(2,1)S(1)} %copy-done.41, f32[1536,512]{1,0:T(8,128)} %get-tuple-element.168.refs_2_.wkv_ref, f32[8,512]{1,0:T(8,128)S(1)} %maximum_maximum_fusion.par_ref.refs_3_), custom_call_target="tpu_custom_call" | custom-call | flops 3221225472 | bytes 16269312 | tf_op jit(solution)/shard_map/gate/pallas_call | solution.py:115
  224.5 2.8 convolution_convert_fusion.13
  232.8 10.3 %collective-permute-done.19 = bf16[192,2048]{1,0:T(8,128)(2,1)S(1)} collective-permute-done((bf16[192,2048]{1,0:T(8,128)(2,1)S(1)}, bf16[192,2048]{1,0:T(8,128)(2,1)S(1)}, u32[]{:S(2)}, u32[]{:S(2)}) %collective-permute-start.19) | collective-permute-done | bytes 786464 | tf_op jit(solution)/shard_map/ppermute | solution.py:25
  251.5 2.7 convolution_convert_fusion.15.refs_0_
  254.2 23.3 %collective-permute-done.21.refs_1_ = bf16[384,2048]{1,0:T(8,128)(2,1)} collective-permute-done((bf16[384,2048]{1,0:T(8,128)(2,1)}, bf16[384,2048]{1,0:T(8,128)(2,1)}, u32[]{:S(2)}, u32[]{:S(2)}) %collective-permute-start.21) | collective-permute-done | bytes 1572896 | tf_op jit(solution)/shard_map/ppermute | solution.py:25
  279.3 4.7 after_norm.1
  287.2 27.1 %collective-permute-done.23.refs_1_ = bf16[384,2048]{1,0:T(8,128)(2,1)S(1)} collective-permute-done((bf16[384,2048]{1,0:T(8,128)(2,1)S(1)}, bf16[384,2048]{1,0:T(8,128)(2,1)S(1)}, u32[]{:S(2)}, u32[]{:S(2)}) %collective-permute-start.23) | collective-permute-done | bytes 1572896 | tf_op jit(solution)/shard_map/ppermute | solution.py:25
  314.2 3.4 collective-permute-done.24.refs_2_
  323.4 9.0 %collective-permute-done.25.refs_3_ = bf16[192,2048]{1,0:T(8,128)(2,1)} collective-permute-done((bf16[192,2048]{1,0:T(8,128)(2,1)}, bf16[192,2048]{1,0:T(8,128)(2,1)}, u32[]{:S(2)}, u32[]{:S(2)}) %collective-permute-start.25) | collective-permute-done | bytes 786464 | tf_op jit(solution)/shard_map/ppermute | solution.py:25
  338.7 12.6 %mixes.3 = (bf16[1536,2048]{1,0:T(8,128)(2,1)}, bf16[1536,2048]{1,0:T(8,128)(2,1)}, bf16[1536,2048]{1,0:T(8,128)(2,1)}) custom-call(s32[1]{0:T(128)} %bitcast.here, bf16[384,2048]{1,0:T(8,128)(2,1)S(1)} %copy-done.21, bf16[384,2048]{1,0:T(8,128)(2,1)S(1)} %copy-done.19, bf16[384,2048]{1,0:T(8,128)(2,1)} %copy-done.57, ...), custom_call_target="tpu_custom_call" | custom-call | bytes 26017792 | tf_op jit(solution)/shard_map/mixes/pallas_call | solution.py:115
  351.2 9.5 %divide_convert_fusion = (bf16[1536,512]{1,0:T(8,128)(2,1)}, f32[1536,512]{1,0:T(8,128)}) fusion(bf16[1536,2048]{1,0:T(8,128)(2,1)} %get-tuple-element.221, bf16[2048,2304]{1,0:T(8,128)(2,1)} %all-gather.12.cloned.1.call-done.refs_3_.refs_4_.refs_5_), kind=kOutput, calls=%fused_computation.9 | convolution fusion | flops 3224371200 | bytes 13107200 | tf_op jit(solution)/shard_map/dot_general | solution.py:497
  362.0 22.6 %multiply_convert_fusion.1 = (bf16[1536,1792]{1,0:T(8,128)(2,1)}, bf16[1536,1792]{1,0:T(8,128)(2,1)}) fusion(bf16[1536,2048]{1,0:T(8,128)(2,1)} %get-tuple-element.218, bf16[2048,2304]{1,0:T(8,128)(2,1)S(1)} %copy-done.77), kind=kOutput, calls=%fused_computation.2 | convolution fusion | flops 11312824320 | bytes 24641536 | tf_op jit(solution)/shard_map/dot_general | solution.py:497
  384.6 6.2 value_columns.6
  397.6 6.0 value_columns.7
  404.7 6.0 value_columns.4.refs_5_
  411.9 6.0 value_columns.5
  417.9 3.7 collective-permute-done.36
  422.8 10.1 %spread_columns.2 = bf16[1536,2048]{1,0:T(8,128)(2,1)} custom-call(s32[1]{0:T(128)} %bitcast.here, bf16[384,2048]{1,0:T(8,128)(2,1)S(1)} %bitcast.95, bf16[384,2048]{1,0:T(8,128)(2,1)} %collective-permute-done.15.refs_1_, bf16[384,2048]{1,0:T(8,128)(2,1)} %collective-permute-done.16.refs_2_, bf16[192,2048]{1,0:T(8,128)(2,1)} %collective-permute-done.17.refs_3_, ...), custom_call_target="tpu_custom_call" | custom-call | bytes 18874368 | tf_op jit(solution)/shard_map/spread_columns/pallas_call | solution.py:115
  433.9 15.9 %convolution_convert_fusion.1 = bf16[1792,2048]{1,0:T(8,128)(2,1)} fusion(bf16[1536,1792]{1,0:T(8,128)(2,1)S(1)} %bitcast.99, bf16[1536,2048]{1,0:T(8,128)(2,1)} %spread_columns.2), kind=kOutput, calls=%fused_computation.6 | convolution fusion | flops 11277959168 | bytes 19136512 | tf_op jit(solution)/shard_map/dot_general | solution.py:497
  458.8 17.2 %multiply_convert_fusion.refs_0_ = bf16[1536,1792]{1,0:T(8,128)(2,1)} fusion(bf16[1536,1792]{1,0:T(8,128)(2,1)} %get-tuple-element.214, bf16[1536,2048]{1,0:T(8,128)(2,1)S(1)} %copy-done.56, bf16[1792,2048]{1,0:T(8,128)(2,1)} %all-gather.14.cloned.1.call-done.right_ref), kind=kOutput, calls=%fused_computation.1 | convolution fusion | flops 11282546688 | bytes 24641536 | tf_op jit(solution)/shard_map/dot_general | solution.py:497
  476.0 5.5 collective-permute-done.35.refs_7_
  481.5 3.8 collective-permute-done.34.refs_6_
  486.5 7.7 channel.1
  495.3 29.1 %mixes_back.2 = (bf16[1536,2048]{1,0:T(8,128)(2,1)}, f32[8,2048]{1,0:T(8,128)S(1)}) custom-call(s32[1]{0:T(128)} %bitcast.here, bf16[1536,1792]{1,0:T(8,128)(2,1)} %multiply_convert_fusion.refs_0_, bf16[1536,512]{1,0:T(8,128)(2,1)S(1)} %get-tuple-element.215.refs_1_.refs_2_, bf16[1536,512]{1,0:T(8,128)(2,1)S(1)} %get-tuple-element.215.refs_1_.refs_2_, ...), custom_call_target="tpu_custom_call" | custom-call | flops 14495514624 | bytes 50462720 | tf_op jit(solution)/shard_map/mixes_back/pallas_call | solution.py:115
  524.5 16.5 %convolution_convert_fusion = bf16[2048,1792]{1,0:T(8,128)(2,1)} fusion(bf16[1536,2048]{1,0:T(8,128)(2,1)S(1)} %bitcast.114, bf16[1536,1792]{1,0:T(8,128)(2,1)} %multiply_convert_fusion.refs_0_), kind=kOutput, calls=%fused_computation.5 | convolution fusion | flops 11277959168 | bytes 19136512 | tf_op jit(solution)/shard_map/dot_general | solution.py:497
  545.3 15.5 %collective-permute-done.38 = bf16[192,2048]{1,0:T(8,128)(2,1)S(1)} collective-permute-done((bf16[192,2048]{1,0:T(8,128)(2,1)S(1)}, bf16[192,2048]{1,0:T(8,128)(2,1)S(1)}, u32[]{:S(2)}, u32[]{:S(2)}) %collective-permute-start.38) | collective-permute-done | bytes 786464 | tf_op jit(solution)/shard_map/ppermute | solution.py:25
  567.3 5.1 convolution_convert_fusion.8
  572.4 17.0 %collective-permute-done.40.refs_1_ = bf16[384,2048]{1,0:T(8,128)(2,1)} collective-permute-done((bf16[384,2048]{1,0:T(8,128)(2,1)}, bf16[384,2048]{1,0:T(8,128)(2,1)}, u32[]{:S(2)}, u32[]{:S(2)}) %collective-permute-start.40) | collective-permute-done | bytes 1572896 | tf_op jit(solution)/shard_map/ppermute | solution.py:25
  592.1 6.7 norm_back.2
  600.8 30.3 %collective-permute-done.42 = bf16[384,2048]{1,0:T(8,128)(2,1)S(1)} collective-permute-done((bf16[384,2048]{1,0:T(8,128)(2,1)S(1)}, bf16[384,2048]{1,0:T(8,128)(2,1)S(1)}, u32[]{:S(2)}, u32[]{:S(2)}) %collective-permute-start.42) | collective-permute-done | bytes 1572896 | tf_op jit(solution)/shard_map/ppermute | solution.py:25
  635.1 9.2 %collective-permute-done.44 = bf16[192,2048]{1,0:T(8,128)(2,1)S(1)} collective-permute-done((bf16[192,2048]{1,0:T(8,128)(2,1)S(1)}, bf16[192,2048]{1,0:T(8,128)(2,1)S(1)}, u32[]{:S(2)}, u32[]{:S(2)}) %collective-permute-start.44) | collective-permute-done | bytes 786464 | tf_op jit(solution)/shard_map/ppermute | solution.py:25
  645.5 2.6 copy-done.61
  648.0 4.7 convolution_convert_fusion.6
  653.5 8.2 convolution_convert_fusion.7.d_mixed_ref
  671.9 37.5 %wkv_backward.1 = (bf16[1536,512]{1,0:T(8,128)(2,1)S(1)}, bf16[1536,512]{1,0:T(8,128)(2,1)S(1)}, bf16[1536,512]{1,0:T(8,128)(2,1)}, bf16[1536,512]{1,0:T(8,128)(2,1)}, f32[8,512]{1,0:T(8,128)S(1)}) custom-call(s32[1]{0:T(128)} %bitcast.here, bf16[1536,512]{1,0:T(8,128)(2,1)} %copy-done.47, bf16[1536,512]{1,0:T(8,128)(2,1)} %convolution_convert_fusion.10.k_ref, ...), custom_call_target="tpu_custom_call" | custom-call | flops 25165824000 | bytes 22102016 | tf_op jit(solution)/shard_map/wkv_backward/pallas_call | solution.py:115
  712.9 6.8 convolution_convert_fusion.5
  719.8 6.9 convolution_convert_fusion.4
  726.8 3.7 convolution_convert_fusion.3
  730.5 3.7 convolution_convert_fusion.2
  734.2 4.0 pad_maximum_fusion
  743.7 26.3 %mixes_back.3 = (bf16[1536,2048]{1,0:T(8,128)(2,1)}, f32[8,2048]{1,0:T(8,128)S(1)}) custom-call(s32[1]{0:T(128)} %bitcast.here, bf16[1536,512]{1,0:T(8,128)(2,1)S(1)} %copy-done.49, bf16[1536,512]{1,0:T(8,128)(2,1)S(1)} %copy-done.51, bf16[1536,512]{1,0:T(8,128)(2,1)S(1)} %copy-done.53, bf16[1536,512]{1,0:T(8,128)(2,1)} %get-tuple-element.249.refs_3_, ...), custom_call_target="tpu_custom_call" | custom-call | flops 12884901888 | bytes 40763392 | tf_op jit(solution)/shard_map/mixes_back/pallas_call | solution.py:115
  775.7 17.2 %collective-permute-done.52 = bf16[192,2048]{1,0:T(8,128)(2,1)S(1)} collective-permute-done((bf16[192,2048]{1,0:T(8,128)(2,1)S(1)}, bf16[192,2048]{1,0:T(8,128)(2,1)S(1)}, u32[]{:S(2)}, u32[]{:S(2)}) %collective-permute-start.52) | collective-permute-done | bytes 786464 | tf_op jit(solution)/shard_map/ppermute | solution.py:25
  802.2 15.9 %collective-permute-done.54.refs_1_ = bf16[384,2048]{1,0:T(8,128)(2,1)} collective-permute-done((bf16[384,2048]{1,0:T(8,128)(2,1)}, bf16[384,2048]{1,0:T(8,128)(2,1)}, u32[]{:S(2)}, u32[]{:S(2)}) %collective-permute-start.54) | collective-permute-done | bytes 1572896 | tf_op jit(solution)/shard_map/ppermute | solution.py:25
  818.1 3.4 collective-permute-done.55.refs_2_
  821.5 7.3 norm_back.3
  829.7 8.4 collective-permute-done.62
  839.4 3.2 collective-permute-done.63
  842.7 4.8 collective-permute-done.64
  854.6 2.4 collective-permute-start.58
  859.9 3.9 collective-permute-done.57.refs_2_
  (478 shorter events, 191.2 us)
Async XLA Ops:
  7.2 151.0 %all-gather.8.cloned.1.call-start = ((), (), s32[]{:S(2)}) async-start(), calls=%async_computation.6 | async-start | bytes 7077888 | tf_op jit(solution)/shard_map/all_gather | solution.py:718
  13.3 10.6 %collective-permute-start.13 = (bf16[64,1536]{1,0:T(8,128)(2,1)S(1)}, bf16[64,1536]{1,0:T(8,128)(2,1)S(1)}, u32[]{:S(2)}, u32[]{:S(2)}) collective-permute-start(bf16[64,1536]{1,0:T(8,128)(2,1)S(1)} %get-tuple-element.160), channel_id=1, source_target_pairs={{0,16},{8,24},{16,0},{24,8},{1,17},{9,25},{17,1},{25,9},{2,18},{10... | collective-permute-start | bytes 589832 | tf_op jit(solution)/shard_map/ppermute | solution.py:25
  14.8 9.1 %collective-permute-start.14 = (bf16[64,1536]{1,0:T(8,128)(2,1)S(1)}, bf16[64,1536]{1,0:T(8,128)(2,1)S(1)}, u32[]{:S(2)}, u32[]{:S(2)}) collective-permute-start(bf16[64,1536]{1,0:T(8,128)(2,1)S(1)} %get-tuple-element.161), channel_id=1, source_target_pairs={{0,24},{8,16},{16,8},{24,0},{1,25},{9,17},{17,9},{25,1},{2,26},{10... | collective-permute-start | bytes 589832 | tf_op jit(solution)/shard_map/ppermute | solution.py:25
  24.8 186.9 %all-gather.6.cloned.1.call-start = ((), (), s32[]{:S(2)}) async-start(), calls=%async_computation.5 | async-start | bytes 2359296 | tf_op jit(solution)/shard_map/all_gather | solution.py:718
  26.2 56.8 %collective-permute-start.5 = (bf16[384,2048]{1,0:T(8,128)(2,1)S(1)}, bf16[384,2048]{1,0:T(8,128)(2,1)S(1)}, u32[]{:S(2)}, u32[]{:S(2)}) collective-permute-start(bf16[384,2048]{1,0:T(8,128)(2,1)S(1)} %bitcast.87), channel_id=1, source_target_pairs={{0,8},{8,0},{16,24},{24,16},{1,9},{9,1},{17,25},{25,17},{2,10},{10... | collective-permute-start | bytes 4718600 | tf_op jit(solution)/shard_map/ppermute | solution.py:25
  27.0 56.0 %collective-permute-start.6 = (bf16[384,2048]{1,0:T(8,128)(2,1)S(1)}, bf16[384,2048]{1,0:T(8,128)(2,1)}, u32[]{:S(2)}, u32[]{:S(2)}) collective-permute-start(bf16[384,2048]{1,0:T(8,128)(2,1)S(1)} %bitcast.88), channel_id=1, source_target_pairs={{0,16},{8,24},{16,0},{24,8},{1,17},{9,25},{17,1},{25,9},{2,18},{10... | collective-permute-start | bytes 4718600 | tf_op jit(solution)/shard_map/ppermute | solution.py:25
  28.6 33.0 %collective-permute-start.1 = (bf16[2,14,64]{2,1,0:T(8,128)(2,1)S(1)}, bf16[2,14,64]{2,1,0:T(8,128)(2,1)S(1)}, u32[]{:S(2)}, u32[]{:S(2)}) collective-permute-start(bf16[2,14,64]{2,1,0:T(8,128)(2,1)S(1)} %pad_maximum_fusion.15), channel_id=1, source_target_pairs={{0,16},{8,24},{16,0},{24,8},{1,17},{9,25},{17,1},{25,9},{2,18},{10... | collective-permute-start | bytes 10760 | tf_op jit(solution)/shard_map/ppermute | solution.py:25
  69.8 11.5 %collective-permute-start.4 = (bf16[4,4,14,64]{3,2,1,0:T(8,128)(2,1)S(1)}, bf16[4,4,14,64]{3,2,1,0:T(8,128)(2,1)}, u32[]{:S(2)}, u32[]{:S(2)}) collective-permute-start(bf16[4,4,14,64]{3,2,1,0:T(8,128)(2,1)S(1)} %pad_maximum_fusion.11), channel_id=1, source_target_pairs={{0,4},{1,5},{2,6},{3,7},{4,0},{5,1},{6,2},{7,3},{8,12},{9,13},{10,... | collective-permute-start | bytes 86024 | tf_op jit(solution)/shard_map/ppermute | solution.py:25
  83.0 24.8 %collective-permute-start.7 = (bf16[192,2048]{1,0:T(8,128)(2,1)S(1)}, bf16[192,2048]{1,0:T(8,128)(2,1)S(1)}, u32[]{:S(2)}, u32[]{:S(2)}) collective-permute-start(bf16[192,2048]{1,0:T(8,128)(2,1)S(1)} %slice.325), channel_id=1, source_target_pairs={{0,16},{8,24},{16,0},{24,8},{1,17},{9,25},{17,1},{25,9},{2,18},{10... | collective-permute-start | bytes 2359304 | tf_op jit(solution)/shard_map/ppermute | solution.py:25
  85.6 23.1 %collective-permute-start.8 = (bf16[192,2048]{1,0:T(8,128)(2,1)S(1)}, bf16[192,2048]{1,0:T(8,128)(2,1)S(1)}, u32[]{:S(2)}, u32[]{:S(2)}) collective-permute-start(bf16[192,2048]{1,0:T(8,128)(2,1)S(1)} %slice.326), channel_id=1, source_target_pairs={{0,8},{8,0},{16,24},{24,16},{1,9},{9,1},{17,25},{25,17},{2,10},{10... | collective-permute-start | bytes 2359304 | tf_op jit(solution)/shard_map/ppermute | solution.py:25
  87.1 19.4 %collective-permute-start.9 = (bf16[64,512]{1,0:T(8,128)(2,1)S(1)}, bf16[64,512]{1,0:T(8,128)(2,1)S(1)}, u32[]{:S(2)}, u32[]{:S(2)}) collective-permute-start(bf16[64,512]{1,0:T(8,128)(2,1)S(1)} %get-tuple-element.150), channel_id=1, source_target_pairs={{0,8},{8,0},{16,24},{24,16},{1,9},{9,1},{17,25},{25,17},{2,10},{10... | collective-permute-start | bytes 196616 | tf_op jit(solution)/shard_map/ppermute | solution.py:25
  87.8 18.8 %collective-permute-start.10 = (bf16[64,512]{1,0:T(8,128)(2,1)S(1)}, bf16[64,512]{1,0:T(8,128)(2,1)S(1)}, u32[]{:S(2)}, u32[]{:S(2)}) collective-permute-start(bf16[64,512]{1,0:T(8,128)(2,1)S(1)} %get-tuple-element.151), channel_id=1, source_target_pairs={{0,16},{8,24},{16,0},{24,8},{1,17},{9,25},{17,1},{25,9},{2,18},{10... | collective-permute-start | bytes 196616 | tf_op jit(solution)/shard_map/ppermute | solution.py:25
  88.5 19.3 %collective-permute-start.11 = (bf16[64,512]{1,0:T(8,128)(2,1)S(1)}, bf16[64,512]{1,0:T(8,128)(2,1)S(1)}, u32[]{:S(2)}, u32[]{:S(2)}) collective-permute-start(bf16[64,512]{1,0:T(8,128)(2,1)S(1)} %get-tuple-element.152), channel_id=1, source_target_pairs={{0,24},{8,16},{16,8},{24,0},{1,25},{9,17},{17,9},{25,1},{2,26},{10... | collective-permute-start | bytes 196616 | tf_op jit(solution)/shard_map/ppermute | solution.py:25
  110.3 114.2 %all-gather.10.cloned.1.call-start = ((), (), s32[]{:S(2)}) async-start(), calls=%async_computation.7 | async-start | bytes 2359296 | tf_op jit(solution)/shard_map/all_gather | solution.py:718
  111.1 240.2 %all-gather.12.cloned.1.call-start = ((), (), s32[]{:S(2)}) async-start(), calls=%async_computation.8 | async-start | bytes 10616832 | tf_op jit(solution)/shard_map/all_gather | solution.py:718
  115.2 32.1 %collective-permute-start.27 = (bf16[64,2304]{1,0:T(8,128)(2,1)}, bf16[64,2304]{1,0:T(8,128)(2,1)}, u32[]{:S(2)}, u32[]{:S(2)}) collective-permute-start(bf16[64,2304]{1,0:T(8,128)(2,1)} %get-tuple-element.188), channel_id=1, source_target_pairs={{0,8},{8,0},{16,24},{24,16},{1,9},{9,1},{17,25},{25,17},{2,10},{10... | collective-permute-start | bytes 884744 | tf_op jit(solution)/shard_map/ppermute | solution.py:25
  116.6 30.7 %collective-permute-start.28 = (bf16[64,2304]{1,0:T(8,128)(2,1)}, bf16[64,2304]{1,0:T(8,128)(2,1)}, u32[]{:S(2)}, u32[]{:S(2)}) collective-permute-start(bf16[64,2304]{1,0:T(8,128)(2,1)} %get-tuple-element.189), channel_id=1, source_target_pairs={{0,16},{8,24},{16,0},{24,8},{1,17},{9,25},{17,1},{25,9},{2,18},{10... | collective-permute-start | bytes 884744 | tf_op jit(solution)/shard_map/ppermute | solution.py:25
  117.4 29.9 %collective-permute-start.29 = (bf16[64,2304]{1,0:T(8,128)(2,1)}, bf16[64,2304]{1,0:T(8,128)(2,1)}, u32[]{:S(2)}, u32[]{:S(2)}) collective-permute-start(bf16[64,2304]{1,0:T(8,128)(2,1)} %get-tuple-element.190), channel_id=1, source_target_pairs={{0,24},{8,16},{16,8},{24,0},{1,25},{9,17},{17,9},{25,1},{2,26},{10... | collective-permute-start | bytes 884744 | tf_op jit(solution)/shard_map/ppermute | solution.py:25
  149.7 234.9 %all-gather.14.cloned.1.call-start = ((), (), s32[]{:S(2)}) async-start(), calls=%async_computation.9 | async-start | bytes 8257536 | tf_op jit(solution)/shard_map/all_gather | solution.py:718
  155.8 34.2 %collective-permute-start.15 = (bf16[384,2048]{1,0:T(8,128)(2,1)S(1)}, bf16[384,2048]{1,0:T(8,128)(2,1)}, u32[]{:S(2)}, u32[]{:S(2)}) collective-permute-start(bf16[384,2048]{1,0:T(8,128)(2,1)S(1)} %bitcast.93), channel_id=1, source_target_pairs={{0,8},{8,0},{16,24},{24,16},{1,9},{9,1},{17,25},{25,17},{2,10},{10... | collective-permute-start | bytes 4718600 | tf_op jit(solution)/shard_map/ppermute | solution.py:25
  157.3 33.9 %collective-permute-start.16 = (bf16[384,2048]{1,0:T(8,128)(2,1)S(1)}, bf16[384,2048]{1,0:T(8,128)(2,1)}, u32[]{:S(2)}, u32[]{:S(2)}) collective-permute-start(bf16[384,2048]{1,0:T(8,128)(2,1)S(1)} %bitcast.94), channel_id=1, source_target_pairs={{0,16},{8,24},{16,0},{24,8},{1,17},{9,25},{17,1},{25,9},{2,18},{10... | collective-permute-start | bytes 4718600 | tf_op jit(solution)/shard_map/ppermute | solution.py:25
  158.1 432.5 %reduce-scatter.6.cloned.1.call-start = ((), (), s32[]{:S(2)}) async-start(), calls=%async_computation.10 | async-start | bytes 8257536 | tf_op jit(solution)/shard_map/reduce_scatter | solution.py:721
  193.3 31.2 %collective-permute-start.17 = (bf16[192,2048]{1,0:T(8,128)(2,1)}, bf16[192,2048]{1,0:T(8,128)(2,1)}, u32[]{:S(2)}, u32[]{:S(2)}) collective-permute-start(bf16[192,2048]{1,0:T(8,128)(2,1)} %slice.347), channel_id=1, source_target_pairs={{0,16},{8,24},{16,0},{24,8},{1,17},{9,25},{17,1},{25,9},{2,18},{10... | collective-permute-start | bytes 2359304 | tf_op jit(solution)/shard_map/ppermute | solution.py:25
  195.6 28.9 %collective-permute-start.18 = (bf16[192,2048]{1,0:T(8,128)(2,1)}, bf16[192,2048]{1,0:T(8,128)(2,1)}, u32[]{:S(2)}, u32[]{:S(2)}) collective-permute-start(bf16[192,2048]{1,0:T(8,128)(2,1)} %slice.348), channel_id=1, source_target_pairs={{0,8},{8,0},{16,24},{24,16},{1,9},{9,1},{17,25},{25,17},{2,10},{10... | collective-permute-start | bytes 2359304 | tf_op jit(solution)/shard_map/ppermute | solution.py:25
  227.5 15.6 %collective-permute-start.19 = (bf16[192,2048]{1,0:T(8,128)(2,1)S(1)}, bf16[192,2048]{1,0:T(8,128)(2,1)S(1)}, u32[]{:S(2)}, u32[]{:S(2)}) collective-permute-start(bf16[192,2048]{1,0:T(8,128)(2,1)S(1)} %get-tuple-element.310), channel_id=1, source_target_pairs={{0,8},{8,0},{16,24},{24,16},{1,9},{9,1},{17,25},{25,17},{2,10},{10... | collective-permute-start | bytes 2359304 | tf_op jit(solution)/shard_map/ppermute | solution.py:25
  228.9 15.4 %collective-permute-start.20 = (bf16[192,2048]{1,0:T(8,128)(2,1)S(1)}, bf16[192,2048]{1,0:T(8,128)(2,1)S(1)}, u32[]{:S(2)}, u32[]{:S(2)}) collective-permute-start(bf16[192,2048]{1,0:T(8,128)(2,1)S(1)} %get-tuple-element.309), channel_id=1, source_target_pairs={{0,16},{8,24},{16,0},{24,8},{1,17},{9,25},{17,1},{25,9},{2,18},{10... | collective-permute-start | bytes 2359304 | tf_op jit(solution)/shard_map/ppermute | solution.py:25
  245.8 31.8 %collective-permute-start.21 = (bf16[384,2048]{1,0:T(8,128)(2,1)}, bf16[384,2048]{1,0:T(8,128)(2,1)}, u32[]{:S(2)}, u32[]{:S(2)}) collective-permute-start(bf16[384,2048]{1,0:T(8,128)(2,1)} %pad_maximum_fusion.1), channel_id=1, source_target_pairs={{0,8},{8,0},{16,24},{24,16},{1,9},{9,1},{17,25},{25,17},{2,10},{10... | collective-permute-start | bytes 4718600 | tf_op jit(solution)/shard_map/ppermute | solution.py:25
  247.9 31.4 %collective-permute-start.22 = (bf16[384,2048]{1,0:T(8,128)(2,1)}, bf16[384,2048]{1,0:T(8,128)(2,1)}, u32[]{:S(2)}, u32[]{:S(2)}) collective-permute-start(bf16[384,2048]{1,0:T(8,128)(2,1)} %pad_maximum_fusion.2), channel_id=1, source_target_pairs={{0,16},{8,24},{16,0},{24,8},{1,17},{9,25},{17,1},{25,9},{2,18},{10... | collective-permute-start | bytes 4718600 | tf_op jit(solution)/shard_map/ppermute | solution.py:25
  284.1 30.2 %collective-permute-start.23 = (bf16[384,2048]{1,0:T(8,128)(2,1)S(1)}, bf16[384,2048]{1,0:T(8,128)(2,1)S(1)}, u32[]{:S(2)}, u32[]{:S(2)}) collective-permute-start(bf16[384,2048]{1,0:T(8,128)(2,1)S(1)} %get-tuple-element.181.refs_0_), channel_id=1, source_target_pairs={{0,8},{8,0},{16,24},{24,16},{1,9},{9,1},{17,25},{25,17},{2,10},{10... | collective-permute-start | bytes 4718600 | tf_op jit(solution)/shard_map/ppermute | solution.py:25
  285.5 32.1 %collective-permute-start.24 = (bf16[384,2048]{1,0:T(8,128)(2,1)S(1)}, bf16[384,2048]{1,0:T(8,128)(2,1)S(1)}, u32[]{:S(2)}, u32[]{:S(2)}) collective-permute-start(bf16[384,2048]{1,0:T(8,128)(2,1)S(1)} %get-tuple-element.181.refs_0_), channel_id=1, source_target_pairs={{0,16},{8,24},{16,0},{24,8},{1,17},{9,25},{17,1},{25,9},{2,18},{10... | collective-permute-start | bytes 4718600 | tf_op jit(solution)/shard_map/ppermute | solution.py:25
  319.8 12.6 %collective-permute-start.25 = (bf16[192,2048]{1,0:T(8,128)(2,1)}, bf16[192,2048]{1,0:T(8,128)(2,1)}, u32[]{:S(2)}, u32[]{:S(2)}) collective-permute-start(bf16[192,2048]{1,0:T(8,128)(2,1)} %slice.359), channel_id=1, source_target_pairs={{0,16},{8,24},{16,0},{24,8},{1,17},{9,25},{17,1},{25,9},{2,18},{10... | collective-permute-start | bytes 2359304 | tf_op jit(solution)/shard_map/ppermute | solution.py:25
  322.4 12.3 %collective-permute-start.26 = (bf16[192,2048]{1,0:T(8,128)(2,1)}, bf16[192,2048]{1,0:T(8,128)(2,1)}, u32[]{:S(2)}, u32[]{:S(2)}) collective-permute-start(bf16[192,2048]{1,0:T(8,128)(2,1)} %slice.360), channel_id=1, source_target_pairs={{0,8},{8,0},{16,24},{24,16},{1,9},{9,1},{17,25},{25,17},{2,10},{10... | collective-permute-start | bytes 2359304 | tf_op jit(solution)/shard_map/ppermute | solution.py:25
  360.7 33.0 %collective-permute-start.30 = (bf16[1536,512]{1,0:T(8,128)(2,1)}, bf16[1536,512]{1,0:T(8,128)(2,1)}, u32[]{:S(2)}, u32[]{:S(2)}) collective-permute-start(bf16[1536,512]{1,0:T(8,128)(2,1)} %get-tuple-element.207.refs_5_), channel_id=1, source_target_pairs={{0,8},{8,0},{16,24},{24,16},{1,9},{9,1},{17,25},{25,17},{2,10},{10... | collective-permute-start | bytes 4718600 | tf_op jit(solution)/shard_map/ppermute | solution.py:25
  362.0 31.8 %collective-permute-start.31 = (bf16[1536,512]{1,0:T(8,128)(2,1)}, bf16[1536,512]{1,0:T(8,128)(2,1)}, u32[]{:S(2)}, u32[]{:S(2)}) collective-permute-start(bf16[1536,512]{1,0:T(8,128)(2,1)} %get-tuple-element.207.refs_5_), channel_id=1, source_target_pairs={{0,16},{8,24},{16,0},{24,8},{1,17},{9,25},{17,1},{25,9},{2,18},{10... | collective-permute-start | bytes 4718600 | tf_op jit(solution)/shard_map/ppermute | solution.py:25
  390.9 42.1 %collective-permute-start.32 = (bf16[768,512]{1,0:T(8,128)(2,1)S(1)}, bf16[768,512]{1,0:T(8,128)(2,1)S(1)}, u32[]{:S(2)}, u32[]{:S(2)}) collective-permute-start(bf16[768,512]{1,0:T(8,128)(2,1)S(1)} %get-tuple-element.308), channel_id=1, source_target_pairs={{0,8},{8,0},{16,24},{24,16},{1,9},{9,1},{17,25},{25,17},{2,10},{10... | collective-permute-start | bytes 2359304 | tf_op jit(solution)/shard_map/ppermute | solution.py:25
  392.1 41.8 %collective-permute-start.33 = (bf16[768,512]{1,0:T(8,128)(2,1)S(1)}, bf16[768,512]{1,0:T(8,128)(2,1)}, u32[]{:S(2)}, u32[]{:S(2)}) collective-permute-start(bf16[768,512]{1,0:T(8,128)(2,1)S(1)} %get-tuple-element.307), channel_id=1, source_target_pairs={{0,16},{8,24},{16,0},{24,8},{1,17},{9,25},{17,1},{25,9},{2,18},{10... | collective-permute-start | bytes 2359304 | tf_op jit(solution)/shard_map/ppermute | solution.py:25
  395.0 26.6 %collective-permute-start.36 = (bf16[768,512]{1,0:T(8,128)(2,1)S(1)}, bf16[768,512]{1,0:T(8,128)(2,1)S(1)}, u32[]{:S(2)}, u32[]{:S(2)}) collective-permute-start(bf16[768,512]{1,0:T(8,128)(2,1)S(1)} %slice.377), channel_id=1, source_target_pairs={{0,16},{8,24},{16,0},{24,8},{1,17},{9,25},{17,1},{25,9},{2,18},{10... | collective-permute-start | bytes 2359304 | tf_op jit(solution)/shard_map/ppermute | solution.py:25
  396.6 25.0 %collective-permute-start.37 = (bf16[768,512]{1,0:T(8,128)(2,1)S(1)}, bf16[768,512]{1,0:T(8,128)(2,1)S(1)}, u32[]{:S(2)}, u32[]{:S(2)}) collective-permute-start(bf16[768,512]{1,0:T(8,128)(2,1)S(1)} %slice.378), channel_id=1, source_target_pairs={{0,8},{8,0},{16,24},{24,16},{1,9},{9,1},{17,25},{25,17},{2,10},{10... | collective-permute-start | bytes 2359304 | tf_op jit(solution)/shard_map/ppermute | solution.py:25
  449.8 212.0 %reduce-scatter.8.cloned.1.call-start = ((), (), s32[]{:S(2)}) async-start(), calls=%async_computation.11 | async-start | bytes 8257536 | tf_op jit(solution)/shard_map/reduce_scatter | solution.py:721
  452.8 28.7 %collective-permute-start.35 = (bf16[1536,512]{1,0:T(8,128)(2,1)S(1)}, bf16[1536,512]{1,0:T(8,128)(2,1)}, u32[]{:S(2)}, u32[]{:S(2)}) collective-permute-start(bf16[1536,512]{1,0:T(8,128)(2,1)S(1)} %pad_maximum_fusion.4), channel_id=1, source_target_pairs={{0,16},{8,24},{16,0},{24,8},{1,17},{9,25},{17,1},{25,9},{2,18},{10... | collective-permute-start | bytes 4718600 | tf_op jit(solution)/shard_map/ppermute | solution.py:25
  457.5 27.7 %collective-permute-start.34 = (bf16[1536,512]{1,0:T(8,128)(2,1)}, bf16[1536,512]{1,0:T(8,128)(2,1)S(1)}, u32[]{:S(2)}, u32[]{:S(2)}) collective-permute-start(bf16[1536,512]{1,0:T(8,128)(2,1)} %pad_maximum_fusion.3), channel_id=1, source_target_pairs={{0,8},{8,0},{16,24},{24,16},{1,9},{9,1},{17,25},{25,17},{2,10},{10... | collective-permute-start | bytes 4718600 | tf_op jit(solution)/shard_map/ppermute | solution.py:25
  541.0 198.1 %reduce-scatter.10.cloned.1.call-start = ((), (), s32[]{:S(2)}) async-start(), calls=%async_computation.12 | async-start | bytes 2359296 | tf_op jit(solution)/shard_map/reduce_scatter | solution.py:721
  543.3 17.6 %collective-permute-start.38 = (bf16[192,2048]{1,0:T(8,128)(2,1)S(1)}, bf16[192,2048]{1,0:T(8,128)(2,1)S(1)}, u32[]{:S(2)}, u32[]{:S(2)}) collective-permute-start(bf16[192,2048]{1,0:T(8,128)(2,1)S(1)} %get-tuple-element.301), channel_id=1, source_target_pairs={{0,8},{8,0},{16,24},{24,16},{1,9},{9,1},{17,25},{25,17},{2,10},{10... | collective-permute-start | bytes 2359304 | tf_op jit(solution)/shard_map/ppermute | solution.py:25
  544.4 16.5 %collective-permute-start.39 = (bf16[192,2048]{1,0:T(8,128)(2,1)S(1)}, bf16[192,2048]{1,0:T(8,128)(2,1)S(1)}, u32[]{:S(2)}, u32[]{:S(2)}) collective-permute-start(bf16[192,2048]{1,0:T(8,128)(2,1)S(1)} %get-tuple-element.300), channel_id=1, source_target_pairs={{0,16},{8,24},{16,0},{24,8},{1,17},{9,25},{17,1},{25,9},{2,18},{10... | collective-permute-start | bytes 2359304 | tf_op jit(solution)/shard_map/ppermute | solution.py:25
  562.7 26.7 %collective-permute-start.40 = (bf16[384,2048]{1,0:T(8,128)(2,1)}, bf16[384,2048]{1,0:T(8,128)(2,1)}, u32[]{:S(2)}, u32[]{:S(2)}) collective-permute-start(bf16[384,2048]{1,0:T(8,128)(2,1)} %pad_maximum_fusion.6), channel_id=1, source_target_pairs={{0,8},{8,0},{16,24},{24,16},{1,9},{9,1},{17,25},{25,17},{2,10},{10... | collective-permute-start | bytes 4718600 | tf_op jit(solution)/shard_map/ppermute | solution.py:25
  565.0 25.6 %collective-permute-start.41 = (bf16[384,2048]{1,0:T(8,128)(2,1)}, bf16[384,2048]{1,0:T(8,128)(2,1)}, u32[]{:S(2)}, u32[]{:S(2)}) collective-permute-start(bf16[384,2048]{1,0:T(8,128)(2,1)} %pad_maximum_fusion.7), channel_id=1, source_target_pairs={{0,16},{8,24},{16,0},{24,8},{1,17},{9,25},{17,1},{25,9},{2,18},{10... | collective-permute-start | bytes 4718600 | tf_op jit(solution)/shard_map/ppermute | solution.py:25
  598.8 32.4 %collective-permute-start.42 = (bf16[384,2048]{1,0:T(8,128)(2,1)S(1)}, bf16[384,2048]{1,0:T(8,128)(2,1)S(1)}, u32[]{:S(2)}, u32[]{:S(2)}) collective-permute-start(bf16[384,2048]{1,0:T(8,128)(2,1)S(1)} %get-tuple-element.225), channel_id=1, source_target_pairs={{0,8},{8,0},{16,24},{24,16},{1,9},{9,1},{17,25},{25,17},{2,10},{10... | collective-permute-start | bytes 4718600 | tf_op jit(solution)/shard_map/ppermute | solution.py:25
  599.9 32.3 %collective-permute-start.43 = (bf16[384,2048]{1,0:T(8,128)(2,1)S(1)}, bf16[384,2048]{1,0:T(8,128)(2,1)S(1)}, u32[]{:S(2)}, u32[]{:S(2)}) collective-permute-start(bf16[384,2048]{1,0:T(8,128)(2,1)S(1)} %get-tuple-element.225), channel_id=1, source_target_pairs={{0,16},{8,24},{16,0},{24,8},{1,17},{9,25},{17,1},{25,9},{2,18},{10... | collective-permute-start | bytes 4718600 | tf_op jit(solution)/shard_map/ppermute | solution.py:25
  632.3 12.1 %collective-permute-start.44 = (bf16[192,2048]{1,0:T(8,128)(2,1)S(1)}, bf16[192,2048]{1,0:T(8,128)(2,1)S(1)}, u32[]{:S(2)}, u32[]{:S(2)}) collective-permute-start(bf16[192,2048]{1,0:T(8,128)(2,1)S(1)} %slice.386), channel_id=1, source_target_pairs={{0,16},{8,24},{16,0},{24,8},{1,17},{9,25},{17,1},{25,9},{2,18},{10... | collective-permute-start | bytes 2359304 | tf_op jit(solution)/shard_map/ppermute | solution.py:25
  633.3 12.1 %collective-permute-start.45 = (bf16[192,2048]{1,0:T(8,128)(2,1)S(1)}, bf16[192,2048]{1,0:T(8,128)(2,1)S(1)}, u32[]{:S(2)}, u32[]{:S(2)}) collective-permute-start(bf16[192,2048]{1,0:T(8,128)(2,1)S(1)} %slice.387), channel_id=1, source_target_pairs={{0,8},{8,0},{16,24},{24,16},{1,9},{9,1},{17,25},{25,17},{2,10},{10... | collective-permute-start | bytes 2359304 | tf_op jit(solution)/shard_map/ppermute | solution.py:25
  652.7 194.9 %reduce-scatter.14.cloned.1.call-start = ((), (), s32[]{:S(2)}) async-start(), calls=%async_computation.14 | async-start | bytes 2359296 | tf_op jit(solution)/shard_map/reduce_scatter | solution.py:721
  653.5 198.7 %reduce-scatter.12.cloned.1.call-start = ((), (), s32[]{:S(2)}) async-start(), calls=%async_computation.13 | async-start | bytes 9437184 | tf_op jit(solution)/shard_map/reduce_scatter | solution.py:721
  666.0 44.9 %collective-permute-start.46 = (bf16[384,512]{1,0:T(8,128)(2,1)S(1)}, bf16[384,512]{1,0:T(8,128)(2,1)S(1)}, u32[]{:S(2)}, u32[]{:S(2)}) collective-permute-start(bf16[384,512]{1,0:T(8,128)(2,1)S(1)} %get-tuple-element.305), channel_id=1, source_target_pairs={{0,8},{8,0},{16,24},{24,16},{1,9},{9,1},{17,25},{25,17},{2,10},{10... | collective-permute-start | bytes 1179656 | tf_op jit(solution)/shard_map/ppermute | solution.py:25
  666.9 44.0 %collective-permute-start.47 = (bf16[384,512]{1,0:T(8,128)(2,1)S(1)}, bf16[384,512]{1,0:T(8,128)(2,1)S(1)}, u32[]{:S(2)}, u32[]{:S(2)}) collective-permute-start(bf16[384,512]{1,0:T(8,128)(2,1)S(1)} %get-tuple-element.304), channel_id=1, source_target_pairs={{0,16},{8,24},{16,0},{24,8},{1,17},{9,25},{17,1},{25,9},{2,18},{10... | collective-permute-start | bytes 1179656 | tf_op jit(solution)/shard_map/ppermute | solution.py:25
  667.8 43.1 %collective-permute-start.48 = (bf16[384,512]{1,0:T(8,128)(2,1)S(1)}, bf16[384,512]{1,0:T(8,128)(2,1)S(1)}, u32[]{:S(2)}, u32[]{:S(2)}) collective-permute-start(bf16[384,512]{1,0:T(8,128)(2,1)S(1)} %get-tuple-element.303), channel_id=1, source_target_pairs={{0,24},{8,16},{16,8},{24,0},{1,25},{9,17},{17,9},{25,1},{2,26},{10... | collective-permute-start | bytes 1179656 | tf_op jit(solution)/shard_map/ppermute | solution.py:25
  669.6 39.8 %collective-permute-start.50 = (bf16[64,1792]{1,0:T(8,128)(2,1)S(1)}, bf16[64,1792]{1,0:T(8,128)(2,1)S(1)}, u32[]{:S(2)}, u32[]{:S(2)}) collective-permute-start(bf16[64,1792]{1,0:T(8,128)(2,1)S(1)} %get-tuple-element.316), channel_id=1, source_target_pairs={{0,16},{8,24},{16,0},{24,8},{1,17},{9,25},{17,1},{25,9},{2,18},{10... | collective-permute-start | bytes 688136 | tf_op jit(solution)/shard_map/ppermute | solution.py:25
  670.2 39.1 %collective-permute-start.51 = (bf16[64,1792]{1,0:T(8,128)(2,1)S(1)}, bf16[64,1792]{1,0:T(8,128)(2,1)S(1)}, u32[]{:S(2)}, u32[]{:S(2)}) collective-permute-start(bf16[64,1792]{1,0:T(8,128)(2,1)S(1)} %get-tuple-element.315), channel_id=1, source_target_pairs={{0,24},{8,16},{16,8},{24,0},{1,25},{9,17},{17,9},{25,1},{2,26},{10... | collective-permute-start | bytes 688136 | tf_op jit(solution)/shard_map/ppermute | solution.py:25
  772.3 20.5 %collective-permute-start.52 = (bf16[192,2048]{1,0:T(8,128)(2,1)S(1)}, bf16[192,2048]{1,0:T(8,128)(2,1)S(1)}, u32[]{:S(2)}, u32[]{:S(2)}) collective-permute-start(bf16[192,2048]{1,0:T(8,128)(2,1)S(1)} %get-tuple-element.295), channel_id=1, source_target_pairs={{0,8},{8,0},{16,24},{24,16},{1,9},{9,1},{17,25},{25,17},{2,10},{10... | collective-permute-start | bytes 2359304 | tf_op jit(solution)/shard_map/ppermute | solution.py:25
  773.3 20.4 %collective-permute-start.53 = (bf16[192,2048]{1,0:T(8,128)(2,1)S(1)}, bf16[192,2048]{1,0:T(8,128)(2,1)S(1)}, u32[]{:S(2)}, u32[]{:S(2)}) collective-permute-start(bf16[192,2048]{1,0:T(8,128)(2,1)S(1)} %get-tuple-element.294), channel_id=1, source_target_pairs={{0,16},{8,24},{16,0},{24,8},{1,17},{9,25},{17,1},{25,9},{2,18},{10... | collective-permute-start | bytes 2359304 | tf_op jit(solution)/shard_map/ppermute | solution.py:25
  797.0 21.1 %collective-permute-start.54 = (bf16[384,2048]{1,0:T(8,128)(2,1)}, bf16[384,2048]{1,0:T(8,128)(2,1)}, u32[]{:S(2)}, u32[]{:S(2)}) collective-permute-start(bf16[384,2048]{1,0:T(8,128)(2,1)} %pad_maximum_fusion.8), channel_id=1, source_target_pairs={{0,8},{8,0},{16,24},{24,16},{1,9},{9,1},{17,25},{25,17},{2,10},{10... | collective-permute-start | bytes 4718600 | tf_op jit(solution)/shard_map/ppermute | solution.py:25
  799.4 22.1 %collective-permute-start.55 = (bf16[384,2048]{1,0:T(8,128)(2,1)}, bf16[384,2048]{1,0:T(8,128)(2,1)}, u32[]{:S(2)}, u32[]{:S(2)}) collective-permute-start(bf16[384,2048]{1,0:T(8,128)(2,1)} %pad_maximum_fusion.9), channel_id=1, source_target_pairs={{0,16},{8,24},{16,0},{24,8},{1,17},{9,25},{17,1},{25,9},{2,18},{10... | collective-permute-start | bytes 4718600 | tf_op jit(solution)/shard_map/ppermute | solution.py:25
  829.1 9.1 %collective-permute-start.62 = (f32[16,14,64]{2,1,0:T(8,128)S(1)}, f32[16,14,64]{2,1,0:T(8,128)S(1)}, u32[]{:S(2)}, u32[]{:S(2)}) collective-permute-start(f32[16,14,64]{2,1,0:T(8,128)S(1)} %copy.95), channel_id=1, source_target_pairs={{0,16},{8,24},{16,0},{24,8},{1,17},{9,25},{17,1},{25,9},{2,18},{10... | collective-permute-start | bytes 172040 | tf_op jit(solution)/shard_map/ppermute | solution.py:25
  854.6 9.2 %collective-permute-start.57 = (bf16[64,2048]{1,0:T(8,128)(2,1)S(1)}, bf16[64,2048]{1,0:T(8,128)(2,1)S(1)}, u32[]{:S(2)}, u32[]{:S(2)}) collective-permute-start(bf16[64,2048]{1,0:T(8,128)(2,1)S(1)} %get-tuple-element.312), channel_id=1, source_target_pairs={{0,16},{8,24},{16,0},{24,8},{1,17},{9,25},{17,1},{25,9},{2,18},{10... | collective-permute-start | bytes 786440 | tf_op jit(solution)/shard_map/ppermute | solution.py:25
  854.6 9.2 %collective-permute-start.58 = (bf16[64,2048]{1,0:T(8,128)(2,1)S(1)}, bf16[64,2048]{1,0:T(8,128)(2,1)S(1)}, u32[]{:S(2)}, u32[]{:S(2)}) collective-permute-start(bf16[64,2048]{1,0:T(8,128)(2,1)S(1)} %get-tuple-element.311), channel_id=1, source_target_pairs={{0,24},{8,16},{16,8},{24,0},{1,25},{9,17},{17,9},{25,1},{2,26},{10... | collective-permute-start | bytes 786440 | tf_op jit(solution)/shard_map/ppermute | solution.py:25
  (109 other events, 1041.6 us)
Sparse Core Ops, SparseCore 0:
  24.9 67.7 all-gather.7
  110.4 27.5 all-gather.5
  139.6 28.7 all-gather.9
  169.9 90.0 all-gather.11
  261.5 71.8 all-gather.13
  449.9 77.2 reduce-scatter.5
  541.1 76.8 reduce-scatter.7
  652.8 33.1 reduce-scatter.9
  688.3 34.5 reduce-scatter.13
  738.4 87.0 reduce-scatter.11

commit v6 on v5

--- a/solution.py
+++ b/solution.py
@@ -53,17 +53,22 @@
     return swap(parts[3][:half], "seq", 1), swap(parts[3][half:], "seq", 2)
 
 
-def scatter_seq(parts, first=(), second=(), started=None):
-    started = scatter_start(parts) if started is None else started
-    size = lax.axis_size("seq")
-    if size == 4:
-        own, one, two, far = parts
-        half = far.shape[0] // 2
-        low, high = after(started, first)
-        two = jnp.concatenate([(two[:half].astype(F32) + low.astype(F32)).astype(BF), two[half:]], axis=0)
-        one = jnp.concatenate([one[:half], (one[half:].astype(F32) + high.astype(F32)).astype(BF)], axis=0)
-        return after([own, swap(one, "seq", 1), swap(two, "seq", 2)], second)
-    return after([parts[0]] + [swap(parts[distance], "seq", distance) for distance in range(1, size)], first, second)
+def scatter_relay(parts, started):
+    if lax.axis_size("seq") != 4:
+        return parts[1:]
+    (_, one, two, _), (low, high) = parts, started
+    half = low.shape[0]
+    two = jnp.concatenate([(two[:half].astype(F32) + low.astype(F32)).astype(BF), two[half:]], axis=0)
+    one = jnp.concatenate([one[:half], (one[half:].astype(F32) + high.astype(F32)).astype(BF)], axis=0)
+    return [one, two]
+
+
+def scatter_end(own, relayed):
+    return [own] + [swap(part, "seq", j + 1) for j, part in enumerate(relayed)]
+
+
+def scatter_seq(parts):
+    return scatter_end(parts[0], scatter_relay(parts, scatter_start(parts)))
 
 
 def trade_seq(parts):
@@ -122,7 +127,6 @@
             out_specs=[spec for _, _, spec in outs],
             scratch_shapes=list(scratch),
         ),
-        cost_estimate=pl.CostEstimate(flops=flops, bytes_accessed=moved, transcendentals=0),
         compiler_params=pltpu.CompilerParams(vmem_limit_bytes=vmem * 2**20),
         name=name,
     )(here, *[array for array, _ in ins])
@@ -185,18 +189,35 @@
 
 
 def stack_body(parts, here, *refs):
-    for j in range(parts):
-        refs[-1][here[0] ^ j] = refs[j][...]
-
-
-def stack_rows(pieces, here):
-    parts, (rows, width) = len(pieces), pieces[0].shape
-    (stacked,) = kernel(
+    start = 0
+    for out in refs[parts:]:
+        for j in range(parts):
+            out[here[0] ^ j] = refs[j][:, start : start + out.shape[2]]
+        start += out.shape[2]
+
+
+def stack_rows(pieces, widths, here):
+    parts, rows = len(pieces), pieces[0].shape[0]
+    return kernel(
         partial(stack_body, parts), "stack_rows", (1,), here,
         [(p, fixed(p.shape)) for p in pieces],
-        [((parts, rows, width), BF, fixed((parts, rows, width)))],
-    )
-    return stacked
+        [((parts, rows, width), BF, fixed((parts, rows, width))) for width in widths],
+    )
+
+
+def hold_body(here, in_ref, *refs):
+    refs[-1][...] = in_ref[...]
+
+
+def held_back(values, here, *others):
+    rows, width = values.shape
+    own = block((rows // 2, width), lambda i, h: (i, 0))
+    (copy,) = kernel(
+        hold_body, "hold", (2,), here,
+        [(values, own)] + [(o, pl.BlockSpec(memory_space=pl.ANY)) for o in others],
+        [((rows, width), values.dtype, own)],
+    )
+    return copy
 
 
 def join_body(parts, count, here, *refs):
@@ -308,54 +329,85 @@
     )
 
 
-def mixes_back_body(which, here, *refs):
+def mixes_back_body(which, first, seq, here, *refs):
     count = len(which)
-    grads, weights = refs[:count], refs[count : 2 * count]
-    step_ref, marks_ref, vec_ref, out_ref, sums_ref, later = refs[2 * count :]
+    grads, nexts, weights = refs[:count], refs[count : 2 * count], refs[2 * count : 3 * count]
+    step_ref, marks_ref, next_marks_ref, vec_ref, out_ref, sums_ref = refs[3 * count :]
 
     @pl.when(pl.program_id(1) == 0)
     def _():
-        later[...] = jnp.zeros_like(later)
         sums_ref[...] = jnp.zeros_like(sums_ref)
 
     step = step_ref[...].astype(F32)
+    rows = step.shape[0]
     total = straight = None
     for i in range(which[-1] + 1):
-        grad = sum(dot(grads[k][...], weights[k][...], NT) for k in range(count) if which[k] == i)
-        sums_ref[i : i + 1, :] += jnp.sum(grad * step, axis=0, keepdims=True)
+        grad = sum(
+            dot(jnp.concatenate([grads[k][...], nexts[k][...]], axis=0), weights[k][...], NT)
+            for k in range(count)
+            if which[k] == i
+        )
+        sums_ref[i : i + 1, :] += jnp.sum(grad[:rows] * step, axis=0, keepdims=True)
         part = grad * vec_ref[i : i + 1, :]
         total, straight = (total + grad, straight + part) if i else (grad, part)
-    kept = (total - straight) * marks_ref[:, 3:4]
-    rows = kept.shape[0]
-    up = jnp.where(row_index(rows) == rows - 1, later[0:1, :], pltpu.roll(kept, rows - 1, 0))
-    later[0:1, :] = kept[0:1, :]
-    out_ref[...] = (straight + up).astype(BF)
-
-
-def mixes_back(terms, step, marks, vec, here, seq):
+    inside = ((first + pl.program_id(1)) ^ here[0]) < seq - 1
+    keep = jnp.concatenate([marks_ref[:, 3:4], jnp.where(inside, next_marks_ref[:, 3:4], 0.0)], axis=0)
+    kept = (total - straight) * keep
+    up = pltpu.roll(kept, kept.shape[0] - 1, 0)
+    out_ref[...] = (straight[:rows] + up[:rows]).astype(BF)
+
+
+EXTRA = 16
+
+
+def mixes_back(terms, step, marks, vec, here, seq, first, count):
     rows, width = step.shape
     tile, columns = rows // seq, min(512, width)
-    last = rows // tile - 1
-
-    def own(i, h):
-        return relative(last - i, 1, h)
-
-    ins = [(g, block((tile, n), lambda c, i, h, at=at: (own(i, h), at))) for _, g, at, _, _, n in terms]
+    extras = tile // EXTRA
+
+    def following(i, h):
+        return jnp.minimum(((first + i) ^ h) + 1, seq - 1)
+
+    ins = [(g, block((tile, n), lambda c, i, h, at=at: (first + i, at))) for _, g, at, _, _, n in terms]
+    ins += [
+        (g, block((EXTRA, n), lambda c, i, h, at=at: ((following(i, h) ^ h) * extras, at)))
+        for _, g, at, _, _, n in terms
+    ]
     ins += [(w, block((columns, n), lambda c, i, h, at=at: (c, at))) for _, _, _, w, at, n in terms]
     ins += [
-        (step, block((tile, columns), lambda c, i, h: (own(i, h), c))),
-        (marks, block((tile, PAIR), lambda c, i, h: (last - i, 0))),
+        (step, block((tile, columns), lambda c, i, h: (first + i, c))),
+        (marks, block((tile, PAIR), lambda c, i, h: ((first + i) ^ h, 0))),
+        (marks, block((EXTRA, PAIR), lambda c, i, h: (following(i, h) * extras, 0))),
         (vec, block((8, columns), lambda c, i, h: (0, c))),
     ]
     return kernel(
-        partial(mixes_back_body, [t[0] for t in terms]), "mixes_back", (width // columns, last + 1), here, ins,
+        partial(mixes_back_body, [t[0] for t in terms], first, seq), "mixes_back", (width // columns, count), here, ins,
         [
-            ((rows, width), BF, block((tile, columns), lambda c, i, h: (own(i, h), c))),
+            ((count * tile, width), BF, block((tile, columns), lambda c, i, h: (i, c))),
             ((8, width), F32, block((8, columns), lambda c, i, h: (0, c))),
         ],
-        [pltpu.VMEM((8, columns), F32)],
-        flops=2 * rows * width * sum(t[-1] for t in terms),
-    )
+        flops=2 * count * tile * width * sum(t[-1] for t in terms),
+    )
+
+
+def mixes_back_scatter(terms, step, marks, vec, here, seq, beside, ready=()):
+    if seq != 4:
+        grad, sums = mixes_back(terms, step, marks, vec, here, seq, 0, seq)
+        return after(scatter_seq(blocks_of(grad, seq)), beside(grad)), sums
+
+    def call(first, count, *before):
+        ordered = after([t[1] for t in terms], *before)
+        return mixes_back(
+            [(t[0], g) + t[2:] for t, g in zip(terms, ordered)], step, marks, vec, here, seq, first, count
+        )
+
+    far, sums_far = call(3, 1, ready)
+    near, sums_near = call(1, 2, far)
+    parts = [None] + blocks_of(near, 2) + [far]
+    started = after(scatter_start(parts), near)
+    relayed = scatter_relay(parts, started)
+    own, sums_own = call(0, 1, near, relayed)
+    return after(scatter_end(own, relayed), beside(relayed)), sums_far + sums_near + sums_own
 
 
 def after_body(count, here, x_ref, vec_ref, *refs):
@@ -710,9 +762,9 @@
     groups = (seq, dp)
     within = groups if unit == HEAD else None
 
-    def stacked_columns(weights, beside=()):
-        stacked = stack_rows(after(trade_seq(cut_columns(weights, here, seq)), beside), here)
-        return stacked.reshape(-1, stacked.shape[-1])
+    def stacked_columns(weights, widths, beside=()):
+        stacked = stack_rows(after(trade_seq(cut_columns(weights, here, seq)), beside), widths, here)
+        return [w.reshape(-1, w.shape[-1]) for w in stacked]
 
     def gather_dp(rows):
         return lax.all_gather(rows, "dp", axis=0, tiled=True)
@@ -730,40 +782,40 @@
             return pieces
         return [outside(p, groups, unit) for p in pieces]
 
+    positions = jnp.arange(length, dtype=jnp.int32)
+    piece, first_flags = segment_of(seq_lengths[0], positions)
+
+    columns_in, columns_g = stacked_columns([w_receptance, w_key, w_value, w_gate], [3 * part, part])
+    full_in = gather_dp(columns_in)
     vec_seq = gather_small(vectors[None], "seq")
-    columns_in = stacked_columns([w_receptance, w_key, w_value])
-    full_in = gather_dp(columns_in)
-    vec_parts = gather_small(vec_seq[None], "dp")
-    tokens_all = gather_seq(after(inputs_b, vec_seq), vec_parts)
-    arrived = tokens_all[1:3] + [vec_parts]
-    vec_parts = vec_parts.astype(F32)
+    tokens_held = held_back(inputs_b, here, vec_seq)
+    vec_parts = gather_small(vec_seq[None], "dp").astype(F32)
     vec = vec_parts.transpose(2, 1, 0, 3).reshape(-1, width)
     turned = vec_parts.transpose(2, 0, 1, 3).reshape(-1, width)
     vec_own = lax.dynamic_slice_in_dim(vec, place * part, part, 1)
-    full_g = gather_dp(stacked_columns([after(w_gate, arrived)], tokens_all))
-    own_o = gather_dp(after(w_output, tokens_all))
-    grad_b_later = after(grad_b, tokens_all)
-
-    positions = jnp.arange(length, dtype=jnp.int32)
-    piece, first_flags = segment_of(seq_lengths[0], positions)
     log_decay = -jnp.exp(vec_own[6])
     tables = wkv_tables(
         piece, 1.0 - first_flags.astype(F32), log_decay, vec_own[7], vec_own[8], vec_own[9]
     )
     marks = tables[0]
+    rows_one = rows_of(turned, 0, 1, 2, 3, 4, 5)
+    tokens_all = gather_seq(tokens_held, (rows_one, tables))
+    full_g = gather_dp(after(columns_g, tokens_all[1:3], rows_one))
+    own_o = gather_dp(after(w_output, tokens_all))
 
     mix_r, mix_k, mix_v, mix_g, step = mixes(
-        turn_pieces(tokens_all), marks, rows_of(turned, 0, 1, 2, 3, 4, 5), 4, True, within, here, tile, own_rows // tile
-    )
-    full_c = gather_dp(stacked_columns(after([ffn_key, ffn_receptance], arrived), mix_r))
-    full_ck, full_cr = full_c[:, :hidden_width], full_c[:, hidden_width:]
-    full_cv = gather_dp(after(ffn_value, mix_r))
+        turn_pieces(tokens_all), marks, rows_one, 4, True, within, here, tile, own_rows // tile
+    )
     recept, keyed, valued = (
         dot(m, full_in[:, i * part : (i + 1) * part], NN).astype(BF)
         for i, m in enumerate((mix_r, mix_k, mix_v))
     )
     projected = (recept, keyed, valued)
-    grad_all = gather_seq(grad_b_later, projected)
+    (columns_c,) = stacked_columns(after([ffn_key, ffn_receptance], mix_r), [hidden_width + part], projected)
+    full_c = gather_dp(columns_c)
+    full_ck, full_cr = full_c[:, :hidden_width], full_c[:, hidden_width:]
+    full_cv = gather_dp(after(ffn_value, columns_c))
+    grad_all = gather_seq(after(grad_b, mix_r), projected)
     wkv, states = wkv_forward(recept, keyed, valued, tables, here, per)
     gate_pre, mixed = gated(mix_g, full_g, wkv, tables[5], here, seq)
     attn = [dot(rows, own_o, NN).astype(BF) for rows in blocks_of(after(mixed, grad_all[3:]), seq)]
@@ -782,33 +834,37 @@
     hidden, slope = lax.optimization_barrier((hidden, slope))
     later = after(hidden, opened[1:3])
     value_parts = [columns_product(later if j < 2 else hidden, full_cv, part, j, here, seq) for j in reversed(range(seq))]
-    value_started = scatter_start(value_parts[::-1])
-    d_value = spread_columns(grad_all, by_block(after(opened, value_parts)), here, True, True, tile, own_rows // tile)
-
-    grad_cv = dot(hidden, after(d_value, value_started), TN).astype(BF)
+    value_parts = value_parts[::-1]
+    value_relayed = scatter_relay(value_parts, scatter_start(value_parts))
+    d_value = spread_columns(
+        grad_all, by_block(after(opened, value_parts, value_relayed)), here, True, True, tile, own_rows // tile
+    )
+
+    grad_cv = dot(hidden, d_value, TN).astype(BF)
     summed_cv = scatter_dp(grad_cv)
+    value_terms = scatter_end(value_parts[0], value_relayed)
     d_hidden = dot(after(d_value, grad_cv), full_cv, NT)
     d_key_two = (d_hidden * slope.astype(F32)).astype(BF)
-    value_terms = scatter_seq(value_parts[::-1], started=value_started)
     channel, d_recept_two = channel_out(value_terms, recept_pre, grad_all, here, tile)
     half, first = part // 2, hidden_width // (part // 2)
-    d_normed_two, sums_two = mixes_back(
+    grad_ck, grad_cr = [], []
+
+    def beside_two(relayed):
+        grad_ck.append(dot(after(mix_k2, relayed), d_key_two, TN).astype(BF))
+        grad_cr.append(dot(after(mix_r2, relayed, grad_ck), d_recept_two, TN).astype(BF))
+        return grad_ck, grad_cr
+
+    terms_two, sums_two = mixes_back_scatter(
         [(0, d_key_two, 0, full_c, 0, hidden_width)]
         + [(1, d_recept_two, i, full_c, first + i, half) for i in range(2)],
-        step_two, marks, rows_of(turned, 12, 13), here, seq,
-    )
-    grad_ck = dot(after(mix_k2, d_normed_two), d_key_two, TN).astype(BF)
-    d_normed_two = blocks_of(d_normed_two, seq)
-    started = scatter_start(d_normed_two)
-    grad_cr = dot(after(mix_r2, grad_ck, started), d_recept_two, TN).astype(BF)
-    terms_two = scatter_seq(d_normed_two, grad_ck, (grad_cr, summed_cv), started)
-    summed_ck = scatter_dp(grad_ck)
-    summed_cr = scatter_dp(grad_cr)
+        step_two, marks, rows_of(turned, 12, 13), here, seq, beside_two,
+    )
+    summed_ck, summed_cr = scatter_dp(grad_ck[0]), scatter_dp(grad_cr[0])
     if within is None:
         terms_two = [outside(t, groups, unit, back=True) for t in terms_two]
     d_after, d_attn, norm_sums_two = norm_back(terms_two, after_mix, grad_b, rows_of(vec, 10), within, here)
 
-    d_attn = jnp.concatenate(gather_seq(d_attn), axis=0)
+    d_attn = jnp.concatenate(after(gather_seq(d_attn), summed_cv), axis=0)
     d_mixed = dot(d_attn, own_o, NT).astype(BF)
     grad_wo = dot(mixed, d_attn, TN).astype(BF)
     d_mixed = after(d_mixed, grad_wo)
@@ -816,29 +872,37 @@
     d_recept, d_keyed, d_valued, d_gate, sums = wkv_backward(
         recept, keyed, valued, gate_pre, wkv, d_mixed, states, tables, here, per
     )
-    channel = after(trade_seq(blocks_of(after(channel, d_mixed), seq)), d_recept)
-    out_rows = spread_columns([after_mix], channel, here, False, False, CHUNK, per)
-    (sum_ck,) = owners_rows(after(summed_ck, d_mixed), [ffn_key.shape[1]], d_recept)
-    grads_in = [
-        dot(after(m, out_rows, sum_ck), d, TN).astype(BF)
-        for m, d in ((mix_r, d_recept), (mix_k, d_keyed), (mix_v, d_valued), (mix_g, d_gate))
-    ]
-    summed_in = scatter_dp(jnp.concatenate(grads_in, axis=1))
-    d_recept = after(d_recept, grads_in, summed_o)
-    d_normed, sums_one = mixes_back(
+    channel = trade_seq(blocks_of(after(channel, d_mixed), seq))
+    channel = after(channel, d_recept)
+    grads_vg = [dot(mix_v, d_valued, TN).astype(BF), dot(mix_g, d_gate, TN).astype(BF)]
+    summed_vg = scatter_dp(jnp.concatenate(grads_vg, axis=1))
+    grads_rk, out_rows, sums_early = [], [], []
+
+    def beside(relayed):
+        grads_rk.extend(
+            dot(after(m, relayed), d, TN).astype(BF) for m, d in ((mix_r, d_recept), (mix_k, d_keyed))
+        )
+        out_rows.append(spread_columns([after_mix], after(channel, relayed), here, False, False, CHUNK, per))
+        sums_early.append(after(summed_cv, relayed).astype(F32))
+        sums_early.extend(owners_rows(summed_ck, [ffn_key.shape[1]], relayed))
+        return grads_rk, out_rows, sums_early
+
+    d_recept, d_keyed = after((d_recept, d_keyed), grads_vg, summed_o, channel)
+    terms, sums_one = mixes_back_scatter(
         [(i, d, 0, full_in, i, part) for i, d in enumerate((d_recept, d_keyed, d_valued))]
         + [(3, d_gate, 0, full_g, 0, part)],
-        step, marks, rows_of(turned, 2, 3, 4, 5), here, seq,
-    )
-    sum_cv = after(summed_cv, d_normed).astype(F32)
-    terms = scatter_seq(blocks_of(d_normed, seq), sum_cv)
+        step, marks, rows_of(turned, 2, 3, 4, 5), here, seq, beside, summed_ck,
+    )
+    summed_rk = scatter_dp(jnp.concatenate(grads_rk, axis=1))
+    (out_rows,), (sum_cv, sum_ck) = out_rows, sums_early
     if within is None:
         terms = [outside(t, groups, unit, back=True) for t in terms]
     tokens_grad, _, norm_sums = norm_back(terms, inputs_b, d_after, rows_of(vec, 0), within, here)
 
     (sum_cr,) = owners_rows(summed_cr, [width])
     sum_o = summed_o.astype(F32)
-    sum_r, sum_k, sum_v, sum_g = owners_rows(summed_in, [width] * 4)
+    sum_v, sum_g = owners_rows(summed_vg, [width] * 2)
+    sum_r, sum_k = owners_rows(summed_rk, [width] * 2)
 
     def by_device(rows, turn):
         if turn:

time: 882 us -> 913 us (1.035)
  waiting for transfers between devices: 313 us -> 328 us
  Pallas kernels: 217 us -> 228 us
    reduce_scatter x5 -> x6, waiting for transfers between devices: 0.09 us -> 38 us  [scatter_dp(): return lax.psum_scatter(grad, 'dp', scatter_dimension=0, tiled=True)]
    ppermute x67, waiting for transfers between devices: 311 us -> 288 us  [swap(): return lax.ppermute(value, axis, [(i, i ^ distance) for i in range(size)])]
    pallas_call x26 -> x30, Pallas kernels: 217 us -> 228 us  [kernel(): pl.pallas_call(body, out_shape=[jax.ShapeDtypeStruct(shape, kind) for sha...]
    unnamed x197 -> x215, local copies, waits for them, and re-layouts: 40.1 us -> 46.2 us
  transfers between devices with their start and end apart: 77 -> 78, of which waited for: 38 -> 40; matrix products, arithmetic and copies ran while one was open for 23% -> 21% of each run, Pallas kernels for 25% -> 24%
where the time goes in v6:
time: 913 us; the launch traced here: 907 us
  waiting for transfers between devices  328 us (36%)
  Pallas kernels  228 us (25%)
  matrix products  156 us (17%)
  local copies, waits for them, and re-layouts  76.8 us (8%)
  starting transfers between devices  75.2 us (8%)
  other arithmetic  27.8 us (3%)
  between operations  15.5 us (2%)
    ppermute x67, waiting for transfers between devices, swap(): return lax.ppermute(value, axis, [(i, i ^ distance) for i in range(size)])  288 us
    pallas_call x30, Pallas kernels, kernel(): pl.pallas_call(body, out_shape=[jax.ShapeDtypeStruct(shape, kind) for sha...  228 us
    dot_general x19, matrix products, dot(): return lax.dot_general(left, right, dims, preferred_element_type=F32)  156 us
    ppermute x67, starting transfers between devices, swap(): return lax.ppermute(value, axis, [(i, i ^ distance) for i in range(size)])  74.3 us
    unnamed x215, local copies, waits for them, and re-layouts  46.2 us
    reduce_scatter x6, waiting for transfers between devices, scatter_dp(): return lax.psum_scatter(grad, 'dp', scatter_dimension=0, tiled=True)  38 us
  transfers between devices with their start and end apart: 78, of which 40 were waited for; matrix products, arithmetic and copies ran while one was open for 21% of the time, Pallas kernels for 24%

profile of v6, /device:TPU:0, one launch (start us, length us, event | category | flops | bytes accessed | tf_op | source)
XLA Modules:
  0.0 907.0 jit_solution(13609000099831287082)
XLA Ops:
  11.2 3.0 collective-permute-start.9
  15.8 5.6 collective-permute-done.9.refs_1_
  21.4 6.2 collective-permute-done.10.refs_2_
  41.3 5.8 collective-permute-done.3
  47.7 8.8 collective-permute-done.4
  60.3 14.3 %collective-permute-done.6.refs_2_ = bf16[384,2048]{1,0:T(8,128)(2,1)} collective-permute-done((bf16[384,2048]{1,0:T(8,128)(2,1)}, bf16[384,2048]{1,0:T(8,128)(2,1)}, u32[]{:S(2)}, u32[]{:S(2)}) %collective-permute-start.6) | collective-permute-done | bytes 1572896 | tf_op jit(solution)/shard_map/ppermute | solution.py:25
  80.8 17.0 %collective-permute-done.8.refs_4_ = bf16[192,2048]{1,0:T(8,128)(2,1)S(1)} collective-permute-done((bf16[192,2048]{1,0:T(8,128)(2,1)S(1)}, bf16[192,2048]{1,0:T(8,128)(2,1)S(1)}, u32[]{:S(2)}, u32[]{:S(2)}) %collective-permute-start.8) | collective-permute-done | bytes 786464 | tf_op jit(solution)/shard_map/ppermute | solution.py:25
  103.0 17.9 %mixes.2 = (bf16[1536,2048]{1,0:T(8,128)(2,1)}, bf16[1536,2048]{1,0:T(8,128)(2,1)}, bf16[1536,2048]{1,0:T(8,128)(2,1)}, bf16[1536,2048]{1,0:T(8,128)(2,1)}, bf16[1536,2048]{1,0:T(8,128)(2,1)}) custom-call(s32[1]{0:T(128)} %bitcast.here, bf16[384,2048]{1,0:T(8,128)(2,1)} %hold.1.refs_0_, bf16[384,2048]{1,0:T(8,128)(2,1)} %collective-permute-done.5.refs_1_, ...), custom_call_target="tpu_custom_call" | custom-call | tf_op jit(solution)/shard_map/mixes/pallas_call | solution.py:120
  126.2 8.1 convolution_convert_fusion.11.r_ref
  134.4 7.7 convolution_convert_fusion.10.k_ref
  142.1 4.5 convolution_convert_fusion.9.v_ref
  150.8 31.2 %collective-permute-done.13.refs_2_ = bf16[384,2048]{1,0:T(8,128)(2,1)S(1)} collective-permute-done((bf16[384,2048]{1,0:T(8,128)(2,1)}, bf16[384,2048]{1,0:T(8,128)(2,1)S(1)}, u32[]{:S(2)}, u32[]{:S(2)}) %collective-permute-start.13) | collective-permute-done | bytes 1572896 | tf_op jit(solution)/shard_map/ppermute | solution.py:25
  192.1 13.4 %wkv_forward.1 = (f32[1536,512]{1,0:T(8,128)}, bf16[12,512,128]{2,1,0:T(8,128)(2,1)S(1)}) custom-call(s32[1]{0:T(128)} %bitcast.here, bf16[1536,512]{1,0:T(8,128)(2,1)S(1)} %copy-done.13, bf16[1536,512]{1,0:T(8,128)(2,1)} %convolution_convert_fusion.10.k_ref, bf16[1536,512]{1,0:T(8,128)(2,1)} %convolution_convert_fusion.9.v_ref, ...), custom_call_target="tpu_custom_call" | custom-call | tf_op jit(solution)/shard_map/wkv_forward/pallas_call | solution.py:120
  208.3 10.0 %gate.1 = (f32[1536,512]{1,0:T(8,128)}, bf16[1536,512]{1,0:T(8,128)(2,1)S(1)}) custom-call(s32[1]{0:T(128)} %bitcast.here, bf16[1536,2048]{1,0:T(8,128)(2,1)} %get-tuple-element.168.refs_0_, bf16[2048,512]{1,0:T(8,128)(2,1)S(1)} %copy-done.5, f32[1536,512]{1,0:T(8,128)} %get-tuple-element.183.refs_2_.wkv_ref, f32[8,512]{1,0:T(8,128)S(1)} %maximum_maximum_fusion.par_ref.refs_3_), custom_call_target="tpu_custom_call" | custom-call | tf_op jit(solution)/shard_map/gate/pallas_call | solution.py:120
  219.6 2.8 convolution_convert_fusion.13
  226.9 11.1 %collective-permute-done.16 = bf16[192,2048]{1,0:T(8,128)(2,1)S(1)} collective-permute-done((bf16[192,2048]{1,0:T(8,128)(2,1)S(1)}, bf16[192,2048]{1,0:T(8,128)(2,1)S(1)}, u32[]{:S(2)}, u32[]{:S(2)}) %collective-permute-start.16) | collective-permute-done | bytes 786464 | tf_op jit(solution)/shard_map/ppermute | solution.py:25
  245.1 2.7 convolution_convert_fusion.15.refs_0_
  247.8 24.8 %collective-permute-done.17.refs_1_ = bf16[384,2048]{1,0:T(8,128)(2,1)} collective-permute-done((bf16[384,2048]{1,0:T(8,128)(2,1)}, bf16[384,2048]{1,0:T(8,128)(2,1)}, u32[]{:S(2)}, u32[]{:S(2)}) %collective-permute-start.17) | collective-permute-done | bytes 1572896 | tf_op jit(solution)/shard_map/ppermute | solution.py:25
  274.1 4.7 after_norm.1
  281.6 28.3 %collective-permute-done.21.refs_2_ = bf16[384,2048]{1,0:T(8,128)(2,1)S(1)} collective-permute-done((bf16[384,2048]{1,0:T(8,128)(2,1)S(1)}, bf16[384,2048]{1,0:T(8,128)(2,1)S(1)}, u32[]{:S(2)}, u32[]{:S(2)}) %collective-permute-start.21) | collective-permute-done | bytes 1572896 | tf_op jit(solution)/shard_map/ppermute | solution.py:25
  318.9 8.0 collective-permute-done.23.refs_4_
  328.4 12.5 %mixes.3 = (bf16[1536,2048]{1,0:T(8,128)(2,1)}, bf16[1536,2048]{1,0:T(8,128)(2,1)}, bf16[1536,2048]{1,0:T(8,128)(2,1)}) custom-call(s32[1]{0:T(128)} %bitcast.here, bf16[384,2048]{1,0:T(8,128)(2,1)S(1)} %copy-done.21, bf16[384,2048]{1,0:T(8,128)(2,1)S(1)} %collective-permute-done.20.refs_1_, bf16[384,2048]{1,0:T(8,128)(2,1)} %copy-done.62, ...), custom_call_target="tpu_custom_call" | custom-call | tf_op jit(solution)/shard_map/mixes/pallas_call | solution.py:120
  340.9 9.5 %divide_convert_fusion = (bf16[1536,512]{1,0:T(8,128)(2,1)}, f32[1536,512]{1,0:T(8,128)}) fusion(bf16[1536,2048]{1,0:T(8,128)(2,1)} %get-tuple-element.236, bf16[2048,2304]{1,0:T(8,128)(2,1)} %all-gather.12.cloned.1.call-done.refs_6_.refs_7_.refs_8_), kind=kOutput, calls=%fused_computation.10 | convolution fusion | flops 3224371200 | bytes 13107200 | tf_op jit(solution)/shard_map/dot_general | solution.py:549
  353.3 22.6 %multiply_convert_fusion.1 = (bf16[1536,1792]{1,0:T(8,128)(2,1)}, bf16[1536,1792]{1,0:T(8,128)(2,1)}) fusion(bf16[1536,2048]{1,0:T(8,128)(2,1)} %get-tuple-element.235, bf16[2048,2304]{1,0:T(8,128)(2,1)S(1)} %copy-done.59), kind=kOutput, calls=%fused_computation.2 | convolution fusion | flops 11312824320 | bytes 24641536 | tf_op jit(solution)/shard_map/dot_general | solution.py:549
  375.9 6.0 value_columns.6
  383.3 6.2 value_columns.7
  389.6 7.5 collective-permute-done.31
  404.0 6.0 value_columns.5
  410.1 6.0 value_columns.4.refs_5_
  420.2 9.6 %spread_columns.2 = bf16[1536,2048]{1,0:T(8,128)(2,1)} custom-call(s32[1]{0:T(128)} %bitcast.here, bf16[384,2048]{1,0:T(8,128)(2,1)S(1)} %bitcast.93, bf16[384,2048]{1,0:T(8,128)(2,1)S(1)} %copy-done.12, bf16[384,2048]{1,0:T(8,128)(2,1)} %copy-done.61, bf16[192,2048]{1,0:T(8,128)(2,1)} %collective-permute-done.14.refs_3_, ...), custom_call_target="tpu_custom_call" | custom-call | tf_op jit(solution)/shard_map/spread_columns/pallas_call | solution.py:120
  429.8 15.9 %convolution_convert_fusion.1 = bf16[1792,2048]{1,0:T(8,128)(2,1)} fusion(bf16[1536,1792]{1,0:T(8,128)(2,1)S(1)} %bitcast.98, bf16[1536,2048]{1,0:T(8,128)(2,1)} %spread_columns.2), kind=kOutput, calls=%fused_computation.5 | convolution fusion | flops 11277959168 | bytes 19136512 | tf_op jit(solution)/shard_map/dot_general | solution.py:549
  448.3 19.0 %multiply_convert_fusion.refs_0_.refs_3_ = bf16[1536,1792]{1,0:T(8,128)(2,1)} fusion(bf16[1536,1792]{1,0:T(8,128)(2,1)} %get-tuple-element.218, bf16[1536,2048]{1,0:T(8,128)(2,1)} %spread_columns.2, bf16[1792,2048]{1,0:T(8,128)(2,1)} %all-gather.14.cloned.1.call-done.right_ref), kind=kOutput, calls=%fused_computation.1 | convolution fusion | flops 11282546688 | bytes 24641536 | tf_op jit(solution)/shard_map/dot_general | solution.py:549
  467.3 10.6 %collective-permute-done.32.refs_7_ = bf16[1536,512]{1,0:T(8,128)(2,1)S(1)} collective-permute-done((bf16[1536,512]{1,0:T(8,128)(2,1)S(1)}, bf16[1536,512]{1,0:T(8,128)(2,1)S(1)}, u32[]{:S(2)}, u32[]{:S(2)}) %collective-permute-start.32) | collective-permute-done | bytes 1572896 | tf_op jit(solution)/shard_map/ppermute | solution.py:25
  479.9 7.0 channel.1
  488.2 9.0 mixes_back.6
  498.2 16.0 %mixes_back.7 = (bf16[768,2048]{1,0:T(8,128)(2,1)S(1)}, f32[8,2048]{1,0:T(8,128)S(1)}) custom-call(s32[1]{0:T(128)} %bitcast.here, bf16[1536,1792]{1,0:T(8,128)(2,1)} %multiply_convert_fusion.refs_0_.refs_3_, bf16[1536,512]{1,0:T(8,128)(2,1)S(1)} %get-tuple-element.233.refs_1_.refs_2_.refs_4_.refs_5_, ...), custom_call_target="tpu_custom_call" | custom-call | tf_op jit(solution)/shard_map/mixes_back/pallas_call | solution.py:120
  521.0 16.1 %convolution_convert_fusion = bf16[2048,1792]{1,0:T(8,128)(2,1)} fusion(bf16[1536,2048]{1,0:T(8,128)(2,1)} %get-tuple-element.235, bf16[1536,1792]{1,0:T(8,128)(2,1)S(1)} %bitcast.96), kind=kOutput, calls=%fused_computation.4 | convolution fusion | flops 11277959168 | bytes 19136512 | tf_op jit(solution)/shard_map/dot_general | solution.py:549
  537.1 8.3 mixes_back.8
  547.2 7.6 convolution_convert_fusion.8
  557.7 6.6 norm_back.2
  565.8 30.8 %collective-permute-done.40 = bf16[384,2048]{1,0:T(8,128)(2,1)S(1)} collective-permute-done((bf16[384,2048]{1,0:T(8,128)(2,1)S(1)}, bf16[384,2048]{1,0:T(8,128)(2,1)S(1)}, u32[]{:S(2)}, u32[]{:S(2)}) %collective-permute-start.40) | collective-permute-done | bytes 1572896 | tf_op jit(solution)/shard_map/ppermute | solution.py:25
  600.9 10.4 %collective-permute-done.42 = bf16[192,2048]{1,0:T(8,128)(2,1)} collective-permute-done((bf16[192,2048]{1,0:T(8,128)(2,1)S(1)}, bf16[192,2048]{1,0:T(8,128)(2,1)}, u32[]{:S(2)}, u32[]{:S(2)}) %collective-permute-start.42) | collective-permute-done | bytes 786464 | tf_op jit(solution)/shard_map/ppermute | solution.py:25
  617.0 2.7 copy-done.72
  619.7 4.8 convolution_convert_fusion.6
  626.1 8.1 convolution_convert_fusion.7.d_mixed_ref
  634.2 37.1 %wkv_backward.1 = (bf16[1536,512]{1,0:T(8,128)(2,1)S(1)}, bf16[1536,512]{1,0:T(8,128)(2,1)S(1)}, bf16[1536,512]{1,0:T(8,128)(2,1)}, bf16[1536,512]{1,0:T(8,128)(2,1)}, f32[8,512]{1,0:T(8,128)S(1)}) custom-call(s32[1]{0:T(128)} %bitcast.here, bf16[1536,512]{1,0:T(8,128)(2,1)} %convolution_convert_fusion.11.r_ref, ...), custom_call_target="tpu_custom_call" | custom-call | tf_op jit(solution)/shard_map/wkv_backward/pallas_call | solution.py:120
  671.4 7.3 convolution_convert_fusion.4
  678.7 6.7 convolution_convert_fusion.5
  693.3 5.2 collective-permute-done.45.refs_4_
  699.2 3.4 collective-permute-done.44.refs_3_
  704.1 38.0 %reduce-scatter.11.cloned.1.call-done = bf16[256,1792]{1,0:T(8,128)(2,1)} async-done(((bf16[2048,1792]{1,0:T(8,128)(2,1)}), bf16[256,1792]{1,0:T(8,128)(2,1)}) %reduce-scatter.11.cloned.1.call-update) | async-done | bytes 917520 | tf_op jit(solution)/shard_map/reduce_scatter | solution.py:773
  743.5 8.7 mixes_back.9
  755.0 15.2 %mixes_back.10 = (bf16[768,2048]{1,0:T(8,128)(2,1)}, f32[8,2048]{1,0:T(8,128)S(1)}) custom-call(s32[1]{0:T(128)} %bitcast.here, bf16[1536,512]{1,0:T(8,128)(2,1)S(1)} %get-tuple-element.280.refs_0_.refs_4_, bf16[1536,512]{1,0:T(8,128)(2,1)S(1)} %copy-done.1, bf16[1536,512]{1,0:T(8,128)(2,1)S(1)} %copy-done.4, ...), custom_call_target="tpu_custom_call" | custom-call | tf_op jit(solution)/shard_map/mixes_back/pallas_call | solution.py:120
  776.0 6.9 convolution_convert_fusion.2
  782.9 3.7 convolution_convert_fusion.3
  786.6 2.6 pad_maximum_fusion
  800.4 30.0 %collective-permute-done.52.refs_3_ = bf16[64,1792]{1,0:T(8,128)(2,1)S(1)} collective-permute-done((bf16[64,1792]{1,0:T(8,128)(2,1)}, bf16[64,1792]{1,0:T(8,128)(2,1)S(1)}, u32[]{:S(2)}, u32[]{:S(2)}) %collective-permute-start.52) | collective-permute-done | bytes 229408 | tf_op jit(solution)/shard_map/ppermute | solution.py:25
  830.4 2.8 collective-permute-done.51.refs_2_
  834.6 8.5 mixes_back.11
  844.4 2.7 convert_element_type.278
  853.5 7.3 norm_back.3
  862.0 4.1 collective-permute-done.62
  867.6 2.8 collective-permute-done.63
  870.5 4.3 collective-permute-start.64
  (501 shorter events, 199.1 us)
Async XLA Ops:
  7.2 119.0 %all-gather.8.cloned.1.call-start = ((), (), s32[]{:S(2)}) async-start(), calls=%async_computation.7 | async-start | bytes 7077888 | tf_op jit(solution)/shard_map/all_gather | solution.py:770
  11.2 10.1 %collective-permute-start.9 = (bf16[64,2048]{1,0:T(8,128)(2,1)S(1)}, bf16[64,2048]{1,0:T(8,128)(2,1)S(1)}, u32[]{:S(2)}, u32[]{:S(2)}) collective-permute-start(bf16[64,2048]{1,0:T(8,128)(2,1)S(1)} %get-tuple-element.170), channel_id=1, source_target_pairs={{0,8},{8,0},{16,24},{24,16},{1,9},{9,1},{17,25},{25,17},{2,10},{10... | collective-permute-start | bytes 786440 | tf_op jit(solution)/shard_map/ppermute | solution.py:25
  14.2 13.4 %collective-permute-start.10 = (bf16[64,2048]{1,0:T(8,128)(2,1)S(1)}, bf16[64,2048]{1,0:T(8,128)(2,1)S(1)}, u32[]{:S(2)}, u32[]{:S(2)}) collective-permute-start(bf16[64,2048]{1,0:T(8,128)(2,1)S(1)} %get-tuple-element.171), channel_id=1, source_target_pairs={{0,16},{8,24},{16,0},{24,8},{1,17},{9,25},{17,1},{25,9},{2,18},{10... | collective-permute-start | bytes 786440 | tf_op jit(solution)/shard_map/ppermute | solution.py:25
  15.8 11.9 %collective-permute-start.11 = (bf16[64,2048]{1,0:T(8,128)(2,1)S(1)}, bf16[64,2048]{1,0:T(8,128)(2,1)S(1)}, u32[]{:S(2)}, u32[]{:S(2)}) collective-permute-start(bf16[64,2048]{1,0:T(8,128)(2,1)S(1)} %get-tuple-element.172), channel_id=1, source_target_pairs={{0,24},{8,16},{16,8},{24,0},{1,25},{9,17},{17,9},{25,1},{2,26},{10... | collective-permute-start | bytes 786440 | tf_op jit(solution)/shard_map/ppermute | solution.py:25
  28.7 178.0 %all-gather.6.cloned.1.call-start = ((), (), s32[]{:S(2)}) async-start(), calls=%async_computation.6 | async-start | bytes 2359296 | tf_op jit(solution)/shard_map/all_gather | solution.py:770
  37.5 37.1 %collective-permute-start.6 = (bf16[384,2048]{1,0:T(8,128)(2,1)}, bf16[384,2048]{1,0:T(8,128)(2,1)}, u32[]{:S(2)}, u32[]{:S(2)}) collective-permute-start(bf16[384,2048]{1,0:T(8,128)(2,1)} %hold.1.refs_0_), channel_id=1, source_target_pairs={{0,16},{8,24},{16,0},{24,8},{1,17},{9,25},{17,1},{25,9},{2,18},{10... | collective-permute-start | bytes 4718600 | tf_op jit(solution)/shard_map/ppermute | solution.py:25
  39.1 36.8 %collective-permute-start.5 = (bf16[384,2048]{1,0:T(8,128)(2,1)}, bf16[384,2048]{1,0:T(8,128)(2,1)}, u32[]{:S(2)}, u32[]{:S(2)}) collective-permute-start(bf16[384,2048]{1,0:T(8,128)(2,1)} %hold.1.refs_0_), channel_id=1, source_target_pairs={{0,8},{8,0},{16,24},{24,16},{1,9},{9,1},{17,25},{25,17},{2,10},{10... | collective-permute-start | bytes 4718600 | tf_op jit(solution)/shard_map/ppermute | solution.py:25
  47.1 9.3 %collective-permute-start.4 = (bf16[4,4,14,64]{3,2,1,0:T(8,128)(2,1)S(1)}, bf16[4,4,14,64]{3,2,1,0:T(8,128)(2,1)S(1)}, u32[]{:S(2)}, u32[]{:S(2)}) collective-permute-start(bf16[4,4,14,64]{3,2,1,0:T(8,128)(2,1)S(1)} %pad_maximum_fusion.12), channel_id=1, source_target_pairs={{0,4},{1,5},{2,6},{3,7},{4,0},{5,1},{6,2},{7,3},{8,12},{9,13},{10,... | collective-permute-start | bytes 86024 | tf_op jit(solution)/shard_map/ppermute | solution.py:25
  76.5 143.0 %all-gather.10.cloned.1.call-start = ((), (), s32[]{:S(2)}) async-start(), calls=%async_computation.8 | async-start | bytes 2359296 | tf_op jit(solution)/shard_map/all_gather | solution.py:770
  79.0 18.9 %collective-permute-start.8 = (bf16[192,2048]{1,0:T(8,128)(2,1)S(1)}, bf16[192,2048]{1,0:T(8,128)(2,1)S(1)}, u32[]{:S(2)}, u32[]{:S(2)}) collective-permute-start(bf16[192,2048]{1,0:T(8,128)(2,1)S(1)} %slice.331), channel_id=1, source_target_pairs={{0,8},{8,0},{16,24},{24,16},{1,9},{9,1},{17,25},{25,17},{2,10},{10... | collective-permute-start | bytes 2359304 | tf_op jit(solution)/shard_map/ppermute | solution.py:25
  79.6 19.1 %collective-permute-start.7 = (bf16[192,2048]{1,0:T(8,128)(2,1)S(1)}, bf16[192,2048]{1,0:T(8,128)(2,1)S(1)}, u32[]{:S(2)}, u32[]{:S(2)}) collective-permute-start(bf16[192,2048]{1,0:T(8,128)(2,1)S(1)} %slice.330), channel_id=1, source_target_pairs={{0,16},{8,24},{16,0},{24,8},{1,17},{9,25},{17,1},{25,9},{2,18},{10... | collective-permute-start | bytes 2359304 | tf_op jit(solution)/shard_map/ppermute | solution.py:25
  99.7 241.3 %all-gather.12.cloned.1.call-start = ((), (), s32[]{:S(2)}) async-start(), calls=%async_computation.9 | async-start | bytes 10616832 | tf_op jit(solution)/shard_map/all_gather | solution.py:770
  122.7 23.9 %collective-permute-start.24 = (bf16[64,2304]{1,0:T(8,128)(2,1)}, bf16[64,2304]{1,0:T(8,128)(2,1)S(1)}, u32[]{:S(2)}, u32[]{:S(2)}) collective-permute-start(bf16[64,2304]{1,0:T(8,128)(2,1)} %get-tuple-element.198), channel_id=1, source_target_pairs={{0,8},{8,0},{16,24},{24,16},{1,9},{9,1},{17,25},{25,17},{2,10},{10... | collective-permute-start | bytes 884744 | tf_op jit(solution)/shard_map/ppermute | solution.py:25
  124.8 21.8 %collective-permute-start.25 = (bf16[64,2304]{1,0:T(8,128)(2,1)}, bf16[64,2304]{1,0:T(8,128)(2,1)S(1)}, u32[]{:S(2)}, u32[]{:S(2)}) collective-permute-start(bf16[64,2304]{1,0:T(8,128)(2,1)} %get-tuple-element.199), channel_id=1, source_target_pairs={{0,16},{8,24},{16,0},{24,8},{1,17},{9,25},{17,1},{25,9},{2,18},{10... | collective-permute-start | bytes 884744 | tf_op jit(solution)/shard_map/ppermute | solution.py:25
  125.6 21.0 %collective-permute-start.26 = (bf16[64,2304]{1,0:T(8,128)(2,1)}, bf16[64,2304]{1,0:T(8,128)(2,1)S(1)}, u32[]{:S(2)}, u32[]{:S(2)}) collective-permute-start(bf16[64,2304]{1,0:T(8,128)(2,1)} %get-tuple-element.200), channel_id=1, source_target_pairs={{0,24},{8,16},{16,8},{24,0},{1,25},{9,17},{17,9},{25,1},{2,26},{10... | collective-permute-start | bytes 884744 | tf_op jit(solution)/shard_map/ppermute | solution.py:25
  147.8 228.1 %all-gather.14.cloned.1.call-start = ((), (), s32[]{:S(2)}) async-start(), calls=%async_computation.10 | async-start | bytes 8257536 | tf_op jit(solution)/shard_map/all_gather | solution.py:770
  147.8 34.2 %collective-permute-start.13 = (bf16[384,2048]{1,0:T(8,128)(2,1)}, bf16[384,2048]{1,0:T(8,128)(2,1)S(1)}, u32[]{:S(2)}, u32[]{:S(2)}) collective-permute-start(bf16[384,2048]{1,0:T(8,128)(2,1)} %bitcast.90), channel_id=1, source_target_pairs={{0,16},{8,24},{16,0},{24,8},{1,17},{9,25},{17,1},{25,9},{2,18},{10... | collective-permute-start | bytes 4718600 | tf_op jit(solution)/shard_map/ppermute | solution.py:25
  149.7 33.8 %collective-permute-start.12 = (bf16[384,2048]{1,0:T(8,128)(2,1)}, bf16[384,2048]{1,0:T(8,128)(2,1)S(1)}, u32[]{:S(2)}, u32[]{:S(2)}) collective-permute-start(bf16[384,2048]{1,0:T(8,128)(2,1)} %bitcast.91), channel_id=1, source_target_pairs={{0,8},{8,0},{16,24},{24,16},{1,9},{9,1},{17,25},{25,17},{2,10},{10... | collective-permute-start | bytes 4718600 | tf_op jit(solution)/shard_map/ppermute | solution.py:25
  186.6 31.8 %collective-permute-start.15 = (bf16[192,2048]{1,0:T(8,128)(2,1)}, bf16[192,2048]{1,0:T(8,128)(2,1)S(1)}, u32[]{:S(2)}, u32[]{:S(2)}) collective-permute-start(bf16[192,2048]{1,0:T(8,128)(2,1)} %slice.336), channel_id=1, source_target_pairs={{0,8},{8,0},{16,24},{24,16},{1,9},{9,1},{17,25},{25,17},{2,10},{10... | collective-permute-start | bytes 2359304 | tf_op jit(solution)/shard_map/ppermute | solution.py:25
  187.6 32.0 %collective-permute-start.14 = (bf16[192,2048]{1,0:T(8,128)(2,1)}, bf16[192,2048]{1,0:T(8,128)(2,1)}, u32[]{:S(2)}, u32[]{:S(2)}) collective-permute-start(bf16[192,2048]{1,0:T(8,128)(2,1)} %slice.335), channel_id=1, source_target_pairs={{0,16},{8,24},{16,0},{24,8},{1,17},{9,25},{17,1},{25,9},{2,18},{10... | collective-permute-start | bytes 2359304 | tf_op jit(solution)/shard_map/ppermute | solution.py:25
  188.6 423.9 %reduce-scatter.7.cloned.1.call-start = ((), (), s32[]{:S(2)}) async-start(), calls=%async_computation.11 | async-start | bytes 8257536 | tf_op jit(solution)/shard_map/reduce_scatter | solution.py:773
  222.5 15.5 %collective-permute-start.16 = (bf16[192,2048]{1,0:T(8,128)(2,1)S(1)}, bf16[192,2048]{1,0:T(8,128)(2,1)S(1)}, u32[]{:S(2)}, u32[]{:S(2)}) collective-permute-start(bf16[192,2048]{1,0:T(8,128)(2,1)S(1)} %get-tuple-element.354), channel_id=1, source_target_pairs={{0,16},{8,24},{16,0},{24,8},{1,17},{9,25},{17,1},{25,9},{2,18},{10... | collective-permute-start | bytes 2359304 | tf_op jit(solution)/shard_map/ppermute | solution.py:25
  223.6 17.1 %collective-permute-start.18 = (bf16[192,2048]{1,0:T(8,128)(2,1)S(1)}, bf16[192,2048]{1,0:T(8,128)(2,1)S(1)}, u32[]{:S(2)}, u32[]{:S(2)}) collective-permute-start(bf16[192,2048]{1,0:T(8,128)(2,1)S(1)} %get-tuple-element.353), channel_id=1, source_target_pairs={{0,8},{8,0},{16,24},{24,16},{1,9},{9,1},{17,25},{25,17},{2,10},{10... | collective-permute-start | bytes 2359304 | tf_op jit(solution)/shard_map/ppermute | solution.py:25
  239.6 33.0 %collective-permute-start.17 = (bf16[384,2048]{1,0:T(8,128)(2,1)}, bf16[384,2048]{1,0:T(8,128)(2,1)}, u32[]{:S(2)}, u32[]{:S(2)}) collective-permute-start(bf16[384,2048]{1,0:T(8,128)(2,1)} %pad_maximum_fusion.2), channel_id=1, source_target_pairs={{0,8},{8,0},{16,24},{24,16},{1,9},{9,1},{17,25},{25,17},{2,10},{10... | collective-permute-start | bytes 4718600 | tf_op jit(solution)/shard_map/ppermute | solution.py:25
  242.3 31.8 %collective-permute-start.19 = (bf16[384,2048]{1,0:T(8,128)(2,1)}, bf16[384,2048]{1,0:T(8,128)(2,1)}, u32[]{:S(2)}, u32[]{:S(2)}) collective-permute-start(bf16[384,2048]{1,0:T(8,128)(2,1)} %pad_maximum_fusion.3), channel_id=1, source_target_pairs={{0,16},{8,24},{16,0},{24,8},{1,17},{9,25},{17,1},{25,9},{2,18},{10... | collective-permute-start | bytes 4718600 | tf_op jit(solution)/shard_map/ppermute | solution.py:25
  278.8 31.1 %collective-permute-start.21 = (bf16[384,2048]{1,0:T(8,128)(2,1)S(1)}, bf16[384,2048]{1,0:T(8,128)(2,1)S(1)}, u32[]{:S(2)}, u32[]{:S(2)}) collective-permute-start(bf16[384,2048]{1,0:T(8,128)(2,1)S(1)} %get-tuple-element.191.refs_0_), channel_id=1, source_target_pairs={{0,16},{8,24},{16,0},{24,8},{1,17},{9,25},{17,1},{25,9},{2,18},{10... | collective-permute-start | bytes 4718600 | tf_op jit(solution)/shard_map/ppermute | solution.py:25
  279.5 32.0 %collective-permute-start.20 = (bf16[384,2048]{1,0:T(8,128)(2,1)S(1)}, bf16[384,2048]{1,0:T(8,128)(2,1)S(1)}, u32[]{:S(2)}, u32[]{:S(2)}) collective-permute-start(bf16[384,2048]{1,0:T(8,128)(2,1)S(1)} %get-tuple-element.191.refs_0_), channel_id=1, source_target_pairs={{0,8},{8,0},{16,24},{24,16},{1,9},{9,1},{17,25},{25,17},{2,10},{10... | collective-permute-start | bytes 4718600 | tf_op jit(solution)/shard_map/ppermute | solution.py:25
  313.4 13.4 %collective-permute-start.23 = (bf16[192,2048]{1,0:T(8,128)(2,1)}, bf16[192,2048]{1,0:T(8,128)(2,1)}, u32[]{:S(2)}, u32[]{:S(2)}) collective-permute-start(bf16[192,2048]{1,0:T(8,128)(2,1)} %slice.348), channel_id=1, source_target_pairs={{0,8},{8,0},{16,24},{24,16},{1,9},{9,1},{17,25},{25,17},{2,10},{10... | collective-permute-start | bytes 2359304 | tf_op jit(solution)/shard_map/ppermute | solution.py:25
  314.6 12.3 %collective-permute-start.22 = (bf16[192,2048]{1,0:T(8,128)(2,1)}, bf16[192,2048]{1,0:T(8,128)(2,1)}, u32[]{:S(2)}, u32[]{:S(2)}) collective-permute-start(bf16[192,2048]{1,0:T(8,128)(2,1)} %slice.347), channel_id=1, source_target_pairs={{0,16},{8,24},{16,0},{24,8},{1,17},{9,25},{17,1},{25,9},{2,18},{10... | collective-permute-start | bytes 2359304 | tf_op jit(solution)/shard_map/ppermute | solution.py:25
  350.5 46.9 %collective-permute-start.28 = (bf16[1536,512]{1,0:T(8,128)(2,1)}, bf16[1536,512]{1,0:T(8,128)(2,1)}, u32[]{:S(2)}, u32[]{:S(2)}) collective-permute-start(bf16[1536,512]{1,0:T(8,128)(2,1)} %get-tuple-element.212.refs_5_), channel_id=1, source_target_pairs={{0,16},{8,24},{16,0},{24,8},{1,17},{9,25},{17,1},{25,9},{2,18},{10... | collective-permute-start | bytes 4718600 | tf_op jit(solution)/shard_map/ppermute | solution.py:25
  351.7 45.7 %collective-permute-start.27 = (bf16[1536,512]{1,0:T(8,128)(2,1)}, bf16[1536,512]{1,0:T(8,128)(2,1)}, u32[]{:S(2)}, u32[]{:S(2)}) collective-permute-start(bf16[1536,512]{1,0:T(8,128)(2,1)} %get-tuple-element.212.refs_5_), channel_id=1, source_target_pairs={{0,8},{8,0},{16,24},{24,16},{1,9},{9,1},{17,25},{25,17},{2,10},{10... | collective-permute-start | bytes 4718600 | tf_op jit(solution)/shard_map/ppermute | solution.py:25
  382.0 15.1 %collective-permute-start.31 = (bf16[768,512]{1,0:T(8,128)(2,1)S(1)}, bf16[768,512]{1,0:T(8,128)(2,1)S(1)}, u32[]{:S(2)}, u32[]{:S(2)}) collective-permute-start(bf16[768,512]{1,0:T(8,128)(2,1)S(1)} %get-tuple-element.351), channel_id=1, source_target_pairs={{0,8},{8,0},{16,24},{24,16},{1,9},{9,1},{17,25},{25,17},{2,10},{10... | collective-permute-start | bytes 2359304 | tf_op jit(solution)/shard_map/ppermute | solution.py:25
  382.5 34.8 %collective-permute-start.29 = (bf16[768,512]{1,0:T(8,128)(2,1)S(1)}, bf16[768,512]{1,0:T(8,128)(2,1)S(1)}, u32[]{:S(2)}, u32[]{:S(2)}) collective-permute-start(bf16[768,512]{1,0:T(8,128)(2,1)S(1)} %get-tuple-element.352), channel_id=1, source_target_pairs={{0,16},{8,24},{16,0},{24,8},{1,17},{9,25},{17,1},{25,9},{2,18},{10... | collective-permute-start | bytes 2359304 | tf_op jit(solution)/shard_map/ppermute | solution.py:25
  399.8 19.0 %collective-permute-start.34 = (bf16[768,512]{1,0:T(8,128)(2,1)S(1)}, bf16[768,512]{1,0:T(8,128)(2,1)S(1)}, u32[]{:S(2)}, u32[]{:S(2)}) collective-permute-start(bf16[768,512]{1,0:T(8,128)(2,1)S(1)} %slice.366), channel_id=1, source_target_pairs={{0,8},{8,0},{16,24},{24,16},{1,9},{9,1},{17,25},{25,17},{2,10},{10... | collective-permute-start | bytes 2359304 | tf_op jit(solution)/shard_map/ppermute | solution.py:25
  401.5 17.3 %collective-permute-start.33 = (bf16[768,512]{1,0:T(8,128)(2,1)S(1)}, bf16[768,512]{1,0:T(8,128)(2,1)S(1)}, u32[]{:S(2)}, u32[]{:S(2)}) collective-permute-start(bf16[768,512]{1,0:T(8,128)(2,1)S(1)} %slice.365), channel_id=1, source_target_pairs={{0,16},{8,24},{16,0},{24,8},{1,17},{9,25},{17,1},{25,9},{2,18},{10... | collective-permute-start | bytes 2359304 | tf_op jit(solution)/shard_map/ppermute | solution.py:25
  445.7 258.4 %reduce-scatter.9.cloned.1.call-start = ((), (), s32[]{:S(2)}) async-start(), calls=%async_computation.12 | async-start | bytes 2359296 | tf_op jit(solution)/shard_map/reduce_scatter | solution.py:773
  447.1 30.8 %collective-permute-start.32 = (bf16[1536,512]{1,0:T(8,128)(2,1)S(1)}, bf16[1536,512]{1,0:T(8,128)(2,1)S(1)}, u32[]{:S(2)}, u32[]{:S(2)}) collective-permute-start(bf16[1536,512]{1,0:T(8,128)(2,1)S(1)} %copy-done.68), channel_id=1, source_target_pairs={{0,16},{8,24},{16,0},{24,8},{1,17},{9,25},{17,1},{25,9},{2,18},{10... | collective-permute-start | bytes 4718600 | tf_op jit(solution)/shard_map/ppermute | solution.py:25
  447.9 30.8 %collective-permute-start.30 = (bf16[1536,512]{1,0:T(8,128)(2,1)}, bf16[1536,512]{1,0:T(8,128)(2,1)S(1)}, u32[]{:S(2)}, u32[]{:S(2)}) collective-permute-start(bf16[1536,512]{1,0:T(8,128)(2,1)} %pad_maximum_fusion.4), channel_id=1, source_target_pairs={{0,8},{8,0},{16,24},{24,16},{1,9},{9,1},{17,25},{25,17},{2,10},{10... | collective-permute-start | bytes 4718600 | tf_op jit(solution)/shard_map/ppermute | solution.py:25
  497.3 17.2 %collective-permute-start.36 = (bf16[192,2048]{1,0:T(8,128)(2,1)S(1)}, bf16[192,2048]{1,0:T(8,128)(2,1)S(1)}, u32[]{:S(2)}, u32[]{:S(2)}) collective-permute-start(bf16[192,2048]{1,0:T(8,128)(2,1)S(1)} %get-tuple-element.349), channel_id=1, source_target_pairs={{0,16},{8,24},{16,0},{24,8},{1,17},{9,25},{17,1},{25,9},{2,18},{10... | collective-permute-start | bytes 2359304 | tf_op jit(solution)/shard_map/ppermute | solution.py:25
  498.0 16.5 %collective-permute-start.35 = (bf16[192,2048]{1,0:T(8,128)(2,1)S(1)}, bf16[192,2048]{1,0:T(8,128)(2,1)S(1)}, u32[]{:S(2)}, u32[]{:S(2)}) collective-permute-start(bf16[192,2048]{1,0:T(8,128)(2,1)S(1)} %get-tuple-element.350), channel_id=1, source_target_pairs={{0,8},{8,0},{16,24},{24,16},{1,9},{9,1},{17,25},{25,17},{2,10},{10... | collective-permute-start | bytes 2359304 | tf_op jit(solution)/shard_map/ppermute | solution.py:25
  516.5 38.4 %collective-permute-start.37 = (bf16[384,2048]{1,0:T(8,128)(2,1)}, bf16[384,2048]{1,0:T(8,128)(2,1)}, u32[]{:S(2)}, u32[]{:S(2)}) collective-permute-start(bf16[384,2048]{1,0:T(8,128)(2,1)} %pad_maximum_fusion.7), channel_id=1, source_target_pairs={{0,8},{8,0},{16,24},{24,16},{1,9},{9,1},{17,25},{25,17},{2,10},{10... | collective-permute-start | bytes 4718600 | tf_op jit(solution)/shard_map/ppermute | solution.py:25
  519.5 35.3 %collective-permute-start.38 = (bf16[384,2048]{1,0:T(8,128)(2,1)}, bf16[384,2048]{1,0:T(8,128)(2,1)}, u32[]{:S(2)}, u32[]{:S(2)}) collective-permute-start(bf16[384,2048]{1,0:T(8,128)(2,1)} %pad_maximum_fusion.8), channel_id=1, source_target_pairs={{0,16},{8,24},{16,0},{24,8},{1,17},{9,25},{17,1},{25,9},{2,18},{10... | collective-permute-start | bytes 4718600 | tf_op jit(solution)/shard_map/ppermute | solution.py:25
  564.3 32.4 %collective-permute-start.40 = (bf16[384,2048]{1,0:T(8,128)(2,1)S(1)}, bf16[384,2048]{1,0:T(8,128)(2,1)S(1)}, u32[]{:S(2)}, u32[]{:S(2)}) collective-permute-start(bf16[384,2048]{1,0:T(8,128)(2,1)S(1)} %get-tuple-element.243), channel_id=1, source_target_pairs={{0,16},{8,24},{16,0},{24,8},{1,17},{9,25},{17,1},{25,9},{2,18},{10... | collective-permute-start | bytes 4718600 | tf_op jit(solution)/shard_map/ppermute | solution.py:25
  564.8 33.2 %collective-permute-start.39 = (bf16[384,2048]{1,0:T(8,128)(2,1)S(1)}, bf16[384,2048]{1,0:T(8,128)(2,1)S(1)}, u32[]{:S(2)}, u32[]{:S(2)}) collective-permute-start(bf16[384,2048]{1,0:T(8,128)(2,1)S(1)} %get-tuple-element.243), channel_id=1, source_target_pairs={{0,8},{8,0},{16,24},{24,16},{1,9},{9,1},{17,25},{25,17},{2,10},{10... | collective-permute-start | bytes 4718600 | tf_op jit(solution)/shard_map/ppermute | solution.py:25
  599.1 12.1 %collective-permute-start.42 = (bf16[192,2048]{1,0:T(8,128)(2,1)S(1)}, bf16[192,2048]{1,0:T(8,128)(2,1)}, u32[]{:S(2)}, u32[]{:S(2)}) collective-permute-start(bf16[192,2048]{1,0:T(8,128)(2,1)S(1)} %slice.374), channel_id=1, source_target_pairs={{0,8},{8,0},{16,24},{24,16},{1,9},{9,1},{17,25},{25,17},{2,10},{10... | collective-permute-start | bytes 2359304 | tf_op jit(solution)/shard_map/ppermute | solution.py:25
  600.4 12.1 %collective-permute-start.41 = (bf16[192,2048]{1,0:T(8,128)(2,1)S(1)}, bf16[192,2048]{1,0:T(8,128)(2,1)}, u32[]{:S(2)}, u32[]{:S(2)}) collective-permute-start(bf16[192,2048]{1,0:T(8,128)(2,1)S(1)} %slice.373), channel_id=1, source_target_pairs={{0,16},{8,24},{16,0},{24,8},{1,17},{9,25},{17,1},{25,9},{2,18},{10... | collective-permute-start | bytes 2359304 | tf_op jit(solution)/shard_map/ppermute | solution.py:25
  624.6 117.5 %reduce-scatter.11.cloned.1.call-start = ((), (), s32[]{:S(2)}) async-start(), calls=%async_computation.13 | async-start | bytes 8257536 | tf_op jit(solution)/shard_map/reduce_scatter | solution.py:773
  625.3 249.5 %reduce-scatter.17.cloned.1.call-start = ((), (), s32[]{:S(2)}) async-start(), calls=%async_computation.16 | async-start | bytes 2359296 | tf_op jit(solution)/shard_map/reduce_scatter | solution.py:773
  626.1 257.5 %reduce-scatter.15.cloned.1.call-start = ((), (), s32[]{:S(2)}) async-start(), calls=%async_computation.15 | async-start | bytes 4718592 | tf_op jit(solution)/shard_map/reduce_scatter | solution.py:773
  688.1 200.2 %reduce-scatter.13.cloned.1.call-start = ((), (), s32[]{:S(2)}) async-start(), calls=%async_computation.14 | async-start | bytes 4718592 | tf_op jit(solution)/shard_map/reduce_scatter | solution.py:773
  689.6 8.8 collective-permute-start.45
  691.6 11.0 %collective-permute-start.44 = (bf16[384,512]{1,0:T(8,128)(2,1)S(1)}, bf16[384,512]{1,0:T(8,128)(2,1)S(1)}, u32[]{:S(2)}, u32[]{:S(2)}) collective-permute-start(bf16[384,512]{1,0:T(8,128)(2,1)S(1)} %get-tuple-element.346), channel_id=1, source_target_pairs={{0,16},{8,24},{16,0},{24,8},{1,17},{9,25},{17,1},{25,9},{2,18},{10... | collective-permute-start | bytes 1179656 | tf_op jit(solution)/shard_map/ppermute | solution.py:25
  691.9 11.4 %collective-permute-start.43 = (bf16[384,512]{1,0:T(8,128)(2,1)S(1)}, bf16[384,512]{1,0:T(8,128)(2,1)S(1)}, u32[]{:S(2)}, u32[]{:S(2)}) collective-permute-start(bf16[384,512]{1,0:T(8,128)(2,1)S(1)} %get-tuple-element.347), channel_id=1, source_target_pairs={{0,8},{8,0},{16,24},{24,16},{1,9},{9,1},{17,25},{25,17},{2,10},{10... | collective-permute-start | bytes 1179656 | tf_op jit(solution)/shard_map/ppermute | solution.py:25
  752.4 19.6 %collective-permute-start.47 = (bf16[192,2048]{1,0:T(8,128)(2,1)S(1)}, bf16[192,2048]{1,0:T(8,128)(2,1)S(1)}, u32[]{:S(2)}, u32[]{:S(2)}) collective-permute-start(bf16[192,2048]{1,0:T(8,128)(2,1)S(1)} %get-tuple-element.343), channel_id=1, source_target_pairs={{0,16},{8,24},{16,0},{24,8},{1,17},{9,25},{17,1},{25,9},{2,18},{10... | collective-permute-start | bytes 2359304 | tf_op jit(solution)/shard_map/ppermute | solution.py:25
  753.5 18.4 %collective-permute-start.46 = (bf16[192,2048]{1,0:T(8,128)(2,1)S(1)}, bf16[192,2048]{1,0:T(8,128)(2,1)S(1)}, u32[]{:S(2)}, u32[]{:S(2)}) collective-permute-start(bf16[192,2048]{1,0:T(8,128)(2,1)S(1)} %get-tuple-element.344), channel_id=1, source_target_pairs={{0,8},{8,0},{16,24},{24,16},{1,9},{9,1},{17,25},{25,17},{2,10},{10... | collective-permute-start | bytes 2359304 | tf_op jit(solution)/shard_map/ppermute | solution.py:25
  789.3 64.2 %collective-permute-start.48 = (bf16[384,2048]{1,0:T(8,128)(2,1)}, bf16[384,2048]{1,0:T(8,128)(2,1)}, u32[]{:S(2)}, u32[]{:S(2)}) collective-permute-start(bf16[384,2048]{1,0:T(8,128)(2,1)} %pad_maximum_fusion.9), channel_id=1, source_target_pairs={{0,8},{8,0},{16,24},{24,16},{1,9},{9,1},{17,25},{25,17},{2,10},{10... | collective-permute-start | bytes 4718600 | tf_op jit(solution)/shard_map/ppermute | solution.py:25
  789.8 63.6 %collective-permute-start.49 = (bf16[384,2048]{1,0:T(8,128)(2,1)}, bf16[384,2048]{1,0:T(8,128)(2,1)}, u32[]{:S(2)}, u32[]{:S(2)}) collective-permute-start(bf16[384,2048]{1,0:T(8,128)(2,1)} %pad_maximum_fusion.10), channel_id=1, source_target_pairs={{0,16},{8,24},{16,0},{24,8},{1,17},{9,25},{17,1},{25,9},{2,18},{10... | collective-permute-start | bytes 4718600 | tf_op jit(solution)/shard_map/ppermute | solution.py:25
  795.4 35.0 %collective-permute-start.52 = (bf16[64,1792]{1,0:T(8,128)(2,1)}, bf16[64,1792]{1,0:T(8,128)(2,1)S(1)}, u32[]{:S(2)}, u32[]{:S(2)}) collective-permute-start(bf16[64,1792]{1,0:T(8,128)(2,1)} %get-tuple-element.355), channel_id=1, source_target_pairs={{0,24},{8,16},{16,8},{24,0},{1,25},{9,17},{17,9},{25,1},{2,26},{10... | collective-permute-start | bytes 688136 | tf_op jit(solution)/shard_map/ppermute | solution.py:25
  797.4 35.8 %collective-permute-start.51 = (bf16[64,1792]{1,0:T(8,128)(2,1)}, bf16[64,1792]{1,0:T(8,128)(2,1)}, u32[]{:S(2)}, u32[]{:S(2)}) collective-permute-start(bf16[64,1792]{1,0:T(8,128)(2,1)} %get-tuple-element.356), channel_id=1, source_target_pairs={{0,16},{8,24},{16,0},{24,8},{1,17},{9,25},{17,1},{25,9},{2,18},{10... | collective-permute-start | bytes 688136 | tf_op jit(solution)/shard_map/ppermute | solution.py:25
  797.9 35.3 %collective-permute-start.50 = (bf16[64,1792]{1,0:T(8,128)(2,1)}, bf16[64,1792]{1,0:T(8,128)(2,1)}, u32[]{:S(2)}, u32[]{:S(2)}) collective-permute-start(bf16[64,1792]{1,0:T(8,128)(2,1)} %get-tuple-element.357), channel_id=1, source_target_pairs={{0,8},{8,0},{16,24},{24,16},{1,9},{9,1},{17,25},{25,17},{2,10},{10... | collective-permute-start | bytes 688136 | tf_op jit(solution)/shard_map/ppermute | solution.py:25
  870.5 8.8 collective-permute-start.64
  884.7 7.9 collective-permute-start.58
  886.3 7.7 collective-permute-start.57
  891.0 8.1 collective-permute-start.54
  (117 other events, 884.5 us)
Sparse Core Ops, SparseCore 0:
  28.8 67.8 all-gather.7
  98.9 27.7 all-gather.5
  128.2 28.5 all-gather.9
  158.4 90.2 all-gather.11
  250.1 71.8 all-gather.13
  445.9 79.5 reduce-scatter.6
  624.7 36.7 reduce-scatter.8
  663.8 78.2 reduce-scatter.10
  744.4 34.1 reduce-scatter.16
  780.7 48.6 reduce-scatter.14
  831.7 49.0 reduce-scatter.12

commit v7 on v6

--- a/solution.py
+++ b/solution.py
@@ -1,4 +1,3 @@
-import math
 from functools import partial
 
 import jax
@@ -93,7 +92,7 @@
 
 
 def scatter_small(parts):
-    for axis in ("seq", "dp"):
+    for axis in ("dp", "seq"):
         for bit in reversed(bits_of(lax.axis_size(axis))):
             half = parts.shape[0] // 2
             second = (lax.axis_index(axis) & bit) != 0
@@ -114,9 +113,7 @@
     return (lax.div(tile, per) ^ here) * per + lax.rem(tile, per)
 
 
-def kernel(body, name, grid, here, ins, outs, scratch=(), vmem=48, flops=0):
-    moved = sum(a.size * a.dtype.itemsize for a, _ in ins)
-    moved += sum(math.prod(shape) * jnp.dtype(kind).itemsize for shape, kind, _ in outs)
+def kernel(body, name, grid, here, ins, outs, scratch=(), vmem=48):
     return pl.pallas_call(
         body,
         out_shape=[jax.ShapeDtypeStruct(shape, kind) for shape, kind, _ in outs],
@@ -386,11 +383,10 @@
             ((count * tile, width), BF, block((tile, columns), lambda c, i, h: (i, c))),
             ((8, width), F32, block((8, columns), lambda c, i, h: (0, c))),
         ],
-        flops=2 * count * tile * width * sum(t[-1] for t in terms),
-    )
-
-
-def mixes_back_scatter(terms, step, marks, vec, here, seq, beside, ready=()):
+    )
+
+
+def mixes_back_scatter(terms, step, marks, vec, here, seq, beside):
     if seq != 4:
         grad, sums = mixes_back(terms, step, marks, vec, here, seq, 0, seq)
         return after(scatter_seq(blocks_of(grad, seq)), beside(grad)), sums
@@ -401,7 +397,7 @@
             [(t[0], g) + t[2:] for t, g in zip(terms, ordered)], step, marks, vec, here, seq, first, count
         )
 
-    far, sums_far = call(3, 1, ready)
+    far, sums_far = call(3, 1)
     near, sums_near = call(1, 2, far)
     parts = [None] + blocks_of(near, 2) + [far]
     started = after(scatter_start(parts), near)
@@ -489,7 +485,6 @@
             (params, fixed(params.shape)),
         ],
         [((rows, part), F32, own), ((rows, part), BF, own)],
-        flops=2 * rows * width * part,
     )
 
 
@@ -507,7 +502,6 @@
             (right, block((depth, part), lambda i, h: (0, h ^ relative_to))),
         ],
         [((rows, part), BF, block((tile, part), lambda i, h: (i ^ relative_to, 0)))],
-        flops=2 * rows * depth * part,
     )
     return result
 
@@ -700,7 +694,6 @@
         [(a, tokens) for a in (r, k, v)] + list(zip(tables, blocks)),
         [((length, width), F32, tokens), ((chunks, width, PAIR), BF, states)],
         [pltpu.VMEM((width, PAIR), F32)],
-        flops=length * width * 8000,
     )
 
 
@@ -713,7 +706,6 @@
         [(a, tokens) for a in (r, k, v, gate, wkv, d_mixed)] + [(states_kept, states)] + list(zip(tables, blocks)),
         [((length, width), BF, tokens)] * 4 + [((8, width), F32, fixed((8, width)))],
         [pltpu.VMEM((width, PAIR), F32)],
-        flops=length * width * 32000,
     )
 
 
@@ -772,10 +764,10 @@
     def scatter_dp(grad):
         return lax.psum_scatter(grad, "dp", scatter_dimension=0, tiled=True)
 
-    def owners_rows(summed, widths, beside=()):
+    def owners_rows(summed, widths):
         rows = summed.shape[0] // seq
         parts = [lax.dynamic_slice_in_dim(summed, (place ^ j) * rows, rows, 0) for j in range(seq)]
-        return join_columns(after(trade_seq(parts), beside), widths, here)
+        return join_columns(trade_seq(parts), widths, here)
 
     def turn_pieces(pieces):
         if within is not None:
@@ -785,10 +777,10 @@
     positions = jnp.arange(length, dtype=jnp.int32)
     piece, first_flags = segment_of(seq_lengths[0], positions)
 
-    columns_in, columns_g = stacked_columns([w_receptance, w_key, w_value, w_gate], [3 * part, part])
-    full_in = gather_dp(columns_in)
     vec_seq = gather_small(vectors[None], "seq")
     tokens_held = held_back(inputs_b, here, vec_seq)
+    columns_in, columns_g = stacked_columns([w_receptance, w_key, w_value, w_gate], [3 * part, part], tokens_held)
+    full_in = gather_dp(columns_in)
     vec_parts = gather_small(vec_seq[None], "dp").astype(F32)
     vec = vec_parts.transpose(2, 1, 0, 3).reshape(-1, width)
     turned = vec_parts.transpose(2, 0, 1, 3).reshape(-1, width)
@@ -815,8 +807,8 @@
     full_c = gather_dp(columns_c)
     full_ck, full_cr = full_c[:, :hidden_width], full_c[:, hidden_width:]
     full_cv = gather_dp(after(ffn_value, columns_c))
-    grad_all = gather_seq(after(grad_b, mix_r), projected)
     wkv, states = wkv_forward(recept, keyed, valued, tables, here, per)
+    grad_all = gather_seq(after(grad_b, mix_r), wkv)
     gate_pre, mixed = gated(mix_g, full_g, wkv, tables[5], here, seq)
     attn = [dot(rows, own_o, NN).astype(BF) for rows in blocks_of(after(mixed, grad_all[3:]), seq)]
     after_mix, normed_two = after_norm(inputs_b, scatter_seq(attn), rows_of(vec, 10, 11), here)
@@ -867,47 +859,46 @@
     d_attn = jnp.concatenate(after(gather_seq(d_attn), summed_cv), axis=0)
     d_mixed = dot(d_attn, own_o, NT).astype(BF)
     grad_wo = dot(mixed, d_attn, TN).astype(BF)
-    d_mixed = after(d_mixed, grad_wo)
+    d_mixed = after(d_mixed, grad_wo, summed_ck)
     summed_o = scatter_dp(grad_wo)
     d_recept, d_keyed, d_valued, d_gate, sums = wkv_backward(
         recept, keyed, valued, gate_pre, wkv, d_mixed, states, tables, here, per
     )
-    channel = trade_seq(blocks_of(after(channel, d_mixed), seq))
-    channel = after(channel, d_recept)
     grads_vg = [dot(mix_v, d_valued, TN).astype(BF), dot(mix_g, d_gate, TN).astype(BF)]
     summed_vg = scatter_dp(jnp.concatenate(grads_vg, axis=1))
-    grads_rk, out_rows, sums_early = [], [], []
+    grads_rk, sum_cv = [], []
 
     def beside(relayed):
         grads_rk.extend(
             dot(after(m, relayed), d, TN).astype(BF) for m, d in ((mix_r, d_recept), (mix_k, d_keyed))
         )
-        out_rows.append(spread_columns([after_mix], after(channel, relayed), here, False, False, CHUNK, per))
-        sums_early.append(after(summed_cv, relayed).astype(F32))
-        sums_early.extend(owners_rows(summed_ck, [ffn_key.shape[1]], relayed))
-        return grads_rk, out_rows, sums_early
-
-    d_recept, d_keyed = after((d_recept, d_keyed), grads_vg, summed_o, channel)
+        sum_cv.append(after(summed_cv, relayed).astype(F32))
+        return grads_rk, sum_cv
+
+    d_recept, d_keyed = after((d_recept, d_keyed), grads_vg, summed_o)
     terms, sums_one = mixes_back_scatter(
         [(i, d, 0, full_in, i, part) for i, d in enumerate((d_recept, d_keyed, d_valued))]
         + [(3, d_gate, 0, full_g, 0, part)],
-        step, marks, rows_of(turned, 2, 3, 4, 5), here, seq, beside, summed_ck,
+        step, marks, rows_of(turned, 2, 3, 4, 5), here, seq, beside,
     )
     summed_rk = scatter_dp(jnp.concatenate(grads_rk, axis=1))
-    (out_rows,), (sum_cv, sum_ck) = out_rows, sums_early
+    channel = trade_seq(blocks_of(after(channel, terms), seq))
+    out_rows = spread_columns([after_mix], channel, here, False, False, CHUNK, per)
+    (sum_ck,) = owners_rows(after(summed_ck, terms), [ffn_key.shape[1]])
     if within is None:
         terms = [outside(t, groups, unit, back=True) for t in terms]
     tokens_grad, _, norm_sums = norm_back(terms, inputs_b, d_after, rows_of(vec, 0), within, here)
 
-    (sum_cr,) = owners_rows(summed_cr, [width])
+    (sum_cr,) = owners_rows(after(summed_cr, terms), [width])
+    (sum_cv,) = sum_cv
     sum_o = summed_o.astype(F32)
     sum_v, sum_g = owners_rows(summed_vg, [width] * 2)
     sum_r, sum_k = owners_rows(summed_rk, [width] * 2)
 
     def by_device(rows, turn):
         if turn:
-            return rows.reshape(-1, dp, seq, unit).transpose(2, 1, 0, 3)
-        return rows.reshape(-1, seq, dp, unit).transpose(1, 2, 0, 3)
+            return rows.reshape(-1, dp, seq, unit).transpose(1, 2, 0, 3)
+        return rows.reshape(-1, seq, dp, unit).transpose(2, 1, 0, 3)
 
     own_sums = jnp.stack([sums[0] * log_decay, sums[1], sums[2], sums[3]])
     own_sums = lax.dynamic_update_slice(jnp.zeros((4, width), F32), own_sums, (0, place * part))

time: 913 us -> 859 us (0.941)
  waiting for transfers between devices: 328 us -> 270 us
    reduce_scatter x6, waiting for transfers between devices: 38 us -> 0.03 us  [scatter_dp(): return lax.psum_scatter(grad, 'dp', scatter_dimension=0, tiled=True)]
    ppermute x67, waiting for transfers between devices: 288 us -> 270 us  [swap(): return lax.ppermute(value, axis, [(i, i ^ distance) for i in range(size)])]
    unnamed x215 -> x213, local copies, waits for them, and re-layouts: 46.2 us -> 47.7 us
  transfers between devices with their start and end apart: 78 -> 78, of which waited for: 40 -> 36; matrix products, arithmetic and copies ran while one was open for 21% -> 23% of each run, Pallas kernels for 24% -> 26%
where the time goes in v7:
time: 859 us; the launch traced here: 853 us
  waiting for transfers between devices  270 us (31%)
  Pallas kernels  230 us (27%)
  matrix products  156 us (18%)
  starting transfers between devices  79.2 us (9%)
  local copies, waits for them, and re-layouts  74.8 us (9%)
  other arithmetic  26.3 us (3%)
  between operations  15.4 us (2%)
    ppermute x67, waiting for transfers between devices, swap(): return lax.ppermute(value, axis, [(i, i ^ distance) for i in range(size)])  270 us
    pallas_call x30, Pallas kernels, kernel(): pl.pallas_call(body, out_shape=[jax.ShapeDtypeStruct(shape, kind) for sha...  230 us
    dot_general x19, matrix products, dot(): return lax.dot_general(left, right, dims, preferred_element_type=F32)  156 us
    ppermute x67, starting transfers between devices, swap(): return lax.ppermute(value, axis, [(i, i ^ distance) for i in range(size)])  78 us
    unnamed x213, local copies, waits for them, and re-layouts  47.7 us
  transfers between devices with their start and end apart: 78, of which 36 were waited for; matrix products, arithmetic and copies ran while one was open for 23% of the time, Pallas kernels for 26%

profile of v7, /device:TPU:0, one launch (start us, length us, event | category | flops | bytes accessed | tf_op | source)
XLA Modules:
  0.0 853.0 jit_solution(1288329586002831323)
XLA Ops:
  7.2 3.0 collective-permute-start
  23.9 4.2 collective-permute-done.9.refs_1_
  28.0 4.2 collective-permute-done.10.refs_2_
  40.9 2.7 collective-permute-start.4
  44.1 2.8 collective-permute-done.4
  49.6 22.5 %collective-permute-done.6.refs_2_ = bf16[384,2048]{1,0:T(8,128)(2,1)} collective-permute-done((bf16[384,2048]{1,0:T(8,128)(2,1)S(1)}, bf16[384,2048]{1,0:T(8,128)(2,1)}, u32[]{:S(2)}, u32[]{:S(2)}) %collective-permute-start.6) | collective-permute-done | bytes 1572896 | tf_op jit(solution)/shard_map/ppermute | solution.py:24
  76.9 16.9 %collective-permute-done.8.refs_4_ = bf16[192,2048]{1,0:T(8,128)(2,1)S(1)} collective-permute-done((bf16[192,2048]{1,0:T(8,128)(2,1)S(1)}, bf16[192,2048]{1,0:T(8,128)(2,1)S(1)}, u32[]{:S(2)}, u32[]{:S(2)}) %collective-permute-start.8) | collective-permute-done | bytes 786464 | tf_op jit(solution)/shard_map/ppermute | solution.py:24
  98.5 17.6 %mixes.2 = (bf16[1536,2048]{1,0:T(8,128)(2,1)}, bf16[1536,2048]{1,0:T(8,128)(2,1)}, bf16[1536,2048]{1,0:T(8,128)(2,1)}, bf16[1536,2048]{1,0:T(8,128)(2,1)}, bf16[1536,2048]{1,0:T(8,128)(2,1)}) custom-call(s32[1]{0:T(128)} %bitcast.here, bf16[384,2048]{1,0:T(8,128)(2,1)S(1)} %hold.1.refs_0_, bf16[384,2048]{1,0:T(8,128)(2,1)} %collective-permute-done.5.refs_1_, ...), custom_call_target="tpu_custom_call" | custom-call | tf_op jit(solution)/shard_map/mixes/pallas_call | solution.py:117
  120.5 8.2 convolution_convert_fusion.11.r_ref
  128.7 7.5 convolution_convert_fusion.10.k_ref
  136.2 4.5 convolution_convert_fusion.9.v_ref
  147.7 13.4 %wkv_forward.1 = (f32[1536,512]{1,0:T(8,128)}, bf16[12,512,128]{2,1,0:T(8,128)(2,1)S(1)}) custom-call(s32[1]{0:T(128)} %bitcast.here, bf16[1536,512]{1,0:T(8,128)(2,1)S(1)} %copy-done.14, bf16[1536,512]{1,0:T(8,128)(2,1)} %convolution_convert_fusion.10.k_ref, bf16[1536,512]{1,0:T(8,128)(2,1)} %convolution_convert_fusion.9.v_ref, ...), custom_call_target="tpu_custom_call" | custom-call | tf_op jit(solution)/shard_map/wkv_forward/pallas_call | solution.py:117
  161.1 16.5 %collective-permute-done.13.refs_2_ = bf16[384,2048]{1,0:T(8,128)(2,1)S(1)} collective-permute-done((bf16[384,2048]{1,0:T(8,128)(2,1)S(1)}, bf16[384,2048]{1,0:T(8,128)(2,1)S(1)}, u32[]{:S(2)}, u32[]{:S(2)}) %collective-permute-start.13) | collective-permute-done | bytes 1572896 | tf_op jit(solution)/shard_map/ppermute | solution.py:24
  185.9 10.1 %gate.1 = (f32[1536,512]{1,0:T(8,128)}, bf16[1536,512]{1,0:T(8,128)(2,1)S(1)}) custom-call(s32[1]{0:T(128)} %bitcast.here, bf16[1536,2048]{1,0:T(8,128)(2,1)} %get-tuple-element.146.refs_0_, bf16[2048,512]{1,0:T(8,128)(2,1)S(1)} %copy-done.5, f32[1536,512]{1,0:T(8,128)} %get-tuple-element.161.refs_2_.wkv_ref, f32[8,512]{1,0:T(8,128)S(1)} %maximum_maximum_fusion.par_ref.refs_3_), custom_call_target="tpu_custom_call" | custom-call | tf_op jit(solution)/shard_map/gate/pallas_call | solution.py:117
  196.0 2.5 collective-permute-done.15.refs_4_
  198.9 2.8 convolution_convert_fusion.13
  206.4 10.5 %collective-permute-done.16 = bf16[192,2048]{1,0:T(8,128)(2,1)S(1)} collective-permute-done((bf16[192,2048]{1,0:T(8,128)(2,1)S(1)}, bf16[192,2048]{1,0:T(8,128)(2,1)S(1)}, u32[]{:S(2)}, u32[]{:S(2)}) %collective-permute-start.16) | collective-permute-done | bytes 786464 | tf_op jit(solution)/shard_map/ppermute | solution.py:24
  224.4 2.8 convolution_convert_fusion.15.refs_0_
  227.3 24.6 %collective-permute-done.17.refs_1_ = bf16[384,2048]{1,0:T(8,128)(2,1)} collective-permute-done((bf16[384,2048]{1,0:T(8,128)(2,1)}, bf16[384,2048]{1,0:T(8,128)(2,1)}, u32[]{:S(2)}, u32[]{:S(2)}) %collective-permute-start.17) | collective-permute-done | bytes 1572896 | tf_op jit(solution)/shard_map/ppermute | solution.py:24
  252.5 4.7 after_norm.1
  259.3 29.4 %collective-permute-done.21.refs_2_ = bf16[384,2048]{1,0:T(8,128)(2,1)S(1)} collective-permute-done((bf16[384,2048]{1,0:T(8,128)(2,1)S(1)}, bf16[384,2048]{1,0:T(8,128)(2,1)S(1)}, u32[]{:S(2)}, u32[]{:S(2)}) %collective-permute-start.21) | collective-permute-done | bytes 1572896 | tf_op jit(solution)/shard_map/ppermute | solution.py:24
  294.8 11.3 %collective-permute-done.23.refs_4_ = bf16[192,2048]{1,0:T(8,128)(2,1)} collective-permute-done((bf16[192,2048]{1,0:T(8,128)(2,1)}, bf16[192,2048]{1,0:T(8,128)(2,1)}, u32[]{:S(2)}, u32[]{:S(2)}) %collective-permute-start.23) | collective-permute-done | bytes 786464 | tf_op jit(solution)/shard_map/ppermute | solution.py:24
  309.6 12.2 %mixes.3 = (bf16[1536,2048]{1,0:T(8,128)(2,1)}, bf16[1536,2048]{1,0:T(8,128)(2,1)}, bf16[1536,2048]{1,0:T(8,128)(2,1)}) custom-call(s32[1]{0:T(128)} %bitcast.here, bf16[384,2048]{1,0:T(8,128)(2,1)S(1)} %copy-done.26, bf16[384,2048]{1,0:T(8,128)(2,1)S(1)} %copy-done.17, bf16[384,2048]{1,0:T(8,128)(2,1)} %copy-done.64, ...), custom_call_target="tpu_custom_call" | custom-call | tf_op jit(solution)/shard_map/mixes/pallas_call | solution.py:117
  321.8 9.5 %divide_convert_fusion = (bf16[1536,512]{1,0:T(8,128)(2,1)}, f32[1536,512]{1,0:T(8,128)}) fusion(bf16[1536,2048]{1,0:T(8,128)(2,1)} %get-tuple-element.215, bf16[2048,2304]{1,0:T(8,128)(2,1)} %all-gather.12.cloned.1.call-done.refs_6_.refs_7_.refs_8_), kind=kOutput, calls=%fused_computation.10 | convolution fusion | flops 3224371200 | bytes 13107200 | tf_op jit(solution)/shard_map/dot_general | solution.py:543
  334.2 22.9 %multiply_convert_fusion.1 = (bf16[1536,1792]{1,0:T(8,128)(2,1)}, bf16[1536,1792]{1,0:T(8,128)(2,1)}) fusion(bf16[1536,2048]{1,0:T(8,128)(2,1)} %get-tuple-element.214, bf16[2048,2304]{1,0:T(8,128)(2,1)S(1)} %copy-done.61), kind=kOutput, calls=%fused_computation.2 | convolution fusion | flops 11312824320 | bytes 24641536 | tf_op jit(solution)/shard_map/dot_general | solution.py:543
  357.2 6.0 value_columns.6
  364.6 6.0 value_columns.7
  370.7 8.3 collective-permute-done.31
  385.4 6.0 value_columns.5
  391.5 6.0 value_columns.4.refs_5_
  401.6 9.5 %spread_columns.2 = bf16[1536,2048]{1,0:T(8,128)(2,1)} custom-call(s32[1]{0:T(128)} %bitcast.here, bf16[384,2048]{1,0:T(8,128)(2,1)S(1)} %bitcast.97, bf16[384,2048]{1,0:T(8,128)(2,1)S(1)} %copy-done.13, bf16[384,2048]{1,0:T(8,128)(2,1)} %copy-done.63, bf16[192,2048]{1,0:T(8,128)(2,1)} %collective-permute-done.14.refs_3_, ...), custom_call_target="tpu_custom_call" | custom-call | tf_op jit(solution)/shard_map/spread_columns/pallas_call | solution.py:117
  411.1 16.1 %convolution_convert_fusion.1 = bf16[1792,2048]{1,0:T(8,128)(2,1)} fusion(bf16[1536,1792]{1,0:T(8,128)(2,1)S(1)} %bitcast.103, bf16[1536,2048]{1,0:T(8,128)(2,1)} %spread_columns.2), kind=kOutput, calls=%fused_computation.5 | convolution fusion | flops 11277959168 | bytes 19136512 | tf_op jit(solution)/shard_map/dot_general | solution.py:543
  430.2 18.8 %multiply_convert_fusion.refs_0_.refs_3_ = bf16[1536,1792]{1,0:T(8,128)(2,1)} fusion(bf16[1536,1792]{1,0:T(8,128)(2,1)} %get-tuple-element.197, bf16[1536,2048]{1,0:T(8,128)(2,1)} %spread_columns.2, bf16[1792,2048]{1,0:T(8,128)(2,1)} %all-gather.14.cloned.1.call-done.right_ref), kind=kOutput, calls=%fused_computation.1 | convolution fusion | flops 11282546688 | bytes 24641536 | tf_op jit(solution)/shard_map/dot_general | solution.py:543
  449.0 10.7 %collective-permute-done.32.refs_7_ = bf16[1536,512]{1,0:T(8,128)(2,1)S(1)} collective-permute-done((bf16[1536,512]{1,0:T(8,128)(2,1)S(1)}, bf16[1536,512]{1,0:T(8,128)(2,1)S(1)}, u32[]{:S(2)}, u32[]{:S(2)}) %collective-permute-start.32) | collective-permute-done | bytes 1572896 | tf_op jit(solution)/shard_map/ppermute | solution.py:24
  462.2 7.0 channel.1
  469.2 9.0 %mixes_back.6 = (bf16[384,2048]{1,0:T(8,128)(2,1)S(1)}, f32[8,2048]{1,0:T(8,128)S(1)}) custom-call(s32[1]{0:T(128)} %bitcast.here, bf16[1536,1792]{1,0:T(8,128)(2,1)} %multiply_convert_fusion.refs_0_.refs_3_, bf16[1536,512]{1,0:T(8,128)(2,1)S(1)} %get-tuple-element.212.refs_1_.refs_2_.refs_4_.refs_5_, ...), custom_call_target="tpu_custom_call" | custom-call | tf_op jit(solution)/shard_map/mixes_back/pallas_call | solution.py:117
  479.3 16.0 %mixes_back.7 = (bf16[768,2048]{1,0:T(8,128)(2,1)S(1)}, f32[8,2048]{1,0:T(8,128)S(1)}) custom-call(s32[1]{0:T(128)} %bitcast.here, bf16[1536,1792]{1,0:T(8,128)(2,1)} %multiply_convert_fusion.refs_0_.refs_3_, bf16[1536,512]{1,0:T(8,128)(2,1)S(1)} %get-tuple-element.212.refs_1_.refs_2_.refs_4_.refs_5_, ...), custom_call_target="tpu_custom_call" | custom-call | tf_op jit(solution)/shard_map/mixes_back/pallas_call | solution.py:117
  498.7 16.1 %convolution_convert_fusion = bf16[2048,1792]{1,0:T(8,128)(2,1)} fusion(bf16[1536,2048]{1,0:T(8,128)(2,1)} %get-tuple-element.214, bf16[1536,1792]{1,0:T(8,128)(2,1)S(1)} %bitcast.101), kind=kOutput, calls=%fused_computation.4 | convolution fusion | flops 11277959168 | bytes 19136512 | tf_op jit(solution)/shard_map/dot_general | solution.py:543
  518.1 8.8 %mixes_back.8 = (bf16[384,2048]{1,0:T(8,128)(2,1)S(1)}, f32[8,2048]{1,0:T(8,128)S(1)}) custom-call(s32[1]{0:T(128)} %bitcast.here, bf16[1536,1792]{1,0:T(8,128)(2,1)} %multiply_convert_fusion.refs_0_.refs_3_, bf16[1536,512]{1,0:T(8,128)(2,1)S(1)} %get-tuple-element.212.refs_1_.refs_2_.refs_4_.refs_5_, ...), custom_call_target="tpu_custom_call" | custom-call | tf_op jit(solution)/shard_map/mixes_back/pallas_call | solution.py:117
  528.1 7.8 convolution_convert_fusion.8
  535.9 9.6 %collective-permute-done.37.refs_1_ = bf16[384,2048]{1,0:T(8,128)(2,1)} collective-permute-done((bf16[384,2048]{1,0:T(8,128)(2,1)}, bf16[384,2048]{1,0:T(8,128)(2,1)}, u32[]{:S(2)}, u32[]{:S(2)}) %collective-permute-start.37) | collective-permute-done | bytes 1572896 | tf_op jit(solution)/shard_map/ppermute | solution.py:24
  549.8 6.6 norm_back.2
  557.9 30.9 %collective-permute-done.40 = bf16[384,2048]{1,0:T(8,128)(2,1)S(1)} collective-permute-done((bf16[384,2048]{1,0:T(8,128)(2,1)S(1)}, bf16[384,2048]{1,0:T(8,128)(2,1)S(1)}, u32[]{:S(2)}, u32[]{:S(2)}) %collective-permute-start.40) | collective-permute-done | bytes 1572896 | tf_op jit(solution)/shard_map/ppermute | solution.py:24
  593.3 10.1 %collective-permute-done.42 = bf16[192,2048]{1,0:T(8,128)(2,1)S(1)} collective-permute-done((bf16[192,2048]{1,0:T(8,128)(2,1)S(1)}, bf16[192,2048]{1,0:T(8,128)(2,1)S(1)}, u32[]{:S(2)}, u32[]{:S(2)}) %collective-permute-start.42) | collective-permute-done | bytes 786464 | tf_op jit(solution)/shard_map/ppermute | solution.py:24
  607.2 2.7 copy-done.76
  609.9 4.6 convolution_convert_fusion.6
  615.4 8.1 convolution_convert_fusion.7.d_mixed_ref
  623.5 37.3 %wkv_backward.1 = (bf16[1536,512]{1,0:T(8,128)(2,1)S(1)}, bf16[1536,512]{1,0:T(8,128)(2,1)S(1)}, bf16[1536,512]{1,0:T(8,128)(2,1)}, bf16[1536,512]{1,0:T(8,128)(2,1)}, f32[8,512]{1,0:T(8,128)S(1)}) custom-call(s32[1]{0:T(128)} %bitcast.here, bf16[1536,512]{1,0:T(8,128)(2,1)} %convolution_convert_fusion.11.r_ref, ...), custom_call_target="tpu_custom_call" | custom-call | tf_op jit(solution)/shard_map/wkv_backward/pallas_call | solution.py:117
  660.8 7.3 convolution_convert_fusion.4
  668.1 6.7 convolution_convert_fusion.5
  674.8 2.6 pad_maximum_fusion.1
  679.7 8.6 %mixes_back.9 = (bf16[384,2048]{1,0:T(8,128)(2,1)S(1)}, f32[8,2048]{1,0:T(8,128)S(1)}) custom-call(s32[1]{0:T(128)} %bitcast.here, bf16[1536,512]{1,0:T(8,128)(2,1)S(1)} %get-tuple-element.248.refs_0_.refs_4_, bf16[1536,512]{1,0:T(8,128)(2,1)S(1)} %copy-done.1, bf16[1536,512]{1,0:T(8,128)(2,1)} %get-tuple-element.250.refs_2_.refs_6_, ...), custom_call_target="tpu_custom_call" | custom-call | tf_op jit(solution)/shard_map/mixes_back/pallas_call | solution.py:117
  691.5 15.6 %mixes_back.10 = (bf16[768,2048]{1,0:T(8,128)(2,1)}, f32[8,2048]{1,0:T(8,128)S(1)}) custom-call(s32[1]{0:T(128)} %bitcast.here, bf16[1536,512]{1,0:T(8,128)(2,1)S(1)} %get-tuple-element.248.refs_0_.refs_4_, bf16[1536,512]{1,0:T(8,128)(2,1)S(1)} %copy-done.1, bf16[1536,512]{1,0:T(8,128)(2,1)S(1)} %copy-done.4, ...), custom_call_target="tpu_custom_call" | custom-call | tf_op jit(solution)/shard_map/mixes_back/pallas_call | solution.py:117
  712.8 6.9 convolution_convert_fusion.2
  719.7 3.7 convolution_convert_fusion.3
  723.4 2.6 pad_maximum_fusion
  731.7 8.2 mixes_back.11
  743.3 8.2 collective-permute-done.45.refs_1_
  754.1 7.2 norm_back.3
  762.1 3.9 collective-permute-start.62
  766.1 8.7 %collective-permute-done.62 = f32[16,14,64]{2,1,0:T(8,128)S(1)} collective-permute-done((f32[16,14,64]{2,1,0:T(8,128)S(1)}, f32[16,14,64]{2,1,0:T(8,128)S(1)}, u32[]{:S(2)}, u32[]{:S(2)}) %collective-permute-start.62) | collective-permute-done | bytes 57376 | tf_op jit(solution)/shard_map/ppermute | solution.py:24
  776.0 4.9 collective-permute-done.63
  796.1 16.9 %collective-permute-done.66 = f32[1,14,64]{2,1,0:T(8,128)S(1)} collective-permute-done((f32[1,14,64]{2,1,0:T(8,128)S(1)}, f32[1,14,64]{2,1,0:T(8,128)S(1)}, u32[]{:S(2)}, u32[]{:S(2)}) %collective-permute-start.66) | collective-permute-done | bytes 3616 | tf_op jit(solution)/shard_map/ppermute | solution.py:24
  839.6 3.6 spread_columns.3
  (503 shorter events, 192.2 us)
Async XLA Ops:
  7.2 113.3 %all-gather.8.cloned.1.call-start = ((), (), s32[]{:S(2)}) async-start(), calls=%async_computation.7 | async-start | bytes 7077888 | tf_op jit(solution)/shard_map/all_gather | solution.py:762
  20.3 12.0 %collective-permute-start.10 = (bf16[64,2048]{1,0:T(8,128)(2,1)S(1)}, bf16[64,2048]{1,0:T(8,128)(2,1)S(1)}, u32[]{:S(2)}, u32[]{:S(2)}) collective-permute-start(bf16[64,2048]{1,0:T(8,128)(2,1)S(1)} %get-tuple-element.149), channel_id=1, source_target_pairs={{0,16},{8,24},{16,0},{24,8},{1,17},{9,25},{17,1},{25,9},{2,18},{10... | collective-permute-start | bytes 786440 | tf_op jit(solution)/shard_map/ppermute | solution.py:24
  33.9 150.4 %all-gather.6.cloned.1.call-start = ((), (), s32[]{:S(2)}) async-start(), calls=%async_computation.6 | async-start | bytes 2359296 | tf_op jit(solution)/shard_map/all_gather | solution.py:762
  35.1 37.0 %collective-permute-start.6 = (bf16[384,2048]{1,0:T(8,128)(2,1)S(1)}, bf16[384,2048]{1,0:T(8,128)(2,1)}, u32[]{:S(2)}, u32[]{:S(2)}) collective-permute-start(bf16[384,2048]{1,0:T(8,128)(2,1)S(1)} %hold.1.refs_0_), channel_id=1, source_target_pairs={{0,16},{8,24},{16,0},{24,8},{1,17},{9,25},{17,1},{25,9},{2,18},{10... | collective-permute-start | bytes 4718600 | tf_op jit(solution)/shard_map/ppermute | solution.py:24
  35.6 36.6 %collective-permute-start.5 = (bf16[384,2048]{1,0:T(8,128)(2,1)S(1)}, bf16[384,2048]{1,0:T(8,128)(2,1)}, u32[]{:S(2)}, u32[]{:S(2)}) collective-permute-start(bf16[384,2048]{1,0:T(8,128)(2,1)S(1)} %hold.1.refs_0_), channel_id=1, source_target_pairs={{0,8},{8,0},{16,24},{24,16},{1,9},{9,1},{17,25},{25,17},{2,10},{10... | collective-permute-start | bytes 4718600 | tf_op jit(solution)/shard_map/ppermute | solution.py:24
  72.3 126.6 %all-gather.10.cloned.1.call-start = ((), (), s32[]{:S(2)}) async-start(), calls=%async_computation.8 | async-start | bytes 2359296 | tf_op jit(solution)/shard_map/all_gather | solution.py:762
  74.8 19.0 %collective-permute-start.8 = (bf16[192,2048]{1,0:T(8,128)(2,1)S(1)}, bf16[192,2048]{1,0:T(8,128)(2,1)S(1)}, u32[]{:S(2)}, u32[]{:S(2)}) collective-permute-start(bf16[192,2048]{1,0:T(8,128)(2,1)S(1)} %slice.331), channel_id=1, source_target_pairs={{0,8},{8,0},{16,24},{24,16},{1,9},{9,1},{17,25},{25,17},{2,10},{10... | collective-permute-start | bytes 2359304 | tf_op jit(solution)/shard_map/ppermute | solution.py:24
  76.1 18.6 %collective-permute-start.7 = (bf16[192,2048]{1,0:T(8,128)(2,1)S(1)}, bf16[192,2048]{1,0:T(8,128)(2,1)S(1)}, u32[]{:S(2)}, u32[]{:S(2)}) collective-permute-start(bf16[192,2048]{1,0:T(8,128)(2,1)S(1)} %slice.330), channel_id=1, source_target_pairs={{0,16},{8,24},{16,0},{24,8},{1,17},{9,25},{17,1},{25,9},{2,18},{10... | collective-permute-start | bytes 2359304 | tf_op jit(solution)/shard_map/ppermute | solution.py:24
  95.6 226.3 %all-gather.12.cloned.1.call-start = ((), (), s32[]{:S(2)}) async-start(), calls=%async_computation.9 | async-start | bytes 10616832 | tf_op jit(solution)/shard_map/all_gather | solution.py:762
  117.0 23.8 %collective-permute-start.24 = (bf16[64,2304]{1,0:T(8,128)(2,1)}, bf16[64,2304]{1,0:T(8,128)(2,1)}, u32[]{:S(2)}, u32[]{:S(2)}) collective-permute-start(bf16[64,2304]{1,0:T(8,128)(2,1)} %get-tuple-element.176), channel_id=1, source_target_pairs={{0,8},{8,0},{16,24},{24,16},{1,9},{9,1},{17,25},{25,17},{2,10},{10... | collective-permute-start | bytes 884744 | tf_op jit(solution)/shard_map/ppermute | solution.py:24
  118.8 22.0 %collective-permute-start.25 = (bf16[64,2304]{1,0:T(8,128)(2,1)}, bf16[64,2304]{1,0:T(8,128)(2,1)}, u32[]{:S(2)}, u32[]{:S(2)}) collective-permute-start(bf16[64,2304]{1,0:T(8,128)(2,1)} %get-tuple-element.177), channel_id=1, source_target_pairs={{0,16},{8,24},{16,0},{24,8},{1,17},{9,25},{17,1},{25,9},{2,18},{10... | collective-permute-start | bytes 884744 | tf_op jit(solution)/shard_map/ppermute | solution.py:24
  119.9 20.8 %collective-permute-start.26 = (bf16[64,2304]{1,0:T(8,128)(2,1)}, bf16[64,2304]{1,0:T(8,128)(2,1)}, u32[]{:S(2)}, u32[]{:S(2)}) collective-permute-start(bf16[64,2304]{1,0:T(8,128)(2,1)} %get-tuple-element.178), channel_id=1, source_target_pairs={{0,24},{8,16},{16,8},{24,0},{1,25},{9,17},{17,9},{25,1},{2,26},{10... | collective-permute-start | bytes 884744 | tf_op jit(solution)/shard_map/ppermute | solution.py:24
  143.2 214.0 %all-gather.14.cloned.1.call-start = ((), (), s32[]{:S(2)}) async-start(), calls=%async_computation.10 | async-start | bytes 8257536 | tf_op jit(solution)/shard_map/all_gather | solution.py:762
  143.2 34.4 %collective-permute-start.13 = (bf16[384,2048]{1,0:T(8,128)(2,1)S(1)}, bf16[384,2048]{1,0:T(8,128)(2,1)S(1)}, u32[]{:S(2)}, u32[]{:S(2)}) collective-permute-start(bf16[384,2048]{1,0:T(8,128)(2,1)S(1)} %bitcast.95), channel_id=1, source_target_pairs={{0,16},{8,24},{16,0},{24,8},{1,17},{9,25},{17,1},{25,9},{2,18},{10... | collective-permute-start | bytes 4718600 | tf_op jit(solution)/shard_map/ppermute | solution.py:24
  145.3 33.8 %collective-permute-start.12 = (bf16[384,2048]{1,0:T(8,128)(2,1)S(1)}, bf16[384,2048]{1,0:T(8,128)(2,1)S(1)}, u32[]{:S(2)}, u32[]{:S(2)}) collective-permute-start(bf16[384,2048]{1,0:T(8,128)(2,1)S(1)} %bitcast.96), channel_id=1, source_target_pairs={{0,8},{8,0},{16,24},{24,16},{1,9},{9,1},{17,25},{25,17},{2,10},{10... | collective-permute-start | bytes 4718600 | tf_op jit(solution)/shard_map/ppermute | solution.py:24
  182.2 16.3 %collective-permute-start.15 = (bf16[192,2048]{1,0:T(8,128)(2,1)}, bf16[192,2048]{1,0:T(8,128)(2,1)S(1)}, u32[]{:S(2)}, u32[]{:S(2)}) collective-permute-start(bf16[192,2048]{1,0:T(8,128)(2,1)} %slice.336), channel_id=1, source_target_pairs={{0,8},{8,0},{16,24},{24,16},{1,9},{9,1},{17,25},{25,17},{2,10},{10... | collective-permute-start | bytes 2359304 | tf_op jit(solution)/shard_map/ppermute | solution.py:24
  182.8 16.1 %collective-permute-start.14 = (bf16[192,2048]{1,0:T(8,128)(2,1)}, bf16[192,2048]{1,0:T(8,128)(2,1)}, u32[]{:S(2)}, u32[]{:S(2)}) collective-permute-start(bf16[192,2048]{1,0:T(8,128)(2,1)} %slice.335), channel_id=1, source_target_pairs={{0,16},{8,24},{16,0},{24,8},{1,17},{9,25},{17,1},{25,9},{2,18},{10... | collective-permute-start | bytes 2359304 | tf_op jit(solution)/shard_map/ppermute | solution.py:24
  184.1 419.7 %reduce-scatter.7.cloned.1.call-start = ((), (), s32[]{:S(2)}) async-start(), calls=%async_computation.11 | async-start | bytes 8257536 | tf_op jit(solution)/shard_map/reduce_scatter | solution.py:765
  201.9 15.1 %collective-permute-start.16 = (bf16[192,2048]{1,0:T(8,128)(2,1)S(1)}, bf16[192,2048]{1,0:T(8,128)(2,1)S(1)}, u32[]{:S(2)}, u32[]{:S(2)}) collective-permute-start(bf16[192,2048]{1,0:T(8,128)(2,1)S(1)} %get-tuple-element.310), channel_id=1, source_target_pairs={{0,16},{8,24},{16,0},{24,8},{1,17},{9,25},{17,1},{25,9},{2,18},{10... | collective-permute-start | bytes 2359304 | tf_op jit(solution)/shard_map/ppermute | solution.py:24
  203.3 16.7 %collective-permute-start.18 = (bf16[192,2048]{1,0:T(8,128)(2,1)S(1)}, bf16[192,2048]{1,0:T(8,128)(2,1)S(1)}, u32[]{:S(2)}, u32[]{:S(2)}) collective-permute-start(bf16[192,2048]{1,0:T(8,128)(2,1)S(1)} %get-tuple-element.309), channel_id=1, source_target_pairs={{0,8},{8,0},{16,24},{24,16},{1,9},{9,1},{17,25},{25,17},{2,10},{10... | collective-permute-start | bytes 2359304 | tf_op jit(solution)/shard_map/ppermute | solution.py:24
  218.5 33.4 %collective-permute-start.17 = (bf16[384,2048]{1,0:T(8,128)(2,1)}, bf16[384,2048]{1,0:T(8,128)(2,1)}, u32[]{:S(2)}, u32[]{:S(2)}) collective-permute-start(bf16[384,2048]{1,0:T(8,128)(2,1)} %pad_maximum_fusion.2), channel_id=1, source_target_pairs={{0,8},{8,0},{16,24},{24,16},{1,9},{9,1},{17,25},{25,17},{2,10},{10... | collective-permute-start | bytes 4718600 | tf_op jit(solution)/shard_map/ppermute | solution.py:24
  221.6 30.9 %collective-permute-start.19 = (bf16[384,2048]{1,0:T(8,128)(2,1)}, bf16[384,2048]{1,0:T(8,128)(2,1)}, u32[]{:S(2)}, u32[]{:S(2)}) collective-permute-start(bf16[384,2048]{1,0:T(8,128)(2,1)} %pad_maximum_fusion.3), channel_id=1, source_target_pairs={{0,16},{8,24},{16,0},{24,8},{1,17},{9,25},{17,1},{25,9},{2,18},{10... | collective-permute-start | bytes 4718600 | tf_op jit(solution)/shard_map/ppermute | solution.py:24
  257.2 31.6 %collective-permute-start.21 = (bf16[384,2048]{1,0:T(8,128)(2,1)S(1)}, bf16[384,2048]{1,0:T(8,128)(2,1)S(1)}, u32[]{:S(2)}, u32[]{:S(2)}) collective-permute-start(bf16[384,2048]{1,0:T(8,128)(2,1)S(1)} %get-tuple-element.169.refs_0_), channel_id=1, source_target_pairs={{0,16},{8,24},{16,0},{24,8},{1,17},{9,25},{17,1},{25,9},{2,18},{10... | collective-permute-start | bytes 4718600 | tf_op jit(solution)/shard_map/ppermute | solution.py:24
  258.6 30.2 %collective-permute-start.20 = (bf16[384,2048]{1,0:T(8,128)(2,1)S(1)}, bf16[384,2048]{1,0:T(8,128)(2,1)S(1)}, u32[]{:S(2)}, u32[]{:S(2)}) collective-permute-start(bf16[384,2048]{1,0:T(8,128)(2,1)S(1)} %get-tuple-element.169.refs_0_), channel_id=1, source_target_pairs={{0,8},{8,0},{16,24},{24,16},{1,9},{9,1},{17,25},{25,17},{2,10},{10... | collective-permute-start | bytes 4718600 | tf_op jit(solution)/shard_map/ppermute | solution.py:24
  292.1 14.1 %collective-permute-start.23 = (bf16[192,2048]{1,0:T(8,128)(2,1)}, bf16[192,2048]{1,0:T(8,128)(2,1)}, u32[]{:S(2)}, u32[]{:S(2)}) collective-permute-start(bf16[192,2048]{1,0:T(8,128)(2,1)} %slice.348), channel_id=1, source_target_pairs={{0,8},{8,0},{16,24},{24,16},{1,9},{9,1},{17,25},{25,17},{2,10},{10... | collective-permute-start | bytes 2359304 | tf_op jit(solution)/shard_map/ppermute | solution.py:24
  293.3 13.5 %collective-permute-start.22 = (bf16[192,2048]{1,0:T(8,128)(2,1)}, bf16[192,2048]{1,0:T(8,128)(2,1)}, u32[]{:S(2)}, u32[]{:S(2)}) collective-permute-start(bf16[192,2048]{1,0:T(8,128)(2,1)} %slice.347), channel_id=1, source_target_pairs={{0,16},{8,24},{16,0},{24,8},{1,17},{9,25},{17,1},{25,9},{2,18},{10... | collective-permute-start | bytes 2359304 | tf_op jit(solution)/shard_map/ppermute | solution.py:24
  331.4 47.9 %collective-permute-start.28 = (bf16[1536,512]{1,0:T(8,128)(2,1)}, bf16[1536,512]{1,0:T(8,128)(2,1)}, u32[]{:S(2)}, u32[]{:S(2)}) collective-permute-start(bf16[1536,512]{1,0:T(8,128)(2,1)} %get-tuple-element.191.refs_5_), channel_id=1, source_target_pairs={{0,16},{8,24},{16,0},{24,8},{1,17},{9,25},{17,1},{25,9},{2,18},{10... | collective-permute-start | bytes 4718600 | tf_op jit(solution)/shard_map/ppermute | solution.py:24
  332.7 46.6 %collective-permute-start.27 = (bf16[1536,512]{1,0:T(8,128)(2,1)}, bf16[1536,512]{1,0:T(8,128)(2,1)}, u32[]{:S(2)}, u32[]{:S(2)}) collective-permute-start(bf16[1536,512]{1,0:T(8,128)(2,1)} %get-tuple-element.191.refs_5_), channel_id=1, source_target_pairs={{0,8},{8,0},{16,24},{24,16},{1,9},{9,1},{17,25},{25,17},{2,10},{10... | collective-permute-start | bytes 4718600 | tf_op jit(solution)/shard_map/ppermute | solution.py:24
  363.3 15.7 %collective-permute-start.31 = (bf16[768,512]{1,0:T(8,128)(2,1)S(1)}, bf16[768,512]{1,0:T(8,128)(2,1)S(1)}, u32[]{:S(2)}, u32[]{:S(2)}) collective-permute-start(bf16[768,512]{1,0:T(8,128)(2,1)S(1)} %get-tuple-element.307), channel_id=1, source_target_pairs={{0,8},{8,0},{16,24},{24,16},{1,9},{9,1},{17,25},{25,17},{2,10},{10... | collective-permute-start | bytes 2359304 | tf_op jit(solution)/shard_map/ppermute | solution.py:24
  363.9 34.9 %collective-permute-start.29 = (bf16[768,512]{1,0:T(8,128)(2,1)S(1)}, bf16[768,512]{1,0:T(8,128)(2,1)S(1)}, u32[]{:S(2)}, u32[]{:S(2)}) collective-permute-start(bf16[768,512]{1,0:T(8,128)(2,1)S(1)} %get-tuple-element.308), channel_id=1, source_target_pairs={{0,16},{8,24},{16,0},{24,8},{1,17},{9,25},{17,1},{25,9},{2,18},{10... | collective-permute-start | bytes 2359304 | tf_op jit(solution)/shard_map/ppermute | solution.py:24
  381.6 18.6 %collective-permute-start.34 = (bf16[768,512]{1,0:T(8,128)(2,1)S(1)}, bf16[768,512]{1,0:T(8,128)(2,1)S(1)}, u32[]{:S(2)}, u32[]{:S(2)}) collective-permute-start(bf16[768,512]{1,0:T(8,128)(2,1)S(1)} %slice.366), channel_id=1, source_target_pairs={{0,8},{8,0},{16,24},{24,16},{1,9},{9,1},{17,25},{25,17},{2,10},{10... | collective-permute-start | bytes 2359304 | tf_op jit(solution)/shard_map/ppermute | solution.py:24
  383.1 17.2 %collective-permute-start.33 = (bf16[768,512]{1,0:T(8,128)(2,1)S(1)}, bf16[768,512]{1,0:T(8,128)(2,1)S(1)}, u32[]{:S(2)}, u32[]{:S(2)}) collective-permute-start(bf16[768,512]{1,0:T(8,128)(2,1)S(1)} %slice.365), channel_id=1, source_target_pairs={{0,16},{8,24},{16,0},{24,8},{1,17},{9,25},{17,1},{25,9},{2,18},{10... | collective-permute-start | bytes 2359304 | tf_op jit(solution)/shard_map/ppermute | solution.py:24
  427.2 196.2 %reduce-scatter.9.cloned.1.call-start = ((), (), s32[]{:S(2)}) async-start(), calls=%async_computation.12 | async-start | bytes 8257536 | tf_op jit(solution)/shard_map/reduce_scatter | solution.py:765
  428.6 31.2 %collective-permute-start.32 = (bf16[1536,512]{1,0:T(8,128)(2,1)S(1)}, bf16[1536,512]{1,0:T(8,128)(2,1)S(1)}, u32[]{:S(2)}, u32[]{:S(2)}) collective-permute-start(bf16[1536,512]{1,0:T(8,128)(2,1)S(1)} %copy-done.70), channel_id=1, source_target_pairs={{0,16},{8,24},{16,0},{24,8},{1,17},{9,25},{17,1},{25,9},{2,18},{10... | collective-permute-start | bytes 4718600 | tf_op jit(solution)/shard_map/ppermute | solution.py:24
  429.5 31.5 %collective-permute-start.30 = (bf16[1536,512]{1,0:T(8,128)(2,1)}, bf16[1536,512]{1,0:T(8,128)(2,1)S(1)}, u32[]{:S(2)}, u32[]{:S(2)}) collective-permute-start(bf16[1536,512]{1,0:T(8,128)(2,1)} %pad_maximum_fusion.4), channel_id=1, source_target_pairs={{0,8},{8,0},{16,24},{24,16},{1,9},{9,1},{17,25},{25,17},{2,10},{10... | collective-permute-start | bytes 4718600 | tf_op jit(solution)/shard_map/ppermute | solution.py:24
  478.4 17.2 %collective-permute-start.36 = (bf16[192,2048]{1,0:T(8,128)(2,1)S(1)}, bf16[192,2048]{1,0:T(8,128)(2,1)S(1)}, u32[]{:S(2)}, u32[]{:S(2)}) collective-permute-start(bf16[192,2048]{1,0:T(8,128)(2,1)S(1)} %get-tuple-element.305), channel_id=1, source_target_pairs={{0,16},{8,24},{16,0},{24,8},{1,17},{9,25},{17,1},{25,9},{2,18},{10... | collective-permute-start | bytes 2359304 | tf_op jit(solution)/shard_map/ppermute | solution.py:24
  479.2 16.4 %collective-permute-start.35 = (bf16[192,2048]{1,0:T(8,128)(2,1)S(1)}, bf16[192,2048]{1,0:T(8,128)(2,1)S(1)}, u32[]{:S(2)}, u32[]{:S(2)}) collective-permute-start(bf16[192,2048]{1,0:T(8,128)(2,1)S(1)} %get-tuple-element.306), channel_id=1, source_target_pairs={{0,8},{8,0},{16,24},{24,16},{1,9},{9,1},{17,25},{25,17},{2,10},{10... | collective-permute-start | bytes 2359304 | tf_op jit(solution)/shard_map/ppermute | solution.py:24
  514.9 163.4 %reduce-scatter.11.cloned.1.call-start = ((), (), s32[]{:S(2)}) async-start(), calls=%async_computation.13 | async-start | bytes 2359296 | tf_op jit(solution)/shard_map/reduce_scatter | solution.py:765
  514.9 30.5 %collective-permute-start.37 = (bf16[384,2048]{1,0:T(8,128)(2,1)}, bf16[384,2048]{1,0:T(8,128)(2,1)}, u32[]{:S(2)}, u32[]{:S(2)}) collective-permute-start(bf16[384,2048]{1,0:T(8,128)(2,1)} %pad_maximum_fusion.7), channel_id=1, source_target_pairs={{0,8},{8,0},{16,24},{24,16},{1,9},{9,1},{17,25},{25,17},{2,10},{10... | collective-permute-start | bytes 4718600 | tf_op jit(solution)/shard_map/ppermute | solution.py:24
  516.8 30.1 %collective-permute-start.38 = (bf16[384,2048]{1,0:T(8,128)(2,1)}, bf16[384,2048]{1,0:T(8,128)(2,1)}, u32[]{:S(2)}, u32[]{:S(2)}) collective-permute-start(bf16[384,2048]{1,0:T(8,128)(2,1)} %pad_maximum_fusion.8), channel_id=1, source_target_pairs={{0,16},{8,24},{16,0},{24,8},{1,17},{9,25},{17,1},{25,9},{2,18},{10... | collective-permute-start | bytes 4718600 | tf_op jit(solution)/shard_map/ppermute | solution.py:24
  556.4 32.3 %collective-permute-start.40 = (bf16[384,2048]{1,0:T(8,128)(2,1)S(1)}, bf16[384,2048]{1,0:T(8,128)(2,1)S(1)}, u32[]{:S(2)}, u32[]{:S(2)}) collective-permute-start(bf16[384,2048]{1,0:T(8,128)(2,1)S(1)} %get-tuple-element.222), channel_id=1, source_target_pairs={{0,16},{8,24},{16,0},{24,8},{1,17},{9,25},{17,1},{25,9},{2,18},{10... | collective-permute-start | bytes 4718600 | tf_op jit(solution)/shard_map/ppermute | solution.py:24
  557.5 32.8 %collective-permute-start.39 = (bf16[384,2048]{1,0:T(8,128)(2,1)S(1)}, bf16[384,2048]{1,0:T(8,128)(2,1)S(1)}, u32[]{:S(2)}, u32[]{:S(2)}) collective-permute-start(bf16[384,2048]{1,0:T(8,128)(2,1)S(1)} %get-tuple-element.222), channel_id=1, source_target_pairs={{0,8},{8,0},{16,24},{24,16},{1,9},{9,1},{17,25},{25,17},{2,10},{10... | collective-permute-start | bytes 4718600 | tf_op jit(solution)/shard_map/ppermute | solution.py:24
  591.4 12.0 %collective-permute-start.42 = (bf16[192,2048]{1,0:T(8,128)(2,1)S(1)}, bf16[192,2048]{1,0:T(8,128)(2,1)S(1)}, u32[]{:S(2)}, u32[]{:S(2)}) collective-permute-start(bf16[192,2048]{1,0:T(8,128)(2,1)S(1)} %slice.374), channel_id=1, source_target_pairs={{0,8},{8,0},{16,24},{24,16},{1,9},{9,1},{17,25},{25,17},{2,10},{10... | collective-permute-start | bytes 2359304 | tf_op jit(solution)/shard_map/ppermute | solution.py:24
  591.7 12.1 %collective-permute-start.41 = (bf16[192,2048]{1,0:T(8,128)(2,1)S(1)}, bf16[192,2048]{1,0:T(8,128)(2,1)}, u32[]{:S(2)}, u32[]{:S(2)}) collective-permute-start(bf16[192,2048]{1,0:T(8,128)(2,1)S(1)} %slice.373), channel_id=1, source_target_pairs={{0,16},{8,24},{16,0},{24,8},{1,17},{9,25},{17,1},{25,9},{2,18},{10... | collective-permute-start | bytes 2359304 | tf_op jit(solution)/shard_map/ppermute | solution.py:24
  614.5 167.3 %reduce-scatter.17.cloned.1.call-start = ((), (), s32[]{:S(2)}) async-start(), calls=%async_computation.16 | async-start | bytes 2359296 | tf_op jit(solution)/shard_map/reduce_scatter | solution.py:765
  615.3 200.5 %reduce-scatter.15.cloned.1.call-start = ((), (), s32[]{:S(2)}) async-start(), calls=%async_computation.15 | async-start | bytes 4718592 | tf_op jit(solution)/shard_map/reduce_scatter | solution.py:765
  677.5 149.8 %reduce-scatter.13.cloned.1.call-start = ((), (), s32[]{:S(2)}) async-start(), calls=%async_computation.14 | async-start | bytes 4718592 | tf_op jit(solution)/shard_map/reduce_scatter | solution.py:765
  688.5 20.3 %collective-permute-start.44 = (bf16[192,2048]{1,0:T(8,128)(2,1)S(1)}, bf16[192,2048]{1,0:T(8,128)(2,1)S(1)}, u32[]{:S(2)}, u32[]{:S(2)}) collective-permute-start(bf16[192,2048]{1,0:T(8,128)(2,1)S(1)} %get-tuple-element.303), channel_id=1, source_target_pairs={{0,16},{8,24},{16,0},{24,8},{1,17},{9,25},{17,1},{25,9},{2,18},{10... | collective-permute-start | bytes 2359304 | tf_op jit(solution)/shard_map/ppermute | solution.py:24
  689.9 18.9 %collective-permute-start.43 = (bf16[192,2048]{1,0:T(8,128)(2,1)S(1)}, bf16[192,2048]{1,0:T(8,128)(2,1)S(1)}, u32[]{:S(2)}, u32[]{:S(2)}) collective-permute-start(bf16[192,2048]{1,0:T(8,128)(2,1)S(1)} %get-tuple-element.304), channel_id=1, source_target_pairs={{0,8},{8,0},{16,24},{24,16},{1,9},{9,1},{17,25},{25,17},{2,10},{10... | collective-permute-start | bytes 2359304 | tf_op jit(solution)/shard_map/ppermute | solution.py:24
  726.1 25.4 %collective-permute-start.45 = (bf16[384,2048]{1,0:T(8,128)(2,1)}, bf16[384,2048]{1,0:T(8,128)(2,1)}, u32[]{:S(2)}, u32[]{:S(2)}) collective-permute-start(bf16[384,2048]{1,0:T(8,128)(2,1)} %pad_maximum_fusion.9), channel_id=1, source_target_pairs={{0,8},{8,0},{16,24},{24,16},{1,9},{9,1},{17,25},{25,17},{2,10},{10... | collective-permute-start | bytes 4718600 | tf_op jit(solution)/shard_map/ppermute | solution.py:24
  726.2 26.4 %collective-permute-start.46 = (bf16[384,2048]{1,0:T(8,128)(2,1)}, bf16[384,2048]{1,0:T(8,128)(2,1)}, u32[]{:S(2)}, u32[]{:S(2)}) collective-permute-start(bf16[384,2048]{1,0:T(8,128)(2,1)} %pad_maximum_fusion.10), channel_id=1, source_target_pairs={{0,16},{8,24},{16,0},{24,8},{1,17},{9,25},{17,1},{25,9},{2,18},{10... | collective-permute-start | bytes 4718600 | tf_op jit(solution)/shard_map/ppermute | solution.py:24
  762.1 12.7 %collective-permute-start.62 = (f32[16,14,64]{2,1,0:T(8,128)S(1)}, f32[16,14,64]{2,1,0:T(8,128)S(1)}, u32[]{:S(2)}, u32[]{:S(2)}) collective-permute-start(f32[16,14,64]{2,1,0:T(8,128)S(1)} %bitcast.109), channel_id=1, source_target_pairs={{0,4},{1,5},{2,6},{3,7},{4,0},{5,1},{6,2},{7,3},{8,12},{9,13},{10,... | collective-permute-start | bytes 172040 | tf_op jit(solution)/shard_map/ppermute | solution.py:24
  788.5 25.8 %collective-permute-start.58 = (bf16[64,1792]{1,0:T(8,128)(2,1)S(1)}, bf16[64,1792]{1,0:T(8,128)(2,1)S(1)}, u32[]{:S(2)}, u32[]{:S(2)}) collective-permute-start(bf16[64,1792]{1,0:T(8,128)(2,1)S(1)} %get-tuple-element.311), channel_id=1, source_target_pairs={{0,24},{8,16},{16,8},{24,0},{1,25},{9,17},{17,9},{25,1},{2,26},{10... | collective-permute-start | bytes 688136 | tf_op jit(solution)/shard_map/ppermute | solution.py:24
  789.7 39.7 %collective-permute-start.49 = (bf16[384,512]{1,0:T(8,128)(2,1)}, bf16[384,512]{1,0:T(8,128)(2,1)}, u32[]{:S(2)}, u32[]{:S(2)}) collective-permute-start(bf16[384,512]{1,0:T(8,128)(2,1)} %get-tuple-element.299), channel_id=1, source_target_pairs={{0,24},{8,16},{16,8},{24,0},{1,25},{9,17},{17,9},{25,1},{2,26},{10... | collective-permute-start | bytes 1179656 | tf_op jit(solution)/shard_map/ppermute | solution.py:24
  792.0 38.4 %collective-permute-start.48 = (bf16[384,512]{1,0:T(8,128)(2,1)}, bf16[384,512]{1,0:T(8,128)(2,1)}, u32[]{:S(2)}, u32[]{:S(2)}) collective-permute-start(bf16[384,512]{1,0:T(8,128)(2,1)} %get-tuple-element.300), channel_id=1, source_target_pairs={{0,16},{8,24},{16,0},{24,8},{1,17},{9,25},{17,1},{25,9},{2,18},{10... | collective-permute-start | bytes 1179656 | tf_op jit(solution)/shard_map/ppermute | solution.py:24
  793.5 38.5 %collective-permute-start.47 = (bf16[384,512]{1,0:T(8,128)(2,1)}, bf16[384,512]{1,0:T(8,128)(2,1)}, u32[]{:S(2)}, u32[]{:S(2)}) collective-permute-start(bf16[384,512]{1,0:T(8,128)(2,1)} %get-tuple-element.301), channel_id=1, source_target_pairs={{0,8},{8,0},{16,24},{24,16},{1,9},{9,1},{17,25},{25,17},{2,10},{10... | collective-permute-start | bytes 1179656 | tf_op jit(solution)/shard_map/ppermute | solution.py:24
  795.1 18.0 %collective-permute-start.66 = (f32[1,14,64]{2,1,0:T(8,128)S(1)}, f32[1,14,64]{2,1,0:T(8,128)S(1)}, u32[]{:S(2)}, u32[]{:S(2)}) collective-permute-start(f32[1,14,64]{2,1,0:T(8,128)S(1)} %slice_select_fusion.5), channel_id=1, source_target_pairs={{0,8},{8,0},{16,24},{24,16},{1,9},{9,1},{17,25},{25,17},{2,10},{10... | collective-permute-start | bytes 10760 | tf_op jit(solution)/shard_map/ppermute | solution.py:24
  815.0 13.5 %collective-permute-start.56 = (bf16[64,1792]{1,0:T(8,128)(2,1)}, bf16[64,1792]{1,0:T(8,128)(2,1)}, u32[]{:S(2)}, u32[]{:S(2)}) collective-permute-start(bf16[64,1792]{1,0:T(8,128)(2,1)} %get-tuple-element.313), channel_id=1, source_target_pairs={{0,8},{8,0},{16,24},{24,16},{1,9},{9,1},{17,25},{25,17},{2,10},{10... | collective-permute-start | bytes 688136 | tf_op jit(solution)/shard_map/ppermute | solution.py:24
  819.8 13.1 %collective-permute-start.55 = (bf16[64,1024]{1,0:T(8,128)(2,1)}, bf16[64,1024]{1,0:T(8,128)(2,1)}, u32[]{:S(2)}, u32[]{:S(2)}) collective-permute-start(bf16[64,1024]{1,0:T(8,128)(2,1)} %get-tuple-element.315), channel_id=1, source_target_pairs={{0,24},{8,16},{16,8},{24,0},{1,25},{9,17},{17,9},{25,1},{2,26},{10... | collective-permute-start | bytes 393224 | tf_op jit(solution)/shard_map/ppermute | solution.py:24
  828.4 14.7 %collective-permute-start.54 = (bf16[64,1024]{1,0:T(8,128)(2,1)}, bf16[64,1024]{1,0:T(8,128)(2,1)S(1)}, u32[]{:S(2)}, u32[]{:S(2)}) collective-permute-start(bf16[64,1024]{1,0:T(8,128)(2,1)} %get-tuple-element.316), channel_id=1, source_target_pairs={{0,16},{8,24},{16,0},{24,8},{1,17},{9,25},{17,1},{25,9},{2,18},{10... | collective-permute-start | bytes 393224 | tf_op jit(solution)/shard_map/ppermute | solution.py:24
  829.4 13.8 %collective-permute-start.53 = (bf16[64,1024]{1,0:T(8,128)(2,1)}, bf16[64,1024]{1,0:T(8,128)(2,1)S(1)}, u32[]{:S(2)}, u32[]{:S(2)}) collective-permute-start(bf16[64,1024]{1,0:T(8,128)(2,1)} %get-tuple-element.317), channel_id=1, source_target_pairs={{0,8},{8,0},{16,24},{24,16},{1,9},{9,1},{17,25},{25,17},{2,10},{10... | collective-permute-start | bytes 393224 | tf_op jit(solution)/shard_map/ppermute | solution.py:24
  830.5 14.6 %collective-permute-start.52 = (bf16[64,1024]{1,0:T(8,128)(2,1)S(1)}, bf16[64,1024]{1,0:T(8,128)(2,1)S(1)}, u32[]{:S(2)}, u32[]{:S(2)}) collective-permute-start(bf16[64,1024]{1,0:T(8,128)(2,1)S(1)} %get-tuple-element.319), channel_id=1, source_target_pairs={{0,24},{8,16},{16,8},{24,0},{1,25},{9,17},{17,9},{25,1},{2,26},{10... | collective-permute-start | bytes 393224 | tf_op jit(solution)/shard_map/ppermute | solution.py:24
  832.0 13.1 %collective-permute-start.51 = (bf16[64,1024]{1,0:T(8,128)(2,1)S(1)}, bf16[64,1024]{1,0:T(8,128)(2,1)S(1)}, u32[]{:S(2)}, u32[]{:S(2)}) collective-permute-start(bf16[64,1024]{1,0:T(8,128)(2,1)S(1)} %get-tuple-element.320), channel_id=1, source_target_pairs={{0,16},{8,24},{16,0},{24,8},{1,17},{9,25},{17,1},{25,9},{2,18},{10... | collective-permute-start | bytes 393224 | tf_op jit(solution)/shard_map/ppermute | solution.py:24
  832.9 12.2 %collective-permute-start.50 = (bf16[64,1024]{1,0:T(8,128)(2,1)S(1)}, bf16[64,1024]{1,0:T(8,128)(2,1)S(1)}, u32[]{:S(2)}, u32[]{:S(2)}) collective-permute-start(bf16[64,1024]{1,0:T(8,128)(2,1)S(1)} %get-tuple-element.321), channel_id=1, source_target_pairs={{0,8},{8,0},{16,24},{24,16},{1,9},{9,1},{17,25},{25,17},{2,10},{10... | collective-permute-start | bytes 393224 | tf_op jit(solution)/shard_map/ppermute | solution.py:24
  (118 other events, 1000.9 us)
Sparse Core Ops, SparseCore 0:
  34.1 65.4 all-gather.7
  101.8 29.0 all-gather.5
  132.5 28.5 all-gather.9
  162.6 90.2 all-gather.11
  254.4 71.8 all-gather.13
  427.3 79.7 reduce-scatter.6
  515.0 81.0 reduce-scatter.8
  614.7 37.3 reduce-scatter.10
  654.3 34.6 reduce-scatter.16
  691.1 48.6 reduce-scatter.14
  742.1 52.3 reduce-scatter.12

commit v8 on v7

--- a/solution.py
+++ b/solution.py
@@ -48,26 +48,36 @@
 def scatter_start(parts):
     if lax.axis_size("seq") != 4:
         return ()
-    half = parts[3].shape[0] // 2
-    return swap(parts[3][:half], "seq", 1), swap(parts[3][half:], "seq", 2)
-
-
-def scatter_relay(parts, started):
+    low, high = parts[3:] if len(parts) == 5 else blocks_of(parts[3], 2)
+    return swap(low, "seq", 1), swap(high, "seq", 2)
+
+
+def relay_body(here, one_ref, two_ref, low_ref, high_ref, one_out, two_out):
+    one, two = one_ref[...], two_ref[...]
+    first = pl.program_id(0) == 0
+    low, high = low_ref[...].astype(F32), high_ref[...].astype(F32)
+    one_out[...] = jnp.where(first, one, (one.astype(F32) + high).astype(BF))
+    two_out[...] = jnp.where(first, (two.astype(F32) + low).astype(BF), two)
+
+
+def scatter_relay(parts, started, here):
     if lax.axis_size("seq") != 4:
         return parts[1:]
-    (_, one, two, _), (low, high) = parts, started
-    half = low.shape[0]
-    two = jnp.concatenate([(two[:half].astype(F32) + low.astype(F32)).astype(BF), two[half:]], axis=0)
-    one = jnp.concatenate([one[:half], (one[half:].astype(F32) + high.astype(F32)).astype(BF)], axis=0)
-    return [one, two]
+    (_, one, two, *_), (low, high) = parts, started
+    (rows, width), half = one.shape, block(low.shape, lambda i, h: (i, 0))
+    return kernel(
+        relay_body, "relay", (2,), here,
+        [(one, half), (two, half), (low, fixed(low.shape)), (high, fixed(low.shape))],
+        [((rows, width), BF, half)] * 2,
+    )
 
 
 def scatter_end(own, relayed):
     return [own] + [swap(part, "seq", j + 1) for j, part in enumerate(relayed)]
 
 
-def scatter_seq(parts):
-    return scatter_end(parts[0], scatter_relay(parts, scatter_start(parts)))
+def scatter_seq(parts, here):
+    return scatter_end(parts[0], scatter_relay(parts, scatter_start(parts), here))
 
 
 def trade_seq(parts):
@@ -167,38 +177,46 @@
 
 
 def cut_body(count, parts, here, *refs):
-    ins, outs = refs[:count], refs[count:]
+    ins, beside, outs = refs[:count], refs[count], refs[count + 1 :]
+    rows = ins[0].shape[0]
+    for j in range(parts):
+        outs[j][rows:, :] = jnp.zeros_like(outs[j][rows:, :])
+        outs[j][rows:, : beside.shape[1]] = beside[...]
     at = 0
     for ref in ins:
         width = ref.shape[1] // parts
         for j in range(parts):
-            outs[j][:, at : at + width] = ref[:, placed(here[0] ^ j, width)]
+            outs[j][:rows, at : at + width] = ref[:, placed(here[0] ^ j, width)]
         at += width
 
 
-def cut_columns(weights, here, parts):
-    rows, width = weights[0].shape[0], sum(w.shape[1] for w in weights) // parts
+def cut_columns(weights, beside, here, parts):
+    rows, width = weights[0].shape[0] + beside.shape[0], sum(w.shape[1] for w in weights) // parts
     return kernel(
         partial(cut_body, len(weights), parts), "cut_columns", (1,), here,
-        [(w, fixed(w.shape)) for w in weights],
+        [(w, fixed(w.shape)) for w in [*weights, beside]],
         [((rows, width), BF, fixed((rows, width)))] * parts,
     )
 
 
 def stack_body(parts, here, *refs):
     start = 0
-    for out in refs[parts:]:
+    outs, beside = refs[parts:-1], refs[-1]
+    for out in outs:
         for j in range(parts):
-            out[here[0] ^ j] = refs[j][:, start : start + out.shape[2]]
+            out[here[0] ^ j] = refs[j][: out.shape[1], start : start + out.shape[2]]
         start += out.shape[2]
-
-
-def stack_rows(pieces, widths, here):
-    parts, rows = len(pieces), pieces[0].shape[0]
+    for j in range(parts):
+        beside[here[0] ^ j] = refs[j][out.shape[1] :, : beside.shape[2]]
+
+
+def stack_rows(pieces, widths, beside, here):
+    parts, rows = len(pieces), pieces[0].shape[0] - beside.shape[0]
+    shapes = [(parts, rows, width) for width in widths] + [(parts,) + beside.shape]
     return kernel(
         partial(stack_body, parts), "stack_rows", (1,), here,
         [(p, fixed(p.shape)) for p in pieces],
-        [((parts, rows, width), BF, fixed((parts, rows, width))) for width in widths],
+        [(shape, BF, fixed(shape)) for shape in shapes],
     )
 
 
@@ -326,10 +344,10 @@
     )
 
 
-def mixes_back_body(which, first, seq, here, *refs):
+def mixes_back_body(which, first, seq, outs, here, *refs):
     count = len(which)
     grads, nexts, weights = refs[:count], refs[count : 2 * count], refs[2 * count : 3 * count]
-    step_ref, marks_ref, next_marks_ref, vec_ref, out_ref, sums_ref = refs[3 * count :]
+    step_ref, marks_ref, next_marks_ref, vec_ref, *out_refs, sums_ref = refs[3 * count :]
 
     @pl.when(pl.program_id(1) == 0)
     def _():
@@ -351,13 +369,25 @@
     keep = jnp.concatenate([marks_ref[:, 3:4], jnp.where(inside, next_marks_ref[:, 3:4], 0.0)], axis=0)
     kept = (total - straight) * keep
     up = pltpu.roll(kept, kept.shape[0] - 1, 0)
-    out_ref[...] = (straight[:rows] + up[:rows]).astype(BF)
+    result = (straight[:rows] + up[:rows]).astype(BF)
+    if len(out_refs) == 1:
+        out_refs[0][...] = result
+        return
+    if outs == 1:
+        out_refs[0][...] = result[: rows // 2]
+        out_refs[1][...] = result[rows // 2 :]
+        return
+    for k, out_ref in enumerate(out_refs):
+
+        @pl.when(pl.program_id(1) == k)
+        def _(out_ref=out_ref):
+            out_ref[...] = result
 
 
 EXTRA = 16
 
 
-def mixes_back(terms, step, marks, vec, here, seq, first, count):
+def mixes_back(terms, step, marks, vec, here, seq, first, count, halves=False):
     rows, width = step.shape
     tile, columns = rows // seq, min(512, width)
     extras = tile // EXTRA
@@ -377,32 +407,32 @@
         (marks, block((EXTRA, PAIR), lambda c, i, h: (following(i, h) * extras, 0))),
         (vec, block((8, columns), lambda c, i, h: (0, c))),
     ]
-    return kernel(
-        partial(mixes_back_body, [t[0] for t in terms], first, seq), "mixes_back", (width // columns, count), here, ins,
-        [
-            ((count * tile, width), BF, block((tile, columns), lambda c, i, h: (i, c))),
-            ((8, width), F32, block((8, columns), lambda c, i, h: (0, c))),
-        ],
-    )
+    size = tile // 2 if halves else tile
+    *parts, sums = kernel(
+        partial(mixes_back_body, [t[0] for t in terms], first, seq, count), "mixes_back", (width // columns, count), here, ins,
+        [((size, width), BF, block((size, columns), lambda c, i, h: (0, c)))] * (2 if halves else count)
+        + [((8, width), F32, block((8, columns), lambda c, i, h: (0, c)))],
+    )
+    return parts, sums
 
 
 def mixes_back_scatter(terms, step, marks, vec, here, seq, beside):
     if seq != 4:
-        grad, sums = mixes_back(terms, step, marks, vec, here, seq, 0, seq)
-        return after(scatter_seq(blocks_of(grad, seq)), beside(grad)), sums
+        parts, sums = mixes_back(terms, step, marks, vec, here, seq, 0, seq)
+        return after(scatter_seq(parts, here), beside(parts)), sums
 
     def call(first, count, *before):
         ordered = after([t[1] for t in terms], *before)
         return mixes_back(
-            [(t[0], g) + t[2:] for t, g in zip(terms, ordered)], step, marks, vec, here, seq, first, count
+            [(t[0], g) + t[2:] for t, g in zip(terms, ordered)], step, marks, vec, here, seq, first, count, first == 3
         )
 
     far, sums_far = call(3, 1)
     near, sums_near = call(1, 2, far)
-    parts = [None] + blocks_of(near, 2) + [far]
+    parts = [None, *near, *far]
     started = after(scatter_start(parts), near)
-    relayed = scatter_relay(parts, started)
-    own, sums_own = call(0, 1, near, relayed)
+    relayed = scatter_relay(parts, started, here)
+    (own,), sums_own = call(0, 1, near, relayed)
     return after(scatter_end(own, relayed), beside(relayed)), sums_far + sums_near + sums_own
 
 
@@ -754,9 +784,12 @@
     groups = (seq, dp)
     within = groups if unit == HEAD else None
 
+    vectors_b = jnp.pad(vectors, ((0, 16 - vectors.shape[0]), (0, 0)))
+
     def stacked_columns(weights, widths, beside=()):
-        stacked = stack_rows(after(trade_seq(cut_columns(weights, here, seq)), beside), widths, here)
-        return [w.reshape(-1, w.shape[-1]) for w in stacked]
+        cut = cut_columns(weights, vectors_b, here, seq)
+        *stacked, last = stack_rows(after(trade_seq(cut), beside), widths, vectors_b, here)
+        return [w.reshape(-1, w.shape[-1]) for w in stacked] + [last], cut
 
     def gather_dp(rows):
         return lax.all_gather(rows, "dp", axis=0, tiled=True)
@@ -764,10 +797,12 @@
     def scatter_dp(grad):
         return lax.psum_scatter(grad, "dp", scatter_dimension=0, tiled=True)
 
+    def owners_parts(summed):
+        rows = summed.shape[0] // seq
+        return trade_seq([lax.dynamic_slice_in_dim(summed, (place ^ j) * rows, rows, 0) for j in range(seq)])
+
     def owners_rows(summed, widths):
-        rows = summed.shape[0] // seq
-        parts = [lax.dynamic_slice_in_dim(summed, (place ^ j) * rows, rows, 0) for j in range(seq)]
-        return join_columns(trade_seq(parts), widths, here)
+        return join_columns(owners_parts(summed), widths, here)
 
     def turn_pieces(pieces):
         if within is not None:
@@ -777,11 +812,12 @@
     positions = jnp.arange(length, dtype=jnp.int32)
     piece, first_flags = segment_of(seq_lengths[0], positions)
 
-    vec_seq = gather_small(vectors[None], "seq")
-    tokens_held = held_back(inputs_b, here, vec_seq)
-    columns_in, columns_g = stacked_columns([w_receptance, w_key, w_value, w_gate], [3 * part, part], tokens_held)
+    (columns_in, columns_g, vec_seq), cut = stacked_columns(
+        [w_receptance, w_key, w_value, w_gate], [3 * part, part]
+    )
+    tokens_held = held_back(inputs_b, here, *cut)
     full_in = gather_dp(columns_in)
-    vec_parts = gather_small(vec_seq[None], "dp").astype(F32)
+    vec_parts = gather_small(vec_seq[None, :, : vectors.shape[0]], "dp").astype(F32)
     vec = vec_parts.transpose(2, 1, 0, 3).reshape(-1, width)
     turned = vec_parts.transpose(2, 0, 1, 3).reshape(-1, width)
     vec_own = lax.dynamic_slice_in_dim(vec, place * part, part, 1)
@@ -803,7 +839,7 @@
         for i, m in enumerate((mix_r, mix_k, mix_v))
     )
     projected = (recept, keyed, valued)
-    (columns_c,) = stacked_columns(after([ffn_key, ffn_receptance], mix_r), [hidden_width + part], projected)
+    (columns_c, _), _ = stacked_columns(after([ffn_key, ffn_receptance], mix_r), [hidden_width + part], projected)
     full_c = gather_dp(columns_c)
     full_ck, full_cr = full_c[:, :hidden_width], full_c[:, hidden_width:]
     full_cv = gather_dp(after(ffn_value, columns_c))
@@ -811,7 +847,7 @@
     grad_all = gather_seq(after(grad_b, mix_r), wkv)
     gate_pre, mixed = gated(mix_g, full_g, wkv, tables[5], here, seq)
     attn = [dot(rows, own_o, NN).astype(BF) for rows in blocks_of(after(mixed, grad_all[3:]), seq)]
-    after_mix, normed_two = after_norm(inputs_b, scatter_seq(attn), rows_of(vec, 10, 11), here)
+    after_mix, normed_two = after_norm(inputs_b, scatter_seq(attn, here), rows_of(vec, 10, 11), here)
 
     mix_k2, mix_r2, step_two = mixes(
         turn_pieces(gather_seq(normed_two)), marks, rows_of(turned, 10, 11, 12, 13), 2, False, within, here, tile,
@@ -827,7 +863,7 @@
     later = after(hidden, opened[1:3])
     value_parts = [columns_product(later if j < 2 else hidden, full_cv, part, j, here, seq) for j in reversed(range(seq))]
     value_parts = value_parts[::-1]
-    value_relayed = scatter_relay(value_parts, scatter_start(value_parts))
+    value_relayed = scatter_relay(value_parts, scatter_start(value_parts), here)
     d_value = spread_columns(
         grad_all, by_block(after(opened, value_parts, value_relayed)), here, True, True, tile, own_rows // tile
     )
@@ -864,16 +900,20 @@
     d_recept, d_keyed, d_valued, d_gate, sums = wkv_backward(
         recept, keyed, valued, gate_pre, wkv, d_mixed, states, tables, here, per
     )
-    grads_vg = [dot(mix_v, d_valued, TN).astype(BF), dot(mix_g, d_gate, TN).astype(BF)]
+    channel = after(trade_seq(blocks_of(after(channel, d_mixed), seq)), d_recept)
+    grads_vg = [
+        dot(after(m, channel), d, TN).astype(BF) for m, d in ((mix_v, d_valued), (mix_g, d_gate))
+    ]
     summed_vg = scatter_dp(jnp.concatenate(grads_vg, axis=1))
-    grads_rk, sum_cv = [], []
+    grads_rk, others = [], []
 
     def beside(relayed):
         grads_rk.extend(
             dot(after(m, relayed), d, TN).astype(BF) for m, d in ((mix_r, d_recept), (mix_k, d_keyed))
         )
-        sum_cv.append(after(summed_cv, relayed).astype(F32))
-        return grads_rk, sum_cv
+        others.append(spread_columns([after_mix], after(channel, relayed), here, False, False, CHUNK, per))
+        others.append(after(summed_cv, relayed).astype(F32))
+        return grads_rk, others
 
     d_recept, d_keyed = after((d_recept, d_keyed), grads_vg, summed_o)
     terms, sums_one = mixes_back_scatter(
@@ -882,18 +922,15 @@
         step, marks, rows_of(turned, 2, 3, 4, 5), here, seq, beside,
     )
     summed_rk = scatter_dp(jnp.concatenate(grads_rk, axis=1))
-    channel = trade_seq(blocks_of(after(channel, terms), seq))
-    out_rows = spread_columns([after_mix], channel, here, False, False, CHUNK, per)
-    (sum_ck,) = owners_rows(after(summed_ck, terms), [ffn_key.shape[1]])
+    out_rows, sum_cv = others
     if within is None:
         terms = [outside(t, groups, unit, back=True) for t in terms]
     tokens_grad, _, norm_sums = norm_back(terms, inputs_b, d_after, rows_of(vec, 0), within, here)
 
-    (sum_cr,) = owners_rows(after(summed_cr, terms), [width])
-    (sum_cv,) = sum_cv
+    summed_c = jnp.concatenate(after([summed_ck, summed_cr], terms), axis=1)
+    sum_ck, sum_cr = owners_rows(summed_c, [ffn_key.shape[1], width])
     sum_o = summed_o.astype(F32)
     sum_v, sum_g = owners_rows(summed_vg, [width] * 2)
-    sum_r, sum_k = owners_rows(summed_rk, [width] * 2)
 
     def by_device(rows, turn):
         if turn:
@@ -910,6 +947,7 @@
         axis=2,
     )
     sum_vec = scatter_small(vector_rows.reshape((-1,) + vector_rows.shape[2:]))
+    sum_r, sum_k = owners_rows(after(summed_rk, sum_ck, sum_v, sum_vec), [width] * 2)
     return (
         out_rows[None], tokens_grad[None], sum_r, sum_k, sum_v, sum_g, sum_o,
         sum_ck, sum_cr, sum_cv, sum_vec,

time: 859 us -> 811 us (0.944)
  waiting for transfers between devices: 270 us -> 230 us
  other arithmetic: 26.3 us -> 12.9 us
    ppermute x67 -> x62, waiting for transfers between devices: 270 us -> 230 us  [swap(): return lax.ppermute(value, axis, [(i, i ^ distance) for i in range(size)])]
    concatenate x8 -> x0, other arithmetic: 10.3 us -> none  [the longest x4 5.16 us: scatter_relay(): jnp.concatenate([(two[:half].astype(F32) + low.astype(F32)).astype(BF), t...]
    pallas_call x30 -> x33, Pallas kernels: 230 us -> 238 us  [kernel(): pl.pallas_call(body, out_shape=[jax.ShapeDtypeStruct(shape, kind) for sha...]
    ppermute x67 -> x62, starting transfers between devices: 78 us -> 72.4 us  [swap(): return lax.ppermute(value, axis, [(i, i ^ distance) for i in range(size)])]
    unnamed x213 -> x214, local copies, waits for them, and re-layouts: 47.7 us -> 50.1 us
  transfers between devices with their start and end apart: 78 -> 73, of which waited for: 36 -> 38; matrix products, arithmetic and copies ran while one was open for 23% -> 22% of each run, Pallas kernels for 26% -> 28%
where the time goes in v8:
time: 811 us; the launch traced here: 806 us
  Pallas kernels  238 us (29%)
  waiting for transfers between devices  230 us (28%)
  matrix products  163 us (20%)
  starting transfers between devices  73.7 us (9%)
  local copies, waits for them, and re-layouts  71.7 us (9%)
  between operations  15.4 us (2%)
  other arithmetic  12.9 us (2%)
    pallas_call x33, Pallas kernels, kernel(): pl.pallas_call(body, out_shape=[jax.ShapeDtypeStruct(shape, kind) for sha...  238 us
    ppermute x62, waiting for transfers between devices, swap(): return lax.ppermute(value, axis, [(i, i ^ distance) for i in range(size)])  230 us
    dot_general x19, matrix products, dot(): return lax.dot_general(left, right, dims, preferred_element_type=F32)  163 us
    ppermute x62, starting transfers between devices, swap(): return lax.ppermute(value, axis, [(i, i ^ distance) for i in range(size)])  72.4 us
    unnamed x214, local copies, waits for them, and re-layouts  50.1 us
  transfers between devices with their start and end apart: 73, of which 38 were waited for; matrix products, arithmetic and copies ran while one was open for 22% of the time, Pallas kernels for 28%

profile of v8, /device:TPU:0, one launch (start us, length us, event | category | flops | bytes accessed | tf_op | source)
XLA Modules:
  0.0 805.6 jit_solution(9733419985804232621)
XLA Ops:
  11.9 3.0 collective-permute-start
  16.5 7.0 collective-permute-done.refs_1_
  23.5 7.7 collective-permute-done.1.refs_2_
  41.8 2.7 collective-permute-start.5
  44.9 8.5 %collective-permute-done.5 = bf16[4,4,14,64]{3,2,1,0:T(8,128)(2,1)S(1)} collective-permute-done((bf16[4,4,14,64]{3,2,1,0:T(8,128)(2,1)S(1)}, bf16[4,4,14,64]{3,2,1,0:T(8,128)(2,1)S(1)}, u32[]{:S(2)}, u32[]{:S(2)}) %collective-permute-start.5) | collective-permute-done | bytes 28704 | tf_op jit(solution)/shard_map/ppermute | solution.py:24
  55.7 13.1 %collective-permute-done.7.refs_2_ = bf16[384,2048]{1,0:T(8,128)(2,1)} collective-permute-done((bf16[384,2048]{1,0:T(8,128)(2,1)}, bf16[384,2048]{1,0:T(8,128)(2,1)}, u32[]{:S(2)}, u32[]{:S(2)}) %collective-permute-start.7) | collective-permute-done | bytes 1572896 | tf_op jit(solution)/shard_map/ppermute | solution.py:24
  74.6 14.1 %collective-permute-done.9.refs_4_ = bf16[192,2048]{1,0:T(8,128)(2,1)S(1)} collective-permute-done((bf16[192,2048]{1,0:T(8,128)(2,1)S(1)}, bf16[192,2048]{1,0:T(8,128)(2,1)S(1)}, u32[]{:S(2)}, u32[]{:S(2)}) %collective-permute-start.9) | collective-permute-done | bytes 786464 | tf_op jit(solution)/shard_map/ppermute | solution.py:24
  93.7 18.0 %mixes.2 = (bf16[1536,2048]{1,0:T(8,128)(2,1)}, bf16[1536,2048]{1,0:T(8,128)(2,1)}, bf16[1536,2048]{1,0:T(8,128)(2,1)}, bf16[1536,2048]{1,0:T(8,128)(2,1)}, bf16[1536,2048]{1,0:T(8,128)(2,1)}) custom-call(s32[1]{0:T(128)} %bitcast.here, bf16[384,2048]{1,0:T(8,128)(2,1)} %hold.1.refs_0_, bf16[384,2048]{1,0:T(8,128)(2,1)} %collective-permute-done.6.refs_1_, ...), custom_call_target="tpu_custom_call" | custom-call | tf_op jit(solution)/shard_map/mixes/pallas_call | solution.py:127
  117.7 8.2 %convolution_convert_fusion.11.r_ref = bf16[1536,512]{1,0:T(8,128)(2,1)} fusion(bf16[1536,2048]{1,0:T(8,128)(2,1)} %get-tuple-element.306, bf16[2048,1536]{1,0:T(8,128)(2,1)} %all-gather.8.cloned.1.call-done.refs_8_.refs_9_.refs_10_), kind=kOutput, calls=%fused_computation.20 | convolution fusion | flops 3222011904 | bytes 9961472 | tf_op jit(solution)/shard_map/dot_general | solution.py:573
  125.9 7.5 convolution_convert_fusion.10.k_ref
  133.4 4.5 convolution_convert_fusion.9.v_ref
  146.2 13.4 %wkv_forward.1 = (f32[1536,512]{1,0:T(8,128)}, bf16[12,512,128]{2,1,0:T(8,128)(2,1)S(1)}) custom-call(s32[1]{0:T(128)} %bitcast.here, bf16[1536,512]{1,0:T(8,128)(2,1)S(1)} %copy-done.10, bf16[1536,512]{1,0:T(8,128)(2,1)} %convolution_convert_fusion.10.k_ref, bf16[1536,512]{1,0:T(8,128)(2,1)} %convolution_convert_fusion.9.v_ref, ...), custom_call_target="tpu_custom_call" | custom-call | tf_op jit(solution)/shard_map/wkv_forward/pallas_call | solution.py:127
  159.6 14.2 %collective-permute-done.11.refs_2_ = bf16[384,2048]{1,0:T(8,128)(2,1)} collective-permute-done((bf16[384,2048]{1,0:T(8,128)(2,1)}, bf16[384,2048]{1,0:T(8,128)(2,1)}, u32[]{:S(2)}, u32[]{:S(2)}) %collective-permute-start.11) | collective-permute-done | bytes 1572896 | tf_op jit(solution)/shard_map/ppermute | solution.py:24
  183.1 10.1 %gate.1 = (f32[1536,512]{1,0:T(8,128)}, bf16[1536,512]{1,0:T(8,128)(2,1)S(1)}) custom-call(s32[1]{0:T(128)} %bitcast.here, bf16[1536,2048]{1,0:T(8,128)(2,1)} %get-tuple-element.275.refs_0_, bf16[2048,512]{1,0:T(8,128)(2,1)S(1)} %copy-done.4, f32[1536,512]{1,0:T(8,128)} %get-tuple-element.189.refs_2_.wkv_ref, f32[8,512]{1,0:T(8,128)S(1)} %maximum_maximum_fusion.par_ref.refs_3_), custom_call_target="tpu_custom_call" | custom-call | tf_op jit(solution)/shard_map/gate/pallas_call | solution.py:127
  195.6 2.9 convolution_convert_fusion.12
  204.0 8.4 %collective-permute-done.15.high_ref = bf16[192,2048]{1,0:T(8,128)(2,1)S(1)} collective-permute-done((bf16[192,2048]{1,0:T(8,128)(2,1)S(1)}, bf16[192,2048]{1,0:T(8,128)(2,1)S(1)}, u32[]{:S(2)}, u32[]{:S(2)}) %collective-permute-start.15) | collective-permute-done | bytes 786464 | tf_op jit(solution)/shard_map/ppermute | solution.py:24
  213.3 3.3 relay.4
  220.3 2.8 convolution_convert_fusion.15.refs_0_
  223.1 23.2 %collective-permute-done.16.refs_1_ = bf16[384,2048]{1,0:T(8,128)(2,1)} collective-permute-done((bf16[384,2048]{1,0:T(8,128)(2,1)}, bf16[384,2048]{1,0:T(8,128)(2,1)}, u32[]{:S(2)}, u32[]{:S(2)}) %collective-permute-start.16) | collective-permute-done | bytes 1572896 | tf_op jit(solution)/shard_map/ppermute | solution.py:24
  246.3 4.7 after_norm.1
  254.4 27.7 %collective-permute-done.19.refs_2_ = bf16[384,2048]{1,0:T(8,128)(2,1)S(1)} collective-permute-done((bf16[384,2048]{1,0:T(8,128)(2,1)S(1)}, bf16[384,2048]{1,0:T(8,128)(2,1)S(1)}, u32[]{:S(2)}, u32[]{:S(2)}) %collective-permute-start.19) | collective-permute-done | bytes 1572896 | tf_op jit(solution)/shard_map/ppermute | solution.py:24
  287.7 10.2 %collective-permute-done.21.refs_4_ = bf16[192,2048]{1,0:T(8,128)(2,1)} collective-permute-done((bf16[192,2048]{1,0:T(8,128)(2,1)}, bf16[192,2048]{1,0:T(8,128)(2,1)}, u32[]{:S(2)}, u32[]{:S(2)}) %collective-permute-start.21) | collective-permute-done | bytes 786464 | tf_op jit(solution)/shard_map/ppermute | solution.py:24
  299.8 12.3 %mixes.3 = (bf16[1536,2048]{1,0:T(8,128)(2,1)}, bf16[1536,2048]{1,0:T(8,128)(2,1)}, bf16[1536,2048]{1,0:T(8,128)(2,1)}) custom-call(s32[1]{0:T(128)} %bitcast.here, bf16[384,2048]{1,0:T(8,128)(2,1)S(1)} %copy-done.22, bf16[384,2048]{1,0:T(8,128)(2,1)S(1)} %collective-permute-done.18.refs_1_, bf16[384,2048]{1,0:T(8,128)(2,1)} %copy-done.73, ...), custom_call_target="tpu_custom_call" | custom-call | tf_op jit(solution)/shard_map/mixes/pallas_call | solution.py:127
  312.2 9.6 %divide_convert_fusion = (bf16[1536,512]{1,0:T(8,128)(2,1)}, f32[1536,512]{1,0:T(8,128)}) fusion(bf16[1536,2048]{1,0:T(8,128)(2,1)} %get-tuple-element.251, bf16[2048,2304]{1,0:T(8,128)(2,1)} %all-gather.12.cloned.1.call-done.refs_6_.refs_7_.refs_8_), kind=kOutput, calls=%fused_computation.10 | convolution fusion | flops 3224371200 | bytes 13107200 | tf_op jit(solution)/shard_map/dot_general | solution.py:573
  325.3 22.5 %multiply_convert_fusion.1 = (bf16[1536,1792]{1,0:T(8,128)(2,1)}, bf16[1536,1792]{1,0:T(8,128)(2,1)}) fusion(bf16[1536,2048]{1,0:T(8,128)(2,1)} %get-tuple-element.250, bf16[2048,2304]{1,0:T(8,128)(2,1)S(1)} %copy-done.70), kind=kOutput, calls=%fused_computation.2 | convolution fusion | flops 11312824320 | bytes 24641536 | tf_op jit(solution)/shard_map/dot_general | solution.py:573
  347.8 6.0 value_columns.7
  360.0 6.2 value_columns.6.two_ref
  367.4 6.0 value_columns.5.one_ref
  374.7 6.0 value_columns.4.refs_5_
  381.9 2.5 relay.5
  386.8 9.8 %spread_columns.2 = bf16[1536,2048]{1,0:T(8,128)(2,1)} custom-call(s32[1]{0:T(128)} %bitcast.here, bf16[384,2048]{1,0:T(8,128)(2,1)S(1)} %bitcast.96, bf16[384,2048]{1,0:T(8,128)(2,1)} %collective-permute-done.10.refs_1_, bf16[384,2048]{1,0:T(8,128)(2,1)} %collective-permute-done.11.refs_2_, bf16[192,2048]{1,0:T(8,128)(2,1)} %collective-permute-done.12.refs_3_, ...), custom_call_target="tpu_custom_call" | custom-call | tf_op jit(solution)/shard_map/spread_columns/pallas_call | solution.py:127
  396.6 15.9 %convolution_convert_fusion.1 = bf16[1792,2048]{1,0:T(8,128)(2,1)} fusion(bf16[1536,1792]{1,0:T(8,128)(2,1)S(1)} %bitcast.102, bf16[1536,2048]{1,0:T(8,128)(2,1)} %spread_columns.2), kind=kOutput, calls=%fused_computation.5 | convolution fusion | flops 11277959168 | bytes 19136512 | tf_op jit(solution)/shard_map/dot_general | solution.py:573
  413.5 19.0 %multiply_convert_fusion.refs_0_.refs_3_ = bf16[1536,1792]{1,0:T(8,128)(2,1)} fusion(bf16[1536,1792]{1,0:T(8,128)(2,1)} %get-tuple-element.229, bf16[1536,2048]{1,0:T(8,128)(2,1)} %spread_columns.2, bf16[1792,2048]{1,0:T(8,128)(2,1)} %all-gather.14.cloned.1.call-done.right_ref), kind=kOutput, calls=%fused_computation.1 | convolution fusion | flops 11282546688 | bytes 24641536 | tf_op jit(solution)/shard_map/dot_general | solution.py:573
  432.5 5.7 collective-permute-done.29.refs_6_
  440.6 6.9 channel.1
  448.8 9.0 %mixes_back.6 = (bf16[192,2048]{1,0:T(8,128)(2,1)S(1)}, bf16[192,2048]{1,0:T(8,128)(2,1)S(1)}, f32[8,2048]{1,0:T(8,128)S(1)}) custom-call(s32[1]{0:T(128)} %bitcast.here, bf16[1536,1792]{1,0:T(8,128)(2,1)} %multiply_convert_fusion.refs_0_.refs_3_, bf16[1536,512]{1,0:T(8,128)(2,1)S(1)} %get-tuple-element.248.refs_1_.refs_2_.refs_4_.refs_5_, ...), custom_call_target="tpu_custom_call" | custom-call | tf_op jit(solution)/shard_map/mixes_back/pallas_call | solution.py:127
  460.5 16.3 %mixes_back.7 = (bf16[384,2048]{1,0:T(8,128)(2,1)S(1)}, bf16[384,2048]{1,0:T(8,128)(2,1)S(1)}, f32[8,2048]{1,0:T(8,128)S(1)}) custom-call(s32[1]{0:T(128)} %bitcast.here, bf16[1536,1792]{1,0:T(8,128)(2,1)} %multiply_convert_fusion.refs_0_.refs_3_, bf16[1536,512]{1,0:T(8,128)(2,1)S(1)} %get-tuple-element.248.refs_1_.refs_2_.refs_4_.refs_5_, ...), custom_call_target="tpu_custom_call" | custom-call | tf_op jit(solution)/shard_map/mixes_back/pallas_call | solution.py:127
  483.9 16.4 %convolution_convert_fusion = bf16[2048,1792]{1,0:T(8,128)(2,1)} fusion(bf16[1536,2048]{1,0:T(8,128)(2,1)} %get-tuple-element.250, bf16[1536,1792]{1,0:T(8,128)(2,1)S(1)} %bitcast.100), kind=kOutput, calls=%fused_computation.4 | convolution fusion | flops 11277959168 | bytes 19136512 | tf_op jit(solution)/shard_map/dot_general | solution.py:573
  502.9 8.5 %mixes_back.8 = (bf16[384,2048]{1,0:T(8,128)(2,1)S(1)}, f32[8,2048]{1,0:T(8,128)S(1)}) custom-call(s32[1]{0:T(128)} %bitcast.here, bf16[1536,1792]{1,0:T(8,128)(2,1)} %multiply_convert_fusion.refs_0_.refs_3_, bf16[1536,512]{1,0:T(8,128)(2,1)S(1)} %get-tuple-element.248.refs_1_.refs_2_.refs_4_.refs_5_, ...), custom_call_target="tpu_custom_call" | custom-call | tf_op jit(solution)/shard_map/mixes_back/pallas_call | solution.py:127
  513.2 7.7 convolution_convert_fusion.8
  520.9 5.9 collective-permute-done.35.refs_1_
  530.4 6.7 norm_back.2
  539.0 30.5 %collective-permute-done.38 = bf16[384,2048]{1,0:T(8,128)(2,1)S(1)} collective-permute-done((bf16[384,2048]{1,0:T(8,128)(2,1)S(1)}, bf16[384,2048]{1,0:T(8,128)(2,1)S(1)}, u32[]{:S(2)}, u32[]{:S(2)}) %collective-permute-start.38) | collective-permute-done | bytes 1572896 | tf_op jit(solution)/shard_map/ppermute | solution.py:24
  574.9 8.8 %collective-permute-done.40 = bf16[192,2048]{1,0:T(8,128)(2,1)S(1)} collective-permute-done((bf16[192,2048]{1,0:T(8,128)(2,1)S(1)}, bf16[192,2048]{1,0:T(8,128)(2,1)S(1)}, u32[]{:S(2)}, u32[]{:S(2)}) %collective-permute-start.40) | collective-permute-done | bytes 786464 | tf_op jit(solution)/shard_map/ppermute | solution.py:24
  588.4 2.7 copy-done.83
  591.1 4.7 convolution_convert_fusion.6
  596.6 8.2 %convolution_convert_fusion.7.d_mixed_ref = bf16[1536,512]{1,0:T(8,128)(2,1)} fusion(bf16[1536,2048]{1,0:T(8,128)(2,1)} %copy-done.83, bf16[512,2048]{1,0:T(8,128)(2,1)} %all-gather.10.cloned.1.call-done), kind=kOutput, calls=%fused_computation.16 | convolution fusion | flops 3222011904 | bytes 9961472 | tf_op jit(solution)/shard_map/dot_general | solution.py:573
  608.5 37.4 %wkv_backward.1 = (bf16[1536,512]{1,0:T(8,128)(2,1)S(1)}, bf16[1536,512]{1,0:T(8,128)(2,1)S(1)}, bf16[1536,512]{1,0:T(8,128)(2,1)}, bf16[1536,512]{1,0:T(8,128)(2,1)}, f32[8,512]{1,0:T(8,128)S(1)}) custom-call(s32[1]{0:T(128)} %bitcast.here, bf16[1536,512]{1,0:T(8,128)(2,1)} %convolution_convert_fusion.11.r_ref, ...), custom_call_target="tpu_custom_call" | custom-call | tf_op jit(solution)/shard_map/wkv_backward/pallas_call | solution.py:127
  646.0 7.7 convolution_convert_fusion.4
  653.8 6.7 convolution_convert_fusion.5
  660.5 2.6 pad_maximum_fusion.1
  665.3 8.7 %mixes_back.9 = (bf16[192,2048]{1,0:T(8,128)(2,1)S(1)}, bf16[192,2048]{1,0:T(8,128)(2,1)S(1)}, f32[8,2048]{1,0:T(8,128)S(1)}) custom-call(s32[1]{0:T(128)} %bitcast.here, bf16[1536,512]{1,0:T(8,128)(2,1)S(1)} %get-tuple-element.301.refs_0_.refs_4_, bf16[1536,512]{1,0:T(8,128)(2,1)S(1)} %copy-done.1, bf16[1536,512]{1,0:T(8,128)(2,1)} %get-tuple-element.303.refs_2_.refs_6_, ...), custom_call_target="tpu_custom_call" | custom-call | tf_op jit(solution)/shard_map/mixes_back/pallas_call | solution.py:127
  676.6 15.4 %mixes_back.10 = (bf16[384,2048]{1,0:T(8,128)(2,1)S(1)}, bf16[384,2048]{1,0:T(8,128)(2,1)S(1)}, f32[8,2048]{1,0:T(8,128)S(1)}) custom-call(s32[1]{0:T(128)} %bitcast.here, bf16[1536,512]{1,0:T(8,128)(2,1)S(1)} %get-tuple-element.301.refs_0_.refs_4_, bf16[1536,512]{1,0:T(8,128)(2,1)} %copy-done, bf16[1536,512]{1,0:T(8,128)(2,1)} %get-tuple-element.303.refs_2_.refs_6_, ...), custom_call_target="tpu_custom_call" | custom-call | tf_op jit(solution)/shard_map/mixes_back/pallas_call | solution.py:127
  694.3 2.5 relay.7
  696.9 7.8 convolution_convert_fusion.2
  704.7 6.7 convolution_convert_fusion.3
  711.4 2.8 pad_maximum_fusion
  720.0 8.2 %mixes_back.11 = (bf16[384,2048]{1,0:T(8,128)(2,1)S(1)}, f32[8,2048]{1,0:T(8,128)S(1)}) custom-call(s32[1]{0:T(128)} %bitcast.here, bf16[1536,512]{1,0:T(8,128)(2,1)S(1)} %get-tuple-element.301.refs_0_.refs_4_, bf16[1536,512]{1,0:T(8,128)(2,1)S(1)} %copy-done.3, bf16[1536,512]{1,0:T(8,128)(2,1)} %get-tuple-element.303.refs_2_.refs_6_, ...), custom_call_target="tpu_custom_call" | custom-call | tf_op jit(solution)/shard_map/mixes_back/pallas_call | solution.py:127
  729.4 2.7 convert_element_type.184
  736.5 7.2 norm_back.3
  744.3 3.3 collective-permute-start.54
  747.6 8.7 %collective-permute-done.54 = f32[16,14,64]{2,1,0:T(8,128)S(1)} collective-permute-done((f32[16,14,64]{2,1,0:T(8,128)S(1)}, f32[16,14,64]{2,1,0:T(8,128)S(1)}, u32[]{:S(2)}, u32[]{:S(2)}) %collective-permute-start.54) | collective-permute-done | bytes 57376 | tf_op jit(solution)/shard_map/ppermute | solution.py:24
  756.6 5.8 collective-permute-done.55
  772.2 9.6 %collective-permute-done.58 = f32[1,14,64]{2,1,0:T(8,128)S(1)} collective-permute-done((f32[1,14,64]{2,1,0:T(8,128)S(1)}, f32[1,14,64]{2,1,0:T(8,128)S(1)}, u32[]{:S(2)}, u32[]{:S(2)}) %collective-permute-start.58) | collective-permute-done | bytes 3616 | tf_op jit(solution)/shard_map/ppermute | solution.py:24
  (472 shorter events, 177.5 us)
Async XLA Ops:
  7.2 110.5 %all-gather.8.cloned.1.call-start = ((), (), s32[]{:S(2)}) async-start(), calls=%async_computation.7 | async-start | bytes 7077888 | tf_op jit(solution)/shard_map/all_gather | solution.py:795
  11.9 11.5 %collective-permute-start = (bf16[80,2048]{1,0:T(8,128)(2,1)S(1)}, bf16[80,2048]{1,0:T(8,128)(2,1)S(1)}, u32[]{:S(2)}, u32[]{:S(2)}) collective-permute-start(bf16[80,2048]{1,0:T(8,128)(2,1)S(1)} %get-tuple-element.172.refs_1_), channel_id=1, source_target_pairs={{0,8},{8,0},{16,24},{24,16},{1,9},{9,1},{17,25},{25,17},{2,10},{10... | collective-permute-start | bytes 983048 | tf_op jit(solution)/shard_map/ppermute | solution.py:24
  15.0 16.2 %collective-permute-start.1 = (bf16[80,2048]{1,0:T(8,128)(2,1)S(1)}, bf16[80,2048]{1,0:T(8,128)(2,1)S(1)}, u32[]{:S(2)}, u32[]{:S(2)}) collective-permute-start(bf16[80,2048]{1,0:T(8,128)(2,1)S(1)} %get-tuple-element.173.refs_2_), channel_id=1, source_target_pairs={{0,16},{8,24},{16,0},{24,8},{1,17},{9,25},{17,1},{25,9},{2,18},{10... | collective-permute-start | bytes 983048 | tf_op jit(solution)/shard_map/ppermute | solution.py:24
  16.5 14.7 %collective-permute-start.2 = (bf16[80,2048]{1,0:T(8,128)(2,1)S(1)}, bf16[80,2048]{1,0:T(8,128)(2,1)S(1)}, u32[]{:S(2)}, u32[]{:S(2)}) collective-permute-start(bf16[80,2048]{1,0:T(8,128)(2,1)S(1)} %get-tuple-element.174.refs_3_), channel_id=1, source_target_pairs={{0,24},{8,16},{16,8},{24,0},{1,25},{9,17},{17,9},{25,1},{2,26},{10... | collective-permute-start | bytes 983048 | tf_op jit(solution)/shard_map/ppermute | solution.py:24
  32.2 149.3 %all-gather.6.cloned.1.call-start = ((), (), s32[]{:S(2)}) async-start(), calls=%async_computation.6 | async-start | bytes 2359296 | tf_op jit(solution)/shard_map/all_gather | solution.py:795
  33.5 35.4 %collective-permute-start.7 = (bf16[384,2048]{1,0:T(8,128)(2,1)}, bf16[384,2048]{1,0:T(8,128)(2,1)}, u32[]{:S(2)}, u32[]{:S(2)}) collective-permute-start(bf16[384,2048]{1,0:T(8,128)(2,1)} %hold.1.refs_0_), channel_id=1, source_target_pairs={{0,16},{8,24},{16,0},{24,8},{1,17},{9,25},{17,1},{25,9},{2,18},{10... | collective-permute-start | bytes 4718600 | tf_op jit(solution)/shard_map/ppermute | solution.py:24
  35.0 34.1 %collective-permute-start.6 = (bf16[384,2048]{1,0:T(8,128)(2,1)}, bf16[384,2048]{1,0:T(8,128)(2,1)}, u32[]{:S(2)}, u32[]{:S(2)}) collective-permute-start(bf16[384,2048]{1,0:T(8,128)(2,1)} %hold.1.refs_0_), channel_id=1, source_target_pairs={{0,8},{8,0},{16,24},{24,16},{1,9},{9,1},{17,25},{25,17},{2,10},{10... | collective-permute-start | bytes 4718600 | tf_op jit(solution)/shard_map/ppermute | solution.py:24
  41.8 11.6 %collective-permute-start.5 = (bf16[4,4,14,64]{3,2,1,0:T(8,128)(2,1)S(1)}, bf16[4,4,14,64]{3,2,1,0:T(8,128)(2,1)S(1)}, u32[]{:S(2)}, u32[]{:S(2)}) collective-permute-start(bf16[4,4,14,64]{3,2,1,0:T(8,128)(2,1)S(1)} %pad_maximum_fusion.4), channel_id=1, source_target_pairs={{0,4},{1,5},{2,6},{3,7},{4,0},{5,1},{6,2},{7,3},{8,12},{9,13},{10,... | collective-permute-start | bytes 86024 | tf_op jit(solution)/shard_map/ppermute | solution.py:24
  69.2 126.4 %all-gather.10.cloned.1.call-start = ((), (), s32[]{:S(2)}) async-start(), calls=%async_computation.8 | async-start | bytes 2359296 | tf_op jit(solution)/shard_map/all_gather | solution.py:795
  71.6 17.1 %collective-permute-start.9 = (bf16[192,2048]{1,0:T(8,128)(2,1)S(1)}, bf16[192,2048]{1,0:T(8,128)(2,1)S(1)}, u32[]{:S(2)}, u32[]{:S(2)}) collective-permute-start(bf16[192,2048]{1,0:T(8,128)(2,1)S(1)} %slice.263), channel_id=1, source_target_pairs={{0,8},{8,0},{16,24},{24,16},{1,9},{9,1},{17,25},{25,17},{2,10},{10... | collective-permute-start | bytes 2359304 | tf_op jit(solution)/shard_map/ppermute | solution.py:24
  73.1 17.0 %collective-permute-start.8 = (bf16[192,2048]{1,0:T(8,128)(2,1)S(1)}, bf16[192,2048]{1,0:T(8,128)(2,1)S(1)}, u32[]{:S(2)}, u32[]{:S(2)}) collective-permute-start(bf16[192,2048]{1,0:T(8,128)(2,1)S(1)} %slice.262), channel_id=1, source_target_pairs={{0,16},{8,24},{16,0},{24,8},{1,17},{9,25},{17,1},{25,9},{2,18},{10... | collective-permute-start | bytes 2359304 | tf_op jit(solution)/shard_map/ppermute | solution.py:24
  91.0 221.1 %all-gather.12.cloned.1.call-start = ((), (), s32[]{:S(2)}) async-start(), calls=%async_computation.9 | async-start | bytes 10616832 | tf_op jit(solution)/shard_map/all_gather | solution.py:795
  113.5 24.4 %collective-permute-start.22 = (bf16[80,2304]{1,0:T(8,128)(2,1)}, bf16[80,2304]{1,0:T(8,128)(2,1)}, u32[]{:S(2)}, u32[]{:S(2)}) collective-permute-start(bf16[80,2304]{1,0:T(8,128)(2,1)} %get-tuple-element.206), channel_id=1, source_target_pairs={{0,8},{8,0},{16,24},{24,16},{1,9},{9,1},{17,25},{25,17},{2,10},{10... | collective-permute-start | bytes 1105928 | tf_op jit(solution)/shard_map/ppermute | solution.py:24
  115.9 22.1 %collective-permute-start.23 = (bf16[80,2304]{1,0:T(8,128)(2,1)}, bf16[80,2304]{1,0:T(8,128)(2,1)}, u32[]{:S(2)}, u32[]{:S(2)}) collective-permute-start(bf16[80,2304]{1,0:T(8,128)(2,1)} %get-tuple-element.207), channel_id=1, source_target_pairs={{0,16},{8,24},{16,0},{24,8},{1,17},{9,25},{17,1},{25,9},{2,18},{10... | collective-permute-start | bytes 1105928 | tf_op jit(solution)/shard_map/ppermute | solution.py:24
  117.3 20.7 %collective-permute-start.24 = (bf16[80,2304]{1,0:T(8,128)(2,1)}, bf16[80,2304]{1,0:T(8,128)(2,1)}, u32[]{:S(2)}, u32[]{:S(2)}) collective-permute-start(bf16[80,2304]{1,0:T(8,128)(2,1)} %get-tuple-element.208), channel_id=1, source_target_pairs={{0,24},{8,16},{16,8},{24,0},{1,25},{9,17},{17,9},{25,1},{2,26},{10... | collective-permute-start | bytes 1105928 | tf_op jit(solution)/shard_map/ppermute | solution.py:24
  140.9 206.9 %all-gather.14.cloned.1.call-start = ((), (), s32[]{:S(2)}) async-start(), calls=%async_computation.10 | async-start | bytes 8257536 | tf_op jit(solution)/shard_map/all_gather | solution.py:795
  141.0 32.8 %collective-permute-start.11 = (bf16[384,2048]{1,0:T(8,128)(2,1)}, bf16[384,2048]{1,0:T(8,128)(2,1)}, u32[]{:S(2)}, u32[]{:S(2)}) collective-permute-start(bf16[384,2048]{1,0:T(8,128)(2,1)} %bitcast.93), channel_id=1, source_target_pairs={{0,16},{8,24},{16,0},{24,8},{1,17},{9,25},{17,1},{25,9},{2,18},{10... | collective-permute-start | bytes 4718600 | tf_op jit(solution)/shard_map/ppermute | solution.py:24
  143.1 32.2 %collective-permute-start.10 = (bf16[384,2048]{1,0:T(8,128)(2,1)}, bf16[384,2048]{1,0:T(8,128)(2,1)}, u32[]{:S(2)}, u32[]{:S(2)}) collective-permute-start(bf16[384,2048]{1,0:T(8,128)(2,1)} %bitcast.94), channel_id=1, source_target_pairs={{0,8},{8,0},{16,24},{24,16},{1,9},{9,1},{17,25},{25,17},{2,10},{10... | collective-permute-start | bytes 4718600 | tf_op jit(solution)/shard_map/ppermute | solution.py:24
  144.2 440.8 %reduce-scatter.7.cloned.1.call-start = ((), (), s32[]{:S(2)}) async-start(), calls=%async_computation.11 | async-start | bytes 8257536 | tf_op jit(solution)/shard_map/reduce_scatter | solution.py:798
  179.5 14.4 %collective-permute-start.13 = (bf16[192,2048]{1,0:T(8,128)(2,1)}, bf16[192,2048]{1,0:T(8,128)(2,1)S(1)}, u32[]{:S(2)}, u32[]{:S(2)}) collective-permute-start(bf16[192,2048]{1,0:T(8,128)(2,1)} %slice.268), channel_id=1, source_target_pairs={{0,8},{8,0},{16,24},{24,16},{1,9},{9,1},{17,25},{25,17},{2,10},{10... | collective-permute-start | bytes 2359304 | tf_op jit(solution)/shard_map/ppermute | solution.py:24
  180.8 14.8 %collective-permute-start.12 = (bf16[192,2048]{1,0:T(8,128)(2,1)}, bf16[192,2048]{1,0:T(8,128)(2,1)}, u32[]{:S(2)}, u32[]{:S(2)}) collective-permute-start(bf16[192,2048]{1,0:T(8,128)(2,1)} %slice.267), channel_id=1, source_target_pairs={{0,16},{8,24},{16,0},{24,8},{1,17},{9,25},{17,1},{25,9},{2,18},{10... | collective-permute-start | bytes 2359304 | tf_op jit(solution)/shard_map/ppermute | solution.py:24
  198.7 13.7 %collective-permute-start.15 = (bf16[192,2048]{1,0:T(8,128)(2,1)S(1)}, bf16[192,2048]{1,0:T(8,128)(2,1)S(1)}, u32[]{:S(2)}, u32[]{:S(2)}) collective-permute-start(bf16[192,2048]{1,0:T(8,128)(2,1)S(1)} %get-tuple-element.351), channel_id=1, source_target_pairs={{0,16},{8,24},{16,0},{24,8},{1,17},{9,25},{17,1},{25,9},{2,18},{10... | collective-permute-start | bytes 2359304 | tf_op jit(solution)/shard_map/ppermute | solution.py:24
  199.2 14.1 %collective-permute-start.14 = (bf16[192,2048]{1,0:T(8,128)(2,1)S(1)}, bf16[192,2048]{1,0:T(8,128)(2,1)S(1)}, u32[]{:S(2)}, u32[]{:S(2)}) collective-permute-start(bf16[192,2048]{1,0:T(8,128)(2,1)S(1)} %get-tuple-element.352), channel_id=1, source_target_pairs={{0,8},{8,0},{16,24},{24,16},{1,9},{9,1},{17,25},{25,17},{2,10},{10... | collective-permute-start | bytes 2359304 | tf_op jit(solution)/shard_map/ppermute | solution.py:24
  216.6 29.7 %collective-permute-start.16 = (bf16[384,2048]{1,0:T(8,128)(2,1)}, bf16[384,2048]{1,0:T(8,128)(2,1)}, u32[]{:S(2)}, u32[]{:S(2)}) collective-permute-start(bf16[384,2048]{1,0:T(8,128)(2,1)} %get-tuple-element.196), channel_id=1, source_target_pairs={{0,8},{8,0},{16,24},{24,16},{1,9},{9,1},{17,25},{25,17},{2,10},{10... | collective-permute-start | bytes 4718600 | tf_op jit(solution)/shard_map/ppermute | solution.py:24
  217.1 29.3 %collective-permute-start.17 = (bf16[384,2048]{1,0:T(8,128)(2,1)}, bf16[384,2048]{1,0:T(8,128)(2,1)}, u32[]{:S(2)}, u32[]{:S(2)}) collective-permute-start(bf16[384,2048]{1,0:T(8,128)(2,1)} %get-tuple-element.197), channel_id=1, source_target_pairs={{0,16},{8,24},{16,0},{24,8},{1,17},{9,25},{17,1},{25,9},{2,18},{10... | collective-permute-start | bytes 4718600 | tf_op jit(solution)/shard_map/ppermute | solution.py:24
  251.0 31.1 %collective-permute-start.19 = (bf16[384,2048]{1,0:T(8,128)(2,1)S(1)}, bf16[384,2048]{1,0:T(8,128)(2,1)S(1)}, u32[]{:S(2)}, u32[]{:S(2)}) collective-permute-start(bf16[384,2048]{1,0:T(8,128)(2,1)S(1)} %get-tuple-element.199.refs_0_), channel_id=1, source_target_pairs={{0,16},{8,24},{16,0},{24,8},{1,17},{9,25},{17,1},{25,9},{2,18},{10... | collective-permute-start | bytes 4718600 | tf_op jit(solution)/shard_map/ppermute | solution.py:24
  251.9 31.8 %collective-permute-start.18 = (bf16[384,2048]{1,0:T(8,128)(2,1)S(1)}, bf16[384,2048]{1,0:T(8,128)(2,1)S(1)}, u32[]{:S(2)}, u32[]{:S(2)}) collective-permute-start(bf16[384,2048]{1,0:T(8,128)(2,1)S(1)} %get-tuple-element.199.refs_0_), channel_id=1, source_target_pairs={{0,8},{8,0},{16,24},{24,16},{1,9},{9,1},{17,25},{25,17},{2,10},{10... | collective-permute-start | bytes 4718600 | tf_op jit(solution)/shard_map/ppermute | solution.py:24
  285.7 12.3 %collective-permute-start.21 = (bf16[192,2048]{1,0:T(8,128)(2,1)}, bf16[192,2048]{1,0:T(8,128)(2,1)}, u32[]{:S(2)}, u32[]{:S(2)}) collective-permute-start(bf16[192,2048]{1,0:T(8,128)(2,1)} %slice.276), channel_id=1, source_target_pairs={{0,8},{8,0},{16,24},{24,16},{1,9},{9,1},{17,25},{25,17},{2,10},{10... | collective-permute-start | bytes 2359304 | tf_op jit(solution)/shard_map/ppermute | solution.py:24
  286.1 12.3 %collective-permute-start.20 = (bf16[192,2048]{1,0:T(8,128)(2,1)}, bf16[192,2048]{1,0:T(8,128)(2,1)}, u32[]{:S(2)}, u32[]{:S(2)}) collective-permute-start(bf16[192,2048]{1,0:T(8,128)(2,1)} %slice.275), channel_id=1, source_target_pairs={{0,16},{8,24},{16,0},{24,8},{1,17},{9,25},{17,1},{25,9},{2,18},{10... | collective-permute-start | bytes 2359304 | tf_op jit(solution)/shard_map/ppermute | solution.py:24
  321.8 33.1 %collective-permute-start.26 = (bf16[1536,512]{1,0:T(8,128)(2,1)}, bf16[1536,512]{1,0:T(8,128)(2,1)S(1)}, u32[]{:S(2)}, u32[]{:S(2)}) collective-permute-start(bf16[1536,512]{1,0:T(8,128)(2,1)} %get-tuple-element.223.refs_5_), channel_id=1, source_target_pairs={{0,16},{8,24},{16,0},{24,8},{1,17},{9,25},{17,1},{25,9},{2,18},{10... | collective-permute-start | bytes 4718600 | tf_op jit(solution)/shard_map/ppermute | solution.py:24
  322.9 31.9 %collective-permute-start.25 = (bf16[1536,512]{1,0:T(8,128)(2,1)}, bf16[1536,512]{1,0:T(8,128)(2,1)}, u32[]{:S(2)}, u32[]{:S(2)}) collective-permute-start(bf16[1536,512]{1,0:T(8,128)(2,1)} %get-tuple-element.223.refs_5_), channel_id=1, source_target_pairs={{0,8},{8,0},{16,24},{24,16},{1,9},{9,1},{17,25},{25,17},{2,10},{10... | collective-permute-start | bytes 4718600 | tf_op jit(solution)/shard_map/ppermute | solution.py:24
  354.0 27.9 %collective-permute-start.28 = (bf16[768,512]{1,0:T(8,128)(2,1)S(1)}, bf16[768,512]{1,0:T(8,128)(2,1)S(1)}, u32[]{:S(2)}, u32[]{:S(2)}) collective-permute-start(bf16[768,512]{1,0:T(8,128)(2,1)S(1)} %get-tuple-element.349), channel_id=1, source_target_pairs={{0,16},{8,24},{16,0},{24,8},{1,17},{9,25},{17,1},{25,9},{2,18},{10... | collective-permute-start | bytes 2359304 | tf_op jit(solution)/shard_map/ppermute | solution.py:24
  354.9 27.0 %collective-permute-start.27 = (bf16[768,512]{1,0:T(8,128)(2,1)S(1)}, bf16[768,512]{1,0:T(8,128)(2,1)S(1)}, u32[]{:S(2)}, u32[]{:S(2)}) collective-permute-start(bf16[768,512]{1,0:T(8,128)(2,1)S(1)} %get-tuple-element.350), channel_id=1, source_target_pairs={{0,8},{8,0},{16,24},{24,16},{1,9},{9,1},{17,25},{25,17},{2,10},{10... | collective-permute-start | bytes 2359304 | tf_op jit(solution)/shard_map/ppermute | solution.py:24
  356.7 28.8 %collective-permute-start.32 = (bf16[768,512]{1,0:T(8,128)(2,1)S(1)}, bf16[768,512]{1,0:T(8,128)(2,1)S(1)}, u32[]{:S(2)}, u32[]{:S(2)}) collective-permute-start(bf16[768,512]{1,0:T(8,128)(2,1)S(1)} %slice.290), channel_id=1, source_target_pairs={{0,8},{8,0},{16,24},{24,16},{1,9},{9,1},{17,25},{25,17},{2,10},{10... | collective-permute-start | bytes 2359304 | tf_op jit(solution)/shard_map/ppermute | solution.py:24
  358.8 26.7 %collective-permute-start.31 = (bf16[768,512]{1,0:T(8,128)(2,1)S(1)}, bf16[768,512]{1,0:T(8,128)(2,1)S(1)}, u32[]{:S(2)}, u32[]{:S(2)}) collective-permute-start(bf16[768,512]{1,0:T(8,128)(2,1)S(1)} %slice.289), channel_id=1, source_target_pairs={{0,16},{8,24},{16,0},{24,8},{1,17},{9,25},{17,1},{25,9},{2,18},{10... | collective-permute-start | bytes 2359304 | tf_op jit(solution)/shard_map/ppermute | solution.py:24
  412.5 192.3 %reduce-scatter.9.cloned.1.call-start = ((), (), s32[]{:S(2)}) async-start(), calls=%async_computation.12 | async-start | bytes 8257536 | tf_op jit(solution)/shard_map/reduce_scatter | solution.py:798
  412.6 25.6 %collective-permute-start.29 = (bf16[1536,512]{1,0:T(8,128)(2,1)}, bf16[1536,512]{1,0:T(8,128)(2,1)S(1)}, u32[]{:S(2)}, u32[]{:S(2)}) collective-permute-start(bf16[1536,512]{1,0:T(8,128)(2,1)} %copy-done.67), channel_id=1, source_target_pairs={{0,8},{8,0},{16,24},{24,16},{1,9},{9,1},{17,25},{25,17},{2,10},{10... | collective-permute-start | bytes 4718600 | tf_op jit(solution)/shard_map/ppermute | solution.py:24
  412.7 26.7 %collective-permute-start.30 = (bf16[1536,512]{1,0:T(8,128)(2,1)S(1)}, bf16[1536,512]{1,0:T(8,128)(2,1)S(1)}, u32[]{:S(2)}, u32[]{:S(2)}) collective-permute-start(bf16[1536,512]{1,0:T(8,128)(2,1)S(1)} %get-tuple-element.221), channel_id=1, source_target_pairs={{0,16},{8,24},{16,0},{24,8},{1,17},{9,25},{17,1},{25,9},{2,18},{10... | collective-permute-start | bytes 4718600 | tf_op jit(solution)/shard_map/ppermute | solution.py:24
  458.4 20.8 %collective-permute-start.33 = (bf16[192,2048]{1,0:T(8,128)(2,1)S(1)}, bf16[192,2048]{1,0:T(8,128)(2,1)S(1)}, u32[]{:S(2)}, u32[]{:S(2)}) collective-permute-start(bf16[192,2048]{1,0:T(8,128)(2,1)S(1)} %get-tuple-element.235), channel_id=1, source_target_pairs={{0,8},{8,0},{16,24},{24,16},{1,9},{9,1},{17,25},{25,17},{2,10},{10... | collective-permute-start | bytes 2359304 | tf_op jit(solution)/shard_map/ppermute | solution.py:24
  459.0 20.2 %collective-permute-start.34 = (bf16[192,2048]{1,0:T(8,128)(2,1)S(1)}, bf16[192,2048]{1,0:T(8,128)(2,1)S(1)}, u32[]{:S(2)}, u32[]{:S(2)}) collective-permute-start(bf16[192,2048]{1,0:T(8,128)(2,1)S(1)} %get-tuple-element.236), channel_id=1, source_target_pairs={{0,16},{8,24},{16,0},{24,8},{1,17},{9,25},{17,1},{25,9},{2,18},{10... | collective-permute-start | bytes 2359304 | tf_op jit(solution)/shard_map/ppermute | solution.py:24
  500.3 163.6 %reduce-scatter.11.cloned.1.call-start = ((), (), s32[]{:S(2)}) async-start(), calls=%async_computation.13 | async-start | bytes 2359296 | tf_op jit(solution)/shard_map/reduce_scatter | solution.py:798
  500.4 26.4 %collective-permute-start.35 = (bf16[384,2048]{1,0:T(8,128)(2,1)}, bf16[384,2048]{1,0:T(8,128)(2,1)}, u32[]{:S(2)}, u32[]{:S(2)}) collective-permute-start(bf16[384,2048]{1,0:T(8,128)(2,1)} %copy-done.69), channel_id=1, source_target_pairs={{0,8},{8,0},{16,24},{24,16},{1,9},{9,1},{17,25},{25,17},{2,10},{10... | collective-permute-start | bytes 4718600 | tf_op jit(solution)/shard_map/ppermute | solution.py:24
  501.7 25.8 %collective-permute-start.36 = (bf16[384,2048]{1,0:T(8,128)(2,1)}, bf16[384,2048]{1,0:T(8,128)(2,1)}, u32[]{:S(2)}, u32[]{:S(2)}) collective-permute-start(bf16[384,2048]{1,0:T(8,128)(2,1)} %copy-done.68), channel_id=1, source_target_pairs={{0,16},{8,24},{16,0},{24,8},{1,17},{9,25},{17,1},{25,9},{2,18},{10... | collective-permute-start | bytes 4718600 | tf_op jit(solution)/shard_map/ppermute | solution.py:24
  537.8 31.8 %collective-permute-start.38 = (bf16[384,2048]{1,0:T(8,128)(2,1)S(1)}, bf16[384,2048]{1,0:T(8,128)(2,1)S(1)}, u32[]{:S(2)}, u32[]{:S(2)}) collective-permute-start(bf16[384,2048]{1,0:T(8,128)(2,1)S(1)} %get-tuple-element.258), channel_id=1, source_target_pairs={{0,16},{8,24},{16,0},{24,8},{1,17},{9,25},{17,1},{25,9},{2,18},{10... | collective-permute-start | bytes 4718600 | tf_op jit(solution)/shard_map/ppermute | solution.py:24
  538.1 32.5 %collective-permute-start.37 = (bf16[384,2048]{1,0:T(8,128)(2,1)S(1)}, bf16[384,2048]{1,0:T(8,128)(2,1)S(1)}, u32[]{:S(2)}, u32[]{:S(2)}) collective-permute-start(bf16[384,2048]{1,0:T(8,128)(2,1)S(1)} %get-tuple-element.258), channel_id=1, source_target_pairs={{0,8},{8,0},{16,24},{24,16},{1,9},{9,1},{17,25},{25,17},{2,10},{10... | collective-permute-start | bytes 4718600 | tf_op jit(solution)/shard_map/ppermute | solution.py:24
  571.7 12.0 %collective-permute-start.40 = (bf16[192,2048]{1,0:T(8,128)(2,1)S(1)}, bf16[192,2048]{1,0:T(8,128)(2,1)S(1)}, u32[]{:S(2)}, u32[]{:S(2)}) collective-permute-start(bf16[192,2048]{1,0:T(8,128)(2,1)S(1)} %slice.292), channel_id=1, source_target_pairs={{0,8},{8,0},{16,24},{24,16},{1,9},{9,1},{17,25},{25,17},{2,10},{10... | collective-permute-start | bytes 2359304 | tf_op jit(solution)/shard_map/ppermute | solution.py:24
  572.8 12.2 %collective-permute-start.39 = (bf16[192,2048]{1,0:T(8,128)(2,1)S(1)}, bf16[192,2048]{1,0:T(8,128)(2,1)}, u32[]{:S(2)}, u32[]{:S(2)}) collective-permute-start(bf16[192,2048]{1,0:T(8,128)(2,1)S(1)} %slice.291), channel_id=1, source_target_pairs={{0,16},{8,24},{16,0},{24,8},{1,17},{9,25},{17,1},{25,9},{2,18},{10... | collective-permute-start | bytes 2359304 | tf_op jit(solution)/shard_map/ppermute | solution.py:24
  595.8 151.8 %reduce-scatter.15.cloned.1.call-start = ((), (), s32[]{:S(2)}) async-start(), calls=%async_computation.15 | async-start | bytes 2359296 | tf_op jit(solution)/shard_map/reduce_scatter | solution.py:798
  596.5 173.3 %reduce-scatter.17.cloned.1.call-start = ((), (), s32[]{:S(2)}) async-start(), calls=%async_computation.16 | async-start | bytes 4718592 | tf_op jit(solution)/shard_map/reduce_scatter | solution.py:798
  604.9 41.0 %collective-permute-start.43 = (bf16[384,512]{1,0:T(8,128)(2,1)S(1)}, bf16[384,512]{1,0:T(8,128)(2,1)S(1)}, u32[]{:S(2)}, u32[]{:S(2)}) collective-permute-start(bf16[384,512]{1,0:T(8,128)(2,1)S(1)} %get-tuple-element.345), channel_id=1, source_target_pairs={{0,24},{8,16},{16,8},{24,0},{1,25},{9,17},{17,9},{25,1},{2,26},{10... | collective-permute-start | bytes 1179656 | tf_op jit(solution)/shard_map/ppermute | solution.py:24
  607.3 38.6 %collective-permute-start.42 = (bf16[384,512]{1,0:T(8,128)(2,1)S(1)}, bf16[384,512]{1,0:T(8,128)(2,1)S(1)}, u32[]{:S(2)}, u32[]{:S(2)}) collective-permute-start(bf16[384,512]{1,0:T(8,128)(2,1)S(1)} %get-tuple-element.346), channel_id=1, source_target_pairs={{0,16},{8,24},{16,0},{24,8},{1,17},{9,25},{17,1},{25,9},{2,18},{10... | collective-permute-start | bytes 1179656 | tf_op jit(solution)/shard_map/ppermute | solution.py:24
  607.3 38.6 %collective-permute-start.41 = (bf16[384,512]{1,0:T(8,128)(2,1)S(1)}, bf16[384,512]{1,0:T(8,128)(2,1)S(1)}, u32[]{:S(2)}, u32[]{:S(2)}) collective-permute-start(bf16[384,512]{1,0:T(8,128)(2,1)S(1)} %get-tuple-element.347), channel_id=1, source_target_pairs={{0,8},{8,0},{16,24},{24,16},{1,9},{9,1},{17,25},{25,17},{2,10},{10... | collective-permute-start | bytes 1179656 | tf_op jit(solution)/shard_map/ppermute | solution.py:24
  663.1 125.9 %reduce-scatter.13.cloned.1.call-start = ((), (), s32[]{:S(2)}) async-start(), calls=%async_computation.14 | async-start | bytes 4718592 | tf_op jit(solution)/shard_map/reduce_scatter | solution.py:798
  674.0 20.3 %collective-permute-start.44 = (bf16[192,2048]{1,0:T(8,128)(2,1)S(1)}, bf16[192,2048]{1,0:T(8,128)(2,1)S(1)}, u32[]{:S(2)}, u32[]{:S(2)}) collective-permute-start(bf16[192,2048]{1,0:T(8,128)(2,1)S(1)} %get-tuple-element.284), channel_id=1, source_target_pairs={{0,8},{8,0},{16,24},{24,16},{1,9},{9,1},{17,25},{25,17},{2,10},{10... | collective-permute-start | bytes 2359304 | tf_op jit(solution)/shard_map/ppermute | solution.py:24
  674.6 19.7 %collective-permute-start.45 = (bf16[192,2048]{1,0:T(8,128)(2,1)S(1)}, bf16[192,2048]{1,0:T(8,128)(2,1)S(1)}, u32[]{:S(2)}, u32[]{:S(2)}) collective-permute-start(bf16[192,2048]{1,0:T(8,128)(2,1)S(1)} %get-tuple-element.285), channel_id=1, source_target_pairs={{0,16},{8,24},{16,0},{24,8},{1,17},{9,25},{17,1},{25,9},{2,18},{10... | collective-permute-start | bytes 2359304 | tf_op jit(solution)/shard_map/ppermute | solution.py:24
  714.2 21.8 %collective-permute-start.46 = (bf16[384,2048]{1,0:T(8,128)(2,1)}, bf16[384,2048]{1,0:T(8,128)(2,1)}, u32[]{:S(2)}, u32[]{:S(2)}) collective-permute-start(bf16[384,2048]{1,0:T(8,128)(2,1)} %copy-done.66), channel_id=1, source_target_pairs={{0,8},{8,0},{16,24},{24,16},{1,9},{9,1},{17,25},{25,17},{2,10},{10... | collective-permute-start | bytes 4718600 | tf_op jit(solution)/shard_map/ppermute | solution.py:24
  715.5 20.7 %collective-permute-start.47 = (bf16[384,2048]{1,0:T(8,128)(2,1)}, bf16[384,2048]{1,0:T(8,128)(2,1)}, u32[]{:S(2)}, u32[]{:S(2)}) collective-permute-start(bf16[384,2048]{1,0:T(8,128)(2,1)} %copy-done.65), channel_id=1, source_target_pairs={{0,16},{8,24},{16,0},{24,8},{1,17},{9,25},{17,1},{25,9},{2,18},{10... | collective-permute-start | bytes 4718600 | tf_op jit(solution)/shard_map/ppermute | solution.py:24
  744.3 12.1 %collective-permute-start.54 = (f32[16,14,64]{2,1,0:T(8,128)S(1)}, f32[16,14,64]{2,1,0:T(8,128)S(1)}, u32[]{:S(2)}, u32[]{:S(2)}) collective-permute-start(f32[16,14,64]{2,1,0:T(8,128)S(1)} %bitcast.108), channel_id=1, source_target_pairs={{0,4},{1,5},{2,6},{3,7},{4,0},{5,1},{6,2},{7,3},{8,12},{9,13},{10,... | collective-permute-start | bytes 172040 | tf_op jit(solution)/shard_map/ppermute | solution.py:24
  765.1 17.9 %collective-permute-start.50 = (bf16[64,2304]{1,0:T(8,128)(2,1)S(1)}, bf16[64,2304]{1,0:T(8,128)(2,1)S(1)}, u32[]{:S(2)}, u32[]{:S(2)}) collective-permute-start(bf16[64,2304]{1,0:T(8,128)(2,1)S(1)} %get-tuple-element.353), channel_id=1, source_target_pairs={{0,24},{8,16},{16,8},{24,0},{1,25},{9,17},{17,9},{25,1},{2,26},{10... | collective-permute-start | bytes 884744 | tf_op jit(solution)/shard_map/ppermute | solution.py:24
  766.4 18.3 %collective-permute-start.49 = (bf16[64,2304]{1,0:T(8,128)(2,1)S(1)}, bf16[64,2304]{1,0:T(8,128)(2,1)S(1)}, u32[]{:S(2)}, u32[]{:S(2)}) collective-permute-start(bf16[64,2304]{1,0:T(8,128)(2,1)S(1)} %get-tuple-element.354), channel_id=1, source_target_pairs={{0,16},{8,24},{16,0},{24,8},{1,17},{9,25},{17,1},{25,9},{2,18},{10... | collective-permute-start | bytes 884744 | tf_op jit(solution)/shard_map/ppermute | solution.py:24
  767.7 17.0 %collective-permute-start.48 = (bf16[64,2304]{1,0:T(8,128)(2,1)S(1)}, bf16[64,2304]{1,0:T(8,128)(2,1)S(1)}, u32[]{:S(2)}, u32[]{:S(2)}) collective-permute-start(bf16[64,2304]{1,0:T(8,128)(2,1)S(1)} %get-tuple-element.355), channel_id=1, source_target_pairs={{0,8},{8,0},{16,24},{24,16},{1,9},{9,1},{17,25},{25,17},{2,10},{10... | collective-permute-start | bytes 884744 | tf_op jit(solution)/shard_map/ppermute | solution.py:24
  768.7 13.1 %collective-permute-start.58 = (f32[1,14,64]{2,1,0:T(8,128)S(1)}, f32[1,14,64]{2,1,0:T(8,128)S(1)}, u32[]{:S(2)}, u32[]{:S(2)}) collective-permute-start(f32[1,14,64]{2,1,0:T(8,128)S(1)} %slice_select_fusion.5), channel_id=1, source_target_pairs={{0,8},{8,0},{16,24},{24,16},{1,9},{9,1},{17,25},{25,17},{2,10},{10... | collective-permute-start | bytes 10760 | tf_op jit(solution)/shard_map/ppermute | solution.py:24
  771.0 15.3 %collective-permute-start.53 = (bf16[64,1024]{1,0:T(8,128)(2,1)S(1)}, bf16[64,1024]{1,0:T(8,128)(2,1)S(1)}, u32[]{:S(2)}, u32[]{:S(2)}) collective-permute-start(bf16[64,1024]{1,0:T(8,128)(2,1)S(1)} %get-tuple-element.361), channel_id=1, source_target_pairs={{0,24},{8,16},{16,8},{24,0},{1,25},{9,17},{17,9},{25,1},{2,26},{10... | collective-permute-start | bytes 393224 | tf_op jit(solution)/shard_map/ppermute | solution.py:24
  790.2 6.1 collective-permute-start.61
  (113 other events, 982.5 us)
Sparse Core Ops, SparseCore 0:
  32.3 67.7 all-gather.7
  102.3 27.6 all-gather.5
  131.7 28.5 all-gather.9
  161.8 90.2 all-gather.11
  253.5 71.8 all-gather.13
  412.7 78.9 reduce-scatter.6
  500.4 79.8 reduce-scatter.8
  595.9 36.6 reduce-scatter.10
  634.9 34.4 reduce-scatter.14
  671.5 48.5 reduce-scatter.16
  722.4 52.3 reduce-scatter.12

commit v9 on v8

--- a/solution.py
+++ b/solution.py
@@ -26,6 +26,13 @@
 
 def after(value, *others):
     return lax.optimization_barrier((value, others))[0]
+
+
+def gather_second(part, one, two):
+    half = part.shape[0] // 2
+    columns = part.shape[1]
+    low, high = swap(one[:half, :columns], "seq", 2), swap(two[half : 2 * half, :columns], "seq", 1)
+    return [part, one, two, low, high]
 
 
 def gather_seq(part, first=()):
@@ -220,6 +227,46 @@
     )
 
 
+def ride_body(count, here, *refs):
+    ins, rider, outs = refs[:count], refs[count], refs[count + 1 :]
+    for j, out in enumerate(outs):
+        top, at = 0, 0
+        if j in (1, 2):
+            top = rider.shape[0]
+            out[:top, : rider.shape[1]] = rider[...]
+            out[:top, rider.shape[1] :] = jnp.zeros_like(out[:top, rider.shape[1] :])
+        for ref in ins:
+            width = ref.shape[1] // 4
+            out[top:, at : at + width] = ref[:, placed(here[0] ^ j, width)]
+            at += width
+
+
+def cut_with_rider(weights, rider, here):
+    rows, width = weights[0].shape[0], sum(w.shape[1] for w in weights) // 4
+    return kernel(
+        partial(ride_body, len(weights)), "cut_columns", (1,), here,
+        [(w, fixed(w.shape)) for w in [*weights, rider]],
+        [((n, width), BF, fixed((n, width))) for n in (rows, rows + rider.shape[0], rows + rider.shape[0], rows)],
+    )
+
+
+def unride_body(here, *refs):
+    out = refs[-1]
+    rows = out.shape[1]
+    for j, ref in enumerate(refs[:-1]):
+        out[here[0] ^ j] = ref[ref.shape[0] - rows :, :]
+
+
+def stack_below(pieces, here):
+    shape = (4,) + pieces[0].shape
+    (stacked,) = kernel(
+        unride_body, "stack_rows", (1,), here,
+        [(p, fixed(p.shape)) for p in pieces],
+        [(shape, BF, fixed(shape))],
+    )
+    return stacked.reshape(-1, shape[-1])
+
+
 def hold_body(here, in_ref, *refs):
     refs[-1][...] = in_ref[...]
 
@@ -265,7 +312,7 @@
 
 
 def spread_columns(bases, columns, here, product, turn, tile, per):
-    rows, width = sum(base.shape[0] for base in bases), bases[0].shape[1]
+    rows, width = sum(counts_of(bases, tile)) * tile, bases[0].shape[1]
 
     def turned(i, j):
         return (lax.div(i, per) ^ j) * per + lax.rem(i, per) if turn else i
@@ -839,15 +886,23 @@
         for i, m in enumerate((mix_r, mix_k, mix_v))
     )
     projected = (recept, keyed, valued)
-    (columns_c, _), _ = stacked_columns(after([ffn_key, ffn_receptance], mix_r), [hidden_width + part], projected)
+    ffn_weights = after([ffn_key, ffn_receptance], mix_r)
+    if seq == 4:
+        pieces_c = trade_seq(cut_with_rider(ffn_weights, grad_b, here))
+    else:
+        (columns_c, _), _ = stacked_columns(ffn_weights, [hidden_width + part], projected)
+        grad_all = gather_seq(after(grad_b, mix_r), projected)
+    wkv, states = wkv_forward(recept, keyed, valued, tables, here, per)
+    gate_pre, mixed = gated(mix_g, full_g, wkv, tables[5], here, seq)
+    if seq == 4:
+        pieces_c = after(pieces_c, mixed)
+        columns_c = stack_below(pieces_c, here)
+        grad_all = gather_second(grad_b, *pieces_c[1:3])
     full_c = gather_dp(columns_c)
     full_ck, full_cr = full_c[:, :hidden_width], full_c[:, hidden_width:]
     full_cv = gather_dp(after(ffn_value, columns_c))
-    wkv, states = wkv_forward(recept, keyed, valued, tables, here, per)
-    grad_all = gather_seq(after(grad_b, mix_r), wkv)
-    gate_pre, mixed = gated(mix_g, full_g, wkv, tables[5], here, seq)
-    attn = [dot(rows, own_o, NN).astype(BF) for rows in blocks_of(after(mixed, grad_all[3:]), seq)]
-    after_mix, normed_two = after_norm(inputs_b, scatter_seq(attn, here), rows_of(vec, 10, 11), here)
+    attn = [dot(rows, own_o, NN).astype(BF) for rows in blocks_of(mixed, seq)]
+    after_mix, normed_two = after_norm(inputs_b, after(scatter_seq(attn, here), grad_all[3:]), rows_of(vec, 10, 11), here)
 
     mix_k2, mix_r2, step_two = mixes(
         turn_pieces(gather_seq(normed_two)), marks, rows_of(turned, 10, 11, 12, 13), 2, False, within, here, tile,
@@ -892,11 +947,16 @@
         terms_two = [outside(t, groups, unit, back=True) for t in terms_two]
     d_after, d_attn, norm_sums_two = norm_back(terms_two, after_mix, grad_b, rows_of(vec, 10), within, here)
 
-    d_attn = jnp.concatenate(after(gather_seq(d_attn), summed_cv), axis=0)
-    d_mixed = dot(d_attn, own_o, NT).astype(BF)
-    grad_wo = dot(mixed, d_attn, TN).astype(BF)
-    d_mixed = after(d_mixed, grad_wo, summed_ck)
+    pieces = gather_seq(d_attn)
+    *near, far = by_block(pieces)
+    near_mixed = [dot(d, own_o, NT).astype(BF) for d in near]
+    *near_rows, far_rows = blocks_of(mixed, seq)
+    near_wo = sum(dot(m, d, TN) for m, d in zip(near_rows, near))
+    far = after(far, near_mixed, near_wo, summed_cv)
+    d_mixed = jnp.concatenate([*near_mixed, dot(far, own_o, NT).astype(BF)], axis=0)
+    grad_wo = (near_wo + dot(far_rows, far, TN)).astype(BF)
     summed_o = scatter_dp(grad_wo)
+    d_mixed = after(d_mixed, summed_ck, grad_wo)
     d_recept, d_keyed, d_valued, d_gate, sums = wkv_backward(
         recept, keyed, valued, gate_pre, wkv, d_mixed, states, tables, here, per
     )

time: 811 us -> 827 us (1.020)
    dot_general x19 -> x25, matrix products: 163 us -> 168 us  [dot(): return lax.dot_general(left, right, dims, preferred_element_type=F32)]
    unnamed x214 -> x232, local copies, waits for them, and re-layouts: 50.1 us -> 46.5 us
    ppermute x62 -> x60, waiting for transfers between devices: 230 us -> 233 us  [swap(): return lax.ppermute(value, axis, [(i, i ^ distance) for i in range(size)])]
    ppermute x62 -> x60, starting transfers between devices: 72.4 us -> 71.9 us  [swap(): return lax.ppermute(value, axis, [(i, i ^ distance) for i in range(size)])]
  transfers between devices with their start and end apart: 73 -> 71, of which waited for: 38 -> 38; matrix products, arithmetic and copies ran while one was open for 22% -> 23% of each run, Pallas kernels for 28% -> 28%
where the time goes in v9:
time: 827 us; the launch traced here: 821 us
  Pallas kernels  240 us (29%)
  waiting for transfers between devices  234 us (28%)
  matrix products  168 us (20%)
  starting transfers between devices  73.5 us (9%)
  local copies, waits for them, and re-layouts  72.4 us (9%)
  other arithmetic  17.8 us (2%)
  between operations  15.6 us (2%)
    pallas_call x33, Pallas kernels, kernel(): pl.pallas_call(body, out_shape=[jax.ShapeDtypeStruct(shape, kind) for sha...  240 us
    ppermute x60, waiting for transfers between devices, swap(): return lax.ppermute(value, axis, [(i, i ^ distance) for i in range(size)])  233 us
    dot_general x25, matrix products, dot(): return lax.dot_general(left, right, dims, preferred_element_type=F32)  168 us
    ppermute x60, starting transfers between devices, swap(): return lax.ppermute(value, axis, [(i, i ^ distance) for i in range(size)])  71.9 us
    unnamed x232, local copies, waits for them, and re-layouts  46.5 us
  transfers between devices with their start and end apart: 71, of which 38 were waited for; matrix products, arithmetic and copies ran while one was open for 23% of the time, Pallas kernels for 28%

profile of v9, /device:TPU:0, one launch (start us, length us, event | category | flops | bytes accessed | tf_op | source)
XLA Modules:
  0.0 820.7 jit_solution(2121040789239759034)
XLA Ops:
  11.9 3.0 collective-permute-start
  18.6 4.8 collective-permute-done.refs_1_
  23.5 8.4 %collective-permute-done.1.refs_2_ = bf16[80,2048]{1,0:T(8,128)(2,1)S(1)} collective-permute-done((bf16[80,2048]{1,0:T(8,128)(2,1)S(1)}, bf16[80,2048]{1,0:T(8,128)(2,1)S(1)}, u32[]{:S(2)}, u32[]{:S(2)}) %collective-permute-start.1) | collective-permute-done | bytes 327712 | tf_op jit(solution)/shard_map/ppermute | solution.py:24
  44.6 3.1 collective-permute-start.5
  49.3 6.1 collective-permute-done.5
  59.7 11.3 %collective-permute-done.7.refs_2_ = bf16[384,2048]{1,0:T(8,128)(2,1)} collective-permute-done((bf16[384,2048]{1,0:T(8,128)(2,1)S(1)}, bf16[384,2048]{1,0:T(8,128)(2,1)}, u32[]{:S(2)}, u32[]{:S(2)}) %collective-permute-start.7) | collective-permute-done | bytes 1572896 | tf_op jit(solution)/shard_map/ppermute | solution.py:24
  76.3 15.6 %collective-permute-done.9.refs_4_ = bf16[192,2048]{1,0:T(8,128)(2,1)S(1)} collective-permute-done((bf16[192,2048]{1,0:T(8,128)(2,1)S(1)}, bf16[192,2048]{1,0:T(8,128)(2,1)S(1)}, u32[]{:S(2)}, u32[]{:S(2)}) %collective-permute-start.9) | collective-permute-done | bytes 786464 | tf_op jit(solution)/shard_map/ppermute | solution.py:24
  95.8 17.6 %mixes.2 = (bf16[1536,2048]{1,0:T(8,128)(2,1)}, bf16[1536,2048]{1,0:T(8,128)(2,1)}, bf16[1536,2048]{1,0:T(8,128)(2,1)}, bf16[1536,2048]{1,0:T(8,128)(2,1)}, bf16[1536,2048]{1,0:T(8,128)(2,1)}) custom-call(s32[1]{0:T(128)} %bitcast.here, bf16[384,2048]{1,0:T(8,128)(2,1)S(1)} %copy-done.13, bf16[384,2048]{1,0:T(8,128)(2,1)} %collective-permute-done.6.refs_1_, ...), custom_call_target="tpu_custom_call" | custom-call | tf_op jit(solution)/shard_map/mixes/pallas_call | solution.py:134
  113.4 2.4 cut_columns.3
  119.6 7.0 convolution_convert_fusion.9.r_ref
  126.7 7.9 convolution_convert_fusion.8.k_ref
  134.6 4.5 convolution_convert_fusion.7.v_ref
  139.2 13.5 %wkv_forward.1 = (f32[1536,512]{1,0:T(8,128)}, bf16[12,512,128]{2,1,0:T(8,128)(2,1)S(1)}) custom-call(s32[1]{0:T(128)} %bitcast.here, bf16[1536,512]{1,0:T(8,128)(2,1)S(1)} %convolution_convert_fusion.9.r_ref, bf16[1536,512]{1,0:T(8,128)(2,1)} %convolution_convert_fusion.8.k_ref, bf16[1536,512]{1,0:T(8,128)(2,1)} %convolution_convert_fusion.7.v_ref, ...), custom_call_target="tpu_custom_call" | custom-call | tf_op jit(solution)/shard_map/wkv_forward/pallas_call | solution.py:134
  155.5 10.1 %gate.1 = (f32[1536,512]{1,0:T(8,128)}, bf16[1536,512]{1,0:T(8,128)(2,1)S(1)}) custom-call(s32[1]{0:T(128)} %bitcast.here, bf16[1536,2048]{1,0:T(8,128)(2,1)} %get-tuple-element.263.refs_0_, bf16[2048,512]{1,0:T(8,128)(2,1)S(1)} %copy-done.4, f32[1536,512]{1,0:T(8,128)} %get-tuple-element.183.refs_2_.wkv_ref, f32[8,512]{1,0:T(8,128)S(1)} %maximum_maximum_fusion.par_ref.refs_3_), custom_call_target="tpu_custom_call" | custom-call | tf_op jit(solution)/shard_map/gate/pallas_call | solution.py:134
  167.4 3.3 stack_rows.3
  171.8 2.8 convolution_convert_fusion.10
  181.3 11.0 %collective-permute-done.11.high_ref = bf16[192,2048]{1,0:T(8,128)(2,1)S(1)} collective-permute-done((bf16[192,2048]{1,0:T(8,128)(2,1)S(1)}, bf16[192,2048]{1,0:T(8,128)(2,1)S(1)}, u32[]{:S(2)}, u32[]{:S(2)}) %collective-permute-start.11) | collective-permute-done | bytes 786464 | tf_op jit(solution)/shard_map/ppermute | solution.py:24
  193.8 3.3 relay.4
  207.3 2.8 convolution_convert_fusion.13.refs_0_
  210.1 37.7 %collective-permute-done.18.refs_4_ = bf16[192,2048]{1,0:T(8,128)(2,1)S(1)} collective-permute-done((bf16[192,2048]{1,0:T(8,128)(2,1)}, bf16[192,2048]{1,0:T(8,128)(2,1)S(1)}, u32[]{:S(2)}, u32[]{:S(2)}) %collective-permute-start.18) | collective-permute-done | bytes 786464 | tf_op jit(solution)/shard_map/ppermute | solution.py:24
  247.9 4.7 after_norm.1
  255.0 30.3 %collective-permute-done.20.refs_2_ = bf16[384,2048]{1,0:T(8,128)(2,1)S(1)} collective-permute-done((bf16[384,2048]{1,0:T(8,128)(2,1)S(1)}, bf16[384,2048]{1,0:T(8,128)(2,1)S(1)}, u32[]{:S(2)}, u32[]{:S(2)}) %collective-permute-start.20) | collective-permute-done | bytes 1572896 | tf_op jit(solution)/shard_map/ppermute | solution.py:24
  295.3 9.0 %collective-permute-done.22.refs_4_ = bf16[192,2048]{1,0:T(8,128)(2,1)} collective-permute-done((bf16[192,2048]{1,0:T(8,128)(2,1)}, bf16[192,2048]{1,0:T(8,128)(2,1)}, u32[]{:S(2)}, u32[]{:S(2)}) %collective-permute-start.22) | collective-permute-done | bytes 786464 | tf_op jit(solution)/shard_map/ppermute | solution.py:24
  308.0 12.1 %mixes.3 = (bf16[1536,2048]{1,0:T(8,128)(2,1)}, bf16[1536,2048]{1,0:T(8,128)(2,1)}, bf16[1536,2048]{1,0:T(8,128)(2,1)}) custom-call(s32[1]{0:T(128)} %bitcast.here, bf16[384,2048]{1,0:T(8,128)(2,1)S(1)} %copy-done.28, bf16[384,2048]{1,0:T(8,128)(2,1)S(1)} %copy-done.18, bf16[384,2048]{1,0:T(8,128)(2,1)} %copy-done.77, ...), custom_call_target="tpu_custom_call" | custom-call | tf_op jit(solution)/shard_map/mixes/pallas_call | solution.py:134
  320.1 9.6 %divide_convert_fusion = (bf16[1536,512]{1,0:T(8,128)(2,1)}, f32[1536,512]{1,0:T(8,128)}) fusion(bf16[1536,2048]{1,0:T(8,128)(2,1)} %get-tuple-element.243, bf16[2048,2304]{1,0:T(8,128)(2,1)} %all-gather.12.cloned.1.call-done.refs_6_.refs_7_.refs_8_), kind=kOutput, calls=%fused_computation.12 | convolution fusion | flops 3224371200 | bytes 13107200 | tf_op jit(solution)/shard_map/dot_general | solution.py:620
  332.0 22.7 %multiply_convert_fusion.1 = (bf16[1536,1792]{1,0:T(8,128)(2,1)}, bf16[1536,1792]{1,0:T(8,128)(2,1)}) fusion(bf16[1536,2048]{1,0:T(8,128)(2,1)} %get-tuple-element.242, bf16[2048,2304]{1,0:T(8,128)(2,1)S(1)} %copy-done.73), kind=kOutput, calls=%fused_computation.2 | convolution fusion | flops 11312824320 | bytes 24641536 | tf_op jit(solution)/shard_map/dot_general | solution.py:620
  354.7 6.0 value_columns.7
  366.0 3.3 collective-permute-start.30
  371.1 6.0 value_columns.6.two_ref
  378.3 6.0 value_columns.5.one_ref
  385.5 6.0 value_columns.4.refs_5_
  397.5 10.2 %spread_columns.2 = bf16[1536,2048]{1,0:T(8,128)(2,1)} custom-call(s32[1]{0:T(128)} %bitcast.here, bf16[384,2048]{1,0:T(8,128)(2,1)S(1)} %bitcast.100, bf16[448,2304]{1,0:T(8,128)(2,1)} %collective-permute-done.14.refs_1_, bf16[448,2304]{1,0:T(8,128)(2,1)} %collective-permute-done.15.refs_2_, bf16[192,2048]{1,0:T(8,128)(2,1)} %collective-permute-done.17.refs_3_, ...), custom_call_target="tpu_custom_call" | custom-call | tf_op jit(solution)/shard_map/spread_columns/pallas_call | solution.py:134
  407.8 16.1 %convolution_convert_fusion.1 = bf16[1792,2048]{1,0:T(8,128)(2,1)} fusion(bf16[1536,1792]{1,0:T(8,128)(2,1)S(1)} %bitcast.108, bf16[1536,2048]{1,0:T(8,128)(2,1)} %spread_columns.2), kind=kOutput, calls=%fused_computation.5 | convolution fusion | flops 11277959168 | bytes 19136512 | tf_op jit(solution)/shard_map/dot_general | solution.py:620
  425.6 18.3 %multiply_convert_fusion.refs_0_.refs_3_ = bf16[1536,1792]{1,0:T(8,128)(2,1)} fusion(bf16[1536,1792]{1,0:T(8,128)(2,1)} %get-tuple-element.221, bf16[1536,2048]{1,0:T(8,128)(2,1)} %spread_columns.2, bf16[1792,2048]{1,0:T(8,128)(2,1)} %all-gather.14.cloned.1.call-done.right_ref), kind=kOutput, calls=%fused_computation.1 | convolution fusion | flops 11282546688 | bytes 24641536 | tf_op jit(solution)/shard_map/dot_general | solution.py:620
  443.9 10.5 %collective-permute-done.27.refs_6_ = bf16[1536,512]{1,0:T(8,128)(2,1)S(1)} collective-permute-done((bf16[1536,512]{1,0:T(8,128)(2,1)}, bf16[1536,512]{1,0:T(8,128)(2,1)S(1)}, u32[]{:S(2)}, u32[]{:S(2)}) %collective-permute-start.27) | collective-permute-done | bytes 1572896 | tf_op jit(solution)/shard_map/ppermute | solution.py:24
  456.8 6.9 channel.1
  463.7 9.0 %mixes_back.6 = (bf16[192,2048]{1,0:T(8,128)(2,1)S(1)}, bf16[192,2048]{1,0:T(8,128)(2,1)S(1)}, f32[8,2048]{1,0:T(8,128)S(1)}) custom-call(s32[1]{0:T(128)} %bitcast.here, bf16[1536,1792]{1,0:T(8,128)(2,1)} %multiply_convert_fusion.refs_0_.refs_3_, bf16[1536,512]{1,0:T(8,128)(2,1)S(1)} %get-tuple-element.240.refs_1_.refs_2_.refs_4_.refs_5_, ...), custom_call_target="tpu_custom_call" | custom-call | tf_op jit(solution)/shard_map/mixes_back/pallas_call | solution.py:134
  475.4 16.1 %mixes_back.7 = (bf16[384,2048]{1,0:T(8,128)(2,1)S(1)}, bf16[384,2048]{1,0:T(8,128)(2,1)S(1)}, f32[8,2048]{1,0:T(8,128)S(1)}) custom-call(s32[1]{0:T(128)} %bitcast.here, bf16[1536,1792]{1,0:T(8,128)(2,1)} %multiply_convert_fusion.refs_0_.refs_3_, bf16[1536,512]{1,0:T(8,128)(2,1)S(1)} %get-tuple-element.240.refs_1_.refs_2_.refs_4_.refs_5_, ...), custom_call_target="tpu_custom_call" | custom-call | tf_op jit(solution)/shard_map/mixes_back/pallas_call | solution.py:134
  498.8 16.3 %convolution_convert_fusion = bf16[2048,1792]{1,0:T(8,128)(2,1)} fusion(bf16[1536,2048]{1,0:T(8,128)(2,1)} %get-tuple-element.242, bf16[1536,1792]{1,0:T(8,128)(2,1)S(1)} %bitcast.106), kind=kOutput, calls=%fused_computation.4 | convolution fusion | flops 11277959168 | bytes 19136512 | tf_op jit(solution)/shard_map/dot_general | solution.py:620
  516.7 9.0 %mixes_back.8 = (bf16[384,2048]{1,0:T(8,128)(2,1)S(1)}, f32[8,2048]{1,0:T(8,128)S(1)}) custom-call(s32[1]{0:T(128)} %bitcast.here, bf16[1536,1792]{1,0:T(8,128)(2,1)} %multiply_convert_fusion.refs_0_.refs_3_, bf16[1536,512]{1,0:T(8,128)(2,1)S(1)} %get-tuple-element.240.refs_1_.refs_2_.refs_4_.refs_5_, ...), custom_call_target="tpu_custom_call" | custom-call | tf_op jit(solution)/shard_map/mixes_back/pallas_call | solution.py:134
  526.9 7.7 convolution_convert_fusion.6
  534.6 11.1 %collective-permute-done.33.refs_1_ = bf16[384,2048]{1,0:T(8,128)(2,1)} collective-permute-done((bf16[384,2048]{1,0:T(8,128)(2,1)}, bf16[384,2048]{1,0:T(8,128)(2,1)}, u32[]{:S(2)}, u32[]{:S(2)}) %collective-permute-start.33) | collective-permute-done | bytes 1572896 | tf_op jit(solution)/shard_map/ppermute | solution.py:24
  548.7 6.8 norm_back.2
  560.2 28.4 %collective-permute-done.36 = bf16[384,2048]{1,0:T(8,128)(2,1)S(1)} collective-permute-done((bf16[384,2048]{1,0:T(8,128)(2,1)S(1)}, bf16[384,2048]{1,0:T(8,128)(2,1)S(1)}, u32[]{:S(2)}, u32[]{:S(2)}) %collective-permute-start.36) | collective-permute-done | bytes 1572896 | tf_op jit(solution)/shard_map/ppermute | solution.py:24
  598.5 3.4 add_add_fusion
  605.4 5.3 add_convert_fusion
  612.1 2.7 convolution_convert_fusion.14
  621.2 37.2 %wkv_backward.1 = (bf16[1536,512]{1,0:T(8,128)(2,1)S(1)}, bf16[1536,512]{1,0:T(8,128)(2,1)S(1)}, bf16[1536,512]{1,0:T(8,128)(2,1)}, bf16[1536,512]{1,0:T(8,128)(2,1)}, f32[8,512]{1,0:T(8,128)S(1)}) custom-call(s32[1]{0:T(128)} %bitcast.here, bf16[1536,512]{1,0:T(8,128)(2,1)} %copy-done.11, bf16[1536,512]{1,0:T(8,128)(2,1)} %convolution_convert_fusion.8.k_ref, ...), custom_call_target="tpu_custom_call" | custom-call | tf_op jit(solution)/shard_map/wkv_backward/pallas_call | solution.py:134
  658.4 7.7 convolution_convert_fusion.4
  666.2 6.7 convolution_convert_fusion.5
  672.9 2.5 pad_maximum_fusion.1
  677.7 8.4 %mixes_back.9 = (bf16[192,2048]{1,0:T(8,128)(2,1)S(1)}, bf16[192,2048]{1,0:T(8,128)(2,1)S(1)}, f32[8,2048]{1,0:T(8,128)S(1)}) custom-call(s32[1]{0:T(128)} %bitcast.here, bf16[1536,512]{1,0:T(8,128)(2,1)S(1)} %get-tuple-element.289.refs_0_.refs_4_, bf16[1536,512]{1,0:T(8,128)(2,1)S(1)} %copy-done.1, bf16[1536,512]{1,0:T(8,128)(2,1)} %get-tuple-element.291.refs_2_.refs_6_, ...), custom_call_target="tpu_custom_call" | custom-call | tf_op jit(solution)/shard_map/mixes_back/pallas_call | solution.py:134
  687.7 15.4 %mixes_back.10 = (bf16[384,2048]{1,0:T(8,128)(2,1)S(1)}, bf16[384,2048]{1,0:T(8,128)(2,1)S(1)}, f32[8,2048]{1,0:T(8,128)S(1)}) custom-call(s32[1]{0:T(128)} %bitcast.here, bf16[1536,512]{1,0:T(8,128)(2,1)S(1)} %get-tuple-element.289.refs_0_.refs_4_, bf16[1536,512]{1,0:T(8,128)(2,1)} %copy-done, bf16[1536,512]{1,0:T(8,128)(2,1)} %get-tuple-element.291.refs_2_.refs_6_, ...), custom_call_target="tpu_custom_call" | custom-call | tf_op jit(solution)/shard_map/mixes_back/pallas_call | solution.py:134
  705.4 2.5 relay.7
  708.0 7.8 convolution_convert_fusion.2
  715.8 6.7 convolution_convert_fusion.3
  722.5 2.6 pad_maximum_fusion
  732.8 8.2 mixes_back.11
  747.6 3.4 collective-permute-done.44.refs_1_
  751.3 7.2 norm_back.3
  759.1 2.9 collective-permute-start.52
  762.0 8.8 %collective-permute-done.52 = f32[16,14,64]{2,1,0:T(8,128)S(1)} collective-permute-done((f32[16,14,64]{2,1,0:T(8,128)S(1)}, f32[16,14,64]{2,1,0:T(8,128)S(1)}, u32[]{:S(2)}, u32[]{:S(2)}) %collective-permute-start.52) | collective-permute-done | bytes 57376 | tf_op jit(solution)/shard_map/ppermute | solution.py:24
  771.2 5.9 collective-permute-done.53
  786.9 9.6 %collective-permute-done.56 = f32[1,14,64]{2,1,0:T(8,128)S(1)} collective-permute-done((f32[1,14,64]{2,1,0:T(8,128)S(1)}, f32[1,14,64]{2,1,0:T(8,128)S(1)}, u32[]{:S(2)}, u32[]{:S(2)}) %collective-permute-start.56) | collective-permute-done | bytes 3616 | tf_op jit(solution)/shard_map/ppermute | solution.py:24
  (493 shorter events, 191.3 us)
Async XLA Ops:
  7.2 112.4 %all-gather.8.cloned.1.call-start = ((), (), s32[]{:S(2)}) async-start(), calls=%async_computation.7 | async-start | bytes 7077888 | tf_op jit(solution)/shard_map/all_gather | solution.py:842
  11.9 11.5 %collective-permute-start = (bf16[80,2048]{1,0:T(8,128)(2,1)S(1)}, bf16[80,2048]{1,0:T(8,128)(2,1)S(1)}, u32[]{:S(2)}, u32[]{:S(2)}) collective-permute-start(bf16[80,2048]{1,0:T(8,128)(2,1)S(1)} %get-tuple-element.166.refs_1_), channel_id=1, source_target_pairs={{0,8},{8,0},{16,24},{24,16},{1,9},{9,1},{17,25},{25,17},{2,10},{10... | collective-permute-start | bytes 983048 | tf_op jit(solution)/shard_map/ppermute | solution.py:24
  15.7 16.2 %collective-permute-start.1 = (bf16[80,2048]{1,0:T(8,128)(2,1)S(1)}, bf16[80,2048]{1,0:T(8,128)(2,1)S(1)}, u32[]{:S(2)}, u32[]{:S(2)}) collective-permute-start(bf16[80,2048]{1,0:T(8,128)(2,1)S(1)} %get-tuple-element.167.refs_2_), channel_id=1, source_target_pairs={{0,16},{8,24},{16,0},{24,8},{1,17},{9,25},{17,1},{25,9},{2,18},{10... | collective-permute-start | bytes 983048 | tf_op jit(solution)/shard_map/ppermute | solution.py:24
  17.9 13.9 %collective-permute-start.2 = (bf16[80,2048]{1,0:T(8,128)(2,1)S(1)}, bf16[80,2048]{1,0:T(8,128)(2,1)S(1)}, u32[]{:S(2)}, u32[]{:S(2)}) collective-permute-start(bf16[80,2048]{1,0:T(8,128)(2,1)S(1)} %get-tuple-element.168.refs_3_), channel_id=1, source_target_pairs={{0,24},{8,16},{16,8},{24,0},{1,25},{9,17},{17,9},{25,1},{2,26},{10... | collective-permute-start | bytes 983048 | tf_op jit(solution)/shard_map/ppermute | solution.py:24
  32.9 120.9 %all-gather.6.cloned.1.call-start = ((), (), s32[]{:S(2)}) async-start(), calls=%async_computation.6 | async-start | bytes 2359296 | tf_op jit(solution)/shard_map/all_gather | solution.py:842
  36.1 34.9 %collective-permute-start.7 = (bf16[384,2048]{1,0:T(8,128)(2,1)S(1)}, bf16[384,2048]{1,0:T(8,128)(2,1)}, u32[]{:S(2)}, u32[]{:S(2)}) collective-permute-start(bf16[384,2048]{1,0:T(8,128)(2,1)S(1)} %hold.1.refs_0_), channel_id=1, source_target_pairs={{0,16},{8,24},{16,0},{24,8},{1,17},{9,25},{17,1},{25,9},{2,18},{10... | collective-permute-start | bytes 4718600 | tf_op jit(solution)/shard_map/ppermute | solution.py:24
  37.6 34.8 %collective-permute-start.6 = (bf16[384,2048]{1,0:T(8,128)(2,1)S(1)}, bf16[384,2048]{1,0:T(8,128)(2,1)}, u32[]{:S(2)}, u32[]{:S(2)}) collective-permute-start(bf16[384,2048]{1,0:T(8,128)(2,1)S(1)} %hold.1.refs_0_), channel_id=1, source_target_pairs={{0,8},{8,0},{16,24},{24,16},{1,9},{9,1},{17,25},{25,17},{2,10},{10... | collective-permute-start | bytes 4718600 | tf_op jit(solution)/shard_map/ppermute | solution.py:24
  44.6 10.8 %collective-permute-start.5 = (bf16[4,4,14,64]{3,2,1,0:T(8,128)(2,1)S(1)}, bf16[4,4,14,64]{3,2,1,0:T(8,128)(2,1)S(1)}, u32[]{:S(2)}, u32[]{:S(2)}) collective-permute-start(bf16[4,4,14,64]{3,2,1,0:T(8,128)(2,1)S(1)} %pad_maximum_fusion.6), channel_id=1, source_target_pairs={{0,4},{1,5},{2,6},{3,7},{4,0},{5,1},{6,2},{7,3},{8,12},{9,13},{10,... | collective-permute-start | bytes 86024 | tf_op jit(solution)/shard_map/ppermute | solution.py:24
  72.5 99.3 %all-gather.10.cloned.1.call-start = ((), (), s32[]{:S(2)}) async-start(), calls=%async_computation.8 | async-start | bytes 2359296 | tf_op jit(solution)/shard_map/all_gather | solution.py:842
  75.0 16.9 %collective-permute-start.9 = (bf16[192,2048]{1,0:T(8,128)(2,1)S(1)}, bf16[192,2048]{1,0:T(8,128)(2,1)S(1)}, u32[]{:S(2)}, u32[]{:S(2)}) collective-permute-start(bf16[192,2048]{1,0:T(8,128)(2,1)S(1)} %slice.267), channel_id=1, source_target_pairs={{0,8},{8,0},{16,24},{24,16},{1,9},{9,1},{17,25},{25,17},{2,10},{10... | collective-permute-start | bytes 2359304 | tf_op jit(solution)/shard_map/ppermute | solution.py:24
  75.3 16.6 %collective-permute-start.8 = (bf16[192,2048]{1,0:T(8,128)(2,1)S(1)}, bf16[192,2048]{1,0:T(8,128)(2,1)S(1)}, u32[]{:S(2)}, u32[]{:S(2)}) collective-permute-start(bf16[192,2048]{1,0:T(8,128)(2,1)S(1)} %slice.266), channel_id=1, source_target_pairs={{0,16},{8,24},{16,0},{24,8},{1,17},{9,25},{17,1},{25,9},{2,18},{10... | collective-permute-start | bytes 2359304 | tf_op jit(solution)/shard_map/ppermute | solution.py:24
  92.9 227.3 %all-gather.12.cloned.1.call-start = ((), (), s32[]{:S(2)}) async-start(), calls=%async_computation.9 | async-start | bytes 10616832 | tf_op jit(solution)/shard_map/all_gather | solution.py:842
  115.8 50.9 %collective-permute-start.16 = (bf16[64,2304]{1,0:T(8,128)(2,1)}, bf16[64,2304]{1,0:T(8,128)(2,1)S(1)}, u32[]{:S(2)}, u32[]{:S(2)}) collective-permute-start(bf16[64,2304]{1,0:T(8,128)(2,1)} %get-tuple-element.193), channel_id=1, source_target_pairs={{0,24},{8,16},{16,8},{24,0},{1,25},{9,17},{17,9},{25,1},{2,26},{10... | collective-permute-start | bytes 884744 | tf_op jit(solution)/shard_map/ppermute | solution.py:24
  118.1 49.3 %collective-permute-start.14 = (bf16[448,2304]{1,0:T(8,128)(2,1)}, bf16[448,2304]{1,0:T(8,128)(2,1)}, u32[]{:S(2)}, u32[]{:S(2)}) collective-permute-start(bf16[448,2304]{1,0:T(8,128)(2,1)} %get-tuple-element.191), channel_id=1, source_target_pairs={{0,8},{8,0},{16,24},{24,16},{1,9},{9,1},{17,25},{25,17},{2,10},{10... | collective-permute-start | bytes 6193160 | tf_op jit(solution)/shard_map/ppermute | solution.py:24
  119.2 48.2 %collective-permute-start.15 = (bf16[448,2304]{1,0:T(8,128)(2,1)}, bf16[448,2304]{1,0:T(8,128)(2,1)}, u32[]{:S(2)}, u32[]{:S(2)}) collective-permute-start(bf16[448,2304]{1,0:T(8,128)(2,1)} %get-tuple-element.192), channel_id=1, source_target_pairs={{0,16},{8,24},{16,0},{24,8},{1,17},{9,25},{17,1},{25,9},{2,18},{10... | collective-permute-start | bytes 6193160 | tf_op jit(solution)/shard_map/ppermute | solution.py:24
  170.7 184.0 %all-gather.14.cloned.1.call-start = ((), (), s32[]{:S(2)}) async-start(), calls=%async_computation.10 | async-start | bytes 8257536 | tf_op jit(solution)/shard_map/all_gather | solution.py:842
  171.3 434.1 %reduce-scatter.7.cloned.1.call-start = ((), (), s32[]{:S(2)}) async-start(), calls=%async_computation.11 | async-start | bytes 8257536 | tf_op jit(solution)/shard_map/reduce_scatter | solution.py:845
  174.8 17.6 %collective-permute-start.11 = (bf16[192,2048]{1,0:T(8,128)(2,1)S(1)}, bf16[192,2048]{1,0:T(8,128)(2,1)S(1)}, u32[]{:S(2)}, u32[]{:S(2)}) collective-permute-start(bf16[192,2048]{1,0:T(8,128)(2,1)S(1)} %get-tuple-element.339), channel_id=1, source_target_pairs={{0,16},{8,24},{16,0},{24,8},{1,17},{9,25},{17,1},{25,9},{2,18},{10... | collective-permute-start | bytes 2359304 | tf_op jit(solution)/shard_map/ppermute | solution.py:24
  176.2 17.6 %collective-permute-start.10 = (bf16[192,2048]{1,0:T(8,128)(2,1)S(1)}, bf16[192,2048]{1,0:T(8,128)(2,1)S(1)}, u32[]{:S(2)}, u32[]{:S(2)}) collective-permute-start(bf16[192,2048]{1,0:T(8,128)(2,1)S(1)} %get-tuple-element.340), channel_id=1, source_target_pairs={{0,8},{8,0},{16,24},{24,16},{1,9},{9,1},{17,25},{25,17},{2,10},{10... | collective-permute-start | bytes 2359304 | tf_op jit(solution)/shard_map/ppermute | solution.py:24
  197.1 50.8 %collective-permute-start.12 = (bf16[384,2048]{1,0:T(8,128)(2,1)}, bf16[384,2048]{1,0:T(8,128)(2,1)}, u32[]{:S(2)}, u32[]{:S(2)}) collective-permute-start(bf16[384,2048]{1,0:T(8,128)(2,1)} %get-tuple-element.186), channel_id=1, source_target_pairs={{0,8},{8,0},{16,24},{24,16},{1,9},{9,1},{17,25},{25,17},{2,10},{10... | collective-permute-start | bytes 4718600 | tf_op jit(solution)/shard_map/ppermute | solution.py:24
  197.4 50.5 %collective-permute-start.13 = (bf16[384,2048]{1,0:T(8,128)(2,1)}, bf16[384,2048]{1,0:T(8,128)(2,1)}, u32[]{:S(2)}, u32[]{:S(2)}) collective-permute-start(bf16[384,2048]{1,0:T(8,128)(2,1)} %get-tuple-element.187), channel_id=1, source_target_pairs={{0,16},{8,24},{16,0},{24,8},{1,17},{9,25},{17,1},{25,9},{2,18},{10... | collective-permute-start | bytes 4718600 | tf_op jit(solution)/shard_map/ppermute | solution.py:24
  202.8 45.0 %collective-permute-start.18 = (bf16[192,2048]{1,0:T(8,128)(2,1)}, bf16[192,2048]{1,0:T(8,128)(2,1)S(1)}, u32[]{:S(2)}, u32[]{:S(2)}) collective-permute-start(bf16[192,2048]{1,0:T(8,128)(2,1)} %slice.278), channel_id=1, source_target_pairs={{0,8},{8,0},{16,24},{24,16},{1,9},{9,1},{17,25},{25,17},{2,10},{10... | collective-permute-start | bytes 2359304 | tf_op jit(solution)/shard_map/ppermute | solution.py:24
  203.8 44.1 %collective-permute-start.17 = (bf16[192,2048]{1,0:T(8,128)(2,1)}, bf16[192,2048]{1,0:T(8,128)(2,1)}, u32[]{:S(2)}, u32[]{:S(2)}) collective-permute-start(bf16[192,2048]{1,0:T(8,128)(2,1)} %slice.277), channel_id=1, source_target_pairs={{0,16},{8,24},{16,0},{24,8},{1,17},{9,25},{17,1},{25,9},{2,18},{10... | collective-permute-start | bytes 2359304 | tf_op jit(solution)/shard_map/ppermute | solution.py:24
  252.6 32.7 %collective-permute-start.20 = (bf16[384,2048]{1,0:T(8,128)(2,1)S(1)}, bf16[384,2048]{1,0:T(8,128)(2,1)S(1)}, u32[]{:S(2)}, u32[]{:S(2)}) collective-permute-start(bf16[384,2048]{1,0:T(8,128)(2,1)S(1)} %get-tuple-element.200.refs_0_), channel_id=1, source_target_pairs={{0,16},{8,24},{16,0},{24,8},{1,17},{9,25},{17,1},{25,9},{2,18},{10... | collective-permute-start | bytes 4718600 | tf_op jit(solution)/shard_map/ppermute | solution.py:24
  253.3 32.6 %collective-permute-start.19 = (bf16[384,2048]{1,0:T(8,128)(2,1)S(1)}, bf16[384,2048]{1,0:T(8,128)(2,1)S(1)}, u32[]{:S(2)}, u32[]{:S(2)}) collective-permute-start(bf16[384,2048]{1,0:T(8,128)(2,1)S(1)} %get-tuple-element.200.refs_0_), channel_id=1, source_target_pairs={{0,8},{8,0},{16,24},{24,16},{1,9},{9,1},{17,25},{25,17},{2,10},{10... | collective-permute-start | bytes 4718600 | tf_op jit(solution)/shard_map/ppermute | solution.py:24
  289.0 15.3 %collective-permute-start.22 = (bf16[192,2048]{1,0:T(8,128)(2,1)}, bf16[192,2048]{1,0:T(8,128)(2,1)}, u32[]{:S(2)}, u32[]{:S(2)}) collective-permute-start(bf16[192,2048]{1,0:T(8,128)(2,1)} %slice.280), channel_id=1, source_target_pairs={{0,8},{8,0},{16,24},{24,16},{1,9},{9,1},{17,25},{25,17},{2,10},{10... | collective-permute-start | bytes 2359304 | tf_op jit(solution)/shard_map/ppermute | solution.py:24
  290.5 14.7 %collective-permute-start.21 = (bf16[192,2048]{1,0:T(8,128)(2,1)}, bf16[192,2048]{1,0:T(8,128)(2,1)}, u32[]{:S(2)}, u32[]{:S(2)}) collective-permute-start(bf16[192,2048]{1,0:T(8,128)(2,1)} %slice.279), channel_id=1, source_target_pairs={{0,16},{8,24},{16,0},{24,8},{1,17},{9,25},{17,1},{25,9},{2,18},{10... | collective-permute-start | bytes 2359304 | tf_op jit(solution)/shard_map/ppermute | solution.py:24
  329.7 33.9 %collective-permute-start.24 = (bf16[1536,512]{1,0:T(8,128)(2,1)}, bf16[1536,512]{1,0:T(8,128)(2,1)}, u32[]{:S(2)}, u32[]{:S(2)}) collective-permute-start(bf16[1536,512]{1,0:T(8,128)(2,1)} %get-tuple-element.215.refs_5_), channel_id=1, source_target_pairs={{0,16},{8,24},{16,0},{24,8},{1,17},{9,25},{17,1},{25,9},{2,18},{10... | collective-permute-start | bytes 4718600 | tf_op jit(solution)/shard_map/ppermute | solution.py:24
  330.7 33.0 %collective-permute-start.23 = (bf16[1536,512]{1,0:T(8,128)(2,1)}, bf16[1536,512]{1,0:T(8,128)(2,1)}, u32[]{:S(2)}, u32[]{:S(2)}) collective-permute-start(bf16[1536,512]{1,0:T(8,128)(2,1)} %get-tuple-element.215.refs_5_), channel_id=1, source_target_pairs={{0,8},{8,0},{16,24},{24,16},{1,9},{9,1},{17,25},{25,17},{2,10},{10... | collective-permute-start | bytes 4718600 | tf_op jit(solution)/shard_map/ppermute | solution.py:24
  360.9 31.9 %collective-permute-start.26 = (bf16[768,512]{1,0:T(8,128)(2,1)S(1)}, bf16[768,512]{1,0:T(8,128)(2,1)S(1)}, u32[]{:S(2)}, u32[]{:S(2)}) collective-permute-start(bf16[768,512]{1,0:T(8,128)(2,1)S(1)} %get-tuple-element.337), channel_id=1, source_target_pairs={{0,16},{8,24},{16,0},{24,8},{1,17},{9,25},{17,1},{25,9},{2,18},{10... | collective-permute-start | bytes 2359304 | tf_op jit(solution)/shard_map/ppermute | solution.py:24
  362.3 30.4 %collective-permute-start.25 = (bf16[768,512]{1,0:T(8,128)(2,1)S(1)}, bf16[768,512]{1,0:T(8,128)(2,1)S(1)}, u32[]{:S(2)}, u32[]{:S(2)}) collective-permute-start(bf16[768,512]{1,0:T(8,128)(2,1)S(1)} %get-tuple-element.338), channel_id=1, source_target_pairs={{0,8},{8,0},{16,24},{24,16},{1,9},{9,1},{17,25},{25,17},{2,10},{10... | collective-permute-start | bytes 2359304 | tf_op jit(solution)/shard_map/ppermute | solution.py:24
  366.0 30.2 %collective-permute-start.30 = (bf16[768,512]{1,0:T(8,128)(2,1)S(1)}, bf16[768,512]{1,0:T(8,128)(2,1)S(1)}, u32[]{:S(2)}, u32[]{:S(2)}) collective-permute-start(bf16[768,512]{1,0:T(8,128)(2,1)S(1)} %slice.294), channel_id=1, source_target_pairs={{0,8},{8,0},{16,24},{24,16},{1,9},{9,1},{17,25},{25,17},{2,10},{10... | collective-permute-start | bytes 2359304 | tf_op jit(solution)/shard_map/ppermute | solution.py:24
  369.3 26.9 %collective-permute-start.29 = (bf16[768,512]{1,0:T(8,128)(2,1)S(1)}, bf16[768,512]{1,0:T(8,128)(2,1)S(1)}, u32[]{:S(2)}, u32[]{:S(2)}) collective-permute-start(bf16[768,512]{1,0:T(8,128)(2,1)S(1)} %slice.293), channel_id=1, source_target_pairs={{0,16},{8,24},{16,0},{24,8},{1,17},{9,25},{17,1},{25,9},{2,18},{10... | collective-permute-start | bytes 2359304 | tf_op jit(solution)/shard_map/ppermute | solution.py:24
  423.9 192.2 %reduce-scatter.9.cloned.1.call-start = ((), (), s32[]{:S(2)}) async-start(), calls=%async_computation.12 | async-start | bytes 8257536 | tf_op jit(solution)/shard_map/reduce_scatter | solution.py:845
  424.0 30.4 %collective-permute-start.27 = (bf16[1536,512]{1,0:T(8,128)(2,1)}, bf16[1536,512]{1,0:T(8,128)(2,1)S(1)}, u32[]{:S(2)}, u32[]{:S(2)}) collective-permute-start(bf16[1536,512]{1,0:T(8,128)(2,1)} %copy-done.70), channel_id=1, source_target_pairs={{0,8},{8,0},{16,24},{24,16},{1,9},{9,1},{17,25},{25,17},{2,10},{10... | collective-permute-start | bytes 4718600 | tf_op jit(solution)/shard_map/ppermute | solution.py:24
  425.3 30.3 %collective-permute-start.28 = (bf16[1536,512]{1,0:T(8,128)(2,1)S(1)}, bf16[1536,512]{1,0:T(8,128)(2,1)S(1)}, u32[]{:S(2)}, u32[]{:S(2)}) collective-permute-start(bf16[1536,512]{1,0:T(8,128)(2,1)S(1)} %copy-done.69), channel_id=1, source_target_pairs={{0,16},{8,24},{16,0},{24,8},{1,17},{9,25},{17,1},{25,9},{2,18},{10... | collective-permute-start | bytes 4718600 | tf_op jit(solution)/shard_map/ppermute | solution.py:24
  472.8 21.1 %collective-permute-start.31 = (bf16[192,2048]{1,0:T(8,128)(2,1)S(1)}, bf16[192,2048]{1,0:T(8,128)(2,1)S(1)}, u32[]{:S(2)}, u32[]{:S(2)}) collective-permute-start(bf16[192,2048]{1,0:T(8,128)(2,1)S(1)} %get-tuple-element.227), channel_id=1, source_target_pairs={{0,8},{8,0},{16,24},{24,16},{1,9},{9,1},{17,25},{25,17},{2,10},{10... | collective-permute-start | bytes 2359304 | tf_op jit(solution)/shard_map/ppermute | solution.py:24
  474.3 19.6 %collective-permute-start.32 = (bf16[192,2048]{1,0:T(8,128)(2,1)S(1)}, bf16[192,2048]{1,0:T(8,128)(2,1)S(1)}, u32[]{:S(2)}, u32[]{:S(2)}) collective-permute-start(bf16[192,2048]{1,0:T(8,128)(2,1)S(1)} %get-tuple-element.228), channel_id=1, source_target_pairs={{0,16},{8,24},{16,0},{24,8},{1,17},{9,25},{17,1},{25,9},{2,18},{10... | collective-permute-start | bytes 2359304 | tf_op jit(solution)/shard_map/ppermute | solution.py:24
  515.1 161.2 %reduce-scatter.11.cloned.1.call-start = ((), (), s32[]{:S(2)}) async-start(), calls=%async_computation.13 | async-start | bytes 2359296 | tf_op jit(solution)/shard_map/reduce_scatter | solution.py:845
  515.1 30.6 %collective-permute-start.33 = (bf16[384,2048]{1,0:T(8,128)(2,1)}, bf16[384,2048]{1,0:T(8,128)(2,1)}, u32[]{:S(2)}, u32[]{:S(2)}) collective-permute-start(bf16[384,2048]{1,0:T(8,128)(2,1)} %copy-done.72), channel_id=1, source_target_pairs={{0,8},{8,0},{16,24},{24,16},{1,9},{9,1},{17,25},{25,17},{2,10},{10... | collective-permute-start | bytes 4718600 | tf_op jit(solution)/shard_map/ppermute | solution.py:24
  515.8 30.1 %collective-permute-start.34 = (bf16[384,2048]{1,0:T(8,128)(2,1)}, bf16[384,2048]{1,0:T(8,128)(2,1)}, u32[]{:S(2)}, u32[]{:S(2)}) collective-permute-start(bf16[384,2048]{1,0:T(8,128)(2,1)} %copy-done.71), channel_id=1, source_target_pairs={{0,16},{8,24},{16,0},{24,8},{1,17},{9,25},{17,1},{25,9},{2,18},{10... | collective-permute-start | bytes 4718600 | tf_op jit(solution)/shard_map/ppermute | solution.py:24
  555.5 33.2 %collective-permute-start.36 = (bf16[384,2048]{1,0:T(8,128)(2,1)S(1)}, bf16[384,2048]{1,0:T(8,128)(2,1)S(1)}, u32[]{:S(2)}, u32[]{:S(2)}) collective-permute-start(bf16[384,2048]{1,0:T(8,128)(2,1)S(1)} %get-tuple-element.247), channel_id=1, source_target_pairs={{0,16},{8,24},{16,0},{24,8},{1,17},{9,25},{17,1},{25,9},{2,18},{10... | collective-permute-start | bytes 4718600 | tf_op jit(solution)/shard_map/ppermute | solution.py:24
  556.2 34.0 %collective-permute-start.35 = (bf16[384,2048]{1,0:T(8,128)(2,1)S(1)}, bf16[384,2048]{1,0:T(8,128)(2,1)S(1)}, u32[]{:S(2)}, u32[]{:S(2)}) collective-permute-start(bf16[384,2048]{1,0:T(8,128)(2,1)S(1)} %get-tuple-element.247), channel_id=1, source_target_pairs={{0,8},{8,0},{16,24},{24,16},{1,9},{9,1},{17,25},{25,17},{2,10},{10... | collective-permute-start | bytes 4718600 | tf_op jit(solution)/shard_map/ppermute | solution.py:24
  590.4 12.1 %collective-permute-start.38 = (bf16[192,2048]{1,0:T(8,128)(2,1)S(1)}, bf16[192,2048]{1,0:T(8,128)(2,1)S(1)}, u32[]{:S(2)}, u32[]{:S(2)}) collective-permute-start(bf16[192,2048]{1,0:T(8,128)(2,1)S(1)} %slice.296), channel_id=1, source_target_pairs={{0,8},{8,0},{16,24},{24,16},{1,9},{9,1},{17,25},{25,17},{2,10},{10... | collective-permute-start | bytes 2359304 | tf_op jit(solution)/shard_map/ppermute | solution.py:24
  592.1 12.0 %collective-permute-start.37 = (bf16[192,2048]{1,0:T(8,128)(2,1)S(1)}, bf16[192,2048]{1,0:T(8,128)(2,1)S(1)}, u32[]{:S(2)}, u32[]{:S(2)}) collective-permute-start(bf16[192,2048]{1,0:T(8,128)(2,1)S(1)} %slice.295), channel_id=1, source_target_pairs={{0,16},{8,24},{16,0},{24,8},{1,17},{9,25},{17,1},{25,9},{2,18},{10... | collective-permute-start | bytes 2359304 | tf_op jit(solution)/shard_map/ppermute | solution.py:24
  610.8 151.2 %reduce-scatter.15.cloned.1.call-start = ((), (), s32[]{:S(2)}) async-start(), calls=%async_computation.15 | async-start | bytes 2359296 | tf_op jit(solution)/shard_map/reduce_scatter | solution.py:845
  611.5 173.3 %reduce-scatter.17.cloned.1.call-start = ((), (), s32[]{:S(2)}) async-start(), calls=%async_computation.16 | async-start | bytes 4718592 | tf_op jit(solution)/shard_map/reduce_scatter | solution.py:845
  617.7 40.7 %collective-permute-start.41 = (bf16[384,512]{1,0:T(8,128)(2,1)S(1)}, bf16[384,512]{1,0:T(8,128)(2,1)S(1)}, u32[]{:S(2)}, u32[]{:S(2)}) collective-permute-start(bf16[384,512]{1,0:T(8,128)(2,1)S(1)} %get-tuple-element.333), channel_id=1, source_target_pairs={{0,24},{8,16},{16,8},{24,0},{1,25},{9,17},{17,9},{25,1},{2,26},{10... | collective-permute-start | bytes 1179656 | tf_op jit(solution)/shard_map/ppermute | solution.py:24
  619.0 39.4 %collective-permute-start.40 = (bf16[384,512]{1,0:T(8,128)(2,1)S(1)}, bf16[384,512]{1,0:T(8,128)(2,1)S(1)}, u32[]{:S(2)}, u32[]{:S(2)}) collective-permute-start(bf16[384,512]{1,0:T(8,128)(2,1)S(1)} %get-tuple-element.334), channel_id=1, source_target_pairs={{0,16},{8,24},{16,0},{24,8},{1,17},{9,25},{17,1},{25,9},{2,18},{10... | collective-permute-start | bytes 1179656 | tf_op jit(solution)/shard_map/ppermute | solution.py:24
  619.5 38.9 %collective-permute-start.39 = (bf16[384,512]{1,0:T(8,128)(2,1)S(1)}, bf16[384,512]{1,0:T(8,128)(2,1)S(1)}, u32[]{:S(2)}, u32[]{:S(2)}) collective-permute-start(bf16[384,512]{1,0:T(8,128)(2,1)S(1)} %get-tuple-element.335), channel_id=1, source_target_pairs={{0,8},{8,0},{16,24},{24,16},{1,9},{9,1},{17,25},{25,17},{2,10},{10... | collective-permute-start | bytes 1179656 | tf_op jit(solution)/shard_map/ppermute | solution.py:24
  675.5 127.9 %reduce-scatter.13.cloned.1.call-start = ((), (), s32[]{:S(2)}) async-start(), calls=%async_computation.14 | async-start | bytes 4718592 | tf_op jit(solution)/shard_map/reduce_scatter | solution.py:845
  686.2 19.3 %collective-permute-start.42 = (bf16[192,2048]{1,0:T(8,128)(2,1)S(1)}, bf16[192,2048]{1,0:T(8,128)(2,1)S(1)}, u32[]{:S(2)}, u32[]{:S(2)}) collective-permute-start(bf16[192,2048]{1,0:T(8,128)(2,1)S(1)} %get-tuple-element.272), channel_id=1, source_target_pairs={{0,8},{8,0},{16,24},{24,16},{1,9},{9,1},{17,25},{25,17},{2,10},{10... | collective-permute-start | bytes 2359304 | tf_op jit(solution)/shard_map/ppermute | solution.py:24
  686.2 19.2 %collective-permute-start.43 = (bf16[192,2048]{1,0:T(8,128)(2,1)S(1)}, bf16[192,2048]{1,0:T(8,128)(2,1)S(1)}, u32[]{:S(2)}, u32[]{:S(2)}) collective-permute-start(bf16[192,2048]{1,0:T(8,128)(2,1)S(1)} %get-tuple-element.273), channel_id=1, source_target_pairs={{0,16},{8,24},{16,0},{24,8},{1,17},{9,25},{17,1},{25,9},{2,18},{10... | collective-permute-start | bytes 2359304 | tf_op jit(solution)/shard_map/ppermute | solution.py:24
  725.2 25.9 %collective-permute-start.44 = (bf16[384,2048]{1,0:T(8,128)(2,1)}, bf16[384,2048]{1,0:T(8,128)(2,1)}, u32[]{:S(2)}, u32[]{:S(2)}) collective-permute-start(bf16[384,2048]{1,0:T(8,128)(2,1)} %copy-done.67), channel_id=1, source_target_pairs={{0,8},{8,0},{16,24},{24,16},{1,9},{9,1},{17,25},{25,17},{2,10},{10... | collective-permute-start | bytes 4718600 | tf_op jit(solution)/shard_map/ppermute | solution.py:24
  727.0 24.3 %collective-permute-start.45 = (bf16[384,2048]{1,0:T(8,128)(2,1)}, bf16[384,2048]{1,0:T(8,128)(2,1)}, u32[]{:S(2)}, u32[]{:S(2)}) collective-permute-start(bf16[384,2048]{1,0:T(8,128)(2,1)} %copy-done.66), channel_id=1, source_target_pairs={{0,16},{8,24},{16,0},{24,8},{1,17},{9,25},{17,1},{25,9},{2,18},{10... | collective-permute-start | bytes 4718600 | tf_op jit(solution)/shard_map/ppermute | solution.py:24
  759.1 11.7 %collective-permute-start.52 = (f32[16,14,64]{2,1,0:T(8,128)S(1)}, f32[16,14,64]{2,1,0:T(8,128)S(1)}, u32[]{:S(2)}, u32[]{:S(2)}) collective-permute-start(f32[16,14,64]{2,1,0:T(8,128)S(1)} %bitcast.114), channel_id=1, source_target_pairs={{0,4},{1,5},{2,6},{3,7},{4,0},{5,1},{6,2},{7,3},{8,12},{9,13},{10,... | collective-permute-start | bytes 172040 | tf_op jit(solution)/shard_map/ppermute | solution.py:24
  770.8 6.3 collective-permute-start.53
  779.5 18.0 %collective-permute-start.48 = (bf16[64,2304]{1,0:T(8,128)(2,1)S(1)}, bf16[64,2304]{1,0:T(8,128)(2,1)S(1)}, u32[]{:S(2)}, u32[]{:S(2)}) collective-permute-start(bf16[64,2304]{1,0:T(8,128)(2,1)S(1)} %get-tuple-element.341), channel_id=1, source_target_pairs={{0,24},{8,16},{16,8},{24,0},{1,25},{9,17},{17,9},{25,1},{2,26},{10... | collective-permute-start | bytes 884744 | tf_op jit(solution)/shard_map/ppermute | solution.py:24
  781.6 18.1 %collective-permute-start.47 = (bf16[64,2304]{1,0:T(8,128)(2,1)S(1)}, bf16[64,2304]{1,0:T(8,128)(2,1)S(1)}, u32[]{:S(2)}, u32[]{:S(2)}) collective-permute-start(bf16[64,2304]{1,0:T(8,128)(2,1)S(1)} %get-tuple-element.342), channel_id=1, source_target_pairs={{0,16},{8,24},{16,0},{24,8},{1,17},{9,25},{17,1},{25,9},{2,18},{10... | collective-permute-start | bytes 884744 | tf_op jit(solution)/shard_map/ppermute | solution.py:24
  782.7 17.0 %collective-permute-start.46 = (bf16[64,2304]{1,0:T(8,128)(2,1)S(1)}, bf16[64,2304]{1,0:T(8,128)(2,1)S(1)}, u32[]{:S(2)}, u32[]{:S(2)}) collective-permute-start(bf16[64,2304]{1,0:T(8,128)(2,1)S(1)} %get-tuple-element.343), channel_id=1, source_target_pairs={{0,8},{8,0},{16,24},{24,16},{1,9},{9,1},{17,25},{25,17},{2,10},{10... | collective-permute-start | bytes 884744 | tf_op jit(solution)/shard_map/ppermute | solution.py:24
  783.0 13.5 %collective-permute-start.56 = (f32[1,14,64]{2,1,0:T(8,128)S(1)}, f32[1,14,64]{2,1,0:T(8,128)S(1)}, u32[]{:S(2)}, u32[]{:S(2)}) collective-permute-start(f32[1,14,64]{2,1,0:T(8,128)S(1)} %slice_select_fusion.5), channel_id=1, source_target_pairs={{0,8},{8,0},{16,24},{24,16},{1,9},{9,1},{17,25},{25,17},{2,10},{10... | collective-permute-start | bytes 10760 | tf_op jit(solution)/shard_map/ppermute | solution.py:24
  785.9 15.3 %collective-permute-start.51 = (bf16[64,1024]{1,0:T(8,128)(2,1)S(1)}, bf16[64,1024]{1,0:T(8,128)(2,1)S(1)}, u32[]{:S(2)}, u32[]{:S(2)}) collective-permute-start(bf16[64,1024]{1,0:T(8,128)(2,1)S(1)} %get-tuple-element.349), channel_id=1, source_target_pairs={{0,24},{8,16},{16,8},{24,0},{1,25},{9,17},{17,9},{25,1},{2,26},{10... | collective-permute-start | bytes 393224 | tf_op jit(solution)/shard_map/ppermute | solution.py:24
  804.5 6.0 collective-permute-start.59
  806.6 5.3 collective-permute-start.58
  (122 other events, 1025.5 us)
Sparse Core Ops, SparseCore 0:
  33.0 67.9 all-gather.7
  103.3 27.8 all-gather.5
  132.7 28.6 all-gather.9
  170.8 91.1 all-gather.11
  263.6 71.8 all-gather.13
  424.0 79.9 reduce-scatter.6
  515.2 80.0 reduce-scatter.8
  610.9 36.6 reduce-scatter.10
  649.9 34.4 reduce-scatter.14
  686.5 48.8 reduce-scatter.16
  737.7 52.3 reduce-scatter.12

commit v10 on v9

--- a/solution.py
+++ b/solution.py
@@ -897,19 +897,21 @@
     if seq == 4:
         pieces_c = after(pieces_c, mixed)
         columns_c = stack_below(pieces_c, here)
-        grad_all = gather_second(grad_b, *pieces_c[1:3])
     full_c = gather_dp(columns_c)
     full_ck, full_cr = full_c[:, :hidden_width], full_c[:, hidden_width:]
     full_cv = gather_dp(after(ffn_value, columns_c))
     attn = [dot(rows, own_o, NN).astype(BF) for rows in blocks_of(mixed, seq)]
-    after_mix, normed_two = after_norm(inputs_b, after(scatter_seq(attn, here), grad_all[3:]), rows_of(vec, 10, 11), here)
-
+    after_mix, normed_two = after_norm(inputs_b, scatter_seq(attn, here), rows_of(vec, 10, 11), here)
+
+    normed_two = gather_seq(normed_two)
+    if seq == 4:
+        grad_all = gather_second(grad_b, *after(pieces_c[1:3], normed_two))
     mix_k2, mix_r2, step_two = mixes(
-        turn_pieces(gather_seq(normed_two)), marks, rows_of(turned, 10, 11, 12, 13), 2, False, within, here, tile,
+        turn_pieces(normed_two), marks, rows_of(turned, 10, 11, 12, 13), 2, False, within, here, tile,
         own_rows // tile,
     )
     recept_pre = dot(mix_r2, full_cr, NN)
-    opened = gather_seq(jax.nn.sigmoid(recept_pre).astype(BF))
+    opened = gather_seq(after(jax.nn.sigmoid(recept_pre).astype(BF), grad_all[3:]))
     key_pre = dot(mix_k2, full_ck, NN)
     smooth = jax.nn.softplus(key_pre)
     hidden = (smooth * smooth).astype(BF)

time: 827 us -> 815 us (0.985)
    unnamed x232 -> x236, local copies, waits for them, and re-layouts: 46.5 us -> 43.7 us
  transfers between devices with their start and end apart: 71 -> 71, of which waited for: 38 -> 38; matrix products, arithmetic and copies ran while one was open for 23% -> 24% of each run, Pallas kernels for 28% -> 28%
where the time goes in v10:
time: 815 us; the launch traced here: 809 us
  Pallas kernels  239 us (29%)
  waiting for transfers between devices  227 us (28%)
  matrix products  168 us (21%)
  starting transfers between devices  72.4 us (9%)
  local copies, waits for them, and re-layouts  69.5 us (9%)
  other arithmetic  18 us (2%)
  between operations  15.6 us (2%)
    pallas_call x33, Pallas kernels, kernel(): pl.pallas_call(body, out_shape=[jax.ShapeDtypeStruct(shape, kind) for sha...  239 us
    ppermute x60, waiting for transfers between devices, swap(): return lax.ppermute(value, axis, [(i, i ^ distance) for i in range(size)])  225 us
    dot_general x25, matrix products, dot(): return lax.dot_general(left, right, dims, preferred_element_type=F32)  168 us
    ppermute x60, starting transfers between devices, swap(): return lax.ppermute(value, axis, [(i, i ^ distance) for i in range(size)])  70.8 us
    unnamed x236, local copies, waits for them, and re-layouts  43.7 us
  transfers between devices with their start and end apart: 71, of which 38 were waited for; matrix products, arithmetic and copies ran while one was open for 24% of the time, Pallas kernels for 28%

profile of v10, /device:TPU:0, one launch (start us, length us, event | category | flops | bytes accessed | tf_op | source)
XLA Modules:
  0.0 808.6 jit_solution(14782970660117359161)
XLA Ops:
  11.9 3.0 collective-permute-start
  18.6 4.8 collective-permute-done.refs_1_
  23.5 8.4 %collective-permute-done.1.refs_2_ = bf16[80,2048]{1,0:T(8,128)(2,1)S(1)} collective-permute-done((bf16[80,2048]{1,0:T(8,128)(2,1)S(1)}, bf16[80,2048]{1,0:T(8,128)(2,1)S(1)}, u32[]{:S(2)}, u32[]{:S(2)}) %collective-permute-start.1) | collective-permute-done | bytes 327712 | tf_op jit(solution)/shard_map/ppermute | solution.py:24
  44.6 3.1 collective-permute-start.5
  49.3 6.1 collective-permute-done.5
  59.7 11.3 %collective-permute-done.7.refs_2_ = bf16[384,2048]{1,0:T(8,128)(2,1)} collective-permute-done((bf16[384,2048]{1,0:T(8,128)(2,1)S(1)}, bf16[384,2048]{1,0:T(8,128)(2,1)}, u32[]{:S(2)}, u32[]{:S(2)}) %collective-permute-start.7) | collective-permute-done | bytes 1572896 | tf_op jit(solution)/shard_map/ppermute | solution.py:24
  76.3 15.6 %collective-permute-done.9.refs_4_ = bf16[192,2048]{1,0:T(8,128)(2,1)S(1)} collective-permute-done((bf16[192,2048]{1,0:T(8,128)(2,1)S(1)}, bf16[192,2048]{1,0:T(8,128)(2,1)S(1)}, u32[]{:S(2)}, u32[]{:S(2)}) %collective-permute-start.9) | collective-permute-done | bytes 786464 | tf_op jit(solution)/shard_map/ppermute | solution.py:24
  95.8 17.6 %mixes.2 = (bf16[1536,2048]{1,0:T(8,128)(2,1)}, bf16[1536,2048]{1,0:T(8,128)(2,1)}, bf16[1536,2048]{1,0:T(8,128)(2,1)}, bf16[1536,2048]{1,0:T(8,128)(2,1)}, bf16[1536,2048]{1,0:T(8,128)(2,1)}) custom-call(s32[1]{0:T(128)} %bitcast.here, bf16[384,2048]{1,0:T(8,128)(2,1)S(1)} %copy-done.13, bf16[384,2048]{1,0:T(8,128)(2,1)} %collective-permute-done.6.refs_1_, ...), custom_call_target="tpu_custom_call" | custom-call | tf_op jit(solution)/shard_map/mixes/pallas_call | solution.py:134
  113.4 2.4 cut_columns.3
  119.5 7.0 convolution_convert_fusion.9.r_ref
  126.6 7.9 convolution_convert_fusion.8.k_ref
  134.6 4.5 convolution_convert_fusion.7.v_ref
  139.1 13.5 %wkv_forward.1 = (f32[1536,512]{1,0:T(8,128)}, bf16[12,512,128]{2,1,0:T(8,128)(2,1)S(1)}) custom-call(s32[1]{0:T(128)} %bitcast.here, bf16[1536,512]{1,0:T(8,128)(2,1)S(1)} %convolution_convert_fusion.9.r_ref, bf16[1536,512]{1,0:T(8,128)(2,1)} %convolution_convert_fusion.8.k_ref, bf16[1536,512]{1,0:T(8,128)(2,1)} %convolution_convert_fusion.7.v_ref, ...), custom_call_target="tpu_custom_call" | custom-call | tf_op jit(solution)/shard_map/wkv_forward/pallas_call | solution.py:134
  155.4 10.1 %gate.1 = (f32[1536,512]{1,0:T(8,128)}, bf16[1536,512]{1,0:T(8,128)(2,1)S(1)}) custom-call(s32[1]{0:T(128)} %bitcast.here, bf16[1536,2048]{1,0:T(8,128)(2,1)} %get-tuple-element.263.refs_0_, bf16[2048,512]{1,0:T(8,128)(2,1)S(1)} %copy-done.4, f32[1536,512]{1,0:T(8,128)} %get-tuple-element.183.refs_2_.wkv_ref, f32[8,512]{1,0:T(8,128)S(1)} %maximum_maximum_fusion.par_ref.refs_3_), custom_call_target="tpu_custom_call" | custom-call | tf_op jit(solution)/shard_map/gate/pallas_call | solution.py:134
  167.3 3.3 stack_rows.3
  171.7 2.8 convolution_convert_fusion.10
  181.3 11.0 %collective-permute-done.11.high_ref = bf16[192,2048]{1,0:T(8,128)(2,1)S(1)} collective-permute-done((bf16[192,2048]{1,0:T(8,128)(2,1)S(1)}, bf16[192,2048]{1,0:T(8,128)(2,1)S(1)}, u32[]{:S(2)}, u32[]{:S(2)}) %collective-permute-start.11) | collective-permute-done | bytes 786464 | tf_op jit(solution)/shard_map/ppermute | solution.py:24
  193.7 3.3 relay.4
  200.4 2.8 convolution_convert_fusion.13.refs_0_
  203.2 27.7 %collective-permute-done.12.refs_1_ = bf16[384,2048]{1,0:T(8,128)(2,1)} collective-permute-done((bf16[384,2048]{1,0:T(8,128)(2,1)}, bf16[384,2048]{1,0:T(8,128)(2,1)}, u32[]{:S(2)}, u32[]{:S(2)}) %collective-permute-start.12) | collective-permute-done | bytes 1572896 | tf_op jit(solution)/shard_map/ppermute | solution.py:24
  231.0 4.7 after_norm.1
  238.1 30.4 %collective-permute-done.15.refs_2_ = bf16[384,2048]{1,0:T(8,128)(2,1)S(1)} collective-permute-done((bf16[384,2048]{1,0:T(8,128)(2,1)S(1)}, bf16[384,2048]{1,0:T(8,128)(2,1)S(1)}, u32[]{:S(2)}, u32[]{:S(2)}) %collective-permute-start.15) | collective-permute-done | bytes 1572896 | tf_op jit(solution)/shard_map/ppermute | solution.py:24
  278.6 8.7 %collective-permute-done.17.refs_4_ = bf16[192,2048]{1,0:T(8,128)(2,1)S(1)} collective-permute-done((bf16[192,2048]{1,0:T(8,128)(2,1)}, bf16[192,2048]{1,0:T(8,128)(2,1)S(1)}, u32[]{:S(2)}, u32[]{:S(2)}) %collective-permute-start.17) | collective-permute-done | bytes 786464 | tf_op jit(solution)/shard_map/ppermute | solution.py:24
  295.6 12.0 %mixes.3 = (bf16[1536,2048]{1,0:T(8,128)(2,1)}, bf16[1536,2048]{1,0:T(8,128)(2,1)}, bf16[1536,2048]{1,0:T(8,128)(2,1)}) custom-call(s32[1]{0:T(128)} %bitcast.here, bf16[384,2048]{1,0:T(8,128)(2,1)S(1)} %copy-done.28, bf16[384,2048]{1,0:T(8,128)(2,1)S(1)} %copy-done.18, bf16[384,2048]{1,0:T(8,128)(2,1)} %copy-done.79, ...), custom_call_target="tpu_custom_call" | custom-call | tf_op jit(solution)/shard_map/mixes/pallas_call | solution.py:134
  307.6 9.6 %divide_convert_fusion = (bf16[1536,512]{1,0:T(8,128)(2,1)}, f32[1536,512]{1,0:T(8,128)}) fusion(bf16[1536,2048]{1,0:T(8,128)(2,1)} %get-tuple-element.243, bf16[2048,2304]{1,0:T(8,128)(2,1)} %all-gather.12.cloned.1.call-done.refs_6_.refs_7_.refs_8_), kind=kOutput, calls=%fused_computation.12 | convolution fusion | flops 3224371200 | bytes 13107200 | tf_op jit(solution)/shard_map/dot_general | solution.py:620
  319.8 22.8 %multiply_convert_fusion.1 = (bf16[1536,1792]{1,0:T(8,128)(2,1)}, bf16[1536,1792]{1,0:T(8,128)(2,1)}) fusion(bf16[1536,2048]{1,0:T(8,128)(2,1)} %get-tuple-element.242, bf16[2048,2304]{1,0:T(8,128)(2,1)S(1)} %copy-done.75), kind=kOutput, calls=%fused_computation.2 | convolution fusion | flops 11312824320 | bytes 24641536 | tf_op jit(solution)/shard_map/dot_general | solution.py:620
  342.5 6.0 value_columns.7
  355.9 6.0 value_columns.6.two_ref
  363.1 6.0 value_columns.5.one_ref
  370.3 6.0 value_columns.4.refs_5_
  383.2 9.7 %spread_columns.2 = bf16[1536,2048]{1,0:T(8,128)(2,1)} custom-call(s32[1]{0:T(128)} %bitcast.here, bf16[384,2048]{1,0:T(8,128)(2,1)S(1)} %bitcast.100, bf16[448,2304]{1,0:T(8,128)(2,1)} %collective-permute-done.18.refs_1_, bf16[448,2304]{1,0:T(8,128)(2,1)} %collective-permute-done.19.refs_2_, bf16[192,2048]{1,0:T(8,128)(2,1)} %collective-permute-done.21.refs_3_, ...), custom_call_target="tpu_custom_call" | custom-call | tf_op jit(solution)/shard_map/spread_columns/pallas_call | solution.py:134
  392.9 16.1 %convolution_convert_fusion.1 = bf16[1792,2048]{1,0:T(8,128)(2,1)} fusion(bf16[1536,1792]{1,0:T(8,128)(2,1)S(1)} %bitcast.108, bf16[1536,2048]{1,0:T(8,128)(2,1)} %spread_columns.2), kind=kOutput, calls=%fused_computation.5 | convolution fusion | flops 11277959168 | bytes 19136512 | tf_op jit(solution)/shard_map/dot_general | solution.py:620
  411.6 18.1 %multiply_convert_fusion.refs_0_.refs_3_ = bf16[1536,1792]{1,0:T(8,128)(2,1)} fusion(bf16[1536,1792]{1,0:T(8,128)(2,1)} %get-tuple-element.221, bf16[1536,2048]{1,0:T(8,128)(2,1)} %spread_columns.2, bf16[1792,2048]{1,0:T(8,128)(2,1)} %all-gather.14.cloned.1.call-done.right_ref), kind=kOutput, calls=%fused_computation.1 | convolution fusion | flops 11282546688 | bytes 24641536 | tf_op jit(solution)/shard_map/dot_general | solution.py:620
  429.7 11.4 %collective-permute-done.27.refs_6_ = bf16[1536,512]{1,0:T(8,128)(2,1)S(1)} collective-permute-done((bf16[1536,512]{1,0:T(8,128)(2,1)}, bf16[1536,512]{1,0:T(8,128)(2,1)S(1)}, u32[]{:S(2)}, u32[]{:S(2)}) %collective-permute-start.27) | collective-permute-done | bytes 1572896 | tf_op jit(solution)/shard_map/ppermute | solution.py:24
  443.6 6.9 channel.1
  450.5 9.0 %mixes_back.6 = (bf16[192,2048]{1,0:T(8,128)(2,1)S(1)}, bf16[192,2048]{1,0:T(8,128)(2,1)S(1)}, f32[8,2048]{1,0:T(8,128)S(1)}) custom-call(s32[1]{0:T(128)} %bitcast.here, bf16[1536,1792]{1,0:T(8,128)(2,1)} %multiply_convert_fusion.refs_0_.refs_3_, bf16[1536,512]{1,0:T(8,128)(2,1)S(1)} %get-tuple-element.240.refs_1_.refs_2_.refs_4_.refs_5_, ...), custom_call_target="tpu_custom_call" | custom-call | tf_op jit(solution)/shard_map/mixes_back/pallas_call | solution.py:134
  462.3 16.1 %mixes_back.7 = (bf16[384,2048]{1,0:T(8,128)(2,1)S(1)}, bf16[384,2048]{1,0:T(8,128)(2,1)S(1)}, f32[8,2048]{1,0:T(8,128)S(1)}) custom-call(s32[1]{0:T(128)} %bitcast.here, bf16[1536,1792]{1,0:T(8,128)(2,1)} %multiply_convert_fusion.refs_0_.refs_3_, bf16[1536,512]{1,0:T(8,128)(2,1)S(1)} %get-tuple-element.240.refs_1_.refs_2_.refs_4_.refs_5_, ...), custom_call_target="tpu_custom_call" | custom-call | tf_op jit(solution)/shard_map/mixes_back/pallas_call | solution.py:134
  480.8 2.4 relay.6
  485.7 16.3 %convolution_convert_fusion = bf16[2048,1792]{1,0:T(8,128)(2,1)} fusion(bf16[1536,2048]{1,0:T(8,128)(2,1)} %get-tuple-element.242, bf16[1536,1792]{1,0:T(8,128)(2,1)S(1)} %bitcast.106), kind=kOutput, calls=%fused_computation.4 | convolution fusion | flops 11277959168 | bytes 19136512 | tf_op jit(solution)/shard_map/dot_general | solution.py:620
  503.6 8.9 %mixes_back.8 = (bf16[384,2048]{1,0:T(8,128)(2,1)S(1)}, f32[8,2048]{1,0:T(8,128)S(1)}) custom-call(s32[1]{0:T(128)} %bitcast.here, bf16[1536,1792]{1,0:T(8,128)(2,1)} %multiply_convert_fusion.refs_0_.refs_3_, bf16[1536,512]{1,0:T(8,128)(2,1)S(1)} %get-tuple-element.240.refs_1_.refs_2_.refs_4_.refs_5_, ...), custom_call_target="tpu_custom_call" | custom-call | tf_op jit(solution)/shard_map/mixes_back/pallas_call | solution.py:134
  513.7 7.7 convolution_convert_fusion.6
  521.4 11.9 %collective-permute-done.33.refs_1_ = bf16[384,2048]{1,0:T(8,128)(2,1)} collective-permute-done((bf16[384,2048]{1,0:T(8,128)(2,1)}, bf16[384,2048]{1,0:T(8,128)(2,1)}, u32[]{:S(2)}, u32[]{:S(2)}) %collective-permute-start.33) | collective-permute-done | bytes 1572896 | tf_op jit(solution)/shard_map/ppermute | solution.py:24
  536.2 6.8 norm_back.2
  547.9 27.8 %collective-permute-done.36 = bf16[384,2048]{1,0:T(8,128)(2,1)S(1)} collective-permute-done((bf16[384,2048]{1,0:T(8,128)(2,1)S(1)}, bf16[384,2048]{1,0:T(8,128)(2,1)S(1)}, u32[]{:S(2)}, u32[]{:S(2)}) %collective-permute-start.36) | collective-permute-done | bytes 1572896 | tf_op jit(solution)/shard_map/ppermute | solution.py:24
  575.8 2.5 collective-permute-done.35
  586.1 3.4 add_add_fusion
  593.4 5.3 add_convert_fusion
  600.1 2.7 convolution_convert_fusion.14
  609.2 37.1 %wkv_backward.1 = (bf16[1536,512]{1,0:T(8,128)(2,1)S(1)}, bf16[1536,512]{1,0:T(8,128)(2,1)S(1)}, bf16[1536,512]{1,0:T(8,128)(2,1)}, bf16[1536,512]{1,0:T(8,128)(2,1)}, f32[8,512]{1,0:T(8,128)S(1)}) custom-call(s32[1]{0:T(128)} %bitcast.here, bf16[1536,512]{1,0:T(8,128)(2,1)} %copy-done.11, bf16[1536,512]{1,0:T(8,128)(2,1)} %convolution_convert_fusion.8.k_ref, ...), custom_call_target="tpu_custom_call" | custom-call | tf_op jit(solution)/shard_map/wkv_backward/pallas_call | solution.py:134
  646.4 7.7 convolution_convert_fusion.4
  654.2 6.7 convolution_convert_fusion.5
  660.9 2.5 pad_maximum_fusion.1
  665.7 8.4 %mixes_back.9 = (bf16[192,2048]{1,0:T(8,128)(2,1)S(1)}, bf16[192,2048]{1,0:T(8,128)(2,1)S(1)}, f32[8,2048]{1,0:T(8,128)S(1)}) custom-call(s32[1]{0:T(128)} %bitcast.here, bf16[1536,512]{1,0:T(8,128)(2,1)S(1)} %get-tuple-element.289.refs_0_.refs_4_, bf16[1536,512]{1,0:T(8,128)(2,1)S(1)} %copy-done.1, bf16[1536,512]{1,0:T(8,128)(2,1)} %get-tuple-element.291.refs_2_.refs_6_, ...), custom_call_target="tpu_custom_call" | custom-call | tf_op jit(solution)/shard_map/mixes_back/pallas_call | solution.py:134
  675.3 15.4 %mixes_back.10 = (bf16[384,2048]{1,0:T(8,128)(2,1)S(1)}, bf16[384,2048]{1,0:T(8,128)(2,1)S(1)}, f32[8,2048]{1,0:T(8,128)S(1)}) custom-call(s32[1]{0:T(128)} %bitcast.here, bf16[1536,512]{1,0:T(8,128)(2,1)S(1)} %get-tuple-element.289.refs_0_.refs_4_, bf16[1536,512]{1,0:T(8,128)(2,1)} %copy-done, bf16[1536,512]{1,0:T(8,128)(2,1)} %get-tuple-element.291.refs_2_.refs_6_, ...), custom_call_target="tpu_custom_call" | custom-call | tf_op jit(solution)/shard_map/mixes_back/pallas_call | solution.py:134
  693.0 2.5 relay.7
  695.5 7.8 convolution_convert_fusion.2
  703.4 6.7 convolution_convert_fusion.3
  710.1 2.6 pad_maximum_fusion
  720.5 8.2 %mixes_back.11 = (bf16[384,2048]{1,0:T(8,128)(2,1)S(1)}, f32[8,2048]{1,0:T(8,128)S(1)}) custom-call(s32[1]{0:T(128)} %bitcast.here, bf16[1536,512]{1,0:T(8,128)(2,1)S(1)} %get-tuple-element.289.refs_0_.refs_4_, bf16[1536,512]{1,0:T(8,128)(2,1)S(1)} %copy-done.3, bf16[1536,512]{1,0:T(8,128)(2,1)} %get-tuple-element.291.refs_2_.refs_6_, ...), custom_call_target="tpu_custom_call" | custom-call | tf_op jit(solution)/shard_map/mixes_back/pallas_call | solution.py:134
  735.3 3.5 collective-permute-done.44.refs_1_
  739.1 7.3 norm_back.3
  749.0 9.3 %collective-permute-done.52 = f32[16,14,64]{2,1,0:T(8,128)S(1)} collective-permute-done((f32[16,14,64]{2,1,0:T(8,128)S(1)}, f32[16,14,64]{2,1,0:T(8,128)S(1)}, u32[]{:S(2)}, u32[]{:S(2)}) %collective-permute-start.52) | collective-permute-done | bytes 57376 | tf_op jit(solution)/shard_map/ppermute | solution.py:24
  759.2 5.6 collective-permute-done.53
  774.6 9.6 %collective-permute-done.56 = f32[1,14,64]{2,1,0:T(8,128)S(1)} collective-permute-done((f32[1,14,64]{2,1,0:T(8,128)S(1)}, f32[1,14,64]{2,1,0:T(8,128)S(1)}, u32[]{:S(2)}, u32[]{:S(2)}) %collective-permute-start.56) | collective-permute-done | bytes 3616 | tf_op jit(solution)/shard_map/ppermute | solution.py:24
  (497 shorter events, 190.3 us)
Async XLA Ops:
  7.2 112.4 %all-gather.8.cloned.1.call-start = ((), (), s32[]{:S(2)}) async-start(), calls=%async_computation.7 | async-start | bytes 7077888 | tf_op jit(solution)/shard_map/all_gather | solution.py:842
  11.9 11.5 %collective-permute-start = (bf16[80,2048]{1,0:T(8,128)(2,1)S(1)}, bf16[80,2048]{1,0:T(8,128)(2,1)S(1)}, u32[]{:S(2)}, u32[]{:S(2)}) collective-permute-start(bf16[80,2048]{1,0:T(8,128)(2,1)S(1)} %get-tuple-element.166.refs_1_), channel_id=1, source_target_pairs={{0,8},{8,0},{16,24},{24,16},{1,9},{9,1},{17,25},{25,17},{2,10},{10... | collective-permute-start | bytes 983048 | tf_op jit(solution)/shard_map/ppermute | solution.py:24
  15.7 16.2 %collective-permute-start.1 = (bf16[80,2048]{1,0:T(8,128)(2,1)S(1)}, bf16[80,2048]{1,0:T(8,128)(2,1)S(1)}, u32[]{:S(2)}, u32[]{:S(2)}) collective-permute-start(bf16[80,2048]{1,0:T(8,128)(2,1)S(1)} %get-tuple-element.167.refs_2_), channel_id=1, source_target_pairs={{0,16},{8,24},{16,0},{24,8},{1,17},{9,25},{17,1},{25,9},{2,18},{10... | collective-permute-start | bytes 983048 | tf_op jit(solution)/shard_map/ppermute | solution.py:24
  17.9 13.9 %collective-permute-start.2 = (bf16[80,2048]{1,0:T(8,128)(2,1)S(1)}, bf16[80,2048]{1,0:T(8,128)(2,1)S(1)}, u32[]{:S(2)}, u32[]{:S(2)}) collective-permute-start(bf16[80,2048]{1,0:T(8,128)(2,1)S(1)} %get-tuple-element.168.refs_3_), channel_id=1, source_target_pairs={{0,24},{8,16},{16,8},{24,0},{1,25},{9,17},{17,9},{25,1},{2,26},{10... | collective-permute-start | bytes 983048 | tf_op jit(solution)/shard_map/ppermute | solution.py:24
  32.9 120.8 %all-gather.6.cloned.1.call-start = ((), (), s32[]{:S(2)}) async-start(), calls=%async_computation.6 | async-start | bytes 2359296 | tf_op jit(solution)/shard_map/all_gather | solution.py:842
  36.1 34.9 %collective-permute-start.7 = (bf16[384,2048]{1,0:T(8,128)(2,1)S(1)}, bf16[384,2048]{1,0:T(8,128)(2,1)}, u32[]{:S(2)}, u32[]{:S(2)}) collective-permute-start(bf16[384,2048]{1,0:T(8,128)(2,1)S(1)} %hold.1.refs_0_), channel_id=1, source_target_pairs={{0,16},{8,24},{16,0},{24,8},{1,17},{9,25},{17,1},{25,9},{2,18},{10... | collective-permute-start | bytes 4718600 | tf_op jit(solution)/shard_map/ppermute | solution.py:24
  37.6 34.8 %collective-permute-start.6 = (bf16[384,2048]{1,0:T(8,128)(2,1)S(1)}, bf16[384,2048]{1,0:T(8,128)(2,1)}, u32[]{:S(2)}, u32[]{:S(2)}) collective-permute-start(bf16[384,2048]{1,0:T(8,128)(2,1)S(1)} %hold.1.refs_0_), channel_id=1, source_target_pairs={{0,8},{8,0},{16,24},{24,16},{1,9},{9,1},{17,25},{25,17},{2,10},{10... | collective-permute-start | bytes 4718600 | tf_op jit(solution)/shard_map/ppermute | solution.py:24
  44.6 10.8 %collective-permute-start.5 = (bf16[4,4,14,64]{3,2,1,0:T(8,128)(2,1)S(1)}, bf16[4,4,14,64]{3,2,1,0:T(8,128)(2,1)S(1)}, u32[]{:S(2)}, u32[]{:S(2)}) collective-permute-start(bf16[4,4,14,64]{3,2,1,0:T(8,128)(2,1)S(1)} %pad_maximum_fusion.6), channel_id=1, source_target_pairs={{0,4},{1,5},{2,6},{3,7},{4,0},{5,1},{6,2},{7,3},{8,12},{9,13},{10,... | collective-permute-start | bytes 86024 | tf_op jit(solution)/shard_map/ppermute | solution.py:24
  72.5 99.3 %all-gather.10.cloned.1.call-start = ((), (), s32[]{:S(2)}) async-start(), calls=%async_computation.8 | async-start | bytes 2359296 | tf_op jit(solution)/shard_map/all_gather | solution.py:842
  75.0 16.9 %collective-permute-start.9 = (bf16[192,2048]{1,0:T(8,128)(2,1)S(1)}, bf16[192,2048]{1,0:T(8,128)(2,1)S(1)}, u32[]{:S(2)}, u32[]{:S(2)}) collective-permute-start(bf16[192,2048]{1,0:T(8,128)(2,1)S(1)} %slice.267), channel_id=1, source_target_pairs={{0,8},{8,0},{16,24},{24,16},{1,9},{9,1},{17,25},{25,17},{2,10},{10... | collective-permute-start | bytes 2359304 | tf_op jit(solution)/shard_map/ppermute | solution.py:24
  75.3 16.6 %collective-permute-start.8 = (bf16[192,2048]{1,0:T(8,128)(2,1)S(1)}, bf16[192,2048]{1,0:T(8,128)(2,1)S(1)}, u32[]{:S(2)}, u32[]{:S(2)}) collective-permute-start(bf16[192,2048]{1,0:T(8,128)(2,1)S(1)} %slice.266), channel_id=1, source_target_pairs={{0,16},{8,24},{16,0},{24,8},{1,17},{9,25},{17,1},{25,9},{2,18},{10... | collective-permute-start | bytes 2359304 | tf_op jit(solution)/shard_map/ppermute | solution.py:24
  92.9 214.7 %all-gather.12.cloned.1.call-start = ((), (), s32[]{:S(2)}) async-start(), calls=%async_computation.9 | async-start | bytes 10616832 | tf_op jit(solution)/shard_map/all_gather | solution.py:842
  115.8 50.9 %collective-permute-start.20 = (bf16[64,2304]{1,0:T(8,128)(2,1)}, bf16[64,2304]{1,0:T(8,128)(2,1)S(1)}, u32[]{:S(2)}, u32[]{:S(2)}) collective-permute-start(bf16[64,2304]{1,0:T(8,128)(2,1)} %get-tuple-element.198), channel_id=1, source_target_pairs={{0,24},{8,16},{16,8},{24,0},{1,25},{9,17},{17,9},{25,1},{2,26},{10... | collective-permute-start | bytes 884744 | tf_op jit(solution)/shard_map/ppermute | solution.py:24
  118.0 49.3 %collective-permute-start.18 = (bf16[448,2304]{1,0:T(8,128)(2,1)}, bf16[448,2304]{1,0:T(8,128)(2,1)}, u32[]{:S(2)}, u32[]{:S(2)}) collective-permute-start(bf16[448,2304]{1,0:T(8,128)(2,1)} %get-tuple-element.196), channel_id=1, source_target_pairs={{0,8},{8,0},{16,24},{24,16},{1,9},{9,1},{17,25},{25,17},{2,10},{10... | collective-permute-start | bytes 6193160 | tf_op jit(solution)/shard_map/ppermute | solution.py:24
  119.1 48.2 %collective-permute-start.19 = (bf16[448,2304]{1,0:T(8,128)(2,1)}, bf16[448,2304]{1,0:T(8,128)(2,1)}, u32[]{:S(2)}, u32[]{:S(2)}) collective-permute-start(bf16[448,2304]{1,0:T(8,128)(2,1)} %get-tuple-element.197), channel_id=1, source_target_pairs={{0,16},{8,24},{16,0},{24,8},{1,17},{9,25},{17,1},{25,9},{2,18},{10... | collective-permute-start | bytes 6193160 | tf_op jit(solution)/shard_map/ppermute | solution.py:24
  170.6 171.9 %all-gather.14.cloned.1.call-start = ((), (), s32[]{:S(2)}) async-start(), calls=%async_computation.10 | async-start | bytes 8257536 | tf_op jit(solution)/shard_map/all_gather | solution.py:842
  171.2 422.1 %reduce-scatter.7.cloned.1.call-start = ((), (), s32[]{:S(2)}) async-start(), calls=%async_computation.11 | async-start | bytes 8257536 | tf_op jit(solution)/shard_map/reduce_scatter | solution.py:845
  174.7 17.6 %collective-permute-start.11 = (bf16[192,2048]{1,0:T(8,128)(2,1)S(1)}, bf16[192,2048]{1,0:T(8,128)(2,1)S(1)}, u32[]{:S(2)}, u32[]{:S(2)}) collective-permute-start(bf16[192,2048]{1,0:T(8,128)(2,1)S(1)} %get-tuple-element.339), channel_id=1, source_target_pairs={{0,16},{8,24},{16,0},{24,8},{1,17},{9,25},{17,1},{25,9},{2,18},{10... | collective-permute-start | bytes 2359304 | tf_op jit(solution)/shard_map/ppermute | solution.py:24
  176.2 17.6 %collective-permute-start.10 = (bf16[192,2048]{1,0:T(8,128)(2,1)S(1)}, bf16[192,2048]{1,0:T(8,128)(2,1)S(1)}, u32[]{:S(2)}, u32[]{:S(2)}) collective-permute-start(bf16[192,2048]{1,0:T(8,128)(2,1)S(1)} %get-tuple-element.340), channel_id=1, source_target_pairs={{0,8},{8,0},{16,24},{24,16},{1,9},{9,1},{17,25},{25,17},{2,10},{10... | collective-permute-start | bytes 2359304 | tf_op jit(solution)/shard_map/ppermute | solution.py:24
  197.0 33.9 %collective-permute-start.12 = (bf16[384,2048]{1,0:T(8,128)(2,1)}, bf16[384,2048]{1,0:T(8,128)(2,1)}, u32[]{:S(2)}, u32[]{:S(2)}) collective-permute-start(bf16[384,2048]{1,0:T(8,128)(2,1)} %get-tuple-element.186), channel_id=1, source_target_pairs={{0,8},{8,0},{16,24},{24,16},{1,9},{9,1},{17,25},{25,17},{2,10},{10... | collective-permute-start | bytes 4718600 | tf_op jit(solution)/shard_map/ppermute | solution.py:24
  197.4 33.6 %collective-permute-start.13 = (bf16[384,2048]{1,0:T(8,128)(2,1)}, bf16[384,2048]{1,0:T(8,128)(2,1)}, u32[]{:S(2)}, u32[]{:S(2)}) collective-permute-start(bf16[384,2048]{1,0:T(8,128)(2,1)} %get-tuple-element.187), channel_id=1, source_target_pairs={{0,16},{8,24},{16,0},{24,8},{1,17},{9,25},{17,1},{25,9},{2,18},{10... | collective-permute-start | bytes 4718600 | tf_op jit(solution)/shard_map/ppermute | solution.py:24
  235.7 32.9 %collective-permute-start.15 = (bf16[384,2048]{1,0:T(8,128)(2,1)S(1)}, bf16[384,2048]{1,0:T(8,128)(2,1)S(1)}, u32[]{:S(2)}, u32[]{:S(2)}) collective-permute-start(bf16[384,2048]{1,0:T(8,128)(2,1)S(1)} %get-tuple-element.189.refs_0_), channel_id=1, source_target_pairs={{0,16},{8,24},{16,0},{24,8},{1,17},{9,25},{17,1},{25,9},{2,18},{10... | collective-permute-start | bytes 4718600 | tf_op jit(solution)/shard_map/ppermute | solution.py:24
  236.4 32.7 %collective-permute-start.14 = (bf16[384,2048]{1,0:T(8,128)(2,1)S(1)}, bf16[384,2048]{1,0:T(8,128)(2,1)S(1)}, u32[]{:S(2)}, u32[]{:S(2)}) collective-permute-start(bf16[384,2048]{1,0:T(8,128)(2,1)S(1)} %get-tuple-element.189.refs_0_), channel_id=1, source_target_pairs={{0,8},{8,0},{16,24},{24,16},{1,9},{9,1},{17,25},{25,17},{2,10},{10... | collective-permute-start | bytes 4718600 | tf_op jit(solution)/shard_map/ppermute | solution.py:24
  272.2 15.2 %collective-permute-start.17 = (bf16[192,2048]{1,0:T(8,128)(2,1)}, bf16[192,2048]{1,0:T(8,128)(2,1)S(1)}, u32[]{:S(2)}, u32[]{:S(2)}) collective-permute-start(bf16[192,2048]{1,0:T(8,128)(2,1)} %slice.278), channel_id=1, source_target_pairs={{0,8},{8,0},{16,24},{24,16},{1,9},{9,1},{17,25},{25,17},{2,10},{10... | collective-permute-start | bytes 2359304 | tf_op jit(solution)/shard_map/ppermute | solution.py:24
  273.6 14.8 %collective-permute-start.16 = (bf16[192,2048]{1,0:T(8,128)(2,1)}, bf16[192,2048]{1,0:T(8,128)(2,1)}, u32[]{:S(2)}, u32[]{:S(2)}) collective-permute-start(bf16[192,2048]{1,0:T(8,128)(2,1)} %slice.277), channel_id=1, source_target_pairs={{0,16},{8,24},{16,0},{24,8},{1,17},{9,25},{17,1},{25,9},{2,18},{10... | collective-permute-start | bytes 2359304 | tf_op jit(solution)/shard_map/ppermute | solution.py:24
  292.6 24.5 %collective-permute-start.22 = (bf16[192,2048]{1,0:T(8,128)(2,1)}, bf16[192,2048]{1,0:T(8,128)(2,1)S(1)}, u32[]{:S(2)}, u32[]{:S(2)}) collective-permute-start(bf16[192,2048]{1,0:T(8,128)(2,1)} %slice.289), channel_id=1, source_target_pairs={{0,8},{8,0},{16,24},{24,16},{1,9},{9,1},{17,25},{25,17},{2,10},{10... | collective-permute-start | bytes 2359304 | tf_op jit(solution)/shard_map/ppermute | solution.py:24
  293.5 23.7 %collective-permute-start.21 = (bf16[192,2048]{1,0:T(8,128)(2,1)}, bf16[192,2048]{1,0:T(8,128)(2,1)}, u32[]{:S(2)}, u32[]{:S(2)}) collective-permute-start(bf16[192,2048]{1,0:T(8,128)(2,1)} %slice.288), channel_id=1, source_target_pairs={{0,16},{8,24},{16,0},{24,8},{1,17},{9,25},{17,1},{25,9},{2,18},{10... | collective-permute-start | bytes 2359304 | tf_op jit(solution)/shard_map/ppermute | solution.py:24
  317.2 33.1 %collective-permute-start.24 = (bf16[1536,512]{1,0:T(8,128)(2,1)}, bf16[1536,512]{1,0:T(8,128)(2,1)}, u32[]{:S(2)}, u32[]{:S(2)}) collective-permute-start(bf16[1536,512]{1,0:T(8,128)(2,1)} %get-tuple-element.215.refs_5_), channel_id=1, source_target_pairs={{0,16},{8,24},{16,0},{24,8},{1,17},{9,25},{17,1},{25,9},{2,18},{10... | collective-permute-start | bytes 4718600 | tf_op jit(solution)/shard_map/ppermute | solution.py:24
  318.1 32.4 %collective-permute-start.23 = (bf16[1536,512]{1,0:T(8,128)(2,1)}, bf16[1536,512]{1,0:T(8,128)(2,1)}, u32[]{:S(2)}, u32[]{:S(2)}) collective-permute-start(bf16[1536,512]{1,0:T(8,128)(2,1)} %get-tuple-element.215.refs_5_), channel_id=1, source_target_pairs={{0,8},{8,0},{16,24},{24,16},{1,9},{9,1},{17,25},{25,17},{2,10},{10... | collective-permute-start | bytes 4718600 | tf_op jit(solution)/shard_map/ppermute | solution.py:24
  348.7 28.8 %collective-permute-start.26 = (bf16[768,512]{1,0:T(8,128)(2,1)S(1)}, bf16[768,512]{1,0:T(8,128)(2,1)S(1)}, u32[]{:S(2)}, u32[]{:S(2)}) collective-permute-start(bf16[768,512]{1,0:T(8,128)(2,1)S(1)} %get-tuple-element.337), channel_id=1, source_target_pairs={{0,16},{8,24},{16,0},{24,8},{1,17},{9,25},{17,1},{25,9},{2,18},{10... | collective-permute-start | bytes 2359304 | tf_op jit(solution)/shard_map/ppermute | solution.py:24
  350.1 27.4 %collective-permute-start.25 = (bf16[768,512]{1,0:T(8,128)(2,1)S(1)}, bf16[768,512]{1,0:T(8,128)(2,1)S(1)}, u32[]{:S(2)}, u32[]{:S(2)}) collective-permute-start(bf16[768,512]{1,0:T(8,128)(2,1)S(1)} %get-tuple-element.338), channel_id=1, source_target_pairs={{0,8},{8,0},{16,24},{24,16},{1,9},{9,1},{17,25},{25,17},{2,10},{10... | collective-permute-start | bytes 2359304 | tf_op jit(solution)/shard_map/ppermute | solution.py:24
  353.0 28.9 %collective-permute-start.30 = (bf16[768,512]{1,0:T(8,128)(2,1)S(1)}, bf16[768,512]{1,0:T(8,128)(2,1)S(1)}, u32[]{:S(2)}, u32[]{:S(2)}) collective-permute-start(bf16[768,512]{1,0:T(8,128)(2,1)S(1)} %slice.294), channel_id=1, source_target_pairs={{0,8},{8,0},{16,24},{24,16},{1,9},{9,1},{17,25},{25,17},{2,10},{10... | collective-permute-start | bytes 2359304 | tf_op jit(solution)/shard_map/ppermute | solution.py:24
  354.6 27.2 %collective-permute-start.29 = (bf16[768,512]{1,0:T(8,128)(2,1)S(1)}, bf16[768,512]{1,0:T(8,128)(2,1)S(1)}, u32[]{:S(2)}, u32[]{:S(2)}) collective-permute-start(bf16[768,512]{1,0:T(8,128)(2,1)S(1)} %slice.293), channel_id=1, source_target_pairs={{0,16},{8,24},{16,0},{24,8},{1,17},{9,25},{17,1},{25,9},{2,18},{10... | collective-permute-start | bytes 2359304 | tf_op jit(solution)/shard_map/ppermute | solution.py:24
  409.0 195.1 %reduce-scatter.9.cloned.1.call-start = ((), (), s32[]{:S(2)}) async-start(), calls=%async_computation.12 | async-start | bytes 8257536 | tf_op jit(solution)/shard_map/reduce_scatter | solution.py:845
  409.1 32.1 %collective-permute-start.27 = (bf16[1536,512]{1,0:T(8,128)(2,1)}, bf16[1536,512]{1,0:T(8,128)(2,1)S(1)}, u32[]{:S(2)}, u32[]{:S(2)}) collective-permute-start(bf16[1536,512]{1,0:T(8,128)(2,1)} %copy-done.72), channel_id=1, source_target_pairs={{0,8},{8,0},{16,24},{24,16},{1,9},{9,1},{17,25},{25,17},{2,10},{10... | collective-permute-start | bytes 4718600 | tf_op jit(solution)/shard_map/ppermute | solution.py:24
  410.6 31.8 %collective-permute-start.28 = (bf16[1536,512]{1,0:T(8,128)(2,1)S(1)}, bf16[1536,512]{1,0:T(8,128)(2,1)S(1)}, u32[]{:S(2)}, u32[]{:S(2)}) collective-permute-start(bf16[1536,512]{1,0:T(8,128)(2,1)S(1)} %copy-done.71), channel_id=1, source_target_pairs={{0,16},{8,24},{16,0},{24,8},{1,17},{9,25},{17,1},{25,9},{2,18},{10... | collective-permute-start | bytes 4718600 | tf_op jit(solution)/shard_map/ppermute | solution.py:24
  459.6 21.2 %collective-permute-start.31 = (bf16[192,2048]{1,0:T(8,128)(2,1)S(1)}, bf16[192,2048]{1,0:T(8,128)(2,1)S(1)}, u32[]{:S(2)}, u32[]{:S(2)}) collective-permute-start(bf16[192,2048]{1,0:T(8,128)(2,1)S(1)} %get-tuple-element.227), channel_id=1, source_target_pairs={{0,8},{8,0},{16,24},{24,16},{1,9},{9,1},{17,25},{25,17},{2,10},{10... | collective-permute-start | bytes 2359304 | tf_op jit(solution)/shard_map/ppermute | solution.py:24
  461.1 19.7 %collective-permute-start.32 = (bf16[192,2048]{1,0:T(8,128)(2,1)S(1)}, bf16[192,2048]{1,0:T(8,128)(2,1)S(1)}, u32[]{:S(2)}, u32[]{:S(2)}) collective-permute-start(bf16[192,2048]{1,0:T(8,128)(2,1)S(1)} %get-tuple-element.228), channel_id=1, source_target_pairs={{0,16},{8,24},{16,0},{24,8},{1,17},{9,25},{17,1},{25,9},{2,18},{10... | collective-permute-start | bytes 2359304 | tf_op jit(solution)/shard_map/ppermute | solution.py:24
  502.0 162.3 %reduce-scatter.11.cloned.1.call-start = ((), (), s32[]{:S(2)}) async-start(), calls=%async_computation.13 | async-start | bytes 2359296 | tf_op jit(solution)/shard_map/reduce_scatter | solution.py:845
  502.0 31.2 %collective-permute-start.33 = (bf16[384,2048]{1,0:T(8,128)(2,1)}, bf16[384,2048]{1,0:T(8,128)(2,1)}, u32[]{:S(2)}, u32[]{:S(2)}) collective-permute-start(bf16[384,2048]{1,0:T(8,128)(2,1)} %copy-done.74), channel_id=1, source_target_pairs={{0,8},{8,0},{16,24},{24,16},{1,9},{9,1},{17,25},{25,17},{2,10},{10... | collective-permute-start | bytes 4718600 | tf_op jit(solution)/shard_map/ppermute | solution.py:24
  502.7 30.7 %collective-permute-start.34 = (bf16[384,2048]{1,0:T(8,128)(2,1)}, bf16[384,2048]{1,0:T(8,128)(2,1)}, u32[]{:S(2)}, u32[]{:S(2)}) collective-permute-start(bf16[384,2048]{1,0:T(8,128)(2,1)} %copy-done.73), channel_id=1, source_target_pairs={{0,16},{8,24},{16,0},{24,8},{1,17},{9,25},{17,1},{25,9},{2,18},{10... | collective-permute-start | bytes 4718600 | tf_op jit(solution)/shard_map/ppermute | solution.py:24
  543.0 32.7 %collective-permute-start.36 = (bf16[384,2048]{1,0:T(8,128)(2,1)S(1)}, bf16[384,2048]{1,0:T(8,128)(2,1)S(1)}, u32[]{:S(2)}, u32[]{:S(2)}) collective-permute-start(bf16[384,2048]{1,0:T(8,128)(2,1)S(1)} %get-tuple-element.247), channel_id=1, source_target_pairs={{0,16},{8,24},{16,0},{24,8},{1,17},{9,25},{17,1},{25,9},{2,18},{10... | collective-permute-start | bytes 4718600 | tf_op jit(solution)/shard_map/ppermute | solution.py:24
  544.0 34.2 %collective-permute-start.35 = (bf16[384,2048]{1,0:T(8,128)(2,1)S(1)}, bf16[384,2048]{1,0:T(8,128)(2,1)S(1)}, u32[]{:S(2)}, u32[]{:S(2)}) collective-permute-start(bf16[384,2048]{1,0:T(8,128)(2,1)S(1)} %get-tuple-element.247), channel_id=1, source_target_pairs={{0,8},{8,0},{16,24},{24,16},{1,9},{9,1},{17,25},{25,17},{2,10},{10... | collective-permute-start | bytes 4718600 | tf_op jit(solution)/shard_map/ppermute | solution.py:24
  578.4 12.1 %collective-permute-start.38 = (bf16[192,2048]{1,0:T(8,128)(2,1)S(1)}, bf16[192,2048]{1,0:T(8,128)(2,1)S(1)}, u32[]{:S(2)}, u32[]{:S(2)}) collective-permute-start(bf16[192,2048]{1,0:T(8,128)(2,1)S(1)} %slice.296), channel_id=1, source_target_pairs={{0,8},{8,0},{16,24},{24,16},{1,9},{9,1},{17,25},{25,17},{2,10},{10... | collective-permute-start | bytes 2359304 | tf_op jit(solution)/shard_map/ppermute | solution.py:24
  580.1 12.0 %collective-permute-start.37 = (bf16[192,2048]{1,0:T(8,128)(2,1)S(1)}, bf16[192,2048]{1,0:T(8,128)(2,1)S(1)}, u32[]{:S(2)}, u32[]{:S(2)}) collective-permute-start(bf16[192,2048]{1,0:T(8,128)(2,1)S(1)} %slice.295), channel_id=1, source_target_pairs={{0,16},{8,24},{16,0},{24,8},{1,17},{9,25},{17,1},{25,9},{2,18},{10... | collective-permute-start | bytes 2359304 | tf_op jit(solution)/shard_map/ppermute | solution.py:24
  598.8 150.3 %reduce-scatter.15.cloned.1.call-start = ((), (), s32[]{:S(2)}) async-start(), calls=%async_computation.15 | async-start | bytes 2359296 | tf_op jit(solution)/shard_map/reduce_scatter | solution.py:845
  599.5 173.2 %reduce-scatter.17.cloned.1.call-start = ((), (), s32[]{:S(2)}) async-start(), calls=%async_computation.16 | async-start | bytes 4718592 | tf_op jit(solution)/shard_map/reduce_scatter | solution.py:845
  605.7 40.7 %collective-permute-start.41 = (bf16[384,512]{1,0:T(8,128)(2,1)S(1)}, bf16[384,512]{1,0:T(8,128)(2,1)S(1)}, u32[]{:S(2)}, u32[]{:S(2)}) collective-permute-start(bf16[384,512]{1,0:T(8,128)(2,1)S(1)} %get-tuple-element.333), channel_id=1, source_target_pairs={{0,24},{8,16},{16,8},{24,0},{1,25},{9,17},{17,9},{25,1},{2,26},{10... | collective-permute-start | bytes 1179656 | tf_op jit(solution)/shard_map/ppermute | solution.py:24
  606.6 39.8 %collective-permute-start.40 = (bf16[384,512]{1,0:T(8,128)(2,1)S(1)}, bf16[384,512]{1,0:T(8,128)(2,1)S(1)}, u32[]{:S(2)}, u32[]{:S(2)}) collective-permute-start(bf16[384,512]{1,0:T(8,128)(2,1)S(1)} %get-tuple-element.334), channel_id=1, source_target_pairs={{0,16},{8,24},{16,0},{24,8},{1,17},{9,25},{17,1},{25,9},{2,18},{10... | collective-permute-start | bytes 1179656 | tf_op jit(solution)/shard_map/ppermute | solution.py:24
  607.5 38.9 %collective-permute-start.39 = (bf16[384,512]{1,0:T(8,128)(2,1)S(1)}, bf16[384,512]{1,0:T(8,128)(2,1)S(1)}, u32[]{:S(2)}, u32[]{:S(2)}) collective-permute-start(bf16[384,512]{1,0:T(8,128)(2,1)S(1)} %get-tuple-element.335), channel_id=1, source_target_pairs={{0,8},{8,0},{16,24},{24,16},{1,9},{9,1},{17,25},{25,17},{2,10},{10... | collective-permute-start | bytes 1179656 | tf_op jit(solution)/shard_map/ppermute | solution.py:24
  663.5 127.9 %reduce-scatter.13.cloned.1.call-start = ((), (), s32[]{:S(2)}) async-start(), calls=%async_computation.14 | async-start | bytes 4718592 | tf_op jit(solution)/shard_map/reduce_scatter | solution.py:845
  674.1 18.9 %collective-permute-start.42 = (bf16[192,2048]{1,0:T(8,128)(2,1)S(1)}, bf16[192,2048]{1,0:T(8,128)(2,1)S(1)}, u32[]{:S(2)}, u32[]{:S(2)}) collective-permute-start(bf16[192,2048]{1,0:T(8,128)(2,1)S(1)} %get-tuple-element.272), channel_id=1, source_target_pairs={{0,8},{8,0},{16,24},{24,16},{1,9},{9,1},{17,25},{25,17},{2,10},{10... | collective-permute-start | bytes 2359304 | tf_op jit(solution)/shard_map/ppermute | solution.py:24
  674.2 18.8 %collective-permute-start.43 = (bf16[192,2048]{1,0:T(8,128)(2,1)S(1)}, bf16[192,2048]{1,0:T(8,128)(2,1)S(1)}, u32[]{:S(2)}, u32[]{:S(2)}) collective-permute-start(bf16[192,2048]{1,0:T(8,128)(2,1)S(1)} %get-tuple-element.273), channel_id=1, source_target_pairs={{0,16},{8,24},{16,0},{24,8},{1,17},{9,25},{17,1},{25,9},{2,18},{10... | collective-permute-start | bytes 2359304 | tf_op jit(solution)/shard_map/ppermute | solution.py:24
  712.8 26.0 %collective-permute-start.44 = (bf16[384,2048]{1,0:T(8,128)(2,1)}, bf16[384,2048]{1,0:T(8,128)(2,1)}, u32[]{:S(2)}, u32[]{:S(2)}) collective-permute-start(bf16[384,2048]{1,0:T(8,128)(2,1)} %copy-done.69), channel_id=1, source_target_pairs={{0,8},{8,0},{16,24},{24,16},{1,9},{9,1},{17,25},{25,17},{2,10},{10... | collective-permute-start | bytes 4718600 | tf_op jit(solution)/shard_map/ppermute | solution.py:24
  714.6 24.5 %collective-permute-start.45 = (bf16[384,2048]{1,0:T(8,128)(2,1)}, bf16[384,2048]{1,0:T(8,128)(2,1)}, u32[]{:S(2)}, u32[]{:S(2)}) collective-permute-start(bf16[384,2048]{1,0:T(8,128)(2,1)} %copy-done.68), channel_id=1, source_target_pairs={{0,16},{8,24},{16,0},{24,8},{1,17},{9,25},{17,1},{25,9},{2,18},{10... | collective-permute-start | bytes 4718600 | tf_op jit(solution)/shard_map/ppermute | solution.py:24
  746.9 11.4 %collective-permute-start.52 = (f32[16,14,64]{2,1,0:T(8,128)S(1)}, f32[16,14,64]{2,1,0:T(8,128)S(1)}, u32[]{:S(2)}, u32[]{:S(2)}) collective-permute-start(f32[16,14,64]{2,1,0:T(8,128)S(1)} %bitcast.114), channel_id=1, source_target_pairs={{0,4},{1,5},{2,6},{3,7},{4,0},{5,1},{6,2},{7,3},{8,12},{9,13},{10,... | collective-permute-start | bytes 172040 | tf_op jit(solution)/shard_map/ppermute | solution.py:24
  758.4 6.4 collective-permute-start.53
  767.4 18.0 %collective-permute-start.48 = (bf16[64,2304]{1,0:T(8,128)(2,1)S(1)}, bf16[64,2304]{1,0:T(8,128)(2,1)S(1)}, u32[]{:S(2)}, u32[]{:S(2)}) collective-permute-start(bf16[64,2304]{1,0:T(8,128)(2,1)S(1)} %get-tuple-element.341), channel_id=1, source_target_pairs={{0,24},{8,16},{16,8},{24,0},{1,25},{9,17},{17,9},{25,1},{2,26},{10... | collective-permute-start | bytes 884744 | tf_op jit(solution)/shard_map/ppermute | solution.py:24
  769.0 18.5 %collective-permute-start.47 = (bf16[64,2304]{1,0:T(8,128)(2,1)S(1)}, bf16[64,2304]{1,0:T(8,128)(2,1)S(1)}, u32[]{:S(2)}, u32[]{:S(2)}) collective-permute-start(bf16[64,2304]{1,0:T(8,128)(2,1)S(1)} %get-tuple-element.342), channel_id=1, source_target_pairs={{0,16},{8,24},{16,0},{24,8},{1,17},{9,25},{17,1},{25,9},{2,18},{10... | collective-permute-start | bytes 884744 | tf_op jit(solution)/shard_map/ppermute | solution.py:24
  770.6 17.0 %collective-permute-start.46 = (bf16[64,2304]{1,0:T(8,128)(2,1)S(1)}, bf16[64,2304]{1,0:T(8,128)(2,1)S(1)}, u32[]{:S(2)}, u32[]{:S(2)}) collective-permute-start(bf16[64,2304]{1,0:T(8,128)(2,1)S(1)} %get-tuple-element.343), channel_id=1, source_target_pairs={{0,8},{8,0},{16,24},{24,16},{1,9},{9,1},{17,25},{25,17},{2,10},{10... | collective-permute-start | bytes 884744 | tf_op jit(solution)/shard_map/ppermute | solution.py:24
  771.0 13.2 %collective-permute-start.56 = (f32[1,14,64]{2,1,0:T(8,128)S(1)}, f32[1,14,64]{2,1,0:T(8,128)S(1)}, u32[]{:S(2)}, u32[]{:S(2)}) collective-permute-start(f32[1,14,64]{2,1,0:T(8,128)S(1)} %slice_select_fusion.5), channel_id=1, source_target_pairs={{0,8},{8,0},{16,24},{24,16},{1,9},{9,1},{17,25},{25,17},{2,10},{10... | collective-permute-start | bytes 10760 | tf_op jit(solution)/shard_map/ppermute | solution.py:24
  773.8 15.3 %collective-permute-start.51 = (bf16[64,1024]{1,0:T(8,128)(2,1)S(1)}, bf16[64,1024]{1,0:T(8,128)(2,1)S(1)}, u32[]{:S(2)}, u32[]{:S(2)}) collective-permute-start(bf16[64,1024]{1,0:T(8,128)(2,1)S(1)} %get-tuple-element.349), channel_id=1, source_target_pairs={{0,24},{8,16},{16,8},{24,0},{1,25},{9,17},{17,9},{25,1},{2,26},{10... | collective-permute-start | bytes 393224 | tf_op jit(solution)/shard_map/ppermute | solution.py:24
  792.5 6.0 collective-permute-start.59
  794.1 5.7 collective-permute-start.58
  (124 other events, 1053.4 us)
Sparse Core Ops, SparseCore 0:
  33.0 67.9 all-gather.7
  103.3 27.8 all-gather.5
  132.7 28.6 all-gather.9
  170.8 91.1 all-gather.11
  263.5 71.8 all-gather.13
  409.2 81.4 reduce-scatter.6
  502.1 80.2 reduce-scatter.8
  598.9 35.8 reduce-scatter.10
  637.0 34.8 reduce-scatter.14
  674.1 48.5 reduce-scatter.16
  725.0 52.3 reduce-scatter.12

commit v11 on v10

--- a/solution.py
+++ b/solution.py
@@ -108,8 +108,9 @@
     return part
 
 
-def scatter_small(parts):
+def scatter_small(parts, between):
     for axis in ("dp", "seq"):
+        parts = after(parts, between) if axis == "seq" else parts
         for bit in reversed(bits_of(lax.axis_size(axis))):
             half = parts.shape[0] // 2
             second = (lax.axis_index(axis) & bit) != 0
@@ -678,9 +679,9 @@
 
 
 def wkv_backward_body(
-    here, r_ref, k_ref, v_ref, g_ref, wkv_ref, d_mixed_ref, states_ref,
+    here, r_ref, k_ref, v_ref, d_wkv_ref, states_ref,
     rows_ref, columns_ref, grow_ref, shrink_ref, tail_ref, par_ref,
-    d_r_ref, d_k_ref, d_v_ref, d_g_ref, sums_ref, d_state,
+    d_r_ref, d_k_ref, d_v_ref, sums_ref, d_state,
 ):
     @pl.when(pl.program_id(0) == 0)
     def _():
@@ -694,22 +695,10 @@
     offset = lax.broadcasted_iota(jnp.int32, (CHUNK, PAIR), 0).astype(F32)
     for pair in range(r_ref.shape[1] // PAIR):
         at = slice(pair * PAIR, (pair + 1) * PAIR)
-        bonus, gain, bias, decay = (par_ref[i : i + 1, at] for i in range(4))
-        wkv, gate, d_mixed = wkv_ref[:, at], g_ref[:, at], d_mixed_ref[:, at].astype(F32)
-        centred = wkv - head_sum_fine(wkv, ones) * (1.0 / HEAD)
-        spread = head_sum(centred * centred, ones) * (1.0 / HEAD)
-        inverse = lax.rsqrt(spread + GROUP_EPSILON)
-        normed = centred * inverse
-        opened = 1.0 / (1.0 + jnp.exp(-gate))
-        d_scaled = d_mixed * gate * opened
-        d_g = d_mixed * (normed * gain + bias) * opened * (1.0 + gate * (1.0 - opened))
-        d_g_ref[:, at] = d_g.astype(BF)
-        d_normed = d_scaled * gain
-        mean_one = head_sum(d_normed, ones) * (1.0 / HEAD)
-        mean_two = head_sum(d_normed * normed, ones) * (1.0 / HEAD)
-        d_wkv = inverse * (d_normed - mean_one - normed * mean_two)
+        bonus, decay = par_ref[0:1, at], par_ref[3:4, at]
+        d_wkv = d_wkv_ref[:, at].astype(F32)
         r, k, v = r_ref[:, at].astype(F32), k_ref[:, at].astype(F32), v_ref[:, at].astype(F32)
-        v_b, d_wkv_b = v_ref[:, at], d_wkv.astype(BF)
+        v_b, d_wkv_b = v_ref[:, at], d_wkv_ref[:, at]
         grow, shrink, tail = grow_ref[:, at], shrink_ref[:, at], tail_ref[:, at] * last_same
         held = states_ref[0, at, :]
         later = d_state[at, :]
@@ -745,8 +734,42 @@
         kept = CHUNK * carried * jnp.sum(held.astype(F32) * later, axis=0, keepdims=True)
         sums_ref[0:1, at] += jnp.sum(d_log, axis=0, keepdims=True) + kept
         sums_ref[1:2, at] += jnp.sum(d_share * r * k, axis=0, keepdims=True)
-        sums_ref[2:3, at] += jnp.sum(d_scaled * normed, axis=0, keepdims=True)
-        sums_ref[3:4, at] += jnp.sum(d_scaled, axis=0, keepdims=True)
+
+
+def gate_backward_body(here, wkv_ref, g_ref, d_mixed_ref, par_ref, d_wkv_ref, d_g_ref, sums_ref):
+    @pl.when(pl.program_id(0) == 0)
+    def _():
+        sums_ref[...] = jnp.zeros_like(sums_ref)
+
+    ones = jnp.where(same_head(), 1.0, 0.0).astype(BF)
+    for pair in range(wkv_ref.shape[1] // PAIR):
+        at = slice(pair * PAIR, (pair + 1) * PAIR)
+        gain, bias = par_ref[1:2, at], par_ref[2:3, at]
+        wkv, gate, d_mixed = wkv_ref[:, at], g_ref[:, at], d_mixed_ref[:, at].astype(F32)
+        centred = wkv - head_sum_fine(wkv, ones) * (1.0 / HEAD)
+        spread = head_sum(centred * centred, ones) * (1.0 / HEAD)
+        inverse = lax.rsqrt(spread + GROUP_EPSILON)
+        normed = centred * inverse
+        opened = 1.0 / (1.0 + jnp.exp(-gate))
+        d_scaled = d_mixed * gate * opened
+        d_g = d_mixed * (normed * gain + bias) * opened * (1.0 + gate * (1.0 - opened))
+        d_g_ref[:, at] = d_g.astype(BF)
+        d_normed = d_scaled * gain
+        mean_one = head_sum(d_normed, ones) * (1.0 / HEAD)
+        mean_two = head_sum(d_normed * normed, ones) * (1.0 / HEAD)
+        d_wkv_ref[:, at] = (inverse * (d_normed - mean_one - normed * mean_two)).astype(BF)
+        sums_ref[0:1, at] += jnp.sum(d_scaled * normed, axis=0, keepdims=True)
+        sums_ref[1:2, at] += jnp.sum(d_scaled, axis=0, keepdims=True)
+
+
+def gate_backward(wkv, gate, d_mixed, params, here):
+    rows, part = wkv.shape
+    own = block((2 * CHUNK, part), lambda i, h: (i, 0))
+    return kernel(
+        gate_backward_body, "gate_backward", (rows // (2 * CHUNK),), here,
+        [(a, own) for a in (wkv, gate, d_mixed)] + [(params, fixed(params.shape))],
+        [((rows, part), BF, own)] * 2 + [((8, part), F32, fixed((8, part)))],
+    )
 
 
 def wkv_blocks(width, chunks, per, backward):
@@ -774,14 +797,14 @@
     )
 
 
-def wkv_backward(r, k, v, gate, wkv, d_mixed, states_kept, tables, here, per):
+def wkv_backward(r, k, v, d_wkv, states_kept, tables, here, per):
     length, width = r.shape
     chunks = length // CHUNK
     tokens, states, blocks = wkv_blocks(width, chunks, per, True)
     return kernel(
         wkv_backward_body, "wkv_backward", (chunks,), here,
-        [(a, tokens) for a in (r, k, v, gate, wkv, d_mixed)] + [(states_kept, states)] + list(zip(tables, blocks)),
-        [((length, width), BF, tokens)] * 4 + [((8, width), F32, fixed((8, width)))],
+        [(a, tokens) for a in (r, k, v, d_wkv)] + [(states_kept, states)] + list(zip(tables, blocks)),
+        [((length, width), BF, tokens)] * 3 + [((8, width), F32, fixed((8, width)))],
         [pltpu.VMEM((width, PAIR), F32)],
     )
 
@@ -959,47 +982,46 @@
     grad_wo = (near_wo + dot(far_rows, far, TN)).astype(BF)
     summed_o = scatter_dp(grad_wo)
     d_mixed = after(d_mixed, summed_ck, grad_wo)
-    d_recept, d_keyed, d_valued, d_gate, sums = wkv_backward(
-        recept, keyed, valued, gate_pre, wkv, d_mixed, states, tables, here, per
+    d_wkv, d_gate, gate_sums = gate_backward(wkv, gate_pre, d_mixed, tables[5], here)
+    grad_g = dot(mix_g, d_gate, TN).astype(BF)
+    summed_g = scatter_dp(grad_g)
+    d_recept, d_keyed, d_valued, sums = wkv_backward(
+        recept, keyed, valued, after(d_wkv, grad_g), states, tables, here, per
     )
     channel = after(trade_seq(blocks_of(after(channel, d_mixed), seq)), d_recept)
-    grads_vg = [
-        dot(after(m, channel), d, TN).astype(BF) for m, d in ((mix_v, d_valued), (mix_g, d_gate))
+    grads_in = [
+        dot(after(m, channel), d, TN).astype(BF)
+        for m, d in ((mix_r, d_recept), (mix_k, d_keyed), (mix_v, d_valued))
     ]
-    summed_vg = scatter_dp(jnp.concatenate(grads_vg, axis=1))
-    grads_rk, others = [], []
+    summed_in = scatter_dp(jnp.concatenate(grads_in, axis=1))
+    others = []
 
     def beside(relayed):
-        grads_rk.extend(
-            dot(after(m, relayed), d, TN).astype(BF) for m, d in ((mix_r, d_recept), (mix_k, d_keyed))
-        )
         others.append(spread_columns([after_mix], after(channel, relayed), here, False, False, CHUNK, per))
         others.append(after(summed_cv, relayed).astype(F32))
-        return grads_rk, others
-
-    d_recept, d_keyed = after((d_recept, d_keyed), grads_vg, summed_o)
+        return others
+
+    d_recept, d_keyed = after((d_recept, d_keyed), grads_in, summed_o, summed_cr)
     terms, sums_one = mixes_back_scatter(
         [(i, d, 0, full_in, i, part) for i, d in enumerate((d_recept, d_keyed, d_valued))]
         + [(3, d_gate, 0, full_g, 0, part)],
         step, marks, rows_of(turned, 2, 3, 4, 5), here, seq, beside,
     )
-    summed_rk = scatter_dp(jnp.concatenate(grads_rk, axis=1))
     out_rows, sum_cv = others
     if within is None:
         terms = [outside(t, groups, unit, back=True) for t in terms]
     tokens_grad, _, norm_sums = norm_back(terms, inputs_b, d_after, rows_of(vec, 0), within, here)
 
-    summed_c = jnp.concatenate(after([summed_ck, summed_cr], terms), axis=1)
-    sum_ck, sum_cr = owners_rows(summed_c, [ffn_key.shape[1], width])
+    summed_c = jnp.concatenate(after([summed_ck, summed_cr, summed_g], terms), axis=1)
+    sum_ck, sum_cr, sum_g = owners_rows(summed_c, [ffn_key.shape[1], width, width])
     sum_o = summed_o.astype(F32)
-    sum_v, sum_g = owners_rows(summed_vg, [width] * 2)
 
     def by_device(rows, turn):
         if turn:
             return rows.reshape(-1, dp, seq, unit).transpose(1, 2, 0, 3)
         return rows.reshape(-1, seq, dp, unit).transpose(2, 1, 0, 3)
 
-    own_sums = jnp.stack([sums[0] * log_decay, sums[1], sums[2], sums[3]])
+    own_sums = jnp.stack([sums[0] * log_decay, sums[1], gate_sums[0], gate_sums[1]])
     own_sums = lax.dynamic_update_slice(jnp.zeros((4, width), F32), own_sums, (0, place * part))
     vector_rows = jnp.concatenate(
         [
@@ -1008,8 +1030,8 @@
         ],
         axis=2,
     )
-    sum_vec = scatter_small(vector_rows.reshape((-1,) + vector_rows.shape[2:]))
-    sum_r, sum_k = owners_rows(after(summed_rk, sum_ck, sum_v, sum_vec), [width] * 2)
+    sum_vec = scatter_small(vector_rows.reshape((-1,) + vector_rows.shape[2:]), sum_ck)
+    sum_r, sum_k, sum_v = owners_rows(after(summed_in, sum_vec), [width] * 3)
     return (
         out_rows[None], tokens_grad[None], sum_r, sum_k, sum_v, sum_g, sum_o,
         sum_ck, sum_cr, sum_cv, sum_vec,

time: 815 us -> 798 us (0.979)
    ppermute x60 -> x57, waiting for transfers between devices: 225 us -> 218 us  [swap(): return lax.ppermute(value, axis, [(i, i ^ distance) for i in range(size)])]
    unnamed x236 -> x239, local copies, waits for them, and re-layouts: 43.7 us -> 49.6 us
    ppermute x60 -> x57, starting transfers between devices: 70.8 us -> 66.4 us  [swap(): return lax.ppermute(value, axis, [(i, i ^ distance) for i in range(size)])]
  transfers between devices with their start and end apart: 71 -> 68, of which waited for: 38 -> 35; matrix products, arithmetic and copies ran while one was open for 24% -> 24% of each run, Pallas kernels for 28% -> 28%
where the time goes in v11:
time: 798 us; the launch traced here: 791 us
  Pallas kernels  232 us (29%)
  waiting for transfers between devices  219 us (27%)
  matrix products  165 us (21%)
  local copies, waits for them, and re-layouts  75.8 us (9%)
  starting transfers between devices  67.3 us (8%)
  other arithmetic  17.1 us (2%)
  between operations  15.5 us (2%)
    pallas_call x33, Pallas kernels, kernel(): pl.pallas_call(body, out_shape=[jax.ShapeDtypeStruct(shape, kind) for sha...  232 us
    ppermute x57, waiting for transfers between devices, swap(): return lax.ppermute(value, axis, [(i, i ^ distance) for i in range(size)])  218 us
    dot_general x25, matrix products, dot(): return lax.dot_general(left, right, dims, preferred_element_type=F32)  165 us
    ppermute x57, starting transfers between devices, swap(): return lax.ppermute(value, axis, [(i, i ^ distance) for i in range(size)])  66.4 us
    unnamed x239, local copies, waits for them, and re-layouts  49.6 us
  transfers between devices with their start and end apart: 68, of which 35 were waited for; matrix products, arithmetic and copies ran while one was open for 24% of the time, Pallas kernels for 28%

profile of v11, /device:TPU:0, one launch (start us, length us, event | category | flops | bytes accessed | tf_op | source)
XLA Modules:
  0.0 791.4 jit_solution(10602484410442130443)
XLA Ops:
  11.9 3.0 collective-permute-start
  18.6 4.8 collective-permute-done.refs_1_
  23.5 8.4 %collective-permute-done.1.refs_2_ = bf16[80,2048]{1,0:T(8,128)(2,1)S(1)} collective-permute-done((bf16[80,2048]{1,0:T(8,128)(2,1)S(1)}, bf16[80,2048]{1,0:T(8,128)(2,1)S(1)}, u32[]{:S(2)}, u32[]{:S(2)}) %collective-permute-start.1) | collective-permute-done | bytes 327712 | tf_op jit(solution)/shard_map/ppermute | solution.py:24
  44.6 3.1 collective-permute-start.5
  49.3 6.1 collective-permute-done.5
  59.7 11.3 %collective-permute-done.7.refs_2_ = bf16[384,2048]{1,0:T(8,128)(2,1)} collective-permute-done((bf16[384,2048]{1,0:T(8,128)(2,1)S(1)}, bf16[384,2048]{1,0:T(8,128)(2,1)}, u32[]{:S(2)}, u32[]{:S(2)}) %collective-permute-start.7) | collective-permute-done | bytes 1572896 | tf_op jit(solution)/shard_map/ppermute | solution.py:24
  76.3 15.6 %collective-permute-done.9.refs_4_ = bf16[192,2048]{1,0:T(8,128)(2,1)S(1)} collective-permute-done((bf16[192,2048]{1,0:T(8,128)(2,1)S(1)}, bf16[192,2048]{1,0:T(8,128)(2,1)S(1)}, u32[]{:S(2)}, u32[]{:S(2)}) %collective-permute-start.9) | collective-permute-done | bytes 786464 | tf_op jit(solution)/shard_map/ppermute | solution.py:24
  95.7 17.6 %mixes.2 = (bf16[1536,2048]{1,0:T(8,128)(2,1)}, bf16[1536,2048]{1,0:T(8,128)(2,1)}, bf16[1536,2048]{1,0:T(8,128)(2,1)}, bf16[1536,2048]{1,0:T(8,128)(2,1)}, bf16[1536,2048]{1,0:T(8,128)(2,1)}) custom-call(s32[1]{0:T(128)} %bitcast.here, bf16[384,2048]{1,0:T(8,128)(2,1)S(1)} %copy-done.13, bf16[384,2048]{1,0:T(8,128)(2,1)} %collective-permute-done.6.refs_1_, ...), custom_call_target="tpu_custom_call" | custom-call | tf_op jit(solution)/shard_map/mixes/pallas_call | solution.py:135
  113.3 2.4 cut_columns.3
  119.5 7.0 convolution_convert_fusion.9.r_ref
  126.6 7.9 %convolution_convert_fusion.8.k_ref = bf16[1536,512]{1,0:T(8,128)(2,1)} fusion(bf16[1536,2048]{1,0:T(8,128)(2,1)} %get-tuple-element.269, bf16[2048,1536]{1,0:T(8,128)(2,1)S(1)} %copy-done.75), kind=kOutput, calls=%fused_computation.18 | convolution fusion | flops 3222011904 | bytes 9961472 | tf_op jit(solution)/shard_map/dot_general | solution.py:621
  134.5 4.5 convolution_convert_fusion.7.v_ref
  139.1 13.5 %wkv_forward.1 = (f32[1536,512]{1,0:T(8,128)}, bf16[12,512,128]{2,1,0:T(8,128)(2,1)S(1)}) custom-call(s32[1]{0:T(128)} %bitcast.here, bf16[1536,512]{1,0:T(8,128)(2,1)S(1)} %convolution_convert_fusion.9.r_ref, bf16[1536,512]{1,0:T(8,128)(2,1)} %convolution_convert_fusion.8.k_ref, bf16[1536,512]{1,0:T(8,128)(2,1)} %convolution_convert_fusion.7.v_ref, ...), custom_call_target="tpu_custom_call" | custom-call | tf_op jit(solution)/shard_map/wkv_forward/pallas_call | solution.py:135
  155.4 10.2 %gate.1 = (f32[1536,512]{1,0:T(8,128)}, bf16[1536,512]{1,0:T(8,128)(2,1)S(1)}) custom-call(s32[1]{0:T(128)} %bitcast.here, bf16[1536,2048]{1,0:T(8,128)(2,1)} %get-tuple-element.180.refs_0_, bf16[2048,512]{1,0:T(8,128)(2,1)S(1)} %copy-done.4, f32[1536,512]{1,0:T(8,128)} %get-tuple-element.187.refs_2_.wkv_ref, f32[8,512]{1,0:T(8,128)S(1)} %maximum_maximum_fusion.par_ref.refs_3_), custom_call_target="tpu_custom_call" | custom-call | tf_op jit(solution)/shard_map/gate/pallas_call | solution.py:135
  167.2 3.3 stack_rows.3
  171.5 2.8 convolution_convert_fusion.10
  181.0 11.0 %collective-permute-done.11.high_ref = bf16[192,2048]{1,0:T(8,128)(2,1)S(1)} collective-permute-done((bf16[192,2048]{1,0:T(8,128)(2,1)S(1)}, bf16[192,2048]{1,0:T(8,128)(2,1)S(1)}, u32[]{:S(2)}, u32[]{:S(2)}) %collective-permute-start.11) | collective-permute-done | bytes 786464 | tf_op jit(solution)/shard_map/ppermute | solution.py:24
  193.5 3.3 relay.4
  200.1 2.8 convolution_convert_fusion.13.refs_0_
  203.0 27.8 %collective-permute-done.12.refs_1_ = bf16[384,2048]{1,0:T(8,128)(2,1)} collective-permute-done((bf16[384,2048]{1,0:T(8,128)(2,1)}, bf16[384,2048]{1,0:T(8,128)(2,1)}, u32[]{:S(2)}, u32[]{:S(2)}) %collective-permute-start.12) | collective-permute-done | bytes 1572896 | tf_op jit(solution)/shard_map/ppermute | solution.py:24
  230.7 4.7 after_norm.1
  237.9 30.6 %collective-permute-done.15.refs_2_ = bf16[384,2048]{1,0:T(8,128)(2,1)S(1)} collective-permute-done((bf16[384,2048]{1,0:T(8,128)(2,1)S(1)}, bf16[384,2048]{1,0:T(8,128)(2,1)S(1)}, u32[]{:S(2)}, u32[]{:S(2)}) %collective-permute-start.15) | collective-permute-done | bytes 1572896 | tf_op jit(solution)/shard_map/ppermute | solution.py:24
  278.5 8.5 %collective-permute-done.17.refs_4_ = bf16[192,2048]{1,0:T(8,128)(2,1)S(1)} collective-permute-done((bf16[192,2048]{1,0:T(8,128)(2,1)}, bf16[192,2048]{1,0:T(8,128)(2,1)S(1)}, u32[]{:S(2)}, u32[]{:S(2)}) %collective-permute-start.17) | collective-permute-done | bytes 786464 | tf_op jit(solution)/shard_map/ppermute | solution.py:24
  295.6 12.0 %mixes.3 = (bf16[1536,2048]{1,0:T(8,128)(2,1)}, bf16[1536,2048]{1,0:T(8,128)(2,1)}, bf16[1536,2048]{1,0:T(8,128)(2,1)}) custom-call(s32[1]{0:T(128)} %bitcast.here, bf16[384,2048]{1,0:T(8,128)(2,1)S(1)} %copy-done.29, bf16[384,2048]{1,0:T(8,128)(2,1)S(1)} %copy-done.19, bf16[384,2048]{1,0:T(8,128)(2,1)} %copy-done.78, ...), custom_call_target="tpu_custom_call" | custom-call | tf_op jit(solution)/shard_map/mixes/pallas_call | solution.py:135
  307.5 9.6 %divide_convert_fusion = (bf16[1536,512]{1,0:T(8,128)(2,1)}, f32[1536,512]{1,0:T(8,128)}) fusion(bf16[1536,2048]{1,0:T(8,128)(2,1)} %get-tuple-element.247, bf16[2048,2304]{1,0:T(8,128)(2,1)} %all-gather.12.cloned.1.call-done.refs_6_.refs_7_.refs_8_), kind=kOutput, calls=%fused_computation.11 | convolution fusion | flops 3224371200 | bytes 13107200 | tf_op jit(solution)/shard_map/dot_general | solution.py:621
  319.3 23.0 %multiply_convert_fusion.1 = (bf16[1536,1792]{1,0:T(8,128)(2,1)}, bf16[1536,1792]{1,0:T(8,128)(2,1)}) fusion(bf16[1536,2048]{1,0:T(8,128)(2,1)} %get-tuple-element.246, bf16[2048,2304]{1,0:T(8,128)(2,1)S(1)} %copy-done.74), kind=kOutput, calls=%fused_computation.2 | convolution fusion | flops 11312824320 | bytes 24641536 | tf_op jit(solution)/shard_map/dot_general | solution.py:621
  342.3 6.0 value_columns.7
  356.0 6.0 value_columns.6.two_ref
  363.2 6.0 value_columns.5.one_ref
  370.4 6.0 value_columns.4.refs_5_
  382.6 10.1 %spread_columns.2 = bf16[1536,2048]{1,0:T(8,128)(2,1)} custom-call(s32[1]{0:T(128)} %bitcast.here, bf16[384,2048]{1,0:T(8,128)(2,1)S(1)} %bitcast.100, bf16[448,2304]{1,0:T(8,128)(2,1)} %collective-permute-done.18.refs_1_, bf16[448,2304]{1,0:T(8,128)(2,1)} %collective-permute-done.19.refs_2_, bf16[192,2048]{1,0:T(8,128)(2,1)} %collective-permute-done.21.refs_3_, ...), custom_call_target="tpu_custom_call" | custom-call | tf_op jit(solution)/shard_map/spread_columns/pallas_call | solution.py:135
  392.7 16.1 %convolution_convert_fusion.1 = bf16[1792,2048]{1,0:T(8,128)(2,1)} fusion(bf16[1536,1792]{1,0:T(8,128)(2,1)S(1)} %bitcast.108, bf16[1536,2048]{1,0:T(8,128)(2,1)} %spread_columns.2), kind=kOutput, calls=%fused_computation.5 | convolution fusion | flops 11277959168 | bytes 19136512 | tf_op jit(solution)/shard_map/dot_general | solution.py:621
  411.6 18.3 %multiply_convert_fusion.refs_0_.refs_3_ = bf16[1536,1792]{1,0:T(8,128)(2,1)} fusion(bf16[1536,1792]{1,0:T(8,128)(2,1)} %get-tuple-element.225, bf16[1536,2048]{1,0:T(8,128)(2,1)} %spread_columns.2, bf16[1792,2048]{1,0:T(8,128)(2,1)} %all-gather.14.cloned.1.call-done.right_ref), kind=kOutput, calls=%fused_computation.1 | convolution fusion | flops 11282546688 | bytes 24641536 | tf_op jit(solution)/shard_map/dot_general | solution.py:621
  429.8 11.1 %collective-permute-done.27.refs_6_ = bf16[1536,512]{1,0:T(8,128)(2,1)S(1)} collective-permute-done((bf16[1536,512]{1,0:T(8,128)(2,1)}, bf16[1536,512]{1,0:T(8,128)(2,1)S(1)}, u32[]{:S(2)}, u32[]{:S(2)}) %collective-permute-start.27) | collective-permute-done | bytes 1572896 | tf_op jit(solution)/shard_map/ppermute | solution.py:24
  443.3 6.9 channel.1
  450.2 9.0 %mixes_back.6 = (bf16[192,2048]{1,0:T(8,128)(2,1)S(1)}, bf16[192,2048]{1,0:T(8,128)(2,1)S(1)}, f32[8,2048]{1,0:T(8,128)S(1)}) custom-call(s32[1]{0:T(128)} %bitcast.here, bf16[1536,1792]{1,0:T(8,128)(2,1)} %multiply_convert_fusion.refs_0_.refs_3_, bf16[1536,512]{1,0:T(8,128)(2,1)S(1)} %get-tuple-element.244.refs_1_.refs_2_.refs_4_.refs_5_, ...), custom_call_target="tpu_custom_call" | custom-call | tf_op jit(solution)/shard_map/mixes_back/pallas_call | solution.py:135
  462.3 16.1 %mixes_back.7 = (bf16[384,2048]{1,0:T(8,128)(2,1)S(1)}, bf16[384,2048]{1,0:T(8,128)(2,1)S(1)}, f32[8,2048]{1,0:T(8,128)S(1)}) custom-call(s32[1]{0:T(128)} %bitcast.here, bf16[1536,1792]{1,0:T(8,128)(2,1)} %multiply_convert_fusion.refs_0_.refs_3_, bf16[1536,512]{1,0:T(8,128)(2,1)S(1)} %get-tuple-element.244.refs_1_.refs_2_.refs_4_.refs_5_, ...), custom_call_target="tpu_custom_call" | custom-call | tf_op jit(solution)/shard_map/mixes_back/pallas_call | solution.py:135
  480.8 2.4 relay.6
  485.0 16.3 %convolution_convert_fusion = bf16[2048,1792]{1,0:T(8,128)(2,1)} fusion(bf16[1536,2048]{1,0:T(8,128)(2,1)} %get-tuple-element.246, bf16[1536,1792]{1,0:T(8,128)(2,1)S(1)} %bitcast.106), kind=kOutput, calls=%fused_computation.4 | convolution fusion | flops 11277959168 | bytes 19136512 | tf_op jit(solution)/shard_map/dot_general | solution.py:621
  502.5 7.6 convolution_convert_fusion.6
  510.2 8.6 %mixes_back.8 = (bf16[384,2048]{1,0:T(8,128)(2,1)S(1)}, f32[8,2048]{1,0:T(8,128)S(1)}) custom-call(s32[1]{0:T(128)} %bitcast.here, bf16[1536,1792]{1,0:T(8,128)(2,1)} %multiply_convert_fusion.refs_0_.refs_3_, bf16[1536,512]{1,0:T(8,128)(2,1)S(1)} %get-tuple-element.244.refs_1_.refs_2_.refs_4_.refs_5_, ...), custom_call_target="tpu_custom_call" | custom-call | tf_op jit(solution)/shard_map/mixes_back/pallas_call | solution.py:135
  518.9 13.9 %collective-permute-done.33.refs_1_ = bf16[384,2048]{1,0:T(8,128)(2,1)} collective-permute-done((bf16[384,2048]{1,0:T(8,128)(2,1)}, bf16[384,2048]{1,0:T(8,128)(2,1)}, u32[]{:S(2)}, u32[]{:S(2)}) %collective-permute-start.33) | collective-permute-done | bytes 1572896 | tf_op jit(solution)/shard_map/ppermute | solution.py:24
  532.9 6.9 norm_back.2
  544.5 28.2 %collective-permute-done.36 = bf16[384,2048]{1,0:T(8,128)(2,1)S(1)} collective-permute-done((bf16[384,2048]{1,0:T(8,128)(2,1)S(1)}, bf16[384,2048]{1,0:T(8,128)(2,1)S(1)}, u32[]{:S(2)}, u32[]{:S(2)}) %collective-permute-start.36) | collective-permute-done | bytes 1572896 | tf_op jit(solution)/shard_map/ppermute | solution.py:24
  583.1 3.4 add_add_fusion
  589.9 5.3 add_convert_fusion
  596.7 2.7 convolution_convert_fusion.14
  602.1 8.6 %gate_backward.1 = (bf16[1536,512]{1,0:T(8,128)(2,1)S(1)}, bf16[1536,512]{1,0:T(8,128)(2,1)S(1)}, f32[8,512]{1,0:T(8,128)S(1)}) custom-call(s32[1]{0:T(128)} %bitcast.here, f32[1536,512]{1,0:T(8,128)} %get-tuple-element.187.refs_2_.wkv_ref, f32[1536,512]{1,0:T(8,128)} %get-tuple-element.257.g_ref, bf16[1536,512]{1,0:T(8,128)(2,1)S(1)} %copy-done.17, ...), custom_call_target="tpu_custom_call" | custom-call | tf_op jit(solution)/shard_map/gate_backward/pallas_call | solution.py:135
  611.8 8.2 %convolution_convert_fusion.5 = bf16[2048,512]{1,0:T(8,128)(2,1)} fusion(bf16[1536,2048]{1,0:T(8,128)(2,1)} %get-tuple-element.180.refs_0_, bf16[1536,512]{1,0:T(8,128)(2,1)S(1)} %get-tuple-element.299.refs_3_.refs_7_), kind=kOutput, calls=%fused_computation.15 | convolution fusion | flops 3222274048 | bytes 9961472 | tf_op jit(solution)/shard_map/dot_general | solution.py:621
  625.8 21.0 %wkv_backward.1 = (bf16[1536,512]{1,0:T(8,128)(2,1)S(1)}, bf16[1536,512]{1,0:T(8,128)(2,1)S(1)}, bf16[1536,512]{1,0:T(8,128)(2,1)}, f32[8,512]{1,0:T(8,128)S(1)}) custom-call(s32[1]{0:T(128)} %bitcast.here, bf16[1536,512]{1,0:T(8,128)(2,1)} %copy-done.11, bf16[1536,512]{1,0:T(8,128)(2,1)} %convolution_convert_fusion.8.k_ref, ...), custom_call_target="tpu_custom_call" | custom-call | tf_op jit(solution)/shard_map/wkv_backward/pallas_call | solution.py:135
  646.8 7.7 convolution_convert_fusion.4
  654.6 6.8 convolution_convert_fusion.2
  661.4 3.7 convolution_convert_fusion.3
  665.2 3.1 pad_maximum_fusion
  670.5 8.4 %mixes_back.9 = (bf16[192,2048]{1,0:T(8,128)(2,1)S(1)}, bf16[192,2048]{1,0:T(8,128)(2,1)S(1)}, f32[8,2048]{1,0:T(8,128)S(1)}) custom-call(s32[1]{0:T(128)} %bitcast.here, bf16[1536,512]{1,0:T(8,128)(2,1)S(1)} %get-tuple-element.296.refs_0_.refs_4_, bf16[1536,512]{1,0:T(8,128)(2,1)S(1)} %copy-done.2, bf16[1536,512]{1,0:T(8,128)(2,1)} %get-tuple-element.298.refs_2_.refs_6_, ...), custom_call_target="tpu_custom_call" | custom-call | tf_op jit(solution)/shard_map/mixes_back/pallas_call | solution.py:135
  680.5 15.4 %mixes_back.10 = (bf16[384,2048]{1,0:T(8,128)(2,1)S(1)}, bf16[384,2048]{1,0:T(8,128)(2,1)S(1)}, f32[8,2048]{1,0:T(8,128)S(1)}) custom-call(s32[1]{0:T(128)} %bitcast.here, bf16[1536,512]{1,0:T(8,128)(2,1)S(1)} %get-tuple-element.296.refs_0_.refs_4_, bf16[1536,512]{1,0:T(8,128)(2,1)} %copy-done.1, bf16[1536,512]{1,0:T(8,128)(2,1)} %get-tuple-element.298.refs_2_.refs_6_, ...), custom_call_target="tpu_custom_call" | custom-call | tf_op jit(solution)/shard_map/mixes_back/pallas_call | solution.py:135
  698.2 3.5 relay.7
  709.9 8.4 %mixes_back.11 = (bf16[384,2048]{1,0:T(8,128)(2,1)S(1)}, f32[8,2048]{1,0:T(8,128)S(1)}) custom-call(s32[1]{0:T(128)} %bitcast.here, bf16[1536,512]{1,0:T(8,128)(2,1)S(1)} %get-tuple-element.296.refs_0_.refs_4_, bf16[1536,512]{1,0:T(8,128)(2,1)S(1)} %copy-done.3, bf16[1536,512]{1,0:T(8,128)(2,1)} %get-tuple-element.298.refs_2_.refs_6_, ...), custom_call_target="tpu_custom_call" | custom-call | tf_op jit(solution)/shard_map/mixes_back/pallas_call | solution.py:135
  720.2 2.6 convert_element_type.196
  731.1 7.2 norm_back.3
  742.1 8.0 %collective-permute-done.46 = f32[16,14,64]{2,1,0:T(8,128)S(1)} collective-permute-done((f32[16,14,64]{2,1,0:T(8,128)S(1)}, f32[16,14,64]{2,1,0:T(8,128)S(1)}, u32[]{:S(2)}, u32[]{:S(2)}) %collective-permute-start.46) | collective-permute-done | bytes 57376 | tf_op jit(solution)/shard_map/ppermute | solution.py:24
  759.5 3.9 collective-permute-done.50.refs_2_
  766.0 2.9 collective-permute-done.52
  769.6 3.1 collective-permute-done.53
  (493 shorter events, 191.8 us)
Async XLA Ops:
  7.2 112.3 %all-gather.8.cloned.1.call-start = ((), (), s32[]{:S(2)}) async-start(), calls=%async_computation.7 | async-start | bytes 7077888 | tf_op jit(solution)/shard_map/all_gather | solution.py:865
  11.9 11.5 %collective-permute-start = (bf16[80,2048]{1,0:T(8,128)(2,1)S(1)}, bf16[80,2048]{1,0:T(8,128)(2,1)S(1)}, u32[]{:S(2)}, u32[]{:S(2)}) collective-permute-start(bf16[80,2048]{1,0:T(8,128)(2,1)S(1)} %get-tuple-element.170.refs_1_), channel_id=1, source_target_pairs={{0,8},{8,0},{16,24},{24,16},{1,9},{9,1},{17,25},{25,17},{2,10},{10... | collective-permute-start | bytes 983048 | tf_op jit(solution)/shard_map/ppermute | solution.py:24
  15.7 16.2 %collective-permute-start.1 = (bf16[80,2048]{1,0:T(8,128)(2,1)S(1)}, bf16[80,2048]{1,0:T(8,128)(2,1)S(1)}, u32[]{:S(2)}, u32[]{:S(2)}) collective-permute-start(bf16[80,2048]{1,0:T(8,128)(2,1)S(1)} %get-tuple-element.171.refs_2_), channel_id=1, source_target_pairs={{0,16},{8,24},{16,0},{24,8},{1,17},{9,25},{17,1},{25,9},{2,18},{10... | collective-permute-start | bytes 983048 | tf_op jit(solution)/shard_map/ppermute | solution.py:24
  17.9 13.9 %collective-permute-start.2 = (bf16[80,2048]{1,0:T(8,128)(2,1)S(1)}, bf16[80,2048]{1,0:T(8,128)(2,1)S(1)}, u32[]{:S(2)}, u32[]{:S(2)}) collective-permute-start(bf16[80,2048]{1,0:T(8,128)(2,1)S(1)} %get-tuple-element.172.refs_3_), channel_id=1, source_target_pairs={{0,24},{8,16},{16,8},{24,0},{1,25},{9,17},{17,9},{25,1},{2,26},{10... | collective-permute-start | bytes 983048 | tf_op jit(solution)/shard_map/ppermute | solution.py:24
  32.9 120.8 %all-gather.6.cloned.1.call-start = ((), (), s32[]{:S(2)}) async-start(), calls=%async_computation.6 | async-start | bytes 2359296 | tf_op jit(solution)/shard_map/all_gather | solution.py:865
  36.1 34.9 %collective-permute-start.7 = (bf16[384,2048]{1,0:T(8,128)(2,1)S(1)}, bf16[384,2048]{1,0:T(8,128)(2,1)}, u32[]{:S(2)}, u32[]{:S(2)}) collective-permute-start(bf16[384,2048]{1,0:T(8,128)(2,1)S(1)} %hold.1.refs_0_), channel_id=1, source_target_pairs={{0,16},{8,24},{16,0},{24,8},{1,17},{9,25},{17,1},{25,9},{2,18},{10... | collective-permute-start | bytes 4718600 | tf_op jit(solution)/shard_map/ppermute | solution.py:24
  37.6 34.8 %collective-permute-start.6 = (bf16[384,2048]{1,0:T(8,128)(2,1)S(1)}, bf16[384,2048]{1,0:T(8,128)(2,1)}, u32[]{:S(2)}, u32[]{:S(2)}) collective-permute-start(bf16[384,2048]{1,0:T(8,128)(2,1)S(1)} %hold.1.refs_0_), channel_id=1, source_target_pairs={{0,8},{8,0},{16,24},{24,16},{1,9},{9,1},{17,25},{25,17},{2,10},{10... | collective-permute-start | bytes 4718600 | tf_op jit(solution)/shard_map/ppermute | solution.py:24
  40.4 4.2 collective-permute-start.4
  44.6 10.8 %collective-permute-start.5 = (bf16[4,4,14,64]{3,2,1,0:T(8,128)(2,1)S(1)}, bf16[4,4,14,64]{3,2,1,0:T(8,128)(2,1)S(1)}, u32[]{:S(2)}, u32[]{:S(2)}) collective-permute-start(bf16[4,4,14,64]{3,2,1,0:T(8,128)(2,1)S(1)} %pad_maximum_fusion.5), channel_id=1, source_target_pairs={{0,4},{1,5},{2,6},{3,7},{4,0},{5,1},{6,2},{7,3},{8,12},{9,13},{10,... | collective-permute-start | bytes 86024 | tf_op jit(solution)/shard_map/ppermute | solution.py:24
  72.5 99.0 %all-gather.10.cloned.1.call-start = ((), (), s32[]{:S(2)}) async-start(), calls=%async_computation.8 | async-start | bytes 2359296 | tf_op jit(solution)/shard_map/all_gather | solution.py:865
  75.0 16.9 %collective-permute-start.9 = (bf16[192,2048]{1,0:T(8,128)(2,1)S(1)}, bf16[192,2048]{1,0:T(8,128)(2,1)S(1)}, u32[]{:S(2)}, u32[]{:S(2)}) collective-permute-start(bf16[192,2048]{1,0:T(8,128)(2,1)S(1)} %slice.269), channel_id=1, source_target_pairs={{0,8},{8,0},{16,24},{24,16},{1,9},{9,1},{17,25},{25,17},{2,10},{10... | collective-permute-start | bytes 2359304 | tf_op jit(solution)/shard_map/ppermute | solution.py:24
  75.3 16.6 %collective-permute-start.8 = (bf16[192,2048]{1,0:T(8,128)(2,1)S(1)}, bf16[192,2048]{1,0:T(8,128)(2,1)S(1)}, u32[]{:S(2)}, u32[]{:S(2)}) collective-permute-start(bf16[192,2048]{1,0:T(8,128)(2,1)S(1)} %slice.268), channel_id=1, source_target_pairs={{0,16},{8,24},{16,0},{24,8},{1,17},{9,25},{17,1},{25,9},{2,18},{10... | collective-permute-start | bytes 2359304 | tf_op jit(solution)/shard_map/ppermute | solution.py:24
  92.9 214.7 %all-gather.12.cloned.1.call-start = ((), (), s32[]{:S(2)}) async-start(), calls=%async_computation.9 | async-start | bytes 10616832 | tf_op jit(solution)/shard_map/all_gather | solution.py:865
  115.7 51.0 %collective-permute-start.20 = (bf16[64,2304]{1,0:T(8,128)(2,1)}, bf16[64,2304]{1,0:T(8,128)(2,1)S(1)}, u32[]{:S(2)}, u32[]{:S(2)}) collective-permute-start(bf16[64,2304]{1,0:T(8,128)(2,1)} %get-tuple-element.202), channel_id=1, source_target_pairs={{0,24},{8,16},{16,8},{24,0},{1,25},{9,17},{17,9},{25,1},{2,26},{10... | collective-permute-start | bytes 884744 | tf_op jit(solution)/shard_map/ppermute | solution.py:24
  118.0 49.3 %collective-permute-start.18 = (bf16[448,2304]{1,0:T(8,128)(2,1)}, bf16[448,2304]{1,0:T(8,128)(2,1)}, u32[]{:S(2)}, u32[]{:S(2)}) collective-permute-start(bf16[448,2304]{1,0:T(8,128)(2,1)} %get-tuple-element.200), channel_id=1, source_target_pairs={{0,8},{8,0},{16,24},{24,16},{1,9},{9,1},{17,25},{25,17},{2,10},{10... | collective-permute-start | bytes 6193160 | tf_op jit(solution)/shard_map/ppermute | solution.py:24
  119.1 48.2 %collective-permute-start.19 = (bf16[448,2304]{1,0:T(8,128)(2,1)}, bf16[448,2304]{1,0:T(8,128)(2,1)}, u32[]{:S(2)}, u32[]{:S(2)}) collective-permute-start(bf16[448,2304]{1,0:T(8,128)(2,1)} %get-tuple-element.201), channel_id=1, source_target_pairs={{0,16},{8,24},{16,0},{24,8},{1,17},{9,25},{17,1},{25,9},{2,18},{10... | collective-permute-start | bytes 6193160 | tf_op jit(solution)/shard_map/ppermute | solution.py:24
  170.6 171.7 %all-gather.14.cloned.1.call-start = ((), (), s32[]{:S(2)}) async-start(), calls=%async_computation.10 | async-start | bytes 8257536 | tf_op jit(solution)/shard_map/all_gather | solution.py:865
  171.2 418.7 %reduce-scatter.7.cloned.1.call-start = ((), (), s32[]{:S(2)}) async-start(), calls=%async_computation.11 | async-start | bytes 8257536 | tf_op jit(solution)/shard_map/reduce_scatter | solution.py:868
  174.4 17.6 %collective-permute-start.11 = (bf16[192,2048]{1,0:T(8,128)(2,1)S(1)}, bf16[192,2048]{1,0:T(8,128)(2,1)S(1)}, u32[]{:S(2)}, u32[]{:S(2)}) collective-permute-start(bf16[192,2048]{1,0:T(8,128)(2,1)S(1)} %get-tuple-element.347), channel_id=1, source_target_pairs={{0,16},{8,24},{16,0},{24,8},{1,17},{9,25},{17,1},{25,9},{2,18},{10... | collective-permute-start | bytes 2359304 | tf_op jit(solution)/shard_map/ppermute | solution.py:24
  175.9 17.6 %collective-permute-start.10 = (bf16[192,2048]{1,0:T(8,128)(2,1)S(1)}, bf16[192,2048]{1,0:T(8,128)(2,1)S(1)}, u32[]{:S(2)}, u32[]{:S(2)}) collective-permute-start(bf16[192,2048]{1,0:T(8,128)(2,1)S(1)} %get-tuple-element.348), channel_id=1, source_target_pairs={{0,8},{8,0},{16,24},{24,16},{1,9},{9,1},{17,25},{25,17},{2,10},{10... | collective-permute-start | bytes 2359304 | tf_op jit(solution)/shard_map/ppermute | solution.py:24
  196.8 33.9 %collective-permute-start.12 = (bf16[384,2048]{1,0:T(8,128)(2,1)}, bf16[384,2048]{1,0:T(8,128)(2,1)}, u32[]{:S(2)}, u32[]{:S(2)}) collective-permute-start(bf16[384,2048]{1,0:T(8,128)(2,1)} %get-tuple-element.190), channel_id=1, source_target_pairs={{0,8},{8,0},{16,24},{24,16},{1,9},{9,1},{17,25},{25,17},{2,10},{10... | collective-permute-start | bytes 4718600 | tf_op jit(solution)/shard_map/ppermute | solution.py:24
  197.1 33.6 %collective-permute-start.13 = (bf16[384,2048]{1,0:T(8,128)(2,1)}, bf16[384,2048]{1,0:T(8,128)(2,1)}, u32[]{:S(2)}, u32[]{:S(2)}) collective-permute-start(bf16[384,2048]{1,0:T(8,128)(2,1)} %get-tuple-element.191), channel_id=1, source_target_pairs={{0,16},{8,24},{16,0},{24,8},{1,17},{9,25},{17,1},{25,9},{2,18},{10... | collective-permute-start | bytes 4718600 | tf_op jit(solution)/shard_map/ppermute | solution.py:24
  235.5 33.0 %collective-permute-start.15 = (bf16[384,2048]{1,0:T(8,128)(2,1)S(1)}, bf16[384,2048]{1,0:T(8,128)(2,1)S(1)}, u32[]{:S(2)}, u32[]{:S(2)}) collective-permute-start(bf16[384,2048]{1,0:T(8,128)(2,1)S(1)} %get-tuple-element.193.refs_0_), channel_id=1, source_target_pairs={{0,16},{8,24},{16,0},{24,8},{1,17},{9,25},{17,1},{25,9},{2,18},{10... | collective-permute-start | bytes 4718600 | tf_op jit(solution)/shard_map/ppermute | solution.py:24
  236.2 32.5 %collective-permute-start.14 = (bf16[384,2048]{1,0:T(8,128)(2,1)S(1)}, bf16[384,2048]{1,0:T(8,128)(2,1)S(1)}, u32[]{:S(2)}, u32[]{:S(2)}) collective-permute-start(bf16[384,2048]{1,0:T(8,128)(2,1)S(1)} %get-tuple-element.193.refs_0_), channel_id=1, source_target_pairs={{0,8},{8,0},{16,24},{24,16},{1,9},{9,1},{17,25},{25,17},{2,10},{10... | collective-permute-start | bytes 4718600 | tf_op jit(solution)/shard_map/ppermute | solution.py:24
  272.0 15.0 %collective-permute-start.17 = (bf16[192,2048]{1,0:T(8,128)(2,1)}, bf16[192,2048]{1,0:T(8,128)(2,1)S(1)}, u32[]{:S(2)}, u32[]{:S(2)}) collective-permute-start(bf16[192,2048]{1,0:T(8,128)(2,1)} %slice.280), channel_id=1, source_target_pairs={{0,8},{8,0},{16,24},{24,16},{1,9},{9,1},{17,25},{25,17},{2,10},{10... | collective-permute-start | bytes 2359304 | tf_op jit(solution)/shard_map/ppermute | solution.py:24
  273.5 14.5 %collective-permute-start.16 = (bf16[192,2048]{1,0:T(8,128)(2,1)}, bf16[192,2048]{1,0:T(8,128)(2,1)}, u32[]{:S(2)}, u32[]{:S(2)}) collective-permute-start(bf16[192,2048]{1,0:T(8,128)(2,1)} %slice.279), channel_id=1, source_target_pairs={{0,16},{8,24},{16,0},{24,8},{1,17},{9,25},{17,1},{25,9},{2,18},{10... | collective-permute-start | bytes 2359304 | tf_op jit(solution)/shard_map/ppermute | solution.py:24
  292.2 24.9 %collective-permute-start.22 = (bf16[192,2048]{1,0:T(8,128)(2,1)}, bf16[192,2048]{1,0:T(8,128)(2,1)S(1)}, u32[]{:S(2)}, u32[]{:S(2)}) collective-permute-start(bf16[192,2048]{1,0:T(8,128)(2,1)} %slice.291), channel_id=1, source_target_pairs={{0,8},{8,0},{16,24},{24,16},{1,9},{9,1},{17,25},{25,17},{2,10},{10... | collective-permute-start | bytes 2359304 | tf_op jit(solution)/shard_map/ppermute | solution.py:24
  293.1 24.1 %collective-permute-start.21 = (bf16[192,2048]{1,0:T(8,128)(2,1)}, bf16[192,2048]{1,0:T(8,128)(2,1)}, u32[]{:S(2)}, u32[]{:S(2)}) collective-permute-start(bf16[192,2048]{1,0:T(8,128)(2,1)} %slice.290), channel_id=1, source_target_pairs={{0,16},{8,24},{16,0},{24,8},{1,17},{9,25},{17,1},{25,9},{2,18},{10... | collective-permute-start | bytes 2359304 | tf_op jit(solution)/shard_map/ppermute | solution.py:24
  317.2 33.3 %collective-permute-start.24 = (bf16[1536,512]{1,0:T(8,128)(2,1)}, bf16[1536,512]{1,0:T(8,128)(2,1)}, u32[]{:S(2)}, u32[]{:S(2)}) collective-permute-start(bf16[1536,512]{1,0:T(8,128)(2,1)} %get-tuple-element.219.refs_5_), channel_id=1, source_target_pairs={{0,16},{8,24},{16,0},{24,8},{1,17},{9,25},{17,1},{25,9},{2,18},{10... | collective-permute-start | bytes 4718600 | tf_op jit(solution)/shard_map/ppermute | solution.py:24
  317.8 32.7 %collective-permute-start.23 = (bf16[1536,512]{1,0:T(8,128)(2,1)}, bf16[1536,512]{1,0:T(8,128)(2,1)}, u32[]{:S(2)}, u32[]{:S(2)}) collective-permute-start(bf16[1536,512]{1,0:T(8,128)(2,1)} %get-tuple-element.219.refs_5_), channel_id=1, source_target_pairs={{0,8},{8,0},{16,24},{24,16},{1,9},{9,1},{17,25},{25,17},{2,10},{10... | collective-permute-start | bytes 4718600 | tf_op jit(solution)/shard_map/ppermute | solution.py:24
  348.5 29.2 %collective-permute-start.26 = (bf16[768,512]{1,0:T(8,128)(2,1)S(1)}, bf16[768,512]{1,0:T(8,128)(2,1)S(1)}, u32[]{:S(2)}, u32[]{:S(2)}) collective-permute-start(bf16[768,512]{1,0:T(8,128)(2,1)S(1)} %get-tuple-element.345), channel_id=1, source_target_pairs={{0,16},{8,24},{16,0},{24,8},{1,17},{9,25},{17,1},{25,9},{2,18},{10... | collective-permute-start | bytes 2359304 | tf_op jit(solution)/shard_map/ppermute | solution.py:24
  350.3 27.4 %collective-permute-start.25 = (bf16[768,512]{1,0:T(8,128)(2,1)S(1)}, bf16[768,512]{1,0:T(8,128)(2,1)S(1)}, u32[]{:S(2)}, u32[]{:S(2)}) collective-permute-start(bf16[768,512]{1,0:T(8,128)(2,1)S(1)} %get-tuple-element.346), channel_id=1, source_target_pairs={{0,8},{8,0},{16,24},{24,16},{1,9},{9,1},{17,25},{25,17},{2,10},{10... | collective-permute-start | bytes 2359304 | tf_op jit(solution)/shard_map/ppermute | solution.py:24
  352.8 28.4 %collective-permute-start.30 = (bf16[768,512]{1,0:T(8,128)(2,1)S(1)}, bf16[768,512]{1,0:T(8,128)(2,1)S(1)}, u32[]{:S(2)}, u32[]{:S(2)}) collective-permute-start(bf16[768,512]{1,0:T(8,128)(2,1)S(1)} %slice.296), channel_id=1, source_target_pairs={{0,8},{8,0},{16,24},{24,16},{1,9},{9,1},{17,25},{25,17},{2,10},{10... | collective-permute-start | bytes 2359304 | tf_op jit(solution)/shard_map/ppermute | solution.py:24
  354.8 26.5 %collective-permute-start.29 = (bf16[768,512]{1,0:T(8,128)(2,1)S(1)}, bf16[768,512]{1,0:T(8,128)(2,1)S(1)}, u32[]{:S(2)}, u32[]{:S(2)}) collective-permute-start(bf16[768,512]{1,0:T(8,128)(2,1)S(1)} %slice.295), channel_id=1, source_target_pairs={{0,16},{8,24},{16,0},{24,8},{1,17},{9,25},{17,1},{25,9},{2,18},{10... | collective-permute-start | bytes 2359304 | tf_op jit(solution)/shard_map/ppermute | solution.py:24
  408.8 191.8 %reduce-scatter.9.cloned.1.call-start = ((), (), s32[]{:S(2)}) async-start(), calls=%async_computation.12 | async-start | bytes 8257536 | tf_op jit(solution)/shard_map/reduce_scatter | solution.py:868
  408.9 32.0 %collective-permute-start.27 = (bf16[1536,512]{1,0:T(8,128)(2,1)}, bf16[1536,512]{1,0:T(8,128)(2,1)S(1)}, u32[]{:S(2)}, u32[]{:S(2)}) collective-permute-start(bf16[1536,512]{1,0:T(8,128)(2,1)} %copy-done.72), channel_id=1, source_target_pairs={{0,8},{8,0},{16,24},{24,16},{1,9},{9,1},{17,25},{25,17},{2,10},{10... | collective-permute-start | bytes 4718600 | tf_op jit(solution)/shard_map/ppermute | solution.py:24
  410.2 32.0 %collective-permute-start.28 = (bf16[1536,512]{1,0:T(8,128)(2,1)S(1)}, bf16[1536,512]{1,0:T(8,128)(2,1)S(1)}, u32[]{:S(2)}, u32[]{:S(2)}) collective-permute-start(bf16[1536,512]{1,0:T(8,128)(2,1)S(1)} %copy-done.70), channel_id=1, source_target_pairs={{0,16},{8,24},{16,0},{24,8},{1,17},{9,25},{17,1},{25,9},{2,18},{10... | collective-permute-start | bytes 4718600 | tf_op jit(solution)/shard_map/ppermute | solution.py:24
  459.3 21.5 %collective-permute-start.31 = (bf16[192,2048]{1,0:T(8,128)(2,1)S(1)}, bf16[192,2048]{1,0:T(8,128)(2,1)S(1)}, u32[]{:S(2)}, u32[]{:S(2)}) collective-permute-start(bf16[192,2048]{1,0:T(8,128)(2,1)S(1)} %get-tuple-element.231), channel_id=1, source_target_pairs={{0,8},{8,0},{16,24},{24,16},{1,9},{9,1},{17,25},{25,17},{2,10},{10... | collective-permute-start | bytes 2359304 | tf_op jit(solution)/shard_map/ppermute | solution.py:24
  460.8 20.0 %collective-permute-start.32 = (bf16[192,2048]{1,0:T(8,128)(2,1)S(1)}, bf16[192,2048]{1,0:T(8,128)(2,1)S(1)}, u32[]{:S(2)}, u32[]{:S(2)}) collective-permute-start(bf16[192,2048]{1,0:T(8,128)(2,1)S(1)} %get-tuple-element.232), channel_id=1, source_target_pairs={{0,16},{8,24},{16,0},{24,8},{1,17},{9,25},{17,1},{25,9},{2,18},{10... | collective-permute-start | bytes 2359304 | tf_op jit(solution)/shard_map/ppermute | solution.py:24
  501.3 167.8 %reduce-scatter.13.cloned.1.call-start = ((), (), s32[]{:S(2)}) async-start(), calls=%async_computation.14 | async-start | bytes 2359296 | tf_op jit(solution)/shard_map/reduce_scatter | solution.py:868
  501.3 31.5 %collective-permute-start.33 = (bf16[384,2048]{1,0:T(8,128)(2,1)}, bf16[384,2048]{1,0:T(8,128)(2,1)}, u32[]{:S(2)}, u32[]{:S(2)}) collective-permute-start(bf16[384,2048]{1,0:T(8,128)(2,1)} %copy-done.73), channel_id=1, source_target_pairs={{0,8},{8,0},{16,24},{24,16},{1,9},{9,1},{17,25},{25,17},{2,10},{10... | collective-permute-start | bytes 4718600 | tf_op jit(solution)/shard_map/ppermute | solution.py:24
  502.0 31.0 %collective-permute-start.34 = (bf16[384,2048]{1,0:T(8,128)(2,1)}, bf16[384,2048]{1,0:T(8,128)(2,1)}, u32[]{:S(2)}, u32[]{:S(2)}) collective-permute-start(bf16[384,2048]{1,0:T(8,128)(2,1)} %copy-done.71), channel_id=1, source_target_pairs={{0,16},{8,24},{16,0},{24,8},{1,17},{9,25},{17,1},{25,9},{2,18},{10... | collective-permute-start | bytes 4718600 | tf_op jit(solution)/shard_map/ppermute | solution.py:24
  510.2 158.9 %reduce-scatter.11.cloned.1.call-start = ((), (), s32[]{:S(2)}) async-start(), calls=%async_computation.13 | async-start | bytes 2359296 | tf_op jit(solution)/shard_map/reduce_scatter | solution.py:868
  539.8 32.9 %collective-permute-start.36 = (bf16[384,2048]{1,0:T(8,128)(2,1)S(1)}, bf16[384,2048]{1,0:T(8,128)(2,1)S(1)}, u32[]{:S(2)}, u32[]{:S(2)}) collective-permute-start(bf16[384,2048]{1,0:T(8,128)(2,1)S(1)} %get-tuple-element.251), channel_id=1, source_target_pairs={{0,16},{8,24},{16,0},{24,8},{1,17},{9,25},{17,1},{25,9},{2,18},{10... | collective-permute-start | bytes 4718600 | tf_op jit(solution)/shard_map/ppermute | solution.py:24
  540.5 34.3 %collective-permute-start.35 = (bf16[384,2048]{1,0:T(8,128)(2,1)S(1)}, bf16[384,2048]{1,0:T(8,128)(2,1)S(1)}, u32[]{:S(2)}, u32[]{:S(2)}) collective-permute-start(bf16[384,2048]{1,0:T(8,128)(2,1)S(1)} %get-tuple-element.251), channel_id=1, source_target_pairs={{0,8},{8,0},{16,24},{24,16},{1,9},{9,1},{17,25},{25,17},{2,10},{10... | collective-permute-start | bytes 4718600 | tf_op jit(solution)/shard_map/ppermute | solution.py:24
  574.9 12.5 %collective-permute-start.38 = (bf16[192,2048]{1,0:T(8,128)(2,1)S(1)}, bf16[192,2048]{1,0:T(8,128)(2,1)S(1)}, u32[]{:S(2)}, u32[]{:S(2)}) collective-permute-start(bf16[192,2048]{1,0:T(8,128)(2,1)S(1)} %slice.298), channel_id=1, source_target_pairs={{0,8},{8,0},{16,24},{24,16},{1,9},{9,1},{17,25},{25,17},{2,10},{10... | collective-permute-start | bytes 2359304 | tf_op jit(solution)/shard_map/ppermute | solution.py:24
  576.6 12.0 %collective-permute-start.37 = (bf16[192,2048]{1,0:T(8,128)(2,1)S(1)}, bf16[192,2048]{1,0:T(8,128)(2,1)S(1)}, u32[]{:S(2)}, u32[]{:S(2)}) collective-permute-start(bf16[192,2048]{1,0:T(8,128)(2,1)S(1)} %slice.297), channel_id=1, source_target_pairs={{0,16},{8,24},{16,0},{24,8},{1,17},{9,25},{17,1},{25,9},{2,18},{10... | collective-permute-start | bytes 2359304 | tf_op jit(solution)/shard_map/ppermute | solution.py:24
  595.2 134.4 %reduce-scatter.17.cloned.1.call-start = ((), (), s32[]{:S(2)}) async-start(), calls=%async_computation.16 | async-start | bytes 2359296 | tf_op jit(solution)/shard_map/reduce_scatter | solution.py:868
  620.1 153.3 %reduce-scatter.15.cloned.1.call-start = ((), (), s32[]{:S(2)}) async-start(), calls=%async_computation.15 | async-start | bytes 7077888 | tf_op jit(solution)/shard_map/reduce_scatter | solution.py:868
  622.3 24.5 %collective-permute-start.41 = (bf16[384,512]{1,0:T(8,128)(2,1)S(1)}, bf16[384,512]{1,0:T(8,128)(2,1)S(1)}, u32[]{:S(2)}, u32[]{:S(2)}) collective-permute-start(bf16[384,512]{1,0:T(8,128)(2,1)S(1)} %get-tuple-element.341), channel_id=1, source_target_pairs={{0,24},{8,16},{16,8},{24,0},{1,25},{9,17},{17,9},{25,1},{2,26},{10... | collective-permute-start | bytes 1179656 | tf_op jit(solution)/shard_map/ppermute | solution.py:24
  623.4 23.3 %collective-permute-start.40 = (bf16[384,512]{1,0:T(8,128)(2,1)S(1)}, bf16[384,512]{1,0:T(8,128)(2,1)S(1)}, u32[]{:S(2)}, u32[]{:S(2)}) collective-permute-start(bf16[384,512]{1,0:T(8,128)(2,1)S(1)} %get-tuple-element.342), channel_id=1, source_target_pairs={{0,16},{8,24},{16,0},{24,8},{1,17},{9,25},{17,1},{25,9},{2,18},{10... | collective-permute-start | bytes 1179656 | tf_op jit(solution)/shard_map/ppermute | solution.py:24
  624.1 22.7 %collective-permute-start.39 = (bf16[384,512]{1,0:T(8,128)(2,1)S(1)}, bf16[384,512]{1,0:T(8,128)(2,1)S(1)}, u32[]{:S(2)}, u32[]{:S(2)}) collective-permute-start(bf16[384,512]{1,0:T(8,128)(2,1)S(1)} %get-tuple-element.343), channel_id=1, source_target_pairs={{0,8},{8,0},{16,24},{24,16},{1,9},{9,1},{17,25},{25,17},{2,10},{10... | collective-permute-start | bytes 1179656 | tf_op jit(solution)/shard_map/ppermute | solution.py:24
  678.9 19.3 %collective-permute-start.42 = (bf16[192,2048]{1,0:T(8,128)(2,1)S(1)}, bf16[192,2048]{1,0:T(8,128)(2,1)S(1)}, u32[]{:S(2)}, u32[]{:S(2)}) collective-permute-start(bf16[192,2048]{1,0:T(8,128)(2,1)S(1)} %get-tuple-element.279), channel_id=1, source_target_pairs={{0,8},{8,0},{16,24},{24,16},{1,9},{9,1},{17,25},{25,17},{2,10},{10... | collective-permute-start | bytes 2359304 | tf_op jit(solution)/shard_map/ppermute | solution.py:24
  679.2 19.1 %collective-permute-start.43 = (bf16[192,2048]{1,0:T(8,128)(2,1)S(1)}, bf16[192,2048]{1,0:T(8,128)(2,1)S(1)}, u32[]{:S(2)}, u32[]{:S(2)}) collective-permute-start(bf16[192,2048]{1,0:T(8,128)(2,1)S(1)} %get-tuple-element.280), channel_id=1, source_target_pairs={{0,16},{8,24},{16,0},{24,8},{1,17},{9,25},{17,1},{25,9},{2,18},{10... | collective-permute-start | bytes 2359304 | tf_op jit(solution)/shard_map/ppermute | solution.py:24
  701.8 27.9 %collective-permute-start.44 = (bf16[384,2048]{1,0:T(8,128)(2,1)}, bf16[384,2048]{1,0:T(8,128)(2,1)}, u32[]{:S(2)}, u32[]{:S(2)}) collective-permute-start(bf16[384,2048]{1,0:T(8,128)(2,1)} %get-tuple-element.289), channel_id=1, source_target_pairs={{0,8},{8,0},{16,24},{24,16},{1,9},{9,1},{17,25},{25,17},{2,10},{10... | collective-permute-start | bytes 4718600 | tf_op jit(solution)/shard_map/ppermute | solution.py:24
  703.5 26.1 %collective-permute-start.45 = (bf16[384,2048]{1,0:T(8,128)(2,1)}, bf16[384,2048]{1,0:T(8,128)(2,1)}, u32[]{:S(2)}, u32[]{:S(2)}) collective-permute-start(bf16[384,2048]{1,0:T(8,128)(2,1)} %get-tuple-element.290), channel_id=1, source_target_pairs={{0,16},{8,24},{16,0},{24,8},{1,17},{9,25},{17,1},{25,9},{2,18},{10... | collective-permute-start | bytes 4718600 | tf_op jit(solution)/shard_map/ppermute | solution.py:24
  738.8 11.3 %collective-permute-start.46 = (f32[16,14,64]{2,1,0:T(8,128)S(1)}, f32[16,14,64]{2,1,0:T(8,128)S(1)}, u32[]{:S(2)}, u32[]{:S(2)}) collective-permute-start(f32[16,14,64]{2,1,0:T(8,128)S(1)} %bitcast.114), channel_id=1, source_target_pairs={{0,4},{1,5},{2,6},{3,7},{4,0},{5,1},{6,2},{7,3},{8,12},{9,13},{10,... | collective-permute-start | bytes 172040 | tf_op jit(solution)/shard_map/ppermute | solution.py:24
  750.1 6.4 collective-permute-start.47
  751.0 8.5 %collective-permute-start.51 = (bf16[64,2816]{1,0:T(8,128)(2,1)S(1)}, bf16[64,2816]{1,0:T(8,128)(2,1)S(1)}, u32[]{:S(2)}, u32[]{:S(2)}) collective-permute-start(bf16[64,2816]{1,0:T(8,128)(2,1)S(1)} %get-tuple-element.349), channel_id=1, source_target_pairs={{0,24},{8,16},{16,8},{24,0},{1,25},{9,17},{17,9},{25,1},{2,26},{10... | collective-permute-start | bytes 1081352 | tf_op jit(solution)/shard_map/ppermute | solution.py:24
  751.9 11.5 %collective-permute-start.50 = (bf16[64,2816]{1,0:T(8,128)(2,1)S(1)}, bf16[64,2816]{1,0:T(8,128)(2,1)S(1)}, u32[]{:S(2)}, u32[]{:S(2)}) collective-permute-start(bf16[64,2816]{1,0:T(8,128)(2,1)S(1)} %get-tuple-element.350), channel_id=1, source_target_pairs={{0,16},{8,24},{16,0},{24,8},{1,17},{9,25},{17,1},{25,9},{2,18},{10... | collective-permute-start | bytes 1081352 | tf_op jit(solution)/shard_map/ppermute | solution.py:24
  753.2 10.2 %collective-permute-start.49 = (bf16[64,2816]{1,0:T(8,128)(2,1)S(1)}, bf16[64,2816]{1,0:T(8,128)(2,1)S(1)}, u32[]{:S(2)}, u32[]{:S(2)}) collective-permute-start(bf16[64,2816]{1,0:T(8,128)(2,1)S(1)} %get-tuple-element.351), channel_id=1, source_target_pairs={{0,8},{8,0},{16,24},{24,16},{1,9},{9,1},{17,25},{25,17},{2,10},{10... | collective-permute-start | bytes 1081352 | tf_op jit(solution)/shard_map/ppermute | solution.py:24
  774.6 6.7 collective-permute-start.56
  775.6 7.8 collective-permute-start.55
  776.8 6.5 collective-permute-start.54
  (122 other events, 1017.5 us)
Sparse Core Ops, SparseCore 0:
  33.0 67.9 all-gather.7
  103.3 27.8 all-gather.5
  132.7 28.6 all-gather.9
  170.7 91.1 all-gather.11
  263.4 71.8 all-gather.13
  408.9 81.0 reduce-scatter.6
  501.4 79.9 reduce-scatter.8
  583.6 34.1 reduce-scatter.12
  620.2 34.4 reduce-scatter.10
  657.3 34.5 reduce-scatter.16
  694.2 72.5 reduce-scatter.14

commit v12 on v11

--- a/solution.py
+++ b/solution.py
@@ -355,9 +355,11 @@
     return centred, lax.rsqrt(spread + EPSILON)
 
 
-def mix_body(count, norm, groups, counts, per, here, *refs):
+def mix_body(count, norm, groups, counts, per, mixed, open_up, here, *refs):
     pieces, (marks_ref, vec_ref) = refs[: len(counts)], refs[len(counts) : len(counts) + 2]
-    outs, last, held = refs[len(counts) + 2 : -2], refs[-2], refs[-1]
+    weights = refs[len(counts) + 2 : len(counts) + 2 + len(mixed)]
+    outs, last, held = refs[len(counts) + 2 + len(mixed) : -2], refs[-2], refs[-1]
+    products = outs[count + 1 :]
 
     @pl.when(pl.program_id(0) == 0)
     def _():
@@ -377,18 +379,34 @@
     step = values - previous
     outs[count][...] = step.astype(BF)
     for i in range(count):
-        outs[i][...] = (previous + step * vec_ref[2 + i : 3 + i, :]).astype(BF)
-
-
-def mixes(pieces, marks, vec, count, norm, groups, here, tile, per):
+        mix = (previous + step * vec_ref[2 + i : 3 + i, :]).astype(BF)
+        outs[i][...] = mix
+        if i in mixed:
+            k = mixed.index(i)
+            product = dot(mix, weights[k][...], NN)
+            if open_up:
+                products[0][...] = product
+                products[1][...] = (1.0 / (1.0 + jnp.exp(-product))).astype(BF)
+            else:
+                products[k][...] = product.astype(BF)
+
+
+def mixes(pieces, marks, vec, count, norm, groups, here, tile, per, weights, open_up):
     rows, width = marks.shape[0], pieces[0].shape[1]
     own = block((tile, width), lambda i, h: (relative(i, per, h), 0))
-    return kernel(
-        partial(mix_body, count, norm, groups, counts_of(pieces, tile), per), "mixes", (rows // tile,), here,
+    outs = [((rows, width), BF, own)] * (count + 1)
+    for _, _, _, part in weights:
+        narrow = block((tile, part), lambda i, h: (relative(i, per, h), 0))
+        outs += [((rows, part), F32 if open_up else BF, narrow)] + [((rows, part), BF, narrow)] * open_up
+    return kernel(
+        partial(mix_body, count, norm, groups, counts_of(pieces, tile), per, [w[0] for w in weights], open_up),
+        "mixes", (rows // tile,), here,
         pieced(pieces, tile, width, lambda h: 0, lambda i, h: relative(i, per, h))
-        + [(marks, block((tile, PAIR), lambda i, h: (i, 0))), (vec, fixed(vec.shape))],
-        [((rows, width), BF, own)] * (count + 1),
+        + [(marks, block((tile, PAIR), lambda i, h: (i, 0))), (vec, fixed(vec.shape))]
+        + [(w, pl.BlockSpec((width, part), lambda *_, at=at: (0, at))) for _, w, at, part in weights],
+        outs,
         [pltpu.VMEM((8, width), F32), pltpu.VMEM((tile, width), BF)],
+        vmem=58,
     )
 
 
@@ -901,15 +919,12 @@
     full_g = gather_dp(after(columns_g, tokens_all[1:3], rows_one))
     own_o = gather_dp(after(w_output, tokens_all))
 
-    mix_r, mix_k, mix_v, mix_g, step = mixes(
-        turn_pieces(tokens_all), marks, rows_one, 4, True, within, here, tile, own_rows // tile
-    )
-    recept, keyed, valued = (
-        dot(m, full_in[:, i * part : (i + 1) * part], NN).astype(BF)
-        for i, m in enumerate((mix_r, mix_k, mix_v))
+    mix_r, mix_k, mix_v, mix_g, step, recept, keyed, valued = mixes(
+        turn_pieces(tokens_all), marks, rows_one, 4, True, within, here, tile, own_rows // tile,
+        [(i, full_in, i, part) for i in range(3)], False,
     )
     projected = (recept, keyed, valued)
-    ffn_weights = after([ffn_key, ffn_receptance], mix_r)
+    ffn_weights = after([ffn_key, ffn_receptance], tokens_all)
     if seq == 4:
         pieces_c = trade_seq(cut_with_rider(ffn_weights, grad_b, here))
     else:
@@ -929,12 +944,11 @@
     normed_two = gather_seq(normed_two)
     if seq == 4:
         grad_all = gather_second(grad_b, *after(pieces_c[1:3], normed_two))
-    mix_k2, mix_r2, step_two = mixes(
+    mix_k2, mix_r2, step_two, recept_pre, opened = mixes(
         turn_pieces(normed_two), marks, rows_of(turned, 10, 11, 12, 13), 2, False, within, here, tile,
-        own_rows // tile,
-    )
-    recept_pre = dot(mix_r2, full_cr, NN)
-    opened = gather_seq(after(jax.nn.sigmoid(recept_pre).astype(BF), grad_all[3:]))
+        own_rows // tile, [(1, full_cr, 0, part)], True,
+    )
+    opened = gather_seq(after(opened, grad_all[3:]))
     key_pre = dot(mix_k2, full_ck, NN)
     smooth = jax.nn.softplus(key_pre)
     hidden = (smooth * smooth).astype(BF)
@@ -954,7 +968,6 @@
     d_hidden = dot(after(d_value, grad_cv), full_cv, NT)
     d_key_two = (d_hidden * slope.astype(F32)).astype(BF)
     channel, d_recept_two = channel_out(value_terms, recept_pre, grad_all, here, tile)
-    half, first = part // 2, hidden_width // (part // 2)
     grad_ck, grad_cr = [], []
 
     def beside_two(relayed):
@@ -963,11 +976,10 @@
         return grad_ck, grad_cr
 
     terms_two, sums_two = mixes_back_scatter(
-        [(0, d_key_two, 0, full_c, 0, hidden_width)]
-        + [(1, d_recept_two, i, full_c, first + i, half) for i in range(2)],
+        [(0, d_key_two, 0, full_c, 0, hidden_width), (1, d_recept_two, 0, full_cr, 0, part)],
         step_two, marks, rows_of(turned, 12, 13), here, seq, beside_two,
     )
-    summed_ck, summed_cr = scatter_dp(grad_ck[0]), scatter_dp(grad_cr[0])
+    summed_ck = scatter_dp(grad_ck[0])
     if within is None:
         terms_two = [outside(t, groups, unit, back=True) for t in terms_two]
     d_after, d_attn, norm_sums_two = norm_back(terms_two, after_mix, grad_b, rows_of(vec, 10), within, here)
@@ -984,7 +996,7 @@
     d_mixed = after(d_mixed, summed_ck, grad_wo)
     d_wkv, d_gate, gate_sums = gate_backward(wkv, gate_pre, d_mixed, tables[5], here)
     grad_g = dot(mix_g, d_gate, TN).astype(BF)
-    summed_g = scatter_dp(grad_g)
+    summed_crg = scatter_dp(jnp.concatenate([grad_cr[0], grad_g], axis=1))
     d_recept, d_keyed, d_valued, sums = wkv_backward(
         recept, keyed, valued, after(d_wkv, grad_g), states, tables, here, per
     )
@@ -1001,7 +1013,7 @@
         others.append(after(summed_cv, relayed).astype(F32))
         return others
 
-    d_recept, d_keyed = after((d_recept, d_keyed), grads_in, summed_o, summed_cr)
+    d_recept, d_keyed = after((d_recept, d_keyed), grads_in, summed_o)
     terms, sums_one = mixes_back_scatter(
         [(i, d, 0, full_in, i, part) for i, d in enumerate((d_recept, d_keyed, d_valued))]
         + [(3, d_gate, 0, full_g, 0, part)],
@@ -1012,7 +1024,7 @@
         terms = [outside(t, groups, unit, back=True) for t in terms]
     tokens_grad, _, norm_sums = norm_back(terms, inputs_b, d_after, rows_of(vec, 0), within, here)
 
-    summed_c = jnp.concatenate(after([summed_ck, summed_cr, summed_g], terms), axis=1)
+    summed_c = jnp.concatenate(after([summed_ck, summed_crg], terms), axis=1)
     sum_ck, sum_cr, sum_g = owners_rows(summed_c, [ffn_key.shape[1], width, width])
     sum_o = summed_o.astype(F32)
 

time: 798 us -> 801 us (level)
  matrix products: 165 us -> 137 us
  waiting for transfers between devices: 219 us -> 245 us
  local copies, waits for them, and re-layouts: 75.8 us -> 63.3 us
  Pallas kernels: 232 us -> 244 us
    dot_general x25 -> x21, matrix products: 165 us -> 137 us  [dot(): return lax.dot_general(left, right, dims, preferred_element_type=F32)]
    ppermute x57, waiting for transfers between devices: 218 us -> 240 us  [swap(): return lax.ppermute(value, axis, [(i, i ^ distance) for i in range(size)])]
    pallas_call x33, Pallas kernels: 232 us -> 244 us  [kernel(): pl.pallas_call(body, out_shape=[jax.ShapeDtypeStruct(shape, kind) for sha...]
    unnamed x239 -> x216, local copies, waits for them, and re-layouts: 49.6 us -> 38.7 us
  transfers between devices with their start and end apart: 68 -> 67, of which waited for: 35 -> 38; matrix products, arithmetic and copies ran while one was open for 24% -> 20% of each run, Pallas kernels for 28% -> 29%
where the time goes in v12:
time: 801 us; the launch traced here: 790 us
  waiting for transfers between devices  245 us (31%)
  Pallas kernels  244 us (30%)
  matrix products  137 us (17%)
  starting transfers between devices  67.7 us (8%)
  local copies, waits for them, and re-layouts  63.3 us (8%)
  other arithmetic  17.2 us (2%)
  between operations  15.8 us (2%)
    pallas_call x33, Pallas kernels, kernel(): pl.pallas_call(body, out_shape=[jax.ShapeDtypeStruct(shape, kind) for sha...  244 us
    ppermute x57, waiting for transfers between devices, swap(): return lax.ppermute(value, axis, [(i, i ^ distance) for i in range(size)])  240 us
    dot_general x21, matrix products, dot(): return lax.dot_general(left, right, dims, preferred_element_type=F32)  137 us
    ppermute x57, starting transfers between devices, swap(): return lax.ppermute(value, axis, [(i, i ^ distance) for i in range(size)])  66.8 us
    unnamed x216, local copies, waits for them, and re-layouts  38.7 us
  transfers between devices with their start and end apart: 67, of which 38 were waited for; matrix products, arithmetic and copies ran while one was open for 20% of the time, Pallas kernels for 29%

profile of v12, /device:TPU:0, one launch (start us, length us, event | category | flops | bytes accessed | tf_op | source)
XLA Modules:
  0.0 790.4 jit_solution(12581050767633946514)
XLA Ops:
  11.9 3.0 collective-permute-start
  16.5 7.0 collective-permute-done.refs_1_
  23.5 7.7 collective-permute-done.1.refs_2_
  41.8 2.7 collective-permute-start.5
  45.8 7.6 collective-permute-done.5
  56.6 12.3 %collective-permute-done.7.refs_2_ = bf16[384,2048]{1,0:T(8,128)(2,1)} collective-permute-done((bf16[384,2048]{1,0:T(8,128)(2,1)}, bf16[384,2048]{1,0:T(8,128)(2,1)}, u32[]{:S(2)}, u32[]{:S(2)}) %collective-permute-start.7) | collective-permute-done | bytes 1572896 | tf_op jit(solution)/shard_map/ppermute | solution.py:24
  74.6 14.2 %collective-permute-done.9.refs_4_ = bf16[192,2048]{1,0:T(8,128)(2,1)} collective-permute-done((bf16[192,2048]{1,0:T(8,128)(2,1)S(1)}, bf16[192,2048]{1,0:T(8,128)(2,1)}, u32[]{:S(2)}, u32[]{:S(2)}) %collective-permute-start.9) | collective-permute-done | bytes 786464 | tf_op jit(solution)/shard_map/ppermute | solution.py:24
  97.4 2.8 all-gather.6.cloned.1.call-done.refs_7_.refs_8_.refs_9_.refs_10_
  100.2 25.9 %mixes.2 = (bf16[1536,2048]{1,0:T(8,128)(2,1)}, bf16[1536,2048]{1,0:T(8,128)(2,1)}, bf16[1536,2048]{1,0:T(8,128)(2,1)}, bf16[1536,2048]{1,0:T(8,128)(2,1)}, bf16...) custom-call(s32[1]{0:T(128)} %bitcast.here, ...), custom_call_target="tpu_custom_call" | custom-call | tf_op jit(solution)/shard_map/mixes/pallas_call | solution.py:135
  127.5 13.4 %wkv_forward.1 = (f32[1536,512]{1,0:T(8,128)}, bf16[12,512,128]{2,1,0:T(8,128)(2,1)S(1)}) custom-call(s32[1]{0:T(128)} %bitcast.here, bf16[1536,512]{1,0:T(8,128)(2,1)S(1)} %copy-done.15, bf16[1536,512]{1,0:T(8,128)(2,1)} %get-tuple-element.186.k_ref, bf16[1536,512]{1,0:T(8,128)(2,1)} %get-tuple-element.187.v_ref, f32[1536,128]{1,0:T(8,128)S(1)} %copy-done, ...), custom_call_target="tpu_custom_call" | custom-call | tf_op jit(solution)/shard_map/wkv_forward/pallas_call | solution.py:135
  143.7 10.1 %gate.1 = (f32[1536,512]{1,0:T(8,128)}, bf16[1536,512]{1,0:T(8,128)(2,1)S(1)}) custom-call(s32[1]{0:T(128)} %bitcast.here, bf16[1536,2048]{1,0:T(8,128)(2,1)} %get-tuple-element.182.refs_0_, bf16[2048,512]{1,0:T(8,128)(2,1)S(1)} %copy-done.8, f32[1536,512]{1,0:T(8,128)} %get-tuple-element.188.refs_2_.wkv_ref, f32[8,512]{1,0:T(8,128)S(1)} %maximum_maximum_fusion.par_ref.refs_3_), custom_call_target="tpu_custom_call" | custom-call | tf_op jit(solution)/shard_map/gate/pallas_call | solution.py:135
  155.0 3.4 stack_rows.3
  160.4 2.8 convolution_convert_fusion.7
  170.7 12.4 %collective-permute-done.11.high_ref = bf16[192,2048]{1,0:T(8,128)(2,1)S(1)} collective-permute-done((bf16[192,2048]{1,0:T(8,128)(2,1)S(1)}, bf16[192,2048]{1,0:T(8,128)(2,1)S(1)}, u32[]{:S(2)}, u32[]{:S(2)}) %collective-permute-start.11) | collective-permute-done | bytes 786464 | tf_op jit(solution)/shard_map/ppermute | solution.py:24
  184.3 3.3 relay.4
  191.5 2.8 convolution_convert_fusion.10.refs_0_
  194.3 29.1 %collective-permute-done.12.refs_1_ = bf16[384,2048]{1,0:T(8,128)(2,1)} collective-permute-done((bf16[384,2048]{1,0:T(8,128)(2,1)}, bf16[384,2048]{1,0:T(8,128)(2,1)}, u32[]{:S(2)}, u32[]{:S(2)}) %collective-permute-start.12) | collective-permute-done | bytes 1572896 | tf_op jit(solution)/shard_map/ppermute | solution.py:24
  224.6 4.8 after_norm.1
  230.5 33.1 %collective-permute-done.15.refs_2_ = bf16[384,2048]{1,0:T(8,128)(2,1)S(1)} collective-permute-done((bf16[384,2048]{1,0:T(8,128)(2,1)S(1)}, bf16[384,2048]{1,0:T(8,128)(2,1)S(1)}, u32[]{:S(2)}, u32[]{:S(2)}) %collective-permute-start.15) | collective-permute-done | bytes 1572896 | tf_op jit(solution)/shard_map/ppermute | solution.py:24
  266.6 14.3 %collective-permute-done.17.refs_4_ = bf16[192,2048]{1,0:T(8,128)(2,1)S(1)} collective-permute-done((bf16[192,2048]{1,0:T(8,128)(2,1)S(1)}, bf16[192,2048]{1,0:T(8,128)(2,1)S(1)}, u32[]{:S(2)}, u32[]{:S(2)}) %collective-permute-start.17) | collective-permute-done | bytes 786464 | tf_op jit(solution)/shard_map/ppermute | solution.py:24
  280.9 2.7 slice.278
  289.1 3.0 slice.326.refs_7_.refs_5_
  292.1 16.1 %mixes.3 = (bf16[1536,2048]{1,0:T(8,128)(2,1)}, bf16[1536,2048]{1,0:T(8,128)(2,1)}, bf16[1536,2048]{1,0:T(8,128)(2,1)}, f32[1536,512]{1,0:T(8,128)}, bf16[1536,512]{1,0:T(8,128)(2,1)}) custom-call(s32[1]{0:T(128)} %bitcast.here, bf16[384,2048]{1,0:T(8,128)(2,1)} %copy-done.33, bf16[384,2048]{1,0:T(8,128)(2,1)} %copy-done.73, bf16[384,2048]{1,0:T(8,128)(2,1)} %copy-done.72, ...), custom_call_target="tpu_custom_call" | custom-call | tf_op jit(solution)/shard_map/mixes/pallas_call | solution.py:135
  311.9 25.2 %multiply_convert_fusion.1 = (bf16[1536,1792]{1,0:T(8,128)(2,1)}, bf16[1536,1792]{1,0:T(8,128)(2,1)}) fusion(bf16[1536,2048]{1,0:T(8,128)(2,1)} %get-tuple-element.245, bf16[2048,2304]{1,0:T(8,128)(2,1)} %all-gather.12.cloned.1.call-done.refs_4_), kind=kOutput, calls=%fused_computation.2 | convolution fusion | flops 11312824320 | bytes 24641536 | tf_op jit(solution)/shard_map/dot_general | solution.py:639
  337.1 6.0 value_columns.7
  350.2 6.0 value_columns.6.two_ref
  357.5 6.0 value_columns.5.one_ref
  364.7 6.0 value_columns.4.refs_5_
  377.7 9.2 %spread_columns.2 = bf16[1536,2048]{1,0:T(8,128)(2,1)} custom-call(s32[1]{0:T(128)} %bitcast.here, bf16[384,2048]{1,0:T(8,128)(2,1)S(1)} %bitcast.96, bf16[448,2304]{1,0:T(8,128)(2,1)} %collective-permute-done.18.refs_1_, bf16[448,2304]{1,0:T(8,128)(2,1)} %collective-permute-done.19.refs_2_, bf16[192,2048]{1,0:T(8,128)(2,1)S(1)} %collective-permute-done.21.refs_3_, ...), custom_call_target="tpu_custom_call" | custom-call | tf_op jit(solution)/shard_map/spread_columns/pallas_call | solution.py:135
  386.9 16.1 %convolution_convert_fusion.1 = bf16[1792,2048]{1,0:T(8,128)(2,1)} fusion(bf16[1536,1792]{1,0:T(8,128)(2,1)S(1)} %bitcast.104, bf16[1536,2048]{1,0:T(8,128)(2,1)} %spread_columns.2), kind=kOutput, calls=%fused_computation.5 | convolution fusion | flops 11277959168 | bytes 19136512 | tf_op jit(solution)/shard_map/dot_general | solution.py:639
  406.1 18.8 %multiply_convert_fusion.refs_0_.refs_2_ = bf16[1536,1792]{1,0:T(8,128)(2,1)} fusion(bf16[1536,1792]{1,0:T(8,128)(2,1)} %get-tuple-element.227, bf16[1536,2048]{1,0:T(8,128)(2,1)} %spread_columns.2, bf16[1792,2048]{1,0:T(8,128)(2,1)} %all-gather.14.cloned.1.call-done.right_ref), kind=kOutput, calls=%fused_computation.1 | convolution fusion | flops 11282546688 | bytes 24641536 | tf_op jit(solution)/shard_map/dot_general | solution.py:639
  424.9 10.2 %collective-permute-done.27.refs_6_ = bf16[1536,512]{1,0:T(8,128)(2,1)S(1)} collective-permute-done((bf16[1536,512]{1,0:T(8,128)(2,1)}, bf16[1536,512]{1,0:T(8,128)(2,1)S(1)}, u32[]{:S(2)}, u32[]{:S(2)}) %collective-permute-start.27) | collective-permute-done | bytes 1572896 | tf_op jit(solution)/shard_map/ppermute | solution.py:24
  437.5 7.0 channel.1
  444.6 8.6 %mixes_back.6 = (bf16[192,2048]{1,0:T(8,128)(2,1)S(1)}, bf16[192,2048]{1,0:T(8,128)(2,1)S(1)}, f32[8,2048]{1,0:T(8,128)S(1)}) custom-call(s32[1]{0:T(128)} %bitcast.here, bf16[1536,1792]{1,0:T(8,128)(2,1)} %multiply_convert_fusion.refs_0_.refs_2_, bf16[1536,512]{1,0:T(8,128)(2,1)S(1)} %get-tuple-element.243.refs_1_.refs_3_, ...), custom_call_target="tpu_custom_call" | custom-call | tf_op jit(solution)/shard_map/mixes_back/pallas_call | solution.py:135
  456.3 16.1 %mixes_back.7 = (bf16[384,2048]{1,0:T(8,128)(2,1)S(1)}, bf16[384,2048]{1,0:T(8,128)(2,1)S(1)}, f32[8,2048]{1,0:T(8,128)S(1)}) custom-call(s32[1]{0:T(128)} %bitcast.here, bf16[1536,1792]{1,0:T(8,128)(2,1)} %multiply_convert_fusion.refs_0_.refs_2_, bf16[1536,512]{1,0:T(8,128)(2,1)S(1)} %get-tuple-element.243.refs_1_.refs_3_, ...), custom_call_target="tpu_custom_call" | custom-call | tf_op jit(solution)/shard_map/mixes_back/pallas_call | solution.py:135
  478.9 16.2 %convolution_convert_fusion = bf16[2048,1792]{1,0:T(8,128)(2,1)} fusion(bf16[1536,2048]{1,0:T(8,128)(2,1)} %get-tuple-element.245, bf16[1536,1792]{1,0:T(8,128)(2,1)S(1)} %bitcast.102), kind=kOutput, calls=%fused_computation.4 | convolution fusion | flops 11277959168 | bytes 19136512 | tf_op jit(solution)/shard_map/dot_general | solution.py:639
  498.0 8.9 %mixes_back.8 = (bf16[384,2048]{1,0:T(8,128)(2,1)S(1)}, f32[8,2048]{1,0:T(8,128)S(1)}) custom-call(s32[1]{0:T(128)} %bitcast.here, bf16[1536,1792]{1,0:T(8,128)(2,1)} %multiply_convert_fusion.refs_0_.refs_2_, bf16[1536,512]{1,0:T(8,128)(2,1)S(1)} %get-tuple-element.243.refs_1_.refs_3_, bf16[1536,1792]{1,0:T(8,128)(2,1)} %multiply_convert_fusion.refs_0_.refs_2_, ...), custom_call_target="tpu_custom_call" | custom-call | tf_op jit(solution)/shard_map/mixes_back/pallas_call | solution.py:135
  507.0 7.9 convolution_convert_fusion.6
  514.9 11.4 %collective-permute-done.33.refs_1_ = bf16[384,2048]{1,0:T(8,128)(2,1)S(1)} collective-permute-done((bf16[384,2048]{1,0:T(8,128)(2,1)}, bf16[384,2048]{1,0:T(8,128)(2,1)S(1)}, u32[]{:S(2)}, u32[]{:S(2)}) %collective-permute-start.33) | collective-permute-done | bytes 1572896 | tf_op jit(solution)/shard_map/ppermute | solution.py:24
  527.9 6.9 norm_back.2
  539.7 29.7 %collective-permute-done.36 = bf16[384,2048]{1,0:T(8,128)(2,1)S(1)} collective-permute-done((bf16[384,2048]{1,0:T(8,128)(2,1)S(1)}, bf16[384,2048]{1,0:T(8,128)(2,1)S(1)}, u32[]{:S(2)}, u32[]{:S(2)}) %collective-permute-start.36) | collective-permute-done | bytes 1572896 | tf_op jit(solution)/shard_map/ppermute | solution.py:24
  576.8 3.5 add_add_fusion
  584.9 5.3 add_convert_fusion
  591.7 2.6 convolution_convert_fusion.11
  596.9 8.6 %gate_backward.1 = (bf16[1536,512]{1,0:T(8,128)(2,1)S(1)}, bf16[1536,512]{1,0:T(8,128)(2,1)S(1)}, f32[8,512]{1,0:T(8,128)S(1)}) custom-call(s32[1]{0:T(128)} %bitcast.here, f32[1536,512]{1,0:T(8,128)} %get-tuple-element.188.refs_2_.wkv_ref, f32[1536,512]{1,0:T(8,128)} %get-tuple-element.257.g_ref, bf16[1536,512]{1,0:T(8,128)(2,1)S(1)} %copy-done.19, ...), custom_call_target="tpu_custom_call" | custom-call | tf_op jit(solution)/shard_map/gate_backward/pallas_call | solution.py:135
  605.6 7.8 convolution_convert_fusion.5
  613.5 2.6 pad_maximum_fusion.1
  621.2 20.8 %wkv_backward.1 = (bf16[1536,512]{1,0:T(8,128)(2,1)S(1)}, bf16[1536,512]{1,0:T(8,128)(2,1)S(1)}, bf16[1536,512]{1,0:T(8,128)(2,1)}, f32[8,512]{1,0:T(8,128)S(1)}) custom-call(s32[1]{0:T(128)} %bitcast.here, bf16[1536,512]{1,0:T(8,128)(2,1)} %get-tuple-element.185.r_ref, bf16[1536,512]{1,0:T(8,128)(2,1)} %get-tuple-element.186.k_ref, ...), custom_call_target="tpu_custom_call" | custom-call | tf_op jit(solution)/shard_map/wkv_backward/pallas_call | solution.py:135
  642.0 7.7 convolution_convert_fusion.4
  649.8 6.9 convolution_convert_fusion.2
  656.7 3.7 convolution_convert_fusion.3
  660.4 3.1 pad_maximum_fusion
  665.8 8.4 %mixes_back.9 = (bf16[192,2048]{1,0:T(8,128)(2,1)S(1)}, bf16[192,2048]{1,0:T(8,128)(2,1)S(1)}, f32[8,2048]{1,0:T(8,128)S(1)}) custom-call(s32[1]{0:T(128)} %bitcast.here, bf16[1536,512]{1,0:T(8,128)(2,1)S(1)} %get-tuple-element.299.refs_0_.refs_4_, bf16[1536,512]{1,0:T(8,128)(2,1)S(1)} %copy-done.4, bf16[1536,512]{1,0:T(8,128)(2,1)} %get-tuple-element.301.refs_2_.refs_6_, ...), custom_call_target="tpu_custom_call" | custom-call | tf_op jit(solution)/shard_map/mixes_back/pallas_call | solution.py:135
  676.4 15.3 %mixes_back.10 = (bf16[384,2048]{1,0:T(8,128)(2,1)S(1)}, bf16[384,2048]{1,0:T(8,128)(2,1)S(1)}, f32[8,2048]{1,0:T(8,128)S(1)}) custom-call(s32[1]{0:T(128)} %bitcast.here, bf16[1536,512]{1,0:T(8,128)(2,1)S(1)} %get-tuple-element.299.refs_0_.refs_4_, bf16[1536,512]{1,0:T(8,128)(2,1)} %copy-done.3, bf16[1536,512]{1,0:T(8,128)(2,1)} %get-tuple-element.301.refs_2_.refs_6_, ...), custom_call_target="tpu_custom_call" | custom-call | tf_op jit(solution)/shard_map/mixes_back/pallas_call | solution.py:135
  694.0 3.3 relay.7
  705.0 8.4 %mixes_back.11 = (bf16[384,2048]{1,0:T(8,128)(2,1)S(1)}, f32[8,2048]{1,0:T(8,128)S(1)}) custom-call(s32[1]{0:T(128)} %bitcast.here, bf16[1536,512]{1,0:T(8,128)(2,1)S(1)} %get-tuple-element.299.refs_0_.refs_4_, bf16[1536,512]{1,0:T(8,128)(2,1)S(1)} %copy-done.5, bf16[1536,512]{1,0:T(8,128)(2,1)} %get-tuple-element.301.refs_2_.refs_6_, ...), custom_call_target="tpu_custom_call" | custom-call | tf_op jit(solution)/shard_map/mixes_back/pallas_call | solution.py:135
  714.7 2.7 convert_element_type.180
  724.3 7.2 norm_back.3
  734.4 9.2 %collective-permute-done.46 = f32[16,14,64]{2,1,0:T(8,128)S(1)} collective-permute-done((f32[16,14,64]{2,1,0:T(8,128)S(1)}, f32[16,14,64]{2,1,0:T(8,128)S(1)}, u32[]{:S(2)}, u32[]{:S(2)}) %collective-permute-start.46) | collective-permute-done | bytes 57376 | tf_op jit(solution)/shard_map/ppermute | solution.py:24
  743.8 4.9 collective-permute-done.47
  754.7 3.7 collective-permute-done.51.refs_3_
  758.4 3.9 collective-permute-done.50.refs_2_
  764.8 3.0 collective-permute-done.52
  768.4 3.1 collective-permute-done.53
  (464 shorter events, 177.9 us)
Async XLA Ops:
  7.2 93.0 %all-gather.6.cloned.1.call-start = ((), (), s32[]{:S(2)}) async-start(), calls=%async_computation.5 | async-start | bytes 7077888 | tf_op jit(solution)/shard_map/all_gather | solution.py:883
  11.9 11.5 %collective-permute-start = (bf16[80,2048]{1,0:T(8,128)(2,1)S(1)}, bf16[80,2048]{1,0:T(8,128)(2,1)S(1)}, u32[]{:S(2)}, u32[]{:S(2)}) collective-permute-start(bf16[80,2048]{1,0:T(8,128)(2,1)S(1)} %get-tuple-element.171.refs_1_), channel_id=1, source_target_pairs={{0,8},{8,0},{16,24},{24,16},{1,9},{9,1},{17,25},{25,17},{2,10},{10... | collective-permute-start | bytes 983048 | tf_op jit(solution)/shard_map/ppermute | solution.py:24
  15.0 16.2 %collective-permute-start.1 = (bf16[80,2048]{1,0:T(8,128)(2,1)S(1)}, bf16[80,2048]{1,0:T(8,128)(2,1)S(1)}, u32[]{:S(2)}, u32[]{:S(2)}) collective-permute-start(bf16[80,2048]{1,0:T(8,128)(2,1)S(1)} %get-tuple-element.172.refs_2_), channel_id=1, source_target_pairs={{0,16},{8,24},{16,0},{24,8},{1,17},{9,25},{17,1},{25,9},{2,18},{10... | collective-permute-start | bytes 983048 | tf_op jit(solution)/shard_map/ppermute | solution.py:24
  16.5 14.7 %collective-permute-start.2 = (bf16[80,2048]{1,0:T(8,128)(2,1)S(1)}, bf16[80,2048]{1,0:T(8,128)(2,1)S(1)}, u32[]{:S(2)}, u32[]{:S(2)}) collective-permute-start(bf16[80,2048]{1,0:T(8,128)(2,1)S(1)} %get-tuple-element.173.refs_3_), channel_id=1, source_target_pairs={{0,24},{8,16},{16,8},{24,0},{1,25},{9,17},{17,9},{25,1},{2,26},{10... | collective-permute-start | bytes 983048 | tf_op jit(solution)/shard_map/ppermute | solution.py:24
  32.2 109.9 %all-gather.8.cloned.1.call-start = ((), (), s32[]{:S(2)}) async-start(), calls=%async_computation.6 | async-start | bytes 2359296 | tf_op jit(solution)/shard_map/all_gather | solution.py:883
  33.5 35.4 %collective-permute-start.7 = (bf16[384,2048]{1,0:T(8,128)(2,1)}, bf16[384,2048]{1,0:T(8,128)(2,1)}, u32[]{:S(2)}, u32[]{:S(2)}) collective-permute-start(bf16[384,2048]{1,0:T(8,128)(2,1)} %hold.1.refs_0_), channel_id=1, source_target_pairs={{0,16},{8,24},{16,0},{24,8},{1,17},{9,25},{17,1},{25,9},{2,18},{10... | collective-permute-start | bytes 4718600 | tf_op jit(solution)/shard_map/ppermute | solution.py:24
  35.0 34.1 %collective-permute-start.6 = (bf16[384,2048]{1,0:T(8,128)(2,1)}, bf16[384,2048]{1,0:T(8,128)(2,1)}, u32[]{:S(2)}, u32[]{:S(2)}) collective-permute-start(bf16[384,2048]{1,0:T(8,128)(2,1)} %hold.1.refs_0_), channel_id=1, source_target_pairs={{0,8},{8,0},{16,24},{24,16},{1,9},{9,1},{17,25},{25,17},{2,10},{10... | collective-permute-start | bytes 4718600 | tf_op jit(solution)/shard_map/ppermute | solution.py:24
  37.8 4.0 collective-permute-start.4
  41.8 11.6 %collective-permute-start.5 = (bf16[4,4,14,64]{3,2,1,0:T(8,128)(2,1)S(1)}, bf16[4,4,14,64]{3,2,1,0:T(8,128)(2,1)S(1)}, u32[]{:S(2)}, u32[]{:S(2)}) collective-permute-start(bf16[4,4,14,64]{3,2,1,0:T(8,128)(2,1)S(1)} %pad_maximum_fusion.6), channel_id=1, source_target_pairs={{0,4},{1,5},{2,6},{3,7},{4,0},{5,1},{6,2},{7,3},{8,12},{9,13},{10,... | collective-permute-start | bytes 86024 | tf_op jit(solution)/shard_map/ppermute | solution.py:24
  69.2 91.2 %all-gather.10.cloned.1.call-start = ((), (), s32[]{:S(2)}) async-start(), calls=%async_computation.7 | async-start | bytes 2359296 | tf_op jit(solution)/shard_map/all_gather | solution.py:883
  71.7 17.2 %collective-permute-start.9 = (bf16[192,2048]{1,0:T(8,128)(2,1)S(1)}, bf16[192,2048]{1,0:T(8,128)(2,1)}, u32[]{:S(2)}, u32[]{:S(2)}) collective-permute-start(bf16[192,2048]{1,0:T(8,128)(2,1)S(1)} %slice.260), channel_id=1, source_target_pairs={{0,8},{8,0},{16,24},{24,16},{1,9},{9,1},{17,25},{25,17},{2,10},{10... | collective-permute-start | bytes 2359304 | tf_op jit(solution)/shard_map/ppermute | solution.py:24
  73.1 17.1 %collective-permute-start.8 = (bf16[192,2048]{1,0:T(8,128)(2,1)S(1)}, bf16[192,2048]{1,0:T(8,128)(2,1)}, u32[]{:S(2)}, u32[]{:S(2)}) collective-permute-start(bf16[192,2048]{1,0:T(8,128)(2,1)S(1)} %slice.259), channel_id=1, source_target_pairs={{0,16},{8,24},{16,0},{24,8},{1,17},{9,25},{17,1},{25,9},{2,18},{10... | collective-permute-start | bytes 2359304 | tf_op jit(solution)/shard_map/ppermute | solution.py:24
  90.3 198.8 %all-gather.12.cloned.1.call-start = ((), (), s32[]{:S(2)}) async-start(), calls=%async_computation.8 | async-start | bytes 10616832 | tf_op jit(solution)/shard_map/all_gather | solution.py:883
  93.9 61.1 %collective-permute-start.18 = (bf16[448,2304]{1,0:T(8,128)(2,1)}, bf16[448,2304]{1,0:T(8,128)(2,1)}, u32[]{:S(2)}, u32[]{:S(2)}) collective-permute-start(bf16[448,2304]{1,0:T(8,128)(2,1)} %get-tuple-element.200), channel_id=1, source_target_pairs={{0,8},{8,0},{16,24},{24,16},{1,9},{9,1},{17,25},{25,17},{2,10},{10... | collective-permute-start | bytes 6193160 | tf_op jit(solution)/shard_map/ppermute | solution.py:24
  94.3 60.7 %collective-permute-start.19 = (bf16[448,2304]{1,0:T(8,128)(2,1)}, bf16[448,2304]{1,0:T(8,128)(2,1)}, u32[]{:S(2)}, u32[]{:S(2)}) collective-permute-start(bf16[448,2304]{1,0:T(8,128)(2,1)} %get-tuple-element.201), channel_id=1, source_target_pairs={{0,16},{8,24},{16,0},{24,8},{1,17},{9,25},{17,1},{25,9},{2,18},{10... | collective-permute-start | bytes 6193160 | tf_op jit(solution)/shard_map/ppermute | solution.py:24
  95.7 59.2 %collective-permute-start.20 = (bf16[64,2304]{1,0:T(8,128)(2,1)}, bf16[64,2304]{1,0:T(8,128)(2,1)}, u32[]{:S(2)}, u32[]{:S(2)}) collective-permute-start(bf16[64,2304]{1,0:T(8,128)(2,1)} %get-tuple-element.202), channel_id=1, source_target_pairs={{0,24},{8,16},{16,8},{24,0},{1,25},{9,17},{17,9},{25,1},{2,26},{10... | collective-permute-start | bytes 884744 | tf_op jit(solution)/shard_map/ppermute | solution.py:24
  158.4 178.7 %all-gather.14.cloned.1.call-start = ((), (), s32[]{:S(2)}) async-start(), calls=%async_computation.9 | async-start | bytes 8257536 | tf_op jit(solution)/shard_map/all_gather | solution.py:883
  159.0 425.9 %reduce-scatter.6.cloned.1.call-start = ((), (), s32[]{:S(2)}) async-start(), calls=%async_computation.10 | async-start | bytes 8257536 | tf_op jit(solution)/shard_map/reduce_scatter | solution.py:886
  163.4 19.7 %collective-permute-start.11 = (bf16[192,2048]{1,0:T(8,128)(2,1)S(1)}, bf16[192,2048]{1,0:T(8,128)(2,1)S(1)}, u32[]{:S(2)}, u32[]{:S(2)}) collective-permute-start(bf16[192,2048]{1,0:T(8,128)(2,1)S(1)} %get-tuple-element.349), channel_id=1, source_target_pairs={{0,16},{8,24},{16,0},{24,8},{1,17},{9,25},{17,1},{25,9},{2,18},{10... | collective-permute-start | bytes 2359304 | tf_op jit(solution)/shard_map/ppermute | solution.py:24
  164.9 19.4 %collective-permute-start.10 = (bf16[192,2048]{1,0:T(8,128)(2,1)S(1)}, bf16[192,2048]{1,0:T(8,128)(2,1)S(1)}, u32[]{:S(2)}, u32[]{:S(2)}) collective-permute-start(bf16[192,2048]{1,0:T(8,128)(2,1)S(1)} %get-tuple-element.350), channel_id=1, source_target_pairs={{0,8},{8,0},{16,24},{24,16},{1,9},{9,1},{17,25},{25,17},{2,10},{10... | collective-permute-start | bytes 2359304 | tf_op jit(solution)/shard_map/ppermute | solution.py:24
  187.6 35.8 %collective-permute-start.12 = (bf16[384,2048]{1,0:T(8,128)(2,1)}, bf16[384,2048]{1,0:T(8,128)(2,1)}, u32[]{:S(2)}, u32[]{:S(2)}) collective-permute-start(bf16[384,2048]{1,0:T(8,128)(2,1)} %get-tuple-element.191), channel_id=1, source_target_pairs={{0,8},{8,0},{16,24},{24,16},{1,9},{9,1},{17,25},{25,17},{2,10},{10... | collective-permute-start | bytes 4718600 | tf_op jit(solution)/shard_map/ppermute | solution.py:24
  189.1 35.5 %collective-permute-start.13 = (bf16[384,2048]{1,0:T(8,128)(2,1)}, bf16[384,2048]{1,0:T(8,128)(2,1)}, u32[]{:S(2)}, u32[]{:S(2)}) collective-permute-start(bf16[384,2048]{1,0:T(8,128)(2,1)} %get-tuple-element.192), channel_id=1, source_target_pairs={{0,16},{8,24},{16,0},{24,8},{1,17},{9,25},{17,1},{25,9},{2,18},{10... | collective-permute-start | bytes 4718600 | tf_op jit(solution)/shard_map/ppermute | solution.py:24
  229.4 34.2 %collective-permute-start.15 = (bf16[384,2048]{1,0:T(8,128)(2,1)S(1)}, bf16[384,2048]{1,0:T(8,128)(2,1)S(1)}, u32[]{:S(2)}, u32[]{:S(2)}) collective-permute-start(bf16[384,2048]{1,0:T(8,128)(2,1)S(1)} %get-tuple-element.194.refs_0_), channel_id=1, source_target_pairs={{0,16},{8,24},{16,0},{24,8},{1,17},{9,25},{17,1},{25,9},{2,18},{10... | collective-permute-start | bytes 4718600 | tf_op jit(solution)/shard_map/ppermute | solution.py:24
  230.1 34.3 %collective-permute-start.14 = (bf16[384,2048]{1,0:T(8,128)(2,1)S(1)}, bf16[384,2048]{1,0:T(8,128)(2,1)S(1)}, u32[]{:S(2)}, u32[]{:S(2)}) collective-permute-start(bf16[384,2048]{1,0:T(8,128)(2,1)S(1)} %get-tuple-element.194.refs_0_), channel_id=1, source_target_pairs={{0,8},{8,0},{16,24},{24,16},{1,9},{9,1},{17,25},{25,17},{2,10},{10... | collective-permute-start | bytes 4718600 | tf_op jit(solution)/shard_map/ppermute | solution.py:24
  264.6 16.3 %collective-permute-start.17 = (bf16[192,2048]{1,0:T(8,128)(2,1)S(1)}, bf16[192,2048]{1,0:T(8,128)(2,1)S(1)}, u32[]{:S(2)}, u32[]{:S(2)}) collective-permute-start(bf16[192,2048]{1,0:T(8,128)(2,1)S(1)} %slice.268), channel_id=1, source_target_pairs={{0,8},{8,0},{16,24},{24,16},{1,9},{9,1},{17,25},{25,17},{2,10},{10... | collective-permute-start | bytes 2359304 | tf_op jit(solution)/shard_map/ppermute | solution.py:24
  265.1 15.9 %collective-permute-start.16 = (bf16[192,2048]{1,0:T(8,128)(2,1)S(1)}, bf16[192,2048]{1,0:T(8,128)(2,1)S(1)}, u32[]{:S(2)}, u32[]{:S(2)}) collective-permute-start(bf16[192,2048]{1,0:T(8,128)(2,1)S(1)} %slice.267), channel_id=1, source_target_pairs={{0,16},{8,24},{16,0},{24,8},{1,17},{9,25},{17,1},{25,9},{2,18},{10... | collective-permute-start | bytes 2359304 | tf_op jit(solution)/shard_map/ppermute | solution.py:24
  285.8 22.5 %collective-permute-start.22 = (bf16[192,2048]{1,0:T(8,128)(2,1)}, bf16[192,2048]{1,0:T(8,128)(2,1)S(1)}, u32[]{:S(2)}, u32[]{:S(2)}) collective-permute-start(bf16[192,2048]{1,0:T(8,128)(2,1)} %slice.279), channel_id=1, source_target_pairs={{0,8},{8,0},{16,24},{24,16},{1,9},{9,1},{17,25},{25,17},{2,10},{10... | collective-permute-start | bytes 2359304 | tf_op jit(solution)/shard_map/ppermute | solution.py:24
  286.8 21.5 %collective-permute-start.21 = (bf16[192,2048]{1,0:T(8,128)(2,1)}, bf16[192,2048]{1,0:T(8,128)(2,1)S(1)}, u32[]{:S(2)}, u32[]{:S(2)}) collective-permute-start(bf16[192,2048]{1,0:T(8,128)(2,1)} %slice.278), channel_id=1, source_target_pairs={{0,16},{8,24},{16,0},{24,8},{1,17},{9,25},{17,1},{25,9},{2,18},{10... | collective-permute-start | bytes 2359304 | tf_op jit(solution)/shard_map/ppermute | solution.py:24
  308.3 36.9 %collective-permute-start.24 = (bf16[1536,512]{1,0:T(8,128)(2,1)}, bf16[1536,512]{1,0:T(8,128)(2,1)}, u32[]{:S(2)}, u32[]{:S(2)}) collective-permute-start(bf16[1536,512]{1,0:T(8,128)(2,1)} %get-tuple-element.221.refs_5_), channel_id=1, source_target_pairs={{0,16},{8,24},{16,0},{24,8},{1,17},{9,25},{17,1},{25,9},{2,18},{10... | collective-permute-start | bytes 4718600 | tf_op jit(solution)/shard_map/ppermute | solution.py:24
  310.7 34.5 %collective-permute-start.23 = (bf16[1536,512]{1,0:T(8,128)(2,1)}, bf16[1536,512]{1,0:T(8,128)(2,1)}, u32[]{:S(2)}, u32[]{:S(2)}) collective-permute-start(bf16[1536,512]{1,0:T(8,128)(2,1)} %get-tuple-element.221.refs_5_), channel_id=1, source_target_pairs={{0,8},{8,0},{16,24},{24,16},{1,9},{9,1},{17,25},{25,17},{2,10},{10... | collective-permute-start | bytes 4718600 | tf_op jit(solution)/shard_map/ppermute | solution.py:24
  343.2 28.7 %collective-permute-start.26 = (bf16[768,512]{1,0:T(8,128)(2,1)S(1)}, bf16[768,512]{1,0:T(8,128)(2,1)S(1)}, u32[]{:S(2)}, u32[]{:S(2)}) collective-permute-start(bf16[768,512]{1,0:T(8,128)(2,1)S(1)} %get-tuple-element.347), channel_id=1, source_target_pairs={{0,16},{8,24},{16,0},{24,8},{1,17},{9,25},{17,1},{25,9},{2,18},{10... | collective-permute-start | bytes 2359304 | tf_op jit(solution)/shard_map/ppermute | solution.py:24
  345.2 26.7 %collective-permute-start.25 = (bf16[768,512]{1,0:T(8,128)(2,1)S(1)}, bf16[768,512]{1,0:T(8,128)(2,1)S(1)}, u32[]{:S(2)}, u32[]{:S(2)}) collective-permute-start(bf16[768,512]{1,0:T(8,128)(2,1)S(1)} %get-tuple-element.348), channel_id=1, source_target_pairs={{0,8},{8,0},{16,24},{24,16},{1,9},{9,1},{17,25},{25,17},{2,10},{10... | collective-permute-start | bytes 2359304 | tf_op jit(solution)/shard_map/ppermute | solution.py:24
  347.6 28.5 %collective-permute-start.30 = (bf16[768,512]{1,0:T(8,128)(2,1)S(1)}, bf16[768,512]{1,0:T(8,128)(2,1)S(1)}, u32[]{:S(2)}, u32[]{:S(2)}) collective-permute-start(bf16[768,512]{1,0:T(8,128)(2,1)S(1)} %slice.284), channel_id=1, source_target_pairs={{0,8},{8,0},{16,24},{24,16},{1,9},{9,1},{17,25},{25,17},{2,10},{10... | collective-permute-start | bytes 2359304 | tf_op jit(solution)/shard_map/ppermute | solution.py:24
  349.6 26.5 %collective-permute-start.29 = (bf16[768,512]{1,0:T(8,128)(2,1)S(1)}, bf16[768,512]{1,0:T(8,128)(2,1)S(1)}, u32[]{:S(2)}, u32[]{:S(2)}) collective-permute-start(bf16[768,512]{1,0:T(8,128)(2,1)S(1)} %slice.283), channel_id=1, source_target_pairs={{0,16},{8,24},{16,0},{24,8},{1,17},{9,25},{17,1},{25,9},{2,18},{10... | collective-permute-start | bytes 2359304 | tf_op jit(solution)/shard_map/ppermute | solution.py:24
  403.0 192.5 %reduce-scatter.8.cloned.1.call-start = ((), (), s32[]{:S(2)}) async-start(), calls=%async_computation.11 | async-start | bytes 8257536 | tf_op jit(solution)/shard_map/reduce_scatter | solution.py:886
  403.1 32.0 %collective-permute-start.27 = (bf16[1536,512]{1,0:T(8,128)(2,1)}, bf16[1536,512]{1,0:T(8,128)(2,1)S(1)}, u32[]{:S(2)}, u32[]{:S(2)}) collective-permute-start(bf16[1536,512]{1,0:T(8,128)(2,1)} %copy-done.67), channel_id=1, source_target_pairs={{0,8},{8,0},{16,24},{24,16},{1,9},{9,1},{17,25},{25,17},{2,10},{10... | collective-permute-start | bytes 4718600 | tf_op jit(solution)/shard_map/ppermute | solution.py:24
  404.4 32.0 %collective-permute-start.28 = (bf16[1536,512]{1,0:T(8,128)(2,1)S(1)}, bf16[1536,512]{1,0:T(8,128)(2,1)S(1)}, u32[]{:S(2)}, u32[]{:S(2)}) collective-permute-start(bf16[1536,512]{1,0:T(8,128)(2,1)S(1)} %copy-done.66), channel_id=1, source_target_pairs={{0,16},{8,24},{16,0},{24,8},{1,17},{9,25},{17,1},{25,9},{2,18},{10... | collective-permute-start | bytes 4718600 | tf_op jit(solution)/shard_map/ppermute | solution.py:24
  453.3 21.5 %collective-permute-start.31 = (bf16[192,2048]{1,0:T(8,128)(2,1)S(1)}, bf16[192,2048]{1,0:T(8,128)(2,1)S(1)}, u32[]{:S(2)}, u32[]{:S(2)}) collective-permute-start(bf16[192,2048]{1,0:T(8,128)(2,1)S(1)} %get-tuple-element.232), channel_id=1, source_target_pairs={{0,8},{8,0},{16,24},{24,16},{1,9},{9,1},{17,25},{25,17},{2,10},{10... | collective-permute-start | bytes 2359304 | tf_op jit(solution)/shard_map/ppermute | solution.py:24
  454.9 19.9 %collective-permute-start.32 = (bf16[192,2048]{1,0:T(8,128)(2,1)S(1)}, bf16[192,2048]{1,0:T(8,128)(2,1)S(1)}, u32[]{:S(2)}, u32[]{:S(2)}) collective-permute-start(bf16[192,2048]{1,0:T(8,128)(2,1)S(1)} %get-tuple-element.233), channel_id=1, source_target_pairs={{0,16},{8,24},{16,0},{24,8},{1,17},{9,25},{17,1},{25,9},{2,18},{10... | collective-permute-start | bytes 2359304 | tf_op jit(solution)/shard_map/ppermute | solution.py:24
  495.1 169.2 %reduce-scatter.10.cloned.1.call-start = ((), (), s32[]{:S(2)}) async-start(), calls=%async_computation.12 | async-start | bytes 2359296 | tf_op jit(solution)/shard_map/reduce_scatter | solution.py:886
  495.2 31.1 %collective-permute-start.33 = (bf16[384,2048]{1,0:T(8,128)(2,1)}, bf16[384,2048]{1,0:T(8,128)(2,1)S(1)}, u32[]{:S(2)}, u32[]{:S(2)}) collective-permute-start(bf16[384,2048]{1,0:T(8,128)(2,1)} %copy-done.69), channel_id=1, source_target_pairs={{0,8},{8,0},{16,24},{24,16},{1,9},{9,1},{17,25},{25,17},{2,10},{10... | collective-permute-start | bytes 4718600 | tf_op jit(solution)/shard_map/ppermute | solution.py:24
  495.6 30.7 %collective-permute-start.34 = (bf16[384,2048]{1,0:T(8,128)(2,1)}, bf16[384,2048]{1,0:T(8,128)(2,1)S(1)}, u32[]{:S(2)}, u32[]{:S(2)}) collective-permute-start(bf16[384,2048]{1,0:T(8,128)(2,1)} %copy-done.68), channel_id=1, source_target_pairs={{0,16},{8,24},{16,0},{24,8},{1,17},{9,25},{17,1},{25,9},{2,18},{10... | collective-permute-start | bytes 4718600 | tf_op jit(solution)/shard_map/ppermute | solution.py:24
  535.4 33.9 %collective-permute-start.36 = (bf16[384,2048]{1,0:T(8,128)(2,1)S(1)}, bf16[384,2048]{1,0:T(8,128)(2,1)S(1)}, u32[]{:S(2)}, u32[]{:S(2)}) collective-permute-start(bf16[384,2048]{1,0:T(8,128)(2,1)S(1)} %get-tuple-element.251), channel_id=1, source_target_pairs={{0,16},{8,24},{16,0},{24,8},{1,17},{9,25},{17,1},{25,9},{2,18},{10... | collective-permute-start | bytes 4718600 | tf_op jit(solution)/shard_map/ppermute | solution.py:24
  536.2 34.2 %collective-permute-start.35 = (bf16[384,2048]{1,0:T(8,128)(2,1)S(1)}, bf16[384,2048]{1,0:T(8,128)(2,1)S(1)}, u32[]{:S(2)}, u32[]{:S(2)}) collective-permute-start(bf16[384,2048]{1,0:T(8,128)(2,1)S(1)} %get-tuple-element.251), channel_id=1, source_target_pairs={{0,8},{8,0},{16,24},{24,16},{1,9},{9,1},{17,25},{25,17},{2,10},{10... | collective-permute-start | bytes 4718600 | tf_op jit(solution)/shard_map/ppermute | solution.py:24
  570.5 12.1 %collective-permute-start.38 = (bf16[192,2048]{1,0:T(8,128)(2,1)S(1)}, bf16[192,2048]{1,0:T(8,128)(2,1)S(1)}, u32[]{:S(2)}, u32[]{:S(2)}) collective-permute-start(bf16[192,2048]{1,0:T(8,128)(2,1)S(1)} %slice.286), channel_id=1, source_target_pairs={{0,8},{8,0},{16,24},{24,16},{1,9},{9,1},{17,25},{25,17},{2,10},{10... | collective-permute-start | bytes 2359304 | tf_op jit(solution)/shard_map/ppermute | solution.py:24
  571.6 12.0 %collective-permute-start.37 = (bf16[192,2048]{1,0:T(8,128)(2,1)S(1)}, bf16[192,2048]{1,0:T(8,128)(2,1)S(1)}, u32[]{:S(2)}, u32[]{:S(2)}) collective-permute-start(bf16[192,2048]{1,0:T(8,128)(2,1)S(1)} %slice.285), channel_id=1, source_target_pairs={{0,16},{8,24},{16,0},{24,8},{1,17},{9,25},{17,1},{25,9},{2,18},{10... | collective-permute-start | bytes 2359304 | tf_op jit(solution)/shard_map/ppermute | solution.py:24
  590.3 158.4 %reduce-scatter.14.cloned.1.call-start = ((), (), s32[]{:S(2)}) async-start(), calls=%async_computation.14 | async-start | bytes 4718592 | tf_op jit(solution)/shard_map/reduce_scatter | solution.py:886
  616.1 156.0 %reduce-scatter.12.cloned.1.call-start = ((), (), s32[]{:S(2)}) async-start(), calls=%async_computation.13 | async-start | bytes 7077888 | tf_op jit(solution)/shard_map/reduce_scatter | solution.py:886
  617.6 24.4 %collective-permute-start.41 = (bf16[384,512]{1,0:T(8,128)(2,1)S(1)}, bf16[384,512]{1,0:T(8,128)(2,1)S(1)}, u32[]{:S(2)}, u32[]{:S(2)}) collective-permute-start(bf16[384,512]{1,0:T(8,128)(2,1)S(1)} %get-tuple-element.343), channel_id=1, source_target_pairs={{0,24},{8,16},{16,8},{24,0},{1,25},{9,17},{17,9},{25,1},{2,26},{10... | collective-permute-start | bytes 1179656 | tf_op jit(solution)/shard_map/ppermute | solution.py:24
  619.5 22.5 %collective-permute-start.40 = (bf16[384,512]{1,0:T(8,128)(2,1)S(1)}, bf16[384,512]{1,0:T(8,128)(2,1)S(1)}, u32[]{:S(2)}, u32[]{:S(2)}) collective-permute-start(bf16[384,512]{1,0:T(8,128)(2,1)S(1)} %get-tuple-element.344), channel_id=1, source_target_pairs={{0,16},{8,24},{16,0},{24,8},{1,17},{9,25},{17,1},{25,9},{2,18},{10... | collective-permute-start | bytes 1179656 | tf_op jit(solution)/shard_map/ppermute | solution.py:24
  620.2 21.8 %collective-permute-start.39 = (bf16[384,512]{1,0:T(8,128)(2,1)S(1)}, bf16[384,512]{1,0:T(8,128)(2,1)S(1)}, u32[]{:S(2)}, u32[]{:S(2)}) collective-permute-start(bf16[384,512]{1,0:T(8,128)(2,1)S(1)} %get-tuple-element.345), channel_id=1, source_target_pairs={{0,8},{8,0},{16,24},{24,16},{1,9},{9,1},{17,25},{25,17},{2,10},{10... | collective-permute-start | bytes 1179656 | tf_op jit(solution)/shard_map/ppermute | solution.py:24
  674.2 19.7 %collective-permute-start.42 = (bf16[192,2048]{1,0:T(8,128)(2,1)S(1)}, bf16[192,2048]{1,0:T(8,128)(2,1)S(1)}, u32[]{:S(2)}, u32[]{:S(2)}) collective-permute-start(bf16[192,2048]{1,0:T(8,128)(2,1)S(1)} %get-tuple-element.282), channel_id=1, source_target_pairs={{0,8},{8,0},{16,24},{24,16},{1,9},{9,1},{17,25},{25,17},{2,10},{10... | collective-permute-start | bytes 2359304 | tf_op jit(solution)/shard_map/ppermute | solution.py:24
  675.0 18.9 %collective-permute-start.43 = (bf16[192,2048]{1,0:T(8,128)(2,1)S(1)}, bf16[192,2048]{1,0:T(8,128)(2,1)S(1)}, u32[]{:S(2)}, u32[]{:S(2)}) collective-permute-start(bf16[192,2048]{1,0:T(8,128)(2,1)S(1)} %get-tuple-element.283), channel_id=1, source_target_pairs={{0,16},{8,24},{16,0},{24,8},{1,17},{9,25},{17,1},{25,9},{2,18},{10... | collective-permute-start | bytes 2359304 | tf_op jit(solution)/shard_map/ppermute | solution.py:24
  697.3 25.8 %collective-permute-start.44 = (bf16[384,2048]{1,0:T(8,128)(2,1)}, bf16[384,2048]{1,0:T(8,128)(2,1)}, u32[]{:S(2)}, u32[]{:S(2)}) collective-permute-start(bf16[384,2048]{1,0:T(8,128)(2,1)} %get-tuple-element.292), channel_id=1, source_target_pairs={{0,8},{8,0},{16,24},{24,16},{1,9},{9,1},{17,25},{25,17},{2,10},{10... | collective-permute-start | bytes 4718600 | tf_op jit(solution)/shard_map/ppermute | solution.py:24
  698.6 25.7 %collective-permute-start.45 = (bf16[384,2048]{1,0:T(8,128)(2,1)}, bf16[384,2048]{1,0:T(8,128)(2,1)}, u32[]{:S(2)}, u32[]{:S(2)}) collective-permute-start(bf16[384,2048]{1,0:T(8,128)(2,1)} %get-tuple-element.293), channel_id=1, source_target_pairs={{0,16},{8,24},{16,0},{24,8},{1,17},{9,25},{17,1},{25,9},{2,18},{10... | collective-permute-start | bytes 4718600 | tf_op jit(solution)/shard_map/ppermute | solution.py:24
  732.0 11.6 %collective-permute-start.46 = (f32[16,14,64]{2,1,0:T(8,128)S(1)}, f32[16,14,64]{2,1,0:T(8,128)S(1)}, u32[]{:S(2)}, u32[]{:S(2)}) collective-permute-start(f32[16,14,64]{2,1,0:T(8,128)S(1)} %bitcast.110), channel_id=1, source_target_pairs={{0,4},{1,5},{2,6},{3,7},{4,0},{5,1},{6,2},{7,3},{8,12},{9,13},{10,... | collective-permute-start | bytes 172040 | tf_op jit(solution)/shard_map/ppermute | solution.py:24
  743.7 5.0 collective-permute-start.47
  749.9 8.5 %collective-permute-start.51 = (bf16[64,2816]{1,0:T(8,128)(2,1)S(1)}, bf16[64,2816]{1,0:T(8,128)(2,1)S(1)}, u32[]{:S(2)}, u32[]{:S(2)}) collective-permute-start(bf16[64,2816]{1,0:T(8,128)(2,1)S(1)} %get-tuple-element.351), channel_id=1, source_target_pairs={{0,24},{8,16},{16,8},{24,0},{1,25},{9,17},{17,9},{25,1},{2,26},{10... | collective-permute-start | bytes 1081352 | tf_op jit(solution)/shard_map/ppermute | solution.py:24
  751.4 11.0 %collective-permute-start.50 = (bf16[64,2816]{1,0:T(8,128)(2,1)S(1)}, bf16[64,2816]{1,0:T(8,128)(2,1)S(1)}, u32[]{:S(2)}, u32[]{:S(2)}) collective-permute-start(bf16[64,2816]{1,0:T(8,128)(2,1)S(1)} %get-tuple-element.352), channel_id=1, source_target_pairs={{0,16},{8,24},{16,0},{24,8},{1,17},{9,25},{17,1},{25,9},{2,18},{10... | collective-permute-start | bytes 1081352 | tf_op jit(solution)/shard_map/ppermute | solution.py:24
  752.0 10.4 %collective-permute-start.49 = (bf16[64,2816]{1,0:T(8,128)(2,1)S(1)}, bf16[64,2816]{1,0:T(8,128)(2,1)S(1)}, u32[]{:S(2)}, u32[]{:S(2)}) collective-permute-start(bf16[64,2816]{1,0:T(8,128)(2,1)S(1)} %get-tuple-element.353), channel_id=1, source_target_pairs={{0,8},{8,0},{16,24},{24,16},{1,9},{9,1},{17,25},{25,17},{2,10},{10... | collective-permute-start | bytes 1081352 | tf_op jit(solution)/shard_map/ppermute | solution.py:24
  764.1 3.7 collective-permute-start.52
  773.4 6.7 collective-permute-start.56
  774.9 7.3 collective-permute-start.55
  775.6 6.6 collective-permute-start.54
  (110 other events, 1204.2 us)
Sparse Core Ops, SparseCore 0:
  32.3 67.7 all-gather.5
  102.3 27.6 all-gather.7
  131.7 28.6 all-gather.9
  161.9 90.2 all-gather.11
  253.6 71.8 all-gather.13
  403.2 79.5 reduce-scatter.5
  495.2 77.8 reduce-scatter.7
  590.4 35.1 reduce-scatter.9
  627.9 48.3 reduce-scatter.13
  678.5 71.5 reduce-scatter.11

commit v13 on v12

--- a/solution.py
+++ b/solution.py
@@ -108,15 +108,14 @@
     return part
 
 
-def scatter_small(parts, between):
-    for axis in ("dp", "seq"):
-        parts = after(parts, between) if axis == "seq" else parts
-        for bit in reversed(bits_of(lax.axis_size(axis))):
-            half = parts.shape[0] // 2
-            second = (lax.axis_index(axis) & bit) != 0
-            low, high = parts[:half], parts[half:]
-            parts = jnp.where(second, high, low) + swap(jnp.where(second, low, high), axis, bit)
-    return parts[0]
+def scatter_small(parts, axis, before_last=()):
+    for bit in reversed(bits_of(lax.axis_size(axis))):
+        parts = after(parts, before_last) if bit == 1 else parts
+        half = parts.shape[0] // 2
+        second = (lax.axis_index(axis) & bit) != 0
+        low, high = parts[:half], parts[half:]
+        parts = jnp.where(second, high, low) + swap(jnp.where(second, low, high), axis, bit)
+    return parts
 
 
 def block(shape, index):
@@ -1024,14 +1023,12 @@
         terms = [outside(t, groups, unit, back=True) for t in terms]
     tokens_grad, _, norm_sums = norm_back(terms, inputs_b, d_after, rows_of(vec, 0), within, here)
 
-    summed_c = jnp.concatenate(after([summed_ck, summed_crg], terms), axis=1)
-    sum_ck, sum_cr, sum_g = owners_rows(summed_c, [ffn_key.shape[1], width, width])
     sum_o = summed_o.astype(F32)
 
     def by_device(rows, turn):
         if turn:
-            return rows.reshape(-1, dp, seq, unit).transpose(1, 2, 0, 3)
-        return rows.reshape(-1, seq, dp, unit).transpose(2, 1, 0, 3)
+            return rows.reshape(-1, dp, seq, unit).transpose(2, 1, 0, 3)
+        return rows.reshape(-1, seq, dp, unit).transpose(1, 2, 0, 3)
 
     own_sums = jnp.stack([sums[0] * log_decay, sums[1], gate_sums[0], gate_sums[1]])
     own_sums = lax.dynamic_update_slice(jnp.zeros((4, width), F32), own_sums, (0, place * part))
@@ -1042,8 +1039,11 @@
         ],
         axis=2,
     )
-    sum_vec = scatter_small(vector_rows.reshape((-1,) + vector_rows.shape[2:]), sum_ck)
-    sum_r, sum_k, sum_v = owners_rows(after(summed_in, sum_vec), [width] * 3)
+    sums_seq = scatter_small(vector_rows.reshape((-1,) + vector_rows.shape[2:]), "seq")
+    summed_c = jnp.concatenate(after([summed_ck, summed_crg], sums_seq), axis=1)
+    sum_ck, sum_cr, sum_g = owners_rows(summed_c, [ffn_key.shape[1], width, width])
+    sum_vec = scatter_small(sums_seq, "dp", sum_ck)[0]
+    sum_r, sum_k, sum_v = owners_rows(after(summed_in, sum_ck), [width] * 3)
     return (
         out_rows[None], tokens_grad[None], sum_r, sum_k, sum_v, sum_g, sum_o,
         sum_ck, sum_cr, sum_cv, sum_vec,

time: 801 us -> 795 us (level)
    unnamed x216 -> x220, local copies, waits for them, and re-layouts: 38.7 us -> 38.7 us
  transfers between devices with their start and end apart: 67 -> 67, of which waited for: 38 -> 37; matrix products, arithmetic and copies ran while one was open for 20% -> 20% of each run, Pallas kernels for 29% -> 30%
where the time goes in v13:
time: 795 us; the launch traced here: 785 us
  Pallas kernels  244 us (31%)
  waiting for transfers between devices  239 us (30%)
  matrix products  137 us (17%)
  starting transfers between devices  69 us (9%)
  local copies, waits for them, and re-layouts  62.9 us (8%)
  other arithmetic  17.2 us (2%)
  between operations  15.8 us (2%)
    pallas_call x33, Pallas kernels, kernel(): pl.pallas_call(body, out_shape=[jax.ShapeDtypeStruct(shape, kind) for sha...  244 us
    ppermute x57, waiting for transfers between devices, swap(): return lax.ppermute(value, axis, [(i, i ^ distance) for i in range(size)])  235 us
    dot_general x21, matrix products, dot(): return lax.dot_general(left, right, dims, preferred_element_type=F32)  137 us
    ppermute x57, starting transfers between devices, swap(): return lax.ppermute(value, axis, [(i, i ^ distance) for i in range(size)])  68.1 us
    unnamed x220, local copies, waits for them, and re-layouts  38.7 us
  transfers between devices with their start and end apart: 67, of which 37 were waited for; matrix products, arithmetic and copies ran while one was open for 20% of the time, Pallas kernels for 30%

profile of v13, /device:TPU:0, one launch (start us, length us, event | category | flops | bytes accessed | tf_op | source)
XLA Modules:
  0.0 785.4 jit_solution(6159714767690696992)
XLA Ops:
  11.9 3.0 collective-permute-start
  16.5 7.0 collective-permute-done.refs_1_
  23.5 7.7 collective-permute-done.1.refs_2_
  41.8 2.7 collective-permute-start.5
  45.8 7.6 collective-permute-done.5
  56.6 12.3 %collective-permute-done.7.refs_2_ = bf16[384,2048]{1,0:T(8,128)(2,1)} collective-permute-done((bf16[384,2048]{1,0:T(8,128)(2,1)}, bf16[384,2048]{1,0:T(8,128)(2,1)}, u32[]{:S(2)}, u32[]{:S(2)}) %collective-permute-start.7) | collective-permute-done | bytes 1572896 | tf_op jit(solution)/shard_map/ppermute | solution.py:24
  74.6 14.2 %collective-permute-done.9.refs_4_ = bf16[192,2048]{1,0:T(8,128)(2,1)} collective-permute-done((bf16[192,2048]{1,0:T(8,128)(2,1)S(1)}, bf16[192,2048]{1,0:T(8,128)(2,1)}, u32[]{:S(2)}, u32[]{:S(2)}) %collective-permute-start.9) | collective-permute-done | bytes 786464 | tf_op jit(solution)/shard_map/ppermute | solution.py:24
  97.4 2.8 all-gather.6.cloned.1.call-done.refs_7_.refs_8_.refs_9_.refs_10_
  100.2 25.9 %mixes.2 = (bf16[1536,2048]{1,0:T(8,128)(2,1)}, bf16[1536,2048]{1,0:T(8,128)(2,1)}, bf16[1536,2048]{1,0:T(8,128)(2,1)}, bf16[1536,2048]{1,0:T(8,128)(2,1)}, bf16...) custom-call(s32[1]{0:T(128)} %bitcast.here, ...), custom_call_target="tpu_custom_call" | custom-call | tf_op jit(solution)/shard_map/mixes/pallas_call | solution.py:134
  127.5 13.4 %wkv_forward.1 = (f32[1536,512]{1,0:T(8,128)}, bf16[12,512,128]{2,1,0:T(8,128)(2,1)S(1)}) custom-call(s32[1]{0:T(128)} %bitcast.here, bf16[1536,512]{1,0:T(8,128)(2,1)S(1)} %copy-done.15, bf16[1536,512]{1,0:T(8,128)(2,1)} %get-tuple-element.186.k_ref, bf16[1536,512]{1,0:T(8,128)(2,1)} %get-tuple-element.187.v_ref, f32[1536,128]{1,0:T(8,128)S(1)} %copy-done, ...), custom_call_target="tpu_custom_call" | custom-call | tf_op jit(solution)/shard_map/wkv_forward/pallas_call | solution.py:134
  143.7 10.1 %gate.1 = (f32[1536,512]{1,0:T(8,128)}, bf16[1536,512]{1,0:T(8,128)(2,1)S(1)}) custom-call(s32[1]{0:T(128)} %bitcast.here, bf16[1536,2048]{1,0:T(8,128)(2,1)} %get-tuple-element.182.refs_0_, bf16[2048,512]{1,0:T(8,128)(2,1)S(1)} %copy-done.8, f32[1536,512]{1,0:T(8,128)} %get-tuple-element.188.refs_2_.wkv_ref, f32[8,512]{1,0:T(8,128)S(1)} %maximum_maximum_fusion.par_ref.refs_3_), custom_call_target="tpu_custom_call" | custom-call | tf_op jit(solution)/shard_map/gate/pallas_call | solution.py:134
  155.0 3.4 stack_rows.3
  160.4 2.8 convolution_convert_fusion.7
  170.7 12.4 %collective-permute-done.11.high_ref = bf16[192,2048]{1,0:T(8,128)(2,1)S(1)} collective-permute-done((bf16[192,2048]{1,0:T(8,128)(2,1)S(1)}, bf16[192,2048]{1,0:T(8,128)(2,1)S(1)}, u32[]{:S(2)}, u32[]{:S(2)}) %collective-permute-start.11) | collective-permute-done | bytes 786464 | tf_op jit(solution)/shard_map/ppermute | solution.py:24
  184.3 3.3 relay.4
  191.5 2.8 convolution_convert_fusion.10.refs_0_
  194.3 29.1 %collective-permute-done.12.refs_1_ = bf16[384,2048]{1,0:T(8,128)(2,1)} collective-permute-done((bf16[384,2048]{1,0:T(8,128)(2,1)}, bf16[384,2048]{1,0:T(8,128)(2,1)}, u32[]{:S(2)}, u32[]{:S(2)}) %collective-permute-start.12) | collective-permute-done | bytes 1572896 | tf_op jit(solution)/shard_map/ppermute | solution.py:24
  224.6 4.8 after_norm.1
  230.5 33.1 %collective-permute-done.15.refs_2_ = bf16[384,2048]{1,0:T(8,128)(2,1)S(1)} collective-permute-done((bf16[384,2048]{1,0:T(8,128)(2,1)S(1)}, bf16[384,2048]{1,0:T(8,128)(2,1)S(1)}, u32[]{:S(2)}, u32[]{:S(2)}) %collective-permute-start.15) | collective-permute-done | bytes 1572896 | tf_op jit(solution)/shard_map/ppermute | solution.py:24
  266.6 14.3 %collective-permute-done.17.refs_4_ = bf16[192,2048]{1,0:T(8,128)(2,1)S(1)} collective-permute-done((bf16[192,2048]{1,0:T(8,128)(2,1)S(1)}, bf16[192,2048]{1,0:T(8,128)(2,1)S(1)}, u32[]{:S(2)}, u32[]{:S(2)}) %collective-permute-start.17) | collective-permute-done | bytes 786464 | tf_op jit(solution)/shard_map/ppermute | solution.py:24
  280.9 2.7 slice.278
  289.1 3.0 slice.326.refs_7_.refs_5_
  292.1 16.1 %mixes.3 = (bf16[1536,2048]{1,0:T(8,128)(2,1)}, bf16[1536,2048]{1,0:T(8,128)(2,1)}, bf16[1536,2048]{1,0:T(8,128)(2,1)}, f32[1536,512]{1,0:T(8,128)}, bf16[1536,512]{1,0:T(8,128)(2,1)}) custom-call(s32[1]{0:T(128)} %bitcast.here, bf16[384,2048]{1,0:T(8,128)(2,1)} %copy-done.33, bf16[384,2048]{1,0:T(8,128)(2,1)} %copy-done.73, bf16[384,2048]{1,0:T(8,128)(2,1)} %copy-done.72, ...), custom_call_target="tpu_custom_call" | custom-call | tf_op jit(solution)/shard_map/mixes/pallas_call | solution.py:134
  311.9 25.2 %multiply_convert_fusion.1 = (bf16[1536,1792]{1,0:T(8,128)(2,1)}, bf16[1536,1792]{1,0:T(8,128)(2,1)}) fusion(bf16[1536,2048]{1,0:T(8,128)(2,1)} %get-tuple-element.245, bf16[2048,2304]{1,0:T(8,128)(2,1)} %all-gather.12.cloned.1.call-done.refs_4_), kind=kOutput, calls=%fused_computation.2 | convolution fusion | flops 11312824320 | bytes 24641536 | tf_op jit(solution)/shard_map/dot_general | solution.py:638
  337.1 6.0 value_columns.7
  350.2 6.0 value_columns.6.two_ref
  357.5 6.0 value_columns.5.one_ref
  364.7 6.0 value_columns.4.refs_5_
  377.7 9.2 %spread_columns.2 = bf16[1536,2048]{1,0:T(8,128)(2,1)} custom-call(s32[1]{0:T(128)} %bitcast.here, bf16[384,2048]{1,0:T(8,128)(2,1)S(1)} %bitcast.92, bf16[448,2304]{1,0:T(8,128)(2,1)} %collective-permute-done.18.refs_1_, bf16[448,2304]{1,0:T(8,128)(2,1)} %collective-permute-done.19.refs_2_, bf16[192,2048]{1,0:T(8,128)(2,1)S(1)} %collective-permute-done.21.refs_3_, ...), custom_call_target="tpu_custom_call" | custom-call | tf_op jit(solution)/shard_map/spread_columns/pallas_call | solution.py:134
  386.9 16.1 %convolution_convert_fusion.1 = bf16[1792,2048]{1,0:T(8,128)(2,1)} fusion(bf16[1536,1792]{1,0:T(8,128)(2,1)S(1)} %bitcast.100, bf16[1536,2048]{1,0:T(8,128)(2,1)} %spread_columns.2), kind=kOutput, calls=%fused_computation.5 | convolution fusion | flops 11277959168 | bytes 19136512 | tf_op jit(solution)/shard_map/dot_general | solution.py:638
  406.1 18.8 %multiply_convert_fusion.refs_0_.refs_2_ = bf16[1536,1792]{1,0:T(8,128)(2,1)} fusion(bf16[1536,1792]{1,0:T(8,128)(2,1)} %get-tuple-element.227, bf16[1536,2048]{1,0:T(8,128)(2,1)} %spread_columns.2, bf16[1792,2048]{1,0:T(8,128)(2,1)} %all-gather.14.cloned.1.call-done.right_ref), kind=kOutput, calls=%fused_computation.1 | convolution fusion | flops 11282546688 | bytes 24641536 | tf_op jit(solution)/shard_map/dot_general | solution.py:638
  424.9 10.2 %collective-permute-done.27.refs_6_ = bf16[1536,512]{1,0:T(8,128)(2,1)S(1)} collective-permute-done((bf16[1536,512]{1,0:T(8,128)(2,1)}, bf16[1536,512]{1,0:T(8,128)(2,1)S(1)}, u32[]{:S(2)}, u32[]{:S(2)}) %collective-permute-start.27) | collective-permute-done | bytes 1572896 | tf_op jit(solution)/shard_map/ppermute | solution.py:24
  437.5 7.0 channel.1
  444.6 8.6 %mixes_back.6 = (bf16[192,2048]{1,0:T(8,128)(2,1)S(1)}, bf16[192,2048]{1,0:T(8,128)(2,1)S(1)}, f32[8,2048]{1,0:T(8,128)S(1)}) custom-call(s32[1]{0:T(128)} %bitcast.here, bf16[1536,1792]{1,0:T(8,128)(2,1)} %multiply_convert_fusion.refs_0_.refs_2_, bf16[1536,512]{1,0:T(8,128)(2,1)S(1)} %get-tuple-element.243.refs_1_.refs_3_, ...), custom_call_target="tpu_custom_call" | custom-call | tf_op jit(solution)/shard_map/mixes_back/pallas_call | solution.py:134
  456.3 16.1 %mixes_back.7 = (bf16[384,2048]{1,0:T(8,128)(2,1)S(1)}, bf16[384,2048]{1,0:T(8,128)(2,1)S(1)}, f32[8,2048]{1,0:T(8,128)S(1)}) custom-call(s32[1]{0:T(128)} %bitcast.here, bf16[1536,1792]{1,0:T(8,128)(2,1)} %multiply_convert_fusion.refs_0_.refs_2_, bf16[1536,512]{1,0:T(8,128)(2,1)S(1)} %get-tuple-element.243.refs_1_.refs_3_, ...), custom_call_target="tpu_custom_call" | custom-call | tf_op jit(solution)/shard_map/mixes_back/pallas_call | solution.py:134
  478.9 16.2 %convolution_convert_fusion = bf16[2048,1792]{1,0:T(8,128)(2,1)} fusion(bf16[1536,2048]{1,0:T(8,128)(2,1)} %get-tuple-element.245, bf16[1536,1792]{1,0:T(8,128)(2,1)S(1)} %bitcast.98), kind=kOutput, calls=%fused_computation.4 | convolution fusion | flops 11277959168 | bytes 19136512 | tf_op jit(solution)/shard_map/dot_general | solution.py:638
  498.0 8.9 %mixes_back.8 = (bf16[384,2048]{1,0:T(8,128)(2,1)S(1)}, f32[8,2048]{1,0:T(8,128)S(1)}) custom-call(s32[1]{0:T(128)} %bitcast.here, bf16[1536,1792]{1,0:T(8,128)(2,1)} %multiply_convert_fusion.refs_0_.refs_2_, bf16[1536,512]{1,0:T(8,128)(2,1)S(1)} %get-tuple-element.243.refs_1_.refs_3_, bf16[1536,1792]{1,0:T(8,128)(2,1)} %multiply_convert_fusion.refs_0_.refs_2_, ...), custom_call_target="tpu_custom_call" | custom-call | tf_op jit(solution)/shard_map/mixes_back/pallas_call | solution.py:134
  507.0 7.9 %convolution_convert_fusion.6 = bf16[2048,512]{1,0:T(8,128)(2,1)} fusion(bf16[1536,2048]{1,0:T(8,128)(2,1)} %get-tuple-element.247, bf16[1536,512]{1,0:T(8,128)(2,1)S(1)} %get-tuple-element.243.refs_1_.refs_3_), kind=kOutput, calls=%fused_computation.16 | convolution fusion | flops 3222274048 | bytes 9961472 | tf_op jit(solution)/shard_map/dot_general | solution.py:638
  514.9 11.4 %collective-permute-done.33.refs_1_ = bf16[384,2048]{1,0:T(8,128)(2,1)S(1)} collective-permute-done((bf16[384,2048]{1,0:T(8,128)(2,1)}, bf16[384,2048]{1,0:T(8,128)(2,1)S(1)}, u32[]{:S(2)}, u32[]{:S(2)}) %collective-permute-start.33) | collective-permute-done | bytes 1572896 | tf_op jit(solution)/shard_map/ppermute | solution.py:24
  527.9 6.9 norm_back.2
  539.7 29.7 %collective-permute-done.36 = bf16[384,2048]{1,0:T(8,128)(2,1)S(1)} collective-permute-done((bf16[384,2048]{1,0:T(8,128)(2,1)S(1)}, bf16[384,2048]{1,0:T(8,128)(2,1)S(1)}, u32[]{:S(2)}, u32[]{:S(2)}) %collective-permute-start.36) | collective-permute-done | bytes 1572896 | tf_op jit(solution)/shard_map/ppermute | solution.py:24
  576.8 3.5 add_add_fusion
  584.9 5.3 add_convert_fusion
  591.7 2.6 convolution_convert_fusion.11
  596.9 8.6 %gate_backward.1 = (bf16[1536,512]{1,0:T(8,128)(2,1)S(1)}, bf16[1536,512]{1,0:T(8,128)(2,1)S(1)}, f32[8,512]{1,0:T(8,128)S(1)}) custom-call(s32[1]{0:T(128)} %bitcast.here, f32[1536,512]{1,0:T(8,128)} %get-tuple-element.188.refs_2_.wkv_ref, f32[1536,512]{1,0:T(8,128)} %get-tuple-element.257.g_ref, bf16[1536,512]{1,0:T(8,128)(2,1)S(1)} %copy-done.19, ...), custom_call_target="tpu_custom_call" | custom-call | tf_op jit(solution)/shard_map/gate_backward/pallas_call | solution.py:134
  605.6 7.8 convolution_convert_fusion.5
  613.5 2.6 pad_maximum_fusion.1
  621.2 20.8 %wkv_backward.1 = (bf16[1536,512]{1,0:T(8,128)(2,1)S(1)}, bf16[1536,512]{1,0:T(8,128)(2,1)S(1)}, bf16[1536,512]{1,0:T(8,128)(2,1)}, f32[8,512]{1,0:T(8,128)S(1)}) custom-call(s32[1]{0:T(128)} %bitcast.here, bf16[1536,512]{1,0:T(8,128)(2,1)} %get-tuple-element.185.r_ref, bf16[1536,512]{1,0:T(8,128)(2,1)} %get-tuple-element.186.k_ref, ...), custom_call_target="tpu_custom_call" | custom-call | tf_op jit(solution)/shard_map/wkv_backward/pallas_call | solution.py:134
  642.0 7.7 convolution_convert_fusion.4
  649.8 6.9 convolution_convert_fusion.2
  656.7 3.7 convolution_convert_fusion.3
  660.4 3.1 pad_maximum_fusion
  665.8 8.4 %mixes_back.9 = (bf16[192,2048]{1,0:T(8,128)(2,1)S(1)}, bf16[192,2048]{1,0:T(8,128)(2,1)S(1)}, f32[8,2048]{1,0:T(8,128)S(1)}) custom-call(s32[1]{0:T(128)} %bitcast.here, bf16[1536,512]{1,0:T(8,128)(2,1)S(1)} %get-tuple-element.299.refs_0_.refs_4_, bf16[1536,512]{1,0:T(8,128)(2,1)S(1)} %copy-done.4, bf16[1536,512]{1,0:T(8,128)(2,1)} %get-tuple-element.301.refs_2_.refs_6_, ...), custom_call_target="tpu_custom_call" | custom-call | tf_op jit(solution)/shard_map/mixes_back/pallas_call | solution.py:134
  676.4 15.3 %mixes_back.10 = (bf16[384,2048]{1,0:T(8,128)(2,1)S(1)}, bf16[384,2048]{1,0:T(8,128)(2,1)S(1)}, f32[8,2048]{1,0:T(8,128)S(1)}) custom-call(s32[1]{0:T(128)} %bitcast.here, bf16[1536,512]{1,0:T(8,128)(2,1)S(1)} %get-tuple-element.299.refs_0_.refs_4_, bf16[1536,512]{1,0:T(8,128)(2,1)} %copy-done.3, bf16[1536,512]{1,0:T(8,128)(2,1)} %get-tuple-element.301.refs_2_.refs_6_, ...), custom_call_target="tpu_custom_call" | custom-call | tf_op jit(solution)/shard_map/mixes_back/pallas_call | solution.py:134
  694.0 3.3 relay.7
  704.8 8.4 %mixes_back.11 = (bf16[384,2048]{1,0:T(8,128)(2,1)S(1)}, f32[8,2048]{1,0:T(8,128)S(1)}) custom-call(s32[1]{0:T(128)} %bitcast.here, bf16[1536,512]{1,0:T(8,128)(2,1)S(1)} %get-tuple-element.299.refs_0_.refs_4_, bf16[1536,512]{1,0:T(8,128)(2,1)S(1)} %copy-done.5, bf16[1536,512]{1,0:T(8,128)(2,1)} %get-tuple-element.301.refs_2_.refs_6_, ...), custom_call_target="tpu_custom_call" | custom-call | tf_op jit(solution)/shard_map/mixes_back/pallas_call | solution.py:134
  714.5 2.7 convert_element_type.180
  723.1 2.6 collective-permute-done.45.refs_2_
  725.7 7.2 norm_back.3
  734.0 4.1 collective-permute-done.46
  738.8 4.5 collective-permute-done.47
  758.0 3.8 collective-permute-done.49.refs_2_
  768.9 4.6 collective-permute-done.53.refs_3_
  773.5 3.6 collective-permute-done.52.refs_2_
  (464 shorter events, 177.7 us)
Async XLA Ops:
  7.2 93.0 %all-gather.6.cloned.1.call-start = ((), (), s32[]{:S(2)}) async-start(), calls=%async_computation.5 | async-start | bytes 7077888 | tf_op jit(solution)/shard_map/all_gather | solution.py:882
  11.9 11.5 %collective-permute-start = (bf16[80,2048]{1,0:T(8,128)(2,1)S(1)}, bf16[80,2048]{1,0:T(8,128)(2,1)S(1)}, u32[]{:S(2)}, u32[]{:S(2)}) collective-permute-start(bf16[80,2048]{1,0:T(8,128)(2,1)S(1)} %get-tuple-element.171.refs_1_), channel_id=1, source_target_pairs={{0,8},{8,0},{16,24},{24,16},{1,9},{9,1},{17,25},{25,17},{2,10},{10... | collective-permute-start | bytes 983048 | tf_op jit(solution)/shard_map/ppermute | solution.py:24
  15.0 16.2 %collective-permute-start.1 = (bf16[80,2048]{1,0:T(8,128)(2,1)S(1)}, bf16[80,2048]{1,0:T(8,128)(2,1)S(1)}, u32[]{:S(2)}, u32[]{:S(2)}) collective-permute-start(bf16[80,2048]{1,0:T(8,128)(2,1)S(1)} %get-tuple-element.172.refs_2_), channel_id=1, source_target_pairs={{0,16},{8,24},{16,0},{24,8},{1,17},{9,25},{17,1},{25,9},{2,18},{10... | collective-permute-start | bytes 983048 | tf_op jit(solution)/shard_map/ppermute | solution.py:24
  16.5 14.7 %collective-permute-start.2 = (bf16[80,2048]{1,0:T(8,128)(2,1)S(1)}, bf16[80,2048]{1,0:T(8,128)(2,1)S(1)}, u32[]{:S(2)}, u32[]{:S(2)}) collective-permute-start(bf16[80,2048]{1,0:T(8,128)(2,1)S(1)} %get-tuple-element.173.refs_3_), channel_id=1, source_target_pairs={{0,24},{8,16},{16,8},{24,0},{1,25},{9,17},{17,9},{25,1},{2,26},{10... | collective-permute-start | bytes 983048 | tf_op jit(solution)/shard_map/ppermute | solution.py:24
  32.2 109.9 %all-gather.8.cloned.1.call-start = ((), (), s32[]{:S(2)}) async-start(), calls=%async_computation.6 | async-start | bytes 2359296 | tf_op jit(solution)/shard_map/all_gather | solution.py:882
  33.5 35.4 %collective-permute-start.7 = (bf16[384,2048]{1,0:T(8,128)(2,1)}, bf16[384,2048]{1,0:T(8,128)(2,1)}, u32[]{:S(2)}, u32[]{:S(2)}) collective-permute-start(bf16[384,2048]{1,0:T(8,128)(2,1)} %hold.1.refs_0_), channel_id=1, source_target_pairs={{0,16},{8,24},{16,0},{24,8},{1,17},{9,25},{17,1},{25,9},{2,18},{10... | collective-permute-start | bytes 4718600 | tf_op jit(solution)/shard_map/ppermute | solution.py:24
  35.0 34.1 %collective-permute-start.6 = (bf16[384,2048]{1,0:T(8,128)(2,1)}, bf16[384,2048]{1,0:T(8,128)(2,1)}, u32[]{:S(2)}, u32[]{:S(2)}) collective-permute-start(bf16[384,2048]{1,0:T(8,128)(2,1)} %hold.1.refs_0_), channel_id=1, source_target_pairs={{0,8},{8,0},{16,24},{24,16},{1,9},{9,1},{17,25},{25,17},{2,10},{10... | collective-permute-start | bytes 4718600 | tf_op jit(solution)/shard_map/ppermute | solution.py:24
  41.8 11.6 %collective-permute-start.5 = (bf16[4,4,14,64]{3,2,1,0:T(8,128)(2,1)S(1)}, bf16[4,4,14,64]{3,2,1,0:T(8,128)(2,1)S(1)}, u32[]{:S(2)}, u32[]{:S(2)}) collective-permute-start(bf16[4,4,14,64]{3,2,1,0:T(8,128)(2,1)S(1)} %pad_maximum_fusion.6), channel_id=1, source_target_pairs={{0,4},{1,5},{2,6},{3,7},{4,0},{5,1},{6,2},{7,3},{8,12},{9,13},{10,... | collective-permute-start | bytes 86024 | tf_op jit(solution)/shard_map/ppermute | solution.py:24
  69.2 91.2 %all-gather.10.cloned.1.call-start = ((), (), s32[]{:S(2)}) async-start(), calls=%async_computation.7 | async-start | bytes 2359296 | tf_op jit(solution)/shard_map/all_gather | solution.py:882
  71.7 17.2 %collective-permute-start.9 = (bf16[192,2048]{1,0:T(8,128)(2,1)S(1)}, bf16[192,2048]{1,0:T(8,128)(2,1)}, u32[]{:S(2)}, u32[]{:S(2)}) collective-permute-start(bf16[192,2048]{1,0:T(8,128)(2,1)S(1)} %slice.260), channel_id=1, source_target_pairs={{0,8},{8,0},{16,24},{24,16},{1,9},{9,1},{17,25},{25,17},{2,10},{10... | collective-permute-start | bytes 2359304 | tf_op jit(solution)/shard_map/ppermute | solution.py:24
  73.1 17.1 %collective-permute-start.8 = (bf16[192,2048]{1,0:T(8,128)(2,1)S(1)}, bf16[192,2048]{1,0:T(8,128)(2,1)}, u32[]{:S(2)}, u32[]{:S(2)}) collective-permute-start(bf16[192,2048]{1,0:T(8,128)(2,1)S(1)} %slice.259), channel_id=1, source_target_pairs={{0,16},{8,24},{16,0},{24,8},{1,17},{9,25},{17,1},{25,9},{2,18},{10... | collective-permute-start | bytes 2359304 | tf_op jit(solution)/shard_map/ppermute | solution.py:24
  90.3 198.8 %all-gather.12.cloned.1.call-start = ((), (), s32[]{:S(2)}) async-start(), calls=%async_computation.8 | async-start | bytes 10616832 | tf_op jit(solution)/shard_map/all_gather | solution.py:882
  93.9 61.1 %collective-permute-start.18 = (bf16[448,2304]{1,0:T(8,128)(2,1)}, bf16[448,2304]{1,0:T(8,128)(2,1)}, u32[]{:S(2)}, u32[]{:S(2)}) collective-permute-start(bf16[448,2304]{1,0:T(8,128)(2,1)} %get-tuple-element.200), channel_id=1, source_target_pairs={{0,8},{8,0},{16,24},{24,16},{1,9},{9,1},{17,25},{25,17},{2,10},{10... | collective-permute-start | bytes 6193160 | tf_op jit(solution)/shard_map/ppermute | solution.py:24
  94.3 60.7 %collective-permute-start.19 = (bf16[448,2304]{1,0:T(8,128)(2,1)}, bf16[448,2304]{1,0:T(8,128)(2,1)}, u32[]{:S(2)}, u32[]{:S(2)}) collective-permute-start(bf16[448,2304]{1,0:T(8,128)(2,1)} %get-tuple-element.201), channel_id=1, source_target_pairs={{0,16},{8,24},{16,0},{24,8},{1,17},{9,25},{17,1},{25,9},{2,18},{10... | collective-permute-start | bytes 6193160 | tf_op jit(solution)/shard_map/ppermute | solution.py:24
  95.7 59.2 %collective-permute-start.20 = (bf16[64,2304]{1,0:T(8,128)(2,1)}, bf16[64,2304]{1,0:T(8,128)(2,1)}, u32[]{:S(2)}, u32[]{:S(2)}) collective-permute-start(bf16[64,2304]{1,0:T(8,128)(2,1)} %get-tuple-element.202), channel_id=1, source_target_pairs={{0,24},{8,16},{16,8},{24,0},{1,25},{9,17},{17,9},{25,1},{2,26},{10... | collective-permute-start | bytes 884744 | tf_op jit(solution)/shard_map/ppermute | solution.py:24
  158.4 178.7 %all-gather.14.cloned.1.call-start = ((), (), s32[]{:S(2)}) async-start(), calls=%async_computation.9 | async-start | bytes 8257536 | tf_op jit(solution)/shard_map/all_gather | solution.py:882
  159.0 425.9 %reduce-scatter.6.cloned.1.call-start = ((), (), s32[]{:S(2)}) async-start(), calls=%async_computation.10 | async-start | bytes 8257536 | tf_op jit(solution)/shard_map/reduce_scatter | solution.py:885
  163.4 19.7 %collective-permute-start.11 = (bf16[192,2048]{1,0:T(8,128)(2,1)S(1)}, bf16[192,2048]{1,0:T(8,128)(2,1)S(1)}, u32[]{:S(2)}, u32[]{:S(2)}) collective-permute-start(bf16[192,2048]{1,0:T(8,128)(2,1)S(1)} %get-tuple-element.349), channel_id=1, source_target_pairs={{0,16},{8,24},{16,0},{24,8},{1,17},{9,25},{17,1},{25,9},{2,18},{10... | collective-permute-start | bytes 2359304 | tf_op jit(solution)/shard_map/ppermute | solution.py:24
  164.9 19.4 %collective-permute-start.10 = (bf16[192,2048]{1,0:T(8,128)(2,1)S(1)}, bf16[192,2048]{1,0:T(8,128)(2,1)S(1)}, u32[]{:S(2)}, u32[]{:S(2)}) collective-permute-start(bf16[192,2048]{1,0:T(8,128)(2,1)S(1)} %get-tuple-element.350), channel_id=1, source_target_pairs={{0,8},{8,0},{16,24},{24,16},{1,9},{9,1},{17,25},{25,17},{2,10},{10... | collective-permute-start | bytes 2359304 | tf_op jit(solution)/shard_map/ppermute | solution.py:24
  187.6 35.8 %collective-permute-start.12 = (bf16[384,2048]{1,0:T(8,128)(2,1)}, bf16[384,2048]{1,0:T(8,128)(2,1)}, u32[]{:S(2)}, u32[]{:S(2)}) collective-permute-start(bf16[384,2048]{1,0:T(8,128)(2,1)} %get-tuple-element.191), channel_id=1, source_target_pairs={{0,8},{8,0},{16,24},{24,16},{1,9},{9,1},{17,25},{25,17},{2,10},{10... | collective-permute-start | bytes 4718600 | tf_op jit(solution)/shard_map/ppermute | solution.py:24
  189.1 35.5 %collective-permute-start.13 = (bf16[384,2048]{1,0:T(8,128)(2,1)}, bf16[384,2048]{1,0:T(8,128)(2,1)}, u32[]{:S(2)}, u32[]{:S(2)}) collective-permute-start(bf16[384,2048]{1,0:T(8,128)(2,1)} %get-tuple-element.192), channel_id=1, source_target_pairs={{0,16},{8,24},{16,0},{24,8},{1,17},{9,25},{17,1},{25,9},{2,18},{10... | collective-permute-start | bytes 4718600 | tf_op jit(solution)/shard_map/ppermute | solution.py:24
  229.4 34.2 %collective-permute-start.15 = (bf16[384,2048]{1,0:T(8,128)(2,1)S(1)}, bf16[384,2048]{1,0:T(8,128)(2,1)S(1)}, u32[]{:S(2)}, u32[]{:S(2)}) collective-permute-start(bf16[384,2048]{1,0:T(8,128)(2,1)S(1)} %get-tuple-element.194.refs_0_), channel_id=1, source_target_pairs={{0,16},{8,24},{16,0},{24,8},{1,17},{9,25},{17,1},{25,9},{2,18},{10... | collective-permute-start | bytes 4718600 | tf_op jit(solution)/shard_map/ppermute | solution.py:24
  230.1 34.3 %collective-permute-start.14 = (bf16[384,2048]{1,0:T(8,128)(2,1)S(1)}, bf16[384,2048]{1,0:T(8,128)(2,1)S(1)}, u32[]{:S(2)}, u32[]{:S(2)}) collective-permute-start(bf16[384,2048]{1,0:T(8,128)(2,1)S(1)} %get-tuple-element.194.refs_0_), channel_id=1, source_target_pairs={{0,8},{8,0},{16,24},{24,16},{1,9},{9,1},{17,25},{25,17},{2,10},{10... | collective-permute-start | bytes 4718600 | tf_op jit(solution)/shard_map/ppermute | solution.py:24
  264.6 16.3 %collective-permute-start.17 = (bf16[192,2048]{1,0:T(8,128)(2,1)S(1)}, bf16[192,2048]{1,0:T(8,128)(2,1)S(1)}, u32[]{:S(2)}, u32[]{:S(2)}) collective-permute-start(bf16[192,2048]{1,0:T(8,128)(2,1)S(1)} %slice.268), channel_id=1, source_target_pairs={{0,8},{8,0},{16,24},{24,16},{1,9},{9,1},{17,25},{25,17},{2,10},{10... | collective-permute-start | bytes 2359304 | tf_op jit(solution)/shard_map/ppermute | solution.py:24
  265.1 15.9 %collective-permute-start.16 = (bf16[192,2048]{1,0:T(8,128)(2,1)S(1)}, bf16[192,2048]{1,0:T(8,128)(2,1)S(1)}, u32[]{:S(2)}, u32[]{:S(2)}) collective-permute-start(bf16[192,2048]{1,0:T(8,128)(2,1)S(1)} %slice.267), channel_id=1, source_target_pairs={{0,16},{8,24},{16,0},{24,8},{1,17},{9,25},{17,1},{25,9},{2,18},{10... | collective-permute-start | bytes 2359304 | tf_op jit(solution)/shard_map/ppermute | solution.py:24
  285.8 22.5 %collective-permute-start.22 = (bf16[192,2048]{1,0:T(8,128)(2,1)}, bf16[192,2048]{1,0:T(8,128)(2,1)S(1)}, u32[]{:S(2)}, u32[]{:S(2)}) collective-permute-start(bf16[192,2048]{1,0:T(8,128)(2,1)} %slice.279), channel_id=1, source_target_pairs={{0,8},{8,0},{16,24},{24,16},{1,9},{9,1},{17,25},{25,17},{2,10},{10... | collective-permute-start | bytes 2359304 | tf_op jit(solution)/shard_map/ppermute | solution.py:24
  286.8 21.5 %collective-permute-start.21 = (bf16[192,2048]{1,0:T(8,128)(2,1)}, bf16[192,2048]{1,0:T(8,128)(2,1)S(1)}, u32[]{:S(2)}, u32[]{:S(2)}) collective-permute-start(bf16[192,2048]{1,0:T(8,128)(2,1)} %slice.278), channel_id=1, source_target_pairs={{0,16},{8,24},{16,0},{24,8},{1,17},{9,25},{17,1},{25,9},{2,18},{10... | collective-permute-start | bytes 2359304 | tf_op jit(solution)/shard_map/ppermute | solution.py:24
  308.3 36.9 %collective-permute-start.24 = (bf16[1536,512]{1,0:T(8,128)(2,1)}, bf16[1536,512]{1,0:T(8,128)(2,1)}, u32[]{:S(2)}, u32[]{:S(2)}) collective-permute-start(bf16[1536,512]{1,0:T(8,128)(2,1)} %get-tuple-element.221.refs_5_), channel_id=1, source_target_pairs={{0,16},{8,24},{16,0},{24,8},{1,17},{9,25},{17,1},{25,9},{2,18},{10... | collective-permute-start | bytes 4718600 | tf_op jit(solution)/shard_map/ppermute | solution.py:24
  310.7 34.5 %collective-permute-start.23 = (bf16[1536,512]{1,0:T(8,128)(2,1)}, bf16[1536,512]{1,0:T(8,128)(2,1)}, u32[]{:S(2)}, u32[]{:S(2)}) collective-permute-start(bf16[1536,512]{1,0:T(8,128)(2,1)} %get-tuple-element.221.refs_5_), channel_id=1, source_target_pairs={{0,8},{8,0},{16,24},{24,16},{1,9},{9,1},{17,25},{25,17},{2,10},{10... | collective-permute-start | bytes 4718600 | tf_op jit(solution)/shard_map/ppermute | solution.py:24
  343.2 28.7 %collective-permute-start.26 = (bf16[768,512]{1,0:T(8,128)(2,1)S(1)}, bf16[768,512]{1,0:T(8,128)(2,1)S(1)}, u32[]{:S(2)}, u32[]{:S(2)}) collective-permute-start(bf16[768,512]{1,0:T(8,128)(2,1)S(1)} %get-tuple-element.347), channel_id=1, source_target_pairs={{0,16},{8,24},{16,0},{24,8},{1,17},{9,25},{17,1},{25,9},{2,18},{10... | collective-permute-start | bytes 2359304 | tf_op jit(solution)/shard_map/ppermute | solution.py:24
  345.2 26.7 %collective-permute-start.25 = (bf16[768,512]{1,0:T(8,128)(2,1)S(1)}, bf16[768,512]{1,0:T(8,128)(2,1)S(1)}, u32[]{:S(2)}, u32[]{:S(2)}) collective-permute-start(bf16[768,512]{1,0:T(8,128)(2,1)S(1)} %get-tuple-element.348), channel_id=1, source_target_pairs={{0,8},{8,0},{16,24},{24,16},{1,9},{9,1},{17,25},{25,17},{2,10},{10... | collective-permute-start | bytes 2359304 | tf_op jit(solution)/shard_map/ppermute | solution.py:24
  347.6 28.5 %collective-permute-start.30 = (bf16[768,512]{1,0:T(8,128)(2,1)S(1)}, bf16[768,512]{1,0:T(8,128)(2,1)S(1)}, u32[]{:S(2)}, u32[]{:S(2)}) collective-permute-start(bf16[768,512]{1,0:T(8,128)(2,1)S(1)} %slice.284), channel_id=1, source_target_pairs={{0,8},{8,0},{16,24},{24,16},{1,9},{9,1},{17,25},{25,17},{2,10},{10... | collective-permute-start | bytes 2359304 | tf_op jit(solution)/shard_map/ppermute | solution.py:24
  349.6 26.5 %collective-permute-start.29 = (bf16[768,512]{1,0:T(8,128)(2,1)S(1)}, bf16[768,512]{1,0:T(8,128)(2,1)S(1)}, u32[]{:S(2)}, u32[]{:S(2)}) collective-permute-start(bf16[768,512]{1,0:T(8,128)(2,1)S(1)} %slice.283), channel_id=1, source_target_pairs={{0,16},{8,24},{16,0},{24,8},{1,17},{9,25},{17,1},{25,9},{2,18},{10... | collective-permute-start | bytes 2359304 | tf_op jit(solution)/shard_map/ppermute | solution.py:24
  403.0 192.5 %reduce-scatter.8.cloned.1.call-start = ((), (), s32[]{:S(2)}) async-start(), calls=%async_computation.11 | async-start | bytes 8257536 | tf_op jit(solution)/shard_map/reduce_scatter | solution.py:885
  403.1 32.0 %collective-permute-start.27 = (bf16[1536,512]{1,0:T(8,128)(2,1)}, bf16[1536,512]{1,0:T(8,128)(2,1)S(1)}, u32[]{:S(2)}, u32[]{:S(2)}) collective-permute-start(bf16[1536,512]{1,0:T(8,128)(2,1)} %copy-done.67), channel_id=1, source_target_pairs={{0,8},{8,0},{16,24},{24,16},{1,9},{9,1},{17,25},{25,17},{2,10},{10... | collective-permute-start | bytes 4718600 | tf_op jit(solution)/shard_map/ppermute | solution.py:24
  404.4 32.0 %collective-permute-start.28 = (bf16[1536,512]{1,0:T(8,128)(2,1)S(1)}, bf16[1536,512]{1,0:T(8,128)(2,1)S(1)}, u32[]{:S(2)}, u32[]{:S(2)}) collective-permute-start(bf16[1536,512]{1,0:T(8,128)(2,1)S(1)} %copy-done.66), channel_id=1, source_target_pairs={{0,16},{8,24},{16,0},{24,8},{1,17},{9,25},{17,1},{25,9},{2,18},{10... | collective-permute-start | bytes 4718600 | tf_op jit(solution)/shard_map/ppermute | solution.py:24
  453.3 21.5 %collective-permute-start.31 = (bf16[192,2048]{1,0:T(8,128)(2,1)S(1)}, bf16[192,2048]{1,0:T(8,128)(2,1)S(1)}, u32[]{:S(2)}, u32[]{:S(2)}) collective-permute-start(bf16[192,2048]{1,0:T(8,128)(2,1)S(1)} %get-tuple-element.232), channel_id=1, source_target_pairs={{0,8},{8,0},{16,24},{24,16},{1,9},{9,1},{17,25},{25,17},{2,10},{10... | collective-permute-start | bytes 2359304 | tf_op jit(solution)/shard_map/ppermute | solution.py:24
  454.9 19.9 %collective-permute-start.32 = (bf16[192,2048]{1,0:T(8,128)(2,1)S(1)}, bf16[192,2048]{1,0:T(8,128)(2,1)S(1)}, u32[]{:S(2)}, u32[]{:S(2)}) collective-permute-start(bf16[192,2048]{1,0:T(8,128)(2,1)S(1)} %get-tuple-element.233), channel_id=1, source_target_pairs={{0,16},{8,24},{16,0},{24,8},{1,17},{9,25},{17,1},{25,9},{2,18},{10... | collective-permute-start | bytes 2359304 | tf_op jit(solution)/shard_map/ppermute | solution.py:24
  495.1 169.2 %reduce-scatter.10.cloned.1.call-start = ((), (), s32[]{:S(2)}) async-start(), calls=%async_computation.12 | async-start | bytes 2359296 | tf_op jit(solution)/shard_map/reduce_scatter | solution.py:885
  495.2 31.1 %collective-permute-start.33 = (bf16[384,2048]{1,0:T(8,128)(2,1)}, bf16[384,2048]{1,0:T(8,128)(2,1)S(1)}, u32[]{:S(2)}, u32[]{:S(2)}) collective-permute-start(bf16[384,2048]{1,0:T(8,128)(2,1)} %copy-done.69), channel_id=1, source_target_pairs={{0,8},{8,0},{16,24},{24,16},{1,9},{9,1},{17,25},{25,17},{2,10},{10... | collective-permute-start | bytes 4718600 | tf_op jit(solution)/shard_map/ppermute | solution.py:24
  495.6 30.7 %collective-permute-start.34 = (bf16[384,2048]{1,0:T(8,128)(2,1)}, bf16[384,2048]{1,0:T(8,128)(2,1)S(1)}, u32[]{:S(2)}, u32[]{:S(2)}) collective-permute-start(bf16[384,2048]{1,0:T(8,128)(2,1)} %copy-done.68), channel_id=1, source_target_pairs={{0,16},{8,24},{16,0},{24,8},{1,17},{9,25},{17,1},{25,9},{2,18},{10... | collective-permute-start | bytes 4718600 | tf_op jit(solution)/shard_map/ppermute | solution.py:24
  535.4 33.9 %collective-permute-start.36 = (bf16[384,2048]{1,0:T(8,128)(2,1)S(1)}, bf16[384,2048]{1,0:T(8,128)(2,1)S(1)}, u32[]{:S(2)}, u32[]{:S(2)}) collective-permute-start(bf16[384,2048]{1,0:T(8,128)(2,1)S(1)} %get-tuple-element.251), channel_id=1, source_target_pairs={{0,16},{8,24},{16,0},{24,8},{1,17},{9,25},{17,1},{25,9},{2,18},{10... | collective-permute-start | bytes 4718600 | tf_op jit(solution)/shard_map/ppermute | solution.py:24
  536.2 34.2 %collective-permute-start.35 = (bf16[384,2048]{1,0:T(8,128)(2,1)S(1)}, bf16[384,2048]{1,0:T(8,128)(2,1)S(1)}, u32[]{:S(2)}, u32[]{:S(2)}) collective-permute-start(bf16[384,2048]{1,0:T(8,128)(2,1)S(1)} %get-tuple-element.251), channel_id=1, source_target_pairs={{0,8},{8,0},{16,24},{24,16},{1,9},{9,1},{17,25},{25,17},{2,10},{10... | collective-permute-start | bytes 4718600 | tf_op jit(solution)/shard_map/ppermute | solution.py:24
  570.5 12.1 %collective-permute-start.38 = (bf16[192,2048]{1,0:T(8,128)(2,1)S(1)}, bf16[192,2048]{1,0:T(8,128)(2,1)S(1)}, u32[]{:S(2)}, u32[]{:S(2)}) collective-permute-start(bf16[192,2048]{1,0:T(8,128)(2,1)S(1)} %slice.286), channel_id=1, source_target_pairs={{0,8},{8,0},{16,24},{24,16},{1,9},{9,1},{17,25},{25,17},{2,10},{10... | collective-permute-start | bytes 2359304 | tf_op jit(solution)/shard_map/ppermute | solution.py:24
  571.6 12.0 %collective-permute-start.37 = (bf16[192,2048]{1,0:T(8,128)(2,1)S(1)}, bf16[192,2048]{1,0:T(8,128)(2,1)S(1)}, u32[]{:S(2)}, u32[]{:S(2)}) collective-permute-start(bf16[192,2048]{1,0:T(8,128)(2,1)S(1)} %slice.285), channel_id=1, source_target_pairs={{0,16},{8,24},{16,0},{24,8},{1,17},{9,25},{17,1},{25,9},{2,18},{10... | collective-permute-start | bytes 2359304 | tf_op jit(solution)/shard_map/ppermute | solution.py:24
  590.3 158.0 %reduce-scatter.14.cloned.1.call-start = ((), (), s32[]{:S(2)}) async-start(), calls=%async_computation.14 | async-start | bytes 4718592 | tf_op jit(solution)/shard_map/reduce_scatter | solution.py:885
  616.1 147.4 %reduce-scatter.12.cloned.1.call-start = ((), (), s32[]{:S(2)}) async-start(), calls=%async_computation.13 | async-start | bytes 7077888 | tf_op jit(solution)/shard_map/reduce_scatter | solution.py:885
  617.6 24.4 %collective-permute-start.41 = (bf16[384,512]{1,0:T(8,128)(2,1)S(1)}, bf16[384,512]{1,0:T(8,128)(2,1)S(1)}, u32[]{:S(2)}, u32[]{:S(2)}) collective-permute-start(bf16[384,512]{1,0:T(8,128)(2,1)S(1)} %get-tuple-element.343), channel_id=1, source_target_pairs={{0,24},{8,16},{16,8},{24,0},{1,25},{9,17},{17,9},{25,1},{2,26},{10... | collective-permute-start | bytes 1179656 | tf_op jit(solution)/shard_map/ppermute | solution.py:24
  619.5 22.5 %collective-permute-start.40 = (bf16[384,512]{1,0:T(8,128)(2,1)S(1)}, bf16[384,512]{1,0:T(8,128)(2,1)S(1)}, u32[]{:S(2)}, u32[]{:S(2)}) collective-permute-start(bf16[384,512]{1,0:T(8,128)(2,1)S(1)} %get-tuple-element.344), channel_id=1, source_target_pairs={{0,16},{8,24},{16,0},{24,8},{1,17},{9,25},{17,1},{25,9},{2,18},{10... | collective-permute-start | bytes 1179656 | tf_op jit(solution)/shard_map/ppermute | solution.py:24
  620.2 21.8 %collective-permute-start.39 = (bf16[384,512]{1,0:T(8,128)(2,1)S(1)}, bf16[384,512]{1,0:T(8,128)(2,1)S(1)}, u32[]{:S(2)}, u32[]{:S(2)}) collective-permute-start(bf16[384,512]{1,0:T(8,128)(2,1)S(1)} %get-tuple-element.345), channel_id=1, source_target_pairs={{0,8},{8,0},{16,24},{24,16},{1,9},{9,1},{17,25},{25,17},{2,10},{10... | collective-permute-start | bytes 1179656 | tf_op jit(solution)/shard_map/ppermute | solution.py:24
  674.2 19.7 %collective-permute-start.42 = (bf16[192,2048]{1,0:T(8,128)(2,1)S(1)}, bf16[192,2048]{1,0:T(8,128)(2,1)S(1)}, u32[]{:S(2)}, u32[]{:S(2)}) collective-permute-start(bf16[192,2048]{1,0:T(8,128)(2,1)S(1)} %get-tuple-element.282), channel_id=1, source_target_pairs={{0,8},{8,0},{16,24},{24,16},{1,9},{9,1},{17,25},{25,17},{2,10},{10... | collective-permute-start | bytes 2359304 | tf_op jit(solution)/shard_map/ppermute | solution.py:24
  675.0 18.9 %collective-permute-start.43 = (bf16[192,2048]{1,0:T(8,128)(2,1)S(1)}, bf16[192,2048]{1,0:T(8,128)(2,1)S(1)}, u32[]{:S(2)}, u32[]{:S(2)}) collective-permute-start(bf16[192,2048]{1,0:T(8,128)(2,1)S(1)} %get-tuple-element.283), channel_id=1, source_target_pairs={{0,16},{8,24},{16,0},{24,8},{1,17},{9,25},{17,1},{25,9},{2,18},{10... | collective-permute-start | bytes 2359304 | tf_op jit(solution)/shard_map/ppermute | solution.py:24
  697.3 25.8 %collective-permute-start.44 = (bf16[384,2048]{1,0:T(8,128)(2,1)}, bf16[384,2048]{1,0:T(8,128)(2,1)}, u32[]{:S(2)}, u32[]{:S(2)}) collective-permute-start(bf16[384,2048]{1,0:T(8,128)(2,1)} %get-tuple-element.292), channel_id=1, source_target_pairs={{0,8},{8,0},{16,24},{24,16},{1,9},{9,1},{17,25},{25,17},{2,10},{10... | collective-permute-start | bytes 4718600 | tf_op jit(solution)/shard_map/ppermute | solution.py:24
  698.6 27.1 %collective-permute-start.45 = (bf16[384,2048]{1,0:T(8,128)(2,1)}, bf16[384,2048]{1,0:T(8,128)(2,1)}, u32[]{:S(2)}, u32[]{:S(2)}) collective-permute-start(bf16[384,2048]{1,0:T(8,128)(2,1)} %get-tuple-element.293), channel_id=1, source_target_pairs={{0,16},{8,24},{16,0},{24,8},{1,17},{9,25},{17,1},{25,9},{2,18},{10... | collective-permute-start | bytes 4718600 | tf_op jit(solution)/shard_map/ppermute | solution.py:24
  733.1 5.0 collective-permute-start.46
  738.2 5.1 collective-permute-start.47
  743.4 4.9 collective-permute-start.54
  749.5 8.5 %collective-permute-start.50 = (bf16[64,2816]{1,0:T(8,128)(2,1)S(1)}, bf16[64,2816]{1,0:T(8,128)(2,1)S(1)}, u32[]{:S(2)}, u32[]{:S(2)}) collective-permute-start(bf16[64,2816]{1,0:T(8,128)(2,1)S(1)} %get-tuple-element.351), channel_id=1, source_target_pairs={{0,24},{8,16},{16,8},{24,0},{1,25},{9,17},{17,9},{25,1},{2,26},{10... | collective-permute-start | bytes 1081352 | tf_op jit(solution)/shard_map/ppermute | solution.py:24
  750.6 11.1 %collective-permute-start.49 = (bf16[64,2816]{1,0:T(8,128)(2,1)S(1)}, bf16[64,2816]{1,0:T(8,128)(2,1)S(1)}, u32[]{:S(2)}, u32[]{:S(2)}) collective-permute-start(bf16[64,2816]{1,0:T(8,128)(2,1)S(1)} %get-tuple-element.352), channel_id=1, source_target_pairs={{0,16},{8,24},{16,0},{24,8},{1,17},{9,25},{17,1},{25,9},{2,18},{10... | collective-permute-start | bytes 1081352 | tf_op jit(solution)/shard_map/ppermute | solution.py:24
  751.6 10.2 %collective-permute-start.48 = (bf16[64,2816]{1,0:T(8,128)(2,1)S(1)}, bf16[64,2816]{1,0:T(8,128)(2,1)S(1)}, u32[]{:S(2)}, u32[]{:S(2)}) collective-permute-start(bf16[64,2816]{1,0:T(8,128)(2,1)S(1)} %get-tuple-element.353), channel_id=1, source_target_pairs={{0,8},{8,0},{16,24},{24,16},{1,9},{9,1},{17,25},{25,17},{2,10},{10... | collective-permute-start | bytes 1081352 | tf_op jit(solution)/shard_map/ppermute | solution.py:24
  763.5 4.9 collective-permute-start.56
  764.8 8.7 %collective-permute-start.53 = (bf16[64,1536]{1,0:T(8,128)(2,1)S(1)}, bf16[64,1536]{1,0:T(8,128)(2,1)S(1)}, u32[]{:S(2)}, u32[]{:S(2)}) collective-permute-start(bf16[64,1536]{1,0:T(8,128)(2,1)S(1)} %get-tuple-element.355), channel_id=1, source_target_pairs={{0,24},{8,16},{16,8},{24,0},{1,25},{9,17},{17,9},{25,1},{2,26},{10... | collective-permute-start | bytes 589832 | tf_op jit(solution)/shard_map/ppermute | solution.py:24
  765.9 11.2 %collective-permute-start.52 = (bf16[64,1536]{1,0:T(8,128)(2,1)S(1)}, bf16[64,1536]{1,0:T(8,128)(2,1)S(1)}, u32[]{:S(2)}, u32[]{:S(2)}) collective-permute-start(bf16[64,1536]{1,0:T(8,128)(2,1)S(1)} %get-tuple-element.356), channel_id=1, source_target_pairs={{0,16},{8,24},{16,0},{24,8},{1,17},{9,25},{17,1},{25,9},{2,18},{10... | collective-permute-start | bytes 589832 | tf_op jit(solution)/shard_map/ppermute | solution.py:24
  766.8 10.3 %collective-permute-start.51 = (bf16[64,1536]{1,0:T(8,128)(2,1)S(1)}, bf16[64,1536]{1,0:T(8,128)(2,1)S(1)}, u32[]{:S(2)}, u32[]{:S(2)}) collective-permute-start(bf16[64,1536]{1,0:T(8,128)(2,1)S(1)} %get-tuple-element.357), channel_id=1, source_target_pairs={{0,8},{8,0},{16,24},{24,16},{1,9},{9,1},{17,25},{25,17},{2,10},{10... | collective-permute-start | bytes 589832 | tf_op jit(solution)/shard_map/ppermute | solution.py:24
  (110 other events, 1185.7 us)
Sparse Core Ops, SparseCore 0:
  32.3 67.7 all-gather.5
  102.3 27.6 all-gather.7
  131.7 28.6 all-gather.9
  161.9 90.2 all-gather.11
  253.6 71.8 all-gather.13
  403.2 79.5 reduce-scatter.5
  495.2 77.8 reduce-scatter.7
  590.4 35.1 reduce-scatter.9
  627.9 48.3 reduce-scatter.13
  678.5 68.4 reduce-scatter.11

commit v14 on v13

--- a/solution.py
+++ b/solution.py
@@ -108,9 +108,8 @@
     return part
 
 
-def scatter_small(parts, axis, before_last=()):
+def scatter_small(parts, axis):
     for bit in reversed(bits_of(lax.axis_size(axis))):
-        parts = after(parts, before_last) if bit == 1 else parts
         half = parts.shape[0] // 2
         second = (lax.axis_index(axis) & bit) != 0
         low, high = parts[:half], parts[half:]
@@ -1019,6 +1018,9 @@
         step, marks, rows_of(turned, 2, 3, 4, 5), here, seq, beside,
     )
     out_rows, sum_cv = others
+    summed_c = jnp.concatenate(after([summed_ck, summed_crg], sums_one), axis=1)
+    sent_c = owners_parts(summed_c)
+    terms = after(terms, summed_c, sent_c[0])
     if within is None:
         terms = [outside(t, groups, unit, back=True) for t in terms]
     tokens_grad, _, norm_sums = norm_back(terms, inputs_b, d_after, rows_of(vec, 0), within, here)
@@ -1039,11 +1041,12 @@
         ],
         axis=2,
     )
+    parts_c = after(sent_c, tokens_grad)
+    sum_ck, sum_cr, sum_g = join_columns(parts_c, [ffn_key.shape[1], width, width], here)
+    vector_rows = after(vector_rows, sum_ck)
     sums_seq = scatter_small(vector_rows.reshape((-1,) + vector_rows.shape[2:]), "seq")
-    summed_c = jnp.concatenate(after([summed_ck, summed_crg], sums_seq), axis=1)
-    sum_ck, sum_cr, sum_g = owners_rows(summed_c, [ffn_key.shape[1], width, width])
-    sum_vec = scatter_small(sums_seq, "dp", sum_ck)[0]
-    sum_r, sum_k, sum_v = owners_rows(after(summed_in, sum_ck), [width] * 3)
+    sum_vec = scatter_small(sums_seq, "dp")[0]
+    sum_r, sum_k, sum_v = owners_rows(after(summed_in, sums_seq), [width] * 3)
     return (
         out_rows[None], tokens_grad[None], sum_r, sum_k, sum_v, sum_g, sum_o,
         sum_ck, sum_cr, sum_cv, sum_vec,

time: 795 us -> 799 us (level)
    unnamed x220 -> x236, local copies, waits for them, and re-layouts: 38.7 us -> 40.6 us
  transfers between devices with their start and end apart: 67 -> 67, of which waited for: 37 -> 35; matrix products, arithmetic and copies ran while one was open for 20% -> 21% of each run, Pallas kernels for 30% -> 29%
where the time goes in v14:
time: 799 us; the launch traced here: 789 us
  Pallas kernels  244 us (31%)
  waiting for transfers between devices  236 us (30%)
  matrix products  137 us (17%)
  local copies, waits for them, and re-layouts  69.6 us (9%)
  starting transfers between devices  68.7 us (9%)
  other arithmetic  17.1 us (2%)
  between operations  15.8 us (2%)
    pallas_call x33, Pallas kernels, kernel(): pl.pallas_call(body, out_shape=[jax.ShapeDtypeStruct(shape, kind) for sha...  244 us
    ppermute x57, waiting for transfers between devices, swap(): return lax.ppermute(value, axis, [(i, i ^ distance) for i in range(size)])  232 us
    dot_general x21, matrix products, dot(): return lax.dot_general(left, right, dims, preferred_element_type=F32)  137 us
    ppermute x57, starting transfers between devices, swap(): return lax.ppermute(value, axis, [(i, i ^ distance) for i in range(size)])  67.8 us
    unnamed x236, local copies, waits for them, and re-layouts  40.6 us
  transfers between devices with their start and end apart: 67, of which 35 were waited for; matrix products, arithmetic and copies ran while one was open for 21% of the time, Pallas kernels for 29%

profile of v14, /device:TPU:0, one launch (start us, length us, event | category | flops | bytes accessed | tf_op | source)
XLA Modules:
  0.0 788.6 jit_solution(13154183401359392167)
XLA Ops:
  11.9 3.0 collective-permute-start
  16.5 7.0 collective-permute-done.refs_1_
  23.5 7.7 collective-permute-done.1.refs_2_
  41.8 2.7 collective-permute-start.5
  45.8 7.6 collective-permute-done.5
  56.6 12.3 %collective-permute-done.7.refs_2_ = bf16[384,2048]{1,0:T(8,128)(2,1)} collective-permute-done((bf16[384,2048]{1,0:T(8,128)(2,1)}, bf16[384,2048]{1,0:T(8,128)(2,1)}, u32[]{:S(2)}, u32[]{:S(2)}) %collective-permute-start.7) | collective-permute-done | bytes 1572896 | tf_op jit(solution)/shard_map/ppermute | solution.py:24
  74.6 14.2 %collective-permute-done.9.refs_4_ = bf16[192,2048]{1,0:T(8,128)(2,1)} collective-permute-done((bf16[192,2048]{1,0:T(8,128)(2,1)S(1)}, bf16[192,2048]{1,0:T(8,128)(2,1)}, u32[]{:S(2)}, u32[]{:S(2)}) %collective-permute-start.9) | collective-permute-done | bytes 786464 | tf_op jit(solution)/shard_map/ppermute | solution.py:24
  97.4 2.8 all-gather.6.cloned.1.call-done.refs_7_.refs_8_.refs_9_.refs_10_
  100.2 25.9 %mixes.2 = (bf16[1536,2048]{1,0:T(8,128)(2,1)}, bf16[1536,2048]{1,0:T(8,128)(2,1)}, bf16[1536,2048]{1,0:T(8,128)(2,1)}, bf16[1536,2048]{1,0:T(8,128)(2,1)}, bf16...) custom-call(s32[1]{0:T(128)} %bitcast.here, ...), custom_call_target="tpu_custom_call" | custom-call | tf_op jit(solution)/shard_map/mixes/pallas_call | solution.py:133
  127.5 13.4 %wkv_forward.1 = (f32[1536,512]{1,0:T(8,128)}, bf16[12,512,128]{2,1,0:T(8,128)(2,1)S(1)}) custom-call(s32[1]{0:T(128)} %bitcast.here, bf16[1536,512]{1,0:T(8,128)(2,1)S(1)} %copy-done.15, bf16[1536,512]{1,0:T(8,128)(2,1)} %get-tuple-element.193.k_ref, bf16[1536,512]{1,0:T(8,128)(2,1)} %get-tuple-element.194.v_ref, f32[1536,128]{1,0:T(8,128)S(1)} %copy-done, ...), custom_call_target="tpu_custom_call" | custom-call | tf_op jit(solution)/shard_map/wkv_forward/pallas_call | solution.py:133
  143.7 10.1 %gate.1 = (f32[1536,512]{1,0:T(8,128)}, bf16[1536,512]{1,0:T(8,128)(2,1)S(1)}) custom-call(s32[1]{0:T(128)} %bitcast.here, bf16[1536,2048]{1,0:T(8,128)(2,1)} %get-tuple-element.189.refs_0_, bf16[2048,512]{1,0:T(8,128)(2,1)S(1)} %copy-done.8, f32[1536,512]{1,0:T(8,128)} %get-tuple-element.195.refs_2_.wkv_ref, f32[8,512]{1,0:T(8,128)S(1)} %maximum_maximum_fusion.par_ref.refs_3_), custom_call_target="tpu_custom_call" | custom-call | tf_op jit(solution)/shard_map/gate/pallas_call | solution.py:133
  154.9 3.4 stack_rows.3
  160.4 2.8 convolution_convert_fusion.7
  170.7 12.4 %collective-permute-done.11.high_ref = bf16[192,2048]{1,0:T(8,128)(2,1)S(1)} collective-permute-done((bf16[192,2048]{1,0:T(8,128)(2,1)S(1)}, bf16[192,2048]{1,0:T(8,128)(2,1)S(1)}, u32[]{:S(2)}, u32[]{:S(2)}) %collective-permute-start.11) | collective-permute-done | bytes 786464 | tf_op jit(solution)/shard_map/ppermute | solution.py:24
  184.3 3.3 relay.4
  191.5 2.8 convolution_convert_fusion.10.refs_0_
  194.3 29.1 %collective-permute-done.12.refs_1_ = bf16[384,2048]{1,0:T(8,128)(2,1)} collective-permute-done((bf16[384,2048]{1,0:T(8,128)(2,1)}, bf16[384,2048]{1,0:T(8,128)(2,1)}, u32[]{:S(2)}, u32[]{:S(2)}) %collective-permute-start.12) | collective-permute-done | bytes 1572896 | tf_op jit(solution)/shard_map/ppermute | solution.py:24
  224.6 4.7 after_norm.1
  230.5 33.1 %collective-permute-done.15.refs_2_ = bf16[384,2048]{1,0:T(8,128)(2,1)S(1)} collective-permute-done((bf16[384,2048]{1,0:T(8,128)(2,1)S(1)}, bf16[384,2048]{1,0:T(8,128)(2,1)S(1)}, u32[]{:S(2)}, u32[]{:S(2)}) %collective-permute-start.15) | collective-permute-done | bytes 1572896 | tf_op jit(solution)/shard_map/ppermute | solution.py:24
  266.6 14.2 %collective-permute-done.17.refs_4_ = bf16[192,2048]{1,0:T(8,128)(2,1)S(1)} collective-permute-done((bf16[192,2048]{1,0:T(8,128)(2,1)S(1)}, bf16[192,2048]{1,0:T(8,128)(2,1)S(1)}, u32[]{:S(2)}, u32[]{:S(2)}) %collective-permute-start.17) | collective-permute-done | bytes 786464 | tf_op jit(solution)/shard_map/ppermute | solution.py:24
  280.9 2.7 slice.278
  289.1 3.0 slice.326.refs_7_.refs_5_
  292.1 16.2 %mixes.3 = (bf16[1536,2048]{1,0:T(8,128)(2,1)}, bf16[1536,2048]{1,0:T(8,128)(2,1)}, bf16[1536,2048]{1,0:T(8,128)(2,1)}, f32[1536,512]{1,0:T(8,128)}, bf16[1536,512]{1,0:T(8,128)(2,1)}) custom-call(s32[1]{0:T(128)} %bitcast.here, bf16[384,2048]{1,0:T(8,128)(2,1)} %copy-done.33, bf16[384,2048]{1,0:T(8,128)(2,1)} %copy-done.78, bf16[384,2048]{1,0:T(8,128)(2,1)} %copy-done.77, ...), custom_call_target="tpu_custom_call" | custom-call | tf_op jit(solution)/shard_map/mixes/pallas_call | solution.py:133
  311.9 25.2 %multiply_convert_fusion.1 = (bf16[1536,1792]{1,0:T(8,128)(2,1)}, bf16[1536,1792]{1,0:T(8,128)(2,1)}) fusion(bf16[1536,2048]{1,0:T(8,128)(2,1)} %get-tuple-element.252, bf16[2048,2304]{1,0:T(8,128)(2,1)} %all-gather.12.cloned.1.call-done.refs_4_), kind=kOutput, calls=%fused_computation.2 | convolution fusion | flops 11312824320 | bytes 24641536 | tf_op jit(solution)/shard_map/dot_general | solution.py:637
  337.1 6.0 value_columns.7
  350.2 6.0 value_columns.6.two_ref
  357.5 6.0 value_columns.5.one_ref
  364.7 6.0 value_columns.4.refs_5_
  377.9 9.0 %spread_columns.2 = bf16[1536,2048]{1,0:T(8,128)(2,1)} custom-call(s32[1]{0:T(128)} %bitcast.here, bf16[384,2048]{1,0:T(8,128)(2,1)S(1)} %bitcast.92, bf16[448,2304]{1,0:T(8,128)(2,1)} %collective-permute-done.18.refs_1_, bf16[448,2304]{1,0:T(8,128)(2,1)} %collective-permute-done.19.refs_2_, bf16[192,2048]{1,0:T(8,128)(2,1)S(1)} %collective-permute-done.21.refs_3_, ...), custom_call_target="tpu_custom_call" | custom-call | tf_op jit(solution)/shard_map/spread_columns/pallas_call | solution.py:133
  387.0 16.1 %convolution_convert_fusion.1 = bf16[1792,2048]{1,0:T(8,128)(2,1)} fusion(bf16[1536,1792]{1,0:T(8,128)(2,1)S(1)} %bitcast.100, bf16[1536,2048]{1,0:T(8,128)(2,1)} %spread_columns.2), kind=kOutput, calls=%fused_computation.5 | convolution fusion | flops 11277959168 | bytes 19136512 | tf_op jit(solution)/shard_map/dot_general | solution.py:637
  406.0 18.8 %multiply_convert_fusion.refs_0_.refs_2_ = bf16[1536,1792]{1,0:T(8,128)(2,1)} fusion(bf16[1536,1792]{1,0:T(8,128)(2,1)} %get-tuple-element.234, bf16[1536,2048]{1,0:T(8,128)(2,1)} %spread_columns.2, bf16[1792,2048]{1,0:T(8,128)(2,1)} %all-gather.14.cloned.1.call-done.right_ref), kind=kOutput, calls=%fused_computation.1 | convolution fusion | flops 11282546688 | bytes 24641536 | tf_op jit(solution)/shard_map/dot_general | solution.py:637
  424.8 10.3 %collective-permute-done.27.refs_6_ = bf16[1536,512]{1,0:T(8,128)(2,1)S(1)} collective-permute-done((bf16[1536,512]{1,0:T(8,128)(2,1)}, bf16[1536,512]{1,0:T(8,128)(2,1)S(1)}, u32[]{:S(2)}, u32[]{:S(2)}) %collective-permute-start.27) | collective-permute-done | bytes 1572896 | tf_op jit(solution)/shard_map/ppermute | solution.py:24
  437.5 7.0 channel.1
  444.6 8.6 %mixes_back.6 = (bf16[192,2048]{1,0:T(8,128)(2,1)S(1)}, bf16[192,2048]{1,0:T(8,128)(2,1)S(1)}, f32[8,2048]{1,0:T(8,128)S(1)}) custom-call(s32[1]{0:T(128)} %bitcast.here, bf16[1536,1792]{1,0:T(8,128)(2,1)} %multiply_convert_fusion.refs_0_.refs_2_, bf16[1536,512]{1,0:T(8,128)(2,1)S(1)} %get-tuple-element.250.refs_1_.refs_3_, ...), custom_call_target="tpu_custom_call" | custom-call | tf_op jit(solution)/shard_map/mixes_back/pallas_call | solution.py:133
  456.3 16.1 %mixes_back.7 = (bf16[384,2048]{1,0:T(8,128)(2,1)S(1)}, bf16[384,2048]{1,0:T(8,128)(2,1)S(1)}, f32[8,2048]{1,0:T(8,128)S(1)}) custom-call(s32[1]{0:T(128)} %bitcast.here, bf16[1536,1792]{1,0:T(8,128)(2,1)} %multiply_convert_fusion.refs_0_.refs_2_, bf16[1536,512]{1,0:T(8,128)(2,1)S(1)} %get-tuple-element.250.refs_1_.refs_3_, ...), custom_call_target="tpu_custom_call" | custom-call | tf_op jit(solution)/shard_map/mixes_back/pallas_call | solution.py:133
  478.9 16.2 %convolution_convert_fusion = bf16[2048,1792]{1,0:T(8,128)(2,1)} fusion(bf16[1536,2048]{1,0:T(8,128)(2,1)} %get-tuple-element.252, bf16[1536,1792]{1,0:T(8,128)(2,1)S(1)} %bitcast.98), kind=kOutput, calls=%fused_computation.4 | convolution fusion | flops 11277959168 | bytes 19136512 | tf_op jit(solution)/shard_map/dot_general | solution.py:637
  497.9 8.9 %mixes_back.8 = (bf16[384,2048]{1,0:T(8,128)(2,1)S(1)}, f32[8,2048]{1,0:T(8,128)S(1)}) custom-call(s32[1]{0:T(128)} %bitcast.here, bf16[1536,1792]{1,0:T(8,128)(2,1)} %multiply_convert_fusion.refs_0_.refs_2_, bf16[1536,512]{1,0:T(8,128)(2,1)S(1)} %get-tuple-element.250.refs_1_.refs_3_, bf16[1536,1792]{1,0:T(8,128)(2,1)} %multiply_convert_fusion.refs_0_.refs_2_, ...), custom_call_target="tpu_custom_call" | custom-call | tf_op jit(solution)/shard_map/mixes_back/pallas_call | solution.py:133
  506.9 7.9 convolution_convert_fusion.6
  514.8 11.7 %collective-permute-done.33.refs_1_ = bf16[384,2048]{1,0:T(8,128)(2,1)S(1)} collective-permute-done((bf16[384,2048]{1,0:T(8,128)(2,1)}, bf16[384,2048]{1,0:T(8,128)(2,1)S(1)}, u32[]{:S(2)}, u32[]{:S(2)}) %collective-permute-start.33) | collective-permute-done | bytes 1572896 | tf_op jit(solution)/shard_map/ppermute | solution.py:24
  528.1 6.9 norm_back.2
  539.8 29.5 %collective-permute-done.36 = bf16[384,2048]{1,0:T(8,128)(2,1)S(1)} collective-permute-done((bf16[384,2048]{1,0:T(8,128)(2,1)S(1)}, bf16[384,2048]{1,0:T(8,128)(2,1)S(1)}, u32[]{:S(2)}, u32[]{:S(2)}) %collective-permute-start.36) | collective-permute-done | bytes 1572896 | tf_op jit(solution)/shard_map/ppermute | solution.py:24
  577.0 3.5 add_add_fusion
  584.9 5.3 add_convert_fusion
  591.6 2.6 convolution_convert_fusion.11
  596.9 8.6 %gate_backward.1 = (bf16[1536,512]{1,0:T(8,128)(2,1)S(1)}, bf16[1536,512]{1,0:T(8,128)(2,1)S(1)}, f32[8,512]{1,0:T(8,128)S(1)}) custom-call(s32[1]{0:T(128)} %bitcast.here, f32[1536,512]{1,0:T(8,128)} %get-tuple-element.195.refs_2_.wkv_ref, f32[1536,512]{1,0:T(8,128)} %get-tuple-element.264.g_ref, bf16[1536,512]{1,0:T(8,128)(2,1)S(1)} %copy-done.19, ...), custom_call_target="tpu_custom_call" | custom-call | tf_op jit(solution)/shard_map/gate_backward/pallas_call | solution.py:133
  605.6 7.8 convolution_convert_fusion.5
  613.4 2.6 pad_maximum_fusion.1
  621.1 20.8 %wkv_backward.1 = (bf16[1536,512]{1,0:T(8,128)(2,1)S(1)}, bf16[1536,512]{1,0:T(8,128)(2,1)S(1)}, bf16[1536,512]{1,0:T(8,128)(2,1)}, f32[8,512]{1,0:T(8,128)S(1)}) custom-call(s32[1]{0:T(128)} %bitcast.here, bf16[1536,512]{1,0:T(8,128)(2,1)} %get-tuple-element.192.r_ref, bf16[1536,512]{1,0:T(8,128)(2,1)} %get-tuple-element.193.k_ref, ...), custom_call_target="tpu_custom_call" | custom-call | tf_op jit(solution)/shard_map/wkv_backward/pallas_call | solution.py:133
  642.0 7.7 convolution_convert_fusion.4
  649.8 6.9 convolution_convert_fusion.2
  656.7 3.7 convolution_convert_fusion.3
  660.4 3.1 pad_maximum_fusion
  665.7 8.4 %mixes_back.9 = (bf16[192,2048]{1,0:T(8,128)(2,1)S(1)}, bf16[192,2048]{1,0:T(8,128)(2,1)S(1)}, f32[8,2048]{1,0:T(8,128)S(1)}) custom-call(s32[1]{0:T(128)} %bitcast.here, bf16[1536,512]{1,0:T(8,128)(2,1)S(1)} %get-tuple-element.306.refs_0_.refs_4_, bf16[1536,512]{1,0:T(8,128)(2,1)S(1)} %copy-done.4, bf16[1536,512]{1,0:T(8,128)(2,1)} %get-tuple-element.308.refs_2_.refs_6_, ...), custom_call_target="tpu_custom_call" | custom-call | tf_op jit(solution)/shard_map/mixes_back/pallas_call | solution.py:133
  676.6 15.3 %mixes_back.10 = (bf16[384,2048]{1,0:T(8,128)(2,1)S(1)}, bf16[384,2048]{1,0:T(8,128)(2,1)S(1)}, f32[8,2048]{1,0:T(8,128)S(1)}) custom-call(s32[1]{0:T(128)} %bitcast.here, bf16[1536,512]{1,0:T(8,128)(2,1)S(1)} %get-tuple-element.306.refs_0_.refs_4_, bf16[1536,512]{1,0:T(8,128)(2,1)} %copy-done.3, bf16[1536,512]{1,0:T(8,128)(2,1)} %get-tuple-element.308.refs_2_.refs_6_, ...), custom_call_target="tpu_custom_call" | custom-call | tf_op jit(solution)/shard_map/mixes_back/pallas_call | solution.py:133
  694.2 3.3 relay.7
  707.5 8.4 %mixes_back.11 = (bf16[384,2048]{1,0:T(8,128)(2,1)S(1)}, f32[8,2048]{1,0:T(8,128)S(1)}) custom-call(s32[1]{0:T(128)} %bitcast.here, bf16[1536,512]{1,0:T(8,128)(2,1)S(1)} %get-tuple-element.306.refs_0_.refs_4_, bf16[1536,512]{1,0:T(8,128)(2,1)S(1)} %copy-done.5, bf16[1536,512]{1,0:T(8,128)(2,1)} %get-tuple-element.308.refs_2_.refs_6_, ...), custom_call_target="tpu_custom_call" | custom-call | tf_op jit(solution)/shard_map/mixes_back/pallas_call | solution.py:133
  719.5 2.6 convert_element_type.180
  727.1 4.8 collective-permute-done.45.refs_2_
  737.0 7.2 norm_back.3
  749.0 4.0 collective-permute-done.49
  753.9 3.5 collective-permute-done.50
  759.5 3.2 collective-permute-done.54
  772.1 4.6 collective-permute-done.53.refs_3_
  776.6 3.7 collective-permute-done.52.refs_2_
  (481 shorter events, 180.5 us)
Async XLA Ops:
  7.2 93.0 %all-gather.6.cloned.1.call-start = ((), (), s32[]{:S(2)}) async-start(), calls=%async_computation.5 | async-start | bytes 7077888 | tf_op jit(solution)/shard_map/all_gather | solution.py:881
  11.9 11.5 %collective-permute-start = (bf16[80,2048]{1,0:T(8,128)(2,1)S(1)}, bf16[80,2048]{1,0:T(8,128)(2,1)S(1)}, u32[]{:S(2)}, u32[]{:S(2)}) collective-permute-start(bf16[80,2048]{1,0:T(8,128)(2,1)S(1)} %get-tuple-element.178.refs_1_), channel_id=1, source_target_pairs={{0,8},{8,0},{16,24},{24,16},{1,9},{9,1},{17,25},{25,17},{2,10},{10... | collective-permute-start | bytes 983048 | tf_op jit(solution)/shard_map/ppermute | solution.py:24
  15.0 16.2 %collective-permute-start.1 = (bf16[80,2048]{1,0:T(8,128)(2,1)S(1)}, bf16[80,2048]{1,0:T(8,128)(2,1)S(1)}, u32[]{:S(2)}, u32[]{:S(2)}) collective-permute-start(bf16[80,2048]{1,0:T(8,128)(2,1)S(1)} %get-tuple-element.179.refs_2_), channel_id=1, source_target_pairs={{0,16},{8,24},{16,0},{24,8},{1,17},{9,25},{17,1},{25,9},{2,18},{10... | collective-permute-start | bytes 983048 | tf_op jit(solution)/shard_map/ppermute | solution.py:24
  16.5 14.7 %collective-permute-start.2 = (bf16[80,2048]{1,0:T(8,128)(2,1)S(1)}, bf16[80,2048]{1,0:T(8,128)(2,1)S(1)}, u32[]{:S(2)}, u32[]{:S(2)}) collective-permute-start(bf16[80,2048]{1,0:T(8,128)(2,1)S(1)} %get-tuple-element.180.refs_3_), channel_id=1, source_target_pairs={{0,24},{8,16},{16,8},{24,0},{1,25},{9,17},{17,9},{25,1},{2,26},{10... | collective-permute-start | bytes 983048 | tf_op jit(solution)/shard_map/ppermute | solution.py:24
  32.2 109.9 %all-gather.8.cloned.1.call-start = ((), (), s32[]{:S(2)}) async-start(), calls=%async_computation.6 | async-start | bytes 2359296 | tf_op jit(solution)/shard_map/all_gather | solution.py:881
  33.5 35.4 %collective-permute-start.7 = (bf16[384,2048]{1,0:T(8,128)(2,1)}, bf16[384,2048]{1,0:T(8,128)(2,1)}, u32[]{:S(2)}, u32[]{:S(2)}) collective-permute-start(bf16[384,2048]{1,0:T(8,128)(2,1)} %hold.1.refs_0_), channel_id=1, source_target_pairs={{0,16},{8,24},{16,0},{24,8},{1,17},{9,25},{17,1},{25,9},{2,18},{10... | collective-permute-start | bytes 4718600 | tf_op jit(solution)/shard_map/ppermute | solution.py:24
  35.0 34.1 %collective-permute-start.6 = (bf16[384,2048]{1,0:T(8,128)(2,1)}, bf16[384,2048]{1,0:T(8,128)(2,1)}, u32[]{:S(2)}, u32[]{:S(2)}) collective-permute-start(bf16[384,2048]{1,0:T(8,128)(2,1)} %hold.1.refs_0_), channel_id=1, source_target_pairs={{0,8},{8,0},{16,24},{24,16},{1,9},{9,1},{17,25},{25,17},{2,10},{10... | collective-permute-start | bytes 4718600 | tf_op jit(solution)/shard_map/ppermute | solution.py:24
  41.8 11.6 %collective-permute-start.5 = (bf16[4,4,14,64]{3,2,1,0:T(8,128)(2,1)S(1)}, bf16[4,4,14,64]{3,2,1,0:T(8,128)(2,1)S(1)}, u32[]{:S(2)}, u32[]{:S(2)}) collective-permute-start(bf16[4,4,14,64]{3,2,1,0:T(8,128)(2,1)S(1)} %pad_maximum_fusion.6), channel_id=1, source_target_pairs={{0,4},{1,5},{2,6},{3,7},{4,0},{5,1},{6,2},{7,3},{8,12},{9,13},{10,... | collective-permute-start | bytes 86024 | tf_op jit(solution)/shard_map/ppermute | solution.py:24
  69.2 91.2 %all-gather.10.cloned.1.call-start = ((), (), s32[]{:S(2)}) async-start(), calls=%async_computation.7 | async-start | bytes 2359296 | tf_op jit(solution)/shard_map/all_gather | solution.py:881
  71.7 17.2 %collective-permute-start.9 = (bf16[192,2048]{1,0:T(8,128)(2,1)S(1)}, bf16[192,2048]{1,0:T(8,128)(2,1)}, u32[]{:S(2)}, u32[]{:S(2)}) collective-permute-start(bf16[192,2048]{1,0:T(8,128)(2,1)S(1)} %slice.260), channel_id=1, source_target_pairs={{0,8},{8,0},{16,24},{24,16},{1,9},{9,1},{17,25},{25,17},{2,10},{10... | collective-permute-start | bytes 2359304 | tf_op jit(solution)/shard_map/ppermute | solution.py:24
  73.1 17.1 %collective-permute-start.8 = (bf16[192,2048]{1,0:T(8,128)(2,1)S(1)}, bf16[192,2048]{1,0:T(8,128)(2,1)}, u32[]{:S(2)}, u32[]{:S(2)}) collective-permute-start(bf16[192,2048]{1,0:T(8,128)(2,1)S(1)} %slice.259), channel_id=1, source_target_pairs={{0,16},{8,24},{16,0},{24,8},{1,17},{9,25},{17,1},{25,9},{2,18},{10... | collective-permute-start | bytes 2359304 | tf_op jit(solution)/shard_map/ppermute | solution.py:24
  90.3 198.8 %all-gather.12.cloned.1.call-start = ((), (), s32[]{:S(2)}) async-start(), calls=%async_computation.8 | async-start | bytes 10616832 | tf_op jit(solution)/shard_map/all_gather | solution.py:881
  93.9 61.0 %collective-permute-start.18 = (bf16[448,2304]{1,0:T(8,128)(2,1)}, bf16[448,2304]{1,0:T(8,128)(2,1)}, u32[]{:S(2)}, u32[]{:S(2)}) collective-permute-start(bf16[448,2304]{1,0:T(8,128)(2,1)} %get-tuple-element.207), channel_id=1, source_target_pairs={{0,8},{8,0},{16,24},{24,16},{1,9},{9,1},{17,25},{25,17},{2,10},{10... | collective-permute-start | bytes 6193160 | tf_op jit(solution)/shard_map/ppermute | solution.py:24
  94.3 60.7 %collective-permute-start.19 = (bf16[448,2304]{1,0:T(8,128)(2,1)}, bf16[448,2304]{1,0:T(8,128)(2,1)}, u32[]{:S(2)}, u32[]{:S(2)}) collective-permute-start(bf16[448,2304]{1,0:T(8,128)(2,1)} %get-tuple-element.208), channel_id=1, source_target_pairs={{0,16},{8,24},{16,0},{24,8},{1,17},{9,25},{17,1},{25,9},{2,18},{10... | collective-permute-start | bytes 6193160 | tf_op jit(solution)/shard_map/ppermute | solution.py:24
  95.7 59.2 %collective-permute-start.20 = (bf16[64,2304]{1,0:T(8,128)(2,1)}, bf16[64,2304]{1,0:T(8,128)(2,1)}, u32[]{:S(2)}, u32[]{:S(2)}) collective-permute-start(bf16[64,2304]{1,0:T(8,128)(2,1)} %get-tuple-element.209), channel_id=1, source_target_pairs={{0,24},{8,16},{16,8},{24,0},{1,25},{9,17},{17,9},{25,1},{2,26},{10... | collective-permute-start | bytes 884744 | tf_op jit(solution)/shard_map/ppermute | solution.py:24
  158.4 178.7 %all-gather.14.cloned.1.call-start = ((), (), s32[]{:S(2)}) async-start(), calls=%async_computation.9 | async-start | bytes 8257536 | tf_op jit(solution)/shard_map/all_gather | solution.py:881
  159.0 425.9 %reduce-scatter.6.cloned.1.call-start = ((), (), s32[]{:S(2)}) async-start(), calls=%async_computation.10 | async-start | bytes 8257536 | tf_op jit(solution)/shard_map/reduce_scatter | solution.py:884
  163.4 19.7 %collective-permute-start.11 = (bf16[192,2048]{1,0:T(8,128)(2,1)S(1)}, bf16[192,2048]{1,0:T(8,128)(2,1)S(1)}, u32[]{:S(2)}, u32[]{:S(2)}) collective-permute-start(bf16[192,2048]{1,0:T(8,128)(2,1)S(1)} %get-tuple-element.363), channel_id=1, source_target_pairs={{0,16},{8,24},{16,0},{24,8},{1,17},{9,25},{17,1},{25,9},{2,18},{10... | collective-permute-start | bytes 2359304 | tf_op jit(solution)/shard_map/ppermute | solution.py:24
  164.9 19.4 %collective-permute-start.10 = (bf16[192,2048]{1,0:T(8,128)(2,1)S(1)}, bf16[192,2048]{1,0:T(8,128)(2,1)S(1)}, u32[]{:S(2)}, u32[]{:S(2)}) collective-permute-start(bf16[192,2048]{1,0:T(8,128)(2,1)S(1)} %get-tuple-element.364), channel_id=1, source_target_pairs={{0,8},{8,0},{16,24},{24,16},{1,9},{9,1},{17,25},{25,17},{2,10},{10... | collective-permute-start | bytes 2359304 | tf_op jit(solution)/shard_map/ppermute | solution.py:24
  187.6 35.8 %collective-permute-start.12 = (bf16[384,2048]{1,0:T(8,128)(2,1)}, bf16[384,2048]{1,0:T(8,128)(2,1)}, u32[]{:S(2)}, u32[]{:S(2)}) collective-permute-start(bf16[384,2048]{1,0:T(8,128)(2,1)} %get-tuple-element.198), channel_id=1, source_target_pairs={{0,8},{8,0},{16,24},{24,16},{1,9},{9,1},{17,25},{25,17},{2,10},{10... | collective-permute-start | bytes 4718600 | tf_op jit(solution)/shard_map/ppermute | solution.py:24
  189.1 35.5 %collective-permute-start.13 = (bf16[384,2048]{1,0:T(8,128)(2,1)}, bf16[384,2048]{1,0:T(8,128)(2,1)}, u32[]{:S(2)}, u32[]{:S(2)}) collective-permute-start(bf16[384,2048]{1,0:T(8,128)(2,1)} %get-tuple-element.199), channel_id=1, source_target_pairs={{0,16},{8,24},{16,0},{24,8},{1,17},{9,25},{17,1},{25,9},{2,18},{10... | collective-permute-start | bytes 4718600 | tf_op jit(solution)/shard_map/ppermute | solution.py:24
  229.4 34.2 %collective-permute-start.15 = (bf16[384,2048]{1,0:T(8,128)(2,1)S(1)}, bf16[384,2048]{1,0:T(8,128)(2,1)S(1)}, u32[]{:S(2)}, u32[]{:S(2)}) collective-permute-start(bf16[384,2048]{1,0:T(8,128)(2,1)S(1)} %get-tuple-element.201.refs_0_), channel_id=1, source_target_pairs={{0,16},{8,24},{16,0},{24,8},{1,17},{9,25},{17,1},{25,9},{2,18},{10... | collective-permute-start | bytes 4718600 | tf_op jit(solution)/shard_map/ppermute | solution.py:24
  230.1 34.3 %collective-permute-start.14 = (bf16[384,2048]{1,0:T(8,128)(2,1)S(1)}, bf16[384,2048]{1,0:T(8,128)(2,1)S(1)}, u32[]{:S(2)}, u32[]{:S(2)}) collective-permute-start(bf16[384,2048]{1,0:T(8,128)(2,1)S(1)} %get-tuple-element.201.refs_0_), channel_id=1, source_target_pairs={{0,8},{8,0},{16,24},{24,16},{1,9},{9,1},{17,25},{25,17},{2,10},{10... | collective-permute-start | bytes 4718600 | tf_op jit(solution)/shard_map/ppermute | solution.py:24
  264.6 16.3 %collective-permute-start.17 = (bf16[192,2048]{1,0:T(8,128)(2,1)S(1)}, bf16[192,2048]{1,0:T(8,128)(2,1)S(1)}, u32[]{:S(2)}, u32[]{:S(2)}) collective-permute-start(bf16[192,2048]{1,0:T(8,128)(2,1)S(1)} %slice.268), channel_id=1, source_target_pairs={{0,8},{8,0},{16,24},{24,16},{1,9},{9,1},{17,25},{25,17},{2,10},{10... | collective-permute-start | bytes 2359304 | tf_op jit(solution)/shard_map/ppermute | solution.py:24
  265.1 15.9 %collective-permute-start.16 = (bf16[192,2048]{1,0:T(8,128)(2,1)S(1)}, bf16[192,2048]{1,0:T(8,128)(2,1)S(1)}, u32[]{:S(2)}, u32[]{:S(2)}) collective-permute-start(bf16[192,2048]{1,0:T(8,128)(2,1)S(1)} %slice.267), channel_id=1, source_target_pairs={{0,16},{8,24},{16,0},{24,8},{1,17},{9,25},{17,1},{25,9},{2,18},{10... | collective-permute-start | bytes 2359304 | tf_op jit(solution)/shard_map/ppermute | solution.py:24
  285.8 22.5 %collective-permute-start.22 = (bf16[192,2048]{1,0:T(8,128)(2,1)}, bf16[192,2048]{1,0:T(8,128)(2,1)S(1)}, u32[]{:S(2)}, u32[]{:S(2)}) collective-permute-start(bf16[192,2048]{1,0:T(8,128)(2,1)} %slice.279), channel_id=1, source_target_pairs={{0,8},{8,0},{16,24},{24,16},{1,9},{9,1},{17,25},{25,17},{2,10},{10... | collective-permute-start | bytes 2359304 | tf_op jit(solution)/shard_map/ppermute | solution.py:24
  286.8 21.5 %collective-permute-start.21 = (bf16[192,2048]{1,0:T(8,128)(2,1)}, bf16[192,2048]{1,0:T(8,128)(2,1)S(1)}, u32[]{:S(2)}, u32[]{:S(2)}) collective-permute-start(bf16[192,2048]{1,0:T(8,128)(2,1)} %slice.278), channel_id=1, source_target_pairs={{0,16},{8,24},{16,0},{24,8},{1,17},{9,25},{17,1},{25,9},{2,18},{10... | collective-permute-start | bytes 2359304 | tf_op jit(solution)/shard_map/ppermute | solution.py:24
  308.3 36.8 %collective-permute-start.24 = (bf16[1536,512]{1,0:T(8,128)(2,1)}, bf16[1536,512]{1,0:T(8,128)(2,1)}, u32[]{:S(2)}, u32[]{:S(2)}) collective-permute-start(bf16[1536,512]{1,0:T(8,128)(2,1)} %get-tuple-element.228.refs_5_), channel_id=1, source_target_pairs={{0,16},{8,24},{16,0},{24,8},{1,17},{9,25},{17,1},{25,9},{2,18},{10... | collective-permute-start | bytes 4718600 | tf_op jit(solution)/shard_map/ppermute | solution.py:24
  310.5 34.6 %collective-permute-start.23 = (bf16[1536,512]{1,0:T(8,128)(2,1)}, bf16[1536,512]{1,0:T(8,128)(2,1)}, u32[]{:S(2)}, u32[]{:S(2)}) collective-permute-start(bf16[1536,512]{1,0:T(8,128)(2,1)} %get-tuple-element.228.refs_5_), channel_id=1, source_target_pairs={{0,8},{8,0},{16,24},{24,16},{1,9},{9,1},{17,25},{25,17},{2,10},{10... | collective-permute-start | bytes 4718600 | tf_op jit(solution)/shard_map/ppermute | solution.py:24
  343.2 28.6 %collective-permute-start.26 = (bf16[768,512]{1,0:T(8,128)(2,1)S(1)}, bf16[768,512]{1,0:T(8,128)(2,1)S(1)}, u32[]{:S(2)}, u32[]{:S(2)}) collective-permute-start(bf16[768,512]{1,0:T(8,128)(2,1)S(1)} %get-tuple-element.361), channel_id=1, source_target_pairs={{0,16},{8,24},{16,0},{24,8},{1,17},{9,25},{17,1},{25,9},{2,18},{10... | collective-permute-start | bytes 2359304 | tf_op jit(solution)/shard_map/ppermute | solution.py:24
  345.1 26.8 %collective-permute-start.25 = (bf16[768,512]{1,0:T(8,128)(2,1)S(1)}, bf16[768,512]{1,0:T(8,128)(2,1)S(1)}, u32[]{:S(2)}, u32[]{:S(2)}) collective-permute-start(bf16[768,512]{1,0:T(8,128)(2,1)S(1)} %get-tuple-element.362), channel_id=1, source_target_pairs={{0,8},{8,0},{16,24},{24,16},{1,9},{9,1},{17,25},{25,17},{2,10},{10... | collective-permute-start | bytes 2359304 | tf_op jit(solution)/shard_map/ppermute | solution.py:24
  347.5 28.6 %collective-permute-start.30 = (bf16[768,512]{1,0:T(8,128)(2,1)S(1)}, bf16[768,512]{1,0:T(8,128)(2,1)S(1)}, u32[]{:S(2)}, u32[]{:S(2)}) collective-permute-start(bf16[768,512]{1,0:T(8,128)(2,1)S(1)} %slice.284), channel_id=1, source_target_pairs={{0,8},{8,0},{16,24},{24,16},{1,9},{9,1},{17,25},{25,17},{2,10},{10... | collective-permute-start | bytes 2359304 | tf_op jit(solution)/shard_map/ppermute | solution.py:24
  349.6 26.5 %collective-permute-start.29 = (bf16[768,512]{1,0:T(8,128)(2,1)S(1)}, bf16[768,512]{1,0:T(8,128)(2,1)S(1)}, u32[]{:S(2)}, u32[]{:S(2)}) collective-permute-start(bf16[768,512]{1,0:T(8,128)(2,1)S(1)} %slice.283), channel_id=1, source_target_pairs={{0,16},{8,24},{16,0},{24,8},{1,17},{9,25},{17,1},{25,9},{2,18},{10... | collective-permute-start | bytes 2359304 | tf_op jit(solution)/shard_map/ppermute | solution.py:24
  403.1 192.4 %reduce-scatter.8.cloned.1.call-start = ((), (), s32[]{:S(2)}) async-start(), calls=%async_computation.11 | async-start | bytes 8257536 | tf_op jit(solution)/shard_map/reduce_scatter | solution.py:884
  403.1 32.0 %collective-permute-start.27 = (bf16[1536,512]{1,0:T(8,128)(2,1)}, bf16[1536,512]{1,0:T(8,128)(2,1)S(1)}, u32[]{:S(2)}, u32[]{:S(2)}) collective-permute-start(bf16[1536,512]{1,0:T(8,128)(2,1)} %copy-done.72), channel_id=1, source_target_pairs={{0,8},{8,0},{16,24},{24,16},{1,9},{9,1},{17,25},{25,17},{2,10},{10... | collective-permute-start | bytes 4718600 | tf_op jit(solution)/shard_map/ppermute | solution.py:24
  404.4 31.9 %collective-permute-start.28 = (bf16[1536,512]{1,0:T(8,128)(2,1)S(1)}, bf16[1536,512]{1,0:T(8,128)(2,1)S(1)}, u32[]{:S(2)}, u32[]{:S(2)}) collective-permute-start(bf16[1536,512]{1,0:T(8,128)(2,1)S(1)} %copy-done.71), channel_id=1, source_target_pairs={{0,16},{8,24},{16,0},{24,8},{1,17},{9,25},{17,1},{25,9},{2,18},{10... | collective-permute-start | bytes 4718600 | tf_op jit(solution)/shard_map/ppermute | solution.py:24
  453.3 21.5 %collective-permute-start.31 = (bf16[192,2048]{1,0:T(8,128)(2,1)S(1)}, bf16[192,2048]{1,0:T(8,128)(2,1)S(1)}, u32[]{:S(2)}, u32[]{:S(2)}) collective-permute-start(bf16[192,2048]{1,0:T(8,128)(2,1)S(1)} %get-tuple-element.239), channel_id=1, source_target_pairs={{0,8},{8,0},{16,24},{24,16},{1,9},{9,1},{17,25},{25,17},{2,10},{10... | collective-permute-start | bytes 2359304 | tf_op jit(solution)/shard_map/ppermute | solution.py:24
  454.8 19.9 %collective-permute-start.32 = (bf16[192,2048]{1,0:T(8,128)(2,1)S(1)}, bf16[192,2048]{1,0:T(8,128)(2,1)S(1)}, u32[]{:S(2)}, u32[]{:S(2)}) collective-permute-start(bf16[192,2048]{1,0:T(8,128)(2,1)S(1)} %get-tuple-element.240), channel_id=1, source_target_pairs={{0,16},{8,24},{16,0},{24,8},{1,17},{9,25},{17,1},{25,9},{2,18},{10... | collective-permute-start | bytes 2359304 | tf_op jit(solution)/shard_map/ppermute | solution.py:24
  495.1 169.2 %reduce-scatter.10.cloned.1.call-start = ((), (), s32[]{:S(2)}) async-start(), calls=%async_computation.12 | async-start | bytes 2359296 | tf_op jit(solution)/shard_map/reduce_scatter | solution.py:884
  495.1 31.3 %collective-permute-start.33 = (bf16[384,2048]{1,0:T(8,128)(2,1)}, bf16[384,2048]{1,0:T(8,128)(2,1)S(1)}, u32[]{:S(2)}, u32[]{:S(2)}) collective-permute-start(bf16[384,2048]{1,0:T(8,128)(2,1)} %copy-done.74), channel_id=1, source_target_pairs={{0,8},{8,0},{16,24},{24,16},{1,9},{9,1},{17,25},{25,17},{2,10},{10... | collective-permute-start | bytes 4718600 | tf_op jit(solution)/shard_map/ppermute | solution.py:24
  495.6 30.9 %collective-permute-start.34 = (bf16[384,2048]{1,0:T(8,128)(2,1)}, bf16[384,2048]{1,0:T(8,128)(2,1)S(1)}, u32[]{:S(2)}, u32[]{:S(2)}) collective-permute-start(bf16[384,2048]{1,0:T(8,128)(2,1)} %copy-done.73), channel_id=1, source_target_pairs={{0,16},{8,24},{16,0},{24,8},{1,17},{9,25},{17,1},{25,9},{2,18},{10... | collective-permute-start | bytes 4718600 | tf_op jit(solution)/shard_map/ppermute | solution.py:24
  535.6 33.8 %collective-permute-start.36 = (bf16[384,2048]{1,0:T(8,128)(2,1)S(1)}, bf16[384,2048]{1,0:T(8,128)(2,1)S(1)}, u32[]{:S(2)}, u32[]{:S(2)}) collective-permute-start(bf16[384,2048]{1,0:T(8,128)(2,1)S(1)} %get-tuple-element.258), channel_id=1, source_target_pairs={{0,16},{8,24},{16,0},{24,8},{1,17},{9,25},{17,1},{25,9},{2,18},{10... | collective-permute-start | bytes 4718600 | tf_op jit(solution)/shard_map/ppermute | solution.py:24
  536.3 34.1 %collective-permute-start.35 = (bf16[384,2048]{1,0:T(8,128)(2,1)S(1)}, bf16[384,2048]{1,0:T(8,128)(2,1)S(1)}, u32[]{:S(2)}, u32[]{:S(2)}) collective-permute-start(bf16[384,2048]{1,0:T(8,128)(2,1)S(1)} %get-tuple-element.258), channel_id=1, source_target_pairs={{0,8},{8,0},{16,24},{24,16},{1,9},{9,1},{17,25},{25,17},{2,10},{10... | collective-permute-start | bytes 4718600 | tf_op jit(solution)/shard_map/ppermute | solution.py:24
  570.5 12.4 %collective-permute-start.38 = (bf16[192,2048]{1,0:T(8,128)(2,1)S(1)}, bf16[192,2048]{1,0:T(8,128)(2,1)S(1)}, u32[]{:S(2)}, u32[]{:S(2)}) collective-permute-start(bf16[192,2048]{1,0:T(8,128)(2,1)S(1)} %slice.286), channel_id=1, source_target_pairs={{0,8},{8,0},{16,24},{24,16},{1,9},{9,1},{17,25},{25,17},{2,10},{10... | collective-permute-start | bytes 2359304 | tf_op jit(solution)/shard_map/ppermute | solution.py:24
  571.6 12.0 %collective-permute-start.37 = (bf16[192,2048]{1,0:T(8,128)(2,1)S(1)}, bf16[192,2048]{1,0:T(8,128)(2,1)S(1)}, u32[]{:S(2)}, u32[]{:S(2)}) collective-permute-start(bf16[192,2048]{1,0:T(8,128)(2,1)S(1)} %slice.285), channel_id=1, source_target_pairs={{0,16},{8,24},{16,0},{24,8},{1,17},{9,25},{17,1},{25,9},{2,18},{10... | collective-permute-start | bytes 2359304 | tf_op jit(solution)/shard_map/ppermute | solution.py:24
  590.3 141.6 %reduce-scatter.12.cloned.1.call-start = ((), (), s32[]{:S(2)}) async-start(), calls=%async_computation.13 | async-start | bytes 4718592 | tf_op jit(solution)/shard_map/reduce_scatter | solution.py:884
  616.1 150.5 %reduce-scatter.14.cloned.1.call-start = ((), (), s32[]{:S(2)}) async-start(), calls=%async_computation.14 | async-start | bytes 7077888 | tf_op jit(solution)/shard_map/reduce_scatter | solution.py:884
  617.6 24.4 %collective-permute-start.41 = (bf16[384,512]{1,0:T(8,128)(2,1)S(1)}, bf16[384,512]{1,0:T(8,128)(2,1)S(1)}, u32[]{:S(2)}, u32[]{:S(2)}) collective-permute-start(bf16[384,512]{1,0:T(8,128)(2,1)S(1)} %get-tuple-element.357), channel_id=1, source_target_pairs={{0,24},{8,16},{16,8},{24,0},{1,25},{9,17},{17,9},{25,1},{2,26},{10... | collective-permute-start | bytes 1179656 | tf_op jit(solution)/shard_map/ppermute | solution.py:24
  619.6 22.3 %collective-permute-start.40 = (bf16[384,512]{1,0:T(8,128)(2,1)S(1)}, bf16[384,512]{1,0:T(8,128)(2,1)S(1)}, u32[]{:S(2)}, u32[]{:S(2)}) collective-permute-start(bf16[384,512]{1,0:T(8,128)(2,1)S(1)} %get-tuple-element.358), channel_id=1, source_target_pairs={{0,16},{8,24},{16,0},{24,8},{1,17},{9,25},{17,1},{25,9},{2,18},{10... | collective-permute-start | bytes 1179656 | tf_op jit(solution)/shard_map/ppermute | solution.py:24
  620.2 21.8 %collective-permute-start.39 = (bf16[384,512]{1,0:T(8,128)(2,1)S(1)}, bf16[384,512]{1,0:T(8,128)(2,1)S(1)}, u32[]{:S(2)}, u32[]{:S(2)}) collective-permute-start(bf16[384,512]{1,0:T(8,128)(2,1)S(1)} %get-tuple-element.359), channel_id=1, source_target_pairs={{0,8},{8,0},{16,24},{24,16},{1,9},{9,1},{17,25},{25,17},{2,10},{10... | collective-permute-start | bytes 1179656 | tf_op jit(solution)/shard_map/ppermute | solution.py:24
  674.1 20.0 %collective-permute-start.42 = (bf16[192,2048]{1,0:T(8,128)(2,1)S(1)}, bf16[192,2048]{1,0:T(8,128)(2,1)S(1)}, u32[]{:S(2)}, u32[]{:S(2)}) collective-permute-start(bf16[192,2048]{1,0:T(8,128)(2,1)S(1)} %get-tuple-element.289), channel_id=1, source_target_pairs={{0,8},{8,0},{16,24},{24,16},{1,9},{9,1},{17,25},{25,17},{2,10},{10... | collective-permute-start | bytes 2359304 | tf_op jit(solution)/shard_map/ppermute | solution.py:24
  675.1 19.1 %collective-permute-start.43 = (bf16[192,2048]{1,0:T(8,128)(2,1)S(1)}, bf16[192,2048]{1,0:T(8,128)(2,1)S(1)}, u32[]{:S(2)}, u32[]{:S(2)}) collective-permute-start(bf16[192,2048]{1,0:T(8,128)(2,1)S(1)} %get-tuple-element.290), channel_id=1, source_target_pairs={{0,16},{8,24},{16,0},{24,8},{1,17},{9,25},{17,1},{25,9},{2,18},{10... | collective-permute-start | bytes 2359304 | tf_op jit(solution)/shard_map/ppermute | solution.py:24
  697.5 29.5 %collective-permute-start.44 = (bf16[384,2048]{1,0:T(8,128)(2,1)}, bf16[384,2048]{1,0:T(8,128)(2,1)}, u32[]{:S(2)}, u32[]{:S(2)}) collective-permute-start(bf16[384,2048]{1,0:T(8,128)(2,1)} %get-tuple-element.299), channel_id=1, source_target_pairs={{0,8},{8,0},{16,24},{24,16},{1,9},{9,1},{17,25},{25,17},{2,10},{10... | collective-permute-start | bytes 4718600 | tf_op jit(solution)/shard_map/ppermute | solution.py:24
  698.8 33.1 %collective-permute-start.45 = (bf16[384,2048]{1,0:T(8,128)(2,1)}, bf16[384,2048]{1,0:T(8,128)(2,1)}, u32[]{:S(2)}, u32[]{:S(2)}) collective-permute-start(bf16[384,2048]{1,0:T(8,128)(2,1)} %get-tuple-element.300), channel_id=1, source_target_pairs={{0,16},{8,24},{16,0},{24,8},{1,17},{9,25},{17,1},{25,9},{2,18},{10... | collective-permute-start | bytes 4718600 | tf_op jit(solution)/shard_map/ppermute | solution.py:24
  733.4 11.0 %collective-permute-start.48 = (bf16[64,2816]{1,0:T(8,128)(2,1)S(1)}, bf16[64,2816]{1,0:T(8,128)(2,1)S(1)}, u32[]{:S(2)}, u32[]{:S(2)}) collective-permute-start(bf16[64,2816]{1,0:T(8,128)(2,1)S(1)} %get-tuple-element.365), channel_id=1, source_target_pairs={{0,24},{8,16},{16,8},{24,0},{1,25},{9,17},{17,9},{25,1},{2,26},{10... | collective-permute-start | bytes 1081352 | tf_op jit(solution)/shard_map/ppermute | solution.py:24
  735.1 11.1 %collective-permute-start.47 = (bf16[64,2816]{1,0:T(8,128)(2,1)S(1)}, bf16[64,2816]{1,0:T(8,128)(2,1)S(1)}, u32[]{:S(2)}, u32[]{:S(2)}) collective-permute-start(bf16[64,2816]{1,0:T(8,128)(2,1)S(1)} %get-tuple-element.366), channel_id=1, source_target_pairs={{0,16},{8,24},{16,0},{24,8},{1,17},{9,25},{17,1},{25,9},{2,18},{10... | collective-permute-start | bytes 1081352 | tf_op jit(solution)/shard_map/ppermute | solution.py:24
  735.5 10.7 %collective-permute-start.46 = (bf16[64,2816]{1,0:T(8,128)(2,1)S(1)}, bf16[64,2816]{1,0:T(8,128)(2,1)S(1)}, u32[]{:S(2)}, u32[]{:S(2)}) collective-permute-start(bf16[64,2816]{1,0:T(8,128)(2,1)S(1)} %get-tuple-element.367), channel_id=1, source_target_pairs={{0,8},{8,0},{16,24},{24,16},{1,9},{9,1},{17,25},{25,17},{2,10},{10... | collective-permute-start | bytes 1081352 | tf_op jit(solution)/shard_map/ppermute | solution.py:24
  748.0 5.0 collective-permute-start.49
  753.1 4.3 collective-permute-start.50
  757.5 5.2 collective-permute-start.54
  766.5 5.0 collective-permute-start.56
  767.9 8.7 %collective-permute-start.53 = (bf16[64,1536]{1,0:T(8,128)(2,1)S(1)}, bf16[64,1536]{1,0:T(8,128)(2,1)S(1)}, u32[]{:S(2)}, u32[]{:S(2)}) collective-permute-start(bf16[64,1536]{1,0:T(8,128)(2,1)S(1)} %get-tuple-element.369), channel_id=1, source_target_pairs={{0,24},{8,16},{16,8},{24,0},{1,25},{9,17},{17,9},{25,1},{2,26},{10... | collective-permute-start | bytes 589832 | tf_op jit(solution)/shard_map/ppermute | solution.py:24
  769.2 11.2 %collective-permute-start.52 = (bf16[64,1536]{1,0:T(8,128)(2,1)S(1)}, bf16[64,1536]{1,0:T(8,128)(2,1)S(1)}, u32[]{:S(2)}, u32[]{:S(2)}) collective-permute-start(bf16[64,1536]{1,0:T(8,128)(2,1)S(1)} %get-tuple-element.370), channel_id=1, source_target_pairs={{0,16},{8,24},{16,0},{24,8},{1,17},{9,25},{17,1},{25,9},{2,18},{10... | collective-permute-start | bytes 589832 | tf_op jit(solution)/shard_map/ppermute | solution.py:24
  770.2 10.1 %collective-permute-start.51 = (bf16[64,1536]{1,0:T(8,128)(2,1)S(1)}, bf16[64,1536]{1,0:T(8,128)(2,1)S(1)}, u32[]{:S(2)}, u32[]{:S(2)}) collective-permute-start(bf16[64,1536]{1,0:T(8,128)(2,1)S(1)} %get-tuple-element.371), channel_id=1, source_target_pairs={{0,8},{8,0},{16,24},{24,16},{1,9},{9,1},{17,25},{25,17},{2,10},{10... | collective-permute-start | bytes 589832 | tf_op jit(solution)/shard_map/ppermute | solution.py:24
  (118 other events, 1252.2 us)
Sparse Core Ops, SparseCore 0:
  32.3 67.7 all-gather.5
  102.3 27.6 all-gather.7
  131.7 28.6 all-gather.9
  161.9 90.2 all-gather.11
  253.6 71.8 all-gather.13
  403.2 79.3 reduce-scatter.5
  495.2 77.8 reduce-scatter.7
  590.4 34.9 reduce-scatter.9
  627.6 48.9 reduce-scatter.11
  678.7 67.9 reduce-scatter.13

commit v15 on v13

--- a/solution.py
+++ b/solution.py
@@ -1043,7 +1043,7 @@
     summed_c = jnp.concatenate(after([summed_ck, summed_crg], sums_seq), axis=1)
     sum_ck, sum_cr, sum_g = owners_rows(summed_c, [ffn_key.shape[1], width, width])
     sum_vec = scatter_small(sums_seq, "dp", sum_ck)[0]
-    sum_r, sum_k, sum_v = owners_rows(after(summed_in, sum_ck), [width] * 3)
+    sum_r, sum_k, sum_v = owners_rows(after(summed_in, sums_seq), [width] * 3)
     return (
         out_rows[None], tokens_grad[None], sum_r, sum_k, sum_v, sum_g, sum_o,
         sum_ck, sum_cr, sum_cv, sum_vec,

time: 795 us -> 795 us (level)
  no operation moved by 1% of the time
where the time goes in v15:
time: 795 us; the launch traced here: 785 us
  Pallas kernels  244 us (31%)
  waiting for transfers between devices  239 us (30%)
  matrix products  137 us (17%)
  starting transfers between devices  69 us (9%)
  local copies, waits for them, and re-layouts  62.9 us (8%)
  other arithmetic  17.2 us (2%)
  between operations  15.8 us (2%)
    pallas_call x33, Pallas kernels, kernel(): pl.pallas_call(body, out_shape=[jax.ShapeDtypeStruct(shape, kind) for sha...  244 us
    ppermute x57, waiting for transfers between devices, swap(): return lax.ppermute(value, axis, [(i, i ^ distance) for i in range(size)])  235 us
    dot_general x21, matrix products, dot(): return lax.dot_general(left, right, dims, preferred_element_type=F32)  137 us
    ppermute x57, starting transfers between devices, swap(): return lax.ppermute(value, axis, [(i, i ^ distance) for i in range(size)])  68.1 us
    unnamed x220, local copies, waits for them, and re-layouts  38.7 us
  transfers between devices with their start and end apart: 67, of which 37 were waited for; matrix products, arithmetic and copies ran while one was open for 20% of the time, Pallas kernels for 30%

profile of v15, /device:TPU:0, one launch (start us, length us, event | category | flops | bytes accessed | tf_op | source)
XLA Modules:
  0.0 785.4 jit_solution(6159714767690696992)
XLA Ops:
  11.9 3.0 collective-permute-start
  16.5 7.0 collective-permute-done.refs_1_
  23.5 7.7 collective-permute-done.1.refs_2_
  41.8 2.7 collective-permute-start.5
  45.8 7.6 collective-permute-done.5
  56.6 12.3 %collective-permute-done.7.refs_2_ = bf16[384,2048]{1,0:T(8,128)(2,1)} collective-permute-done((bf16[384,2048]{1,0:T(8,128)(2,1)}, bf16[384,2048]{1,0:T(8,128)(2,1)}, u32[]{:S(2)}, u32[]{:S(2)}) %collective-permute-start.7) | collective-permute-done | bytes 1572896 | tf_op jit(solution)/shard_map/ppermute | solution.py:24
  74.6 14.2 %collective-permute-done.9.refs_4_ = bf16[192,2048]{1,0:T(8,128)(2,1)} collective-permute-done((bf16[192,2048]{1,0:T(8,128)(2,1)S(1)}, bf16[192,2048]{1,0:T(8,128)(2,1)}, u32[]{:S(2)}, u32[]{:S(2)}) %collective-permute-start.9) | collective-permute-done | bytes 786464 | tf_op jit(solution)/shard_map/ppermute | solution.py:24
  97.4 2.8 all-gather.6.cloned.1.call-done.refs_7_.refs_8_.refs_9_.refs_10_
  100.2 25.9 %mixes.2 = (bf16[1536,2048]{1,0:T(8,128)(2,1)}, bf16[1536,2048]{1,0:T(8,128)(2,1)}, bf16[1536,2048]{1,0:T(8,128)(2,1)}, bf16[1536,2048]{1,0:T(8,128)(2,1)}, bf16...) custom-call(s32[1]{0:T(128)} %bitcast.here, ...), custom_call_target="tpu_custom_call" | custom-call | tf_op jit(solution)/shard_map/mixes/pallas_call | solution.py:134
  127.5 13.4 %wkv_forward.1 = (f32[1536,512]{1,0:T(8,128)}, bf16[12,512,128]{2,1,0:T(8,128)(2,1)S(1)}) custom-call(s32[1]{0:T(128)} %bitcast.here, bf16[1536,512]{1,0:T(8,128)(2,1)S(1)} %copy-done.15, bf16[1536,512]{1,0:T(8,128)(2,1)} %get-tuple-element.186.k_ref, bf16[1536,512]{1,0:T(8,128)(2,1)} %get-tuple-element.187.v_ref, f32[1536,128]{1,0:T(8,128)S(1)} %copy-done, ...), custom_call_target="tpu_custom_call" | custom-call | tf_op jit(solution)/shard_map/wkv_forward/pallas_call | solution.py:134
  143.7 10.1 %gate.1 = (f32[1536,512]{1,0:T(8,128)}, bf16[1536,512]{1,0:T(8,128)(2,1)S(1)}) custom-call(s32[1]{0:T(128)} %bitcast.here, bf16[1536,2048]{1,0:T(8,128)(2,1)} %get-tuple-element.182.refs_0_, bf16[2048,512]{1,0:T(8,128)(2,1)S(1)} %copy-done.8, f32[1536,512]{1,0:T(8,128)} %get-tuple-element.188.refs_2_.wkv_ref, f32[8,512]{1,0:T(8,128)S(1)} %maximum_maximum_fusion.par_ref.refs_3_), custom_call_target="tpu_custom_call" | custom-call | tf_op jit(solution)/shard_map/gate/pallas_call | solution.py:134
  155.0 3.4 stack_rows.3
  160.4 2.8 convolution_convert_fusion.7
  170.7 12.4 %collective-permute-done.11.high_ref = bf16[192,2048]{1,0:T(8,128)(2,1)S(1)} collective-permute-done((bf16[192,2048]{1,0:T(8,128)(2,1)S(1)}, bf16[192,2048]{1,0:T(8,128)(2,1)S(1)}, u32[]{:S(2)}, u32[]{:S(2)}) %collective-permute-start.11) | collective-permute-done | bytes 786464 | tf_op jit(solution)/shard_map/ppermute | solution.py:24
  184.3 3.3 relay.4
  191.5 2.8 convolution_convert_fusion.10.refs_0_
  194.3 29.1 %collective-permute-done.12.refs_1_ = bf16[384,2048]{1,0:T(8,128)(2,1)} collective-permute-done((bf16[384,2048]{1,0:T(8,128)(2,1)}, bf16[384,2048]{1,0:T(8,128)(2,1)}, u32[]{:S(2)}, u32[]{:S(2)}) %collective-permute-start.12) | collective-permute-done | bytes 1572896 | tf_op jit(solution)/shard_map/ppermute | solution.py:24
  224.6 4.8 after_norm.1
  230.5 33.1 %collective-permute-done.15.refs_2_ = bf16[384,2048]{1,0:T(8,128)(2,1)S(1)} collective-permute-done((bf16[384,2048]{1,0:T(8,128)(2,1)S(1)}, bf16[384,2048]{1,0:T(8,128)(2,1)S(1)}, u32[]{:S(2)}, u32[]{:S(2)}) %collective-permute-start.15) | collective-permute-done | bytes 1572896 | tf_op jit(solution)/shard_map/ppermute | solution.py:24
  266.6 14.3 %collective-permute-done.17.refs_4_ = bf16[192,2048]{1,0:T(8,128)(2,1)S(1)} collective-permute-done((bf16[192,2048]{1,0:T(8,128)(2,1)S(1)}, bf16[192,2048]{1,0:T(8,128)(2,1)S(1)}, u32[]{:S(2)}, u32[]{:S(2)}) %collective-permute-start.17) | collective-permute-done | bytes 786464 | tf_op jit(solution)/shard_map/ppermute | solution.py:24
  280.9 2.7 slice.278
  289.1 3.0 slice.326.refs_7_.refs_5_
  292.1 16.1 %mixes.3 = (bf16[1536,2048]{1,0:T(8,128)(2,1)}, bf16[1536,2048]{1,0:T(8,128)(2,1)}, bf16[1536,2048]{1,0:T(8,128)(2,1)}, f32[1536,512]{1,0:T(8,128)}, bf16[1536,512]{1,0:T(8,128)(2,1)}) custom-call(s32[1]{0:T(128)} %bitcast.here, bf16[384,2048]{1,0:T(8,128)(2,1)} %copy-done.33, bf16[384,2048]{1,0:T(8,128)(2,1)} %copy-done.73, bf16[384,2048]{1,0:T(8,128)(2,1)} %copy-done.72, ...), custom_call_target="tpu_custom_call" | custom-call | tf_op jit(solution)/shard_map/mixes/pallas_call | solution.py:134
  311.9 25.2 %multiply_convert_fusion.1 = (bf16[1536,1792]{1,0:T(8,128)(2,1)}, bf16[1536,1792]{1,0:T(8,128)(2,1)}) fusion(bf16[1536,2048]{1,0:T(8,128)(2,1)} %get-tuple-element.245, bf16[2048,2304]{1,0:T(8,128)(2,1)} %all-gather.12.cloned.1.call-done.refs_4_), kind=kOutput, calls=%fused_computation.2 | convolution fusion | flops 11312824320 | bytes 24641536 | tf_op jit(solution)/shard_map/dot_general | solution.py:638
  337.1 6.0 value_columns.7
  350.2 6.0 value_columns.6.two_ref
  357.5 6.0 value_columns.5.one_ref
  364.7 6.0 value_columns.4.refs_5_
  377.7 9.2 %spread_columns.2 = bf16[1536,2048]{1,0:T(8,128)(2,1)} custom-call(s32[1]{0:T(128)} %bitcast.here, bf16[384,2048]{1,0:T(8,128)(2,1)S(1)} %bitcast.92, bf16[448,2304]{1,0:T(8,128)(2,1)} %collective-permute-done.18.refs_1_, bf16[448,2304]{1,0:T(8,128)(2,1)} %collective-permute-done.19.refs_2_, bf16[192,2048]{1,0:T(8,128)(2,1)S(1)} %collective-permute-done.21.refs_3_, ...), custom_call_target="tpu_custom_call" | custom-call | tf_op jit(solution)/shard_map/spread_columns/pallas_call | solution.py:134
  386.9 16.1 %convolution_convert_fusion.1 = bf16[1792,2048]{1,0:T(8,128)(2,1)} fusion(bf16[1536,1792]{1,0:T(8,128)(2,1)S(1)} %bitcast.100, bf16[1536,2048]{1,0:T(8,128)(2,1)} %spread_columns.2), kind=kOutput, calls=%fused_computation.5 | convolution fusion | flops 11277959168 | bytes 19136512 | tf_op jit(solution)/shard_map/dot_general | solution.py:638
  406.1 18.8 %multiply_convert_fusion.refs_0_.refs_2_ = bf16[1536,1792]{1,0:T(8,128)(2,1)} fusion(bf16[1536,1792]{1,0:T(8,128)(2,1)} %get-tuple-element.227, bf16[1536,2048]{1,0:T(8,128)(2,1)} %spread_columns.2, bf16[1792,2048]{1,0:T(8,128)(2,1)} %all-gather.14.cloned.1.call-done.right_ref), kind=kOutput, calls=%fused_computation.1 | convolution fusion | flops 11282546688 | bytes 24641536 | tf_op jit(solution)/shard_map/dot_general | solution.py:638
  424.9 10.2 %collective-permute-done.27.refs_6_ = bf16[1536,512]{1,0:T(8,128)(2,1)S(1)} collective-permute-done((bf16[1536,512]{1,0:T(8,128)(2,1)}, bf16[1536,512]{1,0:T(8,128)(2,1)S(1)}, u32[]{:S(2)}, u32[]{:S(2)}) %collective-permute-start.27) | collective-permute-done | bytes 1572896 | tf_op jit(solution)/shard_map/ppermute | solution.py:24
  437.5 7.0 channel.1
  444.6 8.6 %mixes_back.6 = (bf16[192,2048]{1,0:T(8,128)(2,1)S(1)}, bf16[192,2048]{1,0:T(8,128)(2,1)S(1)}, f32[8,2048]{1,0:T(8,128)S(1)}) custom-call(s32[1]{0:T(128)} %bitcast.here, bf16[1536,1792]{1,0:T(8,128)(2,1)} %multiply_convert_fusion.refs_0_.refs_2_, bf16[1536,512]{1,0:T(8,128)(2,1)S(1)} %get-tuple-element.243.refs_1_.refs_3_, ...), custom_call_target="tpu_custom_call" | custom-call | tf_op jit(solution)/shard_map/mixes_back/pallas_call | solution.py:134
  456.3 16.1 %mixes_back.7 = (bf16[384,2048]{1,0:T(8,128)(2,1)S(1)}, bf16[384,2048]{1,0:T(8,128)(2,1)S(1)}, f32[8,2048]{1,0:T(8,128)S(1)}) custom-call(s32[1]{0:T(128)} %bitcast.here, bf16[1536,1792]{1,0:T(8,128)(2,1)} %multiply_convert_fusion.refs_0_.refs_2_, bf16[1536,512]{1,0:T(8,128)(2,1)S(1)} %get-tuple-element.243.refs_1_.refs_3_, ...), custom_call_target="tpu_custom_call" | custom-call | tf_op jit(solution)/shard_map/mixes_back/pallas_call | solution.py:134
  478.9 16.2 %convolution_convert_fusion = bf16[2048,1792]{1,0:T(8,128)(2,1)} fusion(bf16[1536,2048]{1,0:T(8,128)(2,1)} %get-tuple-element.245, bf16[1536,1792]{1,0:T(8,128)(2,1)S(1)} %bitcast.98), kind=kOutput, calls=%fused_computation.4 | convolution fusion | flops 11277959168 | bytes 19136512 | tf_op jit(solution)/shard_map/dot_general | solution.py:638
  498.0 8.9 %mixes_back.8 = (bf16[384,2048]{1,0:T(8,128)(2,1)S(1)}, f32[8,2048]{1,0:T(8,128)S(1)}) custom-call(s32[1]{0:T(128)} %bitcast.here, bf16[1536,1792]{1,0:T(8,128)(2,1)} %multiply_convert_fusion.refs_0_.refs_2_, bf16[1536,512]{1,0:T(8,128)(2,1)S(1)} %get-tuple-element.243.refs_1_.refs_3_, bf16[1536,1792]{1,0:T(8,128)(2,1)} %multiply_convert_fusion.refs_0_.refs_2_, ...), custom_call_target="tpu_custom_call" | custom-call | tf_op jit(solution)/shard_map/mixes_back/pallas_call | solution.py:134
  507.0 7.9 %convolution_convert_fusion.6 = bf16[2048,512]{1,0:T(8,128)(2,1)} fusion(bf16[1536,2048]{1,0:T(8,128)(2,1)} %get-tuple-element.247, bf16[1536,512]{1,0:T(8,128)(2,1)S(1)} %get-tuple-element.243.refs_1_.refs_3_), kind=kOutput, calls=%fused_computation.16 | convolution fusion | flops 3222274048 | bytes 9961472 | tf_op jit(solution)/shard_map/dot_general | solution.py:638
  514.9 11.4 %collective-permute-done.33.refs_1_ = bf16[384,2048]{1,0:T(8,128)(2,1)S(1)} collective-permute-done((bf16[384,2048]{1,0:T(8,128)(2,1)}, bf16[384,2048]{1,0:T(8,128)(2,1)S(1)}, u32[]{:S(2)}, u32[]{:S(2)}) %collective-permute-start.33) | collective-permute-done | bytes 1572896 | tf_op jit(solution)/shard_map/ppermute | solution.py:24
  527.9 6.9 norm_back.2
  539.7 29.7 %collective-permute-done.36 = bf16[384,2048]{1,0:T(8,128)(2,1)S(1)} collective-permute-done((bf16[384,2048]{1,0:T(8,128)(2,1)S(1)}, bf16[384,2048]{1,0:T(8,128)(2,1)S(1)}, u32[]{:S(2)}, u32[]{:S(2)}) %collective-permute-start.36) | collective-permute-done | bytes 1572896 | tf_op jit(solution)/shard_map/ppermute | solution.py:24
  576.8 3.5 add_add_fusion
  584.9 5.3 add_convert_fusion
  591.7 2.6 convolution_convert_fusion.11
  596.9 8.6 %gate_backward.1 = (bf16[1536,512]{1,0:T(8,128)(2,1)S(1)}, bf16[1536,512]{1,0:T(8,128)(2,1)S(1)}, f32[8,512]{1,0:T(8,128)S(1)}) custom-call(s32[1]{0:T(128)} %bitcast.here, f32[1536,512]{1,0:T(8,128)} %get-tuple-element.188.refs_2_.wkv_ref, f32[1536,512]{1,0:T(8,128)} %get-tuple-element.257.g_ref, bf16[1536,512]{1,0:T(8,128)(2,1)S(1)} %copy-done.19, ...), custom_call_target="tpu_custom_call" | custom-call | tf_op jit(solution)/shard_map/gate_backward/pallas_call | solution.py:134
  605.6 7.8 convolution_convert_fusion.5
  613.5 2.6 pad_maximum_fusion.1
  621.2 20.8 %wkv_backward.1 = (bf16[1536,512]{1,0:T(8,128)(2,1)S(1)}, bf16[1536,512]{1,0:T(8,128)(2,1)S(1)}, bf16[1536,512]{1,0:T(8,128)(2,1)}, f32[8,512]{1,0:T(8,128)S(1)}) custom-call(s32[1]{0:T(128)} %bitcast.here, bf16[1536,512]{1,0:T(8,128)(2,1)} %get-tuple-element.185.r_ref, bf16[1536,512]{1,0:T(8,128)(2,1)} %get-tuple-element.186.k_ref, ...), custom_call_target="tpu_custom_call" | custom-call | tf_op jit(solution)/shard_map/wkv_backward/pallas_call | solution.py:134
  642.0 7.7 convolution_convert_fusion.4
  649.8 6.9 convolution_convert_fusion.2
  656.7 3.7 convolution_convert_fusion.3
  660.4 3.1 pad_maximum_fusion
  665.8 8.4 %mixes_back.9 = (bf16[192,2048]{1,0:T(8,128)(2,1)S(1)}, bf16[192,2048]{1,0:T(8,128)(2,1)S(1)}, f32[8,2048]{1,0:T(8,128)S(1)}) custom-call(s32[1]{0:T(128)} %bitcast.here, bf16[1536,512]{1,0:T(8,128)(2,1)S(1)} %get-tuple-element.299.refs_0_.refs_4_, bf16[1536,512]{1,0:T(8,128)(2,1)S(1)} %copy-done.4, bf16[1536,512]{1,0:T(8,128)(2,1)} %get-tuple-element.301.refs_2_.refs_6_, ...), custom_call_target="tpu_custom_call" | custom-call | tf_op jit(solution)/shard_map/mixes_back/pallas_call | solution.py:134
  676.4 15.3 %mixes_back.10 = (bf16[384,2048]{1,0:T(8,128)(2,1)S(1)}, bf16[384,2048]{1,0:T(8,128)(2,1)S(1)}, f32[8,2048]{1,0:T(8,128)S(1)}) custom-call(s32[1]{0:T(128)} %bitcast.here, bf16[1536,512]{1,0:T(8,128)(2,1)S(1)} %get-tuple-element.299.refs_0_.refs_4_, bf16[1536,512]{1,0:T(8,128)(2,1)} %copy-done.3, bf16[1536,512]{1,0:T(8,128)(2,1)} %get-tuple-element.301.refs_2_.refs_6_, ...), custom_call_target="tpu_custom_call" | custom-call | tf_op jit(solution)/shard_map/mixes_back/pallas_call | solution.py:134
  694.0 3.3 relay.7
  704.8 8.4 %mixes_back.11 = (bf16[384,2048]{1,0:T(8,128)(2,1)S(1)}, f32[8,2048]{1,0:T(8,128)S(1)}) custom-call(s32[1]{0:T(128)} %bitcast.here, bf16[1536,512]{1,0:T(8,128)(2,1)S(1)} %get-tuple-element.299.refs_0_.refs_4_, bf16[1536,512]{1,0:T(8,128)(2,1)S(1)} %copy-done.5, bf16[1536,512]{1,0:T(8,128)(2,1)} %get-tuple-element.301.refs_2_.refs_6_, ...), custom_call_target="tpu_custom_call" | custom-call | tf_op jit(solution)/shard_map/mixes_back/pallas_call | solution.py:134
  714.5 2.7 convert_element_type.180
  723.1 2.6 collective-permute-done.45.refs_2_
  725.7 7.2 norm_back.3
  734.0 4.1 collective-permute-done.46
  738.8 4.5 collective-permute-done.47
  758.0 3.8 collective-permute-done.52.refs_2_
  768.9 4.6 collective-permute-done.50.refs_3_
  773.5 3.6 collective-permute-done.49.refs_2_
  (464 shorter events, 177.7 us)
Async XLA Ops:
  7.2 93.0 %all-gather.6.cloned.1.call-start = ((), (), s32[]{:S(2)}) async-start(), calls=%async_computation.5 | async-start | bytes 7077888 | tf_op jit(solution)/shard_map/all_gather | solution.py:882
  11.9 11.5 %collective-permute-start = (bf16[80,2048]{1,0:T(8,128)(2,1)S(1)}, bf16[80,2048]{1,0:T(8,128)(2,1)S(1)}, u32[]{:S(2)}, u32[]{:S(2)}) collective-permute-start(bf16[80,2048]{1,0:T(8,128)(2,1)S(1)} %get-tuple-element.171.refs_1_), channel_id=1, source_target_pairs={{0,8},{8,0},{16,24},{24,16},{1,9},{9,1},{17,25},{25,17},{2,10},{10... | collective-permute-start | bytes 983048 | tf_op jit(solution)/shard_map/ppermute | solution.py:24
  15.0 16.2 %collective-permute-start.1 = (bf16[80,2048]{1,0:T(8,128)(2,1)S(1)}, bf16[80,2048]{1,0:T(8,128)(2,1)S(1)}, u32[]{:S(2)}, u32[]{:S(2)}) collective-permute-start(bf16[80,2048]{1,0:T(8,128)(2,1)S(1)} %get-tuple-element.172.refs_2_), channel_id=1, source_target_pairs={{0,16},{8,24},{16,0},{24,8},{1,17},{9,25},{17,1},{25,9},{2,18},{10... | collective-permute-start | bytes 983048 | tf_op jit(solution)/shard_map/ppermute | solution.py:24
  16.5 14.7 %collective-permute-start.2 = (bf16[80,2048]{1,0:T(8,128)(2,1)S(1)}, bf16[80,2048]{1,0:T(8,128)(2,1)S(1)}, u32[]{:S(2)}, u32[]{:S(2)}) collective-permute-start(bf16[80,2048]{1,0:T(8,128)(2,1)S(1)} %get-tuple-element.173.refs_3_), channel_id=1, source_target_pairs={{0,24},{8,16},{16,8},{24,0},{1,25},{9,17},{17,9},{25,1},{2,26},{10... | collective-permute-start | bytes 983048 | tf_op jit(solution)/shard_map/ppermute | solution.py:24
  32.2 109.9 %all-gather.8.cloned.1.call-start = ((), (), s32[]{:S(2)}) async-start(), calls=%async_computation.6 | async-start | bytes 2359296 | tf_op jit(solution)/shard_map/all_gather | solution.py:882
  33.5 35.4 %collective-permute-start.7 = (bf16[384,2048]{1,0:T(8,128)(2,1)}, bf16[384,2048]{1,0:T(8,128)(2,1)}, u32[]{:S(2)}, u32[]{:S(2)}) collective-permute-start(bf16[384,2048]{1,0:T(8,128)(2,1)} %hold.1.refs_0_), channel_id=1, source_target_pairs={{0,16},{8,24},{16,0},{24,8},{1,17},{9,25},{17,1},{25,9},{2,18},{10... | collective-permute-start | bytes 4718600 | tf_op jit(solution)/shard_map/ppermute | solution.py:24
  35.0 34.1 %collective-permute-start.6 = (bf16[384,2048]{1,0:T(8,128)(2,1)}, bf16[384,2048]{1,0:T(8,128)(2,1)}, u32[]{:S(2)}, u32[]{:S(2)}) collective-permute-start(bf16[384,2048]{1,0:T(8,128)(2,1)} %hold.1.refs_0_), channel_id=1, source_target_pairs={{0,8},{8,0},{16,24},{24,16},{1,9},{9,1},{17,25},{25,17},{2,10},{10... | collective-permute-start | bytes 4718600 | tf_op jit(solution)/shard_map/ppermute | solution.py:24
  41.8 11.6 %collective-permute-start.5 = (bf16[4,4,14,64]{3,2,1,0:T(8,128)(2,1)S(1)}, bf16[4,4,14,64]{3,2,1,0:T(8,128)(2,1)S(1)}, u32[]{:S(2)}, u32[]{:S(2)}) collective-permute-start(bf16[4,4,14,64]{3,2,1,0:T(8,128)(2,1)S(1)} %pad_maximum_fusion.6), channel_id=1, source_target_pairs={{0,4},{1,5},{2,6},{3,7},{4,0},{5,1},{6,2},{7,3},{8,12},{9,13},{10,... | collective-permute-start | bytes 86024 | tf_op jit(solution)/shard_map/ppermute | solution.py:24
  69.2 91.2 %all-gather.10.cloned.1.call-start = ((), (), s32[]{:S(2)}) async-start(), calls=%async_computation.7 | async-start | bytes 2359296 | tf_op jit(solution)/shard_map/all_gather | solution.py:882
  71.7 17.2 %collective-permute-start.9 = (bf16[192,2048]{1,0:T(8,128)(2,1)S(1)}, bf16[192,2048]{1,0:T(8,128)(2,1)}, u32[]{:S(2)}, u32[]{:S(2)}) collective-permute-start(bf16[192,2048]{1,0:T(8,128)(2,1)S(1)} %slice.260), channel_id=1, source_target_pairs={{0,8},{8,0},{16,24},{24,16},{1,9},{9,1},{17,25},{25,17},{2,10},{10... | collective-permute-start | bytes 2359304 | tf_op jit(solution)/shard_map/ppermute | solution.py:24
  73.1 17.1 %collective-permute-start.8 = (bf16[192,2048]{1,0:T(8,128)(2,1)S(1)}, bf16[192,2048]{1,0:T(8,128)(2,1)}, u32[]{:S(2)}, u32[]{:S(2)}) collective-permute-start(bf16[192,2048]{1,0:T(8,128)(2,1)S(1)} %slice.259), channel_id=1, source_target_pairs={{0,16},{8,24},{16,0},{24,8},{1,17},{9,25},{17,1},{25,9},{2,18},{10... | collective-permute-start | bytes 2359304 | tf_op jit(solution)/shard_map/ppermute | solution.py:24
  90.3 198.8 %all-gather.12.cloned.1.call-start = ((), (), s32[]{:S(2)}) async-start(), calls=%async_computation.8 | async-start | bytes 10616832 | tf_op jit(solution)/shard_map/all_gather | solution.py:882
  93.9 61.1 %collective-permute-start.18 = (bf16[448,2304]{1,0:T(8,128)(2,1)}, bf16[448,2304]{1,0:T(8,128)(2,1)}, u32[]{:S(2)}, u32[]{:S(2)}) collective-permute-start(bf16[448,2304]{1,0:T(8,128)(2,1)} %get-tuple-element.200), channel_id=1, source_target_pairs={{0,8},{8,0},{16,24},{24,16},{1,9},{9,1},{17,25},{25,17},{2,10},{10... | collective-permute-start | bytes 6193160 | tf_op jit(solution)/shard_map/ppermute | solution.py:24
  94.3 60.7 %collective-permute-start.19 = (bf16[448,2304]{1,0:T(8,128)(2,1)}, bf16[448,2304]{1,0:T(8,128)(2,1)}, u32[]{:S(2)}, u32[]{:S(2)}) collective-permute-start(bf16[448,2304]{1,0:T(8,128)(2,1)} %get-tuple-element.201), channel_id=1, source_target_pairs={{0,16},{8,24},{16,0},{24,8},{1,17},{9,25},{17,1},{25,9},{2,18},{10... | collective-permute-start | bytes 6193160 | tf_op jit(solution)/shard_map/ppermute | solution.py:24
  95.7 59.2 %collective-permute-start.20 = (bf16[64,2304]{1,0:T(8,128)(2,1)}, bf16[64,2304]{1,0:T(8,128)(2,1)}, u32[]{:S(2)}, u32[]{:S(2)}) collective-permute-start(bf16[64,2304]{1,0:T(8,128)(2,1)} %get-tuple-element.202), channel_id=1, source_target_pairs={{0,24},{8,16},{16,8},{24,0},{1,25},{9,17},{17,9},{25,1},{2,26},{10... | collective-permute-start | bytes 884744 | tf_op jit(solution)/shard_map/ppermute | solution.py:24
  158.4 178.7 %all-gather.14.cloned.1.call-start = ((), (), s32[]{:S(2)}) async-start(), calls=%async_computation.9 | async-start | bytes 8257536 | tf_op jit(solution)/shard_map/all_gather | solution.py:882
  159.0 425.9 %reduce-scatter.6.cloned.1.call-start = ((), (), s32[]{:S(2)}) async-start(), calls=%async_computation.10 | async-start | bytes 8257536 | tf_op jit(solution)/shard_map/reduce_scatter | solution.py:885
  163.4 19.7 %collective-permute-start.11 = (bf16[192,2048]{1,0:T(8,128)(2,1)S(1)}, bf16[192,2048]{1,0:T(8,128)(2,1)S(1)}, u32[]{:S(2)}, u32[]{:S(2)}) collective-permute-start(bf16[192,2048]{1,0:T(8,128)(2,1)S(1)} %get-tuple-element.349), channel_id=1, source_target_pairs={{0,16},{8,24},{16,0},{24,8},{1,17},{9,25},{17,1},{25,9},{2,18},{10... | collective-permute-start | bytes 2359304 | tf_op jit(solution)/shard_map/ppermute | solution.py:24
  164.9 19.4 %collective-permute-start.10 = (bf16[192,2048]{1,0:T(8,128)(2,1)S(1)}, bf16[192,2048]{1,0:T(8,128)(2,1)S(1)}, u32[]{:S(2)}, u32[]{:S(2)}) collective-permute-start(bf16[192,2048]{1,0:T(8,128)(2,1)S(1)} %get-tuple-element.350), channel_id=1, source_target_pairs={{0,8},{8,0},{16,24},{24,16},{1,9},{9,1},{17,25},{25,17},{2,10},{10... | collective-permute-start | bytes 2359304 | tf_op jit(solution)/shard_map/ppermute | solution.py:24
  187.6 35.8 %collective-permute-start.12 = (bf16[384,2048]{1,0:T(8,128)(2,1)}, bf16[384,2048]{1,0:T(8,128)(2,1)}, u32[]{:S(2)}, u32[]{:S(2)}) collective-permute-start(bf16[384,2048]{1,0:T(8,128)(2,1)} %get-tuple-element.191), channel_id=1, source_target_pairs={{0,8},{8,0},{16,24},{24,16},{1,9},{9,1},{17,25},{25,17},{2,10},{10... | collective-permute-start | bytes 4718600 | tf_op jit(solution)/shard_map/ppermute | solution.py:24
  189.1 35.5 %collective-permute-start.13 = (bf16[384,2048]{1,0:T(8,128)(2,1)}, bf16[384,2048]{1,0:T(8,128)(2,1)}, u32[]{:S(2)}, u32[]{:S(2)}) collective-permute-start(bf16[384,2048]{1,0:T(8,128)(2,1)} %get-tuple-element.192), channel_id=1, source_target_pairs={{0,16},{8,24},{16,0},{24,8},{1,17},{9,25},{17,1},{25,9},{2,18},{10... | collective-permute-start | bytes 4718600 | tf_op jit(solution)/shard_map/ppermute | solution.py:24
  229.4 34.2 %collective-permute-start.15 = (bf16[384,2048]{1,0:T(8,128)(2,1)S(1)}, bf16[384,2048]{1,0:T(8,128)(2,1)S(1)}, u32[]{:S(2)}, u32[]{:S(2)}) collective-permute-start(bf16[384,2048]{1,0:T(8,128)(2,1)S(1)} %get-tuple-element.194.refs_0_), channel_id=1, source_target_pairs={{0,16},{8,24},{16,0},{24,8},{1,17},{9,25},{17,1},{25,9},{2,18},{10... | collective-permute-start | bytes 4718600 | tf_op jit(solution)/shard_map/ppermute | solution.py:24
  230.1 34.3 %collective-permute-start.14 = (bf16[384,2048]{1,0:T(8,128)(2,1)S(1)}, bf16[384,2048]{1,0:T(8,128)(2,1)S(1)}, u32[]{:S(2)}, u32[]{:S(2)}) collective-permute-start(bf16[384,2048]{1,0:T(8,128)(2,1)S(1)} %get-tuple-element.194.refs_0_), channel_id=1, source_target_pairs={{0,8},{8,0},{16,24},{24,16},{1,9},{9,1},{17,25},{25,17},{2,10},{10... | collective-permute-start | bytes 4718600 | tf_op jit(solution)/shard_map/ppermute | solution.py:24
  264.6 16.3 %collective-permute-start.17 = (bf16[192,2048]{1,0:T(8,128)(2,1)S(1)}, bf16[192,2048]{1,0:T(8,128)(2,1)S(1)}, u32[]{:S(2)}, u32[]{:S(2)}) collective-permute-start(bf16[192,2048]{1,0:T(8,128)(2,1)S(1)} %slice.268), channel_id=1, source_target_pairs={{0,8},{8,0},{16,24},{24,16},{1,9},{9,1},{17,25},{25,17},{2,10},{10... | collective-permute-start | bytes 2359304 | tf_op jit(solution)/shard_map/ppermute | solution.py:24
  265.1 15.9 %collective-permute-start.16 = (bf16[192,2048]{1,0:T(8,128)(2,1)S(1)}, bf16[192,2048]{1,0:T(8,128)(2,1)S(1)}, u32[]{:S(2)}, u32[]{:S(2)}) collective-permute-start(bf16[192,2048]{1,0:T(8,128)(2,1)S(1)} %slice.267), channel_id=1, source_target_pairs={{0,16},{8,24},{16,0},{24,8},{1,17},{9,25},{17,1},{25,9},{2,18},{10... | collective-permute-start | bytes 2359304 | tf_op jit(solution)/shard_map/ppermute | solution.py:24
  285.8 22.5 %collective-permute-start.22 = (bf16[192,2048]{1,0:T(8,128)(2,1)}, bf16[192,2048]{1,0:T(8,128)(2,1)S(1)}, u32[]{:S(2)}, u32[]{:S(2)}) collective-permute-start(bf16[192,2048]{1,0:T(8,128)(2,1)} %slice.279), channel_id=1, source_target_pairs={{0,8},{8,0},{16,24},{24,16},{1,9},{9,1},{17,25},{25,17},{2,10},{10... | collective-permute-start | bytes 2359304 | tf_op jit(solution)/shard_map/ppermute | solution.py:24
  286.8 21.5 %collective-permute-start.21 = (bf16[192,2048]{1,0:T(8,128)(2,1)}, bf16[192,2048]{1,0:T(8,128)(2,1)S(1)}, u32[]{:S(2)}, u32[]{:S(2)}) collective-permute-start(bf16[192,2048]{1,0:T(8,128)(2,1)} %slice.278), channel_id=1, source_target_pairs={{0,16},{8,24},{16,0},{24,8},{1,17},{9,25},{17,1},{25,9},{2,18},{10... | collective-permute-start | bytes 2359304 | tf_op jit(solution)/shard_map/ppermute | solution.py:24
  308.3 36.9 %collective-permute-start.24 = (bf16[1536,512]{1,0:T(8,128)(2,1)}, bf16[1536,512]{1,0:T(8,128)(2,1)}, u32[]{:S(2)}, u32[]{:S(2)}) collective-permute-start(bf16[1536,512]{1,0:T(8,128)(2,1)} %get-tuple-element.221.refs_5_), channel_id=1, source_target_pairs={{0,16},{8,24},{16,0},{24,8},{1,17},{9,25},{17,1},{25,9},{2,18},{10... | collective-permute-start | bytes 4718600 | tf_op jit(solution)/shard_map/ppermute | solution.py:24
  310.7 34.5 %collective-permute-start.23 = (bf16[1536,512]{1,0:T(8,128)(2,1)}, bf16[1536,512]{1,0:T(8,128)(2,1)}, u32[]{:S(2)}, u32[]{:S(2)}) collective-permute-start(bf16[1536,512]{1,0:T(8,128)(2,1)} %get-tuple-element.221.refs_5_), channel_id=1, source_target_pairs={{0,8},{8,0},{16,24},{24,16},{1,9},{9,1},{17,25},{25,17},{2,10},{10... | collective-permute-start | bytes 4718600 | tf_op jit(solution)/shard_map/ppermute | solution.py:24
  343.2 28.7 %collective-permute-start.26 = (bf16[768,512]{1,0:T(8,128)(2,1)S(1)}, bf16[768,512]{1,0:T(8,128)(2,1)S(1)}, u32[]{:S(2)}, u32[]{:S(2)}) collective-permute-start(bf16[768,512]{1,0:T(8,128)(2,1)S(1)} %get-tuple-element.347), channel_id=1, source_target_pairs={{0,16},{8,24},{16,0},{24,8},{1,17},{9,25},{17,1},{25,9},{2,18},{10... | collective-permute-start | bytes 2359304 | tf_op jit(solution)/shard_map/ppermute | solution.py:24
  345.2 26.7 %collective-permute-start.25 = (bf16[768,512]{1,0:T(8,128)(2,1)S(1)}, bf16[768,512]{1,0:T(8,128)(2,1)S(1)}, u32[]{:S(2)}, u32[]{:S(2)}) collective-permute-start(bf16[768,512]{1,0:T(8,128)(2,1)S(1)} %get-tuple-element.348), channel_id=1, source_target_pairs={{0,8},{8,0},{16,24},{24,16},{1,9},{9,1},{17,25},{25,17},{2,10},{10... | collective-permute-start | bytes 2359304 | tf_op jit(solution)/shard_map/ppermute | solution.py:24
  347.6 28.5 %collective-permute-start.30 = (bf16[768,512]{1,0:T(8,128)(2,1)S(1)}, bf16[768,512]{1,0:T(8,128)(2,1)S(1)}, u32[]{:S(2)}, u32[]{:S(2)}) collective-permute-start(bf16[768,512]{1,0:T(8,128)(2,1)S(1)} %slice.284), channel_id=1, source_target_pairs={{0,8},{8,0},{16,24},{24,16},{1,9},{9,1},{17,25},{25,17},{2,10},{10... | collective-permute-start | bytes 2359304 | tf_op jit(solution)/shard_map/ppermute | solution.py:24
  349.6 26.5 %collective-permute-start.29 = (bf16[768,512]{1,0:T(8,128)(2,1)S(1)}, bf16[768,512]{1,0:T(8,128)(2,1)S(1)}, u32[]{:S(2)}, u32[]{:S(2)}) collective-permute-start(bf16[768,512]{1,0:T(8,128)(2,1)S(1)} %slice.283), channel_id=1, source_target_pairs={{0,16},{8,24},{16,0},{24,8},{1,17},{9,25},{17,1},{25,9},{2,18},{10... | collective-permute-start | bytes 2359304 | tf_op jit(solution)/shard_map/ppermute | solution.py:24
  403.0 192.5 %reduce-scatter.8.cloned.1.call-start = ((), (), s32[]{:S(2)}) async-start(), calls=%async_computation.11 | async-start | bytes 8257536 | tf_op jit(solution)/shard_map/reduce_scatter | solution.py:885
  403.1 32.0 %collective-permute-start.27 = (bf16[1536,512]{1,0:T(8,128)(2,1)}, bf16[1536,512]{1,0:T(8,128)(2,1)S(1)}, u32[]{:S(2)}, u32[]{:S(2)}) collective-permute-start(bf16[1536,512]{1,0:T(8,128)(2,1)} %copy-done.67), channel_id=1, source_target_pairs={{0,8},{8,0},{16,24},{24,16},{1,9},{9,1},{17,25},{25,17},{2,10},{10... | collective-permute-start | bytes 4718600 | tf_op jit(solution)/shard_map/ppermute | solution.py:24
  404.4 32.0 %collective-permute-start.28 = (bf16[1536,512]{1,0:T(8,128)(2,1)S(1)}, bf16[1536,512]{1,0:T(8,128)(2,1)S(1)}, u32[]{:S(2)}, u32[]{:S(2)}) collective-permute-start(bf16[1536,512]{1,0:T(8,128)(2,1)S(1)} %copy-done.66), channel_id=1, source_target_pairs={{0,16},{8,24},{16,0},{24,8},{1,17},{9,25},{17,1},{25,9},{2,18},{10... | collective-permute-start | bytes 4718600 | tf_op jit(solution)/shard_map/ppermute | solution.py:24
  453.3 21.5 %collective-permute-start.31 = (bf16[192,2048]{1,0:T(8,128)(2,1)S(1)}, bf16[192,2048]{1,0:T(8,128)(2,1)S(1)}, u32[]{:S(2)}, u32[]{:S(2)}) collective-permute-start(bf16[192,2048]{1,0:T(8,128)(2,1)S(1)} %get-tuple-element.232), channel_id=1, source_target_pairs={{0,8},{8,0},{16,24},{24,16},{1,9},{9,1},{17,25},{25,17},{2,10},{10... | collective-permute-start | bytes 2359304 | tf_op jit(solution)/shard_map/ppermute | solution.py:24
  454.9 19.9 %collective-permute-start.32 = (bf16[192,2048]{1,0:T(8,128)(2,1)S(1)}, bf16[192,2048]{1,0:T(8,128)(2,1)S(1)}, u32[]{:S(2)}, u32[]{:S(2)}) collective-permute-start(bf16[192,2048]{1,0:T(8,128)(2,1)S(1)} %get-tuple-element.233), channel_id=1, source_target_pairs={{0,16},{8,24},{16,0},{24,8},{1,17},{9,25},{17,1},{25,9},{2,18},{10... | collective-permute-start | bytes 2359304 | tf_op jit(solution)/shard_map/ppermute | solution.py:24
  495.1 169.2 %reduce-scatter.10.cloned.1.call-start = ((), (), s32[]{:S(2)}) async-start(), calls=%async_computation.12 | async-start | bytes 2359296 | tf_op jit(solution)/shard_map/reduce_scatter | solution.py:885
  495.2 31.1 %collective-permute-start.33 = (bf16[384,2048]{1,0:T(8,128)(2,1)}, bf16[384,2048]{1,0:T(8,128)(2,1)S(1)}, u32[]{:S(2)}, u32[]{:S(2)}) collective-permute-start(bf16[384,2048]{1,0:T(8,128)(2,1)} %copy-done.69), channel_id=1, source_target_pairs={{0,8},{8,0},{16,24},{24,16},{1,9},{9,1},{17,25},{25,17},{2,10},{10... | collective-permute-start | bytes 4718600 | tf_op jit(solution)/shard_map/ppermute | solution.py:24
  495.6 30.7 %collective-permute-start.34 = (bf16[384,2048]{1,0:T(8,128)(2,1)}, bf16[384,2048]{1,0:T(8,128)(2,1)S(1)}, u32[]{:S(2)}, u32[]{:S(2)}) collective-permute-start(bf16[384,2048]{1,0:T(8,128)(2,1)} %copy-done.68), channel_id=1, source_target_pairs={{0,16},{8,24},{16,0},{24,8},{1,17},{9,25},{17,1},{25,9},{2,18},{10... | collective-permute-start | bytes 4718600 | tf_op jit(solution)/shard_map/ppermute | solution.py:24
  535.4 33.9 %collective-permute-start.36 = (bf16[384,2048]{1,0:T(8,128)(2,1)S(1)}, bf16[384,2048]{1,0:T(8,128)(2,1)S(1)}, u32[]{:S(2)}, u32[]{:S(2)}) collective-permute-start(bf16[384,2048]{1,0:T(8,128)(2,1)S(1)} %get-tuple-element.251), channel_id=1, source_target_pairs={{0,16},{8,24},{16,0},{24,8},{1,17},{9,25},{17,1},{25,9},{2,18},{10... | collective-permute-start | bytes 4718600 | tf_op jit(solution)/shard_map/ppermute | solution.py:24
  536.2 34.2 %collective-permute-start.35 = (bf16[384,2048]{1,0:T(8,128)(2,1)S(1)}, bf16[384,2048]{1,0:T(8,128)(2,1)S(1)}, u32[]{:S(2)}, u32[]{:S(2)}) collective-permute-start(bf16[384,2048]{1,0:T(8,128)(2,1)S(1)} %get-tuple-element.251), channel_id=1, source_target_pairs={{0,8},{8,0},{16,24},{24,16},{1,9},{9,1},{17,25},{25,17},{2,10},{10... | collective-permute-start | bytes 4718600 | tf_op jit(solution)/shard_map/ppermute | solution.py:24
  570.5 12.1 %collective-permute-start.38 = (bf16[192,2048]{1,0:T(8,128)(2,1)S(1)}, bf16[192,2048]{1,0:T(8,128)(2,1)S(1)}, u32[]{:S(2)}, u32[]{:S(2)}) collective-permute-start(bf16[192,2048]{1,0:T(8,128)(2,1)S(1)} %slice.286), channel_id=1, source_target_pairs={{0,8},{8,0},{16,24},{24,16},{1,9},{9,1},{17,25},{25,17},{2,10},{10... | collective-permute-start | bytes 2359304 | tf_op jit(solution)/shard_map/ppermute | solution.py:24
  571.6 12.0 %collective-permute-start.37 = (bf16[192,2048]{1,0:T(8,128)(2,1)S(1)}, bf16[192,2048]{1,0:T(8,128)(2,1)S(1)}, u32[]{:S(2)}, u32[]{:S(2)}) collective-permute-start(bf16[192,2048]{1,0:T(8,128)(2,1)S(1)} %slice.285), channel_id=1, source_target_pairs={{0,16},{8,24},{16,0},{24,8},{1,17},{9,25},{17,1},{25,9},{2,18},{10... | collective-permute-start | bytes 2359304 | tf_op jit(solution)/shard_map/ppermute | solution.py:24
  590.3 158.0 %reduce-scatter.14.cloned.1.call-start = ((), (), s32[]{:S(2)}) async-start(), calls=%async_computation.14 | async-start | bytes 4718592 | tf_op jit(solution)/shard_map/reduce_scatter | solution.py:885
  616.1 147.4 %reduce-scatter.12.cloned.1.call-start = ((), (), s32[]{:S(2)}) async-start(), calls=%async_computation.13 | async-start | bytes 7077888 | tf_op jit(solution)/shard_map/reduce_scatter | solution.py:885
  617.6 24.4 %collective-permute-start.41 = (bf16[384,512]{1,0:T(8,128)(2,1)S(1)}, bf16[384,512]{1,0:T(8,128)(2,1)S(1)}, u32[]{:S(2)}, u32[]{:S(2)}) collective-permute-start(bf16[384,512]{1,0:T(8,128)(2,1)S(1)} %get-tuple-element.343), channel_id=1, source_target_pairs={{0,24},{8,16},{16,8},{24,0},{1,25},{9,17},{17,9},{25,1},{2,26},{10... | collective-permute-start | bytes 1179656 | tf_op jit(solution)/shard_map/ppermute | solution.py:24
  619.5 22.5 %collective-permute-start.40 = (bf16[384,512]{1,0:T(8,128)(2,1)S(1)}, bf16[384,512]{1,0:T(8,128)(2,1)S(1)}, u32[]{:S(2)}, u32[]{:S(2)}) collective-permute-start(bf16[384,512]{1,0:T(8,128)(2,1)S(1)} %get-tuple-element.344), channel_id=1, source_target_pairs={{0,16},{8,24},{16,0},{24,8},{1,17},{9,25},{17,1},{25,9},{2,18},{10... | collective-permute-start | bytes 1179656 | tf_op jit(solution)/shard_map/ppermute | solution.py:24
  620.2 21.8 %collective-permute-start.39 = (bf16[384,512]{1,0:T(8,128)(2,1)S(1)}, bf16[384,512]{1,0:T(8,128)(2,1)S(1)}, u32[]{:S(2)}, u32[]{:S(2)}) collective-permute-start(bf16[384,512]{1,0:T(8,128)(2,1)S(1)} %get-tuple-element.345), channel_id=1, source_target_pairs={{0,8},{8,0},{16,24},{24,16},{1,9},{9,1},{17,25},{25,17},{2,10},{10... | collective-permute-start | bytes 1179656 | tf_op jit(solution)/shard_map/ppermute | solution.py:24
  674.2 19.7 %collective-permute-start.42 = (bf16[192,2048]{1,0:T(8,128)(2,1)S(1)}, bf16[192,2048]{1,0:T(8,128)(2,1)S(1)}, u32[]{:S(2)}, u32[]{:S(2)}) collective-permute-start(bf16[192,2048]{1,0:T(8,128)(2,1)S(1)} %get-tuple-element.282), channel_id=1, source_target_pairs={{0,8},{8,0},{16,24},{24,16},{1,9},{9,1},{17,25},{25,17},{2,10},{10... | collective-permute-start | bytes 2359304 | tf_op jit(solution)/shard_map/ppermute | solution.py:24
  675.0 18.9 %collective-permute-start.43 = (bf16[192,2048]{1,0:T(8,128)(2,1)S(1)}, bf16[192,2048]{1,0:T(8,128)(2,1)S(1)}, u32[]{:S(2)}, u32[]{:S(2)}) collective-permute-start(bf16[192,2048]{1,0:T(8,128)(2,1)S(1)} %get-tuple-element.283), channel_id=1, source_target_pairs={{0,16},{8,24},{16,0},{24,8},{1,17},{9,25},{17,1},{25,9},{2,18},{10... | collective-permute-start | bytes 2359304 | tf_op jit(solution)/shard_map/ppermute | solution.py:24
  697.3 25.8 %collective-permute-start.44 = (bf16[384,2048]{1,0:T(8,128)(2,1)}, bf16[384,2048]{1,0:T(8,128)(2,1)}, u32[]{:S(2)}, u32[]{:S(2)}) collective-permute-start(bf16[384,2048]{1,0:T(8,128)(2,1)} %get-tuple-element.292), channel_id=1, source_target_pairs={{0,8},{8,0},{16,24},{24,16},{1,9},{9,1},{17,25},{25,17},{2,10},{10... | collective-permute-start | bytes 4718600 | tf_op jit(solution)/shard_map/ppermute | solution.py:24
  698.6 27.1 %collective-permute-start.45 = (bf16[384,2048]{1,0:T(8,128)(2,1)}, bf16[384,2048]{1,0:T(8,128)(2,1)}, u32[]{:S(2)}, u32[]{:S(2)}) collective-permute-start(bf16[384,2048]{1,0:T(8,128)(2,1)} %get-tuple-element.293), channel_id=1, source_target_pairs={{0,16},{8,24},{16,0},{24,8},{1,17},{9,25},{17,1},{25,9},{2,18},{10... | collective-permute-start | bytes 4718600 | tf_op jit(solution)/shard_map/ppermute | solution.py:24
  733.1 5.0 collective-permute-start.46
  738.2 5.1 collective-permute-start.47
  743.4 4.9 collective-permute-start.54
  749.5 8.5 %collective-permute-start.53 = (bf16[64,2816]{1,0:T(8,128)(2,1)S(1)}, bf16[64,2816]{1,0:T(8,128)(2,1)S(1)}, u32[]{:S(2)}, u32[]{:S(2)}) collective-permute-start(bf16[64,2816]{1,0:T(8,128)(2,1)S(1)} %get-tuple-element.351), channel_id=1, source_target_pairs={{0,24},{8,16},{16,8},{24,0},{1,25},{9,17},{17,9},{25,1},{2,26},{10... | collective-permute-start | bytes 1081352 | tf_op jit(solution)/shard_map/ppermute | solution.py:24
  750.6 11.1 %collective-permute-start.52 = (bf16[64,2816]{1,0:T(8,128)(2,1)S(1)}, bf16[64,2816]{1,0:T(8,128)(2,1)S(1)}, u32[]{:S(2)}, u32[]{:S(2)}) collective-permute-start(bf16[64,2816]{1,0:T(8,128)(2,1)S(1)} %get-tuple-element.352), channel_id=1, source_target_pairs={{0,16},{8,24},{16,0},{24,8},{1,17},{9,25},{17,1},{25,9},{2,18},{10... | collective-permute-start | bytes 1081352 | tf_op jit(solution)/shard_map/ppermute | solution.py:24
  751.6 10.2 %collective-permute-start.51 = (bf16[64,2816]{1,0:T(8,128)(2,1)S(1)}, bf16[64,2816]{1,0:T(8,128)(2,1)S(1)}, u32[]{:S(2)}, u32[]{:S(2)}) collective-permute-start(bf16[64,2816]{1,0:T(8,128)(2,1)S(1)} %get-tuple-element.353), channel_id=1, source_target_pairs={{0,8},{8,0},{16,24},{24,16},{1,9},{9,1},{17,25},{25,17},{2,10},{10... | collective-permute-start | bytes 1081352 | tf_op jit(solution)/shard_map/ppermute | solution.py:24
  763.5 4.9 collective-permute-start.56
  764.8 8.7 %collective-permute-start.50 = (bf16[64,1536]{1,0:T(8,128)(2,1)S(1)}, bf16[64,1536]{1,0:T(8,128)(2,1)S(1)}, u32[]{:S(2)}, u32[]{:S(2)}) collective-permute-start(bf16[64,1536]{1,0:T(8,128)(2,1)S(1)} %get-tuple-element.355), channel_id=1, source_target_pairs={{0,24},{8,16},{16,8},{24,0},{1,25},{9,17},{17,9},{25,1},{2,26},{10... | collective-permute-start | bytes 589832 | tf_op jit(solution)/shard_map/ppermute | solution.py:24
  765.9 11.2 %collective-permute-start.49 = (bf16[64,1536]{1,0:T(8,128)(2,1)S(1)}, bf16[64,1536]{1,0:T(8,128)(2,1)S(1)}, u32[]{:S(2)}, u32[]{:S(2)}) collective-permute-start(bf16[64,1536]{1,0:T(8,128)(2,1)S(1)} %get-tuple-element.356), channel_id=1, source_target_pairs={{0,16},{8,24},{16,0},{24,8},{1,17},{9,25},{17,1},{25,9},{2,18},{10... | collective-permute-start | bytes 589832 | tf_op jit(solution)/shard_map/ppermute | solution.py:24
  766.8 10.3 %collective-permute-start.48 = (bf16[64,1536]{1,0:T(8,128)(2,1)S(1)}, bf16[64,1536]{1,0:T(8,128)(2,1)S(1)}, u32[]{:S(2)}, u32[]{:S(2)}) collective-permute-start(bf16[64,1536]{1,0:T(8,128)(2,1)S(1)} %get-tuple-element.357), channel_id=1, source_target_pairs={{0,8},{8,0},{16,24},{24,16},{1,9},{9,1},{17,25},{25,17},{2,10},{10... | collective-permute-start | bytes 589832 | tf_op jit(solution)/shard_map/ppermute | solution.py:24
  (110 other events, 1185.7 us)
Sparse Core Ops, SparseCore 0:
  32.3 67.7 all-gather.5
  102.3 27.6 all-gather.7
  131.7 28.6 all-gather.9
  161.9 90.2 all-gather.11
  253.6 71.8 all-gather.13
  403.2 79.5 reduce-scatter.5
  495.2 77.8 reduce-scatter.7
  590.4 35.1 reduce-scatter.9
  627.9 48.3 reduce-scatter.13
  678.5 68.4 reduce-scatter.11
